TPU v7x, 32 devices: a whole 2x2x4 slice. The times are simulated.
32 devices in a mesh: src: 4 (over z), gx: 2 (over x), gy: 4 (over y, core).
Axes of the slice: x: 2, y: 2, z: 4, core: 2. Of those that a mesh axis runs over, the one named last changes fastest.
Arguments:
- labels: int32 [16, 128, 128], P('gx', 'gy'), may hold values from 0 to 15
- kappa_table: float32 [16], replicated, may hold values from 0.5 to 2
- absorb_table: float32 [16], replicated, may hold values from 0.02 to 0.1
- background: float32 [16, 16, 128, 128], P('src', 'gx', 'gy'), may hold values from 0.1 to 10
- det_cells: int32 [1024], replicated, may hold values from 0 to 262143
- v_kappa: float32 [16, 128, 128], P('gx', 'gy', 'src'), may hold values from -6 to 6
- v_absorb: float32 [16, 128, 128], P('gx', 'gy', 'src'), may hold values from -6 to 6
- q_kappa: float32 [16, 128, 128], P('gx', 'gy', 'src'), may hold values from -6 to 6
- q_absorb: float32 [16, 128, 128], P('gx', 'gy', 'src'), may hold values from -6 to 6
- beta_prev: float32 [1], replicated, may hold values from 0.2 to 2
Outputs:
- next_kappa: float32 [16, 128, 128], P('gx', 'gy', 'src')
- next_absorb: float32 [16, 128, 128], P('gx', 'gy', 'src')
- coefs: float32 [2], replicated
Inputs may be any that keep to these rules, and one draw needn't show every extreme that they name: `labels`: a region number for every cell. `det_cells`: flat index (x * 128 + y) * 128 + z of a grid cell; indices may repeat.
All inputs are finite; a program needn't handle non-finite values.
Results may differ from a plain program's by a relative error of at most 0.0001.
Values sent between devices are 32-bit elements; how exact they have to be, the bound alone decides.
No kernel may reach another device: no remote copies, remote signals or barrier semaphores. Data moves between devices by JAX's collectives and lax.ppermute only.
A program may use at most 128 MiB of HBM per device.

v0:
```python
import jax
import jax.numpy as jnp
from jax import lax
from jax.sharding import PartitionSpec as P

ITERS = 6


lam_low = 0.02
lam_high = 24.1
eps_norm = 1e-06


def padded_2(block, sides, width):
    for axis, dim in sides:
        count = lax.axis_size(axis)
        forward = [(i, i + 1) for i in range(count - 1)]
        backward = [(target, source) for source, target in forward]
        low = lax.ppermute(
            lax.slice_in_dim(block, block.shape[dim] - width, None, axis=dim), axis, forward
        )
        high = lax.ppermute(lax.slice_in_dim(block, 0, width, axis=dim), axis, backward)
        block = jnp.concatenate([low, block, high], axis=dim)
    return block


def regional(labels, table):
    field = jnp.zeros(labels.shape, jnp.float32)
    for region in range(table.shape[0]):
        field = field + jnp.where(labels == region, table[region], 0.0)
    return field


def beside(padded):
    widths = [(0, 0)] * (padded.ndim - 1) + [(1, 1)]
    full = jnp.pad(padded, widths)
    return [
        full[..., 2:, 1:-1, 1:-1],
        full[..., :-2, 1:-1, 1:-1],
        full[..., 1:-1, 2:, 1:-1],
        full[..., 1:-1, :-2, 1:-1],
        full[..., 1:-1, 1:-1, 2:],
        full[..., 1:-1, 1:-1, :-2],
    ]


def chebyshev(rhs, apply_op):
    theta = 0.5 * (lam_high + lam_low)
    delta = 0.5 * (lam_high - lam_low)
    sigma = theta / delta
    rho = 1.0 / sigma
    solution = jnp.zeros_like(rhs)
    remain = rhs
    step_dir = rhs / theta
    for step in range(ITERS):
        solution = solution + step_dir
        if step + 1 < ITERS:
            remain = remain - apply_op(step_dir)
            rho_next = 1.0 / (2.0 * sigma - rho)
            step_dir = rho_next * rho * step_dir + 2.0 * rho_next / delta * remain
            rho = rho_next
    return solution


def per_device(
    labels,
    kappa_table,
    absorb_table,
    background,
    det_cells,
    v_kappa,
    v_absorb,
    q_kappa,
    q_absorb,
    beta_prev,
):
    sources, cx, cy, cz = background.shape
    kappa = regional(labels, kappa_table)
    absorb = regional(labels, absorb_table)
    full_k, full_a = (
        lax.all_gather(v_kappa, "src", axis=2, tiled=True),
        lax.all_gather(v_absorb, "src", axis=2, tiled=True),
    )
    stacked = jnp.concatenate([background, kappa[None], full_k[None]], axis=0)
    rims = padded_2(stacked, (("gx", 1), ("gy", 2)), 1)
    near_all = beside(rims)
    kappa_faces = [0.5 * (kappa + near[sources]) for near in near_all]
    vk_faces = [0.5 * (full_k + near[sources + 1]) for near in near_all]
    phi_near = [near[:sources] for near in near_all]

    def apply_op(field):
        padded = padded_2(field, (("gx", 1), ("gy", 2)), 1)
        result = absorb * field
        for face, near in zip(kappa_faces, beside(padded)):
            result = result + face * (field - near)
        return result

    rhs = full_a * background
    for face, near in zip(vk_faces, phi_near):
        rhs = rhs + face * (background - near)
    rhs = -rhs
    change = chebyshev(rhs, apply_op)
    span_y = cy * lax.axis_size("gy")
    ix = det_cells // (span_y * cz)
    iy = det_cells // cz % span_y
    iz = det_cells % cz
    anchor_x = lax.axis_index("gx") * cx
    anchor_y = lax.axis_index("gy") * cy
    owned = (ix >= anchor_x) & (ix < anchor_x + cx) & (iy >= anchor_y) & (iy < anchor_y + cy)
    local = jnp.where(owned, ((ix - anchor_x) * cy + (iy - anchor_y)) * cz + iz, 0)
    seen_part = jnp.where(owned[None, :], change.reshape(sources, -1)[:, local], 0.0)
    base_part = jnp.where(owned[None, :], background.reshape(sources, -1)[:, local], 0.0)
    seen, base = lax.psum((seen_part, base_part), ("gx", "gy"))
    total = jnp.sum(base, axis=1, keepdims=True)
    mean_base = total / det_cells.shape[0]
    ratio = base / total
    jv_vals = (seen - ratio * jnp.sum(seen, axis=1, keepdims=True)) / mean_base
    weight = (jv_vals - jnp.sum(ratio * jv_vals, axis=1, keepdims=True)) / mean_base
    deposit = jnp.where(owned[None, :], weight, 0.0)
    source = (
        jnp.zeros((sources, cx * cy * cz), jnp.float32)
        .at[:, local]
        .add(deposit)
        .reshape(change.shape)
    )
    dual = chebyshev(source, apply_op)
    dual_rims = padded_2(dual, (("gx", 1), ("gy", 2)), 1)
    grad_a = -jnp.sum(background * dual, axis=0)
    grad_k = jnp.zeros_like(kappa)
    for near_phi, near_dual in zip(phi_near, beside(dual_rims)):
        grad_k = grad_k - 0.5 * jnp.sum((background - near_phi) * (dual - near_dual), axis=0)
    summed_k, summed_a = lax.psum((grad_k, grad_a), "src")
    slab = v_kappa.shape[2]
    offset = lax.axis_index("src") * slab
    hv_k = lax.dynamic_slice_in_dim(summed_k, offset, slab, 2)
    hv_a = lax.dynamic_slice_in_dim(summed_a, offset, slab, 2)
    cell_count = cx * lax.axis_size("gx") * cy * lax.axis_size("gy") * cz
    w_k = hv_k - beta_prev[0] * q_kappa
    w_a = hv_a - beta_prev[0] * q_absorb
    local_wv = jnp.sum(w_k * v_kappa) + jnp.sum(w_a * v_absorb)
    local_vv = jnp.sum(v_kappa * v_kappa) + jnp.sum(v_absorb * v_absorb)
    wv_sum, vv_sum = lax.psum((local_wv, local_vv), ("src", "gx", "gy"))
    alpha = wv_sum / cell_count / (vv_sum / cell_count + eps_norm)
    r_k = w_k - alpha * v_kappa
    r_a = w_a - alpha * v_absorb
    rr_sum = lax.psum(jnp.sum(r_k * r_k) + jnp.sum(r_a * r_a), ("src", "gx", "gy"))
    beta = jnp.sqrt(rr_sum / cell_count + eps_norm)
    return (r_k / beta, r_a / beta, jnp.stack([alpha, beta]))


def solution(mesh):
    return jax.shard_map(
        per_device,
        mesh=mesh,
        in_specs=(
            P("gx", "gy", None),
            P(),
            P(),
            P("src", "gx", "gy", None),
            P(),
            P("gx", "gy", "src"),
            P("gx", "gy", "src"),
            P("gx", "gy", "src"),
            P("gx", "gy", "src"),
            P(),
        ),
        out_specs=(P("gx", "gy", "src"), P("gx", "gy", "src"), P()),
        check_vma=False,
    )
```

profile of v0, /device:TPU:0, one launch (start us, length us, event | category | flops | bytes accessed | tf_op | source)
XLA Modules:
  0.0 524.2 jit_solution(12868290872623267246)
XLA Ops:
  12.2 17.4 %all_gather.6 = f32[8,32,128]{1,0,2:T(8,128)S(1)} all-gather(f32[8,32,32]{1,0,2:T(8,128)S(1)} %copy.423), channel_id=1, replica_groups=mesh['src'=4,'gx'=2,'gy'=4] {'src'}, dimensions={2}, use_global_device_ids=true | all-gather | bytes 163840 | tf_op jit(solution)/shard_map/all_gather | solution.py:81
  29.8 11.2 %broadcast_multiply_fusion.2 = (f32[8,32,128]{2,1,0:T(8,128)}, f32[8,32,128]{2,1,0:T(8,128)S(1)}, pred[8,32,128]{2,1,0:T(8,128)(4,1)S(1)}, pred[8,32,128]{2,1,0:...) fusion(f32[]{:T(128)} %bitcast.39, f32[]{:T(128)} %bitcast.38, ...), kind=kLoop, calls=%fused_computation.460 | loop fusion | flops 1572864 | bytes 917568 | tf_op jit(solution)/shard_map/mul | solution.py:93
  41.0 10.3 %select_add_fusion.1 = f32[8,32,128]{2,1,0:T(8,128)S(1)} fusion(pred[8,32,128]{2,1,0:T(8,128)(4,1)S(1)} %get-tuple-element.64, pred[8,32,128]{2,1,0:T(8,128)(4,1)S(1)} %get-tuple-element.63, pred[8,32,128]{2,1,0:T(8,128)(4,1)S(1)} %get-tuple-element.62, pred[8,32,128]{2,1,0:T(8,128)(4,1)S(1)} %get-tuple-element.61, ...), kind=kLoop, calls=%fused_computation.454 | loop fusion | flops 1015808 | bytes 655424 | tf_op jit(solution)/shard_map/add | solution.py:30
  52.6 4.6 collective-permute-start.1
  57.5 16.1 %all_gather.7 = f32[8,32,128]{1,0,2:T(8,128)S(1)} all-gather(f32[8,32,32]{1,0,2:T(8,128)S(1)} %copy.425), channel_id=1, replica_groups=mesh['src'=4,'gx'=2,'gy'=4] {'src'}, dimensions={2}, use_global_device_ids=true | all-gather | bytes 163840 | tf_op jit(solution)/shard_map/all_gather | solution.py:82
  85.1 4.5 collective-permute-start.5
  123.3 4.9 collective-permute-start.15
  139.5 5.1 collective-permute-start.19
  150.2 5.8 %collective-permute-start.21 = (f32[4,1,32,128]{3,2,1,0:T(8,128)}, f32[4,1,32,128]{3,2,1,0:T(8,128)}, u32[]{:S(2)}, u32[]{:S(2)}) collective-permute-start(f32[4,1,32,128]{3,2,1,0:T(8,128)} %get-tuple-element.124), channel_id=1, source_target_pairs={{0,4},{1,5},{2,6},{3,7},{8,12},{9,13},{10,14},{11,15},{16,20},{17,... | collective-permute-start | bytes 196616 | tf_op jit(solution)/shard_map/ppermute | solution.py:19
  161.1 5.5 %collective-permute-start.23 = (f32[4,10,1,128]{3,0,2,1:T(4,128)}, f32[4,10,1,128]{3,0,2,1:T(4,128)}, u32[]{:S(2)}, u32[]{:S(2)}) collective-permute-start(f32[4,10,1,128]{3,0,2,1:T(4,128)} %copy.459), channel_id=1, source_target_pairs={{0,1},{1,2},{2,3},{4,5},{5,6},{6,7},{8,9},{9,10},{10,11},{12,13},{... | collective-permute-start | bytes 61448 | tf_op jit(solution)/shard_map/ppermute | solution.py:19
  166.6 8.7 %copy.464 = f32[4,8,32,128]{0,3,2,1:T(8,128)} copy(f32[4,8,32,128]{3,2,1,0:T(8,128)S(1)} %copy-done) | data formatting | bytes 1048576 | tf_op args[3]
  175.3 9.8 %gather_fusion.1 = f32[1024,4]{1,0:T(8,128)} fusion(f32[4,32768]{0,1:T(8,128)} %bitcast.132, s32[1024]{0:T(1024)S(1)} %get-tuple-element.67), kind=kCustom, calls=%fused_computation.1 | custom fusion | bytes 36864 | tf_op jit(solution)/shard_map/gather | solution.py:112
  191.0 9.8 %copy.502 = f32[4,8,32,128]{0,3,2,1:T(8,128)} copy(f32[4,8,32,128]{3,2,1,0:T(8,128)} %fusion.113) | data formatting | bytes 1048576 | tf_op jit(solution)/shard_map/reshape | solution.py:111
  200.8 8.6 %gather_fusion = f32[1024,4]{1,0:T(8,128)S(1)} fusion(f32[4,32768]{0,1:T(8,128)} %bitcast.131, s32[1024]{0:T(1024)S(1)} %get-tuple-element.67), kind=kCustom, calls=%fused_computation | custom fusion | bytes 36864 | tf_op jit(solution)/shard_map/gather | solution.py:111
  210.4 53.2 %all-reduce.13 = (f32[4,1024]{0,1:T(8,128)S(1)}, f32[4,1024]{0,1:T(8,128)S(1)}) all-reduce(f32[4,1024]{0,1:T(8,128)} %get-tuple-element.139, f32[4,1024]{0,1:T(8,128)S(1)} %get-tuple-element.138), channel_id=1, replica_groups=mesh['src'=4,'gx'=2,'gy'=4] {'gx','gy'}, use_global_device_ids=true, to_apply=%region_1.2 | all-reduce | flops 8192 | bytes 65536 | tf_op jit(solution)/shard_map/psum | solution.py:113
  264.1 14.3 %scatter_custom_fusion = f32[4,32768]{0,1:T(8,128)} fusion(s32[1024]{0:T(1024)S(1)} %get-tuple-element.68, f32[]{:T(128)} %constant.43.clone.1, f32[4]{0:T(128)S(1)} %multiply_reduce_fusion.1, f32[4]{0:T(128)S(1)} %broadcast_multiply_fusion.3, pred[1024]{0:T(1024)(128)(4,1)S(1)} %get-tuple-element.69, f32[4,1024]{0,1:T(8,128)S(1)} %get-tuple-element.26, ...), kind=kCustom, calls=%fused_computation.3 | custom fusion | flops 32768 | bytes 1576960 | tf_op jit(solution)/shard_map/scatter-add | solution.py:123
  278.4 10.0 %copy.503 = f32[4,8,32,128]{3,2,1,0:T(8,128)S(1)} copy(f32[4,8,32,128]{0,3,2,1:T(8,128)} %bitcast.120) | data formatting | bytes 1048576 | tf_op jit(solution)/shard_map/reshape | solution.py:124
  304.3 4.8 collective-permute-start.29
  341.1 4.9 collective-permute-start.39
  357.4 4.9 collective-permute-start.43
  378.1 4.7 collective-permute-done.46
  388.4 38.7 %all-reduce.17.cloned.1.call-done = (f32[8,32,128]{2,1,0:T(8,128)}, f32[8,32,128]{2,1,0:T(8,128)}) async-done(((f32[8,32,128]{2,1,0:T(8,128)}, f32[8,32,128]{2,1,0:T(8,128)}), (f32[8,32,128]{2,1,0:T(8,128)}, f32[8,32,128]{2,1,0:T(8,128)})) %all-reduce.17.cloned.1.call-update) | async-done | bytes 262160 | tf_op jit(solution)/shard_map/psum | solution.py:132
  431.4 40.1 %all-reduce.12 = (f32[]{:T(128)}, f32[]{:T(128)}) all-reduce(f32[]{:T(128)S(6)} %add.608, f32[]{:T(128)S(6)} %add.609), channel_id=1, replica_groups=mesh['src'=4,'gx'=2,'gy'=4] {'src','gx','gy'}, use_global_device_ids=true, to_apply=%region_17.18 | all-reduce | flops 2 | bytes 16 | tf_op jit(solution)/shard_map/psum | solution.py:142
  475.4 39.3 %psum.55 = f32[]{:T(128)} all-reduce(f32[]{:T(128)S(6)} %add.611), channel_id=1, replica_groups=mesh['src'=4,'gx'=2,'gy'=4] {'src','gx','gy'}, use_global_device_ids=true, to_apply=%region_23.24 | all-reduce | flops 1 | bytes 8 | tf_op jit(solution)/shard_map/psum | solution.py:146
  (249 shorter events, 165.4 us)
Async XLA Ops:
  7.2 419.9 %all-reduce.17.cloned.1.call-start = ((), (), s32[]{:S(2)}) async-start(), calls=%async_computation | async-start | bytes 524288 | tf_op jit(solution)/shard_map/psum | solution.py:132
  51.3 22.4 %collective-permute-start = (f32[6,1,32,128]{3,2,1,0:T(8,128)S(1)}, f32[6,1,32,128]{3,2,1,0:T(8,128)S(1)}, u32[]{:S(2)}, u32[]{:S(2)}) collective-permute-start(f32[6,1,32,128]{3,2,1,0:T(8,128)S(1)} %get-tuple-element.89), channel_id=1, source_target_pairs={{4,0},{5,1},{6,2},{7,3},{12,8},{13,9},{14,10},{15,11},{20,16},{21,... | collective-permute-start | bytes 294920 | tf_op jit(solution)/shard_map/ppermute | solution.py:22
  52.6 21.2 %collective-permute-start.1 = (f32[6,1,32,128]{3,2,1,0:T(8,128)S(1)}, f32[6,1,32,128]{3,2,1,0:T(8,128)S(1)}, u32[]{:S(2)}, u32[]{:S(2)}) collective-permute-start(f32[6,1,32,128]{3,2,1,0:T(8,128)S(1)} %get-tuple-element.88), channel_id=1, source_target_pairs={{0,4},{1,5},{2,6},{3,7},{8,12},{9,13},{10,14},{11,15},{16,20},{17,... | collective-permute-start | bytes 294920 | tf_op jit(solution)/shard_map/ppermute | solution.py:19
  83.8 6.5 %collective-permute-start.4 = (f32[4,1,32,128]{3,2,1,0:T(8,128)S(1)}, f32[4,1,32,128]{3,2,1,0:T(8,128)S(1)}, u32[]{:S(2)}, u32[]{:S(2)}) collective-permute-start(f32[4,1,32,128]{3,2,1,0:T(8,128)S(1)} %get-tuple-element.133), channel_id=1, source_target_pairs={{4,0},{5,1},{6,2},{7,3},{12,8},{13,9},{14,10},{15,11},{20,16},{21,... | collective-permute-start | bytes 196616 | tf_op jit(solution)/shard_map/ppermute | solution.py:22
  85.1 7.0 %collective-permute-start.5 = (f32[4,1,32,128]{3,2,1,0:T(8,128)S(1)}, f32[4,1,32,128]{3,2,1,0:T(8,128)S(1)}, u32[]{:S(2)}, u32[]{:S(2)}) collective-permute-start(f32[4,1,32,128]{3,2,1,0:T(8,128)S(1)} %get-tuple-element.132), channel_id=1, source_target_pairs={{0,4},{1,5},{2,6},{3,7},{8,12},{9,13},{10,14},{11,15},{16,20},{17,... | collective-permute-start | bytes 196616 | tf_op jit(solution)/shard_map/ppermute | solution.py:19
  100.2 6.4 %collective-permute-start.9 = (f32[4,1,32,128]{3,2,1,0:T(8,128)S(1)}, f32[4,1,32,128]{3,2,1,0:T(8,128)S(1)}, u32[]{:S(2)}, u32[]{:S(2)}) collective-permute-start(f32[4,1,32,128]{3,2,1,0:T(8,128)S(1)} %get-tuple-element.130), channel_id=1, source_target_pairs={{0,4},{1,5},{2,6},{3,7},{8,12},{9,13},{10,14},{11,15},{16,20},{17,... | collective-permute-start | bytes 196616 | tf_op jit(solution)/shard_map/ppermute | solution.py:19
  115.5 6.4 %collective-permute-start.13 = (f32[4,1,32,128]{3,2,1,0:T(8,128)S(1)}, f32[4,1,32,128]{3,2,1,0:T(8,128)S(1)}, u32[]{:S(2)}, u32[]{:S(2)}) collective-permute-start(f32[4,1,32,128]{3,2,1,0:T(8,128)S(1)} %get-tuple-element.128), channel_id=1, source_target_pairs={{0,4},{1,5},{2,6},{3,7},{8,12},{9,13},{10,14},{11,15},{16,20},{17,... | collective-permute-start | bytes 196616 | tf_op jit(solution)/shard_map/ppermute | solution.py:19
  122.0 6.2 %collective-permute-start.14 = (f32[4,10,1,128]{3,0,2,1:T(4,128)S(1)}, f32[4,10,1,128]{3,0,2,1:T(4,128)S(1)}, u32[]{:S(2)}, u32[]{:S(2)}) collective-permute-start(f32[4,10,1,128]{3,0,2,1:T(4,128)S(1)} %copy.445), channel_id=1, source_target_pairs={{1,0},{2,1},{3,2},{5,4},{6,5},{7,6},{9,8},{10,9},{11,10},{13,12},{... | collective-permute-start | bytes 61448 | tf_op jit(solution)/shard_map/ppermute | solution.py:22
  131.7 6.4 %collective-permute-start.17 = (f32[4,1,32,128]{3,2,1,0:T(8,128)S(1)}, f32[4,1,32,128]{3,2,1,0:T(8,128)S(1)}, u32[]{:S(2)}, u32[]{:S(2)}) collective-permute-start(f32[4,1,32,128]{3,2,1,0:T(8,128)S(1)} %get-tuple-element.126), channel_id=1, source_target_pairs={{0,4},{1,5},{2,6},{3,7},{8,12},{9,13},{10,14},{11,15},{16,20},{17,... | collective-permute-start | bytes 196616 | tf_op jit(solution)/shard_map/ppermute | solution.py:19
  138.2 6.4 %collective-permute-start.18 = (f32[4,10,1,128]{3,0,2,1:T(4,128)S(1)}, f32[4,10,1,128]{3,0,2,1:T(4,128)S(1)}, u32[]{:S(2)}, u32[]{:S(2)}) collective-permute-start(f32[4,10,1,128]{3,0,2,1:T(4,128)S(1)} %copy.451), channel_id=1, source_target_pairs={{1,0},{2,1},{3,2},{5,4},{6,5},{7,6},{9,8},{10,9},{11,10},{13,12},{... | collective-permute-start | bytes 61448 | tf_op jit(solution)/shard_map/ppermute | solution.py:22
  148.9 7.1 %collective-permute-start.20 = (f32[4,1,32,128]{3,2,1,0:T(8,128)}, f32[4,1,32,128]{3,2,1,0:T(8,128)}, u32[]{:S(2)}, u32[]{:S(2)}) collective-permute-start(f32[4,1,32,128]{3,2,1,0:T(8,128)} %get-tuple-element.125), channel_id=1, source_target_pairs={{4,0},{5,1},{6,2},{7,3},{12,8},{13,9},{14,10},{15,11},{20,16},{21,... | collective-permute-start | bytes 196616 | tf_op jit(solution)/shard_map/ppermute | solution.py:22
  150.2 7.4 %collective-permute-start.21 = (f32[4,1,32,128]{3,2,1,0:T(8,128)}, f32[4,1,32,128]{3,2,1,0:T(8,128)}, u32[]{:S(2)}, u32[]{:S(2)}) collective-permute-start(f32[4,1,32,128]{3,2,1,0:T(8,128)} %get-tuple-element.124), channel_id=1, source_target_pairs={{0,4},{1,5},{2,6},{3,7},{8,12},{9,13},{10,14},{11,15},{16,20},{17,... | collective-permute-start | bytes 196616 | tf_op jit(solution)/shard_map/ppermute | solution.py:19
  159.2 25.9 %collective-permute-start.22 = (f32[4,10,1,128]{3,0,2,1:T(4,128)}, f32[4,10,1,128]{3,0,2,1:T(4,128)}, u32[]{:S(2)}, u32[]{:S(2)}) collective-permute-start(f32[4,10,1,128]{3,0,2,1:T(4,128)} %copy.457), channel_id=1, source_target_pairs={{1,0},{2,1},{3,2},{5,4},{6,5},{7,6},{9,8},{10,9},{11,10},{13,12},{... | collective-permute-start | bytes 61448 | tf_op jit(solution)/shard_map/ppermute | solution.py:22
  161.1 24.9 %collective-permute-start.23 = (f32[4,10,1,128]{3,0,2,1:T(4,128)}, f32[4,10,1,128]{3,0,2,1:T(4,128)}, u32[]{:S(2)}, u32[]{:S(2)}) collective-permute-start(f32[4,10,1,128]{3,0,2,1:T(4,128)} %copy.459), channel_id=1, source_target_pairs={{0,1},{1,2},{2,3},{4,5},{5,6},{6,7},{8,9},{9,10},{10,11},{12,13},{... | collective-permute-start | bytes 61448 | tf_op jit(solution)/shard_map/ppermute | solution.py:19
  288.5 6.3 %collective-permute-start.24 = (f32[4,1,32,128]{3,2,1,0:T(8,128)S(1)}, f32[4,1,32,128]{3,2,1,0:T(8,128)S(1)}, u32[]{:S(2)}, u32[]{:S(2)}) collective-permute-start(f32[4,1,32,128]{3,2,1,0:T(8,128)S(1)} %get-tuple-element.123), channel_id=1, source_target_pairs={{4,0},{5,1},{6,2},{7,3},{12,8},{13,9},{14,10},{15,11},{20,16},{21,... | collective-permute-start | bytes 196616 | tf_op jit(solution)/shard_map/ppermute | solution.py:22
  289.9 6.4 %collective-permute-start.25 = (f32[4,1,32,128]{3,2,1,0:T(8,128)S(1)}, f32[4,1,32,128]{3,2,1,0:T(8,128)S(1)}, u32[]{:S(2)}, u32[]{:S(2)}) collective-permute-start(f32[4,1,32,128]{3,2,1,0:T(8,128)S(1)} %get-tuple-element.122), channel_id=1, source_target_pairs={{0,4},{1,5},{2,6},{3,7},{8,12},{9,13},{10,14},{11,15},{16,20},{17,... | collective-permute-start | bytes 196616 | tf_op jit(solution)/shard_map/ppermute | solution.py:19
  303.0 6.2 %collective-permute-start.28 = (f32[4,1,32,128]{3,2,1,0:T(8,128)S(1)}, f32[4,1,32,128]{3,2,1,0:T(8,128)S(1)}, u32[]{:S(2)}, u32[]{:S(2)}) collective-permute-start(f32[4,1,32,128]{3,2,1,0:T(8,128)S(1)} %get-tuple-element.121), channel_id=1, source_target_pairs={{4,0},{5,1},{6,2},{7,3},{12,8},{13,9},{14,10},{15,11},{20,16},{21,... | collective-permute-start | bytes 196616 | tf_op jit(solution)/shard_map/ppermute | solution.py:22
  304.3 6.4 %collective-permute-start.29 = (f32[4,1,32,128]{3,2,1,0:T(8,128)S(1)}, f32[4,1,32,128]{3,2,1,0:T(8,128)S(1)}, u32[]{:S(2)}, u32[]{:S(2)}) collective-permute-start(f32[4,1,32,128]{3,2,1,0:T(8,128)S(1)} %get-tuple-element.120), channel_id=1, source_target_pairs={{0,4},{1,5},{2,6},{3,7},{8,12},{9,13},{10,14},{11,15},{16,20},{17,... | collective-permute-start | bytes 196616 | tf_op jit(solution)/shard_map/ppermute | solution.py:19
  318.6 6.4 %collective-permute-start.33 = (f32[4,1,32,128]{3,2,1,0:T(8,128)S(1)}, f32[4,1,32,128]{3,2,1,0:T(8,128)S(1)}, u32[]{:S(2)}, u32[]{:S(2)}) collective-permute-start(f32[4,1,32,128]{3,2,1,0:T(8,128)S(1)} %get-tuple-element.118), channel_id=1, source_target_pairs={{0,4},{1,5},{2,6},{3,7},{8,12},{9,13},{10,14},{11,15},{16,20},{17,... | collective-permute-start | bytes 196616 | tf_op jit(solution)/shard_map/ppermute | solution.py:19
  333.3 6.4 %collective-permute-start.37 = (f32[4,1,32,128]{3,2,1,0:T(8,128)S(1)}, f32[4,1,32,128]{3,2,1,0:T(8,128)S(1)}, u32[]{:S(2)}, u32[]{:S(2)}) collective-permute-start(f32[4,1,32,128]{3,2,1,0:T(8,128)S(1)} %get-tuple-element.116), channel_id=1, source_target_pairs={{0,4},{1,5},{2,6},{3,7},{8,12},{9,13},{10,14},{11,15},{16,20},{17,... | collective-permute-start | bytes 196616 | tf_op jit(solution)/shard_map/ppermute | solution.py:19
  339.8 6.2 %collective-permute-start.38 = (f32[4,10,1,128]{3,0,2,1:T(4,128)S(1)}, f32[4,10,1,128]{3,0,2,1:T(4,128)S(1)}, u32[]{:S(2)}, u32[]{:S(2)}) collective-permute-start(f32[4,10,1,128]{3,0,2,1:T(4,128)S(1)} %copy.484), channel_id=1, source_target_pairs={{1,0},{2,1},{3,2},{5,4},{6,5},{7,6},{9,8},{10,9},{11,10},{13,12},{... | collective-permute-start | bytes 61448 | tf_op jit(solution)/shard_map/ppermute | solution.py:22
  349.6 6.4 %collective-permute-start.41 = (f32[4,1,32,128]{3,2,1,0:T(8,128)S(1)}, f32[4,1,32,128]{3,2,1,0:T(8,128)S(1)}, u32[]{:S(2)}, u32[]{:S(2)}) collective-permute-start(f32[4,1,32,128]{3,2,1,0:T(8,128)S(1)} %get-tuple-element.114), channel_id=1, source_target_pairs={{0,4},{1,5},{2,6},{3,7},{8,12},{9,13},{10,14},{11,15},{16,20},{17,... | collective-permute-start | bytes 196616 | tf_op jit(solution)/shard_map/ppermute | solution.py:19
  356.0 6.2 %collective-permute-start.42 = (f32[4,10,1,128]{3,0,2,1:T(4,128)S(1)}, f32[4,10,1,128]{3,0,2,1:T(4,128)S(1)}, u32[]{:S(2)}, u32[]{:S(2)}) collective-permute-start(f32[4,10,1,128]{3,0,2,1:T(4,128)S(1)} %copy.490), channel_id=1, source_target_pairs={{1,0},{2,1},{3,2},{5,4},{6,5},{7,6},{9,8},{10,9},{11,10},{13,12},{... | collective-permute-start | bytes 61448 | tf_op jit(solution)/shard_map/ppermute | solution.py:22
  365.9 6.4 %collective-permute-start.45 = (f32[4,1,32,128]{3,2,1,0:T(8,128)S(1)}, f32[4,1,32,128]{3,2,1,0:T(8,128)S(1)}, u32[]{:S(2)}, u32[]{:S(2)}) collective-permute-start(f32[4,1,32,128]{3,2,1,0:T(8,128)S(1)} %get-tuple-element.112), channel_id=1, source_target_pairs={{0,4},{1,5},{2,6},{3,7},{8,12},{9,13},{10,14},{11,15},{16,20},{17,... | collective-permute-start | bytes 196616 | tf_op jit(solution)/shard_map/ppermute | solution.py:19
  (46 other events, 480.7 us)
Sparse Core Ops, SparseCore 0:
  387.9 39.1 all-reduce.16
where the time goes:
time: 526 us; the launch traced here: 524 us
  blocking collectives  166 us (32%)
  starting transfers between devices  136 us (26%)
  waiting for transfers between devices  71.6 us (14%)
  other arithmetic  69.6 us (13%)
  local copies, waits for them, and re-layouts  58.8 us (11%)
  between operations  21.8 us (4%)
    ppermute x24, starting transfers between devices, padded_2(): lax.ppermute(lax.slice_in_dim(block, block.shape[dim] - width, None, axis...  105 us
    psum x1, blocking collectives, per_device(): seen, base = lax.psum((seen_part, base_part), ('gx', 'gy'))  53.2 us
    psum x1, blocking collectives, per_device(): wv_sum, vv_sum = lax.psum((local_wv, local_vv), ('src', 'gx', 'gy'))  40.1 us
    psum x1, blocking collectives, per_device(): lax.psum(jnp.sum(r_k * r_k) + jnp.sum(r_a * r_a), ('src', 'gx', 'gy'))  39.3 us
    psum x1, waiting for transfers between devices, per_device(): summed_k, summed_a = lax.psum((grad_k, grad_a), 'src')  38.7 us
    ppermute x24, starting transfers between devices, padded_2(): lax.ppermute(lax.slice_in_dim(block, 0, width, axis=dim), axis, backward)  31.1 us
    ppermute x24, waiting for transfers between devices, padded_2(): lax.ppermute(lax.slice_in_dim(block, block.shape[dim] - width, None, axis...  24.9 us
    all_gather x1, blocking collectives, per_device(): lax.all_gather(v_kappa, 'src', axis=2, tiled=True)  17.4 us
  transfers between devices with their start and end apart: 49, of which 33 were waited for; matrix products, arithmetic and copies ran while one was open for 4% of the time, Pallas kernels for 0%

commit v1 on v0

--- a/solution.py
+++ b/solution.py
@@ -1,6 +1,10 @@
+import functools
+
 import jax
 import jax.numpy as jnp
 from jax import lax
+from jax.experimental import pallas as pl
+from jax.experimental.pallas import tpu as pltpu
 from jax.sharding import PartitionSpec as P
 
 ITERS = 6
@@ -148,9 +152,486 @@
     return (r_k / beta, r_a / beta, jnp.stack([alpha, beta]))
 
 
+def chebyshev_scalars():
+    theta = 0.5 * (lam_high + lam_low)
+    delta = 0.5 * (lam_high - lam_low)
+    sigma = theta / delta
+    rho = 1.0 / sigma
+    pairs = []
+    for _ in range(ITERS - 1):
+        rho_next = 1.0 / (2.0 * sigma - rho)
+        pairs.append((rho_next * rho, 2.0 * rho_next / delta))
+        rho = rho_next
+    return theta, pairs
+
+
+def places(split):
+    g = lax.axis_index("gy")
+    return lax.axis_index("src"), lax.axis_index("gx"), g // split, g % split
+
+
+def shifted(value, step, axis):
+    return pltpu.roll(value, step % value.shape[axis], axis)
+
+
+def index_along(shape, axis):
+    return lax.broadcasted_iota(jnp.int32, shape, axis)
+
+
+def beyond(value, step, axis):
+    size = value.shape[axis]
+    at = index_along(value.shape, axis)
+    edge = size - 1 if step == 1 else 0
+    return jnp.where(at == edge, 0.0, shifted(value, -step, axis))
+
+
+def pack_kernel(bg, labels, vk, va, packed, message):
+    _, x, _, _ = places(2)
+    half = bg.shape[0] // 2
+    for i in range(half):
+        message[i] = bg[half * (1 - x) + i]
+    message[half] = labels[...].astype(jnp.float32)
+    per = 128 // vk.shape[2]
+    for f, ref in enumerate((vk, va)):
+        for q in range(ref.shape[0] // per):
+            packed[f, q] = jnp.concatenate([ref[per * q + j] for j in range(per)], axis=1)
+
+
+def count_kernel(dets, count, *, ny, nz, half, halo):
+    _, _, y, _ = places(2)
+    planes, rows, _ = count.shape
+    flat = dets[...]
+    iz = flat % nz
+    line = flat // nz
+    iy = line % ny
+    ix = line // ny
+    row = iy - (half - halo) * y
+    spot = jnp.where((row >= 0) & (row < rows), ix * rows + row, -1)
+    dets_n = flat.shape[1]
+    at_z = (index_along((nz, dets_n), 0) == iz).astype(jnp.float32).astype(jnp.bfloat16)
+
+    def body(i, carry):
+        here = index_along((2 * rows, dets_n), 0) + i * (2 * rows)
+        hot = (here == spot).astype(jnp.float32).astype(jnp.bfloat16)
+        found = lax.dot_general(hot, at_z, (((1,), (1,)), ((), ())), preferred_element_type=jnp.float32)
+        count[pl.ds(2 * i, 2)] = found.reshape(2, rows, nz)
+        return carry
+
+    lax.fori_loop(0, planes // 2, body, 0)
+
+
+def gather_kernel(*refs, n):
+    bg, labels, msg = refs[:3]
+    own_v, other_v = refs[3 : 3 + n], refs[3 + n : 3 + 2 * n]
+    mine, fields, edge_other, edge_mine = refs[3 + 2 * n :]
+    s, x, y, c = places(2)
+    half = bg.shape[0] // 2
+    cx, cy, _ = labels.shape
+    here, there = cx * x, cx * (1 - x)
+    mine[pl.ds(here, cx)] = bg[half * x + c]
+    mine[pl.ds(there, cx)] = msg[c]
+    fields[0, pl.ds(here, cx)] = bg[half * x + 1 - c]
+    fields[0, pl.ds(there, cx)] = msg[1 - c]
+    fields[1, pl.ds(here, cx)] = labels[...].astype(jnp.float32)
+    fields[1, pl.ds(there, cx)] = msg[half]
+    slab = 128 // n
+    lane = index_along((cy, 128), 1) // slab
+    for start, parts in ((here, own_v), (there, other_v)):
+        for f in range(2):
+            for q in range(cx // n):
+                blocks = [part[f, q] for part in parts]
+                for j in range(n):
+                    plane = jnp.zeros((cy, 128), jnp.float32)
+                    for k in range(n):
+                        home = (s - k + n) % n
+                        moved = pltpu.roll(blocks[k], ((home - j + n) % n) * slab, 1)
+                        plane = jnp.where(lane == home, moved, plane)
+                    fields[2 + f, start + n * q + j] = plane
+    halo = edge_mine.shape[2]
+    first = (cy - halo) * (1 - y)
+    edge_other[...] = fields[:, :, pl.ds(first, halo), :]
+    edge_mine[0] = mine[:, pl.ds(first, halo), :]
+    edge_mine[1:] = fields[1:, :, pl.ds(first, halo), :]
+
+
+def solve(rem, sol, dirs, diag, fx, fy, fz):
+    planes = rem.shape[0]
+    _, pairs = chebyshev_scalars()
+    for step, (keep, push) in enumerate(pairs):
+        src, dst = dirs[step % 2], dirs[(step + 1) % 2]
+        last = step + 1 == len(pairs)
+
+        def body(i, carry):
+            d = src[i + 1]
+            coef_y, coef_z = fy[i], fz[i]
+            left = rem[i] - diag[i] * d
+            left = left + fx[i] * src[i] + fx[i + 1] * src[i + 2]
+            left = left + coef_y * shifted(d, -1, 0) + shifted(coef_y * d, 1, 0)
+            left = left + coef_z * shifted(d, -1, 1) + shifted(coef_z * d, 1, 1)
+            d = keep * d + push * left
+            sol[i] = sol[i] + d
+            if not last:
+                rem[i] = left
+                dst[i + 1] = d
+            return carry
+
+        lax.fori_loop(0, planes, body, 0, unroll=2)
+
+
+def folded(value):
+    return jnp.sum(value.reshape(-1, 8, value.shape[1]), axis=0)
+
+
+def first_kernel(
+    kap_table, abs_table, mine, fields, got, edge_other, edge_mine, count,
+    phi, sol, diag, fx, fy, fz, message,
+    labels, vk, va, kap, rem, dir_a, dir_b,
+):
+    _, _, y, c = places(2)
+    planes, cy, lanes = mine.shape
+    halo = edge_mine.shape[2]
+    rows = 2 * cy + halo
+    base = halo * y
+    for f, (ref, own, shift) in enumerate(
+        ((phi, mine, 0), (labels, fields.at[1], 0), (vk, fields.at[2], 1), (va, fields.at[3], 0))
+    ):
+        there = pl.ds(shift, planes)
+        ref[there, pl.ds(base + cy * c, cy), :] = own[...]
+        ref[there, pl.ds(base + cy * (1 - c), cy), :] = got[f]
+        ref[there, pl.ds(2 * cy * (1 - y), halo), :] = edge_other[f] + edge_mine[f]
+    blank = jnp.zeros((rows, lanes), jnp.float32)
+    for ref in (kap, vk, dir_a, dir_b):
+        ref[0] = blank
+        ref[planes + 1] = blank
+
+    lane = index_along((rows, lanes), 1)
+    kap_row, abs_row = blank, blank
+    for region in range(kap_table.shape[0]):
+        kap_row = jnp.where(lane == region, kap_table[region], kap_row)
+        abs_row = jnp.where(lane == region, abs_table[region], abs_row)
+
+    def look_up(i, carry):
+        at = labels[i].astype(jnp.int32)
+        kap[i + 1] = jnp.take_along_axis(kap_row, at, axis=1)
+        diag[i] = jnp.take_along_axis(abs_row, at, axis=1)
+        return carry
+
+    lax.fori_loop(0, planes, look_up, 0)
+    fx[0] = 0.5 * kap[1]
+    theta, _ = chebyshev_scalars()
+
+    def set_up(i, carry):
+        k = kap[i + 1]
+        along_x = 0.5 * (k + kap[i + 2])
+        k_y, k_z = beyond(k, 1, 0), beyond(k, 1, 1)
+        along_y, along_z = 0.5 * (k + k_y), 0.5 * (k + k_z)
+        fx[i + 1] = along_x
+        fy[i] = jnp.where(index_along(k.shape, 0) == rows - 1, 0.0, along_y)
+        fz[i] = jnp.where(lane == lanes - 1, 0.0, along_z)
+        back_y, back_z = 0.5 * (k + beyond(k, -1, 0)), 0.5 * (k + beyond(k, -1, 1))
+        diag[i] = diag[i] + fx[i] + along_x + along_y + back_y + along_z + back_z
+        v, p = vk[i + 1], phi[i]
+        low_v, low_p = vk[i], phi[jnp.maximum(i - 1, 0)] * jnp.where(i > 0, 1.0, 0.0)
+        high_v = vk[i + 2]
+        high_p = phi[jnp.minimum(i + 1, planes - 1)] * jnp.where(i < planes - 1, 1.0, 0.0)
+        total = va[i] * p + 0.5 * (v + low_v) * (p - low_p) + 0.5 * (v + high_v) * (p - high_p)
+        for axis in range(2):
+            for way in (1, -1):
+                total = total + 0.5 * (v + beyond(v, way, axis)) * (p - beyond(p, way, axis))
+        rem[i] = -total
+        d = total * (-1.0 / theta)
+        sol[i] = d
+        dir_a[i + 1] = d
+        return carry
+
+    lax.fori_loop(0, planes, set_up, 0)
+    solve(rem, sol, (dir_a, dir_b), diag, fx, fy, fz)
+
+    at_row = index_along((rows, lanes), 0)
+    owned = (at_row >= base) & (at_row < base + 2 * cy)
+
+    def add_up(i, sums):
+        n = jnp.where(owned, count[i], 0.0)
+        p, u = phi[i], sol[i]
+        np_ = n * p
+        parts = (np_, n * u, np_ * u, np_ * p)
+        return tuple(total + folded(part) for total, part in zip(sums, parts))
+
+    zero = jnp.zeros((8, lanes), jnp.float32)
+    sums = lax.fori_loop(0, planes, add_up, (zero,) * 4)
+    message[pl.ds(0, planes)] = sol[:, pl.ds((2 * cy - halo) * (1 - y) + halo * y, halo), :]
+    for i, part in enumerate(sums):
+        message[planes + i] = part
+
+
+def second_kernel(
+    phi, change, diag, fx, fy, fz, count, sent, came,
+    own, message,
+    rem, sol, dir_a, dir_b, pad,
+    *, dets,
+):
+    _, _, y, c = places(2)
+    planes, rows, lanes = phi.shape
+    halo = came.shape[1]
+    cy = (rows - halo) // 2
+    base = halo * y
+    edge = 2 * cy * (1 - y)
+    total, seen_sum, cross, square = (
+        jnp.sum(sent[planes + i] + came[planes + i]) for i in range(4)
+    )
+    one = jnp.ones((1, 1), jnp.float32)
+    total, seen_sum = total * one, seen_sum * one
+    mean = total / dets
+    part = seen_sum / total
+    level = (cross - part * square) / (total * mean)
+    inverse = 1.0 / mean
+    blank = jnp.zeros((rows, lanes), jnp.float32)
+    for ref in (dir_a, dir_b, pad):
+        ref[0] = blank
+        ref[planes + 1] = blank
+    theta, _ = chebyshev_scalars()
+    sol[...] = change[...]
+    sol[:, pl.ds(edge, halo), :] = came[pl.ds(0, planes)]
+
+    def set_up(i, carry):
+        p = phi[i]
+        jv = (sol[i] - p * part) * inverse
+        b = count[i] * ((jv - level) * inverse)
+        rem[i] = b
+        d = b * (1.0 / theta)
+        sol[i] = d
+        dir_a[i + 1] = d
+        pad[i + 1] = p
+        return carry
+
+    lax.fori_loop(0, planes, set_up, 0)
+    solve(rem, sol, (dir_a, dir_b), diag, fx, fy, fz)
+    dual = dir_a
+
+    def keep(i, carry):
+        dual[i + 1] = sol[i]
+        return carry
+
+    lax.fori_loop(0, planes, keep, 0)
+
+    def product(i, carry):
+        p, u = pad[i + 1], dual[i + 1]
+        grad = (p - pad[i]) * (u - dual[i]) + (p - pad[i + 2]) * (u - dual[i + 2])
+        for axis in range(2):
+            for way in (1, -1):
+                grad = grad + (p - beyond(p, way, axis)) * (u - beyond(u, way, axis))
+        rem[i] = -0.5 * grad
+        sol[i] = -(p * u)
+        return carry
+
+    lax.fori_loop(0, planes, product, 0)
+    for f, ref in enumerate((rem, sol)):
+        own[f] = ref[:, pl.ds(base + cy * c, cy), :]
+        message[f] = ref[:, pl.ds(base + cy * (1 - c), cy), :]
+
+
+def core_kernel(own, came, kept, message):
+    _, x, _, _ = places(2)
+    cx = kept.shape[1]
+    kept[...] = own[:, pl.ds(cx * x, cx)] + came[:, pl.ds(cx * x, cx)]
+    message[...] = own[:, pl.ds(cx * (1 - x), cx)] + came[:, pl.ds(cx * (1 - x), cx)]
+
+
+def slab_kernel(kept, came, *outs):
+    s, _, _, _ = places(2)
+    n = len(outs)
+    slab = 128 // n
+    _, cx, cy, _ = kept.shape
+    lane = index_along((cy, 128), 1) // slab
+    for f in range(2):
+        for q in range(cx // n):
+            planes = [kept[f, n * q + j] + came[f, n * q + j] for j in range(n)]
+            for k in range(n):
+                to = (s + k) % n
+                piece = jnp.zeros((cy, 128), jnp.float32)
+                for j in range(n):
+                    moved = pltpu.roll(planes[j], ((j - to + n) % n) * slab, 1)
+                    piece = jnp.where(lane == j, moved, piece)
+                outs[k][f, q] = piece
+
+
+def project_kernel(*refs, n):
+    beta_prev = refs[0]
+    parts = refs[1 : 1 + n]
+    vk, va, qk, qa, w_k, w_a, tile = refs[1 + n :]
+    s, x, y, c = places(2)
+    slab = 128 // n
+    for f, (q_ref, w) in enumerate(((qk, w_k), (qa, w_a))):
+        for q in range(vk.shape[0] // n):
+            whole = sum(part[f, q] for part in parts[1:]) + parts[0][f, q]
+            for j in range(n):
+                i = n * q + j
+                w[i] = whole[:, slab * j : slab * (j + 1)] - beta_prev[0] * q_ref[i]
+
+    def dot(a, b):
+        return jnp.sum(jnp.sum(a * b, axis=0))
+
+    wk, wa, v_k, v_a = w_k[...], w_a[...], vk[...], va[...]
+    one = jnp.ones((1, 1), jnp.float32)
+    wv = (dot(wk, v_k) + dot(wa, v_a)) * one
+    vv = (dot(v_k, v_k) + dot(v_a, v_a)) * one
+    a = jnp.where(vv > 0.0, wv / jnp.where(vv > 0.0, vv, 1.0), 0.0)
+    u_k, u_a = wk - a * v_k, wa - a * v_a
+    uv = (dot(u_k, v_k) + dot(u_a, v_a)) * one
+    uu = (dot(u_k, u_k) + dot(u_a, u_a)) * one
+    me = ((s * 2 + x) * 2 + y) * 2 + c
+    lane = index_along((8, 128), 1)
+    row = index_along((8, 128), 0)
+    values = jnp.zeros((8, 128), jnp.float32)
+    for i, value in enumerate((wv, vv, a, uv, uu)):
+        values = jnp.where(row == i, value, values)
+    tile[...] = jnp.where(lane == me, values, 0.0)
+
+
+def final_kernel(*refs, cells):
+    tiles, (w_k, w_a, vk, va, next_k, next_a, coefs) = refs[:-7], refs[-7:]
+    tile = tiles[0][...]
+    for other in tiles[1:]:
+        tile = tile + other[...]
+    wv, vv, a, uv, uu = (tile[i : i + 1] for i in range(5))
+    wv_sum = jnp.sum(wv, axis=1, keepdims=True)
+    vv_sum = jnp.sum(vv, axis=1, keepdims=True)
+    alpha = wv_sum / cells / (vv_sum / cells + eps_norm)
+    off = alpha - a
+    rr = jnp.sum(uu - 2.0 * off * uv + off * off * vv, axis=1, keepdims=True)
+    beta = jnp.sqrt(rr / cells + eps_norm)
+    next_k[...] = (w_k[...] - alpha * vk[...]) / beta
+    next_a[...] = (w_a[...] - alpha * va[...]) / beta
+    coefs[0] = jnp.sum(alpha)
+    coefs[1] = jnp.sum(beta)
+
+
+def f32(*shape):
+    return jax.ShapeDtypeStruct(shape, jnp.float32)
+
+
+def run(kernel, outs, *args, scratch=(), smem=(), mib=16, in_smem_out=(), cost=None):
+    vmem = pl.BlockSpec(memory_space=pltpu.VMEM)
+    scalar = pl.BlockSpec(memory_space=pltpu.SMEM)
+    return pl.pallas_call(
+        kernel,
+        out_shape=tuple(outs),
+        in_specs=[scalar if i in smem else vmem for i in range(len(args))],
+        out_specs=tuple(scalar if i in in_smem_out else vmem for i in range(len(outs))),
+        scratch_shapes=[pltpu.VMEM(shape, jnp.float32) for shape in scratch],
+        compiler_params=pltpu.CompilerParams(vmem_limit_bytes=mib * 2**20),
+        cost_estimate=cost,
+    )(*args)
+
+
+HALO = 8
+
+
+def per_device_paired(
+    labels, kappa_table, absorb_table, background, det_cells,
+    v_kappa, v_absorb, q_kappa, q_absorb, beta_prev,
+):
+    sources, cx, cy, cz = background.shape
+    n = lax.axis_size("src")
+    planes, rows = 2 * cx, 2 * cy + HALO
+    ny = cy * lax.axis_size("gy")
+    dets = det_cells.shape[0]
+    cells = planes * ny * cz
+    groups = cx // n
+
+    def swap_x(value):
+        return lax.ppermute(value, "gx", [(0, 1), (1, 0)])
+
+    def swap_core(value):
+        return lax.ppermute(value, "gy", [(0, 1), (1, 0), (2, 3), (3, 2)])
+
+    def along_z(value, k):
+        return lax.ppermute(value, "src", [(i, (i + k) % n) for i in range(n)])
+
+    packed, message = run(
+        pack_kernel, (f32(2, groups, cy, cz), f32(sources // 2 + 1, cx, cy, cz)),
+        background, labels, v_kappa, v_absorb,
+    )
+    other = swap_x(packed)
+    came = swap_x(message)
+    own_v = [packed] + [along_z(packed, k) for k in range(1, n)]
+    other_v = [other] + [along_z(other, k) for k in range(1, n)]
+    (count,) = run(
+        functools.partial(count_kernel, ny=ny, nz=cz, half=2 * cy, halo=HALO),
+        (f32(planes, rows, cz),), det_cells.reshape(1, dets),
+        cost=pl.CostEstimate(flops=2 * planes * rows * cz * dets, bytes_accessed=planes * rows * cz * 4, transcendentals=0),
+    )
+    mine, fields, edge_other, edge_mine = run(
+        functools.partial(gather_kernel, n=n),
+        (f32(planes, cy, cz), f32(4, planes, cy, cz), f32(4, planes, HALO, cz), f32(4, planes, HALO, cz)),
+        background, labels, came, *own_v, *other_v,
+    )
+    edge_other = lax.ppermute(edge_other, "gy", [(1, 2), (2, 1)])
+    edge_mine = lax.ppermute(edge_mine, "gy", [(1, 3), (2, 0)])
+    got = swap_core(fields)
+    frame = (planes, rows, cz)
+    wide = (planes + 2, rows, cz)
+    phi, change, diag, fx, fy, fz, sent = run(
+        first_kernel,
+        (f32(*frame), f32(*frame), f32(*frame), f32(planes + 1, rows, cz), f32(*frame), f32(*frame),
+         f32(planes + 4, HALO, cz)),
+        kappa_table, absorb_table, mine, fields, got, edge_other, edge_mine, count,
+        smem=(0, 1), scratch=(frame, wide, frame, wide, frame, wide, wide), mib=24,
+    )
+    heard = lax.ppermute(sent, "gy", [(i, (i + 2) % 4) for i in range(4)])
+    own, message = run(
+        functools.partial(second_kernel, dets=dets),
+        (f32(2, planes, cy, cz), f32(2, planes, cy, cz)),
+        phi, change, diag, fx, fy, fz, count, sent, heard,
+        scratch=(frame, frame, wide, wide, wide), mib=24,
+    )
+    kept, message = run(
+        core_kernel, (f32(2, cx, cy, cz), f32(2, cx, cy, cz)), own, swap_core(message)
+    )
+    pieces = run(
+        slab_kernel, [f32(2, groups, cy, cz)] * n, kept, swap_x(message)
+    )
+    parts = [pieces[0]] + [along_z(pieces[k], k) for k in range(1, n)]
+    w_k, w_a, tile = run(
+        functools.partial(project_kernel, n=n),
+        (f32(*v_kappa.shape), f32(*v_kappa.shape), f32(8, 128)),
+        beta_prev, *parts, v_kappa, v_absorb, q_kappa, q_absorb, smem=(0,),
+    )
+    tile = tile + sum(along_z(tile, k) for k in range(1, n))
+    over_x, over_core = swap_x(tile), swap_core(tile)
+    over_both = lax.ppermute(
+        tile, ("gx", "gy"), [(4 * a + b, 4 * (1 - a) + (b ^ 1)) for a in range(2) for b in range(4)]
+    )
+    tile = tile + over_x + over_core + over_both
+    over_y = lax.ppermute(tile, "gy", [(i, (i + 2) % 4) for i in range(4)])
+    return tuple(run(
+        functools.partial(final_kernel, cells=cells),
+        (f32(*v_kappa.shape), f32(*v_kappa.shape), f32(2)),
+        tile, over_y, w_k, w_a, v_kappa, v_absorb, in_smem_out=(2,),
+    ))
+
+
+def paired_fits(mesh):
+    return mesh.shape["gx"] == 2 and mesh.shape["gy"] == 4
+
+
+def body_for(mesh):
+    if not paired_fits(mesh):
+        return per_device
+
+    def chosen(*args):
+        sources, cx, cy, cz = args[3].shape
+        n = lax.axis_size("src")
+        fits = sources == 4 and cz == 128 and cx % n == 0 and cz % n == 0 and cy % HALO == 0
+        devices = 8 * n
+        return (per_device_paired if fits and devices <= 128 else per_device)(*args)
+
+    return chosen
+
+
 def solution(mesh):
     return jax.shard_map(
-        per_device,
+        body_for(mesh),
         mesh=mesh,
         in_specs=(
             P("gx", "gy", None),

time: 526 us -> 95.7 us (0.18)
  blocking collectives: 166 us -> 0 us
  starting transfers between devices: 136 us -> 33.9 us
  other arithmetic: 69.6 us -> 0.01 us
  local copies, waits for them, and re-layouts: 58.8 us -> 3.78 us
  waiting for transfers between devices: 71.6 us -> 34.5 us
  Pallas kernels: 0 us -> 21.8 us
  between operations: 21.8 us -> 1.46 us
    psum x3 -> x0, blocking collectives: 133 us -> none  [the longest x1 53.2 us: per_device(): seen, base = lax.psum((seen_part, base_part), ('gx', 'gy'))]
    ppermute x48 -> x24, starting transfers between devices: 136 us -> 33.9 us  [the longest x12 19.5 us: along_z(): return lax.ppermute(value, 'src', [(i, (i + k) % n) for i in range(n)])]
    psum x1 -> x0, waiting for transfers between devices: 38.7 us -> none  [per_device(): summed_k, summed_a = lax.psum((grad_k, grad_a), 'src')]
    all_gather x2 -> x0, blocking collectives: 33.4 us -> none  [the longest x1 17.4 us: per_device(): lax.all_gather(v_kappa, 'src', axis=2, tiled=True)]
    pallas_call x0 -> x9, Pallas kernels: none -> 21.8 us  [run(): pl.pallas_call(kernel, out_shape=tuple(outs), in_specs=[scalar if i in sm...]
    reshape x2 -> x0, local copies, waits for them, and re-layouts: 19.8 us -> none  [the longest x1 10 us: per_device(): source = jnp.zeros((sources, cx * cy * cz), jnp.float32).at[:, local].add...]
    add x11 -> x2, other arithmetic: 19.4 us -> 0.01 us  [the longest x1 0.01 us: per_device_paired(): tile = tile + sum((along_z(tile, k) for k in range(1, n)))]
    gather x2 -> x0, local copies, waits for them, and re-layouts: 18.4 us -> none  [the longest x1 9.79 us: per_device(): background.reshape(sources, -1)[:, local]]
  transfers between devices with their start and end apart: 49 -> 24, of which waited for: 33 -> 16; matrix products, arithmetic and copies ran while one was open for 4% -> 0% of each run, Pallas kernels for 0% -> 2%
where the time goes in v1:
time: 95.7 us; the launch traced here: 95.5 us
  waiting for transfers between devices  34.5 us (36%)
  starting transfers between devices  33.9 us (35%)
  Pallas kernels  21.8 us (23%)
  local copies, waits for them, and re-layouts  3.78 us (4%)
  between operations  1.46 us (2%)
    pallas_call x9, Pallas kernels, run(): pl.pallas_call(kernel, out_shape=tuple(outs), in_specs=[scalar if i in sm...  21.8 us
    ppermute x12, starting transfers between devices, along_z(): return lax.ppermute(value, 'src', [(i, (i + k) % n) for i in range(n)])  19.5 us
    ppermute x4, waiting for transfers between devices, swap_x(): return lax.ppermute(value, 'gx', [(0, 1), (1, 0)])  12.8 us
    ppermute x12, waiting for transfers between devices, along_z(): return lax.ppermute(value, 'src', [(i, (i + k) % n) for i in range(n)])  9.61 us
    ppermute x4, starting transfers between devices, swap_x(): return lax.ppermute(value, 'gx', [(0, 1), (1, 0)])  6.13 us
    ppermute x1, waiting for transfers between devices, per_device_paired(): edge_mine = lax.ppermute(edge_mine, 'gy', [(1, 3), (2, 0)])  4.14 us
    ppermute x1, starting transfers between devices, per_device_paired(): heard = lax.ppermute(sent, 'gy', [(i, (i + 2) % 4) for i in range(4)])  4 us
    unnamed x22, local copies, waits for them, and re-layouts  3.78 us
  transfers between devices with their start and end apart: 24, of which 16 were waited for; matrix products, arithmetic and copies ran while one was open for 0% of the time, Pallas kernels for 2%

profile of v1, /device:TPU:0, one launch (start us, length us, event | category | flops | bytes accessed | tf_op | source)
XLA Modules:
  0.0 95.5 jit_solution(15004905907953200557)
XLA Ops:
  4.5 3.0 %collective-permute-start = (f32[3,8,32,128]{3,2,1,0:T(8,128)S(1)}, f32[3,8,32,128]{3,2,1,0:T(8,128)S(1)}, u32[]{:S(2)}, u32[]{:S(2)}) collective-permute-start(f32[3,8,32,128]{3,2,1,0:T(8,128)S(1)} %get-tuple-element.27), channel_id=1, source_target_pairs={{0,4},{4,0},{1,5},{5,1},{2,6},{6,2},{3,7},{7,3},{8,12},{12,8},{9,1... | collective-permute-start | bytes 1179656 | tf_op jit(solution)/shard_map/ppermute | solution.py:543
  7.6 2.0 %collective-permute-start.1 = (f32[2,2,32,128]{3,2,1,0:T(8,128)S(1)}, f32[2,2,32,128]{3,2,1,0:T(8,128)S(1)}, u32[]{:S(2)}, u32[]{:S(2)}) collective-permute-start(f32[2,2,32,128]{3,2,1,0:T(8,128)S(1)} %get-tuple-element.28.refs_3_), channel_id=1, source_target_pairs={{0,8},{8,16},{16,24},{24,0},{1,9},{9,17},{17,25},{25,1},{2,10},{10... | collective-permute-start | bytes 196616 | tf_op jit(solution)/shard_map/ppermute | solution.py:549
  9.6 2.6 %collective-permute-start.2 = (f32[2,2,32,128]{3,2,1,0:T(8,128)S(1)}, f32[2,2,32,128]{3,2,1,0:T(8,128)S(1)}, u32[]{:S(2)}, u32[]{:S(2)}) collective-permute-start(f32[2,2,32,128]{3,2,1,0:T(8,128)S(1)} %get-tuple-element.28.refs_3_), channel_id=1, source_target_pairs={{0,16},{8,24},{16,0},{24,8},{1,17},{9,25},{17,1},{25,9},{2,18},{10... | collective-permute-start | bytes 196616 | tf_op jit(solution)/shard_map/ppermute | solution.py:549
  13.6 4.5 %collective-permute-done.4.refs_7_ = f32[2,2,32,128]{3,2,1,0:T(8,128)S(1)} collective-permute-done((f32[2,2,32,128]{3,2,1,0:T(8,128)S(1)}, f32[2,2,32,128]{3,2,1,0:T(8,128)S(1)}, u32[]{:S(2)}, u32[]{:S(2)}) %collective-permute-start.4) | collective-permute-done | bytes 65568 | tf_op jit(solution)/shard_map/ppermute | solution.py:543
  18.0 1.8 %collective-permute-start.5 = (f32[2,2,32,128]{3,2,1,0:T(8,128)S(1)}, f32[2,2,32,128]{3,2,1,0:T(8,128)S(1)}, u32[]{:S(2)}, u32[]{:S(2)}) collective-permute-start(f32[2,2,32,128]{3,2,1,0:T(8,128)S(1)} %collective-permute-done.4.refs_7_), channel_id=1, source_target_pairs={{0,8},{8,16},{16,24},{24,0},{1,9},{9,17},{17,25},{25,1},{2,10},{10... | collective-permute-start | bytes 196616 | tf_op jit(solution)/shard_map/ppermute | solution.py:549
  19.9 2.6 %collective-permute-start.6 = (f32[2,2,32,128]{3,2,1,0:T(8,128)S(1)}, f32[2,2,32,128]{3,2,1,0:T(8,128)S(1)}, u32[]{:S(2)}, u32[]{:S(2)}) collective-permute-start(f32[2,2,32,128]{3,2,1,0:T(8,128)S(1)} %collective-permute-done.4.refs_7_), channel_id=1, source_target_pairs={{0,16},{8,24},{16,0},{24,8},{1,17},{9,25},{17,1},{25,9},{2,18},{10... | collective-permute-start | bytes 196616 | tf_op jit(solution)/shard_map/ppermute | solution.py:549
  24.7 2.0 %collective-permute-done.6.refs_9_ = f32[2,2,32,128]{3,2,1,0:T(8,128)S(1)} collective-permute-done((f32[2,2,32,128]{3,2,1,0:T(8,128)S(1)}, f32[2,2,32,128]{3,2,1,0:T(8,128)S(1)}, u32[]{:S(2)}, u32[]{:S(2)}) %collective-permute-start.6) | collective-permute-done | bytes 65568 | tf_op jit(solution)/shard_map/ppermute | solution.py:549
  29.7 2.1 %shard_map.123.count = f32[16,72,128]{2,1,0:T(8,128)S(1)} custom-call(s32[1,1024]{1,0:T(1,128)S(1)} %bitcast.1), custom_call_target="tpu_custom_call" | custom-call | flops 301989888 | bytes 589824 | tf_op jit(solution)/shard_map/pallas_call | solution.py:516
  31.9 4.1 %collective-permute-done.10.edge_mine = f32[4,16,8,128]{3,2,1,0:T(8,128)S(1)} collective-permute-done((f32[4,16,8,128]{3,2,1,0:T(8,128)S(1)}, f32[4,16,8,128]{3,2,1,0:T(8,128)S(1)}, u32[]{:S(2)}, u32[]{:S(2)}) %collective-permute-start.10) | collective-permute-done | bytes 262176 | tf_op jit(solution)/shard_map/ppermute | solution.py:570
  36.0 9.9 %shard_map.124 = (f32[16,72,128]{2,1,0:T(8,128)S(1)}, f32[16,72,128]{2,1,0:T(8,128)S(1)}, f32[16,72,128]{2,1,0:T(8,128)S(1)}, f32[17,72,128]{2,1,0:T(8,128)S(1)}...) custom-call(f32[16]{0:T(128)S(1)} %copy-done.8, f32[16]{0:T(128)S(1)} %copy-done.9, ...), custom_call_target="tpu_custom_call" | custom-call | tf_op jit(solution)/shard_map/pallas_call | solution.py:516
  45.9 4.0 %collective-permute-start.11 = (f32[20,8,128]{2,1,0:T(8,128)S(1)}, f32[20,8,128]{2,1,0:T(8,128)S(1)}, u32[]{:S(2)}, u32[]{:S(2)}) collective-permute-start(f32[20,8,128]{2,1,0:T(8,128)S(1)} %get-tuple-element.39.sent), channel_id=1, source_target_pairs={{0,2},{1,3},{2,0},{3,1},{4,6},{5,7},{6,4},{7,5},{8,10},{9,11},{10,... | collective-permute-start | bytes 245768 | tf_op jit(solution)/shard_map/ppermute | solution.py:581
  49.9 3.0 %collective-permute-done.11.came = f32[20,8,128]{2,1,0:T(8,128)S(1)} collective-permute-done((f32[20,8,128]{2,1,0:T(8,128)S(1)}, f32[20,8,128]{2,1,0:T(8,128)S(1)}, u32[]{:S(2)}, u32[]{:S(2)}) %collective-permute-start.11) | collective-permute-done | bytes 81952 | tf_op jit(solution)/shard_map/ppermute | solution.py:581
  52.9 7.1 %shard_map.125 = (f32[2,16,32,128]{3,2,1,0:T(8,128)S(1)}, f32[2,16,32,128]{3,2,1,0:T(8,128)S(1)}) custom-call(f32[16,72,128]{2,1,0:T(8,128)S(1)} %get-tuple-element.33.phi, f32[16,72,128]{2,1,0:T(8,128)S(1)} %get-tuple-element.34.change, f32[16,72,128]{2,1,0:T(8,128)S(1)} %get-tuple-element.35.diag, f32[17,72,128]{2,1,0:T(8,128)S(1)} %get-tuple-element.36.fx, ...), custom_call_target="tpu_custom_call" | custom-call | tf_op jit(solution)/shard_map/pallas_call | solution.py:516
  60.3 1.8 %collective-permute-done.12.came = f32[2,16,32,128]{3,2,1,0:T(8,128)S(1)} collective-permute-done((f32[2,16,32,128]{3,2,1,0:T(8,128)S(1)}, f32[2,16,32,128]{3,2,1,0:T(8,128)S(1)}, u32[]{:S(2)}, u32[]{:S(2)}) %collective-permute-start.12) | collective-permute-done | bytes 524320 | tf_op jit(solution)/shard_map/ppermute | solution.py:546
  62.1 1.6 %collective-permute-start.13 = (f32[2,8,32,128]{3,2,1,0:T(8,128)S(1)}, f32[2,8,32,128]{3,2,1,0:T(8,128)S(1)}, u32[]{:S(2)}, u32[]{:S(2)}) collective-permute-start(f32[2,8,32,128]{3,2,1,0:T(8,128)S(1)} %get-tuple-element.43), channel_id=1, source_target_pairs={{0,4},{4,0},{1,5},{5,1},{2,6},{6,2},{3,7},{7,3},{8,12},{12,8},{9,1... | collective-permute-start | bytes 786440 | tf_op jit(solution)/shard_map/ppermute | solution.py:543
  63.7 6.9 %collective-permute-done.13.came = f32[2,8,32,128]{3,2,1,0:T(8,128)S(1)} collective-permute-done((f32[2,8,32,128]{3,2,1,0:T(8,128)S(1)}, f32[2,8,32,128]{3,2,1,0:T(8,128)S(1)}, u32[]{:S(2)}, u32[]{:S(2)}) %collective-permute-start.13) | collective-permute-done | bytes 262176 | tf_op jit(solution)/shard_map/ppermute | solution.py:543
  71.8 2.6 %collective-permute-start.15 = (f32[2,2,32,128]{3,2,1,0:T(8,128)S(1)}, f32[2,2,32,128]{3,2,1,0:T(8,128)S(1)}, u32[]{:S(2)}, u32[]{:S(2)}) collective-permute-start(f32[2,2,32,128]{3,2,1,0:T(8,128)S(1)} %get-tuple-element.46), channel_id=1, source_target_pairs={{0,16},{8,24},{16,0},{24,8},{1,17},{9,25},{17,1},{25,9},{2,18},{10... | collective-permute-start | bytes 196616 | tf_op jit(solution)/shard_map/ppermute | solution.py:549
  75.4 2.1 %collective-permute-done.14.refs_2_ = f32[2,2,32,128]{3,2,1,0:T(8,128)S(1)} collective-permute-done((f32[2,2,32,128]{3,2,1,0:T(8,128)S(1)}, f32[2,2,32,128]{3,2,1,0:T(8,128)S(1)}, u32[]{:S(2)}, u32[]{:S(2)}) %collective-permute-start.14) | collective-permute-done | bytes 65568 | tf_op jit(solution)/shard_map/ppermute | solution.py:549
  77.5 1.5 %collective-permute-done.15.refs_3_ = f32[2,2,32,128]{3,2,1,0:T(8,128)S(1)} collective-permute-done((f32[2,2,32,128]{3,2,1,0:T(8,128)S(1)}, f32[2,2,32,128]{3,2,1,0:T(8,128)S(1)}, u32[]{:S(2)}, u32[]{:S(2)}) %collective-permute-start.15) | collective-permute-done | bytes 65568 | tf_op jit(solution)/shard_map/ppermute | solution.py:549
  81.1 1.6 %collective-permute-start.18 = (f32[8,128]{1,0:T(8,128)S(1)}, f32[8,128]{1,0:T(8,128)S(1)}, u32[]{:S(2)}, u32[]{:S(2)}) collective-permute-start(f32[8,128]{1,0:T(8,128)S(1)} %get-tuple-element.48), channel_id=1, source_target_pairs={{0,16},{8,24},{16,0},{24,8},{1,17},{9,25},{17,1},{25,9},{2,18},{10... | collective-permute-start | bytes 12296 | tf_op jit(solution)/shard_map/ppermute | solution.py:549
  83.6 1.6 %collective-permute-done.17 = f32[8,128]{1,0:T(8,128)S(1)} collective-permute-done((f32[8,128]{1,0:T(8,128)S(1)}, f32[8,128]{1,0:T(8,128)S(1)}, u32[]{:S(2)}, u32[]{:S(2)}) %collective-permute-start.17) | collective-permute-done | bytes 4128 | tf_op jit(solution)/shard_map/ppermute | solution.py:549
  86.3 1.5 %collective-permute-start.20 = (f32[8,128]{1,0:T(8,128)S(1)}, f32[8,128]{1,0:T(8,128)S(1)}, u32[]{:S(2)}, u32[]{:S(2)}) collective-permute-start(f32[8,128]{1,0:T(8,128)S(1)} %add_add_fusion.1), channel_id=1, source_target_pairs={{0,4},{4,0},{1,5},{5,1},{2,6},{6,2},{3,7},{7,3},{8,12},{12,8},{9,1... | collective-permute-start | bytes 12296 | tf_op jit(solution)/shard_map/ppermute | solution.py:543
  88.5 1.5 %collective-permute-done.20 = f32[8,128]{1,0:T(8,128)S(1)} collective-permute-done((f32[8,128]{1,0:T(8,128)S(1)}, f32[8,128]{1,0:T(8,128)S(1)}, u32[]{:S(2)}, u32[]{:S(2)}) %collective-permute-start.20) | collective-permute-done | bytes 4128 | tf_op jit(solution)/shard_map/ppermute | solution.py:543
  92.3 2.2 %collective-permute-done.23.refs_1_ = f32[8,128]{1,0:T(8,128)S(1)} collective-permute-done((f32[8,128]{1,0:T(8,128)S(1)}, f32[8,128]{1,0:T(8,128)S(1)}, u32[]{:S(2)}, u32[]{:S(2)}) %collective-permute-start.23) | collective-permute-done | bytes 4128 | tf_op jit(solution)/shard_map/ppermute | solution.py:606
  (57 shorter events, 20.5 us)
Async XLA Ops:
  4.5 22.5 %collective-permute-start = (f32[3,8,32,128]{3,2,1,0:T(8,128)S(1)}, f32[3,8,32,128]{3,2,1,0:T(8,128)S(1)}, u32[]{:S(2)}, u32[]{:S(2)}) collective-permute-start(f32[3,8,32,128]{3,2,1,0:T(8,128)S(1)} %get-tuple-element.27), channel_id=1, source_target_pairs={{0,4},{4,0},{1,5},{5,1},{2,6},{6,2},{3,7},{7,3},{8,12},{12,8},{9,1... | collective-permute-start | bytes 1179656 | tf_op jit(solution)/shard_map/ppermute | solution.py:543
  7.5 10.5 %collective-permute-start.4 = (f32[2,2,32,128]{3,2,1,0:T(8,128)S(1)}, f32[2,2,32,128]{3,2,1,0:T(8,128)S(1)}, u32[]{:S(2)}, u32[]{:S(2)}) collective-permute-start(f32[2,2,32,128]{3,2,1,0:T(8,128)S(1)} %get-tuple-element.28.refs_3_), channel_id=1, source_target_pairs={{0,4},{4,0},{1,5},{5,1},{2,6},{6,2},{3,7},{7,3},{8,12},{12,8},{9,1... | collective-permute-start | bytes 196616 | tf_op jit(solution)/shard_map/ppermute | solution.py:543
  7.6 12.3 %collective-permute-start.1 = (f32[2,2,32,128]{3,2,1,0:T(8,128)S(1)}, f32[2,2,32,128]{3,2,1,0:T(8,128)S(1)}, u32[]{:S(2)}, u32[]{:S(2)}) collective-permute-start(f32[2,2,32,128]{3,2,1,0:T(8,128)S(1)} %get-tuple-element.28.refs_3_), channel_id=1, source_target_pairs={{0,8},{8,16},{16,24},{24,0},{1,9},{9,17},{17,25},{25,1},{2,10},{10... | collective-permute-start | bytes 196616 | tf_op jit(solution)/shard_map/ppermute | solution.py:549
  9.6 12.8 %collective-permute-start.2 = (f32[2,2,32,128]{3,2,1,0:T(8,128)S(1)}, f32[2,2,32,128]{3,2,1,0:T(8,128)S(1)}, u32[]{:S(2)}, u32[]{:S(2)}) collective-permute-start(f32[2,2,32,128]{3,2,1,0:T(8,128)S(1)} %get-tuple-element.28.refs_3_), channel_id=1, source_target_pairs={{0,16},{8,24},{16,0},{24,8},{1,17},{9,25},{17,1},{25,9},{2,18},{10... | collective-permute-start | bytes 196616 | tf_op jit(solution)/shard_map/ppermute | solution.py:549
  12.2 11.6 %collective-permute-start.3 = (f32[2,2,32,128]{3,2,1,0:T(8,128)S(1)}, f32[2,2,32,128]{3,2,1,0:T(8,128)S(1)}, u32[]{:S(2)}, u32[]{:S(2)}) collective-permute-start(f32[2,2,32,128]{3,2,1,0:T(8,128)S(1)} %get-tuple-element.28.refs_3_), channel_id=1, source_target_pairs={{0,24},{8,0},{16,8},{24,16},{1,25},{9,1},{17,9},{25,17},{2,26},{10... | collective-permute-start | bytes 196616 | tf_op jit(solution)/shard_map/ppermute | solution.py:549
  18.0 6.7 %collective-permute-start.5 = (f32[2,2,32,128]{3,2,1,0:T(8,128)S(1)}, f32[2,2,32,128]{3,2,1,0:T(8,128)S(1)}, u32[]{:S(2)}, u32[]{:S(2)}) collective-permute-start(f32[2,2,32,128]{3,2,1,0:T(8,128)S(1)} %collective-permute-done.4.refs_7_), channel_id=1, source_target_pairs={{0,8},{8,16},{16,24},{24,0},{1,9},{9,17},{17,25},{25,1},{2,10},{10... | collective-permute-start | bytes 196616 | tf_op jit(solution)/shard_map/ppermute | solution.py:549
  19.9 6.9 %collective-permute-start.6 = (f32[2,2,32,128]{3,2,1,0:T(8,128)S(1)}, f32[2,2,32,128]{3,2,1,0:T(8,128)S(1)}, u32[]{:S(2)}, u32[]{:S(2)}) collective-permute-start(f32[2,2,32,128]{3,2,1,0:T(8,128)S(1)} %collective-permute-done.4.refs_7_), channel_id=1, source_target_pairs={{0,16},{8,24},{16,0},{24,8},{1,17},{9,25},{17,1},{25,9},{2,18},{10... | collective-permute-start | bytes 196616 | tf_op jit(solution)/shard_map/ppermute | solution.py:549
  22.4 4.5 %collective-permute-start.7 = (f32[2,2,32,128]{3,2,1,0:T(8,128)S(1)}, f32[2,2,32,128]{3,2,1,0:T(8,128)S(1)}, u32[]{:S(2)}, u32[]{:S(2)}) collective-permute-start(f32[2,2,32,128]{3,2,1,0:T(8,128)S(1)} %collective-permute-done.4.refs_7_), channel_id=1, source_target_pairs={{0,24},{8,0},{16,8},{24,16},{1,25},{9,1},{17,9},{25,17},{2,26},{10... | collective-permute-start | bytes 196616 | tf_op jit(solution)/shard_map/ppermute | solution.py:549
  27.7 8.4 %collective-permute-start.8 = (f32[4,16,32,128]{3,2,1,0:T(8,128)S(1)}, f32[4,16,32,128]{3,2,1,0:T(8,128)S(1)}, u32[]{:S(2)}, u32[]{:S(2)}) collective-permute-start(f32[4,16,32,128]{3,2,1,0:T(8,128)S(1)} %get-tuple-element.30.fields), channel_id=1, source_target_pairs={{0,1},{1,0},{2,3},{3,2},{4,5},{5,4},{6,7},{7,6},{8,9},{9,8},{10,11... | collective-permute-start | bytes 3145736 | tf_op jit(solution)/shard_map/ppermute | solution.py:546
  27.7 8.3 %collective-permute-start.10 = (f32[4,16,8,128]{3,2,1,0:T(8,128)S(1)}, f32[4,16,8,128]{3,2,1,0:T(8,128)S(1)}, u32[]{:S(2)}, u32[]{:S(2)}) collective-permute-start(f32[4,16,8,128]{3,2,1,0:T(8,128)S(1)} %get-tuple-element.32), channel_id=1, source_target_pairs={{1,3},{2,0},{5,7},{6,4},{9,11},{10,8},{13,15},{14,12},{17,19},{18,... | collective-permute-start | bytes 786440 | tf_op jit(solution)/shard_map/ppermute | solution.py:570
  29.0 7.0 %collective-permute-start.9 = (f32[4,16,8,128]{3,2,1,0:T(8,128)S(1)}, f32[4,16,8,128]{3,2,1,0:T(8,128)S(1)}, u32[]{:S(2)}, u32[]{:S(2)}) collective-permute-start(f32[4,16,8,128]{3,2,1,0:T(8,128)S(1)} %get-tuple-element.31), channel_id=1, source_target_pairs={{1,2},{2,1},{5,6},{6,5},{9,10},{10,9},{13,14},{14,13},{17,18},{18,... | collective-permute-start | bytes 786440 | tf_op jit(solution)/shard_map/ppermute | solution.py:569
  45.9 7.0 %collective-permute-start.11 = (f32[20,8,128]{2,1,0:T(8,128)S(1)}, f32[20,8,128]{2,1,0:T(8,128)S(1)}, u32[]{:S(2)}, u32[]{:S(2)}) collective-permute-start(f32[20,8,128]{2,1,0:T(8,128)S(1)} %get-tuple-element.39.sent), channel_id=1, source_target_pairs={{0,2},{1,3},{2,0},{3,1},{4,6},{5,7},{6,4},{7,5},{8,10},{9,11},{10,... | collective-permute-start | bytes 245768 | tf_op jit(solution)/shard_map/ppermute | solution.py:581
  60.1 2.0 %collective-permute-start.12 = (f32[2,16,32,128]{3,2,1,0:T(8,128)S(1)}, f32[2,16,32,128]{3,2,1,0:T(8,128)S(1)}, u32[]{:S(2)}, u32[]{:S(2)}) collective-permute-start(f32[2,16,32,128]{3,2,1,0:T(8,128)S(1)} %get-tuple-element.41), channel_id=1, source_target_pairs={{0,1},{1,0},{2,3},{3,2},{4,5},{5,4},{6,7},{7,6},{8,9},{9,8},{10,11... | collective-permute-start | bytes 1572872 | tf_op jit(solution)/shard_map/ppermute | solution.py:546
  62.1 8.4 %collective-permute-start.13 = (f32[2,8,32,128]{3,2,1,0:T(8,128)S(1)}, f32[2,8,32,128]{3,2,1,0:T(8,128)S(1)}, u32[]{:S(2)}, u32[]{:S(2)}) collective-permute-start(f32[2,8,32,128]{3,2,1,0:T(8,128)S(1)} %get-tuple-element.43), channel_id=1, source_target_pairs={{0,4},{4,0},{1,5},{5,1},{2,6},{6,2},{3,7},{7,3},{8,12},{12,8},{9,1... | collective-permute-start | bytes 786440 | tf_op jit(solution)/shard_map/ppermute | solution.py:543
  70.9 6.6 %collective-permute-start.14 = (f32[2,2,32,128]{3,2,1,0:T(8,128)S(1)}, f32[2,2,32,128]{3,2,1,0:T(8,128)S(1)}, u32[]{:S(2)}, u32[]{:S(2)}) collective-permute-start(f32[2,2,32,128]{3,2,1,0:T(8,128)S(1)} %get-tuple-element.45), channel_id=1, source_target_pairs={{0,8},{8,16},{16,24},{24,0},{1,9},{9,17},{17,25},{25,1},{2,10},{10... | collective-permute-start | bytes 196616 | tf_op jit(solution)/shard_map/ppermute | solution.py:549
  71.8 7.3 %collective-permute-start.15 = (f32[2,2,32,128]{3,2,1,0:T(8,128)S(1)}, f32[2,2,32,128]{3,2,1,0:T(8,128)S(1)}, u32[]{:S(2)}, u32[]{:S(2)}) collective-permute-start(f32[2,2,32,128]{3,2,1,0:T(8,128)S(1)} %get-tuple-element.46), channel_id=1, source_target_pairs={{0,16},{8,24},{16,0},{24,8},{1,17},{9,25},{17,1},{25,9},{2,18},{10... | collective-permute-start | bytes 196616 | tf_op jit(solution)/shard_map/ppermute | solution.py:549
  74.3 4.8 %collective-permute-start.16 = (f32[2,2,32,128]{3,2,1,0:T(8,128)S(1)}, f32[2,2,32,128]{3,2,1,0:T(8,128)S(1)}, u32[]{:S(2)}, u32[]{:S(2)}) collective-permute-start(f32[2,2,32,128]{3,2,1,0:T(8,128)S(1)} %get-tuple-element.47), channel_id=1, source_target_pairs={{0,24},{8,0},{16,8},{24,16},{1,25},{9,1},{17,9},{25,17},{2,26},{10... | collective-permute-start | bytes 196616 | tf_op jit(solution)/shard_map/ppermute | solution.py:549
  79.7 5.5 %collective-permute-start.17 = (f32[8,128]{1,0:T(8,128)S(1)}, f32[8,128]{1,0:T(8,128)S(1)}, u32[]{:S(2)}, u32[]{:S(2)}) collective-permute-start(f32[8,128]{1,0:T(8,128)S(1)} %get-tuple-element.48), channel_id=1, source_target_pairs={{0,8},{8,16},{16,24},{24,0},{1,9},{9,17},{17,25},{25,1},{2,10},{10... | collective-permute-start | bytes 12296 | tf_op jit(solution)/shard_map/ppermute | solution.py:549
  81.1 4.5 %collective-permute-start.18 = (f32[8,128]{1,0:T(8,128)S(1)}, f32[8,128]{1,0:T(8,128)S(1)}, u32[]{:S(2)}, u32[]{:S(2)}) collective-permute-start(f32[8,128]{1,0:T(8,128)S(1)} %get-tuple-element.48), channel_id=1, source_target_pairs={{0,16},{8,24},{16,0},{24,8},{1,17},{9,25},{17,1},{25,9},{2,18},{10... | collective-permute-start | bytes 12296 | tf_op jit(solution)/shard_map/ppermute | solution.py:549
  82.7 3.6 %collective-permute-start.19 = (f32[8,128]{1,0:T(8,128)S(1)}, f32[8,128]{1,0:T(8,128)S(1)}, u32[]{:S(2)}, u32[]{:S(2)}) collective-permute-start(f32[8,128]{1,0:T(8,128)S(1)} %get-tuple-element.48), channel_id=1, source_target_pairs={{0,24},{8,0},{16,8},{24,16},{1,25},{9,1},{17,9},{25,17},{2,26},{10... | collective-permute-start | bytes 12296 | tf_op jit(solution)/shard_map/ppermute | solution.py:549
  86.3 3.6 %collective-permute-start.20 = (f32[8,128]{1,0:T(8,128)S(1)}, f32[8,128]{1,0:T(8,128)S(1)}, u32[]{:S(2)}, u32[]{:S(2)}) collective-permute-start(f32[8,128]{1,0:T(8,128)S(1)} %add_add_fusion.1), channel_id=1, source_target_pairs={{0,4},{4,0},{1,5},{5,1},{2,6},{6,2},{3,7},{7,3},{8,12},{12,8},{9,1... | collective-permute-start | bytes 12296 | tf_op jit(solution)/shard_map/ppermute | solution.py:543
  87.8 2.1 %collective-permute-start.21 = (f32[8,128]{1,0:T(8,128)S(1)}, f32[8,128]{1,0:T(8,128)S(1)}, u32[]{:S(2)}, u32[]{:S(2)}) collective-permute-start(f32[8,128]{1,0:T(8,128)S(1)} %add_add_fusion.1), channel_id=1, source_target_pairs={{0,1},{1,0},{2,3},{3,2},{4,5},{5,4},{6,7},{7,6},{8,9},{9,8},{10,11... | collective-permute-start | bytes 12296 | tf_op jit(solution)/shard_map/ppermute | solution.py:546
  87.8 3.0 %collective-permute-start.22 = (f32[8,128]{1,0:T(8,128)S(1)}, f32[8,128]{1,0:T(8,128)S(1)}, u32[]{:S(2)}, u32[]{:S(2)}) collective-permute-start(f32[8,128]{1,0:T(8,128)S(1)} %add_add_fusion.1), channel_id=1, source_target_pairs={{0,5},{1,4},{2,7},{3,6},{4,1},{5,0},{6,3},{7,2},{8,13},{9,12},{10,... | collective-permute-start | bytes 12296 | tf_op jit(solution)/shard_map/ppermute | solution.py:602
  90.9 3.6 %collective-permute-start.23 = (f32[8,128]{1,0:T(8,128)S(1)}, f32[8,128]{1,0:T(8,128)S(1)}, u32[]{:S(2)}, u32[]{:S(2)}) collective-permute-start(f32[8,128]{1,0:T(8,128)S(1)} %add_add_fusion.refs_0_), channel_id=1, source_target_pairs={{0,2},{1,3},{2,0},{3,1},{4,6},{5,7},{6,4},{7,5},{8,10},{9,11},{10,... | collective-permute-start | bytes 12296 | tf_op jit(solution)/shard_map/ppermute | solution.py:606
  (11 other events, 48.4 us)

commit v2 on v1

--- a/solution.py
+++ b/solution.py
@@ -185,16 +185,28 @@
     return jnp.where(at == edge, 0.0, shifted(value, -step, axis))
 
 
-def pack_kernel(bg, labels, vk, va, packed, message):
+def pack_kernel(bg, labels, vk, va, packed, message, raw, v_in, sems):
     _, x, _, _ = places(2)
     half = bg.shape[0] // 2
-    for i in range(half):
-        message[i] = bg[half * (1 - x) + i]
-    message[half] = labels[...].astype(jnp.float32)
+    copies = [
+        pltpu.make_async_copy(src, dst, sems.at[i])
+        for i, (src, dst) in enumerate((
+            (vk, v_in.at[0]),
+            (va, v_in.at[1]),
+            (bg.at[pl.ds(half * (1 - x), half)], message.at[pl.ds(0, half)]),
+            (labels, raw),
+        ))
+    ]
+    for copy in copies:
+        copy.start()
     per = 128 // vk.shape[2]
-    for f, ref in enumerate((vk, va)):
-        for q in range(ref.shape[0] // per):
-            packed[f, q] = jnp.concatenate([ref[per * q + j] for j in range(per)], axis=1)
+    for f in range(2):
+        copies[f].wait()
+        for q in range(vk.shape[0] // per):
+            packed[f, q] = jnp.concatenate([v_in[f, per * q + j] for j in range(per)], axis=1)
+    copies[3].wait()
+    message[half] = raw[...].astype(jnp.float32)
+    copies[2].wait()
 
 
 def count_kernel(dets, count, *, ny, nz, half, halo):
@@ -220,90 +232,123 @@
     lax.fori_loop(0, planes // 2, body, 0)
 
 
-def gather_kernel(*refs, n):
-    bg, labels, msg = refs[:3]
-    own_v, other_v = refs[3 : 3 + n], refs[3 + n : 3 + 2 * n]
-    mine, fields, edge_other, edge_mine = refs[3 + 2 * n :]
-    s, x, y, c = places(2)
+def photon_kernel(bg, labels, msg, mine, fields, edge_other, edge_mine, raw, sems):
+    _, x, y, c = places(2)
     half = bg.shape[0] // 2
     cx, cy, _ = labels.shape
     here, there = cx * x, cx * (1 - x)
-    mine[pl.ds(here, cx)] = bg[half * x + c]
+    copies = [
+        pltpu.make_async_copy(src, dst, sems.at[i])
+        for i, (src, dst) in enumerate((
+            (bg.at[half * x + c], mine.at[pl.ds(here, cx)]),
+            (bg.at[half * x + 1 - c], fields.at[0, pl.ds(here, cx)]),
+            (labels, raw),
+        ))
+    ]
+    for copy in copies:
+        copy.start()
     mine[pl.ds(there, cx)] = msg[c]
-    fields[0, pl.ds(here, cx)] = bg[half * x + 1 - c]
     fields[0, pl.ds(there, cx)] = msg[1 - c]
-    fields[1, pl.ds(here, cx)] = labels[...].astype(jnp.float32)
     fields[1, pl.ds(there, cx)] = msg[half]
-    slab = 128 // n
-    lane = index_along((cy, 128), 1) // slab
-    for start, parts in ((here, own_v), (there, other_v)):
-        for f in range(2):
-            for q in range(cx // n):
-                blocks = [part[f, q] for part in parts]
-                for j in range(n):
-                    plane = jnp.zeros((cy, 128), jnp.float32)
-                    for k in range(n):
-                        home = (s - k + n) % n
-                        moved = pltpu.roll(blocks[k], ((home - j + n) % n) * slab, 1)
-                        plane = jnp.where(lane == home, moved, plane)
-                    fields[2 + f, start + n * q + j] = plane
+    for copy in copies:
+        copy.wait()
+    fields[1, pl.ds(here, cx)] = raw[...].astype(jnp.float32)
     halo = edge_mine.shape[2]
     first = (cy - halo) * (1 - y)
     edge_other[...] = fields[:, :, pl.ds(first, halo), :]
     edge_mine[0] = mine[:, pl.ds(first, halo), :]
-    edge_mine[1:] = fields[1:, :, pl.ds(first, halo), :]
-
-
-def solve(rem, sol, dirs, diag, fx, fy, fz):
-    planes = rem.shape[0]
+    edge_mine[1] = fields[1, :, pl.ds(first, halo), :]
+
+
+def unpack_kernel(*refs):
+    parts, full = refs[:-1], refs[-1]
+    n = len(parts)
+    s, _, _, _ = places(2)
+    slab = 128 // n
+    _, cx, cy, _ = full.shape
+    lane = index_along((cy, 128), 1) // slab
+    for f in range(2):
+        for q in range(cx // n):
+            blocks = [part[f, q] for part in parts]
+            for j in range(n):
+                plane = jnp.zeros((cy, 128), jnp.float32)
+                for k in range(n):
+                    home = (s - k + n) % n
+                    moved = pltpu.roll(blocks[k], ((home - j + n) % n) * slab, 1)
+                    plane = jnp.where(lane == home, moved, plane)
+                full[f, n * q + j] = plane
+
+
+def vector_kernel(own, came, fields, edge):
+    _, x, y, _ = places(2)
+    cx, cy = own.shape[1:3]
+    halo = edge.shape[2]
+    first = (cy - halo) * (1 - y)
+    for start, part in ((cx * x, own), (cx * (1 - x), came)):
+        fields[:, pl.ds(start, cx)] = part[...]
+        edge[:, pl.ds(start, cx)] = part[:, :, pl.ds(first, halo), :]
+
+
+def solve(b, bufs, diag, fx, fy, fz, unroll):
+    planes = b.shape[0]
     _, pairs = chebyshev_scalars()
     for step, (keep, push) in enumerate(pairs):
-        src, dst = dirs[step % 2], dirs[(step + 1) % 2]
-        last = step + 1 == len(pairs)
+        src, dst = bufs[step % 2], bufs[(step + 1) % 2]
 
         def body(i, carry):
-            d = src[i + 1]
+            u = src[i + 1]
             coef_y, coef_z = fy[i], fz[i]
-            left = rem[i] - diag[i] * d
+            left = b[i] - diag[i] * u
             left = left + fx[i] * src[i] + fx[i + 1] * src[i + 2]
-            left = left + coef_y * shifted(d, -1, 0) + shifted(coef_y * d, 1, 0)
-            left = left + coef_z * shifted(d, -1, 1) + shifted(coef_z * d, 1, 1)
-            d = keep * d + push * left
-            sol[i] = sol[i] + d
-            if not last:
-                rem[i] = left
-                dst[i + 1] = d
+            left = left + coef_y * shifted(u, -1, 0) + shifted(coef_y * u, 1, 0)
+            left = left + coef_z * shifted(u, -1, 1) + shifted(coef_z * u, 1, 1)
+            change = u if step == 0 else u - dst[i + 1]
+            dst[i + 1] = u + keep * change + push * left
             return carry
 
-        lax.fori_loop(0, planes, body, 0, unroll=2)
+        lax.fori_loop(0, planes, body, 0, unroll=unroll)
+    return bufs[len(pairs) % 2]
 
 
 def folded(value):
     return jnp.sum(value.reshape(-1, 8, value.shape[1]), axis=0)
 
 
-def first_kernel(
+def framed(ref, shift, parts, planes, cy, halo, y, c):
+    own, got, edge_a, edge_b = parts
+    there = pl.ds(shift, planes)
+    base = halo * y
+    ref[there, pl.ds(base + cy * c, cy), :] = own
+    ref[there, pl.ds(base + cy * (1 - c), cy), :] = got
+    ref[there, pl.ds(2 * cy * (1 - y), halo), :] = edge_a + edge_b
+
+
+def blank_ends(*refs):
+    for ref in refs:
+        blank = jnp.zeros(ref.shape[1:], jnp.float32)
+        ref[0] = blank
+        ref[ref.shape[0] - 1] = blank
+
+
+def owned_rows(shape, base, count):
+    at_row = index_along(shape, 0)
+    return (at_row >= base) & (at_row < base + count)
+
+
+def stencil_kernel(
     kap_table, abs_table, mine, fields, got, edge_other, edge_mine, count,
-    phi, sol, diag, fx, fy, fz, message,
-    labels, vk, va, kap, rem, dir_a, dir_b,
+    phi, diag, fx, fy, fz, sums,
+    labels, kap,
 ):
     _, _, y, c = places(2)
     planes, cy, lanes = mine.shape
     halo = edge_mine.shape[2]
     rows = 2 * cy + halo
-    base = halo * y
-    for f, (ref, own, shift) in enumerate(
-        ((phi, mine, 0), (labels, fields.at[1], 0), (vk, fields.at[2], 1), (va, fields.at[3], 0))
-    ):
-        there = pl.ds(shift, planes)
-        ref[there, pl.ds(base + cy * c, cy), :] = own[...]
-        ref[there, pl.ds(base + cy * (1 - c), cy), :] = got[f]
-        ref[there, pl.ds(2 * cy * (1 - y), halo), :] = edge_other[f] + edge_mine[f]
+    place = (planes, cy, halo, y, c)
+    framed(phi, 1, (mine[...], got[0], edge_other[0], edge_mine[0]), *place)
+    framed(labels, 0, (fields[1], got[1], edge_other[1], edge_mine[1]), *place)
+    blank_ends(phi, kap)
     blank = jnp.zeros((rows, lanes), jnp.float32)
-    for ref in (kap, vk, dir_a, dir_b):
-        ref[0] = blank
-        ref[planes + 1] = blank
-
     lane = index_along((rows, lanes), 1)
     kap_row, abs_row = blank, blank
     for region in range(kap_table.shape[0]):
@@ -316,118 +361,126 @@
         diag[i] = jnp.take_along_axis(abs_row, at, axis=1)
         return carry
 
-    lax.fori_loop(0, planes, look_up, 0)
+    lax.fori_loop(0, planes, look_up, 0, unroll=2)
     fx[0] = 0.5 * kap[1]
-    theta, _ = chebyshev_scalars()
+    owned = owned_rows((rows, lanes), halo * y, 2 * cy)
 
     def set_up(i, carry):
         k = kap[i + 1]
         along_x = 0.5 * (k + kap[i + 2])
-        k_y, k_z = beyond(k, 1, 0), beyond(k, 1, 1)
-        along_y, along_z = 0.5 * (k + k_y), 0.5 * (k + k_z)
+        along_y, along_z = 0.5 * (k + beyond(k, 1, 0)), 0.5 * (k + beyond(k, 1, 1))
         fx[i + 1] = along_x
         fy[i] = jnp.where(index_along(k.shape, 0) == rows - 1, 0.0, along_y)
         fz[i] = jnp.where(lane == lanes - 1, 0.0, along_z)
         back_y, back_z = 0.5 * (k + beyond(k, -1, 0)), 0.5 * (k + beyond(k, -1, 1))
         diag[i] = diag[i] + fx[i] + along_x + along_y + back_y + along_z + back_z
-        v, p = vk[i + 1], phi[i]
-        low_v, low_p = vk[i], phi[jnp.maximum(i - 1, 0)] * jnp.where(i > 0, 1.0, 0.0)
-        high_v = vk[i + 2]
-        high_p = phi[jnp.minimum(i + 1, planes - 1)] * jnp.where(i < planes - 1, 1.0, 0.0)
-        total = va[i] * p + 0.5 * (v + low_v) * (p - low_p) + 0.5 * (v + high_v) * (p - high_p)
+        p = phi[i + 1]
+        part = jnp.where(owned, count[i], 0.0) * p
+        return carry[0] + folded(part), carry[1] + folded(part * p)
+
+    zero = jnp.zeros((8, lanes), jnp.float32)
+    sums[0], sums[1] = lax.fori_loop(0, planes, set_up, (zero, zero), unroll=2)
+
+
+def first_kernel(
+    phi, diag, fx, fy, fz, count, sums, fields, got, edge_a, edge_b,
+    change, message,
+    vk, va, b, buf_a, buf_b,
+):
+    _, _, y, c = places(2)
+    planes, rows, lanes = change.shape
+    halo = edge_a.shape[2]
+    cy = (rows - halo) // 2
+    place = (planes, cy, halo, y, c)
+    framed(vk, 1, (fields[0], got[0], edge_a[0], edge_b[0]), *place)
+    framed(va, 0, (fields[1], got[1], edge_a[1], edge_b[1]), *place)
+    blank_ends(vk, buf_a, buf_b)
+    theta, _ = chebyshev_scalars()
+
+    def set_up(i, carry):
+        v, p = vk[i + 1], phi[i + 1]
+        total = 0.5 * (v + vk[i]) * (p - phi[i]) + 0.5 * (v + vk[i + 2]) * (p - phi[i + 2])
         for axis in range(2):
-            for way in (1, -1):
-                total = total + 0.5 * (v + beyond(v, way, axis)) * (p - beyond(p, way, axis))
-        rem[i] = -total
-        d = total * (-1.0 / theta)
-        sol[i] = d
-        dir_a[i + 1] = d
+            flow = 0.5 * (v + beyond(v, 1, axis)) * (p - beyond(p, 1, axis))
+            first = index_along(v.shape, axis) == 0
+            total = total + flow + jnp.where(first, 0.5 * v * p, -shifted(flow, 1, axis))
+        total = -(va[i] * p + total)
+        b[i] = total
+        buf_a[i + 1] = total * (1.0 / theta)
         return carry
 
-    lax.fori_loop(0, planes, set_up, 0)
-    solve(rem, sol, (dir_a, dir_b), diag, fx, fy, fz)
-
-    at_row = index_along((rows, lanes), 0)
-    owned = (at_row >= base) & (at_row < base + 2 * cy)
-
-    def add_up(i, sums):
-        n = jnp.where(owned, count[i], 0.0)
-        p, u = phi[i], sol[i]
-        np_ = n * p
-        parts = (np_, n * u, np_ * u, np_ * p)
-        return tuple(total + folded(part) for total, part in zip(sums, parts))
+    lax.fori_loop(0, planes, set_up, 0, unroll=2)
+    found = solve(b, (buf_a, buf_b), diag, fx, fy, fz, 8)
+    owned = owned_rows((rows, lanes), halo * y, 2 * cy)
+
+    def add_up(i, carry):
+        u = found[i + 1]
+        change[i] = u
+        part = jnp.where(owned, count[i], 0.0) * u
+        return carry[0] + folded(part), carry[1] + folded(part * phi[i + 1])
 
     zero = jnp.zeros((8, lanes), jnp.float32)
-    sums = lax.fori_loop(0, planes, add_up, (zero,) * 4)
-    message[pl.ds(0, planes)] = sol[:, pl.ds((2 * cy - halo) * (1 - y) + halo * y, halo), :]
-    for i, part in enumerate(sums):
+    seen, cross = lax.fori_loop(0, planes, add_up, (zero, zero), unroll=2)
+    edge = (2 * cy - halo) * (1 - y) + halo * y
+    message[pl.ds(0, planes)] = found[pl.ds(1, planes), pl.ds(edge, halo), :]
+    for i, part in enumerate((sums[0], seen, cross, sums[1])):
         message[planes + i] = part
 
 
 def second_kernel(
     phi, change, diag, fx, fy, fz, count, sent, came,
     own, message,
-    rem, sol, dir_a, dir_b, pad,
+    b, buf_a, buf_b, grad_k, grad_a,
     *, dets,
 ):
     _, _, y, c = places(2)
-    planes, rows, lanes = phi.shape
+    planes, rows, lanes = change.shape
     halo = came.shape[1]
     cy = (rows - halo) // 2
     base = halo * y
-    edge = 2 * cy * (1 - y)
+    edge = pl.ds(2 * cy * (1 - y), halo)
+    one = jnp.ones((1, 1), jnp.float32)
     total, seen_sum, cross, square = (
-        jnp.sum(sent[planes + i] + came[planes + i]) for i in range(4)
-    )
-    one = jnp.ones((1, 1), jnp.float32)
-    total, seen_sum = total * one, seen_sum * one
+        jnp.sum(sent[planes + i] + came[planes + i]) * one for i in range(4)
+    )
     mean = total / dets
     part = seen_sum / total
     level = (cross - part * square) / (total * mean)
     inverse = 1.0 / mean
-    blank = jnp.zeros((rows, lanes), jnp.float32)
-    for ref in (dir_a, dir_b, pad):
-        ref[0] = blank
-        ref[planes + 1] = blank
+    blank_ends(buf_a, buf_b)
     theta, _ = chebyshev_scalars()
-    sol[...] = change[...]
-    sol[:, pl.ds(edge, halo), :] = came[pl.ds(0, planes)]
+
+    def weighted(n, u, p):
+        return n * (((u - p * part) * inverse - level) * inverse)
 
     def set_up(i, carry):
-        p = phi[i]
-        jv = (sol[i] - p * part) * inverse
-        b = count[i] * ((jv - level) * inverse)
-        rem[i] = b
-        d = b * (1.0 / theta)
-        sol[i] = d
-        dir_a[i + 1] = d
-        pad[i + 1] = p
+        value = weighted(count[i], change[i], phi[i + 1])
+        b[i] = value
+        buf_a[i + 1] = value * (1.0 / theta)
+        value = weighted(count[i, edge, :], came[i], phi[i + 1, edge, :])
+        b[i, edge, :] = value
+        buf_a[i + 1, edge, :] = value * (1.0 / theta)
         return carry
 
-    lax.fori_loop(0, planes, set_up, 0)
-    solve(rem, sol, (dir_a, dir_b), diag, fx, fy, fz)
-    dual = dir_a
-
-    def keep(i, carry):
-        dual[i + 1] = sol[i]
+    lax.fori_loop(0, planes, set_up, 0, unroll=2)
+    dual = solve(b, (buf_a, buf_b), diag, fx, fy, fz, 8)
+
+    def product(i, carry):
+        p, u = phi[i + 1], dual[i + 1]
+        grad = (p - phi[i]) * (u - dual[i]) + (p - phi[i + 2]) * (u - dual[i + 2])
+        both = p * u
+        for axis in range(2):
+            flow = (p - beyond(p, 1, axis)) * (u - beyond(u, 1, axis))
+            first = index_along(p.shape, axis) == 0
+            grad = grad + flow + jnp.where(first, both, shifted(flow, 1, axis))
+        grad_k[i] = -0.5 * grad
+        grad_a[i] = -both
+        for f, ref in enumerate((grad_k, grad_a)):
+            own[f, i] = ref[i, pl.ds(base + cy * c, cy), :]
+            message[f, i] = ref[i, pl.ds(base + cy * (1 - c), cy), :]
         return carry
 
-    lax.fori_loop(0, planes, keep, 0)
-
-    def product(i, carry):
-        p, u = pad[i + 1], dual[i + 1]
-        grad = (p - pad[i]) * (u - dual[i]) + (p - pad[i + 2]) * (u - dual[i + 2])
-        for axis in range(2):
-            for way in (1, -1):
-                grad = grad + (p - beyond(p, way, axis)) * (u - beyond(u, way, axis))
-        rem[i] = -0.5 * grad
-        sol[i] = -(p * u)
-        return carry
-
-    lax.fori_loop(0, planes, product, 0)
-    for f, ref in enumerate((rem, sol)):
-        own[f] = ref[:, pl.ds(base + cy * c, cy), :]
-        message[f] = ref[:, pl.ds(base + cy * (1 - c), cy), :]
+    lax.fori_loop(0, planes, product, 0, unroll=2)
 
 
 def core_kernel(own, came, kept, message):
@@ -466,7 +519,7 @@
             whole = sum(part[f, q] for part in parts[1:]) + parts[0][f, q]
             for j in range(n):
                 i = n * q + j
-                w[i] = whole[:, slab * j : slab * (j + 1)] - beta_prev[0] * q_ref[i]
+                w[i] = whole[:, slab * j : slab * (j + 1)] - beta_prev[...] * q_ref[i]
 
     def dot(a, b):
         return jnp.sum(jnp.sum(a * b, axis=0))
@@ -510,15 +563,19 @@
     return jax.ShapeDtypeStruct(shape, jnp.float32)
 
 
-def run(kernel, outs, *args, scratch=(), smem=(), mib=16, in_smem_out=(), cost=None):
+def run(kernel, outs, *args, scratch=(), copies=0, smem=(), hbm=(), mib=16, in_smem_out=(), cost=None):
     vmem = pl.BlockSpec(memory_space=pltpu.VMEM)
     scalar = pl.BlockSpec(memory_space=pltpu.SMEM)
+    far = pl.BlockSpec(memory_space=pltpu.HBM)
+    held = [pltpu.VMEM(shape, dtype) for shape, dtype in scratch]
+    if copies:
+        held.append(pltpu.SemaphoreType.DMA((copies,)))
     return pl.pallas_call(
         kernel,
         out_shape=tuple(outs),
-        in_specs=[scalar if i in smem else vmem for i in range(len(args))],
+        in_specs=[scalar if i in smem else far if i in hbm else vmem for i in range(len(args))],
         out_specs=tuple(scalar if i in in_smem_out else vmem for i in range(len(outs))),
-        scratch_shapes=[pltpu.VMEM(shape, jnp.float32) for shape in scratch],
+        scratch_shapes=held,
         compiler_params=pltpu.CompilerParams(vmem_limit_bytes=mib * 2**20),
         cost_estimate=cost,
     )(*args)
@@ -548,42 +605,58 @@
     def along_z(value, k):
         return lax.ppermute(value, "src", [(i, (i + k) % n) for i in range(n)])
 
+    block = (cx, cy, cz)
+    float_block = lambda *shape: (shape, jnp.float32)
+    raw_labels = (block, jnp.int32)
     packed, message = run(
-        pack_kernel, (f32(2, groups, cy, cz), f32(sources // 2 + 1, cx, cy, cz)),
-        background, labels, v_kappa, v_absorb,
-    )
-    other = swap_x(packed)
+        pack_kernel, (f32(2, groups, cy, cz), f32(sources // 2 + 1, *block)),
+        background, labels, v_kappa, v_absorb, hbm=(0, 1, 2, 3),
+        scratch=(raw_labels, float_block(2, *v_kappa.shape)), copies=4,
+    )
     came = swap_x(message)
-    own_v = [packed] + [along_z(packed, k) for k in range(1, n)]
-    other_v = [other] + [along_z(other, k) for k in range(1, n)]
+    slabs = [packed] + [along_z(packed, k) for k in range(1, n)]
     (count,) = run(
         functools.partial(count_kernel, ny=ny, nz=cz, half=2 * cy, halo=HALO),
         (f32(planes, rows, cz),), det_cells.reshape(1, dets),
         cost=pl.CostEstimate(flops=2 * planes * rows * cz * dets, bytes_accessed=planes * rows * cz * 4, transcendentals=0),
     )
+    (vector,) = run(unpack_kernel, (f32(2, *block),), *slabs)
+    vector_came = swap_x(vector)
+
+    def to_edges(edge_other, edge_mine):
+        return lax.ppermute(edge_other, "gy", [(1, 2), (2, 1)]), lax.ppermute(edge_mine, "gy", [(1, 3), (2, 0)])
+
     mine, fields, edge_other, edge_mine = run(
-        functools.partial(gather_kernel, n=n),
-        (f32(planes, cy, cz), f32(4, planes, cy, cz), f32(4, planes, HALO, cz), f32(4, planes, HALO, cz)),
-        background, labels, came, *own_v, *other_v,
-    )
-    edge_other = lax.ppermute(edge_other, "gy", [(1, 2), (2, 1)])
-    edge_mine = lax.ppermute(edge_mine, "gy", [(1, 3), (2, 0)])
+        photon_kernel,
+        (f32(planes, cy, cz), f32(2, planes, cy, cz), f32(2, planes, HALO, cz), f32(2, planes, HALO, cz)),
+        background, labels, came, hbm=(0, 1), scratch=(raw_labels,), copies=3,
+    )
+    edges = to_edges(edge_other, edge_mine)
     got = swap_core(fields)
-    frame = (planes, rows, cz)
-    wide = (planes + 2, rows, cz)
-    phi, change, diag, fx, fy, fz, sent = run(
-        first_kernel,
-        (f32(*frame), f32(*frame), f32(*frame), f32(planes + 1, rows, cz), f32(*frame), f32(*frame),
-         f32(planes + 4, HALO, cz)),
-        kappa_table, absorb_table, mine, fields, got, edge_other, edge_mine, count,
-        smem=(0, 1), scratch=(frame, wide, frame, wide, frame, wide, wide), mib=24,
+    frame, wide = (planes, rows, cz), (planes + 2, rows, cz)
+    float_frame, float_wide = float_block(*frame), float_block(*wide)
+    phi, diag, fx, fy, fz, sums = run(
+        stencil_kernel,
+        (f32(*wide), f32(*frame), f32(planes + 1, rows, cz), f32(*frame), f32(*frame), f32(2, 8, cz)),
+        kappa_table, absorb_table, mine, fields, got, *edges, count,
+        smem=(0, 1), scratch=(float_frame, float_wide),
+    )
+    fields, edge = run(
+        vector_kernel, (f32(2, planes, cy, cz), f32(2, planes, HALO, cz)), vector, vector_came
+    )
+    edges = to_edges(edge, edge)
+    got = swap_core(fields)
+    change, sent = run(
+        first_kernel, (f32(*frame), f32(planes + 4, HALO, cz)),
+        phi, diag, fx, fy, fz, count, sums, fields, got, *edges,
+        scratch=(float_wide, float_frame, float_frame, float_wide, float_wide),
     )
     heard = lax.ppermute(sent, "gy", [(i, (i + 2) % 4) for i in range(4)])
     own, message = run(
         functools.partial(second_kernel, dets=dets),
         (f32(2, planes, cy, cz), f32(2, planes, cy, cz)),
         phi, change, diag, fx, fy, fz, count, sent, heard,
-        scratch=(frame, frame, wide, wide, wide), mib=24,
+        scratch=(float_frame, float_wide, float_wide, float_frame, float_frame),
     )
     kept, message = run(
         core_kernel, (f32(2, cx, cy, cz), f32(2, cx, cy, cz)), own, swap_core(message)
@@ -595,7 +668,7 @@
     w_k, w_a, tile = run(
         functools.partial(project_kernel, n=n),
         (f32(*v_kappa.shape), f32(*v_kappa.shape), f32(8, 128)),
-        beta_prev, *parts, v_kappa, v_absorb, q_kappa, q_absorb, smem=(0,),
+        beta_prev.reshape(1, 1), *parts, v_kappa, v_absorb, q_kappa, q_absorb,
     )
     tile = tile + sum(along_z(tile, k) for k in range(1, n))
     over_x, over_core = swap_x(tile), swap_core(tile)

time: 95.7 us -> 90.5 us (0.946)
  starting transfers between devices: 33.9 us -> 27.8 us
  waiting for transfers between devices: 34.5 us -> 38.7 us
  Pallas kernels: 21.8 us -> 18.5 us
    ppermute x12 -> x9, starting transfers between devices: 19.5 us -> 13.4 us  [along_z(): return lax.ppermute(value, 'src', [(i, (i + k) % n) for i in range(n)])]
    pallas_call x9 -> x12, Pallas kernels: 21.8 us -> 18.5 us  [run(): pl.pallas_call(kernel, out_shape=tuple(outs), in_specs=[scalar if i in sm...]
    ppermute x4, waiting for transfers between devices: 12.8 us -> 15.1 us  [swap_x(): return lax.ppermute(value, 'gx', [(0, 1), (1, 0)])]
    ppermute x2 -> x4, starting transfers between devices: 1.97 us -> 3.92 us  [the longest x2 2.58 us: to_edges(): lax.ppermute(edge_mine, 'gy', [(1, 3), (2, 0)])]
    ppermute x12 -> x9, waiting for transfers between devices: 9.61 us -> 11.5 us  [along_z(): return lax.ppermute(value, 'src', [(i, (i + k) % n) for i in range(n)])]
    ppermute x3 -> x4, starting transfers between devices: 0.25 us -> 1.49 us  [swap_core(): return lax.ppermute(value, 'gy', [(0, 1), (1, 0), (2, 3), (3, 2)])]
    ppermute x1, starting transfers between devices: 4 us -> 2.76 us  [per_device_paired(): heard = lax.ppermute(sent, 'gy', [(i, (i + 2) % 4) for i in range(4)])]
    ppermute x4, starting transfers between devices: 6.13 us -> 4.95 us  [swap_x(): return lax.ppermute(value, 'gx', [(0, 1), (1, 0)])]
  transfers between devices with their start and end apart: 24 -> 24, of which waited for: 16 -> 15; matrix products, arithmetic and copies ran while one was open for 0% -> 0% of each run, Pallas kernels for 2% -> 7%
where the time goes in v2:
time: 90.5 us; the launch traced here: 90.2 us
  waiting for transfers between devices  38.7 us (43%)
  starting transfers between devices  27.8 us (31%)
  Pallas kernels  18.5 us (20%)
  local copies, waits for them, and re-layouts  3.78 us (4%)
  between operations  1.52 us (2%)
    pallas_call x12, Pallas kernels, run(): pl.pallas_call(kernel, out_shape=tuple(outs), in_specs=[scalar if i in sm...  18.5 us
    ppermute x4, waiting for transfers between devices, swap_x(): return lax.ppermute(value, 'gx', [(0, 1), (1, 0)])  15.1 us
    ppermute x9, starting transfers between devices, along_z(): return lax.ppermute(value, 'src', [(i, (i + k) % n) for i in range(n)])  13.4 us
    ppermute x9, waiting for transfers between devices, along_z(): return lax.ppermute(value, 'src', [(i, (i + k) % n) for i in range(n)])  11.5 us
    ppermute x4, starting transfers between devices, swap_x(): return lax.ppermute(value, 'gx', [(0, 1), (1, 0)])  4.95 us
    unnamed x24, local copies, waits for them, and re-layouts  3.78 us
    ppermute x2, waiting for transfers between devices, to_edges(): lax.ppermute(edge_mine, 'gy', [(1, 3), (2, 0)])  3.71 us
    ppermute x1, waiting for transfers between devices, per_device_paired(): heard = lax.ppermute(sent, 'gy', [(i, (i + 2) % 4) for i in range(4)])  3.28 us
  transfers between devices with their start and end apart: 24, of which 15 were waited for; matrix products, arithmetic and copies ran while one was open for 0% of the time, Pallas kernels for 7%

profile of v2, /device:TPU:0, one launch (start us, length us, event | category | flops | bytes accessed | tf_op | source)
XLA Modules:
  0.0 90.2 jit_solution(17870202983285276954)
XLA Ops:
  5.1 3.0 %collective-permute-start = (f32[3,8,32,128]{3,2,1,0:T(8,128)S(1)}, f32[3,8,32,128]{3,2,1,0:T(8,128)S(1)}, u32[]{:S(2)}, u32[]{:S(2)}) collective-permute-start(f32[3,8,32,128]{3,2,1,0:T(8,128)S(1)} %get-tuple-element.30), channel_id=1, source_target_pairs={{0,4},{4,0},{1,5},{5,1},{2,6},{6,2},{3,7},{7,3},{8,12},{12,8},{9,1... | collective-permute-start | bytes 1179656 | tf_op jit(solution)/shard_map/ppermute | solution.py:600
  8.1 1.6 %collective-permute-start.4 = (f32[2,2,32,128]{3,2,1,0:T(8,128)S(1)}, f32[2,2,32,128]{3,2,1,0:T(8,128)S(1)}, u32[]{:S(2)}, u32[]{:S(2)}) collective-permute-start(f32[2,2,32,128]{3,2,1,0:T(8,128)S(1)} %get-tuple-element.41.refs_0_), channel_id=1, source_target_pairs={{0,8},{8,16},{16,24},{24,0},{1,9},{9,17},{17,25},{25,1},{2,10},{10... | collective-permute-start | bytes 196616 | tf_op jit(solution)/shard_map/ppermute | solution.py:606
  9.7 2.6 %collective-permute-start.5 = (f32[2,2,32,128]{3,2,1,0:T(8,128)S(1)}, f32[2,2,32,128]{3,2,1,0:T(8,128)S(1)}, u32[]{:S(2)}, u32[]{:S(2)}) collective-permute-start(f32[2,2,32,128]{3,2,1,0:T(8,128)S(1)} %get-tuple-element.41.refs_0_), channel_id=1, source_target_pairs={{0,16},{8,24},{16,0},{24,8},{1,17},{9,25},{17,1},{25,9},{2,18},{10... | collective-permute-start | bytes 196616 | tf_op jit(solution)/shard_map/ppermute | solution.py:606
  12.3 1.3 %collective-permute-start.6 = (f32[2,2,32,128]{3,2,1,0:T(8,128)S(1)}, f32[2,2,32,128]{3,2,1,0:T(8,128)S(1)}, u32[]{:S(2)}, u32[]{:S(2)}) collective-permute-start(f32[2,2,32,128]{3,2,1,0:T(8,128)S(1)} %get-tuple-element.41.refs_0_), channel_id=1, source_target_pairs={{0,24},{8,0},{16,8},{24,16},{1,25},{9,1},{17,9},{25,17},{2,26},{10... | collective-permute-start | bytes 196616 | tf_op jit(solution)/shard_map/ppermute | solution.py:606
  13.6 1.3 %collective-permute-done.4.refs_1_ = f32[2,2,32,128]{3,2,1,0:T(8,128)S(1)} collective-permute-done((f32[2,2,32,128]{3,2,1,0:T(8,128)S(1)}, f32[2,2,32,128]{3,2,1,0:T(8,128)S(1)}, u32[]{:S(2)}, u32[]{:S(2)}) %collective-permute-start.4) | collective-permute-done | bytes 65568 | tf_op jit(solution)/shard_map/ppermute | solution.py:606
  15.0 2.1 %collective-permute-done.5.refs_2_ = f32[2,2,32,128]{3,2,1,0:T(8,128)S(1)} collective-permute-done((f32[2,2,32,128]{3,2,1,0:T(8,128)S(1)}, f32[2,2,32,128]{3,2,1,0:T(8,128)S(1)}, u32[]{:S(2)}, u32[]{:S(2)}) %collective-permute-start.5) | collective-permute-done | bytes 65568 | tf_op jit(solution)/shard_map/ppermute | solution.py:606
  18.5 5.5 %collective-permute-done.7.came = f32[2,8,32,128]{3,2,1,0:T(8,128)S(1)} collective-permute-done((f32[2,8,32,128]{3,2,1,0:T(8,128)S(1)}, f32[2,8,32,128]{3,2,1,0:T(8,128)S(1)}, u32[]{:S(2)}, u32[]{:S(2)}) %collective-permute-start.7) | collective-permute-done | bytes 262176 | tf_op jit(solution)/shard_map/ppermute | solution.py:600
  28.1 2.1 %shard_map.123.count = f32[16,72,128]{2,1,0:T(8,128)S(1)} custom-call(s32[1,1024]{1,0:T(1,128)S(1)} %bitcast.3), custom_call_target="tpu_custom_call" | custom-call | flops 301989888 | bytes 589824 | tf_op jit(solution)/shard_map/pallas_call | solution.py:573
  30.3 2.2 %collective-permute-done.3.edge_mine = f32[2,16,8,128]{3,2,1,0:T(8,128)S(1)} collective-permute-done((f32[2,16,8,128]{3,2,1,0:T(8,128)S(1)}, f32[2,16,8,128]{3,2,1,0:T(8,128)S(1)}, u32[]{:S(2)}, u32[]{:S(2)}) %collective-permute-start.3) | collective-permute-done | bytes 131104 | tf_op jit(solution)/shard_map/ppermute | solution.py:627
  32.5 2.9 %shard_map.124 = (f32[18,72,128]{2,1,0:T(8,128)S(1)}, f32[16,72,128]{2,1,0:T(8,128)S(1)}, f32[17,72,128]{2,1,0:T(8,128)S(1)}, f32[16,72,128]{2,1,0:T(8,128)S(1)}...) custom-call(f32[16]{0:T(128)S(1)} %copy-done.9, f32[16]{0:T(128)S(1)} %copy-done.10, ...), custom_call_target="tpu_custom_call" | custom-call | tf_op jit(solution)/shard_map/pallas_call | solution.py:573
  35.4 1.5 %collective-permute-done.10.edge_b = f32[2,16,8,128]{3,2,1,0:T(8,128)S(1)} collective-permute-done((f32[2,16,8,128]{3,2,1,0:T(8,128)S(1)}, f32[2,16,8,128]{3,2,1,0:T(8,128)S(1)}, u32[]{:S(2)}, u32[]{:S(2)}) %collective-permute-start.10) | collective-permute-done | bytes 131104 | tf_op jit(solution)/shard_map/ppermute | solution.py:627
  36.9 4.9 %shard_map.127 = (f32[16,72,128]{2,1,0:T(8,128)S(1)}, f32[20,8,128]{2,1,0:T(8,128)S(1)}) custom-call(f32[18,72,128]{2,1,0:T(8,128)S(1)} %get-tuple-element.35.phi, f32[16,72,128]{2,1,0:T(8,128)S(1)} %get-tuple-element.36.diag, f32[17,72,128]{2,1,0:T(8,128)S(1)} %get-tuple-element.37.fx, f32[16,72,128]{2,1,0:T(8,128)S(1)} %get-tuple-element.38.fy, ...), custom_call_target="tpu_custom_call" | custom-call | tf_op jit(solution)/shard_map/pallas_call | solution.py:573
  41.7 2.8 %collective-permute-start.11 = (f32[20,8,128]{2,1,0:T(8,128)S(1)}, f32[20,8,128]{2,1,0:T(8,128)S(1)}, u32[]{:S(2)}, u32[]{:S(2)}) collective-permute-start(f32[20,8,128]{2,1,0:T(8,128)S(1)} %get-tuple-element.45.sent), channel_id=1, source_target_pairs={{0,2},{1,3},{2,0},{3,1},{4,6},{5,7},{6,4},{7,5},{8,10},{9,11},{10,... | collective-permute-start | bytes 245768 | tf_op jit(solution)/shard_map/ppermute | solution.py:654
  44.5 3.3 %collective-permute-done.11.came = f32[20,8,128]{2,1,0:T(8,128)S(1)} collective-permute-done((f32[20,8,128]{2,1,0:T(8,128)S(1)}, f32[20,8,128]{2,1,0:T(8,128)S(1)}, u32[]{:S(2)}, u32[]{:S(2)}) %collective-permute-start.11) | collective-permute-done | bytes 81952 | tf_op jit(solution)/shard_map/ppermute | solution.py:654
  47.8 4.9 %shard_map.128 = (f32[2,16,32,128]{3,2,1,0:T(8,128)S(1)}, f32[2,16,32,128]{3,2,1,0:T(8,128)S(1)}) custom-call(f32[18,72,128]{2,1,0:T(8,128)S(1)} %get-tuple-element.35.phi, f32[16,72,128]{2,1,0:T(8,128)S(1)} %get-tuple-element.44.change, f32[16,72,128]{2,1,0:T(8,128)S(1)} %get-tuple-element.36.diag, f32[17,72,128]{2,1,0:T(8,128)S(1)} %get-tuple-element.37.fx, ...), custom_call_target="tpu_custom_call" | custom-call | tf_op jit(solution)/shard_map/pallas_call | solution.py:573
  52.8 1.8 %collective-permute-done.12.came = f32[2,16,32,128]{3,2,1,0:T(8,128)S(1)} collective-permute-done((f32[2,16,32,128]{3,2,1,0:T(8,128)S(1)}, f32[2,16,32,128]{3,2,1,0:T(8,128)S(1)}, u32[]{:S(2)}, u32[]{:S(2)}) %collective-permute-start.12) | collective-permute-done | bytes 524320 | tf_op jit(solution)/shard_map/ppermute | solution.py:603
  55.3 7.9 %collective-permute-done.13.came = f32[2,8,32,128]{3,2,1,0:T(8,128)S(1)} collective-permute-done((f32[2,8,32,128]{3,2,1,0:T(8,128)S(1)}, f32[2,8,32,128]{3,2,1,0:T(8,128)S(1)}, u32[]{:S(2)}, u32[]{:S(2)}) %collective-permute-start.13) | collective-permute-done | bytes 262176 | tf_op jit(solution)/shard_map/ppermute | solution.py:600
  63.5 2.3 %collective-permute-start.14 = (f32[2,2,32,128]{3,2,1,0:T(8,128)S(1)}, f32[2,2,32,128]{3,2,1,0:T(8,128)S(1)}, u32[]{:S(2)}, u32[]{:S(2)}) collective-permute-start(f32[2,2,32,128]{3,2,1,0:T(8,128)S(1)} %get-tuple-element.51), channel_id=1, source_target_pairs={{0,8},{8,16},{16,24},{24,0},{1,9},{9,17},{17,25},{25,1},{2,10},{10... | collective-permute-start | bytes 196616 | tf_op jit(solution)/shard_map/ppermute | solution.py:606
  66.8 1.5 %collective-permute-start.16 = (f32[2,2,32,128]{3,2,1,0:T(8,128)S(1)}, f32[2,2,32,128]{3,2,1,0:T(8,128)S(1)}, u32[]{:S(2)}, u32[]{:S(2)}) collective-permute-start(f32[2,2,32,128]{3,2,1,0:T(8,128)S(1)} %get-tuple-element.53), channel_id=1, source_target_pairs={{0,24},{8,0},{16,8},{24,16},{1,25},{9,1},{17,9},{25,17},{2,26},{10... | collective-permute-start | bytes 196616 | tf_op jit(solution)/shard_map/ppermute | solution.py:606
  69.7 2.5 %collective-permute-done.15.refs_3_ = f32[2,2,32,128]{3,2,1,0:T(8,128)S(1)} collective-permute-done((f32[2,2,32,128]{3,2,1,0:T(8,128)S(1)}, f32[2,2,32,128]{3,2,1,0:T(8,128)S(1)}, u32[]{:S(2)}, u32[]{:S(2)}) %collective-permute-start.15) | collective-permute-done | bytes 65568 | tf_op jit(solution)/shard_map/ppermute | solution.py:606
  72.9 2.5 %collective-permute-start.19 = (f32[8,128]{1,0:T(8,128)S(1)}, f32[8,128]{1,0:T(8,128)S(1)}, u32[]{:S(2)}, u32[]{:S(2)}) collective-permute-start(f32[8,128]{1,0:T(8,128)S(1)} %get-tuple-element.54), channel_id=1, source_target_pairs={{0,24},{8,0},{16,8},{24,16},{1,25},{9,1},{17,9},{25,17},{2,26},{10... | collective-permute-start | bytes 12296 | tf_op jit(solution)/shard_map/ppermute | solution.py:606
  76.7 4.1 %collective-permute-done.17 = f32[8,128]{1,0:T(8,128)S(1)} collective-permute-done((f32[8,128]{1,0:T(8,128)S(1)}, f32[8,128]{1,0:T(8,128)S(1)}, u32[]{:S(2)}, u32[]{:S(2)}) %collective-permute-start.17) | collective-permute-done | bytes 4128 | tf_op jit(solution)/shard_map/ppermute | solution.py:606
  83.9 1.7 %collective-permute-done.20 = f32[8,128]{1,0:T(8,128)S(1)} collective-permute-done((f32[8,128]{1,0:T(8,128)S(1)}, f32[8,128]{1,0:T(8,128)S(1)}, u32[]{:S(2)}, u32[]{:S(2)}) %collective-permute-start.20) | collective-permute-done | bytes 4128 | tf_op jit(solution)/shard_map/ppermute | solution.py:600
  86.8 2.4 %collective-permute-done.23.refs_1_ = f32[8,128]{1,0:T(8,128)S(1)} collective-permute-done((f32[8,128]{1,0:T(8,128)S(1)}, f32[8,128]{1,0:T(8,128)S(1)}, u32[]{:S(2)}, u32[]{:S(2)}) %collective-permute-start.23) | collective-permute-done | bytes 4128 | tf_op jit(solution)/shard_map/ppermute | solution.py:679
  (62 shorter events, 20.2 us)
Async XLA Ops:
  5.1 12.7 %collective-permute-start = (f32[3,8,32,128]{3,2,1,0:T(8,128)S(1)}, f32[3,8,32,128]{3,2,1,0:T(8,128)S(1)}, u32[]{:S(2)}, u32[]{:S(2)}) collective-permute-start(f32[3,8,32,128]{3,2,1,0:T(8,128)S(1)} %get-tuple-element.30), channel_id=1, source_target_pairs={{0,4},{4,0},{1,5},{5,1},{2,6},{6,2},{3,7},{7,3},{8,12},{12,8},{9,1... | collective-permute-start | bytes 1179656 | tf_op jit(solution)/shard_map/ppermute | solution.py:600
  8.1 6.9 %collective-permute-start.4 = (f32[2,2,32,128]{3,2,1,0:T(8,128)S(1)}, f32[2,2,32,128]{3,2,1,0:T(8,128)S(1)}, u32[]{:S(2)}, u32[]{:S(2)}) collective-permute-start(f32[2,2,32,128]{3,2,1,0:T(8,128)S(1)} %get-tuple-element.41.refs_0_), channel_id=1, source_target_pairs={{0,8},{8,16},{16,24},{24,0},{1,9},{9,17},{17,25},{25,1},{2,10},{10... | collective-permute-start | bytes 196616 | tf_op jit(solution)/shard_map/ppermute | solution.py:606
  9.7 7.3 %collective-permute-start.5 = (f32[2,2,32,128]{3,2,1,0:T(8,128)S(1)}, f32[2,2,32,128]{3,2,1,0:T(8,128)S(1)}, u32[]{:S(2)}, u32[]{:S(2)}) collective-permute-start(f32[2,2,32,128]{3,2,1,0:T(8,128)S(1)} %get-tuple-element.41.refs_0_), channel_id=1, source_target_pairs={{0,16},{8,24},{16,0},{24,8},{1,17},{9,25},{17,1},{25,9},{2,18},{10... | collective-permute-start | bytes 196616 | tf_op jit(solution)/shard_map/ppermute | solution.py:606
  12.3 4.8 %collective-permute-start.6 = (f32[2,2,32,128]{3,2,1,0:T(8,128)S(1)}, f32[2,2,32,128]{3,2,1,0:T(8,128)S(1)}, u32[]{:S(2)}, u32[]{:S(2)}) collective-permute-start(f32[2,2,32,128]{3,2,1,0:T(8,128)S(1)} %get-tuple-element.41.refs_0_), channel_id=1, source_target_pairs={{0,24},{8,0},{16,8},{24,16},{1,25},{9,1},{17,9},{25,17},{2,26},{10... | collective-permute-start | bytes 196616 | tf_op jit(solution)/shard_map/ppermute | solution.py:606
  17.4 6.6 %collective-permute-start.7 = (f32[2,8,32,128]{3,2,1,0:T(8,128)S(1)}, f32[2,8,32,128]{3,2,1,0:T(8,128)S(1)}, u32[]{:S(2)}, u32[]{:S(2)}) collective-permute-start(f32[2,8,32,128]{3,2,1,0:T(8,128)S(1)} %shard_map.125.own), channel_id=1, source_target_pairs={{0,4},{4,0},{1,5},{5,1},{2,6},{6,2},{3,7},{7,3},{8,12},{12,8},{9,1... | collective-permute-start | bytes 786440 | tf_op jit(solution)/shard_map/ppermute | solution.py:600
  18.5 14.1 %collective-permute-start.1 = (f32[2,16,32,128]{3,2,1,0:T(8,128)S(1)}, f32[2,16,32,128]{3,2,1,0:T(8,128)S(1)}, u32[]{:S(2)}, u32[]{:S(2)}) collective-permute-start(f32[2,16,32,128]{3,2,1,0:T(8,128)S(1)} %get-tuple-element.32.fields), channel_id=1, source_target_pairs={{0,1},{1,0},{2,3},{3,2},{4,5},{5,4},{6,7},{7,6},{8,9},{9,8},{10,11... | collective-permute-start | bytes 1572872 | tf_op jit(solution)/shard_map/ppermute | solution.py:603
  24.1 12.8 %collective-permute-start.8 = (f32[2,16,32,128]{3,2,1,0:T(8,128)S(1)}, f32[2,16,32,128]{3,2,1,0:T(8,128)S(1)}, u32[]{:S(2)}, u32[]{:S(2)}) collective-permute-start(f32[2,16,32,128]{3,2,1,0:T(8,128)S(1)} %get-tuple-element.42.fields), channel_id=1, source_target_pairs={{0,1},{1,0},{2,3},{3,2},{4,5},{5,4},{6,7},{7,6},{8,9},{9,8},{10,11... | collective-permute-start | bytes 1572872 | tf_op jit(solution)/shard_map/ppermute | solution.py:603
  24.2 2.7 %collective-permute-start.2 = (f32[2,16,8,128]{3,2,1,0:T(8,128)S(1)}, f32[2,16,8,128]{3,2,1,0:T(8,128)S(1)}, u32[]{:S(2)}, u32[]{:S(2)}) collective-permute-start(f32[2,16,8,128]{3,2,1,0:T(8,128)S(1)} %get-tuple-element.33), channel_id=1, source_target_pairs={{1,2},{2,1},{5,6},{6,5},{9,10},{10,9},{13,14},{14,13},{17,18},{18,... | collective-permute-start | bytes 393224 | tf_op jit(solution)/shard_map/ppermute | solution.py:627
  24.8 7.7 %collective-permute-start.3 = (f32[2,16,8,128]{3,2,1,0:T(8,128)S(1)}, f32[2,16,8,128]{3,2,1,0:T(8,128)S(1)}, u32[]{:S(2)}, u32[]{:S(2)}) collective-permute-start(f32[2,16,8,128]{3,2,1,0:T(8,128)S(1)} %get-tuple-element.34), channel_id=1, source_target_pairs={{1,3},{2,0},{5,7},{6,4},{9,11},{10,8},{13,15},{14,12},{17,19},{18,... | collective-permute-start | bytes 393224 | tf_op jit(solution)/shard_map/ppermute | solution.py:627
  26.1 9.3 %collective-permute-start.9 = (f32[2,16,8,128]{3,2,1,0:T(8,128)S(1)}, f32[2,16,8,128]{3,2,1,0:T(8,128)S(1)}, u32[]{:S(2)}, u32[]{:S(2)}) collective-permute-start(f32[2,16,8,128]{3,2,1,0:T(8,128)S(1)} %get-tuple-element.43), channel_id=1, source_target_pairs={{1,2},{2,1},{5,6},{6,5},{9,10},{10,9},{13,14},{14,13},{17,18},{18,... | collective-permute-start | bytes 393224 | tf_op jit(solution)/shard_map/ppermute | solution.py:627
  26.8 10.1 %collective-permute-start.10 = (f32[2,16,8,128]{3,2,1,0:T(8,128)S(1)}, f32[2,16,8,128]{3,2,1,0:T(8,128)S(1)}, u32[]{:S(2)}, u32[]{:S(2)}) collective-permute-start(f32[2,16,8,128]{3,2,1,0:T(8,128)S(1)} %get-tuple-element.43), channel_id=1, source_target_pairs={{1,3},{2,0},{5,7},{6,4},{9,11},{10,8},{13,15},{14,12},{17,19},{18,... | collective-permute-start | bytes 393224 | tf_op jit(solution)/shard_map/ppermute | solution.py:627
  41.7 6.0 %collective-permute-start.11 = (f32[20,8,128]{2,1,0:T(8,128)S(1)}, f32[20,8,128]{2,1,0:T(8,128)S(1)}, u32[]{:S(2)}, u32[]{:S(2)}) collective-permute-start(f32[20,8,128]{2,1,0:T(8,128)S(1)} %get-tuple-element.45.sent), channel_id=1, source_target_pairs={{0,2},{1,3},{2,0},{3,1},{4,6},{5,7},{6,4},{7,5},{8,10},{9,11},{10,... | collective-permute-start | bytes 245768 | tf_op jit(solution)/shard_map/ppermute | solution.py:654
  52.7 2.0 %collective-permute-start.12 = (f32[2,16,32,128]{3,2,1,0:T(8,128)S(1)}, f32[2,16,32,128]{3,2,1,0:T(8,128)S(1)}, u32[]{:S(2)}, u32[]{:S(2)}) collective-permute-start(f32[2,16,32,128]{3,2,1,0:T(8,128)S(1)} %get-tuple-element.47), channel_id=1, source_target_pairs={{0,1},{1,0},{2,3},{3,2},{4,5},{5,4},{6,7},{7,6},{8,9},{9,8},{10,11... | collective-permute-start | bytes 1572872 | tf_op jit(solution)/shard_map/ppermute | solution.py:603
  54.7 8.4 %collective-permute-start.13 = (f32[2,8,32,128]{3,2,1,0:T(8,128)S(1)}, f32[2,8,32,128]{3,2,1,0:T(8,128)S(1)}, u32[]{:S(2)}, u32[]{:S(2)}) collective-permute-start(f32[2,8,32,128]{3,2,1,0:T(8,128)S(1)} %get-tuple-element.49), channel_id=1, source_target_pairs={{0,4},{4,0},{1,5},{5,1},{2,6},{6,2},{3,7},{7,3},{8,12},{12,8},{9,1... | collective-permute-start | bytes 786440 | tf_op jit(solution)/shard_map/ppermute | solution.py:600
  63.5 6.2 %collective-permute-start.14 = (f32[2,2,32,128]{3,2,1,0:T(8,128)S(1)}, f32[2,2,32,128]{3,2,1,0:T(8,128)S(1)}, u32[]{:S(2)}, u32[]{:S(2)}) collective-permute-start(f32[2,2,32,128]{3,2,1,0:T(8,128)S(1)} %get-tuple-element.51), channel_id=1, source_target_pairs={{0,8},{8,16},{16,24},{24,0},{1,9},{9,17},{17,25},{25,1},{2,10},{10... | collective-permute-start | bytes 196616 | tf_op jit(solution)/shard_map/ppermute | solution.py:606
  65.8 6.4 %collective-permute-start.15 = (f32[2,2,32,128]{3,2,1,0:T(8,128)S(1)}, f32[2,2,32,128]{3,2,1,0:T(8,128)S(1)}, u32[]{:S(2)}, u32[]{:S(2)}) collective-permute-start(f32[2,2,32,128]{3,2,1,0:T(8,128)S(1)} %get-tuple-element.52), channel_id=1, source_target_pairs={{0,16},{8,24},{16,0},{24,8},{1,17},{9,25},{17,1},{25,9},{2,18},{10... | collective-permute-start | bytes 196616 | tf_op jit(solution)/shard_map/ppermute | solution.py:606
  66.8 5.4 %collective-permute-start.16 = (f32[2,2,32,128]{3,2,1,0:T(8,128)S(1)}, f32[2,2,32,128]{3,2,1,0:T(8,128)S(1)}, u32[]{:S(2)}, u32[]{:S(2)}) collective-permute-start(f32[2,2,32,128]{3,2,1,0:T(8,128)S(1)} %get-tuple-element.53), channel_id=1, source_target_pairs={{0,24},{8,0},{16,8},{24,16},{1,25},{9,1},{17,9},{25,17},{2,26},{10... | collective-permute-start | bytes 196616 | tf_op jit(solution)/shard_map/ppermute | solution.py:606
  72.9 3.8 %collective-permute-start.19 = (f32[8,128]{1,0:T(8,128)S(1)}, f32[8,128]{1,0:T(8,128)S(1)}, u32[]{:S(2)}, u32[]{:S(2)}) collective-permute-start(f32[8,128]{1,0:T(8,128)S(1)} %get-tuple-element.54), channel_id=1, source_target_pairs={{0,24},{8,0},{16,8},{24,16},{1,25},{9,1},{17,9},{25,17},{2,26},{10... | collective-permute-start | bytes 12296 | tf_op jit(solution)/shard_map/ppermute | solution.py:606
  75.4 5.4 %collective-permute-start.17 = (f32[8,128]{1,0:T(8,128)S(1)}, f32[8,128]{1,0:T(8,128)S(1)}, u32[]{:S(2)}, u32[]{:S(2)}) collective-permute-start(f32[8,128]{1,0:T(8,128)S(1)} %get-tuple-element.54), channel_id=1, source_target_pairs={{0,8},{8,16},{16,24},{24,0},{1,9},{9,17},{17,25},{25,1},{2,10},{10... | collective-permute-start | bytes 12296 | tf_op jit(solution)/shard_map/ppermute | solution.py:606
  75.4 5.4 %collective-permute-start.18 = (f32[8,128]{1,0:T(8,128)S(1)}, f32[8,128]{1,0:T(8,128)S(1)}, u32[]{:S(2)}, u32[]{:S(2)}) collective-permute-start(f32[8,128]{1,0:T(8,128)S(1)} %get-tuple-element.54), channel_id=1, source_target_pairs={{0,16},{8,24},{16,0},{24,8},{1,17},{9,25},{17,1},{25,9},{2,18},{10... | collective-permute-start | bytes 12296 | tf_op jit(solution)/shard_map/ppermute | solution.py:606
  80.8 3.1 %collective-permute-start.22 = (f32[8,128]{1,0:T(8,128)S(1)}, f32[8,128]{1,0:T(8,128)S(1)}, u32[]{:S(2)}, u32[]{:S(2)}) collective-permute-start(f32[8,128]{1,0:T(8,128)S(1)} %add_add_fusion.1), channel_id=1, source_target_pairs={{0,5},{1,4},{2,7},{3,6},{4,1},{5,0},{6,3},{7,2},{8,13},{9,12},{10,... | collective-permute-start | bytes 12296 | tf_op jit(solution)/shard_map/ppermute | solution.py:675
  80.9 3.0 %collective-permute-start.21 = (f32[8,128]{1,0:T(8,128)S(1)}, f32[8,128]{1,0:T(8,128)S(1)}, u32[]{:S(2)}, u32[]{:S(2)}) collective-permute-start(f32[8,128]{1,0:T(8,128)S(1)} %add_add_fusion.1), channel_id=1, source_target_pairs={{0,1},{1,0},{2,3},{3,2},{4,5},{5,4},{6,7},{7,6},{8,9},{9,8},{10,11... | collective-permute-start | bytes 12296 | tf_op jit(solution)/shard_map/ppermute | solution.py:603
  82.0 3.6 %collective-permute-start.20 = (f32[8,128]{1,0:T(8,128)S(1)}, f32[8,128]{1,0:T(8,128)S(1)}, u32[]{:S(2)}, u32[]{:S(2)}) collective-permute-start(f32[8,128]{1,0:T(8,128)S(1)} %add_add_fusion.1), channel_id=1, source_target_pairs={{0,4},{4,0},{1,5},{5,1},{2,6},{6,2},{3,7},{7,3},{8,12},{12,8},{9,1... | collective-permute-start | bytes 12296 | tf_op jit(solution)/shard_map/ppermute | solution.py:600
  85.6 3.6 %collective-permute-start.23 = (f32[8,128]{1,0:T(8,128)S(1)}, f32[8,128]{1,0:T(8,128)S(1)}, u32[]{:S(2)}, u32[]{:S(2)}) collective-permute-start(f32[8,128]{1,0:T(8,128)S(1)} %add_add_fusion.refs_0_), channel_id=1, source_target_pairs={{0,2},{1,3},{2,0},{3,1},{4,6},{5,7},{6,4},{7,5},{8,10},{9,11},{10,... | collective-permute-start | bytes 12296 | tf_op jit(solution)/shard_map/ppermute | solution.py:679
  (12 other events, 62.3 us)

commit v3 on v2

--- a/solution.py
+++ b/solution.py
@@ -260,9 +260,8 @@
     edge_mine[1] = fields[1, :, pl.ds(first, halo), :]
 
 
-def unpack_kernel(*refs):
-    parts, full = refs[:-1], refs[-1]
-    n = len(parts)
+def unpack_kernel(*refs, n):
+    own, parts, full = refs[:2], refs[2 : n + 1], refs[-1]
     s, _, _, _ = places(2)
     slab = 128 // n
     _, cx, cy, _ = full.shape
@@ -271,10 +270,10 @@
         for q in range(cx // n):
             blocks = [part[f, q] for part in parts]
             for j in range(n):
-                plane = jnp.zeros((cy, 128), jnp.float32)
-                for k in range(n):
+                plane = jnp.concatenate([own[f][n * q + j]] * n, axis=1)
+                for k in range(1, n):
                     home = (s - k + n) % n
-                    moved = pltpu.roll(blocks[k], ((home - j + n) % n) * slab, 1)
+                    moved = pltpu.roll(blocks[k - 1], ((home - j + n) % n) * slab, 1)
                     plane = jnp.where(lane == home, moved, plane)
                 full[f, n * q + j] = plane
 
@@ -563,15 +562,21 @@
     return jax.ShapeDtypeStruct(shape, jnp.float32)
 
 
-def run(kernel, outs, *args, scratch=(), copies=0, smem=(), hbm=(), mib=16, in_smem_out=(), cost=None):
+def run(kernel, outs, *args, after=(), scratch=(), copies=0, smem=(), hbm=(), mib=16, in_smem_out=(), cost=None):
     vmem = pl.BlockSpec(memory_space=pltpu.VMEM)
     scalar = pl.BlockSpec(memory_space=pltpu.SMEM)
     far = pl.BlockSpec(memory_space=pltpu.HBM)
     held = [pltpu.VMEM(shape, dtype) for shape, dtype in scratch]
+    used, waits = len(args), len(after)
+
+    def body(*refs):
+        kernel(*refs[:used], *refs[used + waits :])
+
+    args = (*args, *after)
     if copies:
         held.append(pltpu.SemaphoreType.DMA((copies,)))
     return pl.pallas_call(
-        kernel,
+        body if waits else kernel,
         out_shape=tuple(outs),
         in_specs=[scalar if i in smem else far if i in hbm else vmem for i in range(len(args))],
         out_specs=tuple(scalar if i in in_smem_out else vmem for i in range(len(outs))),
@@ -611,16 +616,18 @@
     packed, message = run(
         pack_kernel, (f32(2, groups, cy, cz), f32(sources // 2 + 1, *block)),
         background, labels, v_kappa, v_absorb, hbm=(0, 1, 2, 3),
-        scratch=(raw_labels, float_block(2, *v_kappa.shape)), copies=4,
+        scratch=(raw_labels, float_block(2, *v_kappa.shape)), copies=4, mib=60,
     )
     came = swap_x(message)
-    slabs = [packed] + [along_z(packed, k) for k in range(1, n)]
+    slabs = [along_z(packed, k) for k in range(1, n)]
     (count,) = run(
         functools.partial(count_kernel, ny=ny, nz=cz, half=2 * cy, halo=HALO),
         (f32(planes, rows, cz),), det_cells.reshape(1, dets),
         cost=pl.CostEstimate(flops=2 * planes * rows * cz * dets, bytes_accessed=planes * rows * cz * 4, transcendentals=0),
     )
-    (vector,) = run(unpack_kernel, (f32(2, *block),), *slabs)
+    (vector,) = run(
+        functools.partial(unpack_kernel, n=n), (f32(2, *block),), v_kappa, v_absorb, *slabs, after=(count,)
+    )
     vector_came = swap_x(vector)
 
     def to_edges(edge_other, edge_mine):
@@ -629,7 +636,7 @@
     mine, fields, edge_other, edge_mine = run(
         photon_kernel,
         (f32(planes, cy, cz), f32(2, planes, cy, cz), f32(2, planes, HALO, cz), f32(2, planes, HALO, cz)),
-        background, labels, came, hbm=(0, 1), scratch=(raw_labels,), copies=3,
+        background, labels, came, after=(vector,), hbm=(0, 1), scratch=(raw_labels,), copies=3,
     )
     edges = to_edges(edge_other, edge_mine)
     got = swap_core(fields)
@@ -642,7 +649,8 @@
         smem=(0, 1), scratch=(float_frame, float_wide),
     )
     fields, edge = run(
-        vector_kernel, (f32(2, planes, cy, cz), f32(2, planes, HALO, cz)), vector, vector_came
+        vector_kernel, (f32(2, planes, cy, cz), f32(2, planes, HALO, cz)), vector, vector_came,
+        after=(got, *edges),
     )
     edges = to_edges(edge, edge)
     got = swap_core(fields)

time: 90.5 us -> 84.7 us (0.936)
  waiting for transfers between devices: 38.7 us -> 32.3 us
  local copies, waits for them, and re-layouts: 3.78 us -> 0.05 us
  starting transfers between devices: 27.8 us -> 30.9 us
  Pallas kernels: 18.5 us -> 19.8 us
    ppermute x9, waiting for transfers between devices: 11.5 us -> 7.23 us  [along_z(): return lax.ppermute(value, 'src', [(i, (i + k) % n) for i in range(n)])]
    unnamed x24 -> x18, local copies, waits for them, and re-layouts: 3.78 us -> 0.05 us
    ppermute x9, starting transfers between devices: 13.4 us -> 15.1 us  [along_z(): return lax.ppermute(value, 'src', [(i, (i + k) % n) for i in range(n)])]
    ppermute x1, starting transfers between devices: 0.07 us -> 1.71 us  [per_device_paired(): lax.ppermute(tile, ('gx', 'gy'), [(4 * a + b, 4 * (1 - a) + (b ^ 1)) for...]
    pallas_call x12, Pallas kernels: 18.5 us -> 19.8 us  [run(): pl.pallas_call(body if waits else kernel, out_shape=tuple(outs), in_specs...]
    ppermute x4, starting transfers between devices: 1.49 us -> 0.33 us  [swap_core(): return lax.ppermute(value, 'gy', [(0, 1), (1, 0), (2, 3), (3, 2)])]
    ppermute x2, waiting for transfers between devices: 3.71 us -> 2.73 us  [to_edges(): lax.ppermute(edge_mine, 'gy', [(1, 3), (2, 0)])]
  transfers between devices with their start and end apart: 24 -> 24, of which waited for: 15 -> 14; matrix products, arithmetic and copies ran while one was open for 0% -> 0% of each run, Pallas kernels for 7% -> 6%
where the time goes in v3:
time: 84.7 us; the launch traced here: 84.5 us
  waiting for transfers between devices  32.3 us (38%)
  starting transfers between devices  30.9 us (36%)
  Pallas kernels  19.8 us (23%)
  between operations  1.52 us (2%)
    pallas_call x12, Pallas kernels, run(): pl.pallas_call(body if waits else kernel, out_shape=tuple(outs), in_specs...  19.8 us
    ppermute x9, starting transfers between devices, along_z(): return lax.ppermute(value, 'src', [(i, (i + k) % n) for i in range(n)])  15.1 us
    ppermute x4, waiting for transfers between devices, swap_x(): return lax.ppermute(value, 'gx', [(0, 1), (1, 0)])  14.9 us
    ppermute x9, waiting for transfers between devices, along_z(): return lax.ppermute(value, 'src', [(i, (i + k) % n) for i in range(n)])  7.23 us
    ppermute x4, starting transfers between devices, swap_x(): return lax.ppermute(value, 'gx', [(0, 1), (1, 0)])  5.18 us
    ppermute x1, starting transfers between devices, per_device_paired(): heard = lax.ppermute(sent, 'gy', [(i, (i + 2) % 4) for i in range(4)])  3.43 us
    ppermute x1, waiting for transfers between devices, per_device_paired(): heard = lax.ppermute(sent, 'gy', [(i, (i + 2) % 4) for i in range(4)])  3.18 us
    ppermute x2, waiting for transfers between devices, to_edges(): lax.ppermute(edge_mine, 'gy', [(1, 3), (2, 0)])  2.73 us
  transfers between devices with their start and end apart: 24, of which 14 were waited for; matrix products, arithmetic and copies ran while one was open for 0% of the time, Pallas kernels for 6%

profile of v3, /device:TPU:0, one launch (start us, length us, event | category | flops | bytes accessed | tf_op | source)
XLA Modules:
  0.0 84.5 jit_solution(14546290252171771022)
XLA Ops:
  0.6 1.9 %shard_map.121 = (f32[2,2,32,128]{3,2,1,0:T(8,128)}, f32[3,8,32,128]{3,2,1,0:T(8,128)}) custom-call(f32[4,8,32,128]{3,2,1,0:T(8,128)} %refs_0_.3, s32[8,32,128]{2,1,0:T(8,128)} %refs_1_.3, f32[8,32,32]{2,1,0:T(8,128)} %refs_4_.1, f32[8,32,32]{2,1,0:T(8,128)} %refs_5_.3), custom_call_target="tpu_custom_call" | custom-call | tf_op jit(solution)/shard_map/pallas_call | solution.py:578
  2.6 3.0 %collective-permute-start = (f32[3,8,32,128]{3,2,1,0:T(8,128)}, f32[3,8,32,128]{3,2,1,0:T(8,128)S(1)}, u32[]{:S(2)}, u32[]{:S(2)}) collective-permute-start(f32[3,8,32,128]{3,2,1,0:T(8,128)} %get-tuple-element.30), channel_id=1, source_target_pairs={{0,4},{4,0},{1,5},{5,1},{2,6},{6,2},{3,7},{7,3},{8,12},{12,8},{9,1... | collective-permute-start | bytes 1179656 | tf_op jit(solution)/shard_map/ppermute | solution.py:605
  5.6 1.6 %collective-permute-start.1 = (f32[2,2,32,128]{3,2,1,0:T(8,128)}, f32[2,2,32,128]{3,2,1,0:T(8,128)S(1)}, u32[]{:S(2)}, u32[]{:S(2)}) collective-permute-start(f32[2,2,32,128]{3,2,1,0:T(8,128)} %get-tuple-element.31), channel_id=1, source_target_pairs={{0,8},{8,16},{16,24},{24,0},{1,9},{9,17},{17,25},{25,1},{2,10},{10... | collective-permute-start | bytes 196616 | tf_op jit(solution)/shard_map/ppermute | solution.py:611
  7.2 2.6 %collective-permute-start.2 = (f32[2,2,32,128]{3,2,1,0:T(8,128)}, f32[2,2,32,128]{3,2,1,0:T(8,128)S(1)}, u32[]{:S(2)}, u32[]{:S(2)}) collective-permute-start(f32[2,2,32,128]{3,2,1,0:T(8,128)} %get-tuple-element.31), channel_id=1, source_target_pairs={{0,16},{8,24},{16,0},{24,8},{1,17},{9,25},{17,1},{25,9},{2,18},{10... | collective-permute-start | bytes 196616 | tf_op jit(solution)/shard_map/ppermute | solution.py:611
  11.1 2.1 %shard_map.122.refs_5_.count = f32[16,72,128]{2,1,0:T(8,128)S(1)} custom-call(s32[1,1024]{1,0:T(1,128)S(1)} %bitcast.3), custom_call_target="tpu_custom_call" | custom-call | flops 301989888 | bytes 589824 | tf_op jit(solution)/shard_map/pallas_call | solution.py:578
  13.2 1.5 %collective-permute-done.2.refs_3_ = f32[2,2,32,128]{3,2,1,0:T(8,128)S(1)} collective-permute-done((f32[2,2,32,128]{3,2,1,0:T(8,128)}, f32[2,2,32,128]{3,2,1,0:T(8,128)S(1)}, u32[]{:S(2)}, u32[]{:S(2)}) %collective-permute-start.2) | collective-permute-done | bytes 65568 | tf_op jit(solution)/shard_map/ppermute | solution.py:611
  16.0 1.5 %collective-permute-start.7 = (f32[2,8,32,128]{3,2,1,0:T(8,128)S(1)}, f32[2,8,32,128]{3,2,1,0:T(8,128)S(1)}, u32[]{:S(2)}, u32[]{:S(2)}) collective-permute-start(f32[2,8,32,128]{3,2,1,0:T(8,128)S(1)} %shard_map.123.refs_3_.refs_0_), channel_id=1, source_target_pairs={{0,4},{4,0},{1,5},{5,1},{2,6},{6,2},{3,7},{7,3},{8,12},{12,8},{9,1... | collective-permute-start | bytes 786440 | tf_op jit(solution)/shard_map/ppermute | solution.py:605
  19.4 5.3 %collective-permute-done.7.refs_1_ = f32[2,8,32,128]{3,2,1,0:T(8,128)S(1)} collective-permute-done((f32[2,8,32,128]{3,2,1,0:T(8,128)S(1)}, f32[2,8,32,128]{3,2,1,0:T(8,128)S(1)}, u32[]{:S(2)}, u32[]{:S(2)}) %collective-permute-start.7) | collective-permute-done | bytes 262176 | tf_op jit(solution)/shard_map/ppermute | solution.py:605
  27.6 2.9 %shard_map.125 = (f32[18,72,128]{2,1,0:T(8,128)S(1)}, f32[16,72,128]{2,1,0:T(8,128)S(1)}, f32[17,72,128]{2,1,0:T(8,128)S(1)}, f32[16,72,128]{2,1,0:T(8,128)S(1)}...) custom-call(f32[16]{0:T(128)S(1)} %copy-done.6, f32[16]{0:T(128)S(1)} %copy-done.7, ...), custom_call_target="tpu_custom_call" | custom-call | tf_op jit(solution)/shard_map/pallas_call | solution.py:578
  30.5 2.0 %collective-permute-done.10.edge_b = f32[2,16,8,128]{3,2,1,0:T(8,128)S(1)} collective-permute-done((f32[2,16,8,128]{3,2,1,0:T(8,128)S(1)}, f32[2,16,8,128]{3,2,1,0:T(8,128)S(1)}, u32[]{:S(2)}, u32[]{:S(2)}) %collective-permute-start.10) | collective-permute-done | bytes 131104 | tf_op jit(solution)/shard_map/ppermute | solution.py:634
  32.5 4.9 %shard_map.127 = (f32[16,72,128]{2,1,0:T(8,128)S(1)}, f32[20,8,128]{2,1,0:T(8,128)S(1)}) custom-call(f32[18,72,128]{2,1,0:T(8,128)S(1)} %get-tuple-element.36.phi, f32[16,72,128]{2,1,0:T(8,128)S(1)} %get-tuple-element.37.diag, f32[17,72,128]{2,1,0:T(8,128)S(1)} %get-tuple-element.38.fx, f32[16,72,128]{2,1,0:T(8,128)S(1)} %get-tuple-element.39.fy, ...), custom_call_target="tpu_custom_call" | custom-call | tf_op jit(solution)/shard_map/pallas_call | solution.py:578
  37.3 3.4 %collective-permute-start.11 = (f32[20,8,128]{2,1,0:T(8,128)S(1)}, f32[20,8,128]{2,1,0:T(8,128)S(1)}, u32[]{:S(2)}, u32[]{:S(2)}) collective-permute-start(f32[20,8,128]{2,1,0:T(8,128)S(1)} %get-tuple-element.45.sent), channel_id=1, source_target_pairs={{0,2},{1,3},{2,0},{3,1},{4,6},{5,7},{6,4},{7,5},{8,10},{9,11},{10,... | collective-permute-start | bytes 245768 | tf_op jit(solution)/shard_map/ppermute | solution.py:662
  40.8 3.2 %collective-permute-done.11.came = f32[20,8,128]{2,1,0:T(8,128)S(1)} collective-permute-done((f32[20,8,128]{2,1,0:T(8,128)S(1)}, f32[20,8,128]{2,1,0:T(8,128)S(1)}, u32[]{:S(2)}, u32[]{:S(2)}) %collective-permute-start.11) | collective-permute-done | bytes 81952 | tf_op jit(solution)/shard_map/ppermute | solution.py:662
  43.9 4.9 %shard_map.128 = (f32[2,16,32,128]{3,2,1,0:T(8,128)S(1)}, f32[2,16,32,128]{3,2,1,0:T(8,128)S(1)}) custom-call(f32[18,72,128]{2,1,0:T(8,128)S(1)} %get-tuple-element.36.phi, f32[16,72,128]{2,1,0:T(8,128)S(1)} %get-tuple-element.44.change, f32[16,72,128]{2,1,0:T(8,128)S(1)} %get-tuple-element.37.diag, f32[17,72,128]{2,1,0:T(8,128)S(1)} %get-tuple-element.38.fx, ...), custom_call_target="tpu_custom_call" | custom-call | tf_op jit(solution)/shard_map/pallas_call | solution.py:578
  49.0 1.8 %collective-permute-done.12.came = f32[2,16,32,128]{3,2,1,0:T(8,128)S(1)} collective-permute-done((f32[2,16,32,128]{3,2,1,0:T(8,128)S(1)}, f32[2,16,32,128]{3,2,1,0:T(8,128)S(1)}, u32[]{:S(2)}, u32[]{:S(2)}) %collective-permute-start.12) | collective-permute-done | bytes 524320 | tf_op jit(solution)/shard_map/ppermute | solution.py:608
  51.2 8.1 %collective-permute-done.13.came = f32[2,8,32,128]{3,2,1,0:T(8,128)S(1)} collective-permute-done((f32[2,8,32,128]{3,2,1,0:T(8,128)S(1)}, f32[2,8,32,128]{3,2,1,0:T(8,128)S(1)}, u32[]{:S(2)}, u32[]{:S(2)}) %collective-permute-start.13) | collective-permute-done | bytes 262176 | tf_op jit(solution)/shard_map/ppermute | solution.py:605
  59.6 1.7 %collective-permute-start.14 = (f32[2,2,32,128]{3,2,1,0:T(8,128)S(1)}, f32[2,2,32,128]{3,2,1,0:T(8,128)S(1)}, u32[]{:S(2)}, u32[]{:S(2)}) collective-permute-start(f32[2,2,32,128]{3,2,1,0:T(8,128)S(1)} %get-tuple-element.51), channel_id=1, source_target_pairs={{0,8},{8,16},{16,24},{24,0},{1,9},{9,17},{17,25},{25,1},{2,10},{10... | collective-permute-start | bytes 196616 | tf_op jit(solution)/shard_map/ppermute | solution.py:611
  61.4 2.6 %collective-permute-start.15 = (f32[2,2,32,128]{3,2,1,0:T(8,128)S(1)}, f32[2,2,32,128]{3,2,1,0:T(8,128)S(1)}, u32[]{:S(2)}, u32[]{:S(2)}) collective-permute-start(f32[2,2,32,128]{3,2,1,0:T(8,128)S(1)} %get-tuple-element.52), channel_id=1, source_target_pairs={{0,16},{8,24},{16,0},{24,8},{1,17},{9,25},{17,1},{25,9},{2,18},{10... | collective-permute-start | bytes 196616 | tf_op jit(solution)/shard_map/ppermute | solution.py:611
  66.5 2.0 %collective-permute-done.15.refs_3_ = f32[2,2,32,128]{3,2,1,0:T(8,128)S(1)} collective-permute-done((f32[2,2,32,128]{3,2,1,0:T(8,128)S(1)}, f32[2,2,32,128]{3,2,1,0:T(8,128)S(1)}, u32[]{:S(2)}, u32[]{:S(2)}) %collective-permute-start.15) | collective-permute-done | bytes 65568 | tf_op jit(solution)/shard_map/ppermute | solution.py:611
  70.4 2.2 %collective-permute-start.18 = (f32[8,128]{1,0:T(8,128)S(1)}, f32[8,128]{1,0:T(8,128)S(1)}, u32[]{:S(2)}, u32[]{:S(2)}) collective-permute-start(f32[8,128]{1,0:T(8,128)S(1)} %get-tuple-element.54), channel_id=1, source_target_pairs={{0,16},{8,24},{16,0},{24,8},{1,17},{9,25},{17,1},{25,9},{2,18},{10... | collective-permute-start | bytes 12296 | tf_op jit(solution)/shard_map/ppermute | solution.py:611
  73.1 1.6 %collective-permute-done.17 = f32[8,128]{1,0:T(8,128)S(1)} collective-permute-done((f32[8,128]{1,0:T(8,128)S(1)}, f32[8,128]{1,0:T(8,128)S(1)}, u32[]{:S(2)}, u32[]{:S(2)}) %collective-permute-start.17) | collective-permute-done | bytes 4128 | tf_op jit(solution)/shard_map/ppermute | solution.py:611
  76.6 1.7 %collective-permute-start.22 = (f32[8,128]{1,0:T(8,128)S(1)}, f32[8,128]{1,0:T(8,128)S(1)}, u32[]{:S(2)}, u32[]{:S(2)}) collective-permute-start(f32[8,128]{1,0:T(8,128)S(1)} %add_add_fusion.1), channel_id=1, source_target_pairs={{0,5},{1,4},{2,7},{3,6},{4,1},{5,0},{6,3},{7,2},{8,13},{9,12},{10,... | collective-permute-start | bytes 12296 | tf_op jit(solution)/shard_map/ppermute | solution.py:683
  78.4 1.5 %collective-permute-done.20 = f32[8,128]{1,0:T(8,128)S(1)} collective-permute-done((f32[8,128]{1,0:T(8,128)S(1)}, f32[8,128]{1,0:T(8,128)S(1)}, u32[]{:S(2)}, u32[]{:S(2)}) %collective-permute-start.20) | collective-permute-done | bytes 4128 | tf_op jit(solution)/shard_map/ppermute | solution.py:605
  81.1 2.4 %collective-permute-done.23.refs_1_ = f32[8,128]{1,0:T(8,128)S(1)} collective-permute-done((f32[8,128]{1,0:T(8,128)S(1)}, f32[8,128]{1,0:T(8,128)S(1)}, u32[]{:S(2)}, u32[]{:S(2)}) %collective-permute-start.23) | collective-permute-done | bytes 4128 | tf_op jit(solution)/shard_map/ppermute | solution.py:687
  (56 shorter events, 16.7 us)
Async XLA Ops:
  2.6 12.6 %collective-permute-start = (f32[3,8,32,128]{3,2,1,0:T(8,128)}, f32[3,8,32,128]{3,2,1,0:T(8,128)S(1)}, u32[]{:S(2)}, u32[]{:S(2)}) collective-permute-start(f32[3,8,32,128]{3,2,1,0:T(8,128)} %get-tuple-element.30), channel_id=1, source_target_pairs={{0,4},{4,0},{1,5},{5,1},{2,6},{6,2},{3,7},{7,3},{8,12},{12,8},{9,1... | collective-permute-start | bytes 1179656 | tf_op jit(solution)/shard_map/ppermute | solution.py:605
  5.6 7.7 %collective-permute-start.1 = (f32[2,2,32,128]{3,2,1,0:T(8,128)}, f32[2,2,32,128]{3,2,1,0:T(8,128)S(1)}, u32[]{:S(2)}, u32[]{:S(2)}) collective-permute-start(f32[2,2,32,128]{3,2,1,0:T(8,128)} %get-tuple-element.31), channel_id=1, source_target_pairs={{0,8},{8,16},{16,24},{24,0},{1,9},{9,17},{17,25},{25,1},{2,10},{10... | collective-permute-start | bytes 196616 | tf_op jit(solution)/shard_map/ppermute | solution.py:611
  7.2 7.6 %collective-permute-start.2 = (f32[2,2,32,128]{3,2,1,0:T(8,128)}, f32[2,2,32,128]{3,2,1,0:T(8,128)S(1)}, u32[]{:S(2)}, u32[]{:S(2)}) collective-permute-start(f32[2,2,32,128]{3,2,1,0:T(8,128)} %get-tuple-element.31), channel_id=1, source_target_pairs={{0,16},{8,24},{16,0},{24,8},{1,17},{9,25},{17,1},{25,9},{2,18},{10... | collective-permute-start | bytes 196616 | tf_op jit(solution)/shard_map/ppermute | solution.py:611
  9.8 5.0 %collective-permute-start.3 = (f32[2,2,32,128]{3,2,1,0:T(8,128)}, f32[2,2,32,128]{3,2,1,0:T(8,128)S(1)}, u32[]{:S(2)}, u32[]{:S(2)}) collective-permute-start(f32[2,2,32,128]{3,2,1,0:T(8,128)} %get-tuple-element.31), channel_id=1, source_target_pairs={{0,24},{8,0},{16,8},{24,16},{1,25},{9,1},{17,9},{25,17},{2,26},{10... | collective-permute-start | bytes 196616 | tf_op jit(solution)/shard_map/ppermute | solution.py:611
  15.9 9.6 %collective-permute-start.4 = (f32[2,16,32,128]{3,2,1,0:T(8,128)S(1)}, f32[2,16,32,128]{3,2,1,0:T(8,128)S(1)}, u32[]{:S(2)}, u32[]{:S(2)}) collective-permute-start(f32[2,16,32,128]{3,2,1,0:T(8,128)S(1)} %get-tuple-element.33.fields), channel_id=1, source_target_pairs={{0,1},{1,0},{2,3},{3,2},{4,5},{5,4},{6,7},{7,6},{8,9},{9,8},{10,11... | collective-permute-start | bytes 1572872 | tf_op jit(solution)/shard_map/ppermute | solution.py:608
  16.0 8.7 %collective-permute-start.7 = (f32[2,8,32,128]{3,2,1,0:T(8,128)S(1)}, f32[2,8,32,128]{3,2,1,0:T(8,128)S(1)}, u32[]{:S(2)}, u32[]{:S(2)}) collective-permute-start(f32[2,8,32,128]{3,2,1,0:T(8,128)S(1)} %shard_map.123.refs_3_.refs_0_), channel_id=1, source_target_pairs={{0,4},{4,0},{1,5},{5,1},{2,6},{6,2},{3,7},{7,3},{8,12},{12,8},{9,1... | collective-permute-start | bytes 786440 | tf_op jit(solution)/shard_map/ppermute | solution.py:605
  17.4 7.3 %collective-permute-start.5 = (f32[2,16,8,128]{3,2,1,0:T(8,128)S(1)}, f32[2,16,8,128]{3,2,1,0:T(8,128)S(1)}, u32[]{:S(2)}, u32[]{:S(2)}) collective-permute-start(f32[2,16,8,128]{3,2,1,0:T(8,128)S(1)} %get-tuple-element.34), channel_id=1, source_target_pairs={{1,2},{2,1},{5,6},{6,5},{9,10},{10,9},{13,14},{14,13},{17,18},{18,... | collective-permute-start | bytes 393224 | tf_op jit(solution)/shard_map/ppermute | solution.py:634
  18.1 7.4 %collective-permute-start.6 = (f32[2,16,8,128]{3,2,1,0:T(8,128)S(1)}, f32[2,16,8,128]{3,2,1,0:T(8,128)S(1)}, u32[]{:S(2)}, u32[]{:S(2)}) collective-permute-start(f32[2,16,8,128]{3,2,1,0:T(8,128)S(1)} %get-tuple-element.35), channel_id=1, source_target_pairs={{1,3},{2,0},{5,7},{6,4},{9,11},{10,8},{13,15},{14,12},{17,19},{18,... | collective-permute-start | bytes 393224 | tf_op jit(solution)/shard_map/ppermute | solution.py:634
  25.5 7.0 %collective-permute-start.8 = (f32[2,16,32,128]{3,2,1,0:T(8,128)S(1)}, f32[2,16,32,128]{3,2,1,0:T(8,128)S(1)}, u32[]{:S(2)}, u32[]{:S(2)}) collective-permute-start(f32[2,16,32,128]{3,2,1,0:T(8,128)S(1)} %get-tuple-element.42.fields), channel_id=1, source_target_pairs={{0,1},{1,0},{2,3},{3,2},{4,5},{5,4},{6,7},{7,6},{8,9},{9,8},{10,11... | collective-permute-start | bytes 1572872 | tf_op jit(solution)/shard_map/ppermute | solution.py:608
  25.6 6.9 %collective-permute-start.10 = (f32[2,16,8,128]{3,2,1,0:T(8,128)S(1)}, f32[2,16,8,128]{3,2,1,0:T(8,128)S(1)}, u32[]{:S(2)}, u32[]{:S(2)}) collective-permute-start(f32[2,16,8,128]{3,2,1,0:T(8,128)S(1)} %get-tuple-element.43), channel_id=1, source_target_pairs={{1,3},{2,0},{5,7},{6,4},{9,11},{10,8},{13,15},{14,12},{17,19},{18,... | collective-permute-start | bytes 393224 | tf_op jit(solution)/shard_map/ppermute | solution.py:634
  26.9 5.6 %collective-permute-start.9 = (f32[2,16,8,128]{3,2,1,0:T(8,128)S(1)}, f32[2,16,8,128]{3,2,1,0:T(8,128)S(1)}, u32[]{:S(2)}, u32[]{:S(2)}) collective-permute-start(f32[2,16,8,128]{3,2,1,0:T(8,128)S(1)} %get-tuple-element.43), channel_id=1, source_target_pairs={{1,2},{2,1},{5,6},{6,5},{9,10},{10,9},{13,14},{14,13},{17,18},{18,... | collective-permute-start | bytes 393224 | tf_op jit(solution)/shard_map/ppermute | solution.py:634
  37.3 6.6 %collective-permute-start.11 = (f32[20,8,128]{2,1,0:T(8,128)S(1)}, f32[20,8,128]{2,1,0:T(8,128)S(1)}, u32[]{:S(2)}, u32[]{:S(2)}) collective-permute-start(f32[20,8,128]{2,1,0:T(8,128)S(1)} %get-tuple-element.45.sent), channel_id=1, source_target_pairs={{0,2},{1,3},{2,0},{3,1},{4,6},{5,7},{6,4},{7,5},{8,10},{9,11},{10,... | collective-permute-start | bytes 245768 | tf_op jit(solution)/shard_map/ppermute | solution.py:662
  48.8 2.0 %collective-permute-start.12 = (f32[2,16,32,128]{3,2,1,0:T(8,128)S(1)}, f32[2,16,32,128]{3,2,1,0:T(8,128)S(1)}, u32[]{:S(2)}, u32[]{:S(2)}) collective-permute-start(f32[2,16,32,128]{3,2,1,0:T(8,128)S(1)} %get-tuple-element.47), channel_id=1, source_target_pairs={{0,1},{1,0},{2,3},{3,2},{4,5},{5,4},{6,7},{7,6},{8,9},{9,8},{10,11... | collective-permute-start | bytes 1572872 | tf_op jit(solution)/shard_map/ppermute | solution.py:608
  50.9 8.4 %collective-permute-start.13 = (f32[2,8,32,128]{3,2,1,0:T(8,128)S(1)}, f32[2,8,32,128]{3,2,1,0:T(8,128)S(1)}, u32[]{:S(2)}, u32[]{:S(2)}) collective-permute-start(f32[2,8,32,128]{3,2,1,0:T(8,128)S(1)} %get-tuple-element.49), channel_id=1, source_target_pairs={{0,4},{4,0},{1,5},{5,1},{2,6},{6,2},{3,7},{7,3},{8,12},{12,8},{9,1... | collective-permute-start | bytes 786440 | tf_op jit(solution)/shard_map/ppermute | solution.py:605
  59.6 6.9 %collective-permute-start.14 = (f32[2,2,32,128]{3,2,1,0:T(8,128)S(1)}, f32[2,2,32,128]{3,2,1,0:T(8,128)S(1)}, u32[]{:S(2)}, u32[]{:S(2)}) collective-permute-start(f32[2,2,32,128]{3,2,1,0:T(8,128)S(1)} %get-tuple-element.51), channel_id=1, source_target_pairs={{0,8},{8,16},{16,24},{24,0},{1,9},{9,17},{17,25},{25,1},{2,10},{10... | collective-permute-start | bytes 196616 | tf_op jit(solution)/shard_map/ppermute | solution.py:611
  61.4 7.2 %collective-permute-start.15 = (f32[2,2,32,128]{3,2,1,0:T(8,128)S(1)}, f32[2,2,32,128]{3,2,1,0:T(8,128)S(1)}, u32[]{:S(2)}, u32[]{:S(2)}) collective-permute-start(f32[2,2,32,128]{3,2,1,0:T(8,128)S(1)} %get-tuple-element.52), channel_id=1, source_target_pairs={{0,16},{8,24},{16,0},{24,8},{1,17},{9,25},{17,1},{25,9},{2,18},{10... | collective-permute-start | bytes 196616 | tf_op jit(solution)/shard_map/ppermute | solution.py:611
  64.0 4.7 %collective-permute-start.16 = (f32[2,2,32,128]{3,2,1,0:T(8,128)S(1)}, f32[2,2,32,128]{3,2,1,0:T(8,128)S(1)}, u32[]{:S(2)}, u32[]{:S(2)}) collective-permute-start(f32[2,2,32,128]{3,2,1,0:T(8,128)S(1)} %get-tuple-element.53), channel_id=1, source_target_pairs={{0,24},{8,0},{16,8},{24,16},{1,25},{9,1},{17,9},{25,17},{2,26},{10... | collective-permute-start | bytes 196616 | tf_op jit(solution)/shard_map/ppermute | solution.py:611
  69.2 5.5 %collective-permute-start.17 = (f32[8,128]{1,0:T(8,128)S(1)}, f32[8,128]{1,0:T(8,128)S(1)}, u32[]{:S(2)}, u32[]{:S(2)}) collective-permute-start(f32[8,128]{1,0:T(8,128)S(1)} %get-tuple-element.54), channel_id=1, source_target_pairs={{0,8},{8,16},{16,24},{24,0},{1,9},{9,17},{17,25},{25,1},{2,10},{10... | collective-permute-start | bytes 12296 | tf_op jit(solution)/shard_map/ppermute | solution.py:611
  70.4 4.5 %collective-permute-start.18 = (f32[8,128]{1,0:T(8,128)S(1)}, f32[8,128]{1,0:T(8,128)S(1)}, u32[]{:S(2)}, u32[]{:S(2)}) collective-permute-start(f32[8,128]{1,0:T(8,128)S(1)} %get-tuple-element.54), channel_id=1, source_target_pairs={{0,16},{8,24},{16,0},{24,8},{1,17},{9,25},{17,1},{25,9},{2,18},{10... | collective-permute-start | bytes 12296 | tf_op jit(solution)/shard_map/ppermute | solution.py:611
  72.6 3.6 %collective-permute-start.19 = (f32[8,128]{1,0:T(8,128)S(1)}, f32[8,128]{1,0:T(8,128)S(1)}, u32[]{:S(2)}, u32[]{:S(2)}) collective-permute-start(f32[8,128]{1,0:T(8,128)S(1)} %get-tuple-element.54), channel_id=1, source_target_pairs={{0,24},{8,0},{16,8},{24,16},{1,25},{9,1},{17,9},{25,17},{2,26},{10... | collective-permute-start | bytes 12296 | tf_op jit(solution)/shard_map/ppermute | solution.py:611
  76.2 3.6 %collective-permute-start.20 = (f32[8,128]{1,0:T(8,128)S(1)}, f32[8,128]{1,0:T(8,128)S(1)}, u32[]{:S(2)}, u32[]{:S(2)}) collective-permute-start(f32[8,128]{1,0:T(8,128)S(1)} %add_add_fusion.1), channel_id=1, source_target_pairs={{0,4},{4,0},{1,5},{5,1},{2,6},{6,2},{3,7},{7,3},{8,12},{12,8},{9,1... | collective-permute-start | bytes 12296 | tf_op jit(solution)/shard_map/ppermute | solution.py:605
  76.6 3.2 %collective-permute-start.21 = (f32[8,128]{1,0:T(8,128)S(1)}, f32[8,128]{1,0:T(8,128)S(1)}, u32[]{:S(2)}, u32[]{:S(2)}) collective-permute-start(f32[8,128]{1,0:T(8,128)S(1)} %add_add_fusion.1), channel_id=1, source_target_pairs={{0,1},{1,0},{2,3},{3,2},{4,5},{5,4},{6,7},{7,6},{8,9},{9,8},{10,11... | collective-permute-start | bytes 12296 | tf_op jit(solution)/shard_map/ppermute | solution.py:608
  76.6 3.2 %collective-permute-start.22 = (f32[8,128]{1,0:T(8,128)S(1)}, f32[8,128]{1,0:T(8,128)S(1)}, u32[]{:S(2)}, u32[]{:S(2)}) collective-permute-start(f32[8,128]{1,0:T(8,128)S(1)} %add_add_fusion.1), channel_id=1, source_target_pairs={{0,5},{1,4},{2,7},{3,6},{4,1},{5,0},{6,3},{7,2},{8,13},{9,12},{10,... | collective-permute-start | bytes 12296 | tf_op jit(solution)/shard_map/ppermute | solution.py:683
  79.8 3.7 %collective-permute-start.23 = (f32[8,128]{1,0:T(8,128)S(1)}, f32[8,128]{1,0:T(8,128)S(1)}, u32[]{:S(2)}, u32[]{:S(2)}) collective-permute-start(f32[8,128]{1,0:T(8,128)S(1)} %add_add_fusion.refs_0_), channel_id=1, source_target_pairs={{0,2},{1,3},{2,0},{3,1},{4,6},{5,7},{6,4},{7,5},{8,10},{9,11},{10,... | collective-permute-start | bytes 12296 | tf_op jit(solution)/shard_map/ppermute | solution.py:687
  (9 other events, 42.5 us)

commit v4 on v3

--- a/solution.py
+++ b/solution.py
@@ -489,33 +489,28 @@
     message[...] = own[:, pl.ds(cx * (1 - x), cx)] + came[:, pl.ds(cx * (1 - x), cx)]
 
 
-def slab_kernel(kept, came, *outs):
-    s, _, _, _ = places(2)
-    n = len(outs)
+def slab_kernel(kept, came, out):
+    n = out.shape[0]
     slab = 128 // n
     _, cx, cy, _ = kept.shape
     lane = index_along((cy, 128), 1) // slab
     for f in range(2):
         for q in range(cx // n):
             planes = [kept[f, n * q + j] + came[f, n * q + j] for j in range(n)]
-            for k in range(n):
-                to = (s + k) % n
+            for to in range(n):
                 piece = jnp.zeros((cy, 128), jnp.float32)
                 for j in range(n):
-                    moved = pltpu.roll(planes[j], ((j - to + n) % n) * slab, 1)
+                    moved = pltpu.roll(planes[j], ((j - to) % n) * slab, 1)
                     piece = jnp.where(lane == j, moved, piece)
-                outs[k][f, q] = piece
-
-
-def project_kernel(*refs, n):
-    beta_prev = refs[0]
-    parts = refs[1 : 1 + n]
-    vk, va, qk, qa, w_k, w_a, tile = refs[1 + n :]
+                out[to, f, q] = piece
+
+
+def project_kernel(beta_prev, parts, vk, va, qk, qa, w_k, w_a, tile, *, n):
     s, x, y, c = places(2)
     slab = 128 // n
     for f, (q_ref, w) in enumerate(((qk, w_k), (qa, w_a))):
         for q in range(vk.shape[0] // n):
-            whole = sum(part[f, q] for part in parts[1:]) + parts[0][f, q]
+            whole = jnp.sum(parts[:, f, q], axis=0)
             for j in range(n):
                 i = n * q + j
                 w[i] = whole[:, slab * j : slab * (j + 1)] - beta_prev[...] * q_ref[i]
@@ -540,11 +535,8 @@
     tile[...] = jnp.where(lane == me, values, 0.0)
 
 
-def final_kernel(*refs, cells):
-    tiles, (w_k, w_a, vk, va, next_k, next_a, coefs) = refs[:-7], refs[-7:]
-    tile = tiles[0][...]
-    for other in tiles[1:]:
-        tile = tile + other[...]
+def final_kernel(tiles, w_k, w_a, vk, va, next_k, next_a, coefs, *, cells):
+    tile = jnp.sum(tiles[...], axis=0)
     wv, vv, a, uv, uu = (tile[i : i + 1] for i in range(5))
     wv_sum = jnp.sum(wv, axis=1, keepdims=True)
     vv_sum = jnp.sum(vv, axis=1, keepdims=True)
@@ -669,26 +661,19 @@
     kept, message = run(
         core_kernel, (f32(2, cx, cy, cz), f32(2, cx, cy, cz)), own, swap_core(message)
     )
-    pieces = run(
-        slab_kernel, [f32(2, groups, cy, cz)] * n, kept, swap_x(message)
-    )
-    parts = [pieces[0]] + [along_z(pieces[k], k) for k in range(1, n)]
+    (pieces,) = run(slab_kernel, (f32(n, 2, groups, cy, cz),), kept, swap_x(message))
+    parts = lax.all_to_all(pieces, "src", 0, 0)
     w_k, w_a, tile = run(
         functools.partial(project_kernel, n=n),
         (f32(*v_kappa.shape), f32(*v_kappa.shape), f32(8, 128)),
-        beta_prev.reshape(1, 1), *parts, v_kappa, v_absorb, q_kappa, q_absorb,
-    )
-    tile = tile + sum(along_z(tile, k) for k in range(1, n))
-    over_x, over_core = swap_x(tile), swap_core(tile)
-    over_both = lax.ppermute(
-        tile, ("gx", "gy"), [(4 * a + b, 4 * (1 - a) + (b ^ 1)) for a in range(2) for b in range(4)]
-    )
-    tile = tile + over_x + over_core + over_both
-    over_y = lax.ppermute(tile, "gy", [(i, (i + 2) % 4) for i in range(4)])
+        beta_prev.reshape(1, 1), parts, v_kappa, v_absorb, q_kappa, q_absorb,
+    )
+    everyone = ("src", "gx", "gy")
+    tiles = lax.all_to_all(jnp.broadcast_to(tile, (8 * n, 8, 128)), everyone, 0, 0)
     return tuple(run(
         functools.partial(final_kernel, cells=cells),
         (f32(*v_kappa.shape), f32(*v_kappa.shape), f32(2)),
-        tile, over_y, w_k, w_a, v_kappa, v_absorb, in_smem_out=(2,),
+        tiles, w_k, w_a, v_kappa, v_absorb, in_smem_out=(2,),
     ))
 
 

time: 84.7 us -> 85 us (level)
  starting transfers between devices: 30.9 us -> 19.9 us
  blocking collectives: 0 us -> 9.95 us
    all_to_all x0 -> x1, blocking collectives: none -> 9.95 us  [per_device_paired(): lax.all_to_all(jnp.broadcast_to(tile, (8 * n, 8, 128)), everyone, 0, 0)]
    ppermute x9 -> x3, starting transfers between devices: 15.1 us -> 5.51 us  [along_z(): return lax.ppermute(value, 'src', [(i, (i + k) % n) for i in range(n)])]
    all_to_all x0 -> x1, waiting for transfers between devices: none -> 7.7 us  [per_device_paired(): parts = lax.all_to_all(pieces, 'src', 0, 0)]
    ppermute x9 -> x3, waiting for transfers between devices: 7.23 us -> 1.47 us  [along_z(): return lax.ppermute(value, 'src', [(i, (i + k) % n) for i in range(n)])]
    all_to_all x0 -> x1, starting transfers between devices: none -> 5 us  [per_device_paired(): parts = lax.all_to_all(pieces, 'src', 0, 0)]
    ppermute x1, starting transfers between devices: 3.43 us -> 0.07 us  [per_device_paired(): heard = lax.ppermute(sent, 'gy', [(i, (i + 2) % 4) for i in range(4)])]
    ppermute x2 -> x0, starting transfers between devices: 2.95 us -> none  [the longest x1 1.71 us: per_device_paired(): lax.ppermute(tile, ('gx', 'gy'), [(4 * a + b, 4 * (1 - a) + (b ^ 1)) for...]
    ppermute x2 -> x0, waiting for transfers between devices: 2.44 us -> none  [the longest x1 2.44 us: per_device_paired(): over_y = lax.ppermute(tile, 'gy', [(i, (i + 2) % 4) for i in range(4)])]
  transfers between devices with their start and end apart: 24 -> 15, of which waited for: 14 -> 8; matrix products, arithmetic and copies ran while one was open for 0% -> 0% of each run, Pallas kernels for 6% -> 6%
where the time goes in v4:
time: 85 us; the launch traced here: 84.7 us
  waiting for transfers between devices  32.8 us (39%)
  Pallas kernels  20.4 us (24%)
  starting transfers between devices  19.9 us (23%)
  blocking collectives  9.95 us (12%)
  between operations  1.53 us (2%)
    pallas_call x12, Pallas kernels, run(): pl.pallas_call(body if waits else kernel, out_shape=tuple(outs), in_specs...  20.4 us
    ppermute x3, waiting for transfers between devices, swap_x(): return lax.ppermute(value, 'gx', [(0, 1), (1, 0)])  13 us
    all_to_all x1, blocking collectives, per_device_paired(): lax.all_to_all(jnp.broadcast_to(tile, (8 * n, 8, 128)), everyone, 0, 0)  9.95 us
    all_to_all x1, waiting for transfers between devices, per_device_paired(): parts = lax.all_to_all(pieces, 'src', 0, 0)  7.7 us
    ppermute x3, starting transfers between devices, along_z(): return lax.ppermute(value, 'src', [(i, (i + k) % n) for i in range(n)])  5.51 us
    ppermute x3, starting transfers between devices, swap_x(): return lax.ppermute(value, 'gx', [(0, 1), (1, 0)])  5.17 us
    all_to_all x1, starting transfers between devices, per_device_paired(): parts = lax.all_to_all(pieces, 'src', 0, 0)  5 us
    ppermute x1, waiting for transfers between devices, per_device_paired(): heard = lax.ppermute(sent, 'gy', [(i, (i + 2) % 4) for i in range(4)])  4.43 us
  transfers between devices with their start and end apart: 15, of which 8 were waited for; matrix products, arithmetic and copies ran while one was open for 0% of the time, Pallas kernels for 6%

profile of v4, /device:TPU:0, one launch (start us, length us, event | category | flops | bytes accessed | tf_op | source)
XLA Modules:
  0.0 84.7 jit_solution(17687026934243753223)
XLA Ops:
  0.6 1.9 %shard_map.121 = (f32[2,2,32,128]{3,2,1,0:T(8,128)}, f32[3,8,32,128]{3,2,1,0:T(8,128)}) custom-call(f32[4,8,32,128]{3,2,1,0:T(8,128)} %refs_0_.3, s32[8,32,128]{2,1,0:T(8,128)} %refs_1_.3, f32[8,32,32]{2,1,0:T(8,128)} %vk.5, f32[8,32,32]{2,1,0:T(8,128)} %va.5), custom_call_target="tpu_custom_call" | custom-call | tf_op jit(solution)/shard_map/pallas_call | solution.py:570
  2.6 3.0 %collective-permute-start = (f32[3,8,32,128]{3,2,1,0:T(8,128)}, f32[3,8,32,128]{3,2,1,0:T(8,128)S(1)}, u32[]{:S(2)}, u32[]{:S(2)}) collective-permute-start(f32[3,8,32,128]{3,2,1,0:T(8,128)} %get-tuple-element.26), channel_id=1, source_target_pairs={{0,4},{4,0},{1,5},{5,1},{2,6},{6,2},{3,7},{7,3},{8,12},{12,8},{9,1... | collective-permute-start | bytes 1179656 | tf_op jit(solution)/shard_map/ppermute | solution.py:597
  5.6 1.6 %collective-permute-start.1 = (f32[2,2,32,128]{3,2,1,0:T(8,128)}, f32[2,2,32,128]{3,2,1,0:T(8,128)S(1)}, u32[]{:S(2)}, u32[]{:S(2)}) collective-permute-start(f32[2,2,32,128]{3,2,1,0:T(8,128)} %get-tuple-element.27), channel_id=1, source_target_pairs={{0,8},{8,16},{16,24},{24,0},{1,9},{9,17},{17,25},{25,1},{2,10},{10... | collective-permute-start | bytes 196616 | tf_op jit(solution)/shard_map/ppermute | solution.py:603
  7.2 2.6 %collective-permute-start.2 = (f32[2,2,32,128]{3,2,1,0:T(8,128)}, f32[2,2,32,128]{3,2,1,0:T(8,128)S(1)}, u32[]{:S(2)}, u32[]{:S(2)}) collective-permute-start(f32[2,2,32,128]{3,2,1,0:T(8,128)} %get-tuple-element.27), channel_id=1, source_target_pairs={{0,16},{8,24},{16,0},{24,8},{1,17},{9,25},{17,1},{25,9},{2,18},{10... | collective-permute-start | bytes 196616 | tf_op jit(solution)/shard_map/ppermute | solution.py:603
  9.8 1.3 %collective-permute-start.3 = (f32[2,2,32,128]{3,2,1,0:T(8,128)}, f32[2,2,32,128]{3,2,1,0:T(8,128)S(1)}, u32[]{:S(2)}, u32[]{:S(2)}) collective-permute-start(f32[2,2,32,128]{3,2,1,0:T(8,128)} %get-tuple-element.27), channel_id=1, source_target_pairs={{0,24},{8,0},{16,8},{24,16},{1,25},{9,1},{17,9},{25,17},{2,26},{10... | collective-permute-start | bytes 196616 | tf_op jit(solution)/shard_map/ppermute | solution.py:603
  11.1 2.1 %shard_map.122.refs_5_.count = f32[16,72,128]{2,1,0:T(8,128)S(1)} custom-call(s32[1,1024]{1,0:T(1,128)S(1)} %bitcast.3), custom_call_target="tpu_custom_call" | custom-call | flops 301989888 | bytes 589824 | tf_op jit(solution)/shard_map/pallas_call | solution.py:570
  13.3 1.5 %collective-permute-done.2.refs_3_ = f32[2,2,32,128]{3,2,1,0:T(8,128)S(1)} collective-permute-done((f32[2,2,32,128]{3,2,1,0:T(8,128)}, f32[2,2,32,128]{3,2,1,0:T(8,128)S(1)}, u32[]{:S(2)}, u32[]{:S(2)}) %collective-permute-start.2) | collective-permute-done | bytes 65568 | tf_op jit(solution)/shard_map/ppermute | solution.py:603
  16.0 1.5 %collective-permute-start.7 = (f32[2,8,32,128]{3,2,1,0:T(8,128)S(1)}, f32[2,8,32,128]{3,2,1,0:T(8,128)S(1)}, u32[]{:S(2)}, u32[]{:S(2)}) collective-permute-start(f32[2,8,32,128]{3,2,1,0:T(8,128)S(1)} %shard_map.123.refs_3_.refs_0_), channel_id=1, source_target_pairs={{0,4},{4,0},{1,5},{5,1},{2,6},{6,2},{3,7},{7,3},{8,12},{12,8},{9,1... | collective-permute-start | bytes 786440 | tf_op jit(solution)/shard_map/ppermute | solution.py:597
  18.1 1.3 %collective-permute-start.6 = (f32[2,16,8,128]{3,2,1,0:T(8,128)S(1)}, f32[2,16,8,128]{3,2,1,0:T(8,128)S(1)}, u32[]{:S(2)}, u32[]{:S(2)}) collective-permute-start(f32[2,16,8,128]{3,2,1,0:T(8,128)S(1)} %get-tuple-element.31), channel_id=1, source_target_pairs={{1,3},{2,0},{5,7},{6,4},{9,11},{10,8},{13,15},{14,12},{17,19},{18,... | collective-permute-start | bytes 393224 | tf_op jit(solution)/shard_map/ppermute | solution.py:626
  19.4 5.3 %collective-permute-done.7.refs_1_ = f32[2,8,32,128]{3,2,1,0:T(8,128)S(1)} collective-permute-done((f32[2,8,32,128]{3,2,1,0:T(8,128)S(1)}, f32[2,8,32,128]{3,2,1,0:T(8,128)S(1)}, u32[]{:S(2)}, u32[]{:S(2)}) %collective-permute-start.7) | collective-permute-done | bytes 262176 | tf_op jit(solution)/shard_map/ppermute | solution.py:597
  24.7 0.8 collective-permute-done.6.edge_mine.refs_4_
  26.3 1.3 %collective-permute-start.10 = (f32[2,16,8,128]{3,2,1,0:T(8,128)S(1)}, f32[2,16,8,128]{3,2,1,0:T(8,128)S(1)}, u32[]{:S(2)}, u32[]{:S(2)}) collective-permute-start(f32[2,16,8,128]{3,2,1,0:T(8,128)S(1)} %get-tuple-element.39), channel_id=1, source_target_pairs={{1,3},{2,0},{5,7},{6,4},{9,11},{10,8},{13,15},{14,12},{17,19},{18,... | collective-permute-start | bytes 393224 | tf_op jit(solution)/shard_map/ppermute | solution.py:626
  27.6 2.9 %shard_map.125 = (f32[18,72,128]{2,1,0:T(8,128)S(1)}, f32[16,72,128]{2,1,0:T(8,128)S(1)}, f32[17,72,128]{2,1,0:T(8,128)S(1)}, f32[16,72,128]{2,1,0:T(8,128)S(1)}...) custom-call(f32[16]{0:T(128)S(1)} %copy-done.6, f32[16]{0:T(128)S(1)} %copy-done.7, ...), custom_call_target="tpu_custom_call" | custom-call | tf_op jit(solution)/shard_map/pallas_call | solution.py:570
  30.5 3.6 %collective-permute-done.10.edge_b = f32[2,16,8,128]{3,2,1,0:T(8,128)S(1)} collective-permute-done((f32[2,16,8,128]{3,2,1,0:T(8,128)S(1)}, f32[2,16,8,128]{3,2,1,0:T(8,128)S(1)}, u32[]{:S(2)}, u32[]{:S(2)}) %collective-permute-start.10) | collective-permute-done | bytes 131104 | tf_op jit(solution)/shard_map/ppermute | solution.py:626
  34.1 4.9 %shard_map.127 = (f32[16,72,128]{2,1,0:T(8,128)S(1)}, f32[20,8,128]{2,1,0:T(8,128)S(1)}) custom-call(f32[18,72,128]{2,1,0:T(8,128)S(1)} %get-tuple-element.32.phi, f32[16,72,128]{2,1,0:T(8,128)S(1)} %get-tuple-element.33.diag, f32[17,72,128]{2,1,0:T(8,128)S(1)} %get-tuple-element.34.fx, f32[16,72,128]{2,1,0:T(8,128)S(1)} %get-tuple-element.35.fy, ...), custom_call_target="tpu_custom_call" | custom-call | tf_op jit(solution)/shard_map/pallas_call | solution.py:570
  39.0 4.4 %collective-permute-done.11.came = f32[20,8,128]{2,1,0:T(8,128)S(1)} collective-permute-done((f32[20,8,128]{2,1,0:T(8,128)S(1)}, f32[20,8,128]{2,1,0:T(8,128)S(1)}, u32[]{:S(2)}, u32[]{:S(2)}) %collective-permute-start.11) | collective-permute-done | bytes 81952 | tf_op jit(solution)/shard_map/ppermute | solution.py:654
  43.4 4.9 %shard_map.128 = (f32[2,16,32,128]{3,2,1,0:T(8,128)S(1)}, f32[2,16,32,128]{3,2,1,0:T(8,128)S(1)}) custom-call(f32[18,72,128]{2,1,0:T(8,128)S(1)} %get-tuple-element.32.phi, f32[16,72,128]{2,1,0:T(8,128)S(1)} %get-tuple-element.40.change, f32[16,72,128]{2,1,0:T(8,128)S(1)} %get-tuple-element.33.diag, f32[17,72,128]{2,1,0:T(8,128)S(1)} %get-tuple-element.34.fx, ...), custom_call_target="tpu_custom_call" | custom-call | tf_op jit(solution)/shard_map/pallas_call | solution.py:570
  48.4 1.9 %collective-permute-done.12.came = f32[2,16,32,128]{3,2,1,0:T(8,128)S(1)} collective-permute-done((f32[2,16,32,128]{3,2,1,0:T(8,128)S(1)}, f32[2,16,32,128]{3,2,1,0:T(8,128)S(1)}, u32[]{:S(2)}, u32[]{:S(2)}) %collective-permute-start.12) | collective-permute-done | bytes 524320 | tf_op jit(solution)/shard_map/ppermute | solution.py:600
  51.1 7.7 %collective-permute-done.13.came = f32[2,8,32,128]{3,2,1,0:T(8,128)S(1)} collective-permute-done((f32[2,8,32,128]{3,2,1,0:T(8,128)S(1)}, f32[2,8,32,128]{3,2,1,0:T(8,128)S(1)}, u32[]{:S(2)}, u32[]{:S(2)}) %collective-permute-start.13) | collective-permute-done | bytes 262176 | tf_op jit(solution)/shard_map/ppermute | solution.py:597
  58.8 1.0 %shard_map.130 = f32[4,2,2,32,128]{4,3,2,1,0:T(8,128)} custom-call(f32[2,8,32,128]{3,2,1,0:T(8,128)S(1)} %get-tuple-element.44.kept, f32[2,8,32,128]{3,2,1,0:T(8,128)S(1)} %collective-permute-done.13.came), custom_call_target="tpu_custom_call" | custom-call | tf_op jit(solution)/shard_map/pallas_call | solution.py:570
  59.8 5.0 %all-to-all-start = ((f32[4,2,2,32,128]{4,3,2,1,0:T(8,128)}), f32[4,2,2,32,128]{4,3,2,1,0:T(8,128)S(1)}, u32[]{:S(2)}, u32[]{:S(2)}) async-start(f32[4,2,2,32,128]{4,3,2,1,0:T(8,128)} %shard_map.130), calls=%async_computation | async-start | bytes 524288 | tf_op jit(solution)/shard_map/all_to_all | solution.py:665
  65.4 7.7 %all-to-all-done.parts = f32[4,2,2,32,128]{4,3,2,1,0:T(8,128)S(1)} async-done(((f32[4,2,2,32,128]{4,3,2,1,0:T(8,128)}), f32[4,2,2,32,128]{4,3,2,1,0:T(8,128)S(1)}, u32[]{:S(2)}, u32[]{:S(2)}) %all-to-all-start) | async-done | bytes 262176 | tf_op jit(solution)/shard_map/all_to_all | solution.py:665
  73.7 9.9 %all_to_all.10.tiles = f32[32,8,128]{2,1,0:T(8,128)S(1)} all-to-all(f32[32,8,128]{2,1,0:T(8,128)S(1)} %broadcast_in_dim.3), channel_id=1, replica_groups=mesh['src'=4,'gx'=2,'gy'=4] {'src','gx','gy'}, dimensions={0} | all-to-all | bytes 262144 | tf_op jit(solution)/shard_map/all_to_all | solution.py:672
  83.7 1.0 %shard_map.132 = (f32[8,32,32]{2,1,0:T(8,128)}, f32[8,32,32]{2,1,0:T(8,128)}, f32[2]{0:T(128)}) custom-call(f32[32,8,128]{2,1,0:T(8,128)S(1)} %all_to_all.10.tiles, f32[8,32,32]{2,1,0:T(8,128)S(1)} %get-tuple-element.47.w_k, f32[8,32,32]{2,1,0:T(8,128)S(1)} %get-tuple-element.48.w_a, f32[8,32,32]{2,1,0:T(8,128)S(1)} %copy-done, f32[8,32,32]{2,1,0:T(8,128)S(1)} %copy-done.1), custom_call_target="tpu_custom_call" | custom-call | tf_op jit(solution)/shard_map/pallas_call | solution.py:570
  (38 shorter events, 4.2 us)
Async XLA Ops:
  2.6 8.5 %copy-start.8 = (s32[1024]{0:T(1024)S(1)}, s32[1024]{0:T(1024)}, u32[]{:S(2)}) copy-start(s32[1024]{0:T(1024)} %param.14) | copy-start | bytes 12292
  2.6 12.6 %collective-permute-start = (f32[3,8,32,128]{3,2,1,0:T(8,128)}, f32[3,8,32,128]{3,2,1,0:T(8,128)S(1)}, u32[]{:S(2)}, u32[]{:S(2)}) collective-permute-start(f32[3,8,32,128]{3,2,1,0:T(8,128)} %get-tuple-element.26), channel_id=1, source_target_pairs={{0,4},{4,0},{1,5},{5,1},{2,6},{6,2},{3,7},{7,3},{8,12},{12,8},{9,1... | collective-permute-start | bytes 1179656 | tf_op jit(solution)/shard_map/ppermute | solution.py:597
  5.6 7.7 %collective-permute-start.1 = (f32[2,2,32,128]{3,2,1,0:T(8,128)}, f32[2,2,32,128]{3,2,1,0:T(8,128)S(1)}, u32[]{:S(2)}, u32[]{:S(2)}) collective-permute-start(f32[2,2,32,128]{3,2,1,0:T(8,128)} %get-tuple-element.27), channel_id=1, source_target_pairs={{0,8},{8,16},{16,24},{24,0},{1,9},{9,17},{17,25},{25,1},{2,10},{10... | collective-permute-start | bytes 196616 | tf_op jit(solution)/shard_map/ppermute | solution.py:603
  7.2 7.6 %collective-permute-start.2 = (f32[2,2,32,128]{3,2,1,0:T(8,128)}, f32[2,2,32,128]{3,2,1,0:T(8,128)S(1)}, u32[]{:S(2)}, u32[]{:S(2)}) collective-permute-start(f32[2,2,32,128]{3,2,1,0:T(8,128)} %get-tuple-element.27), channel_id=1, source_target_pairs={{0,16},{8,24},{16,0},{24,8},{1,17},{9,25},{17,1},{25,9},{2,18},{10... | collective-permute-start | bytes 196616 | tf_op jit(solution)/shard_map/ppermute | solution.py:603
  9.8 5.0 %collective-permute-start.3 = (f32[2,2,32,128]{3,2,1,0:T(8,128)}, f32[2,2,32,128]{3,2,1,0:T(8,128)S(1)}, u32[]{:S(2)}, u32[]{:S(2)}) collective-permute-start(f32[2,2,32,128]{3,2,1,0:T(8,128)} %get-tuple-element.27), channel_id=1, source_target_pairs={{0,24},{8,0},{16,8},{24,16},{1,25},{9,1},{17,9},{25,17},{2,26},{10... | collective-permute-start | bytes 196616 | tf_op jit(solution)/shard_map/ppermute | solution.py:603
  11.1 3.6 %copy-start = (f32[8,32,32]{2,1,0:T(8,128)S(1)}, f32[8,32,32]{2,1,0:T(8,128)}, u32[]{:S(2)}) copy-start(f32[8,32,32]{2,1,0:T(8,128)} %vk.5) | copy-start | bytes 98308
  11.1 3.6 %copy-start.1 = (f32[8,32,32]{2,1,0:T(8,128)S(1)}, f32[8,32,32]{2,1,0:T(8,128)}, u32[]{:S(2)}) copy-start(f32[8,32,32]{2,1,0:T(8,128)} %va.5) | copy-start | bytes 98308
  13.2 2.0 %copy-start.2 = (f32[4,8,32,128]{3,2,1,0:T(8,128)S(1)}, f32[4,8,32,128]{3,2,1,0:T(8,128)}, u32[]{:S(2)}) copy-start(f32[4,8,32,128]{3,2,1,0:T(8,128)} %refs_0_.3) | copy-start | bytes 1572868
  13.2 2.0 %copy-start.3 = (s32[8,32,128]{2,1,0:T(8,128)S(1)}, s32[8,32,128]{2,1,0:T(8,128)}, u32[]{:S(2)}) copy-start(s32[8,32,128]{2,1,0:T(8,128)} %refs_1_.3) | copy-start | bytes 393220
  15.9 9.6 %collective-permute-start.4 = (f32[2,16,32,128]{3,2,1,0:T(8,128)S(1)}, f32[2,16,32,128]{3,2,1,0:T(8,128)S(1)}, u32[]{:S(2)}, u32[]{:S(2)}) collective-permute-start(f32[2,16,32,128]{3,2,1,0:T(8,128)S(1)} %get-tuple-element.29.fields), channel_id=1, source_target_pairs={{0,1},{1,0},{2,3},{3,2},{4,5},{5,4},{6,7},{7,6},{8,9},{9,8},{10,11... | collective-permute-start | bytes 1572872 | tf_op jit(solution)/shard_map/ppermute | solution.py:600
  16.0 8.7 %collective-permute-start.7 = (f32[2,8,32,128]{3,2,1,0:T(8,128)S(1)}, f32[2,8,32,128]{3,2,1,0:T(8,128)S(1)}, u32[]{:S(2)}, u32[]{:S(2)}) collective-permute-start(f32[2,8,32,128]{3,2,1,0:T(8,128)S(1)} %shard_map.123.refs_3_.refs_0_), channel_id=1, source_target_pairs={{0,4},{4,0},{1,5},{5,1},{2,6},{6,2},{3,7},{7,3},{8,12},{12,8},{9,1... | collective-permute-start | bytes 786440 | tf_op jit(solution)/shard_map/ppermute | solution.py:597
  17.4 7.3 %collective-permute-start.5 = (f32[2,16,8,128]{3,2,1,0:T(8,128)S(1)}, f32[2,16,8,128]{3,2,1,0:T(8,128)S(1)}, u32[]{:S(2)}, u32[]{:S(2)}) collective-permute-start(f32[2,16,8,128]{3,2,1,0:T(8,128)S(1)} %get-tuple-element.30), channel_id=1, source_target_pairs={{1,2},{2,1},{5,6},{6,5},{9,10},{10,9},{13,14},{14,13},{17,18},{18,... | collective-permute-start | bytes 393224 | tf_op jit(solution)/shard_map/ppermute | solution.py:626
  18.1 7.4 %collective-permute-start.6 = (f32[2,16,8,128]{3,2,1,0:T(8,128)S(1)}, f32[2,16,8,128]{3,2,1,0:T(8,128)S(1)}, u32[]{:S(2)}, u32[]{:S(2)}) collective-permute-start(f32[2,16,8,128]{3,2,1,0:T(8,128)S(1)} %get-tuple-element.31), channel_id=1, source_target_pairs={{1,3},{2,0},{5,7},{6,4},{9,11},{10,8},{13,15},{14,12},{17,19},{18,... | collective-permute-start | bytes 393224 | tf_op jit(solution)/shard_map/ppermute | solution.py:626
  25.5 8.6 %collective-permute-start.8 = (f32[2,16,32,128]{3,2,1,0:T(8,128)S(1)}, f32[2,16,32,128]{3,2,1,0:T(8,128)S(1)}, u32[]{:S(2)}, u32[]{:S(2)}) collective-permute-start(f32[2,16,32,128]{3,2,1,0:T(8,128)S(1)} %get-tuple-element.38.fields), channel_id=1, source_target_pairs={{0,1},{1,0},{2,3},{3,2},{4,5},{5,4},{6,7},{7,6},{8,9},{9,8},{10,11... | collective-permute-start | bytes 1572872 | tf_op jit(solution)/shard_map/ppermute | solution.py:600
  25.6 2.0 %copy-start.6 = (f32[16]{0:T(128)S(1)}, f32[16]{0:T(128)}, u32[]{:S(2)}) copy-start(f32[16]{0:T(128)} %kap_table.1) | copy-start | bytes 196
  25.6 2.0 %copy-start.7 = (f32[16]{0:T(128)S(1)}, f32[16]{0:T(128)}, u32[]{:S(2)}) copy-start(f32[16]{0:T(128)} %abs_table.1) | copy-start | bytes 196
  25.6 4.9 %collective-permute-start.9 = (f32[2,16,8,128]{3,2,1,0:T(8,128)S(1)}, f32[2,16,8,128]{3,2,1,0:T(8,128)S(1)}, u32[]{:S(2)}, u32[]{:S(2)}) collective-permute-start(f32[2,16,8,128]{3,2,1,0:T(8,128)S(1)} %get-tuple-element.39), channel_id=1, source_target_pairs={{1,2},{2,1},{5,6},{6,5},{9,10},{10,9},{13,14},{14,13},{17,18},{18,... | collective-permute-start | bytes 393224 | tf_op jit(solution)/shard_map/ppermute | solution.py:626
  26.3 7.8 %collective-permute-start.10 = (f32[2,16,8,128]{3,2,1,0:T(8,128)S(1)}, f32[2,16,8,128]{3,2,1,0:T(8,128)S(1)}, u32[]{:S(2)}, u32[]{:S(2)}) collective-permute-start(f32[2,16,8,128]{3,2,1,0:T(8,128)S(1)} %get-tuple-element.39), channel_id=1, source_target_pairs={{1,3},{2,0},{5,7},{6,4},{9,11},{10,8},{13,15},{14,12},{17,19},{18,... | collective-permute-start | bytes 393224 | tf_op jit(solution)/shard_map/ppermute | solution.py:626
  38.9 4.5 %collective-permute-start.11 = (f32[20,8,128]{2,1,0:T(8,128)S(1)}, f32[20,8,128]{2,1,0:T(8,128)S(1)}, u32[]{:S(2)}, u32[]{:S(2)}) collective-permute-start(f32[20,8,128]{2,1,0:T(8,128)S(1)} %get-tuple-element.41.sent), channel_id=1, source_target_pairs={{0,2},{1,3},{2,0},{3,1},{4,6},{5,7},{6,4},{7,5},{8,10},{9,11},{10,... | collective-permute-start | bytes 245768 | tf_op jit(solution)/shard_map/ppermute | solution.py:654
  48.3 2.0 %collective-permute-start.12 = (f32[2,16,32,128]{3,2,1,0:T(8,128)S(1)}, f32[2,16,32,128]{3,2,1,0:T(8,128)S(1)}, u32[]{:S(2)}, u32[]{:S(2)}) collective-permute-start(f32[2,16,32,128]{3,2,1,0:T(8,128)S(1)} %get-tuple-element.43), channel_id=1, source_target_pairs={{0,1},{1,0},{2,3},{3,2},{4,5},{5,4},{6,7},{7,6},{8,9},{9,8},{10,11... | collective-permute-start | bytes 1572872 | tf_op jit(solution)/shard_map/ppermute | solution.py:600
  50.4 8.4 %collective-permute-start.13 = (f32[2,8,32,128]{3,2,1,0:T(8,128)S(1)}, f32[2,8,32,128]{3,2,1,0:T(8,128)S(1)}, u32[]{:S(2)}, u32[]{:S(2)}) collective-permute-start(f32[2,8,32,128]{3,2,1,0:T(8,128)S(1)} %get-tuple-element.45), channel_id=1, source_target_pairs={{0,4},{4,0},{1,5},{5,1},{2,6},{6,2},{3,7},{7,3},{8,12},{12,8},{9,1... | collective-permute-start | bytes 786440 | tf_op jit(solution)/shard_map/ppermute | solution.py:597
  59.8 13.4 %copy-start.4 = (f32[8,32,32]{2,1,0:T(8,128)S(1)}, f32[8,32,32]{2,1,0:T(8,128)}, u32[]{:S(2)}) copy-start(f32[8,32,32]{2,1,0:T(8,128)} %qk.1) | copy-start | bytes 98308
  59.8 13.4 %copy-start.5 = (f32[8,32,32]{2,1,0:T(8,128)S(1)}, f32[8,32,32]{2,1,0:T(8,128)}, u32[]{:S(2)}) copy-start(f32[8,32,32]{2,1,0:T(8,128)} %qa.1) | copy-start | bytes 98308
  59.8 13.3 %all-to-all-start = ((f32[4,2,2,32,128]{4,3,2,1,0:T(8,128)}), f32[4,2,2,32,128]{4,3,2,1,0:T(8,128)S(1)}, u32[]{:S(2)}, u32[]{:S(2)}) async-start(f32[4,2,2,32,128]{4,3,2,1,0:T(8,128)} %shard_map.130), calls=%async_computation | async-start | bytes 524288 | tf_op jit(solution)/shard_map/all_to_all | solution.py:665

commit v5 on v3

--- a/solution.py
+++ b/solution.py
@@ -185,6 +185,11 @@
     return jnp.where(at == edge, 0.0, shifted(value, -step, axis))
 
 
+def packed_planes(ref, q):
+    per = 128 // ref.shape[2]
+    return jnp.concatenate([ref[per * q + j] for j in range(per)], axis=1)
+
+
 def pack_kernel(bg, labels, vk, va, packed, message, raw, v_in, sems):
     _, x, _, _ = places(2)
     half = bg.shape[0] // 2
@@ -199,11 +204,10 @@
     ]
     for copy in copies:
         copy.start()
-    per = 128 // vk.shape[2]
     for f in range(2):
         copies[f].wait()
-        for q in range(vk.shape[0] // per):
-            packed[f, q] = jnp.concatenate([v_in[f, per * q + j] for j in range(per)], axis=1)
+        for q in range(packed.shape[1]):
+            packed[f, q] = packed_planes(v_in.at[f], q)
     copies[3].wait()
     message[half] = raw[...].astype(jnp.float32)
     copies[2].wait()
@@ -232,10 +236,10 @@
     lax.fori_loop(0, planes // 2, body, 0)
 
 
-def photon_kernel(bg, labels, msg, mine, fields, edge_other, edge_mine, raw, sems):
-    _, x, y, c = places(2)
+def photon_kernel(bg, labels, msg, mine, fields, raw, sems):
+    _, x, _, c = places(2)
     half = bg.shape[0] // 2
-    cx, cy, _ = labels.shape
+    cx = labels.shape[0]
     here, there = cx * x, cx * (1 - x)
     copies = [
         pltpu.make_async_copy(src, dst, sems.at[i])
@@ -253,15 +257,11 @@
     for copy in copies:
         copy.wait()
     fields[1, pl.ds(here, cx)] = raw[...].astype(jnp.float32)
-    halo = edge_mine.shape[2]
-    first = (cy - halo) * (1 - y)
-    edge_other[...] = fields[:, :, pl.ds(first, halo), :]
-    edge_mine[0] = mine[:, pl.ds(first, halo), :]
-    edge_mine[1] = fields[1, :, pl.ds(first, halo), :]
-
-
-def unpack_kernel(*refs, n):
-    own, parts, full = refs[:2], refs[2 : n + 1], refs[-1]
+
+
+def unpack_kernel(*refs):
+    own, parts, full = refs[:2], refs[2:-1], refs[-1]
+    n = len(parts) + 1
     s, _, _, _ = places(2)
     slab = 128 // n
     _, cx, cy, _ = full.shape
@@ -278,14 +278,29 @@
                 full[f, n * q + j] = plane
 
 
-def vector_kernel(own, came, fields, edge):
-    _, x, y, _ = places(2)
-    cx, cy = own.shape[1:3]
+def vector_kernel(own, came, fields):
+    _, x, _, _ = places(2)
+    cx = own.shape[1]
+    fields[:, pl.ds(cx * x, cx)] = own[...]
+    fields[:, pl.ds(cx * (1 - x), cx)] = came[...]
+
+
+def edge_rows(ref, halo, y):
+    return ref[pl.ds(0, ref.shape[0]), pl.ds((ref.shape[1] - halo) * (1 - y), halo), :]
+
+
+def photon_edge_kernel(mine, fields, got, edge):
+    _, _, y, c = places(2)
     halo = edge.shape[2]
-    first = (cy - halo) * (1 - y)
-    for start, part in ((cx * x, own), (cx * (1 - x), came)):
-        fields[:, pl.ds(start, cx)] = part[...]
-        edge[:, pl.ds(start, cx)] = part[:, :, pl.ds(first, halo), :]
+    edge[0] = jnp.where(c != y, edge_rows(mine, halo, y), edge_rows(got.at[0], halo, y))
+    edge[1] = jnp.where(c != y, edge_rows(fields.at[1], halo, y), edge_rows(got.at[1], halo, y))
+
+
+def vector_edge_kernel(fields, got, edge):
+    _, _, y, c = places(2)
+    halo = edge.shape[2]
+    for f in range(2):
+        edge[f] = jnp.where(c != y, edge_rows(fields.at[f], halo, y), edge_rows(got.at[f], halo, y))
 
 
 def solve(b, bufs, diag, fx, fy, fz, unroll):
@@ -314,12 +329,12 @@
 
 
 def framed(ref, shift, parts, planes, cy, halo, y, c):
-    own, got, edge_a, edge_b = parts
+    own, got, edge = parts
     there = pl.ds(shift, planes)
     base = halo * y
     ref[there, pl.ds(base + cy * c, cy), :] = own
     ref[there, pl.ds(base + cy * (1 - c), cy), :] = got
-    ref[there, pl.ds(2 * cy * (1 - y), halo), :] = edge_a + edge_b
+    ref[there, pl.ds(2 * cy * (1 - y), halo), :] = edge
 
 
 def blank_ends(*refs):
@@ -335,17 +350,17 @@
 
 
 def stencil_kernel(
-    kap_table, abs_table, mine, fields, got, edge_other, edge_mine, count,
+    kap_table, abs_table, mine, fields, got, edge, count,
     phi, diag, fx, fy, fz, sums,
     labels, kap,
 ):
     _, _, y, c = places(2)
     planes, cy, lanes = mine.shape
-    halo = edge_mine.shape[2]
+    halo = edge.shape[2]
     rows = 2 * cy + halo
     place = (planes, cy, halo, y, c)
-    framed(phi, 1, (mine[...], got[0], edge_other[0], edge_mine[0]), *place)
-    framed(labels, 0, (fields[1], got[1], edge_other[1], edge_mine[1]), *place)
+    framed(phi, 1, (mine[...], got[0], edge[0]), *place)
+    framed(labels, 0, (fields[1], got[1], edge[1]), *place)
     blank_ends(phi, kap)
     blank = jnp.zeros((rows, lanes), jnp.float32)
     lane = index_along((rows, lanes), 1)
@@ -382,17 +397,17 @@
 
 
 def first_kernel(
-    phi, diag, fx, fy, fz, count, sums, fields, got, edge_a, edge_b,
+    phi, diag, fx, fy, fz, count, sums, fields, got, edge,
     change, message,
     vk, va, b, buf_a, buf_b,
 ):
     _, _, y, c = places(2)
     planes, rows, lanes = change.shape
-    halo = edge_a.shape[2]
+    halo = edge.shape[2]
     cy = (rows - halo) // 2
     place = (planes, cy, halo, y, c)
-    framed(vk, 1, (fields[0], got[0], edge_a[0], edge_b[0]), *place)
-    framed(va, 0, (fields[1], got[1], edge_a[1], edge_b[1]), *place)
+    framed(vk, 1, (fields[0], got[0], edge[0]), *place)
+    framed(va, 0, (fields[1], got[1], edge[1]), *place)
     blank_ends(vk, buf_a, buf_b)
     theta, _ = chebyshev_scalars()
 
@@ -540,11 +555,8 @@
     tile[...] = jnp.where(lane == me, values, 0.0)
 
 
-def final_kernel(*refs, cells):
-    tiles, (w_k, w_a, vk, va, next_k, next_a, coefs) = refs[:-7], refs[-7:]
-    tile = tiles[0][...]
-    for other in tiles[1:]:
-        tile = tile + other[...]
+def final_kernel(tiles, w_k, w_a, vk, va, next_k, next_a, coefs, *, cells):
+    tile = jnp.sum(tiles[...], axis=0)
     wv, vv, a, uv, uu = (tile[i : i + 1] for i in range(5))
     wv_sum = jnp.sum(wv, axis=1, keepdims=True)
     vv_sum = jnp.sum(vv, axis=1, keepdims=True)
@@ -625,41 +637,37 @@
         (f32(planes, rows, cz),), det_cells.reshape(1, dets),
         cost=pl.CostEstimate(flops=2 * planes * rows * cz * dets, bytes_accessed=planes * rows * cz * 4, transcendentals=0),
     )
-    (vector,) = run(
-        functools.partial(unpack_kernel, n=n), (f32(2, *block),), v_kappa, v_absorb, *slabs, after=(count,)
-    )
-    vector_came = swap_x(vector)
-
-    def to_edges(edge_other, edge_mine):
-        return lax.ppermute(edge_other, "gy", [(1, 2), (2, 1)]), lax.ppermute(edge_mine, "gy", [(1, 3), (2, 0)])
-
-    mine, fields, edge_other, edge_mine = run(
-        photon_kernel,
-        (f32(planes, cy, cz), f32(2, planes, cy, cz), f32(2, planes, HALO, cz), f32(2, planes, HALO, cz)),
-        background, labels, came, after=(vector,), hbm=(0, 1), scratch=(raw_labels,), copies=3,
-    )
-    edges = to_edges(edge_other, edge_mine)
+
+    def across_y(value):
+        return lax.ppermute(value, "gy", [(i, (i + 2) % 4) for i in range(4)])
+
+    edges = (f32(2, planes, HALO, cz),)
+    (half_vector,) = run(unpack_kernel, (f32(2, *block),), v_kappa, v_absorb, *slabs, after=(count,))
+    half_came = swap_x(half_vector)
+    mine, fields = run(
+        photon_kernel, (f32(planes, cy, cz), f32(2, planes, cy, cz)),
+        background, labels, came, after=(half_vector,), hbm=(0, 1), scratch=(raw_labels,), copies=3,
+    )
     got = swap_core(fields)
+    (sent,) = run(photon_edge_kernel, edges, mine, fields, got)
+    halo = across_y(sent)
+    (vector,) = run(vector_kernel, (f32(2, planes, cy, cz),), half_vector, half_came, after=(halo,))
+    vector_got = swap_core(vector)
+    (vector_sent,) = run(vector_edge_kernel, edges, vector, vector_got)
     frame, wide = (planes, rows, cz), (planes + 2, rows, cz)
     float_frame, float_wide = float_block(*frame), float_block(*wide)
     phi, diag, fx, fy, fz, sums = run(
         stencil_kernel,
         (f32(*wide), f32(*frame), f32(planes + 1, rows, cz), f32(*frame), f32(*frame), f32(2, 8, cz)),
-        kappa_table, absorb_table, mine, fields, got, *edges, count,
+        kappa_table, absorb_table, mine, fields, got, halo, count, after=(vector_sent,),
         smem=(0, 1), scratch=(float_frame, float_wide),
     )
-    fields, edge = run(
-        vector_kernel, (f32(2, planes, cy, cz), f32(2, planes, HALO, cz)), vector, vector_came,
-        after=(got, *edges),
-    )
-    edges = to_edges(edge, edge)
-    got = swap_core(fields)
     change, sent = run(
         first_kernel, (f32(*frame), f32(planes + 4, HALO, cz)),
-        phi, diag, fx, fy, fz, count, sums, fields, got, *edges,
+        phi, diag, fx, fy, fz, count, sums, vector, vector_got, across_y(vector_sent),
         scratch=(float_wide, float_frame, float_frame, float_wide, float_wide),
     )
-    heard = lax.ppermute(sent, "gy", [(i, (i + 2) % 4) for i in range(4)])
+    heard = across_y(sent)
     own, message = run(
         functools.partial(second_kernel, dets=dets),
         (f32(2, planes, cy, cz), f32(2, planes, cy, cz)),
@@ -678,17 +686,12 @@
         (f32(*v_kappa.shape), f32(*v_kappa.shape), f32(8, 128)),
         beta_prev.reshape(1, 1), *parts, v_kappa, v_absorb, q_kappa, q_absorb,
     )
-    tile = tile + sum(along_z(tile, k) for k in range(1, n))
-    over_x, over_core = swap_x(tile), swap_core(tile)
-    over_both = lax.ppermute(
-        tile, ("gx", "gy"), [(4 * a + b, 4 * (1 - a) + (b ^ 1)) for a in range(2) for b in range(4)]
-    )
-    tile = tile + over_x + over_core + over_both
-    over_y = lax.ppermute(tile, "gy", [(i, (i + 2) % 4) for i in range(4)])
+    everyone = ("src", "gx", "gy")
+    tiles = lax.all_to_all(jnp.broadcast_to(tile, (8 * n, 8, 128)), everyone, 0, 0)
     return tuple(run(
         functools.partial(final_kernel, cells=cells),
         (f32(*v_kappa.shape), f32(*v_kappa.shape), f32(2)),
-        tile, over_y, w_k, w_a, v_kappa, v_absorb, in_smem_out=(2,),
+        tiles, w_k, w_a, v_kappa, v_absorb, in_smem_out=(2,),
     ))
 
 

time: 84.7 us -> 81.1 us (0.957)
  blocking collectives: 0 us -> 13.1 us
  starting transfers between devices: 30.9 us -> 21.9 us
  waiting for transfers between devices: 32.3 us -> 24.6 us
    all_to_all x0 -> x1, blocking collectives: none -> 13.1 us  [per_device_paired(): lax.all_to_all(jnp.broadcast_to(tile, (8 * n, 8, 128)), everyone, 0, 0)]
    ppermute x7 -> x3, starting transfers between devices: 10.3 us -> 4.75 us  [across_y(): return lax.ppermute(value, 'gy', [(i, (i + 2) % 4) for i in range(4)])]
    ppermute x7 -> x3, waiting for transfers between devices: 8.37 us -> 4.06 us  [across_y(): return lax.ppermute(value, 'gy', [(i, (i + 2) % 4) for i in range(4)])]
    ppermute x9 -> x6, starting transfers between devices: 15.1 us -> 11 us  [along_z(): return lax.ppermute(value, 'src', [(i, (i + k) % n) for i in range(n)])]
    ppermute x9 -> x6, waiting for transfers between devices: 7.23 us -> 4.12 us  [along_z(): return lax.ppermute(value, 'src', [(i, (i + k) % n) for i in range(n)])]
    ppermute x4 -> x3, waiting for transfers between devices: 14.9 us -> 12.2 us  [swap_x(): return lax.ppermute(value, 'gx', [(0, 1), (1, 0)])]
    ppermute x4 -> x3, waiting for transfers between devices: 1.79 us -> 4.23 us  [swap_core(): return lax.ppermute(value, 'gy', [(0, 1), (1, 0), (2, 3), (3, 2)])]
    ppermute x4 -> x3, starting transfers between devices: 5.18 us -> 5.92 us  [swap_x(): return lax.ppermute(value, 'gx', [(0, 1), (1, 0)])]
  transfers between devices with their start and end apart: 24 -> 15, of which waited for: 14 -> 11; matrix products, arithmetic and copies ran while one was open for 0% -> 0% of each run, Pallas kernels for 6% -> 7%
where the time goes in v5:
time: 81.1 us; the launch traced here: 80.9 us
  waiting for transfers between devices  24.6 us (30%)
  starting transfers between devices  21.9 us (27%)
  Pallas kernels  19.9 us (25%)
  blocking collectives  13.1 us (16%)
  between operations  1.48 us (2%)
    pallas_call x14, Pallas kernels, run(): pl.pallas_call(body if waits else kernel, out_shape=tuple(outs), in_specs...  19.9 us
    all_to_all x1, blocking collectives, per_device_paired(): lax.all_to_all(jnp.broadcast_to(tile, (8 * n, 8, 128)), everyone, 0, 0)  13.1 us
    ppermute x3, waiting for transfers between devices, swap_x(): return lax.ppermute(value, 'gx', [(0, 1), (1, 0)])  12.2 us
    ppermute x6, starting transfers between devices, along_z(): return lax.ppermute(value, 'src', [(i, (i + k) % n) for i in range(n)])  11 us
    ppermute x3, starting transfers between devices, swap_x(): return lax.ppermute(value, 'gx', [(0, 1), (1, 0)])  5.92 us
    ppermute x3, starting transfers between devices, across_y(): return lax.ppermute(value, 'gy', [(i, (i + 2) % 4) for i in range(4)])  4.75 us
    ppermute x3, waiting for transfers between devices, swap_core(): return lax.ppermute(value, 'gy', [(0, 1), (1, 0), (2, 3), (3, 2)])  4.23 us
    ppermute x6, waiting for transfers between devices, along_z(): return lax.ppermute(value, 'src', [(i, (i + k) % n) for i in range(n)])  4.12 us
  transfers between devices with their start and end apart: 15, of which 11 were waited for; matrix products, arithmetic and copies ran while one was open for 0% of the time, Pallas kernels for 7%

profile of v5, /device:TPU:0, one launch (start us, length us, event | category | flops | bytes accessed | tf_op | source)
XLA Modules:
  0.0 80.9 jit_solution(1095368219307101027)
XLA Ops:
  0.6 1.9 %shard_map.121 = (f32[2,2,32,128]{3,2,1,0:T(8,128)}, f32[3,8,32,128]{3,2,1,0:T(8,128)}) custom-call(f32[4,8,32,128]{3,2,1,0:T(8,128)} %refs_0_.4, s32[8,32,128]{2,1,0:T(8,128)} %refs_1_.4, f32[8,32,32]{2,1,0:T(8,128)} %vk.3, f32[8,32,32]{2,1,0:T(8,128)} %va.3), custom_call_target="tpu_custom_call" | custom-call | tf_op jit(solution)/shard_map/pallas_call | solution.py:590
  2.6 3.0 %collective-permute-start = (f32[3,8,32,128]{3,2,1,0:T(8,128)}, f32[3,8,32,128]{3,2,1,0:T(8,128)S(1)}, u32[]{:S(2)}, u32[]{:S(2)}) collective-permute-start(f32[3,8,32,128]{3,2,1,0:T(8,128)} %get-tuple-element.26), channel_id=1, source_target_pairs={{0,4},{4,0},{1,5},{5,1},{2,6},{6,2},{3,7},{7,3},{8,12},{12,8},{9,1... | collective-permute-start | bytes 1179656 | tf_op jit(solution)/shard_map/ppermute | solution.py:617
  5.6 1.6 %collective-permute-start.1 = (f32[2,2,32,128]{3,2,1,0:T(8,128)}, f32[2,2,32,128]{3,2,1,0:T(8,128)S(1)}, u32[]{:S(2)}, u32[]{:S(2)}) collective-permute-start(f32[2,2,32,128]{3,2,1,0:T(8,128)} %get-tuple-element.27), channel_id=1, source_target_pairs={{0,8},{8,16},{16,24},{24,0},{1,9},{9,17},{17,25},{25,1},{2,10},{10... | collective-permute-start | bytes 196616 | tf_op jit(solution)/shard_map/ppermute | solution.py:623
  7.2 2.6 %collective-permute-start.2 = (f32[2,2,32,128]{3,2,1,0:T(8,128)}, f32[2,2,32,128]{3,2,1,0:T(8,128)S(1)}, u32[]{:S(2)}, u32[]{:S(2)}) collective-permute-start(f32[2,2,32,128]{3,2,1,0:T(8,128)} %get-tuple-element.27), channel_id=1, source_target_pairs={{0,16},{8,24},{16,0},{24,8},{1,17},{9,25},{17,1},{25,9},{2,18},{10... | collective-permute-start | bytes 196616 | tf_op jit(solution)/shard_map/ppermute | solution.py:623
  9.8 1.3 %collective-permute-start.3 = (f32[2,2,32,128]{3,2,1,0:T(8,128)}, f32[2,2,32,128]{3,2,1,0:T(8,128)S(1)}, u32[]{:S(2)}, u32[]{:S(2)}) collective-permute-start(f32[2,2,32,128]{3,2,1,0:T(8,128)} %get-tuple-element.27), channel_id=1, source_target_pairs={{0,24},{8,0},{16,8},{24,16},{1,25},{9,1},{17,9},{25,17},{2,26},{10... | collective-permute-start | bytes 196616 | tf_op jit(solution)/shard_map/ppermute | solution.py:623
  11.1 2.1 %shard_map.122.refs_5_.refs_6_.count = f32[16,72,128]{2,1,0:T(8,128)S(1)} custom-call(s32[1,1024]{1,0:T(1,128)S(1)} %bitcast.3), custom_call_target="tpu_custom_call" | custom-call | flops 301989888 | bytes 589824 | tf_op jit(solution)/shard_map/pallas_call | solution.py:590
  13.3 1.5 %collective-permute-done.2.refs_3_ = f32[2,2,32,128]{3,2,1,0:T(8,128)S(1)} collective-permute-done((f32[2,2,32,128]{3,2,1,0:T(8,128)}, f32[2,2,32,128]{3,2,1,0:T(8,128)S(1)}, u32[]{:S(2)}, u32[]{:S(2)}) %collective-permute-start.2) | collective-permute-done | bytes 65568 | tf_op jit(solution)/shard_map/ppermute | solution.py:623
  15.9 1.5 %collective-permute-start.6 = (f32[2,8,32,128]{3,2,1,0:T(8,128)S(1)}, f32[2,8,32,128]{3,2,1,0:T(8,128)S(1)}, u32[]{:S(2)}, u32[]{:S(2)}) collective-permute-start(f32[2,8,32,128]{3,2,1,0:T(8,128)S(1)} %shard_map.123.refs_3_.refs_0_), channel_id=1, source_target_pairs={{0,4},{4,0},{1,5},{5,1},{2,6},{6,2},{3,7},{7,3},{8,12},{12,8},{9,1... | collective-permute-start | bytes 786440 | tf_op jit(solution)/shard_map/ppermute | solution.py:617
  17.9 1.6 %collective-permute-start.5 = (f32[2,16,8,128]{3,2,1,0:T(8,128)S(1)}, f32[2,16,8,128]{3,2,1,0:T(8,128)S(1)}, u32[]{:S(2)}, u32[]{:S(2)}) collective-permute-start(f32[2,16,8,128]{3,2,1,0:T(8,128)S(1)} %shard_map.125), channel_id=1, source_target_pairs={{0,2},{1,3},{2,0},{3,1},{4,6},{5,7},{6,4},{7,5},{8,10},{9,11},{10,... | collective-permute-start | bytes 393224 | tf_op jit(solution)/shard_map/ppermute | solution.py:642
  19.5 5.2 %collective-permute-done.6.refs_1_ = f32[2,8,32,128]{3,2,1,0:T(8,128)S(1)} collective-permute-done((f32[2,8,32,128]{3,2,1,0:T(8,128)S(1)}, f32[2,8,32,128]{3,2,1,0:T(8,128)S(1)}, u32[]{:S(2)}, u32[]{:S(2)}) %collective-permute-start.6) | collective-permute-done | bytes 262176 | tf_op jit(solution)/shard_map/ppermute | solution.py:617
  24.8 1.9 %collective-permute-done.7.got = f32[2,16,32,128]{3,2,1,0:T(8,128)S(1)} collective-permute-done((f32[2,16,32,128]{3,2,1,0:T(8,128)S(1)}, f32[2,16,32,128]{3,2,1,0:T(8,128)S(1)}, u32[]{:S(2)}, u32[]{:S(2)}) %collective-permute-start.7) | collective-permute-done | bytes 524320 | tf_op jit(solution)/shard_map/ppermute | solution.py:620
  26.8 1.6 %collective-permute-start.8 = (f32[2,16,8,128]{3,2,1,0:T(8,128)S(1)}, f32[2,16,8,128]{3,2,1,0:T(8,128)S(1)}, u32[]{:S(2)}, u32[]{:S(2)}) collective-permute-start(f32[2,16,8,128]{3,2,1,0:T(8,128)S(1)} %shard_map.127.refs_7_), channel_id=1, source_target_pairs={{0,2},{1,3},{2,0},{3,1},{4,6},{5,7},{6,4},{7,5},{8,10},{9,11},{10,... | collective-permute-start | bytes 393224 | tf_op jit(solution)/shard_map/ppermute | solution.py:642
  28.3 2.9 %shard_map.128 = (f32[18,72,128]{2,1,0:T(8,128)S(1)}, f32[16,72,128]{2,1,0:T(8,128)S(1)}, f32[17,72,128]{2,1,0:T(8,128)S(1)}, f32[16,72,128]{2,1,0:T(8,128)S(1)}...) custom-call(f32[16]{0:T(128)S(1)} %copy-done.6, f32[16]{0:T(128)S(1)} %copy-done.7, ...), custom_call_target="tpu_custom_call" | custom-call | tf_op jit(solution)/shard_map/pallas_call | solution.py:590
  32.4 4.9 %shard_map.129 = (f32[16,72,128]{2,1,0:T(8,128)S(1)}, f32[20,8,128]{2,1,0:T(8,128)S(1)}) custom-call(f32[18,72,128]{2,1,0:T(8,128)S(1)} %get-tuple-element.30.phi, f32[16,72,128]{2,1,0:T(8,128)S(1)} %get-tuple-element.31.diag, f32[17,72,128]{2,1,0:T(8,128)S(1)} %get-tuple-element.32.fx, f32[16,72,128]{2,1,0:T(8,128)S(1)} %get-tuple-element.33.fy, ...), custom_call_target="tpu_custom_call" | custom-call | tf_op jit(solution)/shard_map/pallas_call | solution.py:590
  37.2 1.6 %collective-permute-start.9 = (f32[20,8,128]{2,1,0:T(8,128)S(1)}, f32[20,8,128]{2,1,0:T(8,128)S(1)}, u32[]{:S(2)}, u32[]{:S(2)}) collective-permute-start(f32[20,8,128]{2,1,0:T(8,128)S(1)} %get-tuple-element.37.sent), channel_id=1, source_target_pairs={{0,2},{1,3},{2,0},{3,1},{4,6},{5,7},{6,4},{7,5},{8,10},{9,11},{10,... | collective-permute-start | bytes 245768 | tf_op jit(solution)/shard_map/ppermute | solution.py:642
  38.8 2.9 %collective-permute-done.9.came = f32[20,8,128]{2,1,0:T(8,128)S(1)} collective-permute-done((f32[20,8,128]{2,1,0:T(8,128)S(1)}, f32[20,8,128]{2,1,0:T(8,128)S(1)}, u32[]{:S(2)}, u32[]{:S(2)}) %collective-permute-start.9) | collective-permute-done | bytes 81952 | tf_op jit(solution)/shard_map/ppermute | solution.py:642
  41.7 4.9 %shard_map.130 = (f32[2,16,32,128]{3,2,1,0:T(8,128)S(1)}, f32[2,16,32,128]{3,2,1,0:T(8,128)S(1)}) custom-call(f32[18,72,128]{2,1,0:T(8,128)S(1)} %get-tuple-element.30.phi, f32[16,72,128]{2,1,0:T(8,128)S(1)} %get-tuple-element.36.change, f32[16,72,128]{2,1,0:T(8,128)S(1)} %get-tuple-element.31.diag, f32[17,72,128]{2,1,0:T(8,128)S(1)} %get-tuple-element.32.fx, ...), custom_call_target="tpu_custom_call" | custom-call | tf_op jit(solution)/shard_map/pallas_call | solution.py:590
  46.7 1.9 %collective-permute-done.10.came = f32[2,16,32,128]{3,2,1,0:T(8,128)S(1)} collective-permute-done((f32[2,16,32,128]{3,2,1,0:T(8,128)S(1)}, f32[2,16,32,128]{3,2,1,0:T(8,128)S(1)}, u32[]{:S(2)}, u32[]{:S(2)}) %collective-permute-start.10) | collective-permute-done | bytes 524320 | tf_op jit(solution)/shard_map/ppermute | solution.py:620
  48.6 1.5 %collective-permute-start.11 = (f32[2,8,32,128]{3,2,1,0:T(8,128)S(1)}, f32[2,8,32,128]{3,2,1,0:T(8,128)S(1)}, u32[]{:S(2)}, u32[]{:S(2)}) collective-permute-start(f32[2,8,32,128]{3,2,1,0:T(8,128)S(1)} %get-tuple-element.41), channel_id=1, source_target_pairs={{0,4},{4,0},{1,5},{5,1},{2,6},{6,2},{3,7},{7,3},{8,12},{12,8},{9,1... | collective-permute-start | bytes 786440 | tf_op jit(solution)/shard_map/ppermute | solution.py:617
  50.1 7.0 %collective-permute-done.11.came = f32[2,8,32,128]{3,2,1,0:T(8,128)S(1)} collective-permute-done((f32[2,8,32,128]{3,2,1,0:T(8,128)S(1)}, f32[2,8,32,128]{3,2,1,0:T(8,128)S(1)}, u32[]{:S(2)}, u32[]{:S(2)}) %collective-permute-start.11) | collective-permute-done | bytes 262176 | tf_op jit(solution)/shard_map/ppermute | solution.py:617
  57.4 1.5 %collective-permute-start.12 = (f32[2,2,32,128]{3,2,1,0:T(8,128)S(1)}, f32[2,2,32,128]{3,2,1,0:T(8,128)S(1)}, u32[]{:S(2)}, u32[]{:S(2)}) collective-permute-start(f32[2,2,32,128]{3,2,1,0:T(8,128)S(1)} %get-tuple-element.43), channel_id=1, source_target_pairs={{0,8},{8,16},{16,24},{24,0},{1,9},{9,17},{17,25},{25,1},{2,10},{10... | collective-permute-start | bytes 196616 | tf_op jit(solution)/shard_map/ppermute | solution.py:623
  58.9 2.6 %collective-permute-start.13 = (f32[2,2,32,128]{3,2,1,0:T(8,128)S(1)}, f32[2,2,32,128]{3,2,1,0:T(8,128)S(1)}, u32[]{:S(2)}, u32[]{:S(2)}) collective-permute-start(f32[2,2,32,128]{3,2,1,0:T(8,128)S(1)} %get-tuple-element.44), channel_id=1, source_target_pairs={{0,16},{8,24},{16,0},{24,8},{1,17},{9,25},{17,1},{25,9},{2,18},{10... | collective-permute-start | bytes 196616 | tf_op jit(solution)/shard_map/ppermute | solution.py:623
  64.2 1.9 %collective-permute-done.13.refs_3_ = f32[2,2,32,128]{3,2,1,0:T(8,128)S(1)} collective-permute-done((f32[2,2,32,128]{3,2,1,0:T(8,128)S(1)}, f32[2,2,32,128]{3,2,1,0:T(8,128)S(1)}, u32[]{:S(2)}, u32[]{:S(2)}) %collective-permute-start.13) | collective-permute-done | bytes 65568 | tf_op jit(solution)/shard_map/ppermute | solution.py:623
  66.8 13.1 %all_to_all.5.tiles = f32[32,8,128]{2,1,0:T(8,128)S(1)} all-to-all(f32[32,8,128]{2,1,0:T(8,128)S(1)} %broadcast_in_dim.3), channel_id=1, replica_groups=mesh['src'=4,'gx'=2,'gy'=4] {'src','gx','gy'}, dimensions={0} | all-to-all | bytes 262144 | tf_op jit(solution)/shard_map/all_to_all | solution.py:690
  (40 shorter events, 7.2 us)
Async XLA Ops:
  2.6 8.5 %copy-start.8 = (s32[1024]{0:T(1024)S(1)}, s32[1024]{0:T(1024)}, u32[]{:S(2)}) copy-start(s32[1024]{0:T(1024)} %param.14) | copy-start | bytes 12292
  2.6 12.6 %collective-permute-start = (f32[3,8,32,128]{3,2,1,0:T(8,128)}, f32[3,8,32,128]{3,2,1,0:T(8,128)S(1)}, u32[]{:S(2)}, u32[]{:S(2)}) collective-permute-start(f32[3,8,32,128]{3,2,1,0:T(8,128)} %get-tuple-element.26), channel_id=1, source_target_pairs={{0,4},{4,0},{1,5},{5,1},{2,6},{6,2},{3,7},{7,3},{8,12},{12,8},{9,1... | collective-permute-start | bytes 1179656 | tf_op jit(solution)/shard_map/ppermute | solution.py:617
  5.6 7.7 %collective-permute-start.1 = (f32[2,2,32,128]{3,2,1,0:T(8,128)}, f32[2,2,32,128]{3,2,1,0:T(8,128)S(1)}, u32[]{:S(2)}, u32[]{:S(2)}) collective-permute-start(f32[2,2,32,128]{3,2,1,0:T(8,128)} %get-tuple-element.27), channel_id=1, source_target_pairs={{0,8},{8,16},{16,24},{24,0},{1,9},{9,17},{17,25},{25,1},{2,10},{10... | collective-permute-start | bytes 196616 | tf_op jit(solution)/shard_map/ppermute | solution.py:623
  7.2 7.6 %collective-permute-start.2 = (f32[2,2,32,128]{3,2,1,0:T(8,128)}, f32[2,2,32,128]{3,2,1,0:T(8,128)S(1)}, u32[]{:S(2)}, u32[]{:S(2)}) collective-permute-start(f32[2,2,32,128]{3,2,1,0:T(8,128)} %get-tuple-element.27), channel_id=1, source_target_pairs={{0,16},{8,24},{16,0},{24,8},{1,17},{9,25},{17,1},{25,9},{2,18},{10... | collective-permute-start | bytes 196616 | tf_op jit(solution)/shard_map/ppermute | solution.py:623
  9.8 5.0 %collective-permute-start.3 = (f32[2,2,32,128]{3,2,1,0:T(8,128)}, f32[2,2,32,128]{3,2,1,0:T(8,128)S(1)}, u32[]{:S(2)}, u32[]{:S(2)}) collective-permute-start(f32[2,2,32,128]{3,2,1,0:T(8,128)} %get-tuple-element.27), channel_id=1, source_target_pairs={{0,24},{8,0},{16,8},{24,16},{1,25},{9,1},{17,9},{25,17},{2,26},{10... | collective-permute-start | bytes 196616 | tf_op jit(solution)/shard_map/ppermute | solution.py:623
  11.1 3.6 %copy-start = (f32[8,32,32]{2,1,0:T(8,128)S(1)}, f32[8,32,32]{2,1,0:T(8,128)}, u32[]{:S(2)}) copy-start(f32[8,32,32]{2,1,0:T(8,128)} %vk.3) | copy-start | bytes 98308
  11.1 3.6 %copy-start.1 = (f32[8,32,32]{2,1,0:T(8,128)S(1)}, f32[8,32,32]{2,1,0:T(8,128)}, u32[]{:S(2)}) copy-start(f32[8,32,32]{2,1,0:T(8,128)} %va.3) | copy-start | bytes 98308
  13.2 2.0 %copy-start.2 = (f32[4,8,32,128]{3,2,1,0:T(8,128)S(1)}, f32[4,8,32,128]{3,2,1,0:T(8,128)}, u32[]{:S(2)}) copy-start(f32[4,8,32,128]{3,2,1,0:T(8,128)} %refs_0_.4) | copy-start | bytes 1572868
  13.2 2.0 %copy-start.3 = (s32[8,32,128]{2,1,0:T(8,128)S(1)}, s32[8,32,128]{2,1,0:T(8,128)}, u32[]{:S(2)}) copy-start(s32[8,32,128]{2,1,0:T(8,128)} %refs_1_.4) | copy-start | bytes 393220
  15.9 2.0 %collective-permute-start.4 = (f32[2,16,32,128]{3,2,1,0:T(8,128)S(1)}, f32[2,16,32,128]{3,2,1,0:T(8,128)S(1)}, u32[]{:S(2)}, u32[]{:S(2)}) collective-permute-start(f32[2,16,32,128]{3,2,1,0:T(8,128)S(1)} %get-tuple-element.29.fields.refs_3_), channel_id=1, source_target_pairs={{0,1},{1,0},{2,3},{3,2},{4,5},{5,4},{6,7},{7,6},{8,9},{9,8},{10,11... | collective-permute-start | bytes 1572872 | tf_op jit(solution)/shard_map/ppermute | solution.py:620
  15.9 8.7 %collective-permute-start.6 = (f32[2,8,32,128]{3,2,1,0:T(8,128)S(1)}, f32[2,8,32,128]{3,2,1,0:T(8,128)S(1)}, u32[]{:S(2)}, u32[]{:S(2)}) collective-permute-start(f32[2,8,32,128]{3,2,1,0:T(8,128)S(1)} %shard_map.123.refs_3_.refs_0_), channel_id=1, source_target_pairs={{0,4},{4,0},{1,5},{5,1},{2,6},{6,2},{3,7},{7,3},{8,12},{12,8},{9,1... | collective-permute-start | bytes 786440 | tf_op jit(solution)/shard_map/ppermute | solution.py:617
  17.9 6.8 %collective-permute-start.5 = (f32[2,16,8,128]{3,2,1,0:T(8,128)S(1)}, f32[2,16,8,128]{3,2,1,0:T(8,128)S(1)}, u32[]{:S(2)}, u32[]{:S(2)}) collective-permute-start(f32[2,16,8,128]{3,2,1,0:T(8,128)S(1)} %shard_map.125), channel_id=1, source_target_pairs={{0,2},{1,3},{2,0},{3,1},{4,6},{5,7},{6,4},{7,5},{8,10},{9,11},{10,... | collective-permute-start | bytes 393224 | tf_op jit(solution)/shard_map/ppermute | solution.py:642
  24.7 3.6 %copy-start.6 = (f32[16]{0:T(128)S(1)}, f32[16]{0:T(128)}, u32[]{:S(2)}) copy-start(f32[16]{0:T(128)} %refs_0_.5) | copy-start | bytes 196
  24.7 3.6 %copy-start.7 = (f32[16]{0:T(128)S(1)}, f32[16]{0:T(128)}, u32[]{:S(2)}) copy-start(f32[16]{0:T(128)} %refs_1_.5) | copy-start | bytes 196
  24.7 2.0 %collective-permute-start.7 = (f32[2,16,32,128]{3,2,1,0:T(8,128)S(1)}, f32[2,16,32,128]{3,2,1,0:T(8,128)S(1)}, u32[]{:S(2)}, u32[]{:S(2)}) collective-permute-start(f32[2,16,32,128]{3,2,1,0:T(8,128)S(1)} %shard_map.126.fields), channel_id=1, source_target_pairs={{0,1},{1,0},{2,3},{3,2},{4,5},{5,4},{6,7},{7,6},{8,9},{9,8},{10,11... | collective-permute-start | bytes 1572872 | tf_op jit(solution)/shard_map/ppermute | solution.py:620
  26.8 5.6 %collective-permute-start.8 = (f32[2,16,8,128]{3,2,1,0:T(8,128)S(1)}, f32[2,16,8,128]{3,2,1,0:T(8,128)S(1)}, u32[]{:S(2)}, u32[]{:S(2)}) collective-permute-start(f32[2,16,8,128]{3,2,1,0:T(8,128)S(1)} %shard_map.127.refs_7_), channel_id=1, source_target_pairs={{0,2},{1,3},{2,0},{3,1},{4,6},{5,7},{6,4},{7,5},{8,10},{9,11},{10,... | collective-permute-start | bytes 393224 | tf_op jit(solution)/shard_map/ppermute | solution.py:642
  37.2 4.5 %collective-permute-start.9 = (f32[20,8,128]{2,1,0:T(8,128)S(1)}, f32[20,8,128]{2,1,0:T(8,128)S(1)}, u32[]{:S(2)}, u32[]{:S(2)}) collective-permute-start(f32[20,8,128]{2,1,0:T(8,128)S(1)} %get-tuple-element.37.sent), channel_id=1, source_target_pairs={{0,2},{1,3},{2,0},{3,1},{4,6},{5,7},{6,4},{7,5},{8,10},{9,11},{10,... | collective-permute-start | bytes 245768 | tf_op jit(solution)/shard_map/ppermute | solution.py:642
  46.6 2.0 %collective-permute-start.10 = (f32[2,16,32,128]{3,2,1,0:T(8,128)S(1)}, f32[2,16,32,128]{3,2,1,0:T(8,128)S(1)}, u32[]{:S(2)}, u32[]{:S(2)}) collective-permute-start(f32[2,16,32,128]{3,2,1,0:T(8,128)S(1)} %get-tuple-element.39), channel_id=1, source_target_pairs={{0,1},{1,0},{2,3},{3,2},{4,5},{5,4},{6,7},{7,6},{8,9},{9,8},{10,11... | collective-permute-start | bytes 1572872 | tf_op jit(solution)/shard_map/ppermute | solution.py:620
  48.6 8.4 %collective-permute-start.11 = (f32[2,8,32,128]{3,2,1,0:T(8,128)S(1)}, f32[2,8,32,128]{3,2,1,0:T(8,128)S(1)}, u32[]{:S(2)}, u32[]{:S(2)}) collective-permute-start(f32[2,8,32,128]{3,2,1,0:T(8,128)S(1)} %get-tuple-element.41), channel_id=1, source_target_pairs={{0,4},{4,0},{1,5},{5,1},{2,6},{6,2},{3,7},{7,3},{8,12},{12,8},{9,1... | collective-permute-start | bytes 786440 | tf_op jit(solution)/shard_map/ppermute | solution.py:617
  57.1 9.1 %copy-start.4 = (f32[8,32,32]{2,1,0:T(8,128)S(1)}, f32[8,32,32]{2,1,0:T(8,128)}, u32[]{:S(2)}) copy-start(f32[8,32,32]{2,1,0:T(8,128)} %refs_7_.1) | copy-start | bytes 98308
  57.1 9.1 %copy-start.5 = (f32[8,32,32]{2,1,0:T(8,128)S(1)}, f32[8,32,32]{2,1,0:T(8,128)}, u32[]{:S(2)}) copy-start(f32[8,32,32]{2,1,0:T(8,128)} %refs_8_.1) | copy-start | bytes 98308
  57.4 6.8 %collective-permute-start.12 = (f32[2,2,32,128]{3,2,1,0:T(8,128)S(1)}, f32[2,2,32,128]{3,2,1,0:T(8,128)S(1)}, u32[]{:S(2)}, u32[]{:S(2)}) collective-permute-start(f32[2,2,32,128]{3,2,1,0:T(8,128)S(1)} %get-tuple-element.43), channel_id=1, source_target_pairs={{0,8},{8,16},{16,24},{24,0},{1,9},{9,17},{17,25},{25,1},{2,10},{10... | collective-permute-start | bytes 196616 | tf_op jit(solution)/shard_map/ppermute | solution.py:623
  58.9 7.1 %collective-permute-start.13 = (f32[2,2,32,128]{3,2,1,0:T(8,128)S(1)}, f32[2,2,32,128]{3,2,1,0:T(8,128)S(1)}, u32[]{:S(2)}, u32[]{:S(2)}) collective-permute-start(f32[2,2,32,128]{3,2,1,0:T(8,128)S(1)} %get-tuple-element.44), channel_id=1, source_target_pairs={{0,16},{8,24},{16,0},{24,8},{1,17},{9,25},{17,1},{25,9},{2,18},{10... | collective-permute-start | bytes 196616 | tf_op jit(solution)/shard_map/ppermute | solution.py:623
  61.5 4.6 %collective-permute-start.14 = (f32[2,2,32,128]{3,2,1,0:T(8,128)S(1)}, f32[2,2,32,128]{3,2,1,0:T(8,128)S(1)}, u32[]{:S(2)}, u32[]{:S(2)}) collective-permute-start(f32[2,2,32,128]{3,2,1,0:T(8,128)S(1)} %get-tuple-element.45), channel_id=1, source_target_pairs={{0,24},{8,0},{16,8},{24,16},{1,25},{9,1},{17,9},{25,17},{2,26},{10... | collective-permute-start | bytes 196616 | tf_op jit(solution)/shard_map/ppermute | solution.py:623

commit v6 on v5

--- a/solution.py
+++ b/solution.py
@@ -375,7 +375,7 @@
         diag[i] = jnp.take_along_axis(abs_row, at, axis=1)
         return carry
 
-    lax.fori_loop(0, planes, look_up, 0, unroll=2)
+    lax.fori_loop(0, planes, look_up, 0, unroll=4)
     fx[0] = 0.5 * kap[1]
     owned = owned_rows((rows, lanes), halo * y, 2 * cy)
 
@@ -393,7 +393,7 @@
         return carry[0] + folded(part), carry[1] + folded(part * p)
 
     zero = jnp.zeros((8, lanes), jnp.float32)
-    sums[0], sums[1] = lax.fori_loop(0, planes, set_up, (zero, zero), unroll=2)
+    sums[0], sums[1] = lax.fori_loop(0, planes, set_up, (zero, zero), unroll=4)
 
 
 def first_kernel(
@@ -423,8 +423,8 @@
         buf_a[i + 1] = total * (1.0 / theta)
         return carry
 
-    lax.fori_loop(0, planes, set_up, 0, unroll=2)
-    found = solve(b, (buf_a, buf_b), diag, fx, fy, fz, 8)
+    lax.fori_loop(0, planes, set_up, 0, unroll=4)
+    found = solve(b, (buf_a, buf_b), diag, fx, fy, fz, 16)
     owned = owned_rows((rows, lanes), halo * y, 2 * cy)
 
     def add_up(i, carry):
@@ -434,7 +434,7 @@
         return carry[0] + folded(part), carry[1] + folded(part * phi[i + 1])
 
     zero = jnp.zeros((8, lanes), jnp.float32)
-    seen, cross = lax.fori_loop(0, planes, add_up, (zero, zero), unroll=2)
+    seen, cross = lax.fori_loop(0, planes, add_up, (zero, zero), unroll=4)
     edge = (2 * cy - halo) * (1 - y) + halo * y
     message[pl.ds(0, planes)] = found[pl.ds(1, planes), pl.ds(edge, halo), :]
     for i, part in enumerate((sums[0], seen, cross, sums[1])):
@@ -476,8 +476,8 @@
         buf_a[i + 1, edge, :] = value * (1.0 / theta)
         return carry
 
-    lax.fori_loop(0, planes, set_up, 0, unroll=2)
-    dual = solve(b, (buf_a, buf_b), diag, fx, fy, fz, 8)
+    lax.fori_loop(0, planes, set_up, 0, unroll=4)
+    dual = solve(b, (buf_a, buf_b), diag, fx, fy, fz, 16)
 
     def product(i, carry):
         p, u = phi[i + 1], dual[i + 1]
@@ -494,7 +494,7 @@
             message[f, i] = ref[i, pl.ds(base + cy * (1 - c), cy), :]
         return carry
 
-    lax.fori_loop(0, planes, product, 0, unroll=2)
+    lax.fori_loop(0, planes, product, 0, unroll=4)
 
 
 def core_kernel(own, came, kept, message):
@@ -649,9 +649,9 @@
         background, labels, came, after=(half_vector,), hbm=(0, 1), scratch=(raw_labels,), copies=3,
     )
     got = swap_core(fields)
-    (sent,) = run(photon_edge_kernel, edges, mine, fields, got)
+    (vector,) = run(vector_kernel, (f32(2, planes, cy, cz),), half_vector, half_came)
+    (sent,) = run(photon_edge_kernel, edges, mine, fields, got, after=(vector,))
     halo = across_y(sent)
-    (vector,) = run(vector_kernel, (f32(2, planes, cy, cz),), half_vector, half_came, after=(halo,))
     vector_got = swap_core(vector)
     (vector_sent,) = run(vector_edge_kernel, edges, vector, vector_got)
     frame, wide = (planes, rows, cz), (planes + 2, rows, cz)

time: 81.1 us -> 77 us (0.949)
  starting transfers between devices: 21.9 us -> 19.5 us
  Pallas kernels: 19.9 us -> 17.8 us
  waiting for transfers between devices: 24.6 us -> 25.9 us
  blocking collectives: 13.1 us -> 12.1 us
    ppermute x3, waiting for transfers between devices: 4.23 us -> 2.12 us  [swap_core(): return lax.ppermute(value, 'gy', [(0, 1), (1, 0), (2, 3), (3, 2)])]
    pallas_call x14, Pallas kernels: 19.9 us -> 17.8 us  [run(): pl.pallas_call(body if waits else kernel, out_shape=tuple(outs), in_specs...]
    ppermute x3, waiting for transfers between devices: 4.06 us -> 5.89 us  [across_y(): return lax.ppermute(value, 'gy', [(i, (i + 2) % 4) for i in range(4)])]
    ppermute x3, starting transfers between devices: 5.92 us -> 4.22 us  [swap_x(): return lax.ppermute(value, 'gx', [(0, 1), (1, 0)])]
    ppermute x3, waiting for transfers between devices: 12.2 us -> 13.1 us  [swap_x(): return lax.ppermute(value, 'gx', [(0, 1), (1, 0)])]
    all_to_all x1, blocking collectives: 13.1 us -> 12.1 us  [per_device_paired(): lax.all_to_all(jnp.broadcast_to(tile, (8 * n, 8, 128)), everyone, 0, 0)]
  transfers between devices with their start and end apart: 15 -> 15, of which waited for: 11 -> 9; matrix products, arithmetic and copies ran while one was open for 0% -> 0% of each run, Pallas kernels for 7% -> 7%
where the time goes in v6:
time: 77 us; the launch traced here: 76.8 us
  waiting for transfers between devices  25.9 us (34%)
  starting transfers between devices  19.5 us (25%)
  Pallas kernels  17.8 us (23%)
  blocking collectives  12.1 us (16%)
  between operations  1.48 us (2%)
    pallas_call x14, Pallas kernels, run(): pl.pallas_call(body if waits else kernel, out_shape=tuple(outs), in_specs...  17.8 us
    ppermute x3, waiting for transfers between devices, swap_x(): return lax.ppermute(value, 'gx', [(0, 1), (1, 0)])  13.1 us
    all_to_all x1, blocking collectives, per_device_paired(): lax.all_to_all(jnp.broadcast_to(tile, (8 * n, 8, 128)), everyone, 0, 0)  12.1 us
    ppermute x6, starting transfers between devices, along_z(): return lax.ppermute(value, 'src', [(i, (i + k) % n) for i in range(n)])  10.3 us
    ppermute x3, waiting for transfers between devices, across_y(): return lax.ppermute(value, 'gy', [(i, (i + 2) % 4) for i in range(4)])  5.89 us
    ppermute x6, waiting for transfers between devices, along_z(): return lax.ppermute(value, 'src', [(i, (i + k) % n) for i in range(n)])  4.78 us
    ppermute x3, starting transfers between devices, across_y(): return lax.ppermute(value, 'gy', [(i, (i + 2) % 4) for i in range(4)])  4.75 us
    ppermute x3, starting transfers between devices, swap_x(): return lax.ppermute(value, 'gx', [(0, 1), (1, 0)])  4.22 us
  transfers between devices with their start and end apart: 15, of which 9 were waited for; matrix products, arithmetic and copies ran while one was open for 0% of the time, Pallas kernels for 7%

profile of v6, /device:TPU:0, one launch (start us, length us, event | category | flops | bytes accessed | tf_op | source)
XLA Modules:
  0.0 76.8 jit_solution(4616604307360243586)
XLA Ops:
  0.6 1.9 %shard_map.121 = (f32[2,2,32,128]{3,2,1,0:T(8,128)}, f32[3,8,32,128]{3,2,1,0:T(8,128)}) custom-call(f32[4,8,32,128]{3,2,1,0:T(8,128)} %refs_0_.4, s32[8,32,128]{2,1,0:T(8,128)} %refs_1_.4, f32[8,32,32]{2,1,0:T(8,128)} %vk.3, f32[8,32,32]{2,1,0:T(8,128)} %va.3), custom_call_target="tpu_custom_call" | custom-call | tf_op jit(solution)/shard_map/pallas_call | solution.py:590
  2.6 3.0 %collective-permute-start = (f32[3,8,32,128]{3,2,1,0:T(8,128)}, f32[3,8,32,128]{3,2,1,0:T(8,128)S(1)}, u32[]{:S(2)}, u32[]{:S(2)}) collective-permute-start(f32[3,8,32,128]{3,2,1,0:T(8,128)} %get-tuple-element.26), channel_id=1, source_target_pairs={{0,4},{4,0},{1,5},{5,1},{2,6},{6,2},{3,7},{7,3},{8,12},{12,8},{9,1... | collective-permute-start | bytes 1179656 | tf_op jit(solution)/shard_map/ppermute | solution.py:617
  5.6 1.6 %collective-permute-start.1 = (f32[2,2,32,128]{3,2,1,0:T(8,128)}, f32[2,2,32,128]{3,2,1,0:T(8,128)S(1)}, u32[]{:S(2)}, u32[]{:S(2)}) collective-permute-start(f32[2,2,32,128]{3,2,1,0:T(8,128)} %get-tuple-element.27), channel_id=1, source_target_pairs={{0,8},{8,16},{16,24},{24,0},{1,9},{9,17},{17,25},{25,1},{2,10},{10... | collective-permute-start | bytes 196616 | tf_op jit(solution)/shard_map/ppermute | solution.py:623
  7.2 2.6 %collective-permute-start.2 = (f32[2,2,32,128]{3,2,1,0:T(8,128)}, f32[2,2,32,128]{3,2,1,0:T(8,128)S(1)}, u32[]{:S(2)}, u32[]{:S(2)}) collective-permute-start(f32[2,2,32,128]{3,2,1,0:T(8,128)} %get-tuple-element.27), channel_id=1, source_target_pairs={{0,16},{8,24},{16,0},{24,8},{1,17},{9,25},{17,1},{25,9},{2,18},{10... | collective-permute-start | bytes 196616 | tf_op jit(solution)/shard_map/ppermute | solution.py:623
  9.8 1.3 %collective-permute-start.3 = (f32[2,2,32,128]{3,2,1,0:T(8,128)}, f32[2,2,32,128]{3,2,1,0:T(8,128)S(1)}, u32[]{:S(2)}, u32[]{:S(2)}) collective-permute-start(f32[2,2,32,128]{3,2,1,0:T(8,128)} %get-tuple-element.27), channel_id=1, source_target_pairs={{0,24},{8,0},{16,8},{24,16},{1,25},{9,1},{17,9},{25,17},{2,26},{10... | collective-permute-start | bytes 196616 | tf_op jit(solution)/shard_map/ppermute | solution.py:623
  11.1 2.1 %shard_map.122.refs_5_.refs_6_.count = f32[16,72,128]{2,1,0:T(8,128)S(1)} custom-call(s32[1,1024]{1,0:T(1,128)S(1)} %bitcast.3), custom_call_target="tpu_custom_call" | custom-call | flops 301989888 | bytes 589824 | tf_op jit(solution)/shard_map/pallas_call | solution.py:590
  13.3 1.5 %collective-permute-done.2.refs_3_ = f32[2,2,32,128]{3,2,1,0:T(8,128)S(1)} collective-permute-done((f32[2,2,32,128]{3,2,1,0:T(8,128)}, f32[2,2,32,128]{3,2,1,0:T(8,128)S(1)}, u32[]{:S(2)}, u32[]{:S(2)}) %collective-permute-start.2) | collective-permute-done | bytes 65568 | tf_op jit(solution)/shard_map/ppermute | solution.py:623
  16.4 5.5 %collective-permute-done.5.came = f32[2,8,32,128]{3,2,1,0:T(8,128)S(1)} collective-permute-done((f32[2,8,32,128]{3,2,1,0:T(8,128)S(1)}, f32[2,8,32,128]{3,2,1,0:T(8,128)S(1)}, u32[]{:S(2)}, u32[]{:S(2)}) %collective-permute-start.5) | collective-permute-done | bytes 262176 | tf_op jit(solution)/shard_map/ppermute | solution.py:617
  22.0 1.6 %collective-permute-start.6 = (f32[2,16,8,128]{3,2,1,0:T(8,128)S(1)}, f32[2,16,8,128]{3,2,1,0:T(8,128)S(1)}, u32[]{:S(2)}, u32[]{:S(2)}) collective-permute-start(f32[2,16,8,128]{3,2,1,0:T(8,128)S(1)} %shard_map.126), channel_id=1, source_target_pairs={{0,2},{1,3},{2,0},{3,1},{4,6},{5,7},{6,4},{7,5},{8,10},{9,11},{10,... | collective-permute-start | bytes 393224 | tf_op jit(solution)/shard_map/ppermute | solution.py:642
  23.9 1.6 %collective-permute-start.8 = (f32[2,16,8,128]{3,2,1,0:T(8,128)S(1)}, f32[2,16,8,128]{3,2,1,0:T(8,128)S(1)}, u32[]{:S(2)}, u32[]{:S(2)}) collective-permute-start(f32[2,16,8,128]{3,2,1,0:T(8,128)S(1)} %shard_map.127.refs_7_), channel_id=1, source_target_pairs={{0,2},{1,3},{2,0},{3,1},{4,6},{5,7},{6,4},{7,5},{8,10},{9,11},{10,... | collective-permute-start | bytes 393224 | tf_op jit(solution)/shard_map/ppermute | solution.py:642
  25.5 2.9 %collective-permute-done.6.refs_5_ = f32[2,16,8,128]{3,2,1,0:T(8,128)S(1)} collective-permute-done((f32[2,16,8,128]{3,2,1,0:T(8,128)S(1)}, f32[2,16,8,128]{3,2,1,0:T(8,128)S(1)}, u32[]{:S(2)}, u32[]{:S(2)}) %collective-permute-start.6) | collective-permute-done | bytes 131104 | tf_op jit(solution)/shard_map/ppermute | solution.py:642
  28.4 2.3 %shard_map.128 = (f32[18,72,128]{2,1,0:T(8,128)S(1)}, f32[16,72,128]{2,1,0:T(8,128)S(1)}, f32[17,72,128]{2,1,0:T(8,128)S(1)}, f32[16,72,128]{2,1,0:T(8,128)S(1)}...) custom-call(f32[16]{0:T(128)S(1)} %copy-done.6, f32[16]{0:T(128)S(1)} %copy-done.7, ...), custom_call_target="tpu_custom_call" | custom-call | tf_op jit(solution)/shard_map/pallas_call | solution.py:590
  30.8 4.0 %shard_map.129 = (f32[16,72,128]{2,1,0:T(8,128)S(1)}, f32[20,8,128]{2,1,0:T(8,128)S(1)}) custom-call(f32[18,72,128]{2,1,0:T(8,128)S(1)} %get-tuple-element.30.phi, f32[16,72,128]{2,1,0:T(8,128)S(1)} %get-tuple-element.31.diag, f32[17,72,128]{2,1,0:T(8,128)S(1)} %get-tuple-element.32.fx, f32[16,72,128]{2,1,0:T(8,128)S(1)} %get-tuple-element.33.fy, ...), custom_call_target="tpu_custom_call" | custom-call | tf_op jit(solution)/shard_map/pallas_call | solution.py:590
  34.8 1.6 %collective-permute-start.9 = (f32[20,8,128]{2,1,0:T(8,128)S(1)}, f32[20,8,128]{2,1,0:T(8,128)S(1)}, u32[]{:S(2)}, u32[]{:S(2)}) collective-permute-start(f32[20,8,128]{2,1,0:T(8,128)S(1)} %get-tuple-element.37.sent), channel_id=1, source_target_pairs={{0,2},{1,3},{2,0},{3,1},{4,6},{5,7},{6,4},{7,5},{8,10},{9,11},{10,... | collective-permute-start | bytes 245768 | tf_op jit(solution)/shard_map/ppermute | solution.py:642
  36.4 2.9 %collective-permute-done.9.came = f32[20,8,128]{2,1,0:T(8,128)S(1)} collective-permute-done((f32[20,8,128]{2,1,0:T(8,128)S(1)}, f32[20,8,128]{2,1,0:T(8,128)S(1)}, u32[]{:S(2)}, u32[]{:S(2)}) %collective-permute-start.9) | collective-permute-done | bytes 81952 | tf_op jit(solution)/shard_map/ppermute | solution.py:642
  39.3 4.1 %shard_map.130 = (f32[2,16,32,128]{3,2,1,0:T(8,128)S(1)}, f32[2,16,32,128]{3,2,1,0:T(8,128)S(1)}) custom-call(f32[18,72,128]{2,1,0:T(8,128)S(1)} %get-tuple-element.30.phi, f32[16,72,128]{2,1,0:T(8,128)S(1)} %get-tuple-element.36.change, f32[16,72,128]{2,1,0:T(8,128)S(1)} %get-tuple-element.31.diag, f32[17,72,128]{2,1,0:T(8,128)S(1)} %get-tuple-element.32.fx, ...), custom_call_target="tpu_custom_call" | custom-call | tf_op jit(solution)/shard_map/pallas_call | solution.py:590
  43.5 1.9 %collective-permute-done.10.came = f32[2,16,32,128]{3,2,1,0:T(8,128)S(1)} collective-permute-done((f32[2,16,32,128]{3,2,1,0:T(8,128)S(1)}, f32[2,16,32,128]{3,2,1,0:T(8,128)S(1)}, u32[]{:S(2)}, u32[]{:S(2)}) %collective-permute-start.10) | collective-permute-done | bytes 524320 | tf_op jit(solution)/shard_map/ppermute | solution.py:620
  46.3 7.6 %collective-permute-done.11.came = f32[2,8,32,128]{3,2,1,0:T(8,128)S(1)} collective-permute-done((f32[2,8,32,128]{3,2,1,0:T(8,128)S(1)}, f32[2,8,32,128]{3,2,1,0:T(8,128)S(1)}, u32[]{:S(2)}, u32[]{:S(2)}) %collective-permute-start.11) | collective-permute-done | bytes 262176 | tf_op jit(solution)/shard_map/ppermute | solution.py:617
  54.3 2.4 %collective-permute-start.12 = (f32[2,2,32,128]{3,2,1,0:T(8,128)S(1)}, f32[2,2,32,128]{3,2,1,0:T(8,128)S(1)}, u32[]{:S(2)}, u32[]{:S(2)}) collective-permute-start(f32[2,2,32,128]{3,2,1,0:T(8,128)S(1)} %get-tuple-element.43), channel_id=1, source_target_pairs={{0,8},{8,16},{16,24},{24,0},{1,9},{9,17},{17,25},{25,1},{2,10},{10... | collective-permute-start | bytes 196616 | tf_op jit(solution)/shard_map/ppermute | solution.py:623
  56.6 0.8 %collective-permute-start.13 = (f32[2,2,32,128]{3,2,1,0:T(8,128)S(1)}, f32[2,2,32,128]{3,2,1,0:T(8,128)S(1)}, u32[]{:S(2)}, u32[]{:S(2)}) collective-permute-start(f32[2,2,32,128]{3,2,1,0:T(8,128)S(1)} %get-tuple-element.44), channel_id=1, source_target_pairs={{0,16},{8,24},{16,0},{24,8},{1,17},{9,25},{17,1},{25,9},{2,18},{10... | collective-permute-start | bytes 196616 | tf_op jit(solution)/shard_map/ppermute | solution.py:623
  57.5 1.6 %collective-permute-start.14 = (f32[2,2,32,128]{3,2,1,0:T(8,128)S(1)}, f32[2,2,32,128]{3,2,1,0:T(8,128)S(1)}, u32[]{:S(2)}, u32[]{:S(2)}) collective-permute-start(f32[2,2,32,128]{3,2,1,0:T(8,128)S(1)} %get-tuple-element.45), channel_id=1, source_target_pairs={{0,24},{8,0},{16,8},{24,16},{1,25},{9,1},{17,9},{25,17},{2,26},{10... | collective-permute-start | bytes 196616 | tf_op jit(solution)/shard_map/ppermute | solution.py:623
  60.5 2.5 %collective-permute-done.13.refs_3_ = f32[2,2,32,128]{3,2,1,0:T(8,128)S(1)} collective-permute-done((f32[2,2,32,128]{3,2,1,0:T(8,128)S(1)}, f32[2,2,32,128]{3,2,1,0:T(8,128)S(1)}, u32[]{:S(2)}, u32[]{:S(2)}) %collective-permute-start.13) | collective-permute-done | bytes 65568 | tf_op jit(solution)/shard_map/ppermute | solution.py:623
  63.7 12.1 %all_to_all.5.tiles = f32[32,8,128]{2,1,0:T(8,128)S(1)} all-to-all(f32[32,8,128]{2,1,0:T(8,128)S(1)} %broadcast_in_dim.3), channel_id=1, replica_groups=mesh['src'=4,'gx'=2,'gy'=4] {'src','gx','gy'}, dimensions={0} | all-to-all | bytes 262144 | tf_op jit(solution)/shard_map/all_to_all | solution.py:690
  75.8 1.0 %shard_map.134 = (f32[8,32,32]{2,1,0:T(8,128)}, f32[8,32,32]{2,1,0:T(8,128)}, f32[2]{0:T(128)}) custom-call(f32[32,8,128]{2,1,0:T(8,128)S(1)} %all_to_all.5.tiles, f32[8,32,32]{2,1,0:T(8,128)S(1)} %get-tuple-element.47.w_k, f32[8,32,32]{2,1,0:T(8,128)S(1)} %get-tuple-element.48.w_a, f32[8,32,32]{2,1,0:T(8,128)S(1)} %copy-done, f32[8,32,32]{2,1,0:T(8,128)S(1)} %copy-done.1), custom_call_target="tpu_custom_call" | custom-call | tf_op jit(solution)/shard_map/pallas_call | solution.py:590
  (40 shorter events, 4.8 us)
Async XLA Ops:
  2.6 8.5 %copy-start.8 = (s32[1024]{0:T(1024)S(1)}, s32[1024]{0:T(1024)}, u32[]{:S(2)}) copy-start(s32[1024]{0:T(1024)} %param.14) | copy-start | bytes 12292
  2.6 13.1 %collective-permute-start = (f32[3,8,32,128]{3,2,1,0:T(8,128)}, f32[3,8,32,128]{3,2,1,0:T(8,128)S(1)}, u32[]{:S(2)}, u32[]{:S(2)}) collective-permute-start(f32[3,8,32,128]{3,2,1,0:T(8,128)} %get-tuple-element.26), channel_id=1, source_target_pairs={{0,4},{4,0},{1,5},{5,1},{2,6},{6,2},{3,7},{7,3},{8,12},{12,8},{9,1... | collective-permute-start | bytes 1179656 | tf_op jit(solution)/shard_map/ppermute | solution.py:617
  5.6 7.7 %collective-permute-start.1 = (f32[2,2,32,128]{3,2,1,0:T(8,128)}, f32[2,2,32,128]{3,2,1,0:T(8,128)S(1)}, u32[]{:S(2)}, u32[]{:S(2)}) collective-permute-start(f32[2,2,32,128]{3,2,1,0:T(8,128)} %get-tuple-element.27), channel_id=1, source_target_pairs={{0,8},{8,16},{16,24},{24,0},{1,9},{9,17},{17,25},{25,1},{2,10},{10... | collective-permute-start | bytes 196616 | tf_op jit(solution)/shard_map/ppermute | solution.py:623
  7.2 7.6 %collective-permute-start.2 = (f32[2,2,32,128]{3,2,1,0:T(8,128)}, f32[2,2,32,128]{3,2,1,0:T(8,128)S(1)}, u32[]{:S(2)}, u32[]{:S(2)}) collective-permute-start(f32[2,2,32,128]{3,2,1,0:T(8,128)} %get-tuple-element.27), channel_id=1, source_target_pairs={{0,16},{8,24},{16,0},{24,8},{1,17},{9,25},{17,1},{25,9},{2,18},{10... | collective-permute-start | bytes 196616 | tf_op jit(solution)/shard_map/ppermute | solution.py:623
  9.8 5.0 %collective-permute-start.3 = (f32[2,2,32,128]{3,2,1,0:T(8,128)}, f32[2,2,32,128]{3,2,1,0:T(8,128)S(1)}, u32[]{:S(2)}, u32[]{:S(2)}) collective-permute-start(f32[2,2,32,128]{3,2,1,0:T(8,128)} %get-tuple-element.27), channel_id=1, source_target_pairs={{0,24},{8,0},{16,8},{24,16},{1,25},{9,1},{17,9},{25,17},{2,26},{10... | collective-permute-start | bytes 196616 | tf_op jit(solution)/shard_map/ppermute | solution.py:623
  11.1 3.6 %copy-start = (f32[8,32,32]{2,1,0:T(8,128)S(1)}, f32[8,32,32]{2,1,0:T(8,128)}, u32[]{:S(2)}) copy-start(f32[8,32,32]{2,1,0:T(8,128)} %vk.3) | copy-start | bytes 98308
  11.1 3.6 %copy-start.1 = (f32[8,32,32]{2,1,0:T(8,128)S(1)}, f32[8,32,32]{2,1,0:T(8,128)}, u32[]{:S(2)}) copy-start(f32[8,32,32]{2,1,0:T(8,128)} %va.3) | copy-start | bytes 98308
  13.2 2.4 %copy-start.2 = (f32[4,8,32,128]{3,2,1,0:T(8,128)S(1)}, f32[4,8,32,128]{3,2,1,0:T(8,128)}, u32[]{:S(2)}) copy-start(f32[4,8,32,128]{3,2,1,0:T(8,128)} %refs_0_.4) | copy-start | bytes 1572868
  13.2 2.4 %copy-start.3 = (s32[8,32,128]{2,1,0:T(8,128)S(1)}, s32[8,32,128]{2,1,0:T(8,128)}, u32[]{:S(2)}) copy-start(s32[8,32,128]{2,1,0:T(8,128)} %refs_1_.4) | copy-start | bytes 393220
  15.2 6.6 %collective-permute-start.5 = (f32[2,8,32,128]{3,2,1,0:T(8,128)S(1)}, f32[2,8,32,128]{3,2,1,0:T(8,128)S(1)}, u32[]{:S(2)}, u32[]{:S(2)}) collective-permute-start(f32[2,8,32,128]{3,2,1,0:T(8,128)S(1)} %shard_map.123.refs_3_.own), channel_id=1, source_target_pairs={{0,4},{4,0},{1,5},{5,1},{2,6},{6,2},{3,7},{7,3},{8,12},{12,8},{9,1... | collective-permute-start | bytes 786440 | tf_op jit(solution)/shard_map/ppermute | solution.py:617
  16.3 5.7 %collective-permute-start.4 = (f32[2,16,32,128]{3,2,1,0:T(8,128)S(1)}, f32[2,16,32,128]{3,2,1,0:T(8,128)S(1)}, u32[]{:S(2)}, u32[]{:S(2)}) collective-permute-start(f32[2,16,32,128]{3,2,1,0:T(8,128)S(1)} %get-tuple-element.29.refs_1_.refs_3_), channel_id=1, source_target_pairs={{0,1},{1,0},{2,3},{3,2},{4,5},{5,4},{6,7},{7,6},{8,9},{9,8},{10,11... | collective-permute-start | bytes 1572872 | tf_op jit(solution)/shard_map/ppermute | solution.py:620
  21.9 2.0 %collective-permute-start.7 = (f32[2,16,32,128]{3,2,1,0:T(8,128)S(1)}, f32[2,16,32,128]{3,2,1,0:T(8,128)S(1)}, u32[]{:S(2)}, u32[]{:S(2)}) collective-permute-start(f32[2,16,32,128]{3,2,1,0:T(8,128)S(1)} %shard_map.125.refs_3_.fields), channel_id=1, source_target_pairs={{0,1},{1,0},{2,3},{3,2},{4,5},{5,4},{6,7},{7,6},{8,9},{9,8},{10,11... | collective-permute-start | bytes 1572872 | tf_op jit(solution)/shard_map/ppermute | solution.py:620
  22.0 6.4 %copy-start.6 = (f32[16]{0:T(128)S(1)}, f32[16]{0:T(128)}, u32[]{:S(2)}) copy-start(f32[16]{0:T(128)} %refs_0_.5) | copy-start | bytes 196
  22.0 6.4 %copy-start.7 = (f32[16]{0:T(128)S(1)}, f32[16]{0:T(128)}, u32[]{:S(2)}) copy-start(f32[16]{0:T(128)} %refs_1_.5) | copy-start | bytes 196
  22.0 6.4 %collective-permute-start.6 = (f32[2,16,8,128]{3,2,1,0:T(8,128)S(1)}, f32[2,16,8,128]{3,2,1,0:T(8,128)S(1)}, u32[]{:S(2)}, u32[]{:S(2)}) collective-permute-start(f32[2,16,8,128]{3,2,1,0:T(8,128)S(1)} %shard_map.126), channel_id=1, source_target_pairs={{0,2},{1,3},{2,0},{3,1},{4,6},{5,7},{6,4},{7,5},{8,10},{9,11},{10,... | collective-permute-start | bytes 393224 | tf_op jit(solution)/shard_map/ppermute | solution.py:642
  23.9 6.9 %collective-permute-start.8 = (f32[2,16,8,128]{3,2,1,0:T(8,128)S(1)}, f32[2,16,8,128]{3,2,1,0:T(8,128)S(1)}, u32[]{:S(2)}, u32[]{:S(2)}) collective-permute-start(f32[2,16,8,128]{3,2,1,0:T(8,128)S(1)} %shard_map.127.refs_7_), channel_id=1, source_target_pairs={{0,2},{1,3},{2,0},{3,1},{4,6},{5,7},{6,4},{7,5},{8,10},{9,11},{10,... | collective-permute-start | bytes 393224 | tf_op jit(solution)/shard_map/ppermute | solution.py:642
  34.8 4.5 %collective-permute-start.9 = (f32[20,8,128]{2,1,0:T(8,128)S(1)}, f32[20,8,128]{2,1,0:T(8,128)S(1)}, u32[]{:S(2)}, u32[]{:S(2)}) collective-permute-start(f32[20,8,128]{2,1,0:T(8,128)S(1)} %get-tuple-element.37.sent), channel_id=1, source_target_pairs={{0,2},{1,3},{2,0},{3,1},{4,6},{5,7},{6,4},{7,5},{8,10},{9,11},{10,... | collective-permute-start | bytes 245768 | tf_op jit(solution)/shard_map/ppermute | solution.py:642
  43.5 2.0 %collective-permute-start.10 = (f32[2,16,32,128]{3,2,1,0:T(8,128)S(1)}, f32[2,16,32,128]{3,2,1,0:T(8,128)S(1)}, u32[]{:S(2)}, u32[]{:S(2)}) collective-permute-start(f32[2,16,32,128]{3,2,1,0:T(8,128)S(1)} %get-tuple-element.39), channel_id=1, source_target_pairs={{0,1},{1,0},{2,3},{3,2},{4,5},{5,4},{6,7},{7,6},{8,9},{9,8},{10,11... | collective-permute-start | bytes 1572872 | tf_op jit(solution)/shard_map/ppermute | solution.py:620
  45.5 8.4 %collective-permute-start.11 = (f32[2,8,32,128]{3,2,1,0:T(8,128)S(1)}, f32[2,8,32,128]{3,2,1,0:T(8,128)S(1)}, u32[]{:S(2)}, u32[]{:S(2)}) collective-permute-start(f32[2,8,32,128]{3,2,1,0:T(8,128)S(1)} %get-tuple-element.41), channel_id=1, source_target_pairs={{0,4},{4,0},{1,5},{5,1},{2,6},{6,2},{3,7},{7,3},{8,12},{12,8},{9,1... | collective-permute-start | bytes 786440 | tf_op jit(solution)/shard_map/ppermute | solution.py:617
  53.9 9.1 %copy-start.4 = (f32[8,32,32]{2,1,0:T(8,128)S(1)}, f32[8,32,32]{2,1,0:T(8,128)}, u32[]{:S(2)}) copy-start(f32[8,32,32]{2,1,0:T(8,128)} %refs_7_.1) | copy-start | bytes 98308
  53.9 9.1 %copy-start.5 = (f32[8,32,32]{2,1,0:T(8,128)S(1)}, f32[8,32,32]{2,1,0:T(8,128)}, u32[]{:S(2)}) copy-start(f32[8,32,32]{2,1,0:T(8,128)} %refs_8_.1) | copy-start | bytes 98308
  54.3 6.2 %collective-permute-start.12 = (f32[2,2,32,128]{3,2,1,0:T(8,128)S(1)}, f32[2,2,32,128]{3,2,1,0:T(8,128)S(1)}, u32[]{:S(2)}, u32[]{:S(2)}) collective-permute-start(f32[2,2,32,128]{3,2,1,0:T(8,128)S(1)} %get-tuple-element.43), channel_id=1, source_target_pairs={{0,8},{8,16},{16,24},{24,0},{1,9},{9,17},{17,25},{25,1},{2,10},{10... | collective-permute-start | bytes 196616 | tf_op jit(solution)/shard_map/ppermute | solution.py:623
  56.6 6.4 %collective-permute-start.13 = (f32[2,2,32,128]{3,2,1,0:T(8,128)S(1)}, f32[2,2,32,128]{3,2,1,0:T(8,128)S(1)}, u32[]{:S(2)}, u32[]{:S(2)}) collective-permute-start(f32[2,2,32,128]{3,2,1,0:T(8,128)S(1)} %get-tuple-element.44), channel_id=1, source_target_pairs={{0,16},{8,24},{16,0},{24,8},{1,17},{9,25},{17,1},{25,9},{2,18},{10... | collective-permute-start | bytes 196616 | tf_op jit(solution)/shard_map/ppermute | solution.py:623
  57.5 5.6 %collective-permute-start.14 = (f32[2,2,32,128]{3,2,1,0:T(8,128)S(1)}, f32[2,2,32,128]{3,2,1,0:T(8,128)S(1)}, u32[]{:S(2)}, u32[]{:S(2)}) collective-permute-start(f32[2,2,32,128]{3,2,1,0:T(8,128)S(1)} %get-tuple-element.45), channel_id=1, source_target_pairs={{0,24},{8,0},{16,8},{24,16},{1,25},{9,1},{17,9},{25,17},{2,26},{10... | collective-permute-start | bytes 196616 | tf_op jit(solution)/shard_map/ppermute | solution.py:623

commit v7 on v6

--- a/solution.py
+++ b/solution.py
@@ -497,29 +497,33 @@
     lax.fori_loop(0, planes, product, 0, unroll=4)
 
 
-def core_kernel(own, came, kept, message):
-    _, x, _, _ = places(2)
-    cx = kept.shape[1]
-    kept[...] = own[:, pl.ds(cx * x, cx)] + came[:, pl.ds(cx * x, cx)]
-    message[...] = own[:, pl.ds(cx * (1 - x), cx)] + came[:, pl.ds(cx * (1 - x), cx)]
-
-
-def slab_kernel(kept, came, *outs):
-    s, _, _, _ = places(2)
-    n = len(outs)
-    slab = 128 // n
-    _, cx, cy, _ = kept.shape
-    lane = index_along((cy, 128), 1) // slab
-    for f in range(2):
-        for q in range(cx // n):
-            planes = [kept[f, n * q + j] + came[f, n * q + j] for j in range(n)]
-            for k in range(n):
-                to = (s + k) % n
-                piece = jnp.zeros((cy, 128), jnp.float32)
-                for j in range(n):
-                    moved = pltpu.roll(planes[j], ((j - to + n) % n) * slab, 1)
-                    piece = jnp.where(lane == j, moved, piece)
-                outs[k][f, q] = piece
+def core_kernel(own, came, kept, far, near):
+    s, x, _, _ = places(2)
+    n, _, groups, cy, lanes = kept.shape
+    slab = lanes // n
+    lane = index_along((cy, lanes), 1) // slab
+    for h in range(2):
+        for f in range(2):
+            for q in range(groups):
+                at = n * (groups * (x if h == 0 else 1 - x) + q)
+                planes = [own[f, at + j] + came[f, at + j] for j in range(n)]
+                for k in range(n):
+                    to = (s + k) % n
+                    piece = jnp.zeros((cy, lanes), jnp.float32)
+                    for j in range(n):
+                        moved = pltpu.roll(planes[j], ((j - to + n) % n) * slab, 1)
+                        piece = jnp.where(lane == j, moved, piece)
+                    if h == 0:
+                        kept[k, f, q] = piece
+                    elif k >= n // 2:
+                        far[k - n // 2, f, q] = piece
+                    else:
+                        near[k, f, q] = piece
+
+
+def add_kernel(kept, came, *outs, first):
+    for i, out in enumerate(outs):
+        out[...] = kept[first + i] + came[i]
 
 
 def project_kernel(*refs, n):
@@ -674,13 +678,18 @@
         phi, change, diag, fx, fy, fz, count, sent, heard,
         scratch=(float_frame, float_wide, float_wide, float_frame, float_frame),
     )
-    kept, message = run(
-        core_kernel, (f32(2, cx, cy, cz), f32(2, cx, cy, cz)), own, swap_core(message)
-    )
-    pieces = run(
-        slab_kernel, [f32(2, groups, cy, cz)] * n, kept, swap_x(message)
-    )
-    parts = [pieces[0]] + [along_z(pieces[k], k) for k in range(1, n)]
+    piece = f32(2, groups, cy, cz)
+    half = n // 2
+    kept, far, near = run(
+        core_kernel,
+        (f32(n, *piece.shape), f32(n - half, *piece.shape), f32(half, *piece.shape)),
+        own, swap_core(message),
+    )
+    far, near = swap_x(far), swap_x(near)
+    pieces = run(functools.partial(add_kernel, first=half), [piece] * (n - half), kept, far)
+    parts = [along_z(value, half + i) for i, value in enumerate(pieces)]
+    pieces = run(functools.partial(add_kernel, first=0), [piece] * half, kept, near)
+    parts = [pieces[0]] + parts + [along_z(pieces[k], k) for k in range(1, half)]
     w_k, w_a, tile = run(
         functools.partial(project_kernel, n=n),
         (f32(*v_kappa.shape), f32(*v_kappa.shape), f32(8, 128)),

time: 77 us -> 75.1 us (0.975)
  blocking collectives: 12.1 us -> 9.96 us
  starting transfers between devices: 19.5 us -> 20.8 us
  waiting for transfers between devices: 25.9 us -> 24.7 us
    ppermute x3 -> x4, waiting for transfers between devices: 13.1 us -> 9.77 us  [swap_x(): return lax.ppermute(value, 'gx', [(0, 1), (1, 0)])]
    all_to_all x1, blocking collectives: 12.1 us -> 9.96 us  [per_device_paired(): lax.all_to_all(jnp.broadcast_to(tile, (8 * n, 8, 128)), everyone, 0, 0)]
    ppermute x6, waiting for transfers between devices: 4.78 us -> 6.88 us  [along_z(): return lax.ppermute(value, 'src', [(i, (i + k) % n) for i in range(n)])]
    ppermute x3 -> x4, starting transfers between devices: 4.22 us -> 5.53 us  [swap_x(): return lax.ppermute(value, 'gx', [(0, 1), (1, 0)])]
    pallas_call x14 -> x15, Pallas kernels: 17.8 us -> 18 us  [run(): pl.pallas_call(body if waits else kernel, out_shape=tuple(outs), in_specs...]
  transfers between devices with their start and end apart: 15 -> 16, of which waited for: 9 -> 10; matrix products, arithmetic and copies ran while one was open for 0% -> 0% of each run, Pallas kernels for 7% -> 8%
where the time goes in v7:
time: 75.1 us; the launch traced here: 74.9 us
  waiting for transfers between devices  24.7 us (33%)
  starting transfers between devices  20.8 us (28%)
  Pallas kernels  18 us (24%)
  blocking collectives  9.96 us (13%)
  between operations  1.48 us (2%)
    pallas_call x15, Pallas kernels, run(): pl.pallas_call(body if waits else kernel, out_shape=tuple(outs), in_specs...  18 us
    ppermute x6, starting transfers between devices, along_z(): return lax.ppermute(value, 'src', [(i, (i + k) % n) for i in range(n)])  10.3 us
    all_to_all x1, blocking collectives, per_device_paired(): lax.all_to_all(jnp.broadcast_to(tile, (8 * n, 8, 128)), everyone, 0, 0)  9.96 us
    ppermute x4, waiting for transfers between devices, swap_x(): return lax.ppermute(value, 'gx', [(0, 1), (1, 0)])  9.77 us
    ppermute x6, waiting for transfers between devices, along_z(): return lax.ppermute(value, 'src', [(i, (i + k) % n) for i in range(n)])  6.88 us
    ppermute x3, waiting for transfers between devices, across_y(): return lax.ppermute(value, 'gy', [(i, (i + 2) % 4) for i in range(4)])  5.89 us
    ppermute x4, starting transfers between devices, swap_x(): return lax.ppermute(value, 'gx', [(0, 1), (1, 0)])  5.53 us
    ppermute x3, starting transfers between devices, across_y(): return lax.ppermute(value, 'gy', [(i, (i + 2) % 4) for i in range(4)])  4.75 us
  transfers between devices with their start and end apart: 16, of which 10 were waited for; matrix products, arithmetic and copies ran while one was open for 0% of the time, Pallas kernels for 8%

profile of v7, /device:TPU:0, one launch (start us, length us, event | category | flops | bytes accessed | tf_op | source)
XLA Modules:
  0.0 74.9 jit_solution(2843685846765916980)
XLA Ops:
  0.6 1.9 %shard_map.121 = (f32[2,2,32,128]{3,2,1,0:T(8,128)}, f32[3,8,32,128]{3,2,1,0:T(8,128)}) custom-call(f32[4,8,32,128]{3,2,1,0:T(8,128)} %refs_0_.4, s32[8,32,128]{2,1,0:T(8,128)} %refs_1_.4, f32[8,32,32]{2,1,0:T(8,128)} %vk.3, f32[8,32,32]{2,1,0:T(8,128)} %va.3), custom_call_target="tpu_custom_call" | custom-call | tf_op jit(solution)/shard_map/pallas_call | solution.py:594
  2.6 3.0 %collective-permute-start = (f32[3,8,32,128]{3,2,1,0:T(8,128)}, f32[3,8,32,128]{3,2,1,0:T(8,128)S(1)}, u32[]{:S(2)}, u32[]{:S(2)}) collective-permute-start(f32[3,8,32,128]{3,2,1,0:T(8,128)} %get-tuple-element.27), channel_id=1, source_target_pairs={{0,4},{4,0},{1,5},{5,1},{2,6},{6,2},{3,7},{7,3},{8,12},{12,8},{9,1... | collective-permute-start | bytes 1179656 | tf_op jit(solution)/shard_map/ppermute | solution.py:621
  5.6 1.6 %collective-permute-start.1 = (f32[2,2,32,128]{3,2,1,0:T(8,128)}, f32[2,2,32,128]{3,2,1,0:T(8,128)S(1)}, u32[]{:S(2)}, u32[]{:S(2)}) collective-permute-start(f32[2,2,32,128]{3,2,1,0:T(8,128)} %get-tuple-element.28), channel_id=1, source_target_pairs={{0,8},{8,16},{16,24},{24,0},{1,9},{9,17},{17,25},{25,1},{2,10},{10... | collective-permute-start | bytes 196616 | tf_op jit(solution)/shard_map/ppermute | solution.py:627
  7.2 2.6 %collective-permute-start.2 = (f32[2,2,32,128]{3,2,1,0:T(8,128)}, f32[2,2,32,128]{3,2,1,0:T(8,128)S(1)}, u32[]{:S(2)}, u32[]{:S(2)}) collective-permute-start(f32[2,2,32,128]{3,2,1,0:T(8,128)} %get-tuple-element.28), channel_id=1, source_target_pairs={{0,16},{8,24},{16,0},{24,8},{1,17},{9,25},{17,1},{25,9},{2,18},{10... | collective-permute-start | bytes 196616 | tf_op jit(solution)/shard_map/ppermute | solution.py:627
  9.7 1.3 %collective-permute-start.3 = (f32[2,2,32,128]{3,2,1,0:T(8,128)}, f32[2,2,32,128]{3,2,1,0:T(8,128)S(1)}, u32[]{:S(2)}, u32[]{:S(2)}) collective-permute-start(f32[2,2,32,128]{3,2,1,0:T(8,128)} %get-tuple-element.28), channel_id=1, source_target_pairs={{0,24},{8,0},{16,8},{24,16},{1,25},{9,1},{17,9},{25,17},{2,26},{10... | collective-permute-start | bytes 196616 | tf_op jit(solution)/shard_map/ppermute | solution.py:627
  11.1 2.1 %shard_map.122.refs_5_.refs_6_.count = f32[16,72,128]{2,1,0:T(8,128)S(1)} custom-call(s32[1,1024]{1,0:T(1,128)S(1)} %bitcast.3), custom_call_target="tpu_custom_call" | custom-call | flops 301989888 | bytes 589824 | tf_op jit(solution)/shard_map/pallas_call | solution.py:594
  13.2 1.5 %collective-permute-done.2.refs_3_ = f32[2,2,32,128]{3,2,1,0:T(8,128)S(1)} collective-permute-done((f32[2,2,32,128]{3,2,1,0:T(8,128)}, f32[2,2,32,128]{3,2,1,0:T(8,128)S(1)}, u32[]{:S(2)}, u32[]{:S(2)}) %collective-permute-start.2) | collective-permute-done | bytes 65568 | tf_op jit(solution)/shard_map/ppermute | solution.py:627
  16.3 5.5 %collective-permute-done.5.came = f32[2,8,32,128]{3,2,1,0:T(8,128)S(1)} collective-permute-done((f32[2,8,32,128]{3,2,1,0:T(8,128)S(1)}, f32[2,8,32,128]{3,2,1,0:T(8,128)S(1)}, u32[]{:S(2)}, u32[]{:S(2)}) %collective-permute-start.5) | collective-permute-done | bytes 262176 | tf_op jit(solution)/shard_map/ppermute | solution.py:621
  22.0 1.6 %collective-permute-start.6 = (f32[2,16,8,128]{3,2,1,0:T(8,128)S(1)}, f32[2,16,8,128]{3,2,1,0:T(8,128)S(1)}, u32[]{:S(2)}, u32[]{:S(2)}) collective-permute-start(f32[2,16,8,128]{3,2,1,0:T(8,128)S(1)} %shard_map.126), channel_id=1, source_target_pairs={{0,2},{1,3},{2,0},{3,1},{4,6},{5,7},{6,4},{7,5},{8,10},{9,11},{10,... | collective-permute-start | bytes 393224 | tf_op jit(solution)/shard_map/ppermute | solution.py:646
  23.9 1.6 %collective-permute-start.8 = (f32[2,16,8,128]{3,2,1,0:T(8,128)S(1)}, f32[2,16,8,128]{3,2,1,0:T(8,128)S(1)}, u32[]{:S(2)}, u32[]{:S(2)}) collective-permute-start(f32[2,16,8,128]{3,2,1,0:T(8,128)S(1)} %shard_map.127.refs_7_), channel_id=1, source_target_pairs={{0,2},{1,3},{2,0},{3,1},{4,6},{5,7},{6,4},{7,5},{8,10},{9,11},{10,... | collective-permute-start | bytes 393224 | tf_op jit(solution)/shard_map/ppermute | solution.py:646
  25.5 2.9 %collective-permute-done.6.refs_5_ = f32[2,16,8,128]{3,2,1,0:T(8,128)S(1)} collective-permute-done((f32[2,16,8,128]{3,2,1,0:T(8,128)S(1)}, f32[2,16,8,128]{3,2,1,0:T(8,128)S(1)}, u32[]{:S(2)}, u32[]{:S(2)}) %collective-permute-start.6) | collective-permute-done | bytes 131104 | tf_op jit(solution)/shard_map/ppermute | solution.py:646
  28.4 2.3 %shard_map.128 = (f32[18,72,128]{2,1,0:T(8,128)S(1)}, f32[16,72,128]{2,1,0:T(8,128)S(1)}, f32[17,72,128]{2,1,0:T(8,128)S(1)}, f32[16,72,128]{2,1,0:T(8,128)S(1)}...) custom-call(f32[16]{0:T(128)S(1)} %copy-done.6, f32[16]{0:T(128)S(1)} %copy-done.7, ...), custom_call_target="tpu_custom_call" | custom-call | tf_op jit(solution)/shard_map/pallas_call | solution.py:594
  30.8 4.0 %shard_map.129 = (f32[16,72,128]{2,1,0:T(8,128)S(1)}, f32[20,8,128]{2,1,0:T(8,128)S(1)}) custom-call(f32[18,72,128]{2,1,0:T(8,128)S(1)} %get-tuple-element.31.phi, f32[16,72,128]{2,1,0:T(8,128)S(1)} %get-tuple-element.32.diag, f32[17,72,128]{2,1,0:T(8,128)S(1)} %get-tuple-element.33.fx, f32[16,72,128]{2,1,0:T(8,128)S(1)} %get-tuple-element.34.fy, ...), custom_call_target="tpu_custom_call" | custom-call | tf_op jit(solution)/shard_map/pallas_call | solution.py:594
  34.8 1.6 %collective-permute-start.9 = (f32[20,8,128]{2,1,0:T(8,128)S(1)}, f32[20,8,128]{2,1,0:T(8,128)S(1)}, u32[]{:S(2)}, u32[]{:S(2)}) collective-permute-start(f32[20,8,128]{2,1,0:T(8,128)S(1)} %get-tuple-element.38.sent), channel_id=1, source_target_pairs={{0,2},{1,3},{2,0},{3,1},{4,6},{5,7},{6,4},{7,5},{8,10},{9,11},{10,... | collective-permute-start | bytes 245768 | tf_op jit(solution)/shard_map/ppermute | solution.py:646
  36.4 2.9 %collective-permute-done.9.came = f32[20,8,128]{2,1,0:T(8,128)S(1)} collective-permute-done((f32[20,8,128]{2,1,0:T(8,128)S(1)}, f32[20,8,128]{2,1,0:T(8,128)S(1)}, u32[]{:S(2)}, u32[]{:S(2)}) %collective-permute-start.9) | collective-permute-done | bytes 81952 | tf_op jit(solution)/shard_map/ppermute | solution.py:646
  39.3 4.1 %shard_map.130 = (f32[2,16,32,128]{3,2,1,0:T(8,128)S(1)}, f32[2,16,32,128]{3,2,1,0:T(8,128)S(1)}) custom-call(f32[18,72,128]{2,1,0:T(8,128)S(1)} %get-tuple-element.31.phi, f32[16,72,128]{2,1,0:T(8,128)S(1)} %get-tuple-element.37.change, f32[16,72,128]{2,1,0:T(8,128)S(1)} %get-tuple-element.32.diag, f32[17,72,128]{2,1,0:T(8,128)S(1)} %get-tuple-element.33.fx, ...), custom_call_target="tpu_custom_call" | custom-call | tf_op jit(solution)/shard_map/pallas_call | solution.py:594
  43.5 1.9 %collective-permute-done.10.came = f32[2,16,32,128]{3,2,1,0:T(8,128)S(1)} collective-permute-done((f32[2,16,32,128]{3,2,1,0:T(8,128)S(1)}, f32[2,16,32,128]{3,2,1,0:T(8,128)S(1)}, u32[]{:S(2)}, u32[]{:S(2)}) %collective-permute-start.10) | collective-permute-done | bytes 524320 | tf_op jit(solution)/shard_map/ppermute | solution.py:624
  46.8 1.3 %collective-permute-start.11 = (f32[2,2,2,32,128]{4,3,2,1,0:T(8,128)S(1)}, f32[2,2,2,32,128]{4,3,2,1,0:T(8,128)S(1)}, u32[]{:S(2)}, u32[]{:S(2)}) collective-permute-start(f32[2,2,2,32,128]{4,3,2,1,0:T(8,128)S(1)} %get-tuple-element.42), channel_id=1, source_target_pairs={{0,4},{4,0},{1,5},{5,1},{2,6},{6,2},{3,7},{7,3},{8,12},{12,8},{9,1... | collective-permute-start | bytes 393224 | tf_op jit(solution)/shard_map/ppermute | solution.py:621
  48.1 4.3 %collective-permute-done.12.came = f32[2,2,2,32,128]{4,3,2,1,0:T(8,128)S(1)} collective-permute-done((f32[2,2,2,32,128]{4,3,2,1,0:T(8,128)S(1)}, f32[2,2,2,32,128]{4,3,2,1,0:T(8,128)S(1)}, u32[]{:S(2)}, u32[]{:S(2)}) %collective-permute-start.12) | collective-permute-done | bytes 131104 | tf_op jit(solution)/shard_map/ppermute | solution.py:621
  52.5 1.6 %collective-permute-start.13 = (f32[2,2,32,128]{3,2,1,0:T(8,128)S(1)}, f32[2,2,32,128]{3,2,1,0:T(8,128)S(1)}, u32[]{:S(2)}, u32[]{:S(2)}) collective-permute-start(f32[2,2,32,128]{3,2,1,0:T(8,128)S(1)} %get-tuple-element.45), channel_id=1, source_target_pairs={{0,16},{8,24},{16,0},{24,8},{1,17},{9,25},{17,1},{25,9},{2,18},{10... | collective-permute-start | bytes 196616 | tf_op jit(solution)/shard_map/ppermute | solution.py:627
  54.1 3.1 %collective-permute-start.14 = (f32[2,2,32,128]{3,2,1,0:T(8,128)S(1)}, f32[2,2,32,128]{3,2,1,0:T(8,128)S(1)}, u32[]{:S(2)}, u32[]{:S(2)}) collective-permute-start(f32[2,2,32,128]{3,2,1,0:T(8,128)S(1)} %get-tuple-element.46), channel_id=1, source_target_pairs={{0,24},{8,0},{16,8},{24,16},{1,25},{9,1},{17,9},{25,17},{2,26},{10... | collective-permute-start | bytes 196616 | tf_op jit(solution)/shard_map/ppermute | solution.py:627
  58.1 1.0 %collective-permute-done.14.refs_3_ = f32[2,2,32,128]{3,2,1,0:T(8,128)S(1)} collective-permute-done((f32[2,2,32,128]{3,2,1,0:T(8,128)S(1)}, f32[2,2,32,128]{3,2,1,0:T(8,128)S(1)}, u32[]{:S(2)}, u32[]{:S(2)}) %collective-permute-start.14) | collective-permute-done | bytes 65568 | tf_op jit(solution)/shard_map/ppermute | solution.py:627
  59.1 4.2 %collective-permute-done.15.refs_4_ = f32[2,2,32,128]{3,2,1,0:T(8,128)S(1)} collective-permute-done((f32[2,2,32,128]{3,2,1,0:T(8,128)S(1)}, f32[2,2,32,128]{3,2,1,0:T(8,128)S(1)}, u32[]{:S(2)}, u32[]{:S(2)}) %collective-permute-start.15) | collective-permute-done | bytes 65568 | tf_op jit(solution)/shard_map/ppermute | solution.py:627
  64.0 10.0 %all_to_all.5.tiles = f32[32,8,128]{2,1,0:T(8,128)S(1)} all-to-all(f32[32,8,128]{2,1,0:T(8,128)S(1)} %broadcast_in_dim.3), channel_id=1, replica_groups=mesh['src'=4,'gx'=2,'gy'=4] {'src','gx','gy'}, dimensions={0} | all-to-all | bytes 262144 | tf_op jit(solution)/shard_map/all_to_all | solution.py:699
  (43 shorter events, 5.4 us)
Async XLA Ops:
  2.6 8.5 %copy-start.8 = (s32[1024]{0:T(1024)S(1)}, s32[1024]{0:T(1024)}, u32[]{:S(2)}) copy-start(s32[1024]{0:T(1024)} %param.14) | copy-start | bytes 12292
  2.6 13.1 %collective-permute-start = (f32[3,8,32,128]{3,2,1,0:T(8,128)}, f32[3,8,32,128]{3,2,1,0:T(8,128)S(1)}, u32[]{:S(2)}, u32[]{:S(2)}) collective-permute-start(f32[3,8,32,128]{3,2,1,0:T(8,128)} %get-tuple-element.27), channel_id=1, source_target_pairs={{0,4},{4,0},{1,5},{5,1},{2,6},{6,2},{3,7},{7,3},{8,12},{12,8},{9,1... | collective-permute-start | bytes 1179656 | tf_op jit(solution)/shard_map/ppermute | solution.py:621
  5.6 7.7 %collective-permute-start.1 = (f32[2,2,32,128]{3,2,1,0:T(8,128)}, f32[2,2,32,128]{3,2,1,0:T(8,128)S(1)}, u32[]{:S(2)}, u32[]{:S(2)}) collective-permute-start(f32[2,2,32,128]{3,2,1,0:T(8,128)} %get-tuple-element.28), channel_id=1, source_target_pairs={{0,8},{8,16},{16,24},{24,0},{1,9},{9,17},{17,25},{25,1},{2,10},{10... | collective-permute-start | bytes 196616 | tf_op jit(solution)/shard_map/ppermute | solution.py:627
  7.2 7.6 %collective-permute-start.2 = (f32[2,2,32,128]{3,2,1,0:T(8,128)}, f32[2,2,32,128]{3,2,1,0:T(8,128)S(1)}, u32[]{:S(2)}, u32[]{:S(2)}) collective-permute-start(f32[2,2,32,128]{3,2,1,0:T(8,128)} %get-tuple-element.28), channel_id=1, source_target_pairs={{0,16},{8,24},{16,0},{24,8},{1,17},{9,25},{17,1},{25,9},{2,18},{10... | collective-permute-start | bytes 196616 | tf_op jit(solution)/shard_map/ppermute | solution.py:627
  9.7 5.0 %collective-permute-start.3 = (f32[2,2,32,128]{3,2,1,0:T(8,128)}, f32[2,2,32,128]{3,2,1,0:T(8,128)S(1)}, u32[]{:S(2)}, u32[]{:S(2)}) collective-permute-start(f32[2,2,32,128]{3,2,1,0:T(8,128)} %get-tuple-element.28), channel_id=1, source_target_pairs={{0,24},{8,0},{16,8},{24,16},{1,25},{9,1},{17,9},{25,17},{2,26},{10... | collective-permute-start | bytes 196616 | tf_op jit(solution)/shard_map/ppermute | solution.py:627
  11.1 3.6 %copy-start = (f32[8,32,32]{2,1,0:T(8,128)S(1)}, f32[8,32,32]{2,1,0:T(8,128)}, u32[]{:S(2)}) copy-start(f32[8,32,32]{2,1,0:T(8,128)} %vk.3) | copy-start | bytes 98308
  11.1 3.6 %copy-start.1 = (f32[8,32,32]{2,1,0:T(8,128)S(1)}, f32[8,32,32]{2,1,0:T(8,128)}, u32[]{:S(2)}) copy-start(f32[8,32,32]{2,1,0:T(8,128)} %va.3) | copy-start | bytes 98308
  13.2 2.4 %copy-start.2 = (f32[4,8,32,128]{3,2,1,0:T(8,128)S(1)}, f32[4,8,32,128]{3,2,1,0:T(8,128)}, u32[]{:S(2)}) copy-start(f32[4,8,32,128]{3,2,1,0:T(8,128)} %refs_0_.4) | copy-start | bytes 1572868
  15.2 6.6 %collective-permute-start.5 = (f32[2,8,32,128]{3,2,1,0:T(8,128)S(1)}, f32[2,8,32,128]{3,2,1,0:T(8,128)S(1)}, u32[]{:S(2)}, u32[]{:S(2)}) collective-permute-start(f32[2,8,32,128]{3,2,1,0:T(8,128)S(1)} %shard_map.123.refs_3_.own), channel_id=1, source_target_pairs={{0,4},{4,0},{1,5},{5,1},{2,6},{6,2},{3,7},{7,3},{8,12},{12,8},{9,1... | collective-permute-start | bytes 786440 | tf_op jit(solution)/shard_map/ppermute | solution.py:621
  16.3 5.7 %collective-permute-start.4 = (f32[2,16,32,128]{3,2,1,0:T(8,128)S(1)}, f32[2,16,32,128]{3,2,1,0:T(8,128)S(1)}, u32[]{:S(2)}, u32[]{:S(2)}) collective-permute-start(f32[2,16,32,128]{3,2,1,0:T(8,128)S(1)} %get-tuple-element.30.refs_1_.refs_3_), channel_id=1, source_target_pairs={{0,1},{1,0},{2,3},{3,2},{4,5},{5,4},{6,7},{7,6},{8,9},{9,8},{10,11... | collective-permute-start | bytes 1572872 | tf_op jit(solution)/shard_map/ppermute | solution.py:624
  21.9 2.0 %collective-permute-start.7 = (f32[2,16,32,128]{3,2,1,0:T(8,128)S(1)}, f32[2,16,32,128]{3,2,1,0:T(8,128)S(1)}, u32[]{:S(2)}, u32[]{:S(2)}) collective-permute-start(f32[2,16,32,128]{3,2,1,0:T(8,128)S(1)} %shard_map.125.refs_3_.fields), channel_id=1, source_target_pairs={{0,1},{1,0},{2,3},{3,2},{4,5},{5,4},{6,7},{7,6},{8,9},{9,8},{10,11... | collective-permute-start | bytes 1572872 | tf_op jit(solution)/shard_map/ppermute | solution.py:624
  22.0 6.4 %copy-start.6 = (f32[16]{0:T(128)S(1)}, f32[16]{0:T(128)}, u32[]{:S(2)}) copy-start(f32[16]{0:T(128)} %refs_0_.5) | copy-start | bytes 196
  22.0 6.4 %copy-start.7 = (f32[16]{0:T(128)S(1)}, f32[16]{0:T(128)}, u32[]{:S(2)}) copy-start(f32[16]{0:T(128)} %refs_1_.5) | copy-start | bytes 196
  22.0 6.4 %collective-permute-start.6 = (f32[2,16,8,128]{3,2,1,0:T(8,128)S(1)}, f32[2,16,8,128]{3,2,1,0:T(8,128)S(1)}, u32[]{:S(2)}, u32[]{:S(2)}) collective-permute-start(f32[2,16,8,128]{3,2,1,0:T(8,128)S(1)} %shard_map.126), channel_id=1, source_target_pairs={{0,2},{1,3},{2,0},{3,1},{4,6},{5,7},{6,4},{7,5},{8,10},{9,11},{10,... | collective-permute-start | bytes 393224 | tf_op jit(solution)/shard_map/ppermute | solution.py:646
  23.9 6.9 %collective-permute-start.8 = (f32[2,16,8,128]{3,2,1,0:T(8,128)S(1)}, f32[2,16,8,128]{3,2,1,0:T(8,128)S(1)}, u32[]{:S(2)}, u32[]{:S(2)}) collective-permute-start(f32[2,16,8,128]{3,2,1,0:T(8,128)S(1)} %shard_map.127.refs_7_), channel_id=1, source_target_pairs={{0,2},{1,3},{2,0},{3,1},{4,6},{5,7},{6,4},{7,5},{8,10},{9,11},{10,... | collective-permute-start | bytes 393224 | tf_op jit(solution)/shard_map/ppermute | solution.py:646
  34.8 4.5 %collective-permute-start.9 = (f32[20,8,128]{2,1,0:T(8,128)S(1)}, f32[20,8,128]{2,1,0:T(8,128)S(1)}, u32[]{:S(2)}, u32[]{:S(2)}) collective-permute-start(f32[20,8,128]{2,1,0:T(8,128)S(1)} %get-tuple-element.38.sent), channel_id=1, source_target_pairs={{0,2},{1,3},{2,0},{3,1},{4,6},{5,7},{6,4},{7,5},{8,10},{9,11},{10,... | collective-permute-start | bytes 245768 | tf_op jit(solution)/shard_map/ppermute | solution.py:646
  43.4 2.0 %collective-permute-start.10 = (f32[2,16,32,128]{3,2,1,0:T(8,128)S(1)}, f32[2,16,32,128]{3,2,1,0:T(8,128)S(1)}, u32[]{:S(2)}, u32[]{:S(2)}) collective-permute-start(f32[2,16,32,128]{3,2,1,0:T(8,128)S(1)} %get-tuple-element.40), channel_id=1, source_target_pairs={{0,1},{1,0},{2,3},{3,2},{4,5},{5,4},{6,7},{7,6},{8,9},{9,8},{10,11... | collective-permute-start | bytes 1572872 | tf_op jit(solution)/shard_map/ppermute | solution.py:624
  46.0 6.4 %collective-permute-start.12 = (f32[2,2,2,32,128]{4,3,2,1,0:T(8,128)S(1)}, f32[2,2,2,32,128]{4,3,2,1,0:T(8,128)S(1)}, u32[]{:S(2)}, u32[]{:S(2)}) collective-permute-start(f32[2,2,2,32,128]{4,3,2,1,0:T(8,128)S(1)} %get-tuple-element.44), channel_id=1, source_target_pairs={{0,4},{4,0},{1,5},{5,1},{2,6},{6,2},{3,7},{7,3},{8,12},{12,8},{9,1... | collective-permute-start | bytes 393224 | tf_op jit(solution)/shard_map/ppermute | solution.py:621
  46.8 10.4 %collective-permute-start.11 = (f32[2,2,2,32,128]{4,3,2,1,0:T(8,128)S(1)}, f32[2,2,2,32,128]{4,3,2,1,0:T(8,128)S(1)}, u32[]{:S(2)}, u32[]{:S(2)}) collective-permute-start(f32[2,2,2,32,128]{4,3,2,1,0:T(8,128)S(1)} %get-tuple-element.42), channel_id=1, source_target_pairs={{0,4},{4,0},{1,5},{5,1},{2,6},{6,2},{3,7},{7,3},{8,12},{12,8},{9,1... | collective-permute-start | bytes 393224 | tf_op jit(solution)/shard_map/ppermute | solution.py:621
  52.5 5.6 %collective-permute-start.13 = (f32[2,2,32,128]{3,2,1,0:T(8,128)S(1)}, f32[2,2,32,128]{3,2,1,0:T(8,128)S(1)}, u32[]{:S(2)}, u32[]{:S(2)}) collective-permute-start(f32[2,2,32,128]{3,2,1,0:T(8,128)S(1)} %get-tuple-element.45), channel_id=1, source_target_pairs={{0,16},{8,24},{16,0},{24,8},{1,17},{9,25},{17,1},{25,9},{2,18},{10... | collective-permute-start | bytes 196616 | tf_op jit(solution)/shard_map/ppermute | solution.py:627
  54.1 9.2 %copy-start.4 = (f32[8,32,32]{2,1,0:T(8,128)S(1)}, f32[8,32,32]{2,1,0:T(8,128)}, u32[]{:S(2)}) copy-start(f32[8,32,32]{2,1,0:T(8,128)} %refs_7_.1) | copy-start | bytes 98308
  54.1 9.2 %copy-start.5 = (f32[8,32,32]{2,1,0:T(8,128)S(1)}, f32[8,32,32]{2,1,0:T(8,128)}, u32[]{:S(2)}) copy-start(f32[8,32,32]{2,1,0:T(8,128)} %refs_8_.1) | copy-start | bytes 98308
  54.1 5.0 %collective-permute-start.14 = (f32[2,2,32,128]{3,2,1,0:T(8,128)S(1)}, f32[2,2,32,128]{3,2,1,0:T(8,128)S(1)}, u32[]{:S(2)}, u32[]{:S(2)}) collective-permute-start(f32[2,2,32,128]{3,2,1,0:T(8,128)S(1)} %get-tuple-element.46), channel_id=1, source_target_pairs={{0,24},{8,0},{16,8},{24,16},{1,25},{9,1},{17,9},{25,17},{2,26},{10... | collective-permute-start | bytes 196616 | tf_op jit(solution)/shard_map/ppermute | solution.py:627
  57.2 6.1 %collective-permute-start.15 = (f32[2,2,32,128]{3,2,1,0:T(8,128)S(1)}, f32[2,2,32,128]{3,2,1,0:T(8,128)S(1)}, u32[]{:S(2)}, u32[]{:S(2)}) collective-permute-start(f32[2,2,32,128]{3,2,1,0:T(8,128)S(1)} %get-tuple-element.47), channel_id=1, source_target_pairs={{0,8},{8,16},{16,24},{24,0},{1,9},{9,17},{17,25},{25,1},{2,10},{10... | collective-permute-start | bytes 196616 | tf_op jit(solution)/shard_map/ppermute | solution.py:627
  (1 other events, 2.4 us)

commit v8 on v7

--- a/solution.py
+++ b/solution.py
@@ -213,7 +213,8 @@
     copies[2].wait()
 
 
-def count_kernel(dets, count, *, ny, nz, half, halo):
+def count_kernel(dets, beta_prev, count, beta_row, *, ny, nz, half, halo):
+    beta_row[...] = jnp.full(beta_row.shape, beta_prev[0])
     _, _, y, _ = places(2)
     planes, rows, _ = count.shape
     flat = dets[...]
@@ -272,7 +273,7 @@
             for j in range(n):
                 plane = jnp.concatenate([own[f][n * q + j]] * n, axis=1)
                 for k in range(1, n):
-                    home = (s - k + n) % n
+                    home = s ^ k
                     moved = pltpu.roll(blocks[k - 1], ((home - j + n) % n) * slab, 1)
                     plane = jnp.where(lane == home, moved, plane)
                 full[f, n * q + j] = plane
@@ -285,22 +286,44 @@
     fields[:, pl.ds(cx * (1 - x), cx)] = came[...]
 
 
-def edge_rows(ref, halo, y):
-    return ref[pl.ds(0, ref.shape[0]), pl.ds((ref.shape[1] - halo) * (1 - y), halo), :]
+def edge_shape(planes, lanes):
+    return planes // GROUP, GROUP * REACH, lanes
+
+
+def packed_edges(tiles):
+    return jnp.concatenate([tile[:REACH] for tile in tiles], axis=0)
+
+
+def edge_tile(packed, j, y):
+    rows = packed[REACH * j : REACH * (j + 1)]
+    tile = jnp.concatenate([rows, jnp.zeros((HALO - REACH, rows.shape[1]), jnp.float32)], axis=0)
+    return jnp.where(y == 0, tile, shifted(tile, HALO - REACH, 0))
+
+
+def near_rows(ref, i, first, y):
+    tile = ref[i, pl.ds(first, HALO), :]
+    return jnp.where(y == 0, shifted(tile, REACH - HALO, 0), tile)
+
+
+def edges_of(own, got, edge, y, c):
+    first = (own.shape[1] - HALO) * (1 - y)
+    for g in range(edge.shape[0]):
+        edge[g] = packed_edges([
+            jnp.where(c != y, near_rows(own, GROUP * g + j, first, y), near_rows(got, GROUP * g + j, first, y))
+            for j in range(GROUP)
+        ])
 
 
 def photon_edge_kernel(mine, fields, got, edge):
     _, _, y, c = places(2)
-    halo = edge.shape[2]
-    edge[0] = jnp.where(c != y, edge_rows(mine, halo, y), edge_rows(got.at[0], halo, y))
-    edge[1] = jnp.where(c != y, edge_rows(fields.at[1], halo, y), edge_rows(got.at[1], halo, y))
+    edges_of(mine, got.at[0], edge.at[0], y, c)
+    edges_of(fields.at[1], got.at[1], edge.at[1], y, c)
 
 
 def vector_edge_kernel(fields, got, edge):
     _, _, y, c = places(2)
-    halo = edge.shape[2]
     for f in range(2):
-        edge[f] = jnp.where(c != y, edge_rows(fields.at[f], halo, y), edge_rows(got.at[f], halo, y))
+        edges_of(fields.at[f], got.at[f], edge.at[f], y, c)
 
 
 def solve(b, bufs, diag, fx, fy, fz, unroll):
@@ -328,13 +351,16 @@
     return jnp.sum(value.reshape(-1, 8, value.shape[1]), axis=0)
 
 
-def framed(ref, shift, parts, planes, cy, halo, y, c):
-    own, got, edge = parts
+def framed(ref, shift, own, got, edge, y, c):
+    planes, cy, _ = own.shape
     there = pl.ds(shift, planes)
-    base = halo * y
-    ref[there, pl.ds(base + cy * c, cy), :] = own
-    ref[there, pl.ds(base + cy * (1 - c), cy), :] = got
-    ref[there, pl.ds(2 * cy * (1 - y), halo), :] = edge
+    base = HALO * y
+    ref[there, pl.ds(base + cy * c, cy), :] = own[...]
+    ref[there, pl.ds(base + cy * (1 - c), cy), :] = got[...]
+    for g in range(edge.shape[0]):
+        packed = edge[g]
+        for j in range(GROUP):
+            ref[shift + GROUP * g + j, pl.ds(2 * cy * (1 - y), HALO), :] = edge_tile(packed, j, y)
 
 
 def blank_ends(*refs):
@@ -351,17 +377,14 @@
 
 def stencil_kernel(
     kap_table, abs_table, mine, fields, got, edge, count,
-    phi, diag, fx, fy, fz, sums,
+    diag, fx, fy, fz, sums,
     labels, kap,
 ):
     _, _, y, c = places(2)
     planes, cy, lanes = mine.shape
-    halo = edge.shape[2]
-    rows = 2 * cy + halo
-    place = (planes, cy, halo, y, c)
-    framed(phi, 1, (mine[...], got[0], edge[0]), *place)
-    framed(labels, 0, (fields[1], got[1], edge[1]), *place)
-    blank_ends(phi, kap)
+    rows = 2 * cy + HALO
+    framed(labels, 0, fields.at[1], got.at[1], edge.at[1], y, c)
+    blank_ends(kap)
     blank = jnp.zeros((rows, lanes), jnp.float32)
     lane = index_along((rows, lanes), 1)
     kap_row, abs_row = blank, blank
@@ -377,7 +400,7 @@
 
     lax.fori_loop(0, planes, look_up, 0, unroll=4)
     fx[0] = 0.5 * kap[1]
-    owned = owned_rows((rows, lanes), halo * y, 2 * cy)
+    base = HALO * y
 
     def set_up(i, carry):
         k = kap[i + 1]
@@ -388,27 +411,28 @@
         fz[i] = jnp.where(lane == lanes - 1, 0.0, along_z)
         back_y, back_z = 0.5 * (k + beyond(k, -1, 0)), 0.5 * (k + beyond(k, -1, 1))
         diag[i] = diag[i] + fx[i] + along_x + along_y + back_y + along_z + back_z
-        p = phi[i + 1]
-        part = jnp.where(owned, count[i], 0.0) * p
-        return carry[0] + folded(part), carry[1] + folded(part * p)
+        total, square = carry
+        for p, at in ((mine[i], c), (got[0, i], 1 - c)):
+            part = count[i, pl.ds(base + cy * at, cy), :] * p
+            total, square = total + folded(part), square + folded(part * p)
+        return total, square
 
     zero = jnp.zeros((8, lanes), jnp.float32)
     sums[0], sums[1] = lax.fori_loop(0, planes, set_up, (zero, zero), unroll=4)
 
 
 def first_kernel(
-    phi, diag, fx, fy, fz, count, sums, fields, got, edge,
-    change, message,
+    diag, fx, fy, fz, count, sums, mine, got_photon, vector, got_vector, photon_edge, edge,
+    phi, change, message,
     vk, va, b, buf_a, buf_b,
 ):
     _, _, y, c = places(2)
     planes, rows, lanes = change.shape
-    halo = edge.shape[2]
-    cy = (rows - halo) // 2
-    place = (planes, cy, halo, y, c)
-    framed(vk, 1, (fields[0], got[0], edge[0]), *place)
-    framed(va, 0, (fields[1], got[1], edge[1]), *place)
-    blank_ends(vk, buf_a, buf_b)
+    cy = mine.shape[1]
+    framed(phi, 1, mine, got_photon.at[0], photon_edge.at[0], y, c)
+    framed(vk, 1, vector.at[0], got_vector.at[0], edge.at[0], y, c)
+    framed(va, 0, vector.at[1], got_vector.at[1], edge.at[1], y, c)
+    blank_ends(phi, vk, buf_a, buf_b)
     theta, _ = chebyshev_scalars()
 
     def set_up(i, carry):
@@ -425,7 +449,7 @@
 
     lax.fori_loop(0, planes, set_up, 0, unroll=4)
     found = solve(b, (buf_a, buf_b), diag, fx, fy, fz, 16)
-    owned = owned_rows((rows, lanes), halo * y, 2 * cy)
+    owned = owned_rows((rows, lanes), HALO * y, 2 * cy)
 
     def add_up(i, carry):
         u = found[i + 1]
@@ -435,10 +459,12 @@
 
     zero = jnp.zeros((8, lanes), jnp.float32)
     seen, cross = lax.fori_loop(0, planes, add_up, (zero, zero), unroll=4)
-    edge = (2 * cy - halo) * (1 - y) + halo * y
-    message[pl.ds(0, planes)] = found[pl.ds(1, planes), pl.ds(edge, halo), :]
-    for i, part in enumerate((sums[0], seen, cross, sums[1])):
-        message[planes + i] = part
+    first = (2 * cy - HALO) * (1 - y) + HALO * y
+    for g, part in enumerate((sums[0], seen, cross, sums[1])):
+        message[g, pl.ds(0, GROUP * REACH), :] = packed_edges(
+            [near_rows(found, 1 + GROUP * g + j, first, y) for j in range(GROUP)]
+        )
+        message[g, pl.ds(GROUP * REACH, 8), :] = part
 
 
 def second_kernel(
@@ -449,13 +475,13 @@
 ):
     _, _, y, c = places(2)
     planes, rows, lanes = change.shape
-    halo = came.shape[1]
-    cy = (rows - halo) // 2
-    base = halo * y
-    edge = pl.ds(2 * cy * (1 - y), halo)
-    one = jnp.ones((1, 1), jnp.float32)
+    cy = (rows - HALO) // 2
+    base = HALO * y
+    edge = pl.ds(2 * cy * (1 - y), HALO)
+    tail = pl.ds(GROUP * REACH, 8)
     total, seen_sum, cross, square = (
-        jnp.sum(sent[planes + i] + came[planes + i]) * one for i in range(4)
+        jnp.sum(jnp.sum(sent[g, tail, :] + came[g, tail, :], axis=0, keepdims=True), axis=1, keepdims=True)
+        for g in range(4)
     )
     mean = total / dets
     part = seen_sum / total
@@ -471,12 +497,14 @@
         value = weighted(count[i], change[i], phi[i + 1])
         b[i] = value
         buf_a[i + 1] = value * (1.0 / theta)
-        value = weighted(count[i, edge, :], came[i], phi[i + 1, edge, :])
+        return carry
+
+    lax.fori_loop(0, planes, set_up, 0, unroll=4)
+    for i in range(planes):
+        u = edge_tile(came[i // GROUP], i % GROUP, y)
+        value = weighted(count[i, edge, :], u, phi[i + 1, edge, :])
         b[i, edge, :] = value
         buf_a[i + 1, edge, :] = value * (1.0 / theta)
-        return carry
-
-    lax.fori_loop(0, planes, set_up, 0, unroll=4)
     dual = solve(b, (buf_a, buf_b), diag, fx, fy, fz, 16)
 
     def product(i, carry):
@@ -508,7 +536,7 @@
                 at = n * (groups * (x if h == 0 else 1 - x) + q)
                 planes = [own[f, at + j] + came[f, at + j] for j in range(n)]
                 for k in range(n):
-                    to = (s + k) % n
+                    to = s ^ k
                     piece = jnp.zeros((cy, lanes), jnp.float32)
                     for j in range(n):
                         moved = pltpu.roll(planes[j], ((j - to + n) % n) * slab, 1)
@@ -526,10 +554,17 @@
         out[...] = kept[first + i] + came[i]
 
 
-def project_kernel(*refs, n):
+def sum_kernel(*refs):
+    total = refs[0][...]
+    for ref in refs[1:-1]:
+        total = total + ref[...]
+    refs[-1][...] = total
+
+
+def project_kernel(*refs, parts_n, n):
     beta_prev = refs[0]
-    parts = refs[1 : 1 + n]
-    vk, va, qk, qa, w_k, w_a, tile = refs[1 + n :]
+    parts = refs[1 : 1 + parts_n]
+    vk, va, qk, qa, w_k, w_a, tile = refs[1 + parts_n :]
     s, x, y, c = places(2)
     slab = 128 // n
     for f, (q_ref, w) in enumerate(((qk, w_k), (qa, w_a))):
@@ -537,7 +572,7 @@
             whole = sum(part[f, q] for part in parts[1:]) + parts[0][f, q]
             for j in range(n):
                 i = n * q + j
-                w[i] = whole[:, slab * j : slab * (j + 1)] - beta_prev[...] * q_ref[i]
+                w[i] = whole[:, slab * j : slab * (j + 1)] - beta_prev[:, : vk.shape[2]] * q_ref[i]
 
     def dot(a, b):
         return jnp.sum(jnp.sum(a * b, axis=0))
@@ -603,6 +638,8 @@
 
 
 HALO = 8
+REACH = 6
+GROUP = 4
 
 
 def per_device_paired(
@@ -624,7 +661,7 @@
         return lax.ppermute(value, "gy", [(0, 1), (1, 0), (2, 3), (3, 2)])
 
     def along_z(value, k):
-        return lax.ppermute(value, "src", [(i, (i + k) % n) for i in range(n)])
+        return lax.ppermute(value, "src", [(i, i ^ k) for i in range(n)])
 
     block = (cx, cy, cz)
     float_block = lambda *shape: (shape, jnp.float32)
@@ -634,18 +671,18 @@
         background, labels, v_kappa, v_absorb, hbm=(0, 1, 2, 3),
         scratch=(raw_labels, float_block(2, *v_kappa.shape)), copies=4, mib=60,
     )
+    long = pl.CostEstimate(flops=10**9, bytes_accessed=2**26, transcendentals=0)
     came = swap_x(message)
     slabs = [along_z(packed, k) for k in range(1, n)]
-    (count,) = run(
+    count, beta_row = run(
         functools.partial(count_kernel, ny=ny, nz=cz, half=2 * cy, halo=HALO),
-        (f32(planes, rows, cz),), det_cells.reshape(1, dets),
+        (f32(planes, rows, cz), f32(1, cz)), det_cells.reshape(1, dets), beta_prev, smem=(1,),
         cost=pl.CostEstimate(flops=2 * planes * rows * cz * dets, bytes_accessed=planes * rows * cz * 4, transcendentals=0),
     )
 
     def across_y(value):
         return lax.ppermute(value, "gy", [(i, (i + 2) % 4) for i in range(4)])
 
-    edges = (f32(2, planes, HALO, cz),)
     (half_vector,) = run(unpack_kernel, (f32(2, *block),), v_kappa, v_absorb, *slabs, after=(count,))
     half_came = swap_x(half_vector)
     mine, fields = run(
@@ -653,22 +690,24 @@
         background, labels, came, after=(half_vector,), hbm=(0, 1), scratch=(raw_labels,), copies=3,
     )
     got = swap_core(fields)
-    (vector,) = run(vector_kernel, (f32(2, planes, cy, cz),), half_vector, half_came)
-    (sent,) = run(photon_edge_kernel, edges, mine, fields, got, after=(vector,))
-    halo = across_y(sent)
+    (vector,) = run(vector_kernel, (f32(2, planes, cy, cz),), half_vector, half_came, after=(mine,))
+    edge = (f32(2, *edge_shape(planes, cz)),)
+    (sent,) = run(photon_edge_kernel, edge, mine, fields, got, after=(vector,))
+    photon_edge = across_y(sent)
     vector_got = swap_core(vector)
-    (vector_sent,) = run(vector_edge_kernel, edges, vector, vector_got)
+    (vector_sent,) = run(vector_edge_kernel, edge, vector, vector_got, after=(sent,))
     frame, wide = (planes, rows, cz), (planes + 2, rows, cz)
     float_frame, float_wide = float_block(*frame), float_block(*wide)
-    phi, diag, fx, fy, fz, sums = run(
+    diag, fx, fy, fz, sums = run(
         stencil_kernel,
-        (f32(*wide), f32(*frame), f32(planes + 1, rows, cz), f32(*frame), f32(*frame), f32(2, 8, cz)),
-        kappa_table, absorb_table, mine, fields, got, halo, count, after=(vector_sent,),
+        (f32(*frame), f32(planes + 1, rows, cz), f32(*frame), f32(*frame), f32(2, 8, cz)),
+        kappa_table, absorb_table, mine, fields, got, photon_edge, count, after=(vector_sent,), cost=long,
         smem=(0, 1), scratch=(float_frame, float_wide),
     )
-    change, sent = run(
-        first_kernel, (f32(*frame), f32(planes + 4, HALO, cz)),
-        phi, diag, fx, fy, fz, count, sums, vector, vector_got, across_y(vector_sent),
+    phi, change, sent = run(
+        first_kernel, (f32(*wide), f32(*frame), f32(4, GROUP * REACH + 8, cz)),
+        diag, fx, fy, fz, count, sums, mine, got, vector, vector_got,
+        photon_edge, across_y(vector_sent),
         scratch=(float_wide, float_frame, float_frame, float_wide, float_wide),
     )
     heard = across_y(sent)
@@ -687,13 +726,13 @@
     )
     far, near = swap_x(far), swap_x(near)
     pieces = run(functools.partial(add_kernel, first=half), [piece] * (n - half), kept, far)
-    parts = [along_z(value, half + i) for i, value in enumerate(pieces)]
+    (distant,) = run(sum_kernel, (piece,), *(along_z(value, half + i) for i, value in enumerate(pieces)), cost=long)
     pieces = run(functools.partial(add_kernel, first=0), [piece] * half, kept, near)
-    parts = [pieces[0]] + parts + [along_z(pieces[k], k) for k in range(1, half)]
+    parts = [pieces[0], distant] + [along_z(pieces[k], k) for k in range(1, half)]
     w_k, w_a, tile = run(
-        functools.partial(project_kernel, n=n),
+        functools.partial(project_kernel, parts_n=len(parts), n=n),
         (f32(*v_kappa.shape), f32(*v_kappa.shape), f32(8, 128)),
-        beta_prev.reshape(1, 1), *parts, v_kappa, v_absorb, q_kappa, q_absorb,
+        beta_row, *parts, v_kappa, v_absorb, q_kappa, q_absorb,
     )
     everyone = ("src", "gx", "gy")
     tiles = lax.all_to_all(jnp.broadcast_to(tile, (8 * n, 8, 128)), everyone, 0, 0)
@@ -715,7 +754,7 @@
     def chosen(*args):
         sources, cx, cy, cz = args[3].shape
         n = lax.axis_size("src")
-        fits = sources == 4 and cz == 128 and cx % n == 0 and cz % n == 0 and cy % HALO == 0
+        fits = sources == 4 and cz == 128 and cx % n == 0 and cx % GROUP == 0 and cy % HALO == 0 and n & (n - 1) == 0
         devices = 8 * n
         return (per_device_paired if fits and devices <= 128 else per_device)(*args)
 

time: 75.1 us -> 73.9 us (0.984)
  starting transfers between devices: 20.8 us -> 18.6 us
  blocking collectives: 9.96 us -> 11.6 us
  waiting for transfers between devices: 24.7 us -> 23.8 us
    ppermute x6, starting transfers between devices: 10.3 us -> 8.01 us  [along_z(): return lax.ppermute(value, 'src', [(i, i ^ k) for i in range(n)])]
    all_to_all x1, blocking collectives: 9.96 us -> 11.6 us  [per_device_paired(): lax.all_to_all(jnp.broadcast_to(tile, (8 * n, 8, 128)), everyone, 0, 0)]
    ppermute x4, waiting for transfers between devices: 9.77 us -> 10.8 us  [swap_x(): return lax.ppermute(value, 'gx', [(0, 1), (1, 0)])]
    ppermute x3, waiting for transfers between devices: 5.89 us -> 4.96 us  [across_y(): return lax.ppermute(value, 'gy', [(i, (i + 2) % 4) for i in range(4)])]
    ppermute x6, waiting for transfers between devices: 6.88 us -> 5.96 us  [along_z(): return lax.ppermute(value, 'src', [(i, i ^ k) for i in range(n)])]
    pallas_call x15 -> x16, Pallas kernels: 18 us -> 17.9 us  [run(): pl.pallas_call(body if waits else kernel, out_shape=tuple(outs), in_specs...]
  transfers between devices with their start and end apart: 16 -> 16, of which waited for: 10 -> 11; matrix products, arithmetic and copies ran while one was open for 0% -> 0% of each run, Pallas kernels for 8% -> 8%
where the time goes in v8:
time: 73.9 us; the launch traced here: 73.7 us
  waiting for transfers between devices  23.8 us (32%)
  starting transfers between devices  18.6 us (25%)
  Pallas kernels  17.9 us (24%)
  blocking collectives  11.6 us (16%)
  between operations  1.51 us (2%)
    pallas_call x16, Pallas kernels, run(): pl.pallas_call(body if waits else kernel, out_shape=tuple(outs), in_specs...  17.9 us
    all_to_all x1, blocking collectives, per_device_paired(): lax.all_to_all(jnp.broadcast_to(tile, (8 * n, 8, 128)), everyone, 0, 0)  11.6 us
    ppermute x4, waiting for transfers between devices, swap_x(): return lax.ppermute(value, 'gx', [(0, 1), (1, 0)])  10.8 us
    ppermute x6, starting transfers between devices, along_z(): return lax.ppermute(value, 'src', [(i, i ^ k) for i in range(n)])  8.01 us
    ppermute x6, waiting for transfers between devices, along_z(): return lax.ppermute(value, 'src', [(i, i ^ k) for i in range(n)])  5.96 us
    ppermute x4, starting transfers between devices, swap_x(): return lax.ppermute(value, 'gx', [(0, 1), (1, 0)])  5.65 us
    ppermute x3, waiting for transfers between devices, across_y(): return lax.ppermute(value, 'gy', [(i, (i + 2) % 4) for i in range(4)])  4.96 us
    ppermute x3, starting transfers between devices, across_y(): return lax.ppermute(value, 'gy', [(i, (i + 2) % 4) for i in range(4)])  4.77 us
  transfers between devices with their start and end apart: 16, of which 11 were waited for; matrix products, arithmetic and copies ran while one was open for 0% of the time, Pallas kernels for 8%

profile of v8, /device:TPU:0, one launch (start us, length us, event | category | flops | bytes accessed | tf_op | source)
XLA Modules:
  0.0 73.7 jit_solution(11052702182325685322)
XLA Ops:
  0.6 1.9 %shard_map.122 = (f32[2,2,32,128]{3,2,1,0:T(8,128)}, f32[3,8,32,128]{3,2,1,0:T(8,128)}) custom-call(f32[4,8,32,128]{3,2,1,0:T(8,128)} %refs_0_.4, s32[8,32,128]{2,1,0:T(8,128)} %refs_1_.4, f32[8,32,32]{2,1,0:T(8,128)} %vk.3, f32[8,32,32]{2,1,0:T(8,128)} %va.3), custom_call_target="tpu_custom_call" | custom-call | tf_op jit(solution)/shard_map/pallas_call | solution.py:629
  2.6 3.0 %collective-permute-start = (f32[3,8,32,128]{3,2,1,0:T(8,128)}, f32[3,8,32,128]{3,2,1,0:T(8,128)S(1)}, u32[]{:S(2)}, u32[]{:S(2)}) collective-permute-start(f32[3,8,32,128]{3,2,1,0:T(8,128)} %get-tuple-element.30), channel_id=1, source_target_pairs={{0,4},{4,0},{1,5},{5,1},{2,6},{6,2},{3,7},{7,3},{8,12},{12,8},{9,1... | collective-permute-start | bytes 1179656 | tf_op jit(solution)/shard_map/ppermute | solution.py:658
  5.6 3.6 %collective-permute-start.3 = (f32[2,2,32,128]{3,2,1,0:T(8,128)}, f32[2,2,32,128]{3,2,1,0:T(8,128)S(1)}, u32[]{:S(2)}, u32[]{:S(2)}) collective-permute-start(f32[2,2,32,128]{3,2,1,0:T(8,128)} %get-tuple-element.31), channel_id=1, source_target_pairs={{0,24},{8,16},{16,8},{24,0},{1,25},{9,17},{17,9},{25,1},{2,26},{10... | collective-permute-start | bytes 196616 | tf_op jit(solution)/shard_map/ppermute | solution.py:664
  9.2 0.8 %collective-permute-start.1 = (f32[2,2,32,128]{3,2,1,0:T(8,128)}, f32[2,2,32,128]{3,2,1,0:T(8,128)S(1)}, u32[]{:S(2)}, u32[]{:S(2)}) collective-permute-start(f32[2,2,32,128]{3,2,1,0:T(8,128)} %get-tuple-element.31), channel_id=1, source_target_pairs={{0,8},{8,0},{16,24},{24,16},{1,9},{9,1},{17,25},{25,17},{2,10},{10... | collective-permute-start | bytes 196616 | tf_op jit(solution)/shard_map/ppermute | solution.py:664
  10.7 2.1 %shard_map.121 = (f32[16,72,128]{2,1,0:T(8,128)S(1)}, f32[1,128]{1,0:T(1,128)S(1)}) custom-call(s32[1,1024]{1,0:T(1,128)S(1)} %bitcast.1, f32[1]{0:T(128)S(6)} %copy.13.beta_prev), custom_call_target="tpu_custom_call" | custom-call | flops 301989888 | bytes 589824 | tf_op jit(solution)/shard_map/pallas_call | solution.py:629
  12.8 2.0 %collective-permute-done.2.refs_3_ = f32[2,2,32,128]{3,2,1,0:T(8,128)S(1)} collective-permute-done((f32[2,2,32,128]{3,2,1,0:T(8,128)}, f32[2,2,32,128]{3,2,1,0:T(8,128)S(1)}, u32[]{:S(2)}, u32[]{:S(2)}) %collective-permute-start.2) | collective-permute-done | bytes 65568 | tf_op jit(solution)/shard_map/ppermute | solution.py:664
  16.5 6.5 %collective-permute-done.5.refs_1_ = f32[2,8,32,128]{3,2,1,0:T(8,128)S(1)} collective-permute-done((f32[2,8,32,128]{3,2,1,0:T(8,128)S(1)}, f32[2,8,32,128]{3,2,1,0:T(8,128)S(1)}, u32[]{:S(2)}, u32[]{:S(2)}) %collective-permute-start.5) | collective-permute-done | bytes 262176 | tf_op jit(solution)/shard_map/ppermute | solution.py:658
  23.2 1.6 %collective-permute-start.6 = (f32[2,4,24,128]{3,2,1,0:T(8,128)S(1)}, f32[2,4,24,128]{3,2,1,0:T(8,128)S(1)}, u32[]{:S(2)}, u32[]{:S(2)}) collective-permute-start(f32[2,4,24,128]{3,2,1,0:T(8,128)S(1)} %shard_map.126.refs_2_), channel_id=1, source_target_pairs={{0,2},{1,3},{2,0},{3,1},{4,6},{5,7},{6,4},{7,5},{8,10},{9,11},{10,... | collective-permute-start | bytes 294920 | tf_op jit(solution)/shard_map/ppermute | solution.py:684
  25.1 1.6 %collective-permute-start.8 = (f32[2,4,24,128]{3,2,1,0:T(8,128)S(1)}, f32[2,4,24,128]{3,2,1,0:T(8,128)S(1)}, u32[]{:S(2)}, u32[]{:S(2)}) collective-permute-start(f32[2,4,24,128]{3,2,1,0:T(8,128)S(1)} %shard_map.127.refs_7_), channel_id=1, source_target_pairs={{0,2},{1,3},{2,0},{3,1},{4,6},{5,7},{6,4},{7,5},{8,10},{9,11},{10,... | collective-permute-start | bytes 294920 | tf_op jit(solution)/shard_map/ppermute | solution.py:684
  26.7 2.2 %collective-permute-done.6.refs_5_.photon_edge = f32[2,4,24,128]{3,2,1,0:T(8,128)S(1)} collective-permute-done((f32[2,4,24,128]{3,2,1,0:T(8,128)S(1)}, f32[2,4,24,128]{3,2,1,0:T(8,128)S(1)}, u32[]{:S(2)}, u32[]{:S(2)}) %collective-permute-start.6) | collective-permute-done | bytes 98336 | tf_op jit(solution)/shard_map/ppermute | solution.py:684
  28.9 2.3 %shard_map.128 = (f32[16,72,128]{2,1,0:T(8,128)S(1)}, f32[17,72,128]{2,1,0:T(8,128)S(1)}, f32[16,72,128]{2,1,0:T(8,128)S(1)}, f32[16,72,128]{2,1,0:T(8,128)S(1)}, f32[2,8,128]{2,1,0:T(8,128)S(1)}) custom-call(f32[16]{0:T(128)S(1)} %copy-done.7, f32[16]{0:T(128)S(1)} %copy-done.8, f32[16,32,128]{2,1,0:T(8,128)S(1)} %get-tuple-element.33.refs_2_.refs_0_.mine, ...), custom_call_target="tpu_custom_call" | custom-call | flops 1000000000 | bytes 67108864 | tf_op jit(solution)/shard_map/pallas_call | solution.py:629
  31.2 4.1 %shard_map.129 = (f32[18,72,128]{2,1,0:T(8,128)S(1)}, f32[16,72,128]{2,1,0:T(8,128)S(1)}, f32[4,32,128]{2,1,0:T(8,128)S(1)}) custom-call(f32[16,72,128]{2,1,0:T(8,128)S(1)} %get-tuple-element.35.diag, f32[17,72,128]{2,1,0:T(8,128)S(1)} %get-tuple-element.36.fx, f32[16,72,128]{2,1,0:T(8,128)S(1)} %get-tuple-element.37.fy, ...), custom_call_target="tpu_custom_call" | custom-call | tf_op jit(solution)/shard_map/pallas_call | solution.py:629
  35.4 1.6 %collective-permute-start.9 = (f32[4,32,128]{2,1,0:T(8,128)S(1)}, f32[4,32,128]{2,1,0:T(8,128)S(1)}, u32[]{:S(2)}, u32[]{:S(2)}) collective-permute-start(f32[4,32,128]{2,1,0:T(8,128)S(1)} %get-tuple-element.42.sent), channel_id=1, source_target_pairs={{0,2},{1,3},{2,0},{3,1},{4,6},{5,7},{6,4},{7,5},{8,10},{9,11},{10,... | collective-permute-start | bytes 196616 | tf_op jit(solution)/shard_map/ppermute | solution.py:684
  37.0 2.7 %collective-permute-done.9.came = f32[4,32,128]{2,1,0:T(8,128)S(1)} collective-permute-done((f32[4,32,128]{2,1,0:T(8,128)S(1)}, f32[4,32,128]{2,1,0:T(8,128)S(1)}, u32[]{:S(2)}, u32[]{:S(2)}) %collective-permute-start.9) | collective-permute-done | bytes 65568 | tf_op jit(solution)/shard_map/ppermute | solution.py:684
  39.7 4.1 %shard_map.130 = (f32[2,16,32,128]{3,2,1,0:T(8,128)S(1)}, f32[2,16,32,128]{3,2,1,0:T(8,128)S(1)}) custom-call(f32[18,72,128]{2,1,0:T(8,128)S(1)} %get-tuple-element.40.phi, f32[16,72,128]{2,1,0:T(8,128)S(1)} %get-tuple-element.41.change, f32[16,72,128]{2,1,0:T(8,128)S(1)} %get-tuple-element.35.diag, f32[17,72,128]{2,1,0:T(8,128)S(1)} %get-tuple-element.36.fx, ...), custom_call_target="tpu_custom_call" | custom-call | tf_op jit(solution)/shard_map/pallas_call | solution.py:629
  43.9 1.9 %collective-permute-done.10.came = f32[2,16,32,128]{3,2,1,0:T(8,128)S(1)} collective-permute-done((f32[2,16,32,128]{3,2,1,0:T(8,128)S(1)}, f32[2,16,32,128]{3,2,1,0:T(8,128)S(1)}, u32[]{:S(2)}, u32[]{:S(2)}) %collective-permute-start.10) | collective-permute-done | bytes 524320 | tf_op jit(solution)/shard_map/ppermute | solution.py:661
  47.0 1.5 %collective-permute-start.11 = (f32[2,2,2,32,128]{4,3,2,1,0:T(8,128)S(1)}, f32[2,2,2,32,128]{4,3,2,1,0:T(8,128)S(1)}, u32[]{:S(2)}, u32[]{:S(2)}) collective-permute-start(f32[2,2,2,32,128]{4,3,2,1,0:T(8,128)S(1)} %get-tuple-element.46), channel_id=1, source_target_pairs={{0,4},{4,0},{1,5},{5,1},{2,6},{6,2},{3,7},{7,3},{8,12},{12,8},{9,1... | collective-permute-start | bytes 393224 | tf_op jit(solution)/shard_map/ppermute | solution.py:658
  48.5 4.3 %collective-permute-done.12.came = f32[2,2,2,32,128]{4,3,2,1,0:T(8,128)S(1)} collective-permute-done((f32[2,2,2,32,128]{4,3,2,1,0:T(8,128)S(1)}, f32[2,2,2,32,128]{4,3,2,1,0:T(8,128)S(1)}, u32[]{:S(2)}, u32[]{:S(2)}) %collective-permute-start.12) | collective-permute-done | bytes 131104 | tf_op jit(solution)/shard_map/ppermute | solution.py:658
  53.6 1.9 %collective-permute-start.14 = (f32[2,2,32,128]{3,2,1,0:T(8,128)S(1)}, f32[2,2,32,128]{3,2,1,0:T(8,128)S(1)}, u32[]{:S(2)}, u32[]{:S(2)}) collective-permute-start(f32[2,2,32,128]{3,2,1,0:T(8,128)S(1)} %get-tuple-element.50), channel_id=1, source_target_pairs={{0,24},{8,16},{16,8},{24,0},{1,25},{9,17},{17,9},{25,1},{2,26},{10... | collective-permute-start | bytes 196616 | tf_op jit(solution)/shard_map/ppermute | solution.py:664
  55.6 1.0 %collective-permute-start.15 = (f32[2,2,32,128]{3,2,1,0:T(8,128)S(1)}, f32[2,2,32,128]{3,2,1,0:T(8,128)S(1)}, u32[]{:S(2)}, u32[]{:S(2)}) collective-permute-start(f32[2,2,32,128]{3,2,1,0:T(8,128)S(1)} %get-tuple-element.51), channel_id=1, source_target_pairs={{0,8},{8,0},{16,24},{24,16},{1,9},{9,1},{17,25},{25,17},{2,10},{10... | collective-permute-start | bytes 196616 | tf_op jit(solution)/shard_map/ppermute | solution.py:664
  56.5 2.3 %collective-permute-done.13.refs_0_ = f32[2,2,32,128]{3,2,1,0:T(8,128)S(1)} collective-permute-done((f32[2,2,32,128]{3,2,1,0:T(8,128)S(1)}, f32[2,2,32,128]{3,2,1,0:T(8,128)S(1)}, u32[]{:S(2)}, u32[]{:S(2)}) %collective-permute-start.13) | collective-permute-done | bytes 65568 | tf_op jit(solution)/shard_map/ppermute | solution.py:664
  58.8 1.0 %collective-permute-done.14.refs_1_ = f32[2,2,32,128]{3,2,1,0:T(8,128)S(1)} collective-permute-done((f32[2,2,32,128]{3,2,1,0:T(8,128)S(1)}, f32[2,2,32,128]{3,2,1,0:T(8,128)S(1)}, u32[]{:S(2)}, u32[]{:S(2)}) %collective-permute-start.14) | collective-permute-done | bytes 65568 | tf_op jit(solution)/shard_map/ppermute | solution.py:664
  61.0 11.6 %all_to_all.5.tiles = f32[32,8,128]{2,1,0:T(8,128)S(1)} all-to-all(f32[32,8,128]{2,1,0:T(8,128)S(1)} %broadcast_in_dim.3), channel_id=1, replica_groups=mesh['src'=4,'gx'=2,'gy'=4] {'src','gx','gy'}, dimensions={0} | all-to-all | bytes 262144 | tf_op jit(solution)/shard_map/all_to_all | solution.py:738
  72.7 1.0 %shard_map.136 = (f32[8,32,32]{2,1,0:T(8,128)}, f32[8,32,32]{2,1,0:T(8,128)}, f32[2]{0:T(128)}) custom-call(f32[32,8,128]{2,1,0:T(8,128)S(1)} %all_to_all.5.tiles, f32[8,32,32]{2,1,0:T(8,128)S(1)} %get-tuple-element.53.w_k, f32[8,32,32]{2,1,0:T(8,128)S(1)} %get-tuple-element.54.w_a, f32[8,32,32]{2,1,0:T(8,128)S(1)} %copy-done, f32[8,32,32]{2,1,0:T(8,128)S(1)} %copy-done.1), custom_call_target="tpu_custom_call" | custom-call | tf_op jit(solution)/shard_map/pallas_call | solution.py:629
  (44 shorter events, 5.4 us)
Async XLA Ops:
  2.6 8.1 %copy-start.6 = (s32[1024]{0:T(1024)S(1)}, s32[1024]{0:T(1024)}, u32[]{:S(2)}) copy-start(s32[1024]{0:T(1024)} %param.14) | copy-start | bytes 12292
  2.6 13.3 %collective-permute-start = (f32[3,8,32,128]{3,2,1,0:T(8,128)}, f32[3,8,32,128]{3,2,1,0:T(8,128)S(1)}, u32[]{:S(2)}, u32[]{:S(2)}) collective-permute-start(f32[3,8,32,128]{3,2,1,0:T(8,128)} %get-tuple-element.30), channel_id=1, source_target_pairs={{0,4},{4,0},{1,5},{5,1},{2,6},{6,2},{3,7},{7,3},{8,12},{12,8},{9,1... | collective-permute-start | bytes 1179656 | tf_op jit(solution)/shard_map/ppermute | solution.py:658
  5.6 7.2 %collective-permute-start.3 = (f32[2,2,32,128]{3,2,1,0:T(8,128)}, f32[2,2,32,128]{3,2,1,0:T(8,128)S(1)}, u32[]{:S(2)}, u32[]{:S(2)}) collective-permute-start(f32[2,2,32,128]{3,2,1,0:T(8,128)} %get-tuple-element.31), channel_id=1, source_target_pairs={{0,24},{8,16},{16,8},{24,0},{1,25},{9,17},{17,9},{25,1},{2,26},{10... | collective-permute-start | bytes 196616 | tf_op jit(solution)/shard_map/ppermute | solution.py:664
  9.2 5.6 %collective-permute-start.2 = (f32[2,2,32,128]{3,2,1,0:T(8,128)}, f32[2,2,32,128]{3,2,1,0:T(8,128)S(1)}, u32[]{:S(2)}, u32[]{:S(2)}) collective-permute-start(f32[2,2,32,128]{3,2,1,0:T(8,128)} %get-tuple-element.31), channel_id=1, source_target_pairs={{0,16},{8,24},{16,0},{24,8},{1,17},{9,25},{17,1},{25,9},{2,18},{10... | collective-permute-start | bytes 196616 | tf_op jit(solution)/shard_map/ppermute | solution.py:664
  9.2 5.6 %collective-permute-start.1 = (f32[2,2,32,128]{3,2,1,0:T(8,128)}, f32[2,2,32,128]{3,2,1,0:T(8,128)S(1)}, u32[]{:S(2)}, u32[]{:S(2)}) collective-permute-start(f32[2,2,32,128]{3,2,1,0:T(8,128)} %get-tuple-element.31), channel_id=1, source_target_pairs={{0,8},{8,0},{16,24},{24,16},{1,9},{9,1},{17,25},{25,17},{2,10},{10... | collective-permute-start | bytes 196616 | tf_op jit(solution)/shard_map/ppermute | solution.py:664
  10.6 4.2 %copy-start = (f32[8,32,32]{2,1,0:T(8,128)S(1)}, f32[8,32,32]{2,1,0:T(8,128)}, u32[]{:S(2)}) copy-start(f32[8,32,32]{2,1,0:T(8,128)} %vk.3) | copy-start | bytes 98308
  10.6 4.2 %copy-start.1 = (f32[8,32,32]{2,1,0:T(8,128)S(1)}, f32[8,32,32]{2,1,0:T(8,128)}, u32[]{:S(2)}) copy-start(f32[8,32,32]{2,1,0:T(8,128)} %va.3) | copy-start | bytes 98308
  14.8 1.1 %copy-start.3 = (s32[8,32,128]{2,1,0:T(8,128)S(1)}, s32[8,32,128]{2,1,0:T(8,128)}, u32[]{:S(2)}) copy-start(s32[8,32,128]{2,1,0:T(8,128)} %refs_1_.4) | copy-start | bytes 393220
  15.3 7.7 %collective-permute-start.5 = (f32[2,8,32,128]{3,2,1,0:T(8,128)S(1)}, f32[2,8,32,128]{3,2,1,0:T(8,128)S(1)}, u32[]{:S(2)}, u32[]{:S(2)}) collective-permute-start(f32[2,8,32,128]{3,2,1,0:T(8,128)S(1)} %shard_map.123.refs_3_.refs_0_), channel_id=1, source_target_pairs={{0,4},{4,0},{1,5},{5,1},{2,6},{6,2},{3,7},{7,3},{8,12},{12,8},{9,1... | collective-permute-start | bytes 786440 | tf_op jit(solution)/shard_map/ppermute | solution.py:658
  16.5 6.7 %collective-permute-start.4 = (f32[2,16,32,128]{3,2,1,0:T(8,128)S(1)}, f32[2,16,32,128]{3,2,1,0:T(8,128)S(1)}, u32[]{:S(2)}, u32[]{:S(2)}) collective-permute-start(f32[2,16,32,128]{3,2,1,0:T(8,128)S(1)} %get-tuple-element.34.refs_1_.refs_3_), channel_id=1, source_target_pairs={{0,1},{1,0},{2,3},{3,2},{4,5},{5,4},{6,7},{7,6},{8,9},{9,8},{10,11... | collective-permute-start | bytes 1572872 | tf_op jit(solution)/shard_map/ppermute | solution.py:661
  23.0 2.0 %collective-permute-start.7 = (f32[2,16,32,128]{3,2,1,0:T(8,128)S(1)}, f32[2,16,32,128]{3,2,1,0:T(8,128)S(1)}, u32[]{:S(2)}, u32[]{:S(2)}) collective-permute-start(f32[2,16,32,128]{3,2,1,0:T(8,128)S(1)} %shard_map.125.refs_3_.refs_0_.vector), channel_id=1, source_target_pairs={{0,1},{1,0},{2,3},{3,2},{4,5},{5,4},{6,7},{7,6},{8,9},{9,8},{10,11... | collective-permute-start | bytes 1572872 | tf_op jit(solution)/shard_map/ppermute | solution.py:661
  23.2 5.7 %copy-start.7 = (f32[16]{0:T(128)S(1)}, f32[16]{0:T(128)}, u32[]{:S(2)}) copy-start(f32[16]{0:T(128)} %refs_0_.5) | copy-start | bytes 196
  23.2 5.7 %copy-start.8 = (f32[16]{0:T(128)S(1)}, f32[16]{0:T(128)}, u32[]{:S(2)}) copy-start(f32[16]{0:T(128)} %refs_1_.5) | copy-start | bytes 196
  23.2 5.7 %collective-permute-start.6 = (f32[2,4,24,128]{3,2,1,0:T(8,128)S(1)}, f32[2,4,24,128]{3,2,1,0:T(8,128)S(1)}, u32[]{:S(2)}, u32[]{:S(2)}) collective-permute-start(f32[2,4,24,128]{3,2,1,0:T(8,128)S(1)} %shard_map.126.refs_2_), channel_id=1, source_target_pairs={{0,2},{1,3},{2,0},{3,1},{4,6},{5,7},{6,4},{7,5},{8,10},{9,11},{10,... | collective-permute-start | bytes 294920 | tf_op jit(solution)/shard_map/ppermute | solution.py:684
  25.1 6.1 %collective-permute-start.8 = (f32[2,4,24,128]{3,2,1,0:T(8,128)S(1)}, f32[2,4,24,128]{3,2,1,0:T(8,128)S(1)}, u32[]{:S(2)}, u32[]{:S(2)}) collective-permute-start(f32[2,4,24,128]{3,2,1,0:T(8,128)S(1)} %shard_map.127.refs_7_), channel_id=1, source_target_pairs={{0,2},{1,3},{2,0},{3,1},{4,6},{5,7},{6,4},{7,5},{8,10},{9,11},{10,... | collective-permute-start | bytes 294920 | tf_op jit(solution)/shard_map/ppermute | solution.py:684
  35.4 4.3 %collective-permute-start.9 = (f32[4,32,128]{2,1,0:T(8,128)S(1)}, f32[4,32,128]{2,1,0:T(8,128)S(1)}, u32[]{:S(2)}, u32[]{:S(2)}) collective-permute-start(f32[4,32,128]{2,1,0:T(8,128)S(1)} %get-tuple-element.42.sent), channel_id=1, source_target_pairs={{0,2},{1,3},{2,0},{3,1},{4,6},{5,7},{6,4},{7,5},{8,10},{9,11},{10,... | collective-permute-start | bytes 196616 | tf_op jit(solution)/shard_map/ppermute | solution.py:684
  43.8 2.0 %collective-permute-start.10 = (f32[2,16,32,128]{3,2,1,0:T(8,128)S(1)}, f32[2,16,32,128]{3,2,1,0:T(8,128)S(1)}, u32[]{:S(2)}, u32[]{:S(2)}) collective-permute-start(f32[2,16,32,128]{3,2,1,0:T(8,128)S(1)} %get-tuple-element.44), channel_id=1, source_target_pairs={{0,1},{1,0},{2,3},{3,2},{4,5},{5,4},{6,7},{7,6},{8,9},{9,8},{10,11... | collective-permute-start | bytes 1572872 | tf_op jit(solution)/shard_map/ppermute | solution.py:661
  46.4 6.4 %collective-permute-start.12 = (f32[2,2,2,32,128]{4,3,2,1,0:T(8,128)S(1)}, f32[2,2,2,32,128]{4,3,2,1,0:T(8,128)S(1)}, u32[]{:S(2)}, u32[]{:S(2)}) collective-permute-start(f32[2,2,2,32,128]{4,3,2,1,0:T(8,128)S(1)} %get-tuple-element.48), channel_id=1, source_target_pairs={{0,4},{4,0},{1,5},{5,1},{2,6},{6,2},{3,7},{7,3},{8,12},{12,8},{9,1... | collective-permute-start | bytes 393224 | tf_op jit(solution)/shard_map/ppermute | solution.py:658
  47.0 8.5 %collective-permute-start.11 = (f32[2,2,2,32,128]{4,3,2,1,0:T(8,128)S(1)}, f32[2,2,2,32,128]{4,3,2,1,0:T(8,128)S(1)}, u32[]{:S(2)}, u32[]{:S(2)}) collective-permute-start(f32[2,2,2,32,128]{4,3,2,1,0:T(8,128)S(1)} %get-tuple-element.46), channel_id=1, source_target_pairs={{0,4},{4,0},{1,5},{5,1},{2,6},{6,2},{3,7},{7,3},{8,12},{12,8},{9,1... | collective-permute-start | bytes 393224 | tf_op jit(solution)/shard_map/ppermute | solution.py:658
  52.9 5.9 %collective-permute-start.13 = (f32[2,2,32,128]{3,2,1,0:T(8,128)S(1)}, f32[2,2,32,128]{3,2,1,0:T(8,128)S(1)}, u32[]{:S(2)}, u32[]{:S(2)}) collective-permute-start(f32[2,2,32,128]{3,2,1,0:T(8,128)S(1)} %get-tuple-element.49), channel_id=1, source_target_pairs={{0,16},{8,24},{16,0},{24,8},{1,17},{9,25},{17,1},{25,9},{2,18},{10... | collective-permute-start | bytes 196616 | tf_op jit(solution)/shard_map/ppermute | solution.py:664
  53.6 6.2 %collective-permute-start.14 = (f32[2,2,32,128]{3,2,1,0:T(8,128)S(1)}, f32[2,2,32,128]{3,2,1,0:T(8,128)S(1)}, u32[]{:S(2)}, u32[]{:S(2)}) collective-permute-start(f32[2,2,32,128]{3,2,1,0:T(8,128)S(1)} %get-tuple-element.50), channel_id=1, source_target_pairs={{0,24},{8,16},{16,8},{24,0},{1,25},{9,17},{17,9},{25,1},{2,26},{10... | collective-permute-start | bytes 196616 | tf_op jit(solution)/shard_map/ppermute | solution.py:664
  55.5 4.9 %copy-start.4 = (f32[8,32,32]{2,1,0:T(8,128)S(1)}, f32[8,32,32]{2,1,0:T(8,128)}, u32[]{:S(2)}) copy-start(f32[8,32,32]{2,1,0:T(8,128)} %refs_6_.1) | copy-start | bytes 98308
  55.5 4.9 %copy-start.5 = (f32[8,32,32]{2,1,0:T(8,128)S(1)}, f32[8,32,32]{2,1,0:T(8,128)}, u32[]{:S(2)}) copy-start(f32[8,32,32]{2,1,0:T(8,128)} %refs_7_.1) | copy-start | bytes 98308
  55.6 4.9 %collective-permute-start.15 = (f32[2,2,32,128]{3,2,1,0:T(8,128)S(1)}, f32[2,2,32,128]{3,2,1,0:T(8,128)S(1)}, u32[]{:S(2)}, u32[]{:S(2)}) collective-permute-start(f32[2,2,32,128]{3,2,1,0:T(8,128)S(1)} %get-tuple-element.51), channel_id=1, source_target_pairs={{0,8},{8,0},{16,24},{24,16},{1,9},{9,1},{17,25},{25,17},{2,10},{10... | collective-permute-start | bytes 196616 | tf_op jit(solution)/shard_map/ppermute | solution.py:664
  (1 other events, 1.0 us)

commit v9 on v8

--- a/solution.py
+++ b/solution.py
@@ -333,17 +333,19 @@
         src, dst = bufs[step % 2], bufs[(step + 1) % 2]
 
         def body(i, carry):
-            u = src[i + 1]
+            u, flow = carry
+            beyond_x = src[i + 2]
             coef_y, coef_z = fy[i], fz[i]
-            left = b[i] - diag[i] * u
-            left = left + fx[i] * src[i] + fx[i + 1] * src[i + 2]
+            next_flow = fx[i + 1] * (beyond_x - u)
+            left = b[i] - diag[i] * u + (next_flow - flow)
             left = left + coef_y * shifted(u, -1, 0) + shifted(coef_y * u, 1, 0)
             left = left + coef_z * shifted(u, -1, 1) + shifted(coef_z * u, 1, 1)
             change = u if step == 0 else u - dst[i + 1]
             dst[i + 1] = u + keep * change + push * left
-            return carry
-
-        lax.fori_loop(0, planes, body, 0, unroll=unroll)
+            return beyond_x, next_flow
+
+        first = src[1]
+        lax.fori_loop(0, planes, body, (first, fx[0] * first), unroll=unroll)
     return bufs[len(pairs) % 2]
 
 
@@ -404,13 +406,12 @@
 
     def set_up(i, carry):
         k = kap[i + 1]
-        along_x = 0.5 * (k + kap[i + 2])
         along_y, along_z = 0.5 * (k + beyond(k, 1, 0)), 0.5 * (k + beyond(k, 1, 1))
-        fx[i + 1] = along_x
+        fx[i + 1] = 0.5 * (k + kap[i + 2])
         fy[i] = jnp.where(index_along(k.shape, 0) == rows - 1, 0.0, along_y)
         fz[i] = jnp.where(lane == lanes - 1, 0.0, along_z)
         back_y, back_z = 0.5 * (k + beyond(k, -1, 0)), 0.5 * (k + beyond(k, -1, 1))
-        diag[i] = diag[i] + fx[i] + along_x + along_y + back_y + along_z + back_z
+        diag[i] = diag[i] + along_y + back_y + along_z + back_z
         total, square = carry
         for p, at in ((mine[i], c), (got[0, i], 1 - c)):
             part = count[i, pl.ds(base + cy * at, cy), :] * p
@@ -525,28 +526,34 @@
     lax.fori_loop(0, planes, product, 0, unroll=4)
 
 
-def core_kernel(own, came, kept, far, near):
-    s, x, _, _ = places(2)
-    n, _, groups, cy, lanes = kept.shape
+def packed_slabs(own, came, half, choices, outs):
+    s, _, _, _ = places(2)
+    _, planes, cy, lanes = own.shape
+    n = planes // 2 // outs.shape[2]
     slab = lanes // n
     lane = index_along((cy, lanes), 1) // slab
-    for h in range(2):
-        for f in range(2):
-            for q in range(groups):
-                at = n * (groups * (x if h == 0 else 1 - x) + q)
-                planes = [own[f, at + j] + came[f, at + j] for j in range(n)]
-                for k in range(n):
-                    to = s ^ k
-                    piece = jnp.zeros((cy, lanes), jnp.float32)
-                    for j in range(n):
-                        moved = pltpu.roll(planes[j], ((j - to + n) % n) * slab, 1)
-                        piece = jnp.where(lane == j, moved, piece)
-                    if h == 0:
-                        kept[k, f, q] = piece
-                    elif k >= n // 2:
-                        far[k - n // 2, f, q] = piece
-                    else:
-                        near[k, f, q] = piece
+    for f in range(2):
+        for q in range(outs.shape[2]):
+            at = planes // 2 * half + n * q
+            parts = [own[f, at + j] + came[f, at + j] for j in range(n)]
+            for i, k in enumerate(choices):
+                to = s ^ k
+                piece = jnp.zeros((cy, lanes), jnp.float32)
+                for j in range(n):
+                    moved = pltpu.roll(parts[j], ((j - to + n) % n) * slab, 1)
+                    piece = jnp.where(lane == j, moved, piece)
+                outs[i, f, q] = piece
+
+
+def far_kernel(own, came, far):
+    _, x, _, _ = places(2)
+    packed_slabs(own, came, 1 - x, range(far.shape[0], 2 * far.shape[0]), far)
+
+
+def near_kernel(own, came, kept, near):
+    _, x, _, _ = places(2)
+    packed_slabs(own, came, 1 - x, range(near.shape[0]), near)
+    packed_slabs(own, came, x, range(kept.shape[0]), kept)
 
 
 def add_kernel(kept, came, *outs, first):
@@ -719,10 +726,10 @@
     )
     piece = f32(2, groups, cy, cz)
     half = n // 2
-    kept, far, near = run(
-        core_kernel,
-        (f32(n, *piece.shape), f32(n - half, *piece.shape), f32(half, *piece.shape)),
-        own, swap_core(message),
+    got = swap_core(message)
+    (far,) = run(far_kernel, (f32(half, *piece.shape),), own, got)
+    kept, near = run(
+        near_kernel, (f32(n, *piece.shape), f32(half, *piece.shape)), own, got, after=(far,)
     )
     far, near = swap_x(far), swap_x(near)
     pieces = run(functools.partial(add_kernel, first=half), [piece] * (n - half), kept, far)
@@ -754,7 +761,7 @@
     def chosen(*args):
         sources, cx, cy, cz = args[3].shape
         n = lax.axis_size("src")
-        fits = sources == 4 and cz == 128 and cx % n == 0 and cx % GROUP == 0 and cy % HALO == 0 and n & (n - 1) == 0
+        fits = sources == 4 and cz == 128 and cx % n == 0 and cx % GROUP == 0 and cy % HALO == 0 and n > 1 and n & (n - 1) == 0
         devices = 8 * n
         return (per_device_paired if fits and devices <= 128 else per_device)(*args)
 

time: 73.9 us -> 73.8 us (level)
    pallas_call x16 -> x17, Pallas kernels: 17.9 us -> 18.4 us  [run(): pl.pallas_call(body if waits else kernel, out_shape=tuple(outs), in_specs...]
where the time goes in v9:
time: 73.8 us; the launch traced here: 73.6 us
  waiting for transfers between devices  23.3 us (32%)
  starting transfers between devices  18.7 us (25%)
  Pallas kernels  18.4 us (25%)
  blocking collectives  11.6 us (16%)
  between operations  1.52 us (2%)
    pallas_call x17, Pallas kernels, run(): pl.pallas_call(body if waits else kernel, out_shape=tuple(outs), in_specs...  18.4 us
    all_to_all x1, blocking collectives, per_device_paired(): lax.all_to_all(jnp.broadcast_to(tile, (8 * n, 8, 128)), everyone, 0, 0)  11.6 us
    ppermute x4, waiting for transfers between devices, swap_x(): return lax.ppermute(value, 'gx', [(0, 1), (1, 0)])  10.2 us
    ppermute x6, starting transfers between devices, along_z(): return lax.ppermute(value, 'src', [(i, i ^ k) for i in range(n)])  8.01 us
    ppermute x6, waiting for transfers between devices, along_z(): return lax.ppermute(value, 'src', [(i, i ^ k) for i in range(n)])  6 us
    ppermute x4, starting transfers between devices, swap_x(): return lax.ppermute(value, 'gx', [(0, 1), (1, 0)])  5.68 us
    ppermute x3, waiting for transfers between devices, across_y(): return lax.ppermute(value, 'gy', [(i, (i + 2) % 4) for i in range(4)])  4.98 us
    ppermute x3, starting transfers between devices, across_y(): return lax.ppermute(value, 'gy', [(i, (i + 2) % 4) for i in range(4)])  4.76 us
  transfers between devices with their start and end apart: 16, of which 11 were waited for; matrix products, arithmetic and copies ran while one was open for 0% of the time, Pallas kernels for 8%

profile of v9, /device:TPU:0, one launch (start us, length us, event | category | flops | bytes accessed | tf_op | source)
XLA Modules:
  0.0 73.6 jit_solution(288920358755976627)
XLA Ops:
  0.6 1.9 %shard_map.122 = (f32[2,2,32,128]{3,2,1,0:T(8,128)}, f32[3,8,32,128]{3,2,1,0:T(8,128)}) custom-call(f32[4,8,32,128]{3,2,1,0:T(8,128)} %refs_0_.4, s32[8,32,128]{2,1,0:T(8,128)} %refs_1_.4, f32[8,32,32]{2,1,0:T(8,128)} %vk.3, f32[8,32,32]{2,1,0:T(8,128)} %va.3), custom_call_target="tpu_custom_call" | custom-call | tf_op jit(solution)/shard_map/pallas_call | solution.py:636
  2.6 3.0 %collective-permute-start = (f32[3,8,32,128]{3,2,1,0:T(8,128)}, f32[3,8,32,128]{3,2,1,0:T(8,128)S(1)}, u32[]{:S(2)}, u32[]{:S(2)}) collective-permute-start(f32[3,8,32,128]{3,2,1,0:T(8,128)} %get-tuple-element.29), channel_id=1, source_target_pairs={{0,4},{4,0},{1,5},{5,1},{2,6},{6,2},{3,7},{7,3},{8,12},{12,8},{9,1... | collective-permute-start | bytes 1179656 | tf_op jit(solution)/shard_map/ppermute | solution.py:665
  5.6 3.6 %collective-permute-start.3 = (f32[2,2,32,128]{3,2,1,0:T(8,128)}, f32[2,2,32,128]{3,2,1,0:T(8,128)S(1)}, u32[]{:S(2)}, u32[]{:S(2)}) collective-permute-start(f32[2,2,32,128]{3,2,1,0:T(8,128)} %get-tuple-element.30), channel_id=1, source_target_pairs={{0,24},{8,16},{16,8},{24,0},{1,25},{9,17},{17,9},{25,1},{2,26},{10... | collective-permute-start | bytes 196616 | tf_op jit(solution)/shard_map/ppermute | solution.py:671
  9.2 0.8 %collective-permute-start.1 = (f32[2,2,32,128]{3,2,1,0:T(8,128)}, f32[2,2,32,128]{3,2,1,0:T(8,128)S(1)}, u32[]{:S(2)}, u32[]{:S(2)}) collective-permute-start(f32[2,2,32,128]{3,2,1,0:T(8,128)} %get-tuple-element.30), channel_id=1, source_target_pairs={{0,8},{8,0},{16,24},{24,16},{1,9},{9,1},{17,25},{25,17},{2,10},{10... | collective-permute-start | bytes 196616 | tf_op jit(solution)/shard_map/ppermute | solution.py:671
  10.7 2.1 %shard_map.121 = (f32[16,72,128]{2,1,0:T(8,128)S(1)}, f32[1,128]{1,0:T(1,128)S(1)}) custom-call(s32[1,1024]{1,0:T(1,128)S(1)} %bitcast.1, f32[1]{0:T(128)S(6)} %copy.13.beta_prev), custom_call_target="tpu_custom_call" | custom-call | flops 301989888 | bytes 589824 | tf_op jit(solution)/shard_map/pallas_call | solution.py:636
  12.8 2.0 %collective-permute-done.2.refs_3_ = f32[2,2,32,128]{3,2,1,0:T(8,128)S(1)} collective-permute-done((f32[2,2,32,128]{3,2,1,0:T(8,128)}, f32[2,2,32,128]{3,2,1,0:T(8,128)S(1)}, u32[]{:S(2)}, u32[]{:S(2)}) %collective-permute-start.2) | collective-permute-done | bytes 65568 | tf_op jit(solution)/shard_map/ppermute | solution.py:671
  16.5 6.5 %collective-permute-done.5.refs_1_ = f32[2,8,32,128]{3,2,1,0:T(8,128)S(1)} collective-permute-done((f32[2,8,32,128]{3,2,1,0:T(8,128)S(1)}, f32[2,8,32,128]{3,2,1,0:T(8,128)S(1)}, u32[]{:S(2)}, u32[]{:S(2)}) %collective-permute-start.5) | collective-permute-done | bytes 262176 | tf_op jit(solution)/shard_map/ppermute | solution.py:665
  23.2 1.6 %collective-permute-start.6 = (f32[2,4,24,128]{3,2,1,0:T(8,128)S(1)}, f32[2,4,24,128]{3,2,1,0:T(8,128)S(1)}, u32[]{:S(2)}, u32[]{:S(2)}) collective-permute-start(f32[2,4,24,128]{3,2,1,0:T(8,128)S(1)} %shard_map.126.refs_2_), channel_id=1, source_target_pairs={{0,2},{1,3},{2,0},{3,1},{4,6},{5,7},{6,4},{7,5},{8,10},{9,11},{10,... | collective-permute-start | bytes 294920 | tf_op jit(solution)/shard_map/ppermute | solution.py:691
  25.1 1.6 %collective-permute-start.8 = (f32[2,4,24,128]{3,2,1,0:T(8,128)S(1)}, f32[2,4,24,128]{3,2,1,0:T(8,128)S(1)}, u32[]{:S(2)}, u32[]{:S(2)}) collective-permute-start(f32[2,4,24,128]{3,2,1,0:T(8,128)S(1)} %shard_map.127.refs_7_), channel_id=1, source_target_pairs={{0,2},{1,3},{2,0},{3,1},{4,6},{5,7},{6,4},{7,5},{8,10},{9,11},{10,... | collective-permute-start | bytes 294920 | tf_op jit(solution)/shard_map/ppermute | solution.py:691
  26.7 2.2 %collective-permute-done.6.refs_5_.photon_edge = f32[2,4,24,128]{3,2,1,0:T(8,128)S(1)} collective-permute-done((f32[2,4,24,128]{3,2,1,0:T(8,128)S(1)}, f32[2,4,24,128]{3,2,1,0:T(8,128)S(1)}, u32[]{:S(2)}, u32[]{:S(2)}) %collective-permute-start.6) | collective-permute-done | bytes 98336 | tf_op jit(solution)/shard_map/ppermute | solution.py:691
  28.9 2.3 %shard_map.128 = (f32[16,72,128]{2,1,0:T(8,128)S(1)}, f32[17,72,128]{2,1,0:T(8,128)S(1)}, f32[16,72,128]{2,1,0:T(8,128)S(1)}, f32[16,72,128]{2,1,0:T(8,128)S(1)}, f32[2,8,128]{2,1,0:T(8,128)S(1)}) custom-call(f32[16]{0:T(128)S(1)} %copy-done.7, f32[16]{0:T(128)S(1)} %copy-done.8, f32[16,32,128]{2,1,0:T(8,128)S(1)} %get-tuple-element.32.refs_2_.refs_0_.mine, ...), custom_call_target="tpu_custom_call" | custom-call | flops 1000000000 | bytes 67108864 | tf_op jit(solution)/shard_map/pallas_call | solution.py:636
  31.2 4.3 %shard_map.129 = (f32[18,72,128]{2,1,0:T(8,128)S(1)}, f32[16,72,128]{2,1,0:T(8,128)S(1)}, f32[4,32,128]{2,1,0:T(8,128)S(1)}) custom-call(f32[16,72,128]{2,1,0:T(8,128)S(1)} %get-tuple-element.34.diag, f32[17,72,128]{2,1,0:T(8,128)S(1)} %get-tuple-element.35.fx, f32[16,72,128]{2,1,0:T(8,128)S(1)} %get-tuple-element.36.fy, ...), custom_call_target="tpu_custom_call" | custom-call | tf_op jit(solution)/shard_map/pallas_call | solution.py:636
  35.6 1.6 %collective-permute-start.9 = (f32[4,32,128]{2,1,0:T(8,128)S(1)}, f32[4,32,128]{2,1,0:T(8,128)S(1)}, u32[]{:S(2)}, u32[]{:S(2)}) collective-permute-start(f32[4,32,128]{2,1,0:T(8,128)S(1)} %get-tuple-element.41.sent), channel_id=1, source_target_pairs={{0,2},{1,3},{2,0},{3,1},{4,6},{5,7},{6,4},{7,5},{8,10},{9,11},{10,... | collective-permute-start | bytes 196616 | tf_op jit(solution)/shard_map/ppermute | solution.py:691
  37.2 2.7 %collective-permute-done.9.came = f32[4,32,128]{2,1,0:T(8,128)S(1)} collective-permute-done((f32[4,32,128]{2,1,0:T(8,128)S(1)}, f32[4,32,128]{2,1,0:T(8,128)S(1)}, u32[]{:S(2)}, u32[]{:S(2)}) %collective-permute-start.9) | collective-permute-done | bytes 65568 | tf_op jit(solution)/shard_map/ppermute | solution.py:691
  39.9 4.3 %shard_map.130 = (f32[2,16,32,128]{3,2,1,0:T(8,128)S(1)}, f32[2,16,32,128]{3,2,1,0:T(8,128)S(1)}) custom-call(f32[18,72,128]{2,1,0:T(8,128)S(1)} %get-tuple-element.39.phi, f32[16,72,128]{2,1,0:T(8,128)S(1)} %get-tuple-element.40.change, f32[16,72,128]{2,1,0:T(8,128)S(1)} %get-tuple-element.34.diag, f32[17,72,128]{2,1,0:T(8,128)S(1)} %get-tuple-element.35.fx, ...), custom_call_target="tpu_custom_call" | custom-call | tf_op jit(solution)/shard_map/pallas_call | solution.py:636
  44.3 1.9 %collective-permute-done.10.came.refs_1_ = f32[2,16,32,128]{3,2,1,0:T(8,128)S(1)} collective-permute-done((f32[2,16,32,128]{3,2,1,0:T(8,128)S(1)}, f32[2,16,32,128]{3,2,1,0:T(8,128)S(1)}, u32[]{:S(2)}, u32[]{:S(2)}) %collective-permute-start.10) | collective-permute-done | bytes 524320 | tf_op jit(solution)/shard_map/ppermute | solution.py:668
  47.5 1.6 %collective-permute-start.11 = (f32[2,2,2,32,128]{4,3,2,1,0:T(8,128)S(1)}, f32[2,2,2,32,128]{4,3,2,1,0:T(8,128)S(1)}, u32[]{:S(2)}, u32[]{:S(2)}) collective-permute-start(f32[2,2,2,32,128]{4,3,2,1,0:T(8,128)S(1)} %get-tuple-element.45), channel_id=1, source_target_pairs={{0,4},{4,0},{1,5},{5,1},{2,6},{6,2},{3,7},{7,3},{8,12},{12,8},{9,1... | collective-permute-start | bytes 393224 | tf_op jit(solution)/shard_map/ppermute | solution.py:665
  49.0 3.8 %collective-permute-done.12.came = f32[2,2,2,32,128]{4,3,2,1,0:T(8,128)S(1)} collective-permute-done((f32[2,2,2,32,128]{4,3,2,1,0:T(8,128)S(1)}, f32[2,2,2,32,128]{4,3,2,1,0:T(8,128)S(1)}, u32[]{:S(2)}, u32[]{:S(2)}) %collective-permute-start.12) | collective-permute-done | bytes 131104 | tf_op jit(solution)/shard_map/ppermute | solution.py:665
  53.6 1.9 %collective-permute-start.14 = (f32[2,2,32,128]{3,2,1,0:T(8,128)S(1)}, f32[2,2,32,128]{3,2,1,0:T(8,128)S(1)}, u32[]{:S(2)}, u32[]{:S(2)}) collective-permute-start(f32[2,2,32,128]{3,2,1,0:T(8,128)S(1)} %get-tuple-element.48), channel_id=1, source_target_pairs={{0,24},{8,16},{16,8},{24,0},{1,25},{9,17},{17,9},{25,1},{2,26},{10... | collective-permute-start | bytes 196616 | tf_op jit(solution)/shard_map/ppermute | solution.py:671
  55.5 0.9 %collective-permute-start.15 = (f32[2,2,32,128]{3,2,1,0:T(8,128)S(1)}, f32[2,2,32,128]{3,2,1,0:T(8,128)S(1)}, u32[]{:S(2)}, u32[]{:S(2)}) collective-permute-start(f32[2,2,32,128]{3,2,1,0:T(8,128)S(1)} %get-tuple-element.49), channel_id=1, source_target_pairs={{0,8},{8,0},{16,24},{24,16},{1,9},{9,1},{17,25},{25,17},{2,10},{10... | collective-permute-start | bytes 196616 | tf_op jit(solution)/shard_map/ppermute | solution.py:671
  56.5 2.3 %collective-permute-done.13.refs_0_ = f32[2,2,32,128]{3,2,1,0:T(8,128)S(1)} collective-permute-done((f32[2,2,32,128]{3,2,1,0:T(8,128)S(1)}, f32[2,2,32,128]{3,2,1,0:T(8,128)S(1)}, u32[]{:S(2)}, u32[]{:S(2)}) %collective-permute-start.13) | collective-permute-done | bytes 65568 | tf_op jit(solution)/shard_map/ppermute | solution.py:671
  58.8 1.0 %collective-permute-done.14.refs_1_ = f32[2,2,32,128]{3,2,1,0:T(8,128)S(1)} collective-permute-done((f32[2,2,32,128]{3,2,1,0:T(8,128)S(1)}, f32[2,2,32,128]{3,2,1,0:T(8,128)S(1)}, u32[]{:S(2)}, u32[]{:S(2)}) %collective-permute-start.14) | collective-permute-done | bytes 65568 | tf_op jit(solution)/shard_map/ppermute | solution.py:671
  61.0 11.6 %all_to_all.5.tiles = f32[32,8,128]{2,1,0:T(8,128)S(1)} all-to-all(f32[32,8,128]{2,1,0:T(8,128)S(1)} %broadcast_in_dim.3), channel_id=1, replica_groups=mesh['src'=4,'gx'=2,'gy'=4] {'src','gx','gy'}, dimensions={0} | all-to-all | bytes 262144 | tf_op jit(solution)/shard_map/all_to_all | solution.py:745
  72.6 1.0 %shard_map.137 = (f32[8,32,32]{2,1,0:T(8,128)}, f32[8,32,32]{2,1,0:T(8,128)}, f32[2]{0:T(128)}) custom-call(f32[32,8,128]{2,1,0:T(8,128)S(1)} %all_to_all.5.tiles, f32[8,32,32]{2,1,0:T(8,128)S(1)} %get-tuple-element.51.w_k, f32[8,32,32]{2,1,0:T(8,128)S(1)} %get-tuple-element.52.w_a, f32[8,32,32]{2,1,0:T(8,128)S(1)} %copy-done, f32[8,32,32]{2,1,0:T(8,128)S(1)} %copy-done.1), custom_call_target="tpu_custom_call" | custom-call | tf_op jit(solution)/shard_map/pallas_call | solution.py:636
  (45 shorter events, 5.5 us)
Async XLA Ops:
  2.6 8.1 %copy-start.6 = (s32[1024]{0:T(1024)S(1)}, s32[1024]{0:T(1024)}, u32[]{:S(2)}) copy-start(s32[1024]{0:T(1024)} %param.14) | copy-start | bytes 12292
  2.6 13.3 %collective-permute-start = (f32[3,8,32,128]{3,2,1,0:T(8,128)}, f32[3,8,32,128]{3,2,1,0:T(8,128)S(1)}, u32[]{:S(2)}, u32[]{:S(2)}) collective-permute-start(f32[3,8,32,128]{3,2,1,0:T(8,128)} %get-tuple-element.29), channel_id=1, source_target_pairs={{0,4},{4,0},{1,5},{5,1},{2,6},{6,2},{3,7},{7,3},{8,12},{12,8},{9,1... | collective-permute-start | bytes 1179656 | tf_op jit(solution)/shard_map/ppermute | solution.py:665
  5.6 7.2 %collective-permute-start.3 = (f32[2,2,32,128]{3,2,1,0:T(8,128)}, f32[2,2,32,128]{3,2,1,0:T(8,128)S(1)}, u32[]{:S(2)}, u32[]{:S(2)}) collective-permute-start(f32[2,2,32,128]{3,2,1,0:T(8,128)} %get-tuple-element.30), channel_id=1, source_target_pairs={{0,24},{8,16},{16,8},{24,0},{1,25},{9,17},{17,9},{25,1},{2,26},{10... | collective-permute-start | bytes 196616 | tf_op jit(solution)/shard_map/ppermute | solution.py:671
  9.2 5.6 %collective-permute-start.2 = (f32[2,2,32,128]{3,2,1,0:T(8,128)}, f32[2,2,32,128]{3,2,1,0:T(8,128)S(1)}, u32[]{:S(2)}, u32[]{:S(2)}) collective-permute-start(f32[2,2,32,128]{3,2,1,0:T(8,128)} %get-tuple-element.30), channel_id=1, source_target_pairs={{0,16},{8,24},{16,0},{24,8},{1,17},{9,25},{17,1},{25,9},{2,18},{10... | collective-permute-start | bytes 196616 | tf_op jit(solution)/shard_map/ppermute | solution.py:671
  9.2 5.6 %collective-permute-start.1 = (f32[2,2,32,128]{3,2,1,0:T(8,128)}, f32[2,2,32,128]{3,2,1,0:T(8,128)S(1)}, u32[]{:S(2)}, u32[]{:S(2)}) collective-permute-start(f32[2,2,32,128]{3,2,1,0:T(8,128)} %get-tuple-element.30), channel_id=1, source_target_pairs={{0,8},{8,0},{16,24},{24,16},{1,9},{9,1},{17,25},{25,17},{2,10},{10... | collective-permute-start | bytes 196616 | tf_op jit(solution)/shard_map/ppermute | solution.py:671
  10.6 4.2 %copy-start = (f32[8,32,32]{2,1,0:T(8,128)S(1)}, f32[8,32,32]{2,1,0:T(8,128)}, u32[]{:S(2)}) copy-start(f32[8,32,32]{2,1,0:T(8,128)} %vk.3) | copy-start | bytes 98308
  10.6 4.2 %copy-start.1 = (f32[8,32,32]{2,1,0:T(8,128)S(1)}, f32[8,32,32]{2,1,0:T(8,128)}, u32[]{:S(2)}) copy-start(f32[8,32,32]{2,1,0:T(8,128)} %va.3) | copy-start | bytes 98308
  14.8 1.1 %copy-start.3 = (s32[8,32,128]{2,1,0:T(8,128)S(1)}, s32[8,32,128]{2,1,0:T(8,128)}, u32[]{:S(2)}) copy-start(s32[8,32,128]{2,1,0:T(8,128)} %refs_1_.4) | copy-start | bytes 393220
  15.3 7.7 %collective-permute-start.5 = (f32[2,8,32,128]{3,2,1,0:T(8,128)S(1)}, f32[2,8,32,128]{3,2,1,0:T(8,128)S(1)}, u32[]{:S(2)}, u32[]{:S(2)}) collective-permute-start(f32[2,8,32,128]{3,2,1,0:T(8,128)S(1)} %shard_map.123.refs_3_.refs_0_), channel_id=1, source_target_pairs={{0,4},{4,0},{1,5},{5,1},{2,6},{6,2},{3,7},{7,3},{8,12},{12,8},{9,1... | collective-permute-start | bytes 786440 | tf_op jit(solution)/shard_map/ppermute | solution.py:665
  16.5 6.7 %collective-permute-start.4 = (f32[2,16,32,128]{3,2,1,0:T(8,128)S(1)}, f32[2,16,32,128]{3,2,1,0:T(8,128)S(1)}, u32[]{:S(2)}, u32[]{:S(2)}) collective-permute-start(f32[2,16,32,128]{3,2,1,0:T(8,128)S(1)} %get-tuple-element.33.refs_1_.refs_3_), channel_id=1, source_target_pairs={{0,1},{1,0},{2,3},{3,2},{4,5},{5,4},{6,7},{7,6},{8,9},{9,8},{10,11... | collective-permute-start | bytes 1572872 | tf_op jit(solution)/shard_map/ppermute | solution.py:668
  23.0 2.0 %collective-permute-start.7 = (f32[2,16,32,128]{3,2,1,0:T(8,128)S(1)}, f32[2,16,32,128]{3,2,1,0:T(8,128)S(1)}, u32[]{:S(2)}, u32[]{:S(2)}) collective-permute-start(f32[2,16,32,128]{3,2,1,0:T(8,128)S(1)} %shard_map.125.refs_3_.refs_0_.vector), channel_id=1, source_target_pairs={{0,1},{1,0},{2,3},{3,2},{4,5},{5,4},{6,7},{7,6},{8,9},{9,8},{10,11... | collective-permute-start | bytes 1572872 | tf_op jit(solution)/shard_map/ppermute | solution.py:668
  23.2 5.7 %copy-start.7 = (f32[16]{0:T(128)S(1)}, f32[16]{0:T(128)}, u32[]{:S(2)}) copy-start(f32[16]{0:T(128)} %refs_0_.5) | copy-start | bytes 196
  23.2 5.7 %copy-start.8 = (f32[16]{0:T(128)S(1)}, f32[16]{0:T(128)}, u32[]{:S(2)}) copy-start(f32[16]{0:T(128)} %refs_1_.5) | copy-start | bytes 196
  23.2 5.7 %collective-permute-start.6 = (f32[2,4,24,128]{3,2,1,0:T(8,128)S(1)}, f32[2,4,24,128]{3,2,1,0:T(8,128)S(1)}, u32[]{:S(2)}, u32[]{:S(2)}) collective-permute-start(f32[2,4,24,128]{3,2,1,0:T(8,128)S(1)} %shard_map.126.refs_2_), channel_id=1, source_target_pairs={{0,2},{1,3},{2,0},{3,1},{4,6},{5,7},{6,4},{7,5},{8,10},{9,11},{10,... | collective-permute-start | bytes 294920 | tf_op jit(solution)/shard_map/ppermute | solution.py:691
  25.1 6.2 %collective-permute-start.8 = (f32[2,4,24,128]{3,2,1,0:T(8,128)S(1)}, f32[2,4,24,128]{3,2,1,0:T(8,128)S(1)}, u32[]{:S(2)}, u32[]{:S(2)}) collective-permute-start(f32[2,4,24,128]{3,2,1,0:T(8,128)S(1)} %shard_map.127.refs_7_), channel_id=1, source_target_pairs={{0,2},{1,3},{2,0},{3,1},{4,6},{5,7},{6,4},{7,5},{8,10},{9,11},{10,... | collective-permute-start | bytes 294920 | tf_op jit(solution)/shard_map/ppermute | solution.py:691
  35.6 4.3 %collective-permute-start.9 = (f32[4,32,128]{2,1,0:T(8,128)S(1)}, f32[4,32,128]{2,1,0:T(8,128)S(1)}, u32[]{:S(2)}, u32[]{:S(2)}) collective-permute-start(f32[4,32,128]{2,1,0:T(8,128)S(1)} %get-tuple-element.41.sent), channel_id=1, source_target_pairs={{0,2},{1,3},{2,0},{3,1},{4,6},{5,7},{6,4},{7,5},{8,10},{9,11},{10,... | collective-permute-start | bytes 196616 | tf_op jit(solution)/shard_map/ppermute | solution.py:691
  44.2 2.0 %collective-permute-start.10 = (f32[2,16,32,128]{3,2,1,0:T(8,128)S(1)}, f32[2,16,32,128]{3,2,1,0:T(8,128)S(1)}, u32[]{:S(2)}, u32[]{:S(2)}) collective-permute-start(f32[2,16,32,128]{3,2,1,0:T(8,128)S(1)} %get-tuple-element.43), channel_id=1, source_target_pairs={{0,1},{1,0},{2,3},{3,2},{4,5},{5,4},{6,7},{7,6},{8,9},{9,8},{10,11... | collective-permute-start | bytes 1572872 | tf_op jit(solution)/shard_map/ppermute | solution.py:668
  46.4 6.4 %collective-permute-start.12 = (f32[2,2,2,32,128]{4,3,2,1,0:T(8,128)S(1)}, f32[2,2,2,32,128]{4,3,2,1,0:T(8,128)S(1)}, u32[]{:S(2)}, u32[]{:S(2)}) collective-permute-start(f32[2,2,2,32,128]{4,3,2,1,0:T(8,128)S(1)} %shard_map.131.refs_2_), channel_id=1, source_target_pairs={{0,4},{4,0},{1,5},{5,1},{2,6},{6,2},{3,7},{7,3},{8,12},{12,8},{9,1... | collective-permute-start | bytes 393224 | tf_op jit(solution)/shard_map/ppermute | solution.py:665
  47.5 8.0 %collective-permute-start.11 = (f32[2,2,2,32,128]{4,3,2,1,0:T(8,128)S(1)}, f32[2,2,2,32,128]{4,3,2,1,0:T(8,128)S(1)}, u32[]{:S(2)}, u32[]{:S(2)}) collective-permute-start(f32[2,2,2,32,128]{4,3,2,1,0:T(8,128)S(1)} %get-tuple-element.45), channel_id=1, source_target_pairs={{0,4},{4,0},{1,5},{5,1},{2,6},{6,2},{3,7},{7,3},{8,12},{12,8},{9,1... | collective-permute-start | bytes 393224 | tf_op jit(solution)/shard_map/ppermute | solution.py:665
  52.8 6.0 %collective-permute-start.13 = (f32[2,2,32,128]{3,2,1,0:T(8,128)S(1)}, f32[2,2,32,128]{3,2,1,0:T(8,128)S(1)}, u32[]{:S(2)}, u32[]{:S(2)}) collective-permute-start(f32[2,2,32,128]{3,2,1,0:T(8,128)S(1)} %get-tuple-element.47), channel_id=1, source_target_pairs={{0,16},{8,24},{16,0},{24,8},{1,17},{9,25},{17,1},{25,9},{2,18},{10... | collective-permute-start | bytes 196616 | tf_op jit(solution)/shard_map/ppermute | solution.py:671
  53.6 6.2 %collective-permute-start.14 = (f32[2,2,32,128]{3,2,1,0:T(8,128)S(1)}, f32[2,2,32,128]{3,2,1,0:T(8,128)S(1)}, u32[]{:S(2)}, u32[]{:S(2)}) collective-permute-start(f32[2,2,32,128]{3,2,1,0:T(8,128)S(1)} %get-tuple-element.48), channel_id=1, source_target_pairs={{0,24},{8,16},{16,8},{24,0},{1,25},{9,17},{17,9},{25,1},{2,26},{10... | collective-permute-start | bytes 196616 | tf_op jit(solution)/shard_map/ppermute | solution.py:671
  55.5 4.9 %copy-start.4 = (f32[8,32,32]{2,1,0:T(8,128)S(1)}, f32[8,32,32]{2,1,0:T(8,128)}, u32[]{:S(2)}) copy-start(f32[8,32,32]{2,1,0:T(8,128)} %refs_6_.1) | copy-start | bytes 98308
  55.5 4.9 %copy-start.5 = (f32[8,32,32]{2,1,0:T(8,128)S(1)}, f32[8,32,32]{2,1,0:T(8,128)}, u32[]{:S(2)}) copy-start(f32[8,32,32]{2,1,0:T(8,128)} %refs_7_.1) | copy-start | bytes 98308
  55.5 4.9 %collective-permute-start.15 = (f32[2,2,32,128]{3,2,1,0:T(8,128)S(1)}, f32[2,2,32,128]{3,2,1,0:T(8,128)S(1)}, u32[]{:S(2)}, u32[]{:S(2)}) collective-permute-start(f32[2,2,32,128]{3,2,1,0:T(8,128)S(1)} %get-tuple-element.49), channel_id=1, source_target_pairs={{0,8},{8,0},{16,24},{24,16},{1,9},{9,1},{17,25},{25,17},{2,10},{10... | collective-permute-start | bytes 196616 | tf_op jit(solution)/shard_map/ppermute | solution.py:671
  (1 other events, 1.0 us)

commit v10 on v9

--- a/solution.py
+++ b/solution.py
@@ -193,24 +193,29 @@
 def pack_kernel(bg, labels, vk, va, packed, message, raw, v_in, sems):
     _, x, _, _ = places(2)
     half = bg.shape[0] // 2
+    cx = labels.shape[0]
     copies = [
         pltpu.make_async_copy(src, dst, sems.at[i])
         for i, (src, dst) in enumerate((
             (vk, v_in.at[0]),
             (va, v_in.at[1]),
-            (bg.at[pl.ds(half * (1 - x), half)], message.at[pl.ds(0, half)]),
             (labels, raw),
+            *((bg.at[half * (1 - x) + i], message.at[pl.ds(cx * i, cx)]) for i in range(half)),
         ))
     ]
     for copy in copies:
         copy.start()
+    groups = packed.shape[0] // 2
     for f in range(2):
         copies[f].wait()
-        for q in range(packed.shape[1]):
-            packed[f, q] = packed_planes(v_in.at[f], q)
-    copies[3].wait()
-    message[half] = raw[...].astype(jnp.float32)
+        for q in range(groups):
+            planes = packed_planes(v_in.at[f], q)
+            packed[groups * f + q] = planes
+            message[cx * (half + 1) + groups * f + q] = planes
     copies[2].wait()
+    message[pl.ds(cx * half, cx)] = raw[...].astype(jnp.float32)
+    for copy in copies[3:]:
+        copy.wait()
 
 
 def count_kernel(dets, beta_prev, count, beta_row, *, ny, nz, half, halo):
@@ -252,38 +257,66 @@
     ]
     for copy in copies:
         copy.start()
-    mine[pl.ds(there, cx)] = msg[c]
-    fields[0, pl.ds(there, cx)] = msg[1 - c]
-    fields[1, pl.ds(there, cx)] = msg[half]
+    mine[pl.ds(there, cx)] = msg[pl.ds(cx * c, cx)]
+    fields[0, pl.ds(there, cx)] = msg[pl.ds(cx * (1 - c), cx)]
+    fields[1, pl.ds(there, cx)] = msg[pl.ds(cx * half, cx)]
     for copy in copies:
         copy.wait()
     fields[1, pl.ds(here, cx)] = raw[...].astype(jnp.float32)
 
 
-def unpack_kernel(*refs):
-    own, parts, full = refs[:2], refs[2:-1], refs[-1]
-    n = len(parts) + 1
+def unpacked(blocks, groups, s, store):
+    n = len(blocks)
+    cy, lanes = blocks[0][0].shape
+    slab = lanes // n
+    lane = index_along((cy, lanes), 1) // slab
+    for f in range(2):
+        for q in range(groups):
+            values = [block[groups * f + q] for block in blocks]
+            for j in range(n):
+                plane = jnp.zeros((cy, lanes), jnp.float32)
+                for k in range(n):
+                    home = s ^ k
+                    moved = pltpu.roll(values[k], ((home - j + n) % n) * slab, 1)
+                    plane = jnp.where(lane == home, moved, plane)
+                store(f, n * q + j, plane)
+
+
+def join_kernel(*refs):
+    joined, size = refs[-1], refs[0].shape[0]
+    for i, ref in enumerate(refs[:-1]):
+        joined[pl.ds(size * i, size)] = ref[...]
+
+
+def own_half_kernel(vk, va, joined, half):
     s, _, _, _ = places(2)
-    slab = 128 // n
-    _, cx, cy, _ = full.shape
-    lane = index_along((cy, 128), 1) // slab
-    for f in range(2):
-        for q in range(cx // n):
-            blocks = [part[f, q] for part in parts]
-            for j in range(n):
-                plane = jnp.concatenate([own[f][n * q + j]] * n, axis=1)
-                for k in range(1, n):
-                    home = s ^ k
-                    moved = pltpu.roll(blocks[k - 1], ((home - j + n) % n) * slab, 1)
-                    plane = jnp.where(lane == home, moved, plane)
-                full[f, n * q + j] = plane
-
-
-def vector_kernel(own, came, fields):
-    _, x, _, _ = places(2)
-    cx = own.shape[1]
-    fields[:, pl.ds(cx * x, cx)] = own[...]
-    fields[:, pl.ds(cx * (1 - x), cx)] = came[...]
+    size = half.shape[1]
+    groups = joined.shape[0] // 2 // (128 // vk.shape[2] - 1)
+    n = size // groups
+    own = [packed_planes(ref, q) for ref in (vk, va) for q in range(groups)]
+    blocks = [own] + [[joined[2 * groups * k + i] for i in range(2 * groups)] for k in range(n - 1)]
+
+    def store(f, i, plane):
+        half[f, i] = plane
+
+    unpacked(blocks, groups, s, store)
+
+
+def vector_kernel(half, msg, joined, fields):
+    s, x, _, _ = places(2)
+    cx = half.shape[1]
+    fields[:, pl.ds(cx * x, cx)] = half[...]
+    n = lax.axis_size("src")
+    groups = cx // n
+    own = msg.shape[0] - 2 * groups
+    blocks = [[msg[own + i] for i in range(2 * groups)]]
+    blocks += [[joined[2 * groups * k + i] for i in range(2 * groups)] for k in range(n - 1)]
+    there = cx * (1 - x)
+
+    def store(f, i, plane):
+        fields[f, there + i] = plane
+
+    unpacked(blocks, groups, s, store)
 
 
 def edge_shape(planes, lanes):
@@ -333,19 +366,17 @@
         src, dst = bufs[step % 2], bufs[(step + 1) % 2]
 
         def body(i, carry):
-            u, flow = carry
-            beyond_x = src[i + 2]
+            u = src[i + 1]
             coef_y, coef_z = fy[i], fz[i]
-            next_flow = fx[i + 1] * (beyond_x - u)
-            left = b[i] - diag[i] * u + (next_flow - flow)
+            left = b[i] - diag[i] * u
+            left = left + fx[i] * src[i] + fx[i + 1] * src[i + 2]
             left = left + coef_y * shifted(u, -1, 0) + shifted(coef_y * u, 1, 0)
             left = left + coef_z * shifted(u, -1, 1) + shifted(coef_z * u, 1, 1)
             change = u if step == 0 else u - dst[i + 1]
             dst[i + 1] = u + keep * change + push * left
-            return beyond_x, next_flow
-
-        first = src[1]
-        lax.fori_loop(0, planes, body, (first, fx[0] * first), unroll=unroll)
+            return carry
+
+        lax.fori_loop(0, planes, body, 0, unroll=unroll)
     return bufs[len(pairs) % 2]
 
 
@@ -406,12 +437,13 @@
 
     def set_up(i, carry):
         k = kap[i + 1]
+        along_x = 0.5 * (k + kap[i + 2])
         along_y, along_z = 0.5 * (k + beyond(k, 1, 0)), 0.5 * (k + beyond(k, 1, 1))
-        fx[i + 1] = 0.5 * (k + kap[i + 2])
+        fx[i + 1] = along_x
         fy[i] = jnp.where(index_along(k.shape, 0) == rows - 1, 0.0, along_y)
         fz[i] = jnp.where(lane == lanes - 1, 0.0, along_z)
         back_y, back_z = 0.5 * (k + beyond(k, -1, 0)), 0.5 * (k + beyond(k, -1, 1))
-        diag[i] = diag[i] + along_y + back_y + along_z + back_z
+        diag[i] = diag[i] + fx[i] + along_x + along_y + back_y + along_z + back_z
         total, square = carry
         for p, at in ((mine[i], c), (got[0, i], 1 - c)):
             part = count[i, pl.ds(base + cy * at, cy), :] * p
@@ -545,20 +577,18 @@
                 outs[i, f, q] = piece
 
 
-def far_kernel(own, came, far):
+def send_kernel(own, came, out, *, k):
     _, x, _, _ = places(2)
-    packed_slabs(own, came, 1 - x, range(far.shape[0], 2 * far.shape[0]), far)
-
-
-def near_kernel(own, came, kept, near):
+    packed_slabs(own, came, 1 - x, (k,), out)
+
+
+def keep_kernel(own, came, kept):
     _, x, _, _ = places(2)
-    packed_slabs(own, came, 1 - x, range(near.shape[0]), near)
     packed_slabs(own, came, x, range(kept.shape[0]), kept)
 
 
-def add_kernel(kept, came, *outs, first):
-    for i, out in enumerate(outs):
-        out[...] = kept[first + i] + came[i]
+def add_kernel(kept, came, out, *, k):
+    out[...] = kept[k] + came[0]
 
 
 def sum_kernel(*refs):
@@ -674,9 +704,9 @@
     float_block = lambda *shape: (shape, jnp.float32)
     raw_labels = (block, jnp.int32)
     packed, message = run(
-        pack_kernel, (f32(2, groups, cy, cz), f32(sources // 2 + 1, *block)),
+        pack_kernel, (f32(2 * groups, cy, cz), f32((sources // 2 + 1) * cx + 2 * groups, cy, cz)),
         background, labels, v_kappa, v_absorb, hbm=(0, 1, 2, 3),
-        scratch=(raw_labels, float_block(2, *v_kappa.shape)), copies=4, mib=60,
+        scratch=(raw_labels, float_block(2, *v_kappa.shape)), copies=3 + sources // 2, mib=60,
     )
     long = pl.CostEstimate(flops=10**9, bytes_accessed=2**26, transcendentals=0)
     came = swap_x(message)
@@ -690,14 +720,17 @@
     def across_y(value):
         return lax.ppermute(value, "gy", [(i, (i + 2) % 4) for i in range(4)])
 
-    (half_vector,) = run(unpack_kernel, (f32(2, *block),), v_kappa, v_absorb, *slabs, after=(count,))
-    half_came = swap_x(half_vector)
+    (joined,) = run(join_kernel, (f32(2 * groups * (n - 1), cy, cz),), *slabs, after=(count,))
+    joined_came = swap_x(joined)
+    (half_vector,) = run(own_half_kernel, (f32(2, *block),), v_kappa, v_absorb, joined)
     mine, fields = run(
         photon_kernel, (f32(planes, cy, cz), f32(2, planes, cy, cz)),
-        background, labels, came, after=(half_vector,), hbm=(0, 1), scratch=(raw_labels,), copies=3,
+        background, labels, came, after=(joined,), hbm=(0, 1), scratch=(raw_labels,), copies=3,
     )
     got = swap_core(fields)
-    (vector,) = run(vector_kernel, (f32(2, planes, cy, cz),), half_vector, half_came, after=(mine,))
+    (vector,) = run(
+        vector_kernel, (f32(2, planes, cy, cz),), half_vector, came, joined_came, after=(mine,)
+    )
     edge = (f32(2, *edge_shape(planes, cz)),)
     (sent,) = run(photon_edge_kernel, edge, mine, fields, got, after=(vector,))
     photon_edge = across_y(sent)
@@ -725,17 +758,18 @@
         scratch=(float_frame, float_wide, float_wide, float_frame, float_frame),
     )
     piece = f32(2, groups, cy, cz)
-    half = n // 2
     got = swap_core(message)
-    (far,) = run(far_kernel, (f32(half, *piece.shape),), own, got)
-    kept, near = run(
-        near_kernel, (f32(n, *piece.shape), f32(half, *piece.shape)), own, got, after=(far,)
-    )
-    far, near = swap_x(far), swap_x(near)
-    pieces = run(functools.partial(add_kernel, first=half), [piece] * (n - half), kept, far)
-    (distant,) = run(sum_kernel, (piece,), *(along_z(value, half + i) for i, value in enumerate(pieces)), cost=long)
-    pieces = run(functools.partial(add_kernel, first=0), [piece] * half, kept, near)
-    parts = [pieces[0], distant] + [along_z(pieces[k], k) for k in range(1, half)]
+    crossed, last = {}, ()
+    for k in reversed(range(n)):
+        last = run(functools.partial(send_kernel, k=k), (f32(1, *piece.shape),), own, got, after=last)
+        crossed[k] = swap_x(last[0])
+    (kept,) = run(keep_kernel, (f32(n, *piece.shape),), own, got, after=last)
+    totals = {
+        k: run(functools.partial(add_kernel, k=k), (piece,), kept, value)[0] for k, value in crossed.items()
+    }
+    received = {k: along_z(totals[k], k) for k in reversed(range(1, n))}
+    (distant,) = run(sum_kernel, (piece,), *(received[k] for k in range(n // 2, n)), cost=long)
+    parts = [distant, totals[0]] + [received[k] for k in range(1, n // 2)]
     w_k, w_a, tile = run(
         functools.partial(project_kernel, parts_n=len(parts), n=n),
         (f32(*v_kappa.shape), f32(*v_kappa.shape), f32(8, 128)),

time: 73.8 us -> 73 us (0.989)
  waiting for transfers between devices: 23.3 us -> 18.1 us
  starting transfers between devices: 18.7 us -> 22 us
  blocking collectives: 11.6 us -> 12.4 us
    ppermute x4 -> x6, waiting for transfers between devices: 10.2 us -> 4.81 us  [swap_x(): return lax.ppermute(value, 'gx', [(0, 1), (1, 0)])]
    ppermute x4 -> x6, starting transfers between devices: 5.68 us -> 7.76 us  [swap_x(): return lax.ppermute(value, 'gx', [(0, 1), (1, 0)])]
    ppermute x6, starting transfers between devices: 8.01 us -> 9.3 us  [along_z(): return lax.ppermute(value, 'src', [(i, i ^ k) for i in range(n)])]
    all_to_all x1, blocking collectives: 11.6 us -> 12.4 us  [per_device_paired(): lax.all_to_all(jnp.broadcast_to(tile, (8 * n, 8, 128)), everyone, 0, 0)]
    pallas_call x17 -> x23, Pallas kernels: 18.4 us -> 18.6 us  [run(): pl.pallas_call(body if waits else kernel, out_shape=tuple(outs), in_specs...]
  transfers between devices with their start and end apart: 16 -> 18, of which waited for: 11 -> 12; matrix products, arithmetic and copies ran while one was open for 0% -> 0% of each run, Pallas kernels for 8% -> 9%
where the time goes in v10:
time: 73 us; the launch traced here: 72.8 us
  starting transfers between devices  22 us (30%)
  Pallas kernels  18.6 us (25%)
  waiting for transfers between devices  18.1 us (25%)
  blocking collectives  12.4 us (17%)
  between operations  1.6 us (2%)
    pallas_call x23, Pallas kernels, run(): pl.pallas_call(body if waits else kernel, out_shape=tuple(outs), in_specs...  18.6 us
    all_to_all x1, blocking collectives, per_device_paired(): lax.all_to_all(jnp.broadcast_to(tile, (8 * n, 8, 128)), everyone, 0, 0)  12.4 us
    ppermute x6, starting transfers between devices, along_z(): return lax.ppermute(value, 'src', [(i, i ^ k) for i in range(n)])  9.3 us
    ppermute x6, starting transfers between devices, swap_x(): return lax.ppermute(value, 'gx', [(0, 1), (1, 0)])  7.76 us
    ppermute x6, waiting for transfers between devices, along_z(): return lax.ppermute(value, 'src', [(i, i ^ k) for i in range(n)])  6.25 us
    ppermute x3, waiting for transfers between devices, across_y(): return lax.ppermute(value, 'gy', [(i, (i + 2) % 4) for i in range(4)])  4.96 us
    ppermute x6, waiting for transfers between devices, swap_x(): return lax.ppermute(value, 'gx', [(0, 1), (1, 0)])  4.81 us
    ppermute x3, starting transfers between devices, across_y(): return lax.ppermute(value, 'gy', [(i, (i + 2) % 4) for i in range(4)])  4.77 us
  transfers between devices with their start and end apart: 18, of which 12 were waited for; matrix products, arithmetic and copies ran while one was open for 0% of the time, Pallas kernels for 9%

profile of v10, /device:TPU:0, one launch (start us, length us, event | category | flops | bytes accessed | tf_op | source)
XLA Modules:
  0.0 72.8 jit_solution(2877510291636765763)
XLA Ops:
  0.6 2.0 %shard_map.122 = (f32[4,32,128]{2,1,0:T(8,128)}, f32[28,32,128]{2,1,0:T(8,128)}) custom-call(f32[4,8,32,128]{3,2,1,0:T(8,128)} %refs_0_.2, s32[8,32,128]{2,1,0:T(8,128)} %refs_1_.2, f32[8,32,32]{2,1,0:T(8,128)} %vk.5, f32[8,32,32]{2,1,0:T(8,128)} %va.5), custom_call_target="tpu_custom_call" | custom-call | tf_op jit(solution)/shard_map/pallas_call | solution.py:666
  2.7 3.0 %collective-permute-start = (f32[28,32,128]{2,1,0:T(8,128)}, f32[28,32,128]{2,1,0:T(8,128)S(1)}, u32[]{:S(2)}, u32[]{:S(2)}) collective-permute-start(f32[28,32,128]{2,1,0:T(8,128)} %get-tuple-element.23), channel_id=1, source_target_pairs={{0,4},{4,0},{1,5},{5,1},{2,6},{6,2},{3,7},{7,3},{8,12},{12,8},{9,1... | collective-permute-start | bytes 1376264 | tf_op jit(solution)/shard_map/ppermute | solution.py:695
  5.7 3.6 %collective-permute-start.3 = (f32[4,32,128]{2,1,0:T(8,128)}, f32[4,32,128]{2,1,0:T(8,128)S(1)}, u32[]{:S(2)}, u32[]{:S(2)}) collective-permute-start(f32[4,32,128]{2,1,0:T(8,128)} %get-tuple-element.24), channel_id=1, source_target_pairs={{0,24},{8,16},{16,8},{24,0},{1,25},{9,17},{17,9},{25,1},{2,26},{10... | collective-permute-start | bytes 196616 | tf_op jit(solution)/shard_map/ppermute | solution.py:701
  10.7 2.1 %shard_map.121 = (f32[16,72,128]{2,1,0:T(8,128)S(1)}, f32[1,128]{1,0:T(1,128)S(1)}) custom-call(s32[1,1024]{1,0:T(1,128)S(1)} %bitcast.1, f32[1]{0:T(128)S(6)} %copy.13.beta_prev), custom_call_target="tpu_custom_call" | custom-call | flops 301989888 | bytes 589824 | tf_op jit(solution)/shard_map/pallas_call | solution.py:666
  12.8 2.0 %collective-permute-done.2.refs_1_ = f32[4,32,128]{2,1,0:T(8,128)S(1)} collective-permute-done((f32[4,32,128]{2,1,0:T(8,128)}, f32[4,32,128]{2,1,0:T(8,128)S(1)}, u32[]{:S(2)}, u32[]{:S(2)}) %collective-permute-start.2) | collective-permute-done | bytes 65568 | tf_op jit(solution)/shard_map/ppermute | solution.py:701
  17.5 3.7 %collective-permute-done.5.refs_2_ = f32[12,32,128]{2,1,0:T(8,128)S(1)} collective-permute-done((f32[12,32,128]{2,1,0:T(8,128)S(1)}, f32[12,32,128]{2,1,0:T(8,128)S(1)}, u32[]{:S(2)}, u32[]{:S(2)}) %collective-permute-start.5) | collective-permute-done | bytes 196640 | tf_op jit(solution)/shard_map/ppermute | solution.py:695
  21.7 1.6 %collective-permute-start.6 = (f32[2,4,24,128]{3,2,1,0:T(8,128)S(1)}, f32[2,4,24,128]{3,2,1,0:T(8,128)S(1)}, u32[]{:S(2)}, u32[]{:S(2)}) collective-permute-start(f32[2,4,24,128]{3,2,1,0:T(8,128)S(1)} %shard_map.127.refs_2_), channel_id=1, source_target_pairs={{0,2},{1,3},{2,0},{3,1},{4,6},{5,7},{6,4},{7,5},{8,10},{9,11},{10,... | collective-permute-start | bytes 294920 | tf_op jit(solution)/shard_map/ppermute | solution.py:721
  23.6 1.6 %collective-permute-start.8 = (f32[2,4,24,128]{3,2,1,0:T(8,128)S(1)}, f32[2,4,24,128]{3,2,1,0:T(8,128)S(1)}, u32[]{:S(2)}, u32[]{:S(2)}) collective-permute-start(f32[2,4,24,128]{3,2,1,0:T(8,128)S(1)} %shard_map.128.refs_7_), channel_id=1, source_target_pairs={{0,2},{1,3},{2,0},{3,1},{4,6},{5,7},{6,4},{7,5},{8,10},{9,11},{10,... | collective-permute-start | bytes 294920 | tf_op jit(solution)/shard_map/ppermute | solution.py:721
  25.2 2.2 %collective-permute-done.6.refs_5_.photon_edge = f32[2,4,24,128]{3,2,1,0:T(8,128)S(1)} collective-permute-done((f32[2,4,24,128]{3,2,1,0:T(8,128)S(1)}, f32[2,4,24,128]{3,2,1,0:T(8,128)S(1)}, u32[]{:S(2)}, u32[]{:S(2)}) %collective-permute-start.6) | collective-permute-done | bytes 98336 | tf_op jit(solution)/shard_map/ppermute | solution.py:721
  27.4 2.3 %shard_map.129 = (f32[16,72,128]{2,1,0:T(8,128)S(1)}, f32[17,72,128]{2,1,0:T(8,128)S(1)}, f32[16,72,128]{2,1,0:T(8,128)S(1)}, f32[16,72,128]{2,1,0:T(8,128)S(1)}, f32[2,8,128]{2,1,0:T(8,128)S(1)}) custom-call(f32[16]{0:T(128)S(1)} %copy-done.7, f32[16]{0:T(128)S(1)} %copy-done.8, f32[16,32,128]{2,1,0:T(8,128)S(1)} %get-tuple-element.26.refs_3_.refs_0_.refs_2_.mine, ...), custom_call_target="tpu_custom_call" | custom-call | flops 1000000000 | bytes 67108864 | tf_op jit(solution)/shard_map/pallas_call | solution.py:666
  29.7 4.1 %shard_map.130 = (f32[18,72,128]{2,1,0:T(8,128)S(1)}, f32[16,72,128]{2,1,0:T(8,128)S(1)}, f32[4,32,128]{2,1,0:T(8,128)S(1)}) custom-call(f32[16,72,128]{2,1,0:T(8,128)S(1)} %get-tuple-element.28.diag, f32[17,72,128]{2,1,0:T(8,128)S(1)} %get-tuple-element.29.fx, f32[16,72,128]{2,1,0:T(8,128)S(1)} %get-tuple-element.30.fy, ...), custom_call_target="tpu_custom_call" | custom-call | tf_op jit(solution)/shard_map/pallas_call | solution.py:666
  33.9 1.6 %collective-permute-start.9 = (f32[4,32,128]{2,1,0:T(8,128)S(1)}, f32[4,32,128]{2,1,0:T(8,128)S(1)}, u32[]{:S(2)}, u32[]{:S(2)}) collective-permute-start(f32[4,32,128]{2,1,0:T(8,128)S(1)} %get-tuple-element.35.sent), channel_id=1, source_target_pairs={{0,2},{1,3},{2,0},{3,1},{4,6},{5,7},{6,4},{7,5},{8,10},{9,11},{10,... | collective-permute-start | bytes 196616 | tf_op jit(solution)/shard_map/ppermute | solution.py:721
  35.5 2.7 %collective-permute-done.9.came = f32[4,32,128]{2,1,0:T(8,128)S(1)} collective-permute-done((f32[4,32,128]{2,1,0:T(8,128)S(1)}, f32[4,32,128]{2,1,0:T(8,128)S(1)}, u32[]{:S(2)}, u32[]{:S(2)}) %collective-permute-start.9) | collective-permute-done | bytes 65568 | tf_op jit(solution)/shard_map/ppermute | solution.py:721
  38.2 4.1 %shard_map.131 = (f32[2,16,32,128]{3,2,1,0:T(8,128)S(1)}, f32[2,16,32,128]{3,2,1,0:T(8,128)S(1)}) custom-call(f32[18,72,128]{2,1,0:T(8,128)S(1)} %get-tuple-element.33.phi, f32[16,72,128]{2,1,0:T(8,128)S(1)} %get-tuple-element.34.change, f32[16,72,128]{2,1,0:T(8,128)S(1)} %get-tuple-element.28.diag, f32[17,72,128]{2,1,0:T(8,128)S(1)} %get-tuple-element.29.fx, ...), custom_call_target="tpu_custom_call" | custom-call | tf_op jit(solution)/shard_map/pallas_call | solution.py:666
  42.4 1.9 %collective-permute-done.10.came.refs_1_ = f32[2,16,32,128]{3,2,1,0:T(8,128)S(1)} collective-permute-done((f32[2,16,32,128]{3,2,1,0:T(8,128)S(1)}, f32[2,16,32,128]{3,2,1,0:T(8,128)S(1)}, u32[]{:S(2)}, u32[]{:S(2)}) %collective-permute-start.10) | collective-permute-done | bytes 524320 | tf_op jit(solution)/shard_map/ppermute | solution.py:698
  44.6 1.2 %collective-permute-start.11 = (f32[1,2,2,32,128]{4,3,2,1,0:T(8,128)S(1)}, f32[1,2,2,32,128]{4,3,2,1,0:T(8,128)S(1)}, u32[]{:S(2)}, u32[]{:S(2)}) collective-permute-start(f32[1,2,2,32,128]{4,3,2,1,0:T(8,128)S(1)} %shard_map.133.refs_2_), channel_id=1, source_target_pairs={{0,4},{4,0},{1,5},{5,1},{2,6},{6,2},{3,7},{7,3},{8,12},{12,8},{9,1... | collective-permute-start | bytes 196616 | tf_op jit(solution)/shard_map/ppermute | solution.py:695
  46.8 1.2 %collective-permute-start.16 = (f32[1,2,2,32,128]{4,3,2,1,0:T(8,128)S(1)}, f32[1,2,2,32,128]{4,3,2,1,0:T(8,128)S(1)}, u32[]{:S(2)}, u32[]{:S(2)}) collective-permute-start(f32[1,2,2,32,128]{4,3,2,1,0:T(8,128)S(1)} %shard_map.134.refs_2_), channel_id=1, source_target_pairs={{0,4},{4,0},{1,5},{5,1},{2,6},{6,2},{3,7},{7,3},{8,12},{12,8},{9,1... | collective-permute-start | bytes 196616 | tf_op jit(solution)/shard_map/ppermute | solution.py:695
  48.2 1.0 %collective-permute-start.15 = (f32[1,2,2,32,128]{4,3,2,1,0:T(8,128)S(1)}, f32[1,2,2,32,128]{4,3,2,1,0:T(8,128)S(1)}, u32[]{:S(2)}, u32[]{:S(2)}) collective-permute-start(f32[1,2,2,32,128]{4,3,2,1,0:T(8,128)S(1)} %shard_map.135.refs_2_), channel_id=1, source_target_pairs={{0,4},{4,0},{1,5},{5,1},{2,6},{6,2},{3,7},{7,3},{8,12},{12,8},{9,1... | collective-permute-start | bytes 196616 | tf_op jit(solution)/shard_map/ppermute | solution.py:695
  49.6 2.2 %collective-permute-start.12 = (f32[2,2,32,128]{3,2,1,0:T(8,128)S(1)}, f32[2,2,32,128]{3,2,1,0:T(8,128)S(1)}, u32[]{:S(2)}, u32[]{:S(2)}) collective-permute-start(f32[2,2,32,128]{3,2,1,0:T(8,128)S(1)} %shard_map.137), channel_id=1, source_target_pairs={{0,16},{8,24},{16,0},{24,8},{1,17},{9,25},{17,1},{25,9},{2,18},{10... | collective-permute-start | bytes 196616 | tf_op jit(solution)/shard_map/ppermute | solution.py:701
  51.8 2.7 %collective-permute-start.14 = (f32[2,2,32,128]{3,2,1,0:T(8,128)S(1)}, f32[2,2,32,128]{3,2,1,0:T(8,128)S(1)}, u32[]{:S(2)}, u32[]{:S(2)}) collective-permute-start(f32[2,2,32,128]{3,2,1,0:T(8,128)S(1)} %shard_map.138), channel_id=1, source_target_pairs={{0,24},{8,16},{16,8},{24,0},{1,25},{9,17},{17,9},{25,1},{2,26},{10... | collective-permute-start | bytes 196616 | tf_op jit(solution)/shard_map/ppermute | solution.py:701
  54.6 2.3 %collective-permute-done.12.refs_0_ = f32[2,2,32,128]{3,2,1,0:T(8,128)S(1)} collective-permute-done((f32[2,2,32,128]{3,2,1,0:T(8,128)S(1)}, f32[2,2,32,128]{3,2,1,0:T(8,128)S(1)}, u32[]{:S(2)}, u32[]{:S(2)}) %collective-permute-start.12) | collective-permute-done | bytes 65568 | tf_op jit(solution)/shard_map/ppermute | solution.py:701
  56.9 1.2 %collective-permute-done.14.refs_1_ = f32[2,2,32,128]{3,2,1,0:T(8,128)S(1)} collective-permute-done((f32[2,2,32,128]{3,2,1,0:T(8,128)S(1)}, f32[2,2,32,128]{3,2,1,0:T(8,128)S(1)}, u32[]{:S(2)}, u32[]{:S(2)}) %collective-permute-start.14) | collective-permute-done | bytes 65568 | tf_op jit(solution)/shard_map/ppermute | solution.py:701
  59.4 12.4 %all_to_all.5.tiles = f32[32,8,128]{2,1,0:T(8,128)S(1)} all-to-all(f32[32,8,128]{2,1,0:T(8,128)S(1)} %broadcast_in_dim.3), channel_id=1, replica_groups=mesh['src'=4,'gx'=2,'gy'=4] {'src','gx','gy'}, dimensions={0} | all-to-all | bytes 262144 | tf_op jit(solution)/shard_map/all_to_all | solution.py:779
  71.8 1.0 %shard_map.143 = (f32[8,32,32]{2,1,0:T(8,128)}, f32[8,32,32]{2,1,0:T(8,128)}, f32[2]{0:T(128)}) custom-call(f32[32,8,128]{2,1,0:T(8,128)S(1)} %all_to_all.5.tiles, f32[8,32,32]{2,1,0:T(8,128)S(1)} %get-tuple-element.39.w_k, f32[8,32,32]{2,1,0:T(8,128)S(1)} %get-tuple-element.40.w_a, f32[8,32,32]{2,1,0:T(8,128)S(1)} %copy-done, f32[8,32,32]{2,1,0:T(8,128)S(1)} %copy-done.1), custom_call_target="tpu_custom_call" | custom-call | tf_op jit(solution)/shard_map/pallas_call | solution.py:666
  (55 shorter events, 7.6 us)
Async XLA Ops:
  2.6 8.1 %copy-start.6 = (s32[1024]{0:T(1024)S(1)}, s32[1024]{0:T(1024)}, u32[]{:S(2)}) copy-start(s32[1024]{0:T(1024)} %param.14) | copy-start | bytes 12292
  2.7 13.7 %collective-permute-start = (f32[28,32,128]{2,1,0:T(8,128)}, f32[28,32,128]{2,1,0:T(8,128)S(1)}, u32[]{:S(2)}, u32[]{:S(2)}) collective-permute-start(f32[28,32,128]{2,1,0:T(8,128)} %get-tuple-element.23), channel_id=1, source_target_pairs={{0,4},{4,0},{1,5},{5,1},{2,6},{6,2},{3,7},{7,3},{8,12},{12,8},{9,1... | collective-permute-start | bytes 1376264 | tf_op jit(solution)/shard_map/ppermute | solution.py:695
  5.7 7.2 %collective-permute-start.3 = (f32[4,32,128]{2,1,0:T(8,128)}, f32[4,32,128]{2,1,0:T(8,128)S(1)}, u32[]{:S(2)}, u32[]{:S(2)}) collective-permute-start(f32[4,32,128]{2,1,0:T(8,128)} %get-tuple-element.24), channel_id=1, source_target_pairs={{0,24},{8,16},{16,8},{24,0},{1,25},{9,17},{17,9},{25,1},{2,26},{10... | collective-permute-start | bytes 196616 | tf_op jit(solution)/shard_map/ppermute | solution.py:701
  9.3 5.6 %collective-permute-start.2 = (f32[4,32,128]{2,1,0:T(8,128)}, f32[4,32,128]{2,1,0:T(8,128)S(1)}, u32[]{:S(2)}, u32[]{:S(2)}) collective-permute-start(f32[4,32,128]{2,1,0:T(8,128)} %get-tuple-element.24), channel_id=1, source_target_pairs={{0,16},{8,24},{16,0},{24,8},{1,17},{9,25},{17,1},{25,9},{2,18},{10... | collective-permute-start | bytes 196616 | tf_op jit(solution)/shard_map/ppermute | solution.py:701
  9.3 5.6 %collective-permute-start.1 = (f32[4,32,128]{2,1,0:T(8,128)}, f32[4,32,128]{2,1,0:T(8,128)S(1)}, u32[]{:S(2)}, u32[]{:S(2)}) collective-permute-start(f32[4,32,128]{2,1,0:T(8,128)} %get-tuple-element.24), channel_id=1, source_target_pairs={{0,8},{8,0},{16,24},{24,16},{1,9},{9,1},{17,25},{25,17},{2,10},{10... | collective-permute-start | bytes 196616 | tf_op jit(solution)/shard_map/ppermute | solution.py:701
  12.8 3.6 %copy-start.2 = (f32[4,8,32,128]{3,2,1,0:T(8,128)S(1)}, f32[4,8,32,128]{3,2,1,0:T(8,128)}, u32[]{:S(2)}) copy-start(f32[4,8,32,128]{3,2,1,0:T(8,128)} %refs_0_.2) | copy-start | bytes 1572868
  14.9 6.3 %collective-permute-start.5 = (f32[12,32,128]{2,1,0:T(8,128)S(1)}, f32[12,32,128]{2,1,0:T(8,128)S(1)}, u32[]{:S(2)}, u32[]{:S(2)}) collective-permute-start(f32[12,32,128]{2,1,0:T(8,128)S(1)} %shard_map.123.refs_3_.joined), channel_id=1, source_target_pairs={{0,4},{4,0},{1,5},{5,1},{2,6},{6,2},{3,7},{7,3},{8,12},{12,8},{9,1... | collective-permute-start | bytes 589832 | tf_op jit(solution)/shard_map/ppermute | solution.py:695
  17.0 4.7 %collective-permute-start.4 = (f32[2,16,32,128]{3,2,1,0:T(8,128)S(1)}, f32[2,16,32,128]{3,2,1,0:T(8,128)S(1)}, u32[]{:S(2)}, u32[]{:S(2)}) collective-permute-start(f32[2,16,32,128]{3,2,1,0:T(8,128)S(1)} %get-tuple-element.27.refs_1_.refs_3_), channel_id=1, source_target_pairs={{0,1},{1,0},{2,3},{3,2},{4,5},{5,4},{6,7},{7,6},{8,9},{9,8},{10,11... | collective-permute-start | bytes 1572872 | tf_op jit(solution)/shard_map/ppermute | solution.py:698
  21.6 2.0 %collective-permute-start.7 = (f32[2,16,32,128]{3,2,1,0:T(8,128)S(1)}, f32[2,16,32,128]{3,2,1,0:T(8,128)S(1)}, u32[]{:S(2)}, u32[]{:S(2)}) collective-permute-start(f32[2,16,32,128]{3,2,1,0:T(8,128)S(1)} %shard_map.126.refs_3_.refs_0_.vector), channel_id=1, source_target_pairs={{0,1},{1,0},{2,3},{3,2},{4,5},{5,4},{6,7},{7,6},{8,9},{9,8},{10,11... | collective-permute-start | bytes 1572872 | tf_op jit(solution)/shard_map/ppermute | solution.py:698
  21.7 5.7 %copy-start.7 = (f32[16]{0:T(128)S(1)}, f32[16]{0:T(128)}, u32[]{:S(2)}) copy-start(f32[16]{0:T(128)} %refs_0_.3) | copy-start | bytes 196
  21.7 5.7 %copy-start.8 = (f32[16]{0:T(128)S(1)}, f32[16]{0:T(128)}, u32[]{:S(2)}) copy-start(f32[16]{0:T(128)} %refs_1_.3) | copy-start | bytes 196
  21.7 5.7 %collective-permute-start.6 = (f32[2,4,24,128]{3,2,1,0:T(8,128)S(1)}, f32[2,4,24,128]{3,2,1,0:T(8,128)S(1)}, u32[]{:S(2)}, u32[]{:S(2)}) collective-permute-start(f32[2,4,24,128]{3,2,1,0:T(8,128)S(1)} %shard_map.127.refs_2_), channel_id=1, source_target_pairs={{0,2},{1,3},{2,0},{3,1},{4,6},{5,7},{6,4},{7,5},{8,10},{9,11},{10,... | collective-permute-start | bytes 294920 | tf_op jit(solution)/shard_map/ppermute | solution.py:721
  23.6 6.1 %collective-permute-start.8 = (f32[2,4,24,128]{3,2,1,0:T(8,128)S(1)}, f32[2,4,24,128]{3,2,1,0:T(8,128)S(1)}, u32[]{:S(2)}, u32[]{:S(2)}) collective-permute-start(f32[2,4,24,128]{3,2,1,0:T(8,128)S(1)} %shard_map.128.refs_7_), channel_id=1, source_target_pairs={{0,2},{1,3},{2,0},{3,1},{4,6},{5,7},{6,4},{7,5},{8,10},{9,11},{10,... | collective-permute-start | bytes 294920 | tf_op jit(solution)/shard_map/ppermute | solution.py:721
  33.9 4.3 %collective-permute-start.9 = (f32[4,32,128]{2,1,0:T(8,128)S(1)}, f32[4,32,128]{2,1,0:T(8,128)S(1)}, u32[]{:S(2)}, u32[]{:S(2)}) collective-permute-start(f32[4,32,128]{2,1,0:T(8,128)S(1)} %get-tuple-element.35.sent), channel_id=1, source_target_pairs={{0,2},{1,3},{2,0},{3,1},{4,6},{5,7},{6,4},{7,5},{8,10},{9,11},{10,... | collective-permute-start | bytes 196616 | tf_op jit(solution)/shard_map/ppermute | solution.py:721
  42.3 2.0 %collective-permute-start.10 = (f32[2,16,32,128]{3,2,1,0:T(8,128)S(1)}, f32[2,16,32,128]{3,2,1,0:T(8,128)S(1)}, u32[]{:S(2)}, u32[]{:S(2)}) collective-permute-start(f32[2,16,32,128]{3,2,1,0:T(8,128)S(1)} %get-tuple-element.37), channel_id=1, source_target_pairs={{0,1},{1,0},{2,3},{3,2},{4,5},{5,4},{6,7},{7,6},{8,9},{9,8},{10,11... | collective-permute-start | bytes 1572872 | tf_op jit(solution)/shard_map/ppermute | solution.py:698
  44.6 5.0 %collective-permute-start.11 = (f32[1,2,2,32,128]{4,3,2,1,0:T(8,128)S(1)}, f32[1,2,2,32,128]{4,3,2,1,0:T(8,128)S(1)}, u32[]{:S(2)}, u32[]{:S(2)}) collective-permute-start(f32[1,2,2,32,128]{4,3,2,1,0:T(8,128)S(1)} %shard_map.133.refs_2_), channel_id=1, source_target_pairs={{0,4},{4,0},{1,5},{5,1},{2,6},{6,2},{3,7},{7,3},{8,12},{12,8},{9,1... | collective-permute-start | bytes 196616 | tf_op jit(solution)/shard_map/ppermute | solution.py:695
  45.8 6.0 %collective-permute-start.13 = (f32[1,2,2,32,128]{4,3,2,1,0:T(8,128)S(1)}, f32[1,2,2,32,128]{4,3,2,1,0:T(8,128)S(1)}, u32[]{:S(2)}, u32[]{:S(2)}) collective-permute-start(f32[1,2,2,32,128]{4,3,2,1,0:T(8,128)S(1)} %shard_map.132.refs_2_), channel_id=1, source_target_pairs={{0,4},{4,0},{1,5},{5,1},{2,6},{6,2},{3,7},{7,3},{8,12},{12,8},{9,1... | collective-permute-start | bytes 196616 | tf_op jit(solution)/shard_map/ppermute | solution.py:695
  46.8 7.7 %collective-permute-start.16 = (f32[1,2,2,32,128]{4,3,2,1,0:T(8,128)S(1)}, f32[1,2,2,32,128]{4,3,2,1,0:T(8,128)S(1)}, u32[]{:S(2)}, u32[]{:S(2)}) collective-permute-start(f32[1,2,2,32,128]{4,3,2,1,0:T(8,128)S(1)} %shard_map.134.refs_2_), channel_id=1, source_target_pairs={{0,4},{4,0},{1,5},{5,1},{2,6},{6,2},{3,7},{7,3},{8,12},{12,8},{9,1... | collective-permute-start | bytes 196616 | tf_op jit(solution)/shard_map/ppermute | solution.py:695
  48.2 6.4 %collective-permute-start.15 = (f32[1,2,2,32,128]{4,3,2,1,0:T(8,128)S(1)}, f32[1,2,2,32,128]{4,3,2,1,0:T(8,128)S(1)}, u32[]{:S(2)}, u32[]{:S(2)}) collective-permute-start(f32[1,2,2,32,128]{4,3,2,1,0:T(8,128)S(1)} %shard_map.135.refs_2_), channel_id=1, source_target_pairs={{0,4},{4,0},{1,5},{5,1},{2,6},{6,2},{3,7},{7,3},{8,12},{12,8},{9,1... | collective-permute-start | bytes 196616 | tf_op jit(solution)/shard_map/ppermute | solution.py:695
  49.6 7.3 %collective-permute-start.12 = (f32[2,2,32,128]{3,2,1,0:T(8,128)S(1)}, f32[2,2,32,128]{3,2,1,0:T(8,128)S(1)}, u32[]{:S(2)}, u32[]{:S(2)}) collective-permute-start(f32[2,2,32,128]{3,2,1,0:T(8,128)S(1)} %shard_map.137), channel_id=1, source_target_pairs={{0,16},{8,24},{16,0},{24,8},{1,17},{9,25},{17,1},{25,9},{2,18},{10... | collective-permute-start | bytes 196616 | tf_op jit(solution)/shard_map/ppermute | solution.py:701
  51.8 6.2 %collective-permute-start.14 = (f32[2,2,32,128]{3,2,1,0:T(8,128)S(1)}, f32[2,2,32,128]{3,2,1,0:T(8,128)S(1)}, u32[]{:S(2)}, u32[]{:S(2)}) collective-permute-start(f32[2,2,32,128]{3,2,1,0:T(8,128)S(1)} %shard_map.138), channel_id=1, source_target_pairs={{0,24},{8,16},{16,8},{24,0},{1,25},{9,17},{17,9},{25,1},{2,26},{10... | collective-permute-start | bytes 196616 | tf_op jit(solution)/shard_map/ppermute | solution.py:701
  54.5 4.3 %collective-permute-start.17 = (f32[2,2,32,128]{3,2,1,0:T(8,128)S(1)}, f32[2,2,32,128]{3,2,1,0:T(8,128)S(1)}, u32[]{:S(2)}, u32[]{:S(2)}) collective-permute-start(f32[2,2,32,128]{3,2,1,0:T(8,128)S(1)} %shard_map.141), channel_id=1, source_target_pairs={{0,8},{8,0},{16,24},{24,16},{1,9},{9,1},{17,25},{25,17},{2,10},{10... | collective-permute-start | bytes 196616 | tf_op jit(solution)/shard_map/ppermute | solution.py:701
  54.6 4.2 %copy-start.4 = (f32[8,32,32]{2,1,0:T(8,128)S(1)}, f32[8,32,32]{2,1,0:T(8,128)}, u32[]{:S(2)}) copy-start(f32[8,32,32]{2,1,0:T(8,128)} %refs_6_.1) | copy-start | bytes 98308
  54.6 4.2 %copy-start.5 = (f32[8,32,32]{2,1,0:T(8,128)S(1)}, f32[8,32,32]{2,1,0:T(8,128)}, u32[]{:S(2)}) copy-start(f32[8,32,32]{2,1,0:T(8,128)} %refs_7_.1) | copy-start | bytes 98308
  (3 other events, 5.8 us)

commit v11 on v10

--- a/solution.py
+++ b/solution.py
@@ -190,32 +190,32 @@
     return jnp.concatenate([ref[per * q + j] for j in range(per)], axis=1)
 
 
-def pack_kernel(bg, labels, vk, va, packed, message, raw, v_in, sems):
+def pack_kernel(bg, labels, vk, va, packed, message, raw, v_in, slabs, floats, sems):
     _, x, _, _ = places(2)
     half = bg.shape[0] // 2
     cx = labels.shape[0]
-    copies = [
-        pltpu.make_async_copy(src, dst, sems.at[i])
-        for i, (src, dst) in enumerate((
-            (vk, v_in.at[0]),
-            (va, v_in.at[1]),
-            (labels, raw),
-            *((bg.at[half * (1 - x) + i], message.at[pl.ds(cx * i, cx)]) for i in range(half)),
-        ))
+    size = slabs.shape[0]
+
+    def copy(i, src, dst):
+        started = pltpu.make_async_copy(src, dst, sems.at[i])
+        started.start()
+        return started
+
+    arrive = [copy(i, src, dst) for i, (src, dst) in enumerate(((vk, v_in.at[0]), (va, v_in.at[1]), (labels, raw)))]
+    leave = [
+        copy(3 + i, bg.at[half * (1 - x) + i], message.at[pl.ds(cx * i, cx)]) for i in range(half)
     ]
-    for copy in copies:
-        copy.start()
-    groups = packed.shape[0] // 2
     for f in range(2):
-        copies[f].wait()
-        for q in range(groups):
-            planes = packed_planes(v_in.at[f], q)
-            packed[groups * f + q] = planes
-            message[cx * (half + 1) + groups * f + q] = planes
-    copies[2].wait()
-    message[pl.ds(cx * half, cx)] = raw[...].astype(jnp.float32)
-    for copy in copies[3:]:
-        copy.wait()
+        arrive[f].wait()
+        for q in range(size // 2):
+            slabs[size // 2 * f + q] = packed_planes(v_in.at[f], q)
+    leave.append(copy(3 + half, slabs, packed))
+    leave.append(copy(4 + half, slabs, message.at[pl.ds(cx * (half + 1), size)]))
+    arrive[2].wait()
+    floats[...] = raw[...].astype(jnp.float32)
+    leave.append(copy(5 + half, floats, message.at[pl.ds(cx * half, cx)]))
+    for left in leave:
+        left.wait()
 
 
 def count_kernel(dets, beta_prev, count, beta_row, *, ny, nz, half, halo):
@@ -384,12 +384,17 @@
     return jnp.sum(value.reshape(-1, 8, value.shape[1]), axis=0)
 
 
-def framed(ref, shift, own, got, edge, y, c):
+def framed_own(ref, shift, own, got, y, c):
     planes, cy, _ = own.shape
     there = pl.ds(shift, planes)
     base = HALO * y
     ref[there, pl.ds(base + cy * c, cy), :] = own[...]
     ref[there, pl.ds(base + cy * (1 - c), cy), :] = got[...]
+
+
+def framed(ref, shift, own, got, edge, y, c):
+    framed_own(ref, shift, own, got, y, c)
+    cy = own.shape[1]
     for g in range(edge.shape[0]):
         packed = edge[g]
         for j in range(GROUP):
@@ -408,39 +413,47 @@
     return (at_row >= base) & (at_row < base + count)
 
 
+def table_rows(kap_table, abs_table, shape):
+    lane = index_along(shape, 1)
+    kap_row = abs_row = jnp.zeros(shape, jnp.float32)
+    for region in range(kap_table.shape[0]):
+        kap_row = jnp.where(lane == region, kap_table[region], kap_row)
+        abs_row = jnp.where(lane == region, abs_table[region], abs_row)
+    return kap_row, abs_row
+
+
 def stencil_kernel(
-    kap_table, abs_table, mine, fields, got, edge, count,
-    diag, fx, fy, fz, sums,
-    labels, kap,
+    kap_table, abs_table, mine, fields, got, count,
+    kap, diag, fx, fy, fz, sums,
+    labels,
 ):
     _, _, y, c = places(2)
     planes, cy, lanes = mine.shape
     rows = 2 * cy + HALO
-    framed(labels, 0, fields.at[1], got.at[1], edge.at[1], y, c)
+    base = HALO * y
+    framed_own(labels, 0, fields.at[1], got.at[1], y, c)
+    labels[:, pl.ds(2 * cy * (1 - y), HALO), :] = jnp.zeros((planes, HALO, lanes), jnp.float32)
     blank_ends(kap)
-    blank = jnp.zeros((rows, lanes), jnp.float32)
-    lane = index_along((rows, lanes), 1)
-    kap_row, abs_row = blank, blank
-    for region in range(kap_table.shape[0]):
-        kap_row = jnp.where(lane == region, kap_table[region], kap_row)
-        abs_row = jnp.where(lane == region, abs_table[region], abs_row)
+    shape = (rows, lanes)
+    lane = index_along(shape, 1)
+    kap_row, abs_row = table_rows(kap_table, abs_table, shape)
+    owned = owned_rows(shape, base, 2 * cy)
 
     def look_up(i, carry):
         at = labels[i].astype(jnp.int32)
-        kap[i + 1] = jnp.take_along_axis(kap_row, at, axis=1)
+        kap[i + 1] = jnp.where(owned, jnp.take_along_axis(kap_row, at, axis=1), 0.0)
         diag[i] = jnp.take_along_axis(abs_row, at, axis=1)
         return carry
 
-    lax.fori_loop(0, planes, look_up, 0, unroll=4)
+    lax.fori_loop(0, planes, look_up, 0, unroll=UNROLL)
     fx[0] = 0.5 * kap[1]
-    base = HALO * y
 
     def set_up(i, carry):
         k = kap[i + 1]
         along_x = 0.5 * (k + kap[i + 2])
         along_y, along_z = 0.5 * (k + beyond(k, 1, 0)), 0.5 * (k + beyond(k, 1, 1))
         fx[i + 1] = along_x
-        fy[i] = jnp.where(index_along(k.shape, 0) == rows - 1, 0.0, along_y)
+        fy[i] = jnp.where(index_along(shape, 0) == rows - 1, 0.0, along_y)
         fz[i] = jnp.where(lane == lanes - 1, 0.0, along_z)
         back_y, back_z = 0.5 * (k + beyond(k, -1, 0)), 0.5 * (k + beyond(k, -1, 1))
         diag[i] = diag[i] + fx[i] + along_x + along_y + back_y + along_z + back_z
@@ -451,7 +464,43 @@
         return total, square
 
     zero = jnp.zeros((8, lanes), jnp.float32)
-    sums[0], sums[1] = lax.fori_loop(0, planes, set_up, (zero, zero), unroll=4)
+    sums[0], sums[1] = lax.fori_loop(0, planes, set_up, (zero, zero), unroll=UNROLL)
+
+
+def halo_kernel(kap_table, abs_table, edge, kap, diag_in, fx_in, fy_in, fz_in, diag, fx, fy, fz):
+    _, _, y, _ = places(2)
+    planes, rows, lanes = diag.shape
+    for ref, old in ((diag, diag_in), (fx, fx_in), (fy, fy_in), (fz, fz_in)):
+        ref[...] = old[...]
+    shape = (HALO, lanes)
+    lane, row = index_along(shape, 1), index_along(shape, 0)
+    kap_row, abs_row = table_rows(kap_table, abs_table, shape)
+    low = y == 0
+    here = pl.ds((rows - HALO) * (1 - y), HALO)
+    beside_it = pl.ds((rows - 2 * HALO) * (1 - y) + HALO * y, HALO)
+    labels = [edge_tile(edge[1, i // GROUP], i % GROUP, y).astype(jnp.int32) for i in range(planes)]
+    tiles = [jnp.take_along_axis(kap_row, at, axis=1) for at in labels]
+    none = jnp.zeros(shape, jnp.float32)
+    before = 0.5 * tiles[0]
+    fx[0, here, :] = before
+    for i, k in enumerate(tiles):
+        after = 0.5 * (k + (tiles[i + 1] if i + 1 < planes else none))
+        own = kap[i + 1, beside_it, :]
+        up, down = shifted(k, -1, 0), shifted(k, 1, 0)
+        k_up = jnp.where(row == HALO - 1, jnp.where(low, 0.0, shifted(own, -1, 0)), up)
+        k_down = jnp.where(row == 0, jnp.where(low, shifted(own, 1, 0), 0.0), down)
+        along_y, back_y = 0.5 * (k + k_up), 0.5 * (k + k_down)
+        along_z, back_z = 0.5 * (k + beyond(k, 1, 1)), 0.5 * (k + beyond(k, -1, 1))
+        fx[i + 1, here, :] = after
+        fy[i, here, :] = jnp.where(low & (row == HALO - 1), 0.0, along_y)
+        fz[i, here, :] = jnp.where(lane == lanes - 1, 0.0, along_z)
+        absorb = jnp.take_along_axis(abs_row, labels[i], axis=1)
+        diag[i, here, :] = absorb + before + after + along_y + back_y + along_z + back_z
+        before = after
+        face_up = jnp.where(low & (row == HALO - 1), 0.5 * up, 0.0)
+        face_down = jnp.where(low | (row > 0), 0.0, 0.5 * down)
+        fy[i, beside_it, :] = fy_in[i, beside_it, :] + face_up
+        diag[i, beside_it, :] = diag_in[i, beside_it, :] + face_up + face_down
 
 
 def first_kernel(
@@ -480,8 +529,8 @@
         buf_a[i + 1] = total * (1.0 / theta)
         return carry
 
-    lax.fori_loop(0, planes, set_up, 0, unroll=4)
-    found = solve(b, (buf_a, buf_b), diag, fx, fy, fz, 16)
+    lax.fori_loop(0, planes, set_up, 0, unroll=UNROLL)
+    found = solve(b, (buf_a, buf_b), diag, fx, fy, fz, UNROLL)
     owned = owned_rows((rows, lanes), HALO * y, 2 * cy)
 
     def add_up(i, carry):
@@ -491,7 +540,7 @@
         return carry[0] + folded(part), carry[1] + folded(part * phi[i + 1])
 
     zero = jnp.zeros((8, lanes), jnp.float32)
-    seen, cross = lax.fori_loop(0, planes, add_up, (zero, zero), unroll=4)
+    seen, cross = lax.fori_loop(0, planes, add_up, (zero, zero), unroll=UNROLL)
     first = (2 * cy - HALO) * (1 - y) + HALO * y
     for g, part in enumerate((sums[0], seen, cross, sums[1])):
         message[g, pl.ds(0, GROUP * REACH), :] = packed_edges(
@@ -532,13 +581,13 @@
         buf_a[i + 1] = value * (1.0 / theta)
         return carry
 
-    lax.fori_loop(0, planes, set_up, 0, unroll=4)
+    lax.fori_loop(0, planes, set_up, 0, unroll=UNROLL)
     for i in range(planes):
         u = edge_tile(came[i // GROUP], i % GROUP, y)
         value = weighted(count[i, edge, :], u, phi[i + 1, edge, :])
         b[i, edge, :] = value
         buf_a[i + 1, edge, :] = value * (1.0 / theta)
-    dual = solve(b, (buf_a, buf_b), diag, fx, fy, fz, 16)
+    dual = solve(b, (buf_a, buf_b), diag, fx, fy, fz, UNROLL)
 
     def product(i, carry):
         p, u = phi[i + 1], dual[i + 1]
@@ -555,7 +604,7 @@
             message[f, i] = ref[i, pl.ds(base + cy * (1 - c), cy), :]
         return carry
 
-    lax.fori_loop(0, planes, product, 0, unroll=4)
+    lax.fori_loop(0, planes, product, 0, unroll=UNROLL)
 
 
 def packed_slabs(own, came, half, choices, outs):
@@ -650,7 +699,7 @@
     return jax.ShapeDtypeStruct(shape, jnp.float32)
 
 
-def run(kernel, outs, *args, after=(), scratch=(), copies=0, smem=(), hbm=(), mib=16, in_smem_out=(), cost=None):
+def run(kernel, outs, *args, after=(), scratch=(), copies=0, smem=(), hbm=(), mib=16, in_smem_out=(), hbm_out=False, cost=None):
     vmem = pl.BlockSpec(memory_space=pltpu.VMEM)
     scalar = pl.BlockSpec(memory_space=pltpu.SMEM)
     far = pl.BlockSpec(memory_space=pltpu.HBM)
@@ -667,7 +716,7 @@
         body if waits else kernel,
         out_shape=tuple(outs),
         in_specs=[scalar if i in smem else far if i in hbm else vmem for i in range(len(args))],
-        out_specs=tuple(scalar if i in in_smem_out else vmem for i in range(len(outs))),
+        out_specs=tuple(scalar if i in in_smem_out else far if hbm_out else vmem for i in range(len(outs))),
         scratch_shapes=held,
         compiler_params=pltpu.CompilerParams(vmem_limit_bytes=mib * 2**20),
         cost_estimate=cost,
@@ -675,6 +724,7 @@
 
 
 HALO = 8
+UNROLL = 16
 REACH = 6
 GROUP = 4
 
@@ -706,7 +756,8 @@
     packed, message = run(
         pack_kernel, (f32(2 * groups, cy, cz), f32((sources // 2 + 1) * cx + 2 * groups, cy, cz)),
         background, labels, v_kappa, v_absorb, hbm=(0, 1, 2, 3),
-        scratch=(raw_labels, float_block(2, *v_kappa.shape)), copies=3 + sources // 2, mib=60,
+        scratch=(raw_labels, float_block(2, *v_kappa.shape), float_block(2 * groups, cy, cz), float_block(*block)),
+        copies=6 + sources // 2, hbm_out=True, mib=60,
     )
     long = pl.CostEstimate(flops=10**9, bytes_accessed=2**26, transcendentals=0)
     came = swap_x(message)
@@ -738,11 +789,14 @@
     (vector_sent,) = run(vector_edge_kernel, edge, vector, vector_got, after=(sent,))
     frame, wide = (planes, rows, cz), (planes + 2, rows, cz)
     float_frame, float_wide = float_block(*frame), float_block(*wide)
-    diag, fx, fy, fz, sums = run(
-        stencil_kernel,
-        (f32(*frame), f32(planes + 1, rows, cz), f32(*frame), f32(*frame), f32(2, 8, cz)),
-        kappa_table, absorb_table, mine, fields, got, photon_edge, count, after=(vector_sent,), cost=long,
-        smem=(0, 1), scratch=(float_frame, float_wide),
+    coefs = (f32(*frame), f32(planes + 1, rows, cz), f32(*frame), f32(*frame))
+    kap, *partial, sums = run(
+        stencil_kernel, (f32(*wide), *coefs, f32(2, 8, cz)),
+        kappa_table, absorb_table, mine, fields, got, count, after=(vector_sent,), cost=long,
+        smem=(0, 1), scratch=(float_frame,),
+    )
+    diag, fx, fy, fz = run(
+        halo_kernel, coefs, kappa_table, absorb_table, photon_edge, kap, *partial, smem=(0, 1)
     )
     phi, change, sent = run(
         first_kernel, (f32(*wide), f32(*frame), f32(4, GROUP * REACH + 8, cz)),

time: 73 us -> 80.4 us (1.10)
  Pallas kernels: 18.6 us -> 27.2 us
  waiting for transfers between devices: 18.1 us -> 17 us
    pallas_call x23 -> x24, Pallas kernels: 18.6 us -> 27.2 us  [run(): pl.pallas_call(body if waits else kernel, out_shape=tuple(outs), in_specs...]
    ppermute x3, waiting for transfers between devices: 4.96 us -> 3.83 us  [across_y(): return lax.ppermute(value, 'gy', [(i, (i + 2) % 4) for i in range(4)])]
  transfers between devices with their start and end apart: 18 -> 18, of which waited for: 12 -> 13; matrix products, arithmetic and copies ran while one was open for 0% -> 0% of each run, Pallas kernels for 9% -> 9%
where the time goes in v11:
time: 80.4 us; the launch traced here: 80.2 us
  Pallas kernels  27.2 us (34%)
  starting transfers between devices  22 us (27%)
  waiting for transfers between devices  17 us (21%)
  blocking collectives  12.4 us (15%)
  between operations  1.59 us (2%)
    pallas_call x24, Pallas kernels, run(): pl.pallas_call(body if waits else kernel, out_shape=tuple(outs), in_specs...  27.2 us
    all_to_all x1, blocking collectives, per_device_paired(): lax.all_to_all(jnp.broadcast_to(tile, (8 * n, 8, 128)), everyone, 0, 0)  12.4 us
    ppermute x6, starting transfers between devices, along_z(): return lax.ppermute(value, 'src', [(i, i ^ k) for i in range(n)])  9.3 us
    ppermute x6, starting transfers between devices, swap_x(): return lax.ppermute(value, 'gx', [(0, 1), (1, 0)])  7.76 us
    ppermute x6, waiting for transfers between devices, along_z(): return lax.ppermute(value, 'src', [(i, i ^ k) for i in range(n)])  6.25 us
    ppermute x6, waiting for transfers between devices, swap_x(): return lax.ppermute(value, 'gx', [(0, 1), (1, 0)])  4.81 us
    ppermute x3, starting transfers between devices, across_y(): return lax.ppermute(value, 'gy', [(i, (i + 2) % 4) for i in range(4)])  4.75 us
    ppermute x3, waiting for transfers between devices, across_y(): return lax.ppermute(value, 'gy', [(i, (i + 2) % 4) for i in range(4)])  3.83 us
  transfers between devices with their start and end apart: 18, of which 13 were waited for; matrix products, arithmetic and copies ran while one was open for 0% of the time, Pallas kernels for 9%

profile of v11, /device:TPU:0, one launch (start us, length us, event | category | flops | bytes accessed | tf_op | source)
XLA Modules:
  0.0 80.2 jit_solution(16091102809141023461)
XLA Ops:
  0.6 9.1 %shard_map.122 = (f32[4,32,128]{2,1,0:T(8,128)}, f32[28,32,128]{2,1,0:T(8,128)}) custom-call(f32[4,8,32,128]{3,2,1,0:T(8,128)} %refs_0_.2, s32[8,32,128]{2,1,0:T(8,128)} %refs_1_.2, f32[8,32,32]{2,1,0:T(8,128)} %vk.5, f32[8,32,32]{2,1,0:T(8,128)} %va.5), custom_call_target="tpu_custom_call" | custom-call | tf_op jit(solution)/shard_map/pallas_call | solution.py:715
  9.8 3.0 %collective-permute-start = (f32[28,32,128]{2,1,0:T(8,128)}, f32[28,32,128]{2,1,0:T(8,128)S(1)}, u32[]{:S(2)}, u32[]{:S(2)}) collective-permute-start(f32[28,32,128]{2,1,0:T(8,128)} %get-tuple-element.28), channel_id=1, source_target_pairs={{0,4},{4,0},{1,5},{5,1},{2,6},{6,2},{3,7},{7,3},{8,12},{12,8},{9,1... | collective-permute-start | bytes 1376264 | tf_op jit(solution)/shard_map/ppermute | solution.py:745
  12.8 3.6 %collective-permute-start.3 = (f32[4,32,128]{2,1,0:T(8,128)}, f32[4,32,128]{2,1,0:T(8,128)S(1)}, u32[]{:S(2)}, u32[]{:S(2)}) collective-permute-start(f32[4,32,128]{2,1,0:T(8,128)} %get-tuple-element.29), channel_id=1, source_target_pairs={{0,24},{8,16},{16,8},{24,0},{1,25},{9,17},{17,9},{25,1},{2,26},{10... | collective-permute-start | bytes 196616 | tf_op jit(solution)/shard_map/ppermute | solution.py:751
  17.8 2.1 %shard_map.121 = (f32[16,72,128]{2,1,0:T(8,128)S(1)}, f32[1,128]{1,0:T(1,128)S(1)}) custom-call(s32[1,1024]{1,0:T(1,128)S(1)} %bitcast.1, f32[1]{0:T(128)S(6)} %copy.13.beta_prev), custom_call_target="tpu_custom_call" | custom-call | flops 301989888 | bytes 589824 | tf_op jit(solution)/shard_map/pallas_call | solution.py:715
  20.0 2.0 %collective-permute-done.2.refs_1_ = f32[4,32,128]{2,1,0:T(8,128)S(1)} collective-permute-done((f32[4,32,128]{2,1,0:T(8,128)}, f32[4,32,128]{2,1,0:T(8,128)S(1)}, u32[]{:S(2)}, u32[]{:S(2)}) %collective-permute-start.2) | collective-permute-done | bytes 65568 | tf_op jit(solution)/shard_map/ppermute | solution.py:751
  22.6 0.9 %collective-permute-done.refs_2_.refs_1_ = f32[28,32,128]{2,1,0:T(8,128)S(1)} collective-permute-done((f32[28,32,128]{2,1,0:T(8,128)}, f32[28,32,128]{2,1,0:T(8,128)S(1)}, u32[]{:S(2)}, u32[]{:S(2)}) %collective-permute-start) | collective-permute-done | bytes 458784 | tf_op jit(solution)/shard_map/ppermute | solution.py:745
  24.6 3.7 %collective-permute-done.5.refs_2_ = f32[12,32,128]{2,1,0:T(8,128)S(1)} collective-permute-done((f32[12,32,128]{2,1,0:T(8,128)S(1)}, f32[12,32,128]{2,1,0:T(8,128)S(1)}, u32[]{:S(2)}, u32[]{:S(2)}) %collective-permute-start.5) | collective-permute-done | bytes 196640 | tf_op jit(solution)/shard_map/ppermute | solution.py:745
  28.9 1.6 %collective-permute-start.6 = (f32[2,4,24,128]{3,2,1,0:T(8,128)S(1)}, f32[2,4,24,128]{3,2,1,0:T(8,128)S(1)}, u32[]{:S(2)}, u32[]{:S(2)}) collective-permute-start(f32[2,4,24,128]{3,2,1,0:T(8,128)S(1)} %shard_map.127.refs_2_), channel_id=1, source_target_pairs={{0,2},{1,3},{2,0},{3,1},{4,6},{5,7},{6,4},{7,5},{8,10},{9,11},{10,... | collective-permute-start | bytes 294920 | tf_op jit(solution)/shard_map/ppermute | solution.py:772
  30.7 1.6 %collective-permute-start.8 = (f32[2,4,24,128]{3,2,1,0:T(8,128)S(1)}, f32[2,4,24,128]{3,2,1,0:T(8,128)S(1)}, u32[]{:S(2)}, u32[]{:S(2)}) collective-permute-start(f32[2,4,24,128]{3,2,1,0:T(8,128)S(1)} %shard_map.128.refs_6_), channel_id=1, source_target_pairs={{0,2},{1,3},{2,0},{3,1},{4,6},{5,7},{6,4},{7,5},{8,10},{9,11},{10,... | collective-permute-start | bytes 294920 | tf_op jit(solution)/shard_map/ppermute | solution.py:772
  32.3 2.0 %shard_map.129 = (f32[18,72,128]{2,1,0:T(8,128)S(1)}, f32[16,72,128]{2,1,0:T(8,128)S(1)}, f32[17,72,128]{2,1,0:T(8,128)S(1)}, f32[16,72,128]{2,1,0:T(8,128)S(1)}...) custom-call(f32[16]{0:T(128)S(1)} %copy-done.6, f32[16]{0:T(128)S(1)} %copy-done.7, ...), custom_call_target="tpu_custom_call" | custom-call | flops 1000000000 | bytes 67108864 | tf_op jit(solution)/shard_map/pallas_call | solution.py:715
  36.2 4.6 %shard_map.131 = (f32[18,72,128]{2,1,0:T(8,128)S(1)}, f32[16,72,128]{2,1,0:T(8,128)S(1)}, f32[4,32,128]{2,1,0:T(8,128)S(1)}) custom-call(f32[16,72,128]{2,1,0:T(8,128)S(1)} %get-tuple-element.38.diag, f32[17,72,128]{2,1,0:T(8,128)S(1)} %get-tuple-element.39.fx, f32[16,72,128]{2,1,0:T(8,128)S(1)} %get-tuple-element.40.fy, ...), custom_call_target="tpu_custom_call" | custom-call | tf_op jit(solution)/shard_map/pallas_call | solution.py:715
  40.8 1.6 %collective-permute-start.9 = (f32[4,32,128]{2,1,0:T(8,128)S(1)}, f32[4,32,128]{2,1,0:T(8,128)S(1)}, u32[]{:S(2)}, u32[]{:S(2)}) collective-permute-start(f32[4,32,128]{2,1,0:T(8,128)S(1)} %get-tuple-element.45.sent), channel_id=1, source_target_pairs={{0,2},{1,3},{2,0},{3,1},{4,6},{5,7},{6,4},{7,5},{8,10},{9,11},{10,... | collective-permute-start | bytes 196616 | tf_op jit(solution)/shard_map/ppermute | solution.py:772
  42.4 2.7 %collective-permute-done.9.came = f32[4,32,128]{2,1,0:T(8,128)S(1)} collective-permute-done((f32[4,32,128]{2,1,0:T(8,128)S(1)}, f32[4,32,128]{2,1,0:T(8,128)S(1)}, u32[]{:S(2)}, u32[]{:S(2)}) %collective-permute-start.9) | collective-permute-done | bytes 65568 | tf_op jit(solution)/shard_map/ppermute | solution.py:772
  45.1 4.7 %shard_map.132 = (f32[2,16,32,128]{3,2,1,0:T(8,128)S(1)}, f32[2,16,32,128]{3,2,1,0:T(8,128)S(1)}) custom-call(f32[18,72,128]{2,1,0:T(8,128)S(1)} %get-tuple-element.43.phi, f32[16,72,128]{2,1,0:T(8,128)S(1)} %get-tuple-element.44.change, f32[16,72,128]{2,1,0:T(8,128)S(1)} %get-tuple-element.38.diag, f32[17,72,128]{2,1,0:T(8,128)S(1)} %get-tuple-element.39.fx, ...), custom_call_target="tpu_custom_call" | custom-call | tf_op jit(solution)/shard_map/pallas_call | solution.py:715
  49.9 1.9 %collective-permute-done.10.came.refs_1_ = f32[2,16,32,128]{3,2,1,0:T(8,128)S(1)} collective-permute-done((f32[2,16,32,128]{3,2,1,0:T(8,128)S(1)}, f32[2,16,32,128]{3,2,1,0:T(8,128)S(1)}, u32[]{:S(2)}, u32[]{:S(2)}) %collective-permute-start.10) | collective-permute-done | bytes 524320 | tf_op jit(solution)/shard_map/ppermute | solution.py:748
  52.1 1.2 %collective-permute-start.11 = (f32[1,2,2,32,128]{4,3,2,1,0:T(8,128)S(1)}, f32[1,2,2,32,128]{4,3,2,1,0:T(8,128)S(1)}, u32[]{:S(2)}, u32[]{:S(2)}) collective-permute-start(f32[1,2,2,32,128]{4,3,2,1,0:T(8,128)S(1)} %shard_map.134.refs_2_), channel_id=1, source_target_pairs={{0,4},{4,0},{1,5},{5,1},{2,6},{6,2},{3,7},{7,3},{8,12},{12,8},{9,1... | collective-permute-start | bytes 196616 | tf_op jit(solution)/shard_map/ppermute | solution.py:745
  54.3 1.2 %collective-permute-start.16 = (f32[1,2,2,32,128]{4,3,2,1,0:T(8,128)S(1)}, f32[1,2,2,32,128]{4,3,2,1,0:T(8,128)S(1)}, u32[]{:S(2)}, u32[]{:S(2)}) collective-permute-start(f32[1,2,2,32,128]{4,3,2,1,0:T(8,128)S(1)} %shard_map.135.refs_2_), channel_id=1, source_target_pairs={{0,4},{4,0},{1,5},{5,1},{2,6},{6,2},{3,7},{7,3},{8,12},{12,8},{9,1... | collective-permute-start | bytes 196616 | tf_op jit(solution)/shard_map/ppermute | solution.py:745
  55.6 1.0 %collective-permute-start.15 = (f32[1,2,2,32,128]{4,3,2,1,0:T(8,128)S(1)}, f32[1,2,2,32,128]{4,3,2,1,0:T(8,128)S(1)}, u32[]{:S(2)}, u32[]{:S(2)}) collective-permute-start(f32[1,2,2,32,128]{4,3,2,1,0:T(8,128)S(1)} %shard_map.136.refs_2_), channel_id=1, source_target_pairs={{0,4},{4,0},{1,5},{5,1},{2,6},{6,2},{3,7},{7,3},{8,12},{12,8},{9,1... | collective-permute-start | bytes 196616 | tf_op jit(solution)/shard_map/ppermute | solution.py:745
  57.1 2.2 %collective-permute-start.12 = (f32[2,2,32,128]{3,2,1,0:T(8,128)S(1)}, f32[2,2,32,128]{3,2,1,0:T(8,128)S(1)}, u32[]{:S(2)}, u32[]{:S(2)}) collective-permute-start(f32[2,2,32,128]{3,2,1,0:T(8,128)S(1)} %shard_map.138), channel_id=1, source_target_pairs={{0,16},{8,24},{16,0},{24,8},{1,17},{9,25},{17,1},{25,9},{2,18},{10... | collective-permute-start | bytes 196616 | tf_op jit(solution)/shard_map/ppermute | solution.py:751
  59.3 2.7 %collective-permute-start.14 = (f32[2,2,32,128]{3,2,1,0:T(8,128)S(1)}, f32[2,2,32,128]{3,2,1,0:T(8,128)S(1)}, u32[]{:S(2)}, u32[]{:S(2)}) collective-permute-start(f32[2,2,32,128]{3,2,1,0:T(8,128)S(1)} %shard_map.139), channel_id=1, source_target_pairs={{0,24},{8,16},{16,8},{24,0},{1,25},{9,17},{17,9},{25,1},{2,26},{10... | collective-permute-start | bytes 196616 | tf_op jit(solution)/shard_map/ppermute | solution.py:751
  62.1 2.3 %collective-permute-done.12.refs_0_ = f32[2,2,32,128]{3,2,1,0:T(8,128)S(1)} collective-permute-done((f32[2,2,32,128]{3,2,1,0:T(8,128)S(1)}, f32[2,2,32,128]{3,2,1,0:T(8,128)S(1)}, u32[]{:S(2)}, u32[]{:S(2)}) %collective-permute-start.12) | collective-permute-done | bytes 65568 | tf_op jit(solution)/shard_map/ppermute | solution.py:751
  64.4 1.2 %collective-permute-done.14.refs_1_ = f32[2,2,32,128]{3,2,1,0:T(8,128)S(1)} collective-permute-done((f32[2,2,32,128]{3,2,1,0:T(8,128)S(1)}, f32[2,2,32,128]{3,2,1,0:T(8,128)S(1)}, u32[]{:S(2)}, u32[]{:S(2)}) %collective-permute-start.14) | collective-permute-done | bytes 65568 | tf_op jit(solution)/shard_map/ppermute | solution.py:751
  66.9 12.4 %all_to_all.5.tiles = f32[32,8,128]{2,1,0:T(8,128)S(1)} all-to-all(f32[32,8,128]{2,1,0:T(8,128)S(1)} %broadcast_in_dim.3), channel_id=1, replica_groups=mesh['src'=4,'gx'=2,'gy'=4] {'src','gx','gy'}, dimensions={0} | all-to-all | bytes 262144 | tf_op jit(solution)/shard_map/all_to_all | solution.py:833
  79.2 1.0 %shard_map.144 = (f32[8,32,32]{2,1,0:T(8,128)}, f32[8,32,32]{2,1,0:T(8,128)}, f32[2]{0:T(128)}) custom-call(f32[32,8,128]{2,1,0:T(8,128)S(1)} %all_to_all.5.tiles, f32[8,32,32]{2,1,0:T(8,128)S(1)} %get-tuple-element.49.w_k, f32[8,32,32]{2,1,0:T(8,128)S(1)} %get-tuple-element.50.w_a, f32[8,32,32]{2,1,0:T(8,128)S(1)} %copy-done, f32[8,32,32]{2,1,0:T(8,128)S(1)} %copy-done.1), custom_call_target="tpu_custom_call" | custom-call | tf_op jit(solution)/shard_map/pallas_call | solution.py:715
  (56 shorter events, 8.5 us)
Async XLA Ops:
  9.8 8.1 %copy-start.8 = (s32[1024]{0:T(1024)S(1)}, s32[1024]{0:T(1024)}, u32[]{:S(2)}) copy-start(s32[1024]{0:T(1024)} %param.14) | copy-start | bytes 12292
  9.8 13.7 %collective-permute-start = (f32[28,32,128]{2,1,0:T(8,128)}, f32[28,32,128]{2,1,0:T(8,128)S(1)}, u32[]{:S(2)}, u32[]{:S(2)}) collective-permute-start(f32[28,32,128]{2,1,0:T(8,128)} %get-tuple-element.28), channel_id=1, source_target_pairs={{0,4},{4,0},{1,5},{5,1},{2,6},{6,2},{3,7},{7,3},{8,12},{12,8},{9,1... | collective-permute-start | bytes 1376264 | tf_op jit(solution)/shard_map/ppermute | solution.py:745
  12.8 7.2 %collective-permute-start.3 = (f32[4,32,128]{2,1,0:T(8,128)}, f32[4,32,128]{2,1,0:T(8,128)S(1)}, u32[]{:S(2)}, u32[]{:S(2)}) collective-permute-start(f32[4,32,128]{2,1,0:T(8,128)} %get-tuple-element.29), channel_id=1, source_target_pairs={{0,24},{8,16},{16,8},{24,0},{1,25},{9,17},{17,9},{25,1},{2,26},{10... | collective-permute-start | bytes 196616 | tf_op jit(solution)/shard_map/ppermute | solution.py:751
  16.4 5.6 %collective-permute-start.2 = (f32[4,32,128]{2,1,0:T(8,128)}, f32[4,32,128]{2,1,0:T(8,128)S(1)}, u32[]{:S(2)}, u32[]{:S(2)}) collective-permute-start(f32[4,32,128]{2,1,0:T(8,128)} %get-tuple-element.29), channel_id=1, source_target_pairs={{0,16},{8,24},{16,0},{24,8},{1,17},{9,25},{17,1},{25,9},{2,18},{10... | collective-permute-start | bytes 196616 | tf_op jit(solution)/shard_map/ppermute | solution.py:751
  16.4 5.6 %collective-permute-start.1 = (f32[4,32,128]{2,1,0:T(8,128)}, f32[4,32,128]{2,1,0:T(8,128)S(1)}, u32[]{:S(2)}, u32[]{:S(2)}) collective-permute-start(f32[4,32,128]{2,1,0:T(8,128)} %get-tuple-element.29), channel_id=1, source_target_pairs={{0,8},{8,0},{16,24},{24,16},{1,9},{9,1},{17,25},{25,17},{2,10},{10... | collective-permute-start | bytes 196616 | tf_op jit(solution)/shard_map/ppermute | solution.py:751
  19.9 3.6 %copy-start.2 = (f32[4,8,32,128]{3,2,1,0:T(8,128)S(1)}, f32[4,8,32,128]{3,2,1,0:T(8,128)}, u32[]{:S(2)}) copy-start(f32[4,8,32,128]{3,2,1,0:T(8,128)} %refs_0_.2) | copy-start | bytes 1572868
  22.1 6.3 %collective-permute-start.5 = (f32[12,32,128]{2,1,0:T(8,128)S(1)}, f32[12,32,128]{2,1,0:T(8,128)S(1)}, u32[]{:S(2)}, u32[]{:S(2)}) collective-permute-start(f32[12,32,128]{2,1,0:T(8,128)S(1)} %shard_map.123.refs_3_.joined), channel_id=1, source_target_pairs={{0,4},{4,0},{1,5},{5,1},{2,6},{6,2},{3,7},{7,3},{8,12},{12,8},{9,1... | collective-permute-start | bytes 589832 | tf_op jit(solution)/shard_map/ppermute | solution.py:745
  24.1 4.7 %collective-permute-start.4 = (f32[2,16,32,128]{3,2,1,0:T(8,128)S(1)}, f32[2,16,32,128]{3,2,1,0:T(8,128)S(1)}, u32[]{:S(2)}, u32[]{:S(2)}) collective-permute-start(f32[2,16,32,128]{3,2,1,0:T(8,128)S(1)} %get-tuple-element.32.refs_1_.refs_3_), channel_id=1, source_target_pairs={{0,1},{1,0},{2,3},{3,2},{4,5},{5,4},{6,7},{7,6},{8,9},{9,8},{10,11... | collective-permute-start | bytes 1572872 | tf_op jit(solution)/shard_map/ppermute | solution.py:748
  28.7 2.0 %collective-permute-start.7 = (f32[2,16,32,128]{3,2,1,0:T(8,128)S(1)}, f32[2,16,32,128]{3,2,1,0:T(8,128)S(1)}, u32[]{:S(2)}, u32[]{:S(2)}) collective-permute-start(f32[2,16,32,128]{3,2,1,0:T(8,128)S(1)} %shard_map.126.refs_3_.refs_0_.vector), channel_id=1, source_target_pairs={{0,1},{1,0},{2,3},{3,2},{4,5},{5,4},{6,7},{7,6},{8,9},{9,8},{10,11... | collective-permute-start | bytes 1572872 | tf_op jit(solution)/shard_map/ppermute | solution.py:748
  28.8 3.5 %copy-start.6 = (f32[16]{0:T(128)S(1)}, f32[16]{0:T(128)}, u32[]{:S(2)}) copy-start(f32[16]{0:T(128)} %kap_table.1) | copy-start | bytes 196
  28.9 3.4 %copy-start.7 = (f32[16]{0:T(128)S(1)}, f32[16]{0:T(128)}, u32[]{:S(2)}) copy-start(f32[16]{0:T(128)} %abs_table.1) | copy-start | bytes 196
  28.9 5.7 %collective-permute-start.6 = (f32[2,4,24,128]{3,2,1,0:T(8,128)S(1)}, f32[2,4,24,128]{3,2,1,0:T(8,128)S(1)}, u32[]{:S(2)}, u32[]{:S(2)}) collective-permute-start(f32[2,4,24,128]{3,2,1,0:T(8,128)S(1)} %shard_map.127.refs_2_), channel_id=1, source_target_pairs={{0,2},{1,3},{2,0},{3,1},{4,6},{5,7},{6,4},{7,5},{8,10},{9,11},{10,... | collective-permute-start | bytes 294920 | tf_op jit(solution)/shard_map/ppermute | solution.py:772
  30.7 5.5 %collective-permute-start.8 = (f32[2,4,24,128]{3,2,1,0:T(8,128)S(1)}, f32[2,4,24,128]{3,2,1,0:T(8,128)S(1)}, u32[]{:S(2)}, u32[]{:S(2)}) collective-permute-start(f32[2,4,24,128]{3,2,1,0:T(8,128)S(1)} %shard_map.128.refs_6_), channel_id=1, source_target_pairs={{0,2},{1,3},{2,0},{3,1},{4,6},{5,7},{6,4},{7,5},{8,10},{9,11},{10,... | collective-permute-start | bytes 294920 | tf_op jit(solution)/shard_map/ppermute | solution.py:772
  40.8 4.3 %collective-permute-start.9 = (f32[4,32,128]{2,1,0:T(8,128)S(1)}, f32[4,32,128]{2,1,0:T(8,128)S(1)}, u32[]{:S(2)}, u32[]{:S(2)}) collective-permute-start(f32[4,32,128]{2,1,0:T(8,128)S(1)} %get-tuple-element.45.sent), channel_id=1, source_target_pairs={{0,2},{1,3},{2,0},{3,1},{4,6},{5,7},{6,4},{7,5},{8,10},{9,11},{10,... | collective-permute-start | bytes 196616 | tf_op jit(solution)/shard_map/ppermute | solution.py:772
  49.8 2.0 %collective-permute-start.10 = (f32[2,16,32,128]{3,2,1,0:T(8,128)S(1)}, f32[2,16,32,128]{3,2,1,0:T(8,128)S(1)}, u32[]{:S(2)}, u32[]{:S(2)}) collective-permute-start(f32[2,16,32,128]{3,2,1,0:T(8,128)S(1)} %get-tuple-element.47), channel_id=1, source_target_pairs={{0,1},{1,0},{2,3},{3,2},{4,5},{5,4},{6,7},{7,6},{8,9},{9,8},{10,11... | collective-permute-start | bytes 1572872 | tf_op jit(solution)/shard_map/ppermute | solution.py:748
  52.1 5.0 %collective-permute-start.11 = (f32[1,2,2,32,128]{4,3,2,1,0:T(8,128)S(1)}, f32[1,2,2,32,128]{4,3,2,1,0:T(8,128)S(1)}, u32[]{:S(2)}, u32[]{:S(2)}) collective-permute-start(f32[1,2,2,32,128]{4,3,2,1,0:T(8,128)S(1)} %shard_map.134.refs_2_), channel_id=1, source_target_pairs={{0,4},{4,0},{1,5},{5,1},{2,6},{6,2},{3,7},{7,3},{8,12},{12,8},{9,1... | collective-permute-start | bytes 196616 | tf_op jit(solution)/shard_map/ppermute | solution.py:745
  53.3 6.0 %collective-permute-start.13 = (f32[1,2,2,32,128]{4,3,2,1,0:T(8,128)S(1)}, f32[1,2,2,32,128]{4,3,2,1,0:T(8,128)S(1)}, u32[]{:S(2)}, u32[]{:S(2)}) collective-permute-start(f32[1,2,2,32,128]{4,3,2,1,0:T(8,128)S(1)} %shard_map.133.refs_2_), channel_id=1, source_target_pairs={{0,4},{4,0},{1,5},{5,1},{2,6},{6,2},{3,7},{7,3},{8,12},{12,8},{9,1... | collective-permute-start | bytes 196616 | tf_op jit(solution)/shard_map/ppermute | solution.py:745
  54.3 7.7 %collective-permute-start.16 = (f32[1,2,2,32,128]{4,3,2,1,0:T(8,128)S(1)}, f32[1,2,2,32,128]{4,3,2,1,0:T(8,128)S(1)}, u32[]{:S(2)}, u32[]{:S(2)}) collective-permute-start(f32[1,2,2,32,128]{4,3,2,1,0:T(8,128)S(1)} %shard_map.135.refs_2_), channel_id=1, source_target_pairs={{0,4},{4,0},{1,5},{5,1},{2,6},{6,2},{3,7},{7,3},{8,12},{12,8},{9,1... | collective-permute-start | bytes 196616 | tf_op jit(solution)/shard_map/ppermute | solution.py:745
  55.6 6.4 %collective-permute-start.15 = (f32[1,2,2,32,128]{4,3,2,1,0:T(8,128)S(1)}, f32[1,2,2,32,128]{4,3,2,1,0:T(8,128)S(1)}, u32[]{:S(2)}, u32[]{:S(2)}) collective-permute-start(f32[1,2,2,32,128]{4,3,2,1,0:T(8,128)S(1)} %shard_map.136.refs_2_), channel_id=1, source_target_pairs={{0,4},{4,0},{1,5},{5,1},{2,6},{6,2},{3,7},{7,3},{8,12},{12,8},{9,1... | collective-permute-start | bytes 196616 | tf_op jit(solution)/shard_map/ppermute | solution.py:745
  57.1 7.3 %collective-permute-start.12 = (f32[2,2,32,128]{3,2,1,0:T(8,128)S(1)}, f32[2,2,32,128]{3,2,1,0:T(8,128)S(1)}, u32[]{:S(2)}, u32[]{:S(2)}) collective-permute-start(f32[2,2,32,128]{3,2,1,0:T(8,128)S(1)} %shard_map.138), channel_id=1, source_target_pairs={{0,16},{8,24},{16,0},{24,8},{1,17},{9,25},{17,1},{25,9},{2,18},{10... | collective-permute-start | bytes 196616 | tf_op jit(solution)/shard_map/ppermute | solution.py:751
  59.3 6.2 %collective-permute-start.14 = (f32[2,2,32,128]{3,2,1,0:T(8,128)S(1)}, f32[2,2,32,128]{3,2,1,0:T(8,128)S(1)}, u32[]{:S(2)}, u32[]{:S(2)}) collective-permute-start(f32[2,2,32,128]{3,2,1,0:T(8,128)S(1)} %shard_map.139), channel_id=1, source_target_pairs={{0,24},{8,16},{16,8},{24,0},{1,25},{9,17},{17,9},{25,1},{2,26},{10... | collective-permute-start | bytes 196616 | tf_op jit(solution)/shard_map/ppermute | solution.py:751
  62.0 4.3 %collective-permute-start.17 = (f32[2,2,32,128]{3,2,1,0:T(8,128)S(1)}, f32[2,2,32,128]{3,2,1,0:T(8,128)S(1)}, u32[]{:S(2)}, u32[]{:S(2)}) collective-permute-start(f32[2,2,32,128]{3,2,1,0:T(8,128)S(1)} %shard_map.142), channel_id=1, source_target_pairs={{0,8},{8,0},{16,24},{24,16},{1,9},{9,1},{17,25},{25,17},{2,10},{10... | collective-permute-start | bytes 196616 | tf_op jit(solution)/shard_map/ppermute | solution.py:751
  62.1 4.2 %copy-start.4 = (f32[8,32,32]{2,1,0:T(8,128)S(1)}, f32[8,32,32]{2,1,0:T(8,128)}, u32[]{:S(2)}) copy-start(f32[8,32,32]{2,1,0:T(8,128)} %refs_6_.1) | copy-start | bytes 98308
  62.1 4.2 %copy-start.5 = (f32[8,32,32]{2,1,0:T(8,128)S(1)}, f32[8,32,32]{2,1,0:T(8,128)}, u32[]{:S(2)}) copy-start(f32[8,32,32]{2,1,0:T(8,128)} %refs_7_.1) | copy-start | bytes 98308
  (3 other events, 5.8 us)

commit v12 on v11

--- a/solution.py
+++ b/solution.py
@@ -190,32 +190,32 @@
     return jnp.concatenate([ref[per * q + j] for j in range(per)], axis=1)
 
 
-def pack_kernel(bg, labels, vk, va, packed, message, raw, v_in, slabs, floats, sems):
+def pack_kernel(bg, labels, vk, va, packed, message, raw, v_in, sems):
     _, x, _, _ = places(2)
     half = bg.shape[0] // 2
     cx = labels.shape[0]
-    size = slabs.shape[0]
-
-    def copy(i, src, dst):
-        started = pltpu.make_async_copy(src, dst, sems.at[i])
-        started.start()
-        return started
-
-    arrive = [copy(i, src, dst) for i, (src, dst) in enumerate(((vk, v_in.at[0]), (va, v_in.at[1]), (labels, raw)))]
-    leave = [
-        copy(3 + i, bg.at[half * (1 - x) + i], message.at[pl.ds(cx * i, cx)]) for i in range(half)
+    copies = [
+        pltpu.make_async_copy(src, dst, sems.at[i])
+        for i, (src, dst) in enumerate((
+            (vk, v_in.at[0]),
+            (va, v_in.at[1]),
+            (labels, raw),
+            *((bg.at[half * (1 - x) + i], message.at[pl.ds(cx * i, cx)]) for i in range(half)),
+        ))
     ]
+    for copy in copies:
+        copy.start()
+    groups = packed.shape[0] // 2
     for f in range(2):
-        arrive[f].wait()
-        for q in range(size // 2):
-            slabs[size // 2 * f + q] = packed_planes(v_in.at[f], q)
-    leave.append(copy(3 + half, slabs, packed))
-    leave.append(copy(4 + half, slabs, message.at[pl.ds(cx * (half + 1), size)]))
-    arrive[2].wait()
-    floats[...] = raw[...].astype(jnp.float32)
-    leave.append(copy(5 + half, floats, message.at[pl.ds(cx * half, cx)]))
-    for left in leave:
-        left.wait()
+        copies[f].wait()
+        for q in range(groups):
+            planes = packed_planes(v_in.at[f], q)
+            packed[groups * f + q] = planes
+            message[cx * (half + 1) + groups * f + q] = planes
+    copies[2].wait()
+    message[pl.ds(cx * half, cx)] = raw[...].astype(jnp.float32)
+    for copy in copies[3:]:
+        copy.wait()
 
 
 def count_kernel(dets, beta_prev, count, beta_row, *, ny, nz, half, halo):
@@ -288,8 +288,8 @@
         joined[pl.ds(size * i, size)] = ref[...]
 
 
-def own_half_kernel(vk, va, joined, half):
-    s, _, _, _ = places(2)
+def own_half_kernel(vk, va, joined, bg, labels, half, straight, across):
+    s, _, y, _ = places(2)
     size = half.shape[1]
     groups = joined.shape[0] // 2 // (128 // vk.shape[2] - 1)
     n = size // groups
@@ -300,27 +300,51 @@
         half[f, i] = plane
 
     unpacked(blocks, groups, s, store)
-
-
-def vector_kernel(half, msg, joined, fields):
-    s, x, _, _ = places(2)
-    cx = half.shape[1]
-    fields[:, pl.ds(cx * x, cx)] = half[...]
+    first = straight.shape[0] - 2
+    photon_edges(bg, labels, straight, across)
+    for f in range(2):
+        for g in range(straight.shape[1]):
+            edge = packed_edges([near_rows(half.at[f], GROUP * g + j, y) for j in range(GROUP)])
+            straight[first + f, g] = across[first + f, g] = edge
+
+
+def vector_kernel(half, msg, joined, straight, across, fields, mine_edge):
+    s, x, _, c = places(2)
+    _, cx, cy, _ = half.shape
     n = lax.axis_size("src")
     groups = cx // n
     own = msg.shape[0] - 2 * groups
     blocks = [[msg[own + i] for i in range(2 * groups)]]
     blocks += [[joined[2 * groups * k + i] for i in range(2 * groups)] for k in range(n - 1)]
-    there = cx * (1 - x)
+    here, there = cx * x, cx * (1 - x)
+    edge_groups = straight.shape[1]
+    labels = straight.shape[0] - 3
 
     def store(f, i, plane):
-        fields[f, there + i] = plane
-
+        fields[f, plane_rows(there + i, cy), :] = plane
+
+    for f in range(2):
+        for i in range(cx):
+            fields[f, plane_rows(here + i, cy), :] = half[f, i]
+    for g in range(edge_groups):
+        for part, at in ((straight, edge_groups * x + g), (across, edge_groups * (1 - x) + g)):
+            mine_edge[at] = part[c, g]
+            for f, second in ((0, 1 - c), (1, labels)):
+                fields[f, edge_rows(2 * cx, cy, 0, at), :] = part[labels + 1 + f, g]
+                fields[f, edge_rows(2 * cx, cy, 1, at), :] = part[second, g]
     unpacked(blocks, groups, s, store)
 
 
-def edge_shape(planes, lanes):
-    return planes // GROUP, GROUP * REACH, lanes
+def edge_rows(planes, cy, which, g):
+    return pl.ds(pl.multiple_of(planes * (cy + REACH * which) + GROUP * REACH * g, 8), GROUP * REACH)
+
+
+def plane_rows(i, cy):
+    return pl.ds(pl.multiple_of(cy * i, 8), cy)
+
+
+def message_rows(planes, cy):
+    return planes * (cy + 2 * REACH)
 
 
 def packed_edges(tiles):
@@ -333,30 +357,40 @@
     return jnp.where(y == 0, tile, shifted(tile, HALO - REACH, 0))
 
 
-def near_rows(ref, i, first, y):
-    tile = ref[i, pl.ds(first, HALO), :]
+def near_tile(tile, y):
     return jnp.where(y == 0, shifted(tile, REACH - HALO, 0), tile)
 
 
-def edges_of(own, got, edge, y, c):
-    first = (own.shape[1] - HALO) * (1 - y)
-    for g in range(edge.shape[0]):
-        edge[g] = packed_edges([
-            jnp.where(c != y, near_rows(own, GROUP * g + j, first, y), near_rows(got, GROUP * g + j, first, y))
-            for j in range(GROUP)
-        ])
-
-
-def photon_edge_kernel(mine, fields, got, edge):
-    _, _, y, c = places(2)
-    edges_of(mine, got.at[0], edge.at[0], y, c)
-    edges_of(fields.at[1], got.at[1], edge.at[1], y, c)
-
-
-def vector_edge_kernel(fields, got, edge):
-    _, _, y, c = places(2)
-    for f in range(2):
-        edges_of(fields.at[f], got.at[f], edge.at[f], y, c)
+def near_rows(ref, i, y):
+    first = (ref.shape[1] - HALO) * (1 - y)
+    return near_tile(ref[i, pl.ds(pl.multiple_of(first, 8), HALO), :], y)
+
+
+def photon_edges(bg, labels, straight, across):
+    _, x, y, _ = places(2)
+    half = bg.shape[0] // 2
+    first = pl.ds(pl.multiple_of((labels.shape[1] - HALO) * (1 - y), 8), HALO)
+    for g in range(straight.shape[1]):
+        tiles = [near_tile(labels[GROUP * g + j, first, :].astype(jnp.float32), y) for j in range(GROUP)]
+        straight[half, g] = across[half, g] = packed_edges(tiles)
+        for out, at in ((straight, half * x), (across, half * (1 - x))):
+            for i in range(half):
+                out[i, g] = packed_edges([near_rows(bg.at[at + i], GROUP * g + j, y) for j in range(GROUP)])
+
+
+def framed_own(ref, shift, planes, cy, own, got, y, c):
+    base = HALO * y
+    for i in range(planes):
+        ref[shift + i, pl.ds(base + cy * c, cy), :] = own(i)
+        ref[shift + i, pl.ds(base + cy * (1 - c), cy), :] = got(i)
+
+
+def framed_edges(ref, shift, planes, own, got, y, c):
+    row = (ref.shape[1] - HALO) * (1 - y)
+    for g in range(planes // GROUP):
+        packed = jnp.where(c != y, own(g), got(g))
+        for j in range(GROUP):
+            ref[shift + GROUP * g + j, pl.ds(row, HALO), :] = edge_tile(packed, j, y)
 
 
 def solve(b, bufs, diag, fx, fy, fz, unroll):
@@ -384,23 +418,6 @@
     return jnp.sum(value.reshape(-1, 8, value.shape[1]), axis=0)
 
 
-def framed_own(ref, shift, own, got, y, c):
-    planes, cy, _ = own.shape
-    there = pl.ds(shift, planes)
-    base = HALO * y
-    ref[there, pl.ds(base + cy * c, cy), :] = own[...]
-    ref[there, pl.ds(base + cy * (1 - c), cy), :] = got[...]
-
-
-def framed(ref, shift, own, got, edge, y, c):
-    framed_own(ref, shift, own, got, y, c)
-    cy = own.shape[1]
-    for g in range(edge.shape[0]):
-        packed = edge[g]
-        for j in range(GROUP):
-            ref[shift + GROUP * g + j, pl.ds(2 * cy * (1 - y), HALO), :] = edge_tile(packed, j, y)
-
-
 def blank_ends(*refs):
     for ref in refs:
         blank = jnp.zeros(ref.shape[1:], jnp.float32)
@@ -431,7 +448,7 @@
     planes, cy, lanes = mine.shape
     rows = 2 * cy + HALO
     base = HALO * y
-    framed_own(labels, 0, fields.at[1], got.at[1], y, c)
+    framed_own(labels, 0, planes, cy, lambda i: fields[1, i], lambda i: got[1, i], y, c)
     labels[:, pl.ds(2 * cy * (1 - y), HALO), :] = jnp.zeros((planes, HALO, lanes), jnp.float32)
     blank_ends(kap)
     shape = (rows, lanes)
@@ -445,7 +462,7 @@
         diag[i] = jnp.take_along_axis(abs_row, at, axis=1)
         return carry
 
-    lax.fori_loop(0, planes, look_up, 0, unroll=UNROLL)
+    lax.fori_loop(0, planes, look_up, 0, unroll=4)
     fx[0] = 0.5 * kap[1]
 
     def set_up(i, carry):
@@ -464,12 +481,17 @@
         return total, square
 
     zero = jnp.zeros((8, lanes), jnp.float32)
-    sums[0], sums[1] = lax.fori_loop(0, planes, set_up, (zero, zero), unroll=UNROLL)
-
-
-def halo_kernel(kap_table, abs_table, edge, kap, diag_in, fx_in, fy_in, fz_in, diag, fx, fy, fz):
-    _, _, y, _ = places(2)
+    sums[0], sums[1] = lax.fori_loop(0, planes, set_up, (zero, zero), unroll=4)
+
+
+def halo_kernel(kap_table, abs_table, vector, got_vector, kap, diag_in, fx_in, fy_in, fz_in, diag, fx, fy, fz):
+    _, _, y, c = places(2)
     planes, rows, lanes = diag.shape
+    cy = (rows - HALO) // 2
+    edges = [
+        jnp.where(c != y, *(ref[1, edge_rows(planes, cy, 1, g), :] for ref in (vector, got_vector)))
+        for g in range(planes // GROUP)
+    ]
     for ref, old in ((diag, diag_in), (fx, fx_in), (fy, fy_in), (fz, fz_in)):
         ref[...] = old[...]
     shape = (HALO, lanes)
@@ -478,7 +500,7 @@
     low = y == 0
     here = pl.ds((rows - HALO) * (1 - y), HALO)
     beside_it = pl.ds((rows - 2 * HALO) * (1 - y) + HALO * y, HALO)
-    labels = [edge_tile(edge[1, i // GROUP], i % GROUP, y).astype(jnp.int32) for i in range(planes)]
+    labels = [edge_tile(edges[i // GROUP], i % GROUP, y).astype(jnp.int32) for i in range(planes)]
     tiles = [jnp.take_along_axis(kap_row, at, axis=1) for at in labels]
     none = jnp.zeros(shape, jnp.float32)
     before = 0.5 * tiles[0]
@@ -504,16 +526,21 @@
 
 
 def first_kernel(
-    diag, fx, fy, fz, count, sums, mine, got_photon, vector, got_vector, photon_edge, edge,
+    diag, fx, fy, fz, count, sums, mine, mine_edge, got_photon, vector, got_vector,
     phi, change, message,
     vk, va, b, buf_a, buf_b,
 ):
     _, _, y, c = places(2)
     planes, rows, lanes = change.shape
     cy = mine.shape[1]
-    framed(phi, 1, mine, got_photon.at[0], photon_edge.at[0], y, c)
-    framed(vk, 1, vector.at[0], got_vector.at[0], edge.at[0], y, c)
-    framed(va, 0, vector.at[1], got_vector.at[1], edge.at[1], y, c)
+    framed_own(phi, 1, planes, cy, lambda i: mine[i], lambda i: got_photon[0, i], y, c)
+    second = lambda g: got_vector[0, edge_rows(planes, cy, 1, g), :]
+    framed_edges(phi, 1, planes, lambda g: mine_edge[g], second, y, c)
+    for ref, shift, f in ((vk, 1, 0), (va, 0, 1)):
+        rows_of = lambda message: lambda i: message[f, plane_rows(i, cy), :]
+        edges_of = lambda message: lambda g: message[f, edge_rows(planes, cy, 0, g), :]
+        framed_own(ref, shift, planes, cy, rows_of(vector), rows_of(got_vector), y, c)
+        framed_edges(ref, shift, planes, edges_of(vector), edges_of(got_vector), y, c)
     blank_ends(phi, vk, buf_a, buf_b)
     theta, _ = chebyshev_scalars()
 
@@ -529,8 +556,8 @@
         buf_a[i + 1] = total * (1.0 / theta)
         return carry
 
-    lax.fori_loop(0, planes, set_up, 0, unroll=UNROLL)
-    found = solve(b, (buf_a, buf_b), diag, fx, fy, fz, UNROLL)
+    lax.fori_loop(0, planes, set_up, 0, unroll=4)
+    found = solve(b, (buf_a, buf_b), diag, fx, fy, fz, 16)
     owned = owned_rows((rows, lanes), HALO * y, 2 * cy)
 
     def add_up(i, carry):
@@ -540,11 +567,11 @@
         return carry[0] + folded(part), carry[1] + folded(part * phi[i + 1])
 
     zero = jnp.zeros((8, lanes), jnp.float32)
-    seen, cross = lax.fori_loop(0, planes, add_up, (zero, zero), unroll=UNROLL)
+    seen, cross = lax.fori_loop(0, planes, add_up, (zero, zero), unroll=4)
     first = (2 * cy - HALO) * (1 - y) + HALO * y
     for g, part in enumerate((sums[0], seen, cross, sums[1])):
         message[g, pl.ds(0, GROUP * REACH), :] = packed_edges(
-            [near_rows(found, 1 + GROUP * g + j, first, y) for j in range(GROUP)]
+            [near_tile(found[1 + GROUP * g + j, pl.ds(first, HALO), :], y) for j in range(GROUP)]
         )
         message[g, pl.ds(GROUP * REACH, 8), :] = part
 
@@ -581,13 +608,13 @@
         buf_a[i + 1] = value * (1.0 / theta)
         return carry
 
-    lax.fori_loop(0, planes, set_up, 0, unroll=UNROLL)
+    lax.fori_loop(0, planes, set_up, 0, unroll=4)
     for i in range(planes):
         u = edge_tile(came[i // GROUP], i % GROUP, y)
         value = weighted(count[i, edge, :], u, phi[i + 1, edge, :])
         b[i, edge, :] = value
         buf_a[i + 1, edge, :] = value * (1.0 / theta)
-    dual = solve(b, (buf_a, buf_b), diag, fx, fy, fz, UNROLL)
+    dual = solve(b, (buf_a, buf_b), diag, fx, fy, fz, 16)
 
     def product(i, carry):
         p, u = phi[i + 1], dual[i + 1]
@@ -604,7 +631,7 @@
             message[f, i] = ref[i, pl.ds(base + cy * (1 - c), cy), :]
         return carry
 
-    lax.fori_loop(0, planes, product, 0, unroll=UNROLL)
+    lax.fori_loop(0, planes, product, 0, unroll=4)
 
 
 def packed_slabs(own, came, half, choices, outs):
@@ -699,7 +726,7 @@
     return jax.ShapeDtypeStruct(shape, jnp.float32)
 
 
-def run(kernel, outs, *args, after=(), scratch=(), copies=0, smem=(), hbm=(), mib=16, in_smem_out=(), hbm_out=False, cost=None):
+def run(kernel, outs, *args, after=(), scratch=(), copies=0, smem=(), hbm=(), mib=16, in_smem_out=(), cost=None):
     vmem = pl.BlockSpec(memory_space=pltpu.VMEM)
     scalar = pl.BlockSpec(memory_space=pltpu.SMEM)
     far = pl.BlockSpec(memory_space=pltpu.HBM)
@@ -715,8 +742,10 @@
     return pl.pallas_call(
         body if waits else kernel,
         out_shape=tuple(outs),
-        in_specs=[scalar if i in smem else far if i in hbm else vmem for i in range(len(args))],
-        out_specs=tuple(scalar if i in in_smem_out else far if hbm_out else vmem for i in range(len(outs))),
+        in_specs=[
+            scalar if i in smem else far if i in hbm or i >= used else vmem for i in range(len(args))
+        ],
+        out_specs=tuple(scalar if i in in_smem_out else vmem for i in range(len(outs))),
         scratch_shapes=held,
         compiler_params=pltpu.CompilerParams(vmem_limit_bytes=mib * 2**20),
         cost_estimate=cost,
@@ -724,7 +753,6 @@
 
 
 HALO = 8
-UNROLL = 16
 REACH = 6
 GROUP = 4
 
@@ -756,52 +784,55 @@
     packed, message = run(
         pack_kernel, (f32(2 * groups, cy, cz), f32((sources // 2 + 1) * cx + 2 * groups, cy, cz)),
         background, labels, v_kappa, v_absorb, hbm=(0, 1, 2, 3),
-        scratch=(raw_labels, float_block(2, *v_kappa.shape), float_block(2 * groups, cy, cz), float_block(*block)),
-        copies=6 + sources // 2, hbm_out=True, mib=60,
+        scratch=(raw_labels, float_block(2, *v_kappa.shape)), copies=3 + sources // 2, mib=60,
     )
     long = pl.CostEstimate(flops=10**9, bytes_accessed=2**26, transcendentals=0)
     came = swap_x(message)
     slabs = [along_z(packed, k) for k in range(1, n)]
+    def to_inner(straight, across):
+        over = [(1, 6), (6, 1), (2, 5), (5, 2)]
+        return lax.ppermute(straight, "gy", [(1, 2), (2, 1)]), lax.ppermute(across, ("gx", "gy"), over)
+
+    def across_y(value):
+        return lax.ppermute(value, "gy", [(i, (i + 2) % 4) for i in range(4)])
+
+    edge = (cx // GROUP, GROUP * REACH, cz)
     count, beta_row = run(
         functools.partial(count_kernel, ny=ny, nz=cz, half=2 * cy, halo=HALO),
         (f32(planes, rows, cz), f32(1, cz)), det_cells.reshape(1, dets), beta_prev, smem=(1,),
         cost=pl.CostEstimate(flops=2 * planes * rows * cz * dets, bytes_accessed=planes * rows * cz * 4, transcendentals=0),
     )
-
-    def across_y(value):
-        return lax.ppermute(value, "gy", [(i, (i + 2) % 4) for i in range(4)])
-
     (joined,) = run(join_kernel, (f32(2 * groups * (n - 1), cy, cz),), *slabs, after=(count,))
     joined_came = swap_x(joined)
-    (half_vector,) = run(own_half_kernel, (f32(2, *block),), v_kappa, v_absorb, joined)
+    half_vector, *edges = run(
+        own_half_kernel, (f32(2, *block), *[f32(sources // 2 + 3, *edge)] * 2),
+        v_kappa, v_absorb, joined, background, labels,
+    )
+    edges = to_inner(*edges)
+    message = f32(2, message_rows(planes, cy), cz)
     mine, fields = run(
         photon_kernel, (f32(planes, cy, cz), f32(2, planes, cy, cz)),
         background, labels, came, after=(joined,), hbm=(0, 1), scratch=(raw_labels,), copies=3,
     )
     got = swap_core(fields)
-    (vector,) = run(
-        vector_kernel, (f32(2, planes, cy, cz),), half_vector, came, joined_came, after=(mine,)
-    )
-    edge = (f32(2, *edge_shape(planes, cz)),)
-    (sent,) = run(photon_edge_kernel, edge, mine, fields, got, after=(vector,))
-    photon_edge = across_y(sent)
+    vector, mine_edge = run(
+        vector_kernel, (message, f32(planes // GROUP, *edge[1:])), half_vector, came, joined_came, *edges, after=(mine,)
+    )
     vector_got = swap_core(vector)
-    (vector_sent,) = run(vector_edge_kernel, edge, vector, vector_got, after=(sent,))
     frame, wide = (planes, rows, cz), (planes + 2, rows, cz)
     float_frame, float_wide = float_block(*frame), float_block(*wide)
     coefs = (f32(*frame), f32(planes + 1, rows, cz), f32(*frame), f32(*frame))
     kap, *partial, sums = run(
         stencil_kernel, (f32(*wide), *coefs, f32(2, 8, cz)),
-        kappa_table, absorb_table, mine, fields, got, count, after=(vector_sent,), cost=long,
+        kappa_table, absorb_table, mine, fields, got, count, after=(vector,),
         smem=(0, 1), scratch=(float_frame,),
     )
     diag, fx, fy, fz = run(
-        halo_kernel, coefs, kappa_table, absorb_table, photon_edge, kap, *partial, smem=(0, 1)
+        halo_kernel, coefs, kappa_table, absorb_table, vector, vector_got, kap, *partial, smem=(0, 1)
     )
     phi, change, sent = run(
         first_kernel, (f32(*wide), f32(*frame), f32(4, GROUP * REACH + 8, cz)),
-        diag, fx, fy, fz, count, sums, mine, got, vector, vector_got,
-        photon_edge, across_y(vector_sent),
+        diag, fx, fy, fz, count, sums, mine, mine_edge, got, vector, vector_got,
         scratch=(float_wide, float_frame, float_frame, float_wide, float_wide),
     )
     heard = across_y(sent)

time: 80.4 us -> 74.7 us (0.929)
  Pallas kernels: 27.2 us -> 19.4 us
  starting transfers between devices: 22 us -> 23.8 us
  blocking collectives: 12.4 us -> 10.9 us
  waiting for transfers between devices: 17 us -> 18.3 us
    pallas_call x24 -> x22, Pallas kernels: 27.2 us -> 19.4 us  [run(): pl.pallas_call(body if waits else kernel, out_shape=tuple(outs), in_specs...]
    ppermute x3, starting transfers between devices: 0.21 us -> 6.02 us  [swap_core(): return lax.ppermute(value, 'gy', [(0, 1), (1, 0), (2, 3), (3, 2)])]
    ppermute x3 -> x1, starting transfers between devices: 4.75 us -> 0.33 us  [across_y(): return lax.ppermute(value, 'gy', [(i, (i + 2) % 4) for i in range(4)])]
    ppermute x3, waiting for transfers between devices: 2.11 us -> 4.39 us  [swap_core(): return lax.ppermute(value, 'gy', [(0, 1), (1, 0), (2, 3), (3, 2)])]
    ppermute x6, waiting for transfers between devices: 4.81 us -> 3.01 us  [swap_x(): return lax.ppermute(value, 'gx', [(0, 1), (1, 0)])]
    all_to_all x1, blocking collectives: 12.4 us -> 10.9 us  [per_device_paired(): lax.all_to_all(jnp.broadcast_to(tile, (8 * n, 8, 128)), everyone, 0, 0)]
    ppermute x0 -> x2, starting transfers between devices: none -> 1.34 us  [the longest x1 0.67 us: to_inner(): lax.ppermute(straight, 'gy', [(1, 2), (2, 1)])]
    ppermute x6, starting transfers between devices: 9.3 us -> 8.36 us  [along_z(): return lax.ppermute(value, 'src', [(i, i ^ k) for i in range(n)])]
  transfers between devices with their start and end apart: 18 -> 18, of which waited for: 13 -> 10; matrix products, arithmetic and copies ran while one was open for 0% -> 0% of each run, Pallas kernels for 9% -> 8%
where the time goes in v12:
time: 74.7 us; the launch traced here: 74.5 us
  starting transfers between devices  23.8 us (32%)
  Pallas kernels  19.4 us (26%)
  waiting for transfers between devices  18.3 us (24%)
  blocking collectives  10.9 us (15%)
  between operations  1.58 us (2%)
    pallas_call x22, Pallas kernels, run(): pl.pallas_call(body if waits else kernel, out_shape=tuple(outs), in_specs...  19.4 us
    all_to_all x1, blocking collectives, per_device_paired(): lax.all_to_all(jnp.broadcast_to(tile, (8 * n, 8, 128)), everyone, 0, 0)  10.9 us
    ppermute x6, starting transfers between devices, along_z(): return lax.ppermute(value, 'src', [(i, i ^ k) for i in range(n)])  8.36 us
    ppermute x6, starting transfers between devices, swap_x(): return lax.ppermute(value, 'gx', [(0, 1), (1, 0)])  7.77 us
    ppermute x6, waiting for transfers between devices, along_z(): return lax.ppermute(value, 'src', [(i, i ^ k) for i in range(n)])  6.76 us
    ppermute x3, starting transfers between devices, swap_core(): return lax.ppermute(value, 'gy', [(0, 1), (1, 0), (2, 3), (3, 2)])  6.02 us
    ppermute x3, waiting for transfers between devices, swap_core(): return lax.ppermute(value, 'gy', [(0, 1), (1, 0), (2, 3), (3, 2)])  4.39 us
    ppermute x1, waiting for transfers between devices, across_y(): return lax.ppermute(value, 'gy', [(i, (i + 2) % 4) for i in range(4)])  4.11 us
  transfers between devices with their start and end apart: 18, of which 10 were waited for; matrix products, arithmetic and copies ran while one was open for 0% of the time, Pallas kernels for 8%

profile of v12, /device:TPU:0, one launch (start us, length us, event | category | flops | bytes accessed | tf_op | source)
XLA Modules:
  0.0 74.5 jit_solution(3863709212453908378)
XLA Ops:
  0.6 2.0 %shard_map.122 = (f32[4,32,128]{2,1,0:T(8,128)}, f32[28,32,128]{2,1,0:T(8,128)}) custom-call(f32[4,8,32,128]{3,2,1,0:T(8,128)} %refs_0_.2, s32[8,32,128]{2,1,0:T(8,128)} %refs_1_.2, f32[8,32,32]{2,1,0:T(8,128)} %vk.5, f32[8,32,32]{2,1,0:T(8,128)} %va.5), custom_call_target="tpu_custom_call" | custom-call | tf_op jit(solution)/shard_map/pallas_call | solution.py:742
  2.7 3.0 %collective-permute-start.3 = (f32[28,32,128]{2,1,0:T(8,128)}, f32[28,32,128]{2,1,0:T(8,128)S(1)}, u32[]{:S(2)}, u32[]{:S(2)}) collective-permute-start(f32[28,32,128]{2,1,0:T(8,128)} %get-tuple-element.36), channel_id=1, source_target_pairs={{0,4},{4,0},{1,5},{5,1},{2,6},{6,2},{3,7},{7,3},{8,12},{12,8},{9,1... | collective-permute-start | bytes 1376264 | tf_op jit(solution)/shard_map/ppermute | solution.py:773
  5.7 3.6 %collective-permute-start.2 = (f32[4,32,128]{2,1,0:T(8,128)}, f32[4,32,128]{2,1,0:T(8,128)S(1)}, u32[]{:S(2)}, u32[]{:S(2)}) collective-permute-start(f32[4,32,128]{2,1,0:T(8,128)} %get-tuple-element.33), channel_id=1, source_target_pairs={{0,24},{8,16},{16,8},{24,0},{1,25},{9,17},{17,9},{25,1},{2,26},{10... | collective-permute-start | bytes 196616 | tf_op jit(solution)/shard_map/ppermute | solution.py:779
  10.7 2.1 %shard_map.121 = (f32[16,72,128]{2,1,0:T(8,128)S(1)}, f32[1,128]{1,0:T(1,128)S(1)}) custom-call(s32[1,1024]{1,0:T(1,128)S(1)} %bitcast.1, f32[1]{0:T(128)S(6)} %copy.13.beta_prev), custom_call_target="tpu_custom_call" | custom-call | flops 301989888 | bytes 589824 | tf_op jit(solution)/shard_map/pallas_call | solution.py:742
  12.8 2.0 %collective-permute-done.1.refs_1_ = f32[4,32,128]{2,1,0:T(8,128)S(1)} collective-permute-done((f32[4,32,128]{2,1,0:T(8,128)}, f32[4,32,128]{2,1,0:T(8,128)S(1)}, u32[]{:S(2)}, u32[]{:S(2)}) %collective-permute-start.1) | collective-permute-done | bytes 65568 | tf_op jit(solution)/shard_map/ppermute | solution.py:779
  18.3 2.9 %collective-permute-done.4.refs_2_ = f32[12,32,128]{2,1,0:T(8,128)S(1)} collective-permute-done((f32[12,32,128]{2,1,0:T(8,128)S(1)}, f32[12,32,128]{2,1,0:T(8,128)S(1)}, u32[]{:S(2)}, u32[]{:S(2)}) %collective-permute-start.4) | collective-permute-done | bytes 196640 | tf_op jit(solution)/shard_map/ppermute | solution.py:773
  21.6 5.9 %collective-permute-start.7 = (f32[2,704,128]{2,1,0:T(8,128)S(1)}, f32[2,704,128]{2,1,0:T(8,128)S(1)}, u32[]{:S(2)}, u32[]{:S(2)}) collective-permute-start(f32[2,704,128]{2,1,0:T(8,128)S(1)} %get-tuple-element.40.refs_6_.vector), channel_id=1, source_target_pairs={{0,1},{1,0},{2,3},{3,2},{4,5},{5,4},{6,7},{7,6},{8,9},{9,8},{10,11... | collective-permute-start | bytes 2162696 | tf_op jit(solution)/shard_map/ppermute | solution.py:776
  27.5 2.5 %collective-permute-done.8.refs_4_.got_photon = f32[2,16,32,128]{3,2,1,0:T(8,128)S(1)} collective-permute-done((f32[2,16,32,128]{3,2,1,0:T(8,128)S(1)}, f32[2,16,32,128]{3,2,1,0:T(8,128)S(1)}, u32[]{:S(2)}, u32[]{:S(2)}) %collective-permute-start.8) | collective-permute-done | bytes 524320 | tf_op jit(solution)/shard_map/ppermute | solution.py:776
  30.0 2.4 %shard_map.127 = (f32[18,72,128]{2,1,0:T(8,128)S(1)}, f32[16,72,128]{2,1,0:T(8,128)S(1)}, f32[17,72,128]{2,1,0:T(8,128)S(1)}, f32[16,72,128]{2,1,0:T(8,128)S(1)}...) custom-call(f32[16]{0:T(128)S(1)} %copy-done.6, f32[16]{0:T(128)S(1)} %copy-done.7, ...), custom_call_target="tpu_custom_call" | custom-call | tf_op jit(solution)/shard_map/pallas_call | solution.py:742
  32.4 0.8 %shard_map.128 = (f32[16,72,128]{2,1,0:T(8,128)S(1)}, f32[17,72,128]{2,1,0:T(8,128)S(1)}, f32[16,72,128]{2,1,0:T(8,128)S(1)}, f32[16,72,128]{2,1,0:T(8,128)S(1)}) custom-call(f32[16]{0:T(128)S(1)} %copy-done.6, f32[16]{0:T(128)S(1)} %copy-done.7, f32[2,704,128]{2,1,0:T(8,128)S(1)} %get-tuple-element.40.refs_6_.vector, ...), custom_call_target="tpu_custom_call" | custom-call | tf_op jit(solution)/shard_map/pallas_call | solution.py:742
  33.2 4.1 %shard_map.129 = (f32[18,72,128]{2,1,0:T(8,128)S(1)}, f32[16,72,128]{2,1,0:T(8,128)S(1)}, f32[4,32,128]{2,1,0:T(8,128)S(1)}) custom-call(f32[16,72,128]{2,1,0:T(8,128)S(1)} %get-tuple-element.47.diag, f32[17,72,128]{2,1,0:T(8,128)S(1)} %get-tuple-element.48.fx, f32[16,72,128]{2,1,0:T(8,128)S(1)} %get-tuple-element.49.fy, ...), custom_call_target="tpu_custom_call" | custom-call | tf_op jit(solution)/shard_map/pallas_call | solution.py:742
  37.7 4.1 %collective-permute-done.9.came = f32[4,32,128]{2,1,0:T(8,128)S(1)} collective-permute-done((f32[4,32,128]{2,1,0:T(8,128)S(1)}, f32[4,32,128]{2,1,0:T(8,128)S(1)}, u32[]{:S(2)}, u32[]{:S(2)}) %collective-permute-start.9) | collective-permute-done | bytes 65568 | tf_op jit(solution)/shard_map/ppermute | solution.py:797
  41.8 4.1 %shard_map.130 = (f32[2,16,32,128]{3,2,1,0:T(8,128)S(1)}, f32[2,16,32,128]{3,2,1,0:T(8,128)S(1)}) custom-call(f32[18,72,128]{2,1,0:T(8,128)S(1)} %get-tuple-element.53.phi, f32[16,72,128]{2,1,0:T(8,128)S(1)} %get-tuple-element.54.change, f32[16,72,128]{2,1,0:T(8,128)S(1)} %get-tuple-element.47.diag, f32[17,72,128]{2,1,0:T(8,128)S(1)} %get-tuple-element.48.fx, ...), custom_call_target="tpu_custom_call" | custom-call | tf_op jit(solution)/shard_map/pallas_call | solution.py:742
  46.0 1.9 %collective-permute-done.10.came.refs_1_ = f32[2,16,32,128]{3,2,1,0:T(8,128)S(1)} collective-permute-done((f32[2,16,32,128]{3,2,1,0:T(8,128)S(1)}, f32[2,16,32,128]{3,2,1,0:T(8,128)S(1)}, u32[]{:S(2)}, u32[]{:S(2)}) %collective-permute-start.10) | collective-permute-done | bytes 524320 | tf_op jit(solution)/shard_map/ppermute | solution.py:776
  48.2 1.2 %collective-permute-start.11 = (f32[1,2,2,32,128]{4,3,2,1,0:T(8,128)S(1)}, f32[1,2,2,32,128]{4,3,2,1,0:T(8,128)S(1)}, u32[]{:S(2)}, u32[]{:S(2)}) collective-permute-start(f32[1,2,2,32,128]{4,3,2,1,0:T(8,128)S(1)} %shard_map.132.refs_2_), channel_id=1, source_target_pairs={{0,4},{4,0},{1,5},{5,1},{2,6},{6,2},{3,7},{7,3},{8,12},{12,8},{9,1... | collective-permute-start | bytes 196616 | tf_op jit(solution)/shard_map/ppermute | solution.py:773
  49.4 0.9 %collective-permute-start.13 = (f32[1,2,2,32,128]{4,3,2,1,0:T(8,128)S(1)}, f32[1,2,2,32,128]{4,3,2,1,0:T(8,128)S(1)}, u32[]{:S(2)}, u32[]{:S(2)}) collective-permute-start(f32[1,2,2,32,128]{4,3,2,1,0:T(8,128)S(1)} %shard_map.131.refs_2_), channel_id=1, source_target_pairs={{0,4},{4,0},{1,5},{5,1},{2,6},{6,2},{3,7},{7,3},{8,12},{12,8},{9,1... | collective-permute-start | bytes 196616 | tf_op jit(solution)/shard_map/ppermute | solution.py:773
  50.4 1.2 %collective-permute-start.16 = (f32[1,2,2,32,128]{4,3,2,1,0:T(8,128)S(1)}, f32[1,2,2,32,128]{4,3,2,1,0:T(8,128)S(1)}, u32[]{:S(2)}, u32[]{:S(2)}) collective-permute-start(f32[1,2,2,32,128]{4,3,2,1,0:T(8,128)S(1)} %shard_map.133.refs_2_), channel_id=1, source_target_pairs={{0,4},{4,0},{1,5},{5,1},{2,6},{6,2},{3,7},{7,3},{8,12},{12,8},{9,1... | collective-permute-start | bytes 196616 | tf_op jit(solution)/shard_map/ppermute | solution.py:773
  51.7 1.0 %collective-permute-start.15 = (f32[1,2,2,32,128]{4,3,2,1,0:T(8,128)S(1)}, f32[1,2,2,32,128]{4,3,2,1,0:T(8,128)S(1)}, u32[]{:S(2)}, u32[]{:S(2)}) collective-permute-start(f32[1,2,2,32,128]{4,3,2,1,0:T(8,128)S(1)} %shard_map.134.refs_2_), channel_id=1, source_target_pairs={{0,4},{4,0},{1,5},{5,1},{2,6},{6,2},{3,7},{7,3},{8,12},{12,8},{9,1... | collective-permute-start | bytes 196616 | tf_op jit(solution)/shard_map/ppermute | solution.py:773
  53.2 1.8 %collective-permute-start.12 = (f32[2,2,32,128]{3,2,1,0:T(8,128)S(1)}, f32[2,2,32,128]{3,2,1,0:T(8,128)S(1)}, u32[]{:S(2)}, u32[]{:S(2)}) collective-permute-start(f32[2,2,32,128]{3,2,1,0:T(8,128)S(1)} %shard_map.136), channel_id=1, source_target_pairs={{0,16},{8,24},{16,0},{24,8},{1,17},{9,25},{17,1},{25,9},{2,18},{10... | collective-permute-start | bytes 196616 | tf_op jit(solution)/shard_map/ppermute | solution.py:779
  55.1 2.1 %collective-permute-start.14 = (f32[2,2,32,128]{3,2,1,0:T(8,128)S(1)}, f32[2,2,32,128]{3,2,1,0:T(8,128)S(1)}, u32[]{:S(2)}, u32[]{:S(2)}) collective-permute-start(f32[2,2,32,128]{3,2,1,0:T(8,128)S(1)} %shard_map.137), channel_id=1, source_target_pairs={{0,24},{8,16},{16,8},{24,0},{1,25},{9,17},{17,9},{25,1},{2,26},{10... | collective-permute-start | bytes 196616 | tf_op jit(solution)/shard_map/ppermute | solution.py:779
  57.3 2.6 %collective-permute-done.12.refs_0_ = f32[2,2,32,128]{3,2,1,0:T(8,128)S(1)} collective-permute-done((f32[2,2,32,128]{3,2,1,0:T(8,128)S(1)}, f32[2,2,32,128]{3,2,1,0:T(8,128)S(1)}, u32[]{:S(2)}, u32[]{:S(2)}) %collective-permute-start.12) | collective-permute-done | bytes 65568 | tf_op jit(solution)/shard_map/ppermute | solution.py:779
  59.9 1.4 %collective-permute-done.14.refs_1_ = f32[2,2,32,128]{3,2,1,0:T(8,128)S(1)} collective-permute-done((f32[2,2,32,128]{3,2,1,0:T(8,128)S(1)}, f32[2,2,32,128]{3,2,1,0:T(8,128)S(1)}, u32[]{:S(2)}, u32[]{:S(2)}) %collective-permute-start.14) | collective-permute-done | bytes 65568 | tf_op jit(solution)/shard_map/ppermute | solution.py:779
  62.6 10.9 %all_to_all.5.tiles = f32[32,8,128]{2,1,0:T(8,128)S(1)} all-to-all(f32[32,8,128]{2,1,0:T(8,128)S(1)} %broadcast_in_dim.3), channel_id=1, replica_groups=mesh['src'=4,'gx'=2,'gy'=4] {'src','gx','gy'}, dimensions={0} | all-to-all | bytes 262144 | tf_op jit(solution)/shard_map/all_to_all | solution.py:864
  73.5 1.0 %shard_map.142 = (f32[8,32,32]{2,1,0:T(8,128)}, f32[8,32,32]{2,1,0:T(8,128)}, f32[2]{0:T(128)}) custom-call(f32[32,8,128]{2,1,0:T(8,128)S(1)} %all_to_all.5.tiles, f32[8,32,32]{2,1,0:T(8,128)S(1)} %get-tuple-element.59.w_k, f32[8,32,32]{2,1,0:T(8,128)S(1)} %get-tuple-element.60.w_a, f32[8,32,32]{2,1,0:T(8,128)S(1)} %copy-done.1, f32[8,32,32]{2,1,0:T(8,128)S(1)} %copy-done.2), custom_call_target="tpu_custom_call" | custom-call | tf_op jit(solution)/shard_map/pallas_call | solution.py:742
  (54 shorter events, 7.4 us)
Async XLA Ops:
  2.6 8.1 %copy-start.8 = (s32[1024]{0:T(1024)S(1)}, s32[1024]{0:T(1024)}, u32[]{:S(2)}) copy-start(s32[1024]{0:T(1024)} %param.14) | copy-start | bytes 12292
  2.7 15.1 %collective-permute-start.3 = (f32[28,32,128]{2,1,0:T(8,128)}, f32[28,32,128]{2,1,0:T(8,128)S(1)}, u32[]{:S(2)}, u32[]{:S(2)}) collective-permute-start(f32[28,32,128]{2,1,0:T(8,128)} %get-tuple-element.36), channel_id=1, source_target_pairs={{0,4},{4,0},{1,5},{5,1},{2,6},{6,2},{3,7},{7,3},{8,12},{12,8},{9,1... | collective-permute-start | bytes 1376264 | tf_op jit(solution)/shard_map/ppermute | solution.py:773
  5.7 7.2 %collective-permute-start.2 = (f32[4,32,128]{2,1,0:T(8,128)}, f32[4,32,128]{2,1,0:T(8,128)S(1)}, u32[]{:S(2)}, u32[]{:S(2)}) collective-permute-start(f32[4,32,128]{2,1,0:T(8,128)} %get-tuple-element.33), channel_id=1, source_target_pairs={{0,24},{8,16},{16,8},{24,0},{1,25},{9,17},{17,9},{25,1},{2,26},{10... | collective-permute-start | bytes 196616 | tf_op jit(solution)/shard_map/ppermute | solution.py:779
  9.3 5.6 %collective-permute-start.1 = (f32[4,32,128]{2,1,0:T(8,128)}, f32[4,32,128]{2,1,0:T(8,128)S(1)}, u32[]{:S(2)}, u32[]{:S(2)}) collective-permute-start(f32[4,32,128]{2,1,0:T(8,128)} %get-tuple-element.33), channel_id=1, source_target_pairs={{0,16},{8,24},{16,0},{24,8},{1,17},{9,25},{17,1},{25,9},{2,18},{10... | collective-permute-start | bytes 196616 | tf_op jit(solution)/shard_map/ppermute | solution.py:779
  9.3 5.6 %collective-permute-start = (f32[4,32,128]{2,1,0:T(8,128)}, f32[4,32,128]{2,1,0:T(8,128)S(1)}, u32[]{:S(2)}, u32[]{:S(2)}) collective-permute-start(f32[4,32,128]{2,1,0:T(8,128)} %get-tuple-element.33), channel_id=1, source_target_pairs={{0,8},{8,0},{16,24},{24,16},{1,9},{9,1},{17,25},{25,17},{2,10},{10... | collective-permute-start | bytes 196616 | tf_op jit(solution)/shard_map/ppermute | solution.py:779
  12.8 2.6 %copy-start = (f32[4,8,32,128]{3,2,1,0:T(8,128)S(1)}, f32[4,8,32,128]{3,2,1,0:T(8,128)}, u32[]{:S(2)}) copy-start(f32[4,8,32,128]{3,2,1,0:T(8,128)} %refs_0_.2) | copy-start | bytes 1572868
  14.9 6.3 %collective-permute-start.4 = (f32[12,32,128]{2,1,0:T(8,128)S(1)}, f32[12,32,128]{2,1,0:T(8,128)S(1)}, u32[]{:S(2)}, u32[]{:S(2)}) collective-permute-start(f32[12,32,128]{2,1,0:T(8,128)S(1)} %shard_map.123.joined.refs_3_), channel_id=1, source_target_pairs={{0,4},{4,0},{1,5},{5,1},{2,6},{6,2},{3,7},{7,3},{8,12},{12,8},{9,1... | collective-permute-start | bytes 589832 | tf_op jit(solution)/shard_map/ppermute | solution.py:773
  16.3 2.0 %collective-permute-start.5 = (f32[5,2,24,128]{3,2,1,0:T(8,128)S(1)}, f32[5,2,24,128]{3,2,1,0:T(8,128)S(1)}, u32[]{:S(2)}, u32[]{:S(2)}) collective-permute-start(f32[5,2,24,128]{3,2,1,0:T(8,128)S(1)} %get-tuple-element.37), channel_id=1, source_target_pairs={{1,2},{2,1},{5,6},{6,5},{9,10},{10,9},{13,14},{14,13},{17,18},{18,... | collective-permute-start | bytes 368648 | tf_op jit(solution)/shard_map/ppermute | solution.py:794
  17.0 1.3 %collective-permute-start.6 = (f32[5,2,24,128]{3,2,1,0:T(8,128)S(1)}, f32[5,2,24,128]{3,2,1,0:T(8,128)S(1)}, u32[]{:S(2)}, u32[]{:S(2)}) collective-permute-start(f32[5,2,24,128]{3,2,1,0:T(8,128)S(1)} %get-tuple-element.38), channel_id=1, source_target_pairs={{1,6},{6,1},{2,5},{5,2},{9,14},{14,9},{10,13},{13,10},{17,22},{22,... | collective-permute-start | bytes 368648 | tf_op jit(solution)/shard_map/ppermute | solution.py:794
  21.5 8.5 %copy-start.6 = (f32[16]{0:T(128)S(1)}, f32[16]{0:T(128)}, u32[]{:S(2)}) copy-start(f32[16]{0:T(128)} %kap_table.1) | copy-start | bytes 196
  21.6 8.5 %copy-start.7 = (f32[16]{0:T(128)S(1)}, f32[16]{0:T(128)}, u32[]{:S(2)}) copy-start(f32[16]{0:T(128)} %abs_table.1) | copy-start | bytes 196
  21.6 10.8 %collective-permute-start.7 = (f32[2,704,128]{2,1,0:T(8,128)S(1)}, f32[2,704,128]{2,1,0:T(8,128)S(1)}, u32[]{:S(2)}, u32[]{:S(2)}) collective-permute-start(f32[2,704,128]{2,1,0:T(8,128)S(1)} %get-tuple-element.40.refs_6_.vector), channel_id=1, source_target_pairs={{0,1},{1,0},{2,3},{3,2},{4,5},{5,4},{6,7},{7,6},{8,9},{9,8},{10,11... | collective-permute-start | bytes 2162696 | tf_op jit(solution)/shard_map/ppermute | solution.py:776
  27.4 2.6 %collective-permute-start.8 = (f32[2,16,32,128]{3,2,1,0:T(8,128)S(1)}, f32[2,16,32,128]{3,2,1,0:T(8,128)S(1)}, u32[]{:S(2)}, u32[]{:S(2)}) collective-permute-start(f32[2,16,32,128]{3,2,1,0:T(8,128)S(1)} %get-tuple-element.41.refs_3_), channel_id=1, source_target_pairs={{0,1},{1,0},{2,3},{3,2},{4,5},{5,4},{6,7},{7,6},{8,9},{9,8},{10,11... | collective-permute-start | bytes 1572872 | tf_op jit(solution)/shard_map/ppermute | solution.py:776
  37.4 4.4 %collective-permute-start.9 = (f32[4,32,128]{2,1,0:T(8,128)S(1)}, f32[4,32,128]{2,1,0:T(8,128)S(1)}, u32[]{:S(2)}, u32[]{:S(2)}) collective-permute-start(f32[4,32,128]{2,1,0:T(8,128)S(1)} %get-tuple-element.55.sent), channel_id=1, source_target_pairs={{0,2},{1,3},{2,0},{3,1},{4,6},{5,7},{6,4},{7,5},{8,10},{9,11},{10,... | collective-permute-start | bytes 196616 | tf_op jit(solution)/shard_map/ppermute | solution.py:797
  45.9 2.0 %collective-permute-start.10 = (f32[2,16,32,128]{3,2,1,0:T(8,128)S(1)}, f32[2,16,32,128]{3,2,1,0:T(8,128)S(1)}, u32[]{:S(2)}, u32[]{:S(2)}) collective-permute-start(f32[2,16,32,128]{3,2,1,0:T(8,128)S(1)} %get-tuple-element.57), channel_id=1, source_target_pairs={{0,1},{1,0},{2,3},{3,2},{4,5},{5,4},{6,7},{7,6},{8,9},{9,8},{10,11... | collective-permute-start | bytes 1572872 | tf_op jit(solution)/shard_map/ppermute | solution.py:776
  48.2 5.0 %collective-permute-start.11 = (f32[1,2,2,32,128]{4,3,2,1,0:T(8,128)S(1)}, f32[1,2,2,32,128]{4,3,2,1,0:T(8,128)S(1)}, u32[]{:S(2)}, u32[]{:S(2)}) collective-permute-start(f32[1,2,2,32,128]{4,3,2,1,0:T(8,128)S(1)} %shard_map.132.refs_2_), channel_id=1, source_target_pairs={{0,4},{4,0},{1,5},{5,1},{2,6},{6,2},{3,7},{7,3},{8,12},{12,8},{9,1... | collective-permute-start | bytes 196616 | tf_op jit(solution)/shard_map/ppermute | solution.py:773
  49.4 5.7 %collective-permute-start.13 = (f32[1,2,2,32,128]{4,3,2,1,0:T(8,128)S(1)}, f32[1,2,2,32,128]{4,3,2,1,0:T(8,128)S(1)}, u32[]{:S(2)}, u32[]{:S(2)}) collective-permute-start(f32[1,2,2,32,128]{4,3,2,1,0:T(8,128)S(1)} %shard_map.131.refs_2_), channel_id=1, source_target_pairs={{0,4},{4,0},{1,5},{5,1},{2,6},{6,2},{3,7},{7,3},{8,12},{12,8},{9,1... | collective-permute-start | bytes 196616 | tf_op jit(solution)/shard_map/ppermute | solution.py:773
  50.4 6.7 %collective-permute-start.16 = (f32[1,2,2,32,128]{4,3,2,1,0:T(8,128)S(1)}, f32[1,2,2,32,128]{4,3,2,1,0:T(8,128)S(1)}, u32[]{:S(2)}, u32[]{:S(2)}) collective-permute-start(f32[1,2,2,32,128]{4,3,2,1,0:T(8,128)S(1)} %shard_map.133.refs_2_), channel_id=1, source_target_pairs={{0,4},{4,0},{1,5},{5,1},{2,6},{6,2},{3,7},{7,3},{8,12},{12,8},{9,1... | collective-permute-start | bytes 196616 | tf_op jit(solution)/shard_map/ppermute | solution.py:773
  51.7 5.5 %collective-permute-start.15 = (f32[1,2,2,32,128]{4,3,2,1,0:T(8,128)S(1)}, f32[1,2,2,32,128]{4,3,2,1,0:T(8,128)S(1)}, u32[]{:S(2)}, u32[]{:S(2)}) collective-permute-start(f32[1,2,2,32,128]{4,3,2,1,0:T(8,128)S(1)} %shard_map.134.refs_2_), channel_id=1, source_target_pairs={{0,4},{4,0},{1,5},{5,1},{2,6},{6,2},{3,7},{7,3},{8,12},{12,8},{9,1... | collective-permute-start | bytes 196616 | tf_op jit(solution)/shard_map/ppermute | solution.py:773
  53.2 6.7 %collective-permute-start.12 = (f32[2,2,32,128]{3,2,1,0:T(8,128)S(1)}, f32[2,2,32,128]{3,2,1,0:T(8,128)S(1)}, u32[]{:S(2)}, u32[]{:S(2)}) collective-permute-start(f32[2,2,32,128]{3,2,1,0:T(8,128)S(1)} %shard_map.136), channel_id=1, source_target_pairs={{0,16},{8,24},{16,0},{24,8},{1,17},{9,25},{17,1},{25,9},{2,18},{10... | collective-permute-start | bytes 196616 | tf_op jit(solution)/shard_map/ppermute | solution.py:779
  55.1 6.3 %collective-permute-start.14 = (f32[2,2,32,128]{3,2,1,0:T(8,128)S(1)}, f32[2,2,32,128]{3,2,1,0:T(8,128)S(1)}, u32[]{:S(2)}, u32[]{:S(2)}) collective-permute-start(f32[2,2,32,128]{3,2,1,0:T(8,128)S(1)} %shard_map.137), channel_id=1, source_target_pairs={{0,24},{8,16},{16,8},{24,0},{1,25},{9,17},{17,9},{25,1},{2,26},{10... | collective-permute-start | bytes 196616 | tf_op jit(solution)/shard_map/ppermute | solution.py:779
  57.2 4.8 %collective-permute-start.17 = (f32[2,2,32,128]{3,2,1,0:T(8,128)S(1)}, f32[2,2,32,128]{3,2,1,0:T(8,128)S(1)}, u32[]{:S(2)}, u32[]{:S(2)}) collective-permute-start(f32[2,2,32,128]{3,2,1,0:T(8,128)S(1)} %shard_map.140), channel_id=1, source_target_pairs={{0,8},{8,0},{16,24},{24,16},{1,9},{9,1},{17,25},{25,17},{2,10},{10... | collective-permute-start | bytes 196616 | tf_op jit(solution)/shard_map/ppermute | solution.py:779
  57.3 4.7 %copy-start.4 = (f32[8,32,32]{2,1,0:T(8,128)S(1)}, f32[8,32,32]{2,1,0:T(8,128)}, u32[]{:S(2)}) copy-start(f32[8,32,32]{2,1,0:T(8,128)} %refs_6_.1) | copy-start | bytes 98308
  57.3 4.7 %copy-start.5 = (f32[8,32,32]{2,1,0:T(8,128)S(1)}, f32[8,32,32]{2,1,0:T(8,128)}, u32[]{:S(2)}) copy-start(f32[8,32,32]{2,1,0:T(8,128)} %refs_7_.1) | copy-start | bytes 98308
  (3 other events, 2.9 us)

commit v13 on v11

--- a/solution.py
+++ b/solution.py
@@ -190,32 +190,32 @@
     return jnp.concatenate([ref[per * q + j] for j in range(per)], axis=1)
 
 
-def pack_kernel(bg, labels, vk, va, packed, message, raw, v_in, slabs, floats, sems):
+def pack_kernel(bg, labels, vk, va, packed, message, raw, v_in, sems):
     _, x, _, _ = places(2)
     half = bg.shape[0] // 2
     cx = labels.shape[0]
-    size = slabs.shape[0]
-
-    def copy(i, src, dst):
-        started = pltpu.make_async_copy(src, dst, sems.at[i])
-        started.start()
-        return started
-
-    arrive = [copy(i, src, dst) for i, (src, dst) in enumerate(((vk, v_in.at[0]), (va, v_in.at[1]), (labels, raw)))]
-    leave = [
-        copy(3 + i, bg.at[half * (1 - x) + i], message.at[pl.ds(cx * i, cx)]) for i in range(half)
+    copies = [
+        pltpu.make_async_copy(src, dst, sems.at[i])
+        for i, (src, dst) in enumerate((
+            (vk, v_in.at[0]),
+            (va, v_in.at[1]),
+            (labels, raw),
+            *((bg.at[half * (1 - x) + i], message.at[pl.ds(cx * i, cx)]) for i in range(half)),
+        ))
     ]
+    for copy in copies:
+        copy.start()
+    groups = packed.shape[0] // 2
     for f in range(2):
-        arrive[f].wait()
-        for q in range(size // 2):
-            slabs[size // 2 * f + q] = packed_planes(v_in.at[f], q)
-    leave.append(copy(3 + half, slabs, packed))
-    leave.append(copy(4 + half, slabs, message.at[pl.ds(cx * (half + 1), size)]))
-    arrive[2].wait()
-    floats[...] = raw[...].astype(jnp.float32)
-    leave.append(copy(5 + half, floats, message.at[pl.ds(cx * half, cx)]))
-    for left in leave:
-        left.wait()
+        copies[f].wait()
+        for q in range(groups):
+            planes = packed_planes(v_in.at[f], q)
+            packed[groups * f + q] = planes
+            message[cx * (half + 1) + groups * f + q] = planes
+    copies[2].wait()
+    message[pl.ds(cx * half, cx)] = raw[...].astype(jnp.float32)
+    for copy in copies[3:]:
+        copy.wait()
 
 
 def count_kernel(dets, beta_prev, count, beta_row, *, ny, nz, half, halo):
@@ -445,7 +445,7 @@
         diag[i] = jnp.take_along_axis(abs_row, at, axis=1)
         return carry
 
-    lax.fori_loop(0, planes, look_up, 0, unroll=UNROLL)
+    lax.fori_loop(0, planes, look_up, 0, unroll=4)
     fx[0] = 0.5 * kap[1]
 
     def set_up(i, carry):
@@ -464,7 +464,7 @@
         return total, square
 
     zero = jnp.zeros((8, lanes), jnp.float32)
-    sums[0], sums[1] = lax.fori_loop(0, planes, set_up, (zero, zero), unroll=UNROLL)
+    sums[0], sums[1] = lax.fori_loop(0, planes, set_up, (zero, zero), unroll=4)
 
 
 def halo_kernel(kap_table, abs_table, edge, kap, diag_in, fx_in, fy_in, fz_in, diag, fx, fy, fz):
@@ -529,7 +529,7 @@
         buf_a[i + 1] = total * (1.0 / theta)
         return carry
 
-    lax.fori_loop(0, planes, set_up, 0, unroll=UNROLL)
+    lax.fori_loop(0, planes, set_up, 0, unroll=4)
     found = solve(b, (buf_a, buf_b), diag, fx, fy, fz, UNROLL)
     owned = owned_rows((rows, lanes), HALO * y, 2 * cy)
 
@@ -540,7 +540,7 @@
         return carry[0] + folded(part), carry[1] + folded(part * phi[i + 1])
 
     zero = jnp.zeros((8, lanes), jnp.float32)
-    seen, cross = lax.fori_loop(0, planes, add_up, (zero, zero), unroll=UNROLL)
+    seen, cross = lax.fori_loop(0, planes, add_up, (zero, zero), unroll=4)
     first = (2 * cy - HALO) * (1 - y) + HALO * y
     for g, part in enumerate((sums[0], seen, cross, sums[1])):
         message[g, pl.ds(0, GROUP * REACH), :] = packed_edges(
@@ -581,7 +581,7 @@
         buf_a[i + 1] = value * (1.0 / theta)
         return carry
 
-    lax.fori_loop(0, planes, set_up, 0, unroll=UNROLL)
+    lax.fori_loop(0, planes, set_up, 0, unroll=4)
     for i in range(planes):
         u = edge_tile(came[i // GROUP], i % GROUP, y)
         value = weighted(count[i, edge, :], u, phi[i + 1, edge, :])
@@ -604,7 +604,7 @@
             message[f, i] = ref[i, pl.ds(base + cy * (1 - c), cy), :]
         return carry
 
-    lax.fori_loop(0, planes, product, 0, unroll=UNROLL)
+    lax.fori_loop(0, planes, product, 0, unroll=4)
 
 
 def packed_slabs(own, came, half, choices, outs):
@@ -699,7 +699,7 @@
     return jax.ShapeDtypeStruct(shape, jnp.float32)
 
 
-def run(kernel, outs, *args, after=(), scratch=(), copies=0, smem=(), hbm=(), mib=16, in_smem_out=(), hbm_out=False, cost=None):
+def run(kernel, outs, *args, after=(), scratch=(), copies=0, smem=(), hbm=(), mib=16, in_smem_out=(), cost=None):
     vmem = pl.BlockSpec(memory_space=pltpu.VMEM)
     scalar = pl.BlockSpec(memory_space=pltpu.SMEM)
     far = pl.BlockSpec(memory_space=pltpu.HBM)
@@ -716,7 +716,7 @@
         body if waits else kernel,
         out_shape=tuple(outs),
         in_specs=[scalar if i in smem else far if i in hbm else vmem for i in range(len(args))],
-        out_specs=tuple(scalar if i in in_smem_out else far if hbm_out else vmem for i in range(len(outs))),
+        out_specs=tuple(scalar if i in in_smem_out else vmem for i in range(len(outs))),
         scratch_shapes=held,
         compiler_params=pltpu.CompilerParams(vmem_limit_bytes=mib * 2**20),
         cost_estimate=cost,
@@ -756,8 +756,7 @@
     packed, message = run(
         pack_kernel, (f32(2 * groups, cy, cz), f32((sources // 2 + 1) * cx + 2 * groups, cy, cz)),
         background, labels, v_kappa, v_absorb, hbm=(0, 1, 2, 3),
-        scratch=(raw_labels, float_block(2, *v_kappa.shape), float_block(2 * groups, cy, cz), float_block(*block)),
-        copies=6 + sources // 2, hbm_out=True, mib=60,
+        scratch=(raw_labels, float_block(2, *v_kappa.shape)), copies=3 + sources // 2, mib=60,
     )
     long = pl.CostEstimate(flops=10**9, bytes_accessed=2**26, transcendentals=0)
     came = swap_x(message)

time: 80.4 us -> 72.6 us (0.903)
  Pallas kernels: 27.2 us -> 19.8 us
    pallas_call x24, Pallas kernels: 27.2 us -> 19.8 us  [run(): pl.pallas_call(body if waits else kernel, out_shape=tuple(outs), in_specs...]
  transfers between devices with their start and end apart: 18 -> 18, of which waited for: 13 -> 12; matrix products, arithmetic and copies ran while one was open for 0% -> 0% of each run, Pallas kernels for 9% -> 10%
where the time goes in v13:
time: 72.6 us; the launch traced here: 72.5 us
  starting transfers between devices  22 us (30%)
  Pallas kernels  19.8 us (27%)
  waiting for transfers between devices  16.7 us (23%)
  blocking collectives  12.4 us (17%)
  between operations  1.6 us (2%)
    pallas_call x24, Pallas kernels, run(): pl.pallas_call(body if waits else kernel, out_shape=tuple(outs), in_specs...  19.8 us
    all_to_all x1, blocking collectives, per_device_paired(): lax.all_to_all(jnp.broadcast_to(tile, (8 * n, 8, 128)), everyone, 0, 0)  12.4 us
    ppermute x6, starting transfers between devices, along_z(): return lax.ppermute(value, 'src', [(i, i ^ k) for i in range(n)])  9.3 us
    ppermute x6, starting transfers between devices, swap_x(): return lax.ppermute(value, 'gx', [(0, 1), (1, 0)])  7.76 us
    ppermute x6, waiting for transfers between devices, along_z(): return lax.ppermute(value, 'src', [(i, i ^ k) for i in range(n)])  6.25 us
    ppermute x6, waiting for transfers between devices, swap_x(): return lax.ppermute(value, 'gx', [(0, 1), (1, 0)])  4.81 us
    ppermute x3, starting transfers between devices, across_y(): return lax.ppermute(value, 'gy', [(i, (i + 2) % 4) for i in range(4)])  4.75 us
    ppermute x3, waiting for transfers between devices, across_y(): return lax.ppermute(value, 'gy', [(i, (i + 2) % 4) for i in range(4)])  3.48 us
  transfers between devices with their start and end apart: 18, of which 12 were waited for; matrix products, arithmetic and copies ran while one was open for 0% of the time, Pallas kernels for 10%

profile of v13, /device:TPU:0, one launch (start us, length us, event | category | flops | bytes accessed | tf_op | source)
XLA Modules:
  0.0 72.5 jit_solution(14066995012973670607)
XLA Ops:
  0.6 2.0 %shard_map.122 = (f32[4,32,128]{2,1,0:T(8,128)}, f32[28,32,128]{2,1,0:T(8,128)}) custom-call(f32[4,8,32,128]{3,2,1,0:T(8,128)} %refs_0_.2, s32[8,32,128]{2,1,0:T(8,128)} %refs_1_.2, f32[8,32,32]{2,1,0:T(8,128)} %vk.5, f32[8,32,32]{2,1,0:T(8,128)} %va.5), custom_call_target="tpu_custom_call" | custom-call | tf_op jit(solution)/shard_map/pallas_call | solution.py:715
  2.7 3.0 %collective-permute-start = (f32[28,32,128]{2,1,0:T(8,128)}, f32[28,32,128]{2,1,0:T(8,128)S(1)}, u32[]{:S(2)}, u32[]{:S(2)}) collective-permute-start(f32[28,32,128]{2,1,0:T(8,128)} %get-tuple-element.28), channel_id=1, source_target_pairs={{0,4},{4,0},{1,5},{5,1},{2,6},{6,2},{3,7},{7,3},{8,12},{12,8},{9,1... | collective-permute-start | bytes 1376264 | tf_op jit(solution)/shard_map/ppermute | solution.py:745
  5.7 3.6 %collective-permute-start.3 = (f32[4,32,128]{2,1,0:T(8,128)}, f32[4,32,128]{2,1,0:T(8,128)S(1)}, u32[]{:S(2)}, u32[]{:S(2)}) collective-permute-start(f32[4,32,128]{2,1,0:T(8,128)} %get-tuple-element.29), channel_id=1, source_target_pairs={{0,24},{8,16},{16,8},{24,0},{1,25},{9,17},{17,9},{25,1},{2,26},{10... | collective-permute-start | bytes 196616 | tf_op jit(solution)/shard_map/ppermute | solution.py:751
  10.7 2.1 %shard_map.121 = (f32[16,72,128]{2,1,0:T(8,128)S(1)}, f32[1,128]{1,0:T(1,128)S(1)}) custom-call(s32[1,1024]{1,0:T(1,128)S(1)} %bitcast.1, f32[1]{0:T(128)S(6)} %copy.13.beta_prev), custom_call_target="tpu_custom_call" | custom-call | flops 301989888 | bytes 589824 | tf_op jit(solution)/shard_map/pallas_call | solution.py:715
  12.8 2.0 %collective-permute-done.2.refs_1_ = f32[4,32,128]{2,1,0:T(8,128)S(1)} collective-permute-done((f32[4,32,128]{2,1,0:T(8,128)}, f32[4,32,128]{2,1,0:T(8,128)S(1)}, u32[]{:S(2)}, u32[]{:S(2)}) %collective-permute-start.2) | collective-permute-done | bytes 65568 | tf_op jit(solution)/shard_map/ppermute | solution.py:751
  15.5 0.9 %collective-permute-done.refs_2_.refs_1_ = f32[28,32,128]{2,1,0:T(8,128)S(1)} collective-permute-done((f32[28,32,128]{2,1,0:T(8,128)}, f32[28,32,128]{2,1,0:T(8,128)S(1)}, u32[]{:S(2)}, u32[]{:S(2)}) %collective-permute-start) | collective-permute-done | bytes 458784 | tf_op jit(solution)/shard_map/ppermute | solution.py:745
  17.5 3.7 %collective-permute-done.5.refs_2_ = f32[12,32,128]{2,1,0:T(8,128)S(1)} collective-permute-done((f32[12,32,128]{2,1,0:T(8,128)S(1)}, f32[12,32,128]{2,1,0:T(8,128)S(1)}, u32[]{:S(2)}, u32[]{:S(2)}) %collective-permute-start.5) | collective-permute-done | bytes 196640 | tf_op jit(solution)/shard_map/ppermute | solution.py:745
  21.7 1.6 %collective-permute-start.6 = (f32[2,4,24,128]{3,2,1,0:T(8,128)S(1)}, f32[2,4,24,128]{3,2,1,0:T(8,128)S(1)}, u32[]{:S(2)}, u32[]{:S(2)}) collective-permute-start(f32[2,4,24,128]{3,2,1,0:T(8,128)S(1)} %shard_map.127.refs_2_), channel_id=1, source_target_pairs={{0,2},{1,3},{2,0},{3,1},{4,6},{5,7},{6,4},{7,5},{8,10},{9,11},{10,... | collective-permute-start | bytes 294920 | tf_op jit(solution)/shard_map/ppermute | solution.py:771
  23.6 1.6 %collective-permute-start.8 = (f32[2,4,24,128]{3,2,1,0:T(8,128)S(1)}, f32[2,4,24,128]{3,2,1,0:T(8,128)S(1)}, u32[]{:S(2)}, u32[]{:S(2)}) collective-permute-start(f32[2,4,24,128]{3,2,1,0:T(8,128)S(1)} %shard_map.128.refs_6_), channel_id=1, source_target_pairs={{0,2},{1,3},{2,0},{3,1},{4,6},{5,7},{6,4},{7,5},{8,10},{9,11},{10,... | collective-permute-start | bytes 294920 | tf_op jit(solution)/shard_map/ppermute | solution.py:771
  25.2 2.3 %shard_map.129 = (f32[18,72,128]{2,1,0:T(8,128)S(1)}, f32[16,72,128]{2,1,0:T(8,128)S(1)}, f32[17,72,128]{2,1,0:T(8,128)S(1)}, f32[16,72,128]{2,1,0:T(8,128)S(1)}...) custom-call(f32[16]{0:T(128)S(1)} %copy-done.6, f32[16]{0:T(128)S(1)} %copy-done.7, ...), custom_call_target="tpu_custom_call" | custom-call | flops 1000000000 | bytes 67108864 | tf_op jit(solution)/shard_map/pallas_call | solution.py:715
  29.1 4.4 %shard_map.131 = (f32[18,72,128]{2,1,0:T(8,128)S(1)}, f32[16,72,128]{2,1,0:T(8,128)S(1)}, f32[4,32,128]{2,1,0:T(8,128)S(1)}) custom-call(f32[16,72,128]{2,1,0:T(8,128)S(1)} %get-tuple-element.38.diag, f32[17,72,128]{2,1,0:T(8,128)S(1)} %get-tuple-element.39.fx, f32[16,72,128]{2,1,0:T(8,128)S(1)} %get-tuple-element.40.fy, ...), custom_call_target="tpu_custom_call" | custom-call | tf_op jit(solution)/shard_map/pallas_call | solution.py:715
  33.5 1.6 %collective-permute-start.9 = (f32[4,32,128]{2,1,0:T(8,128)S(1)}, f32[4,32,128]{2,1,0:T(8,128)S(1)}, u32[]{:S(2)}, u32[]{:S(2)}) collective-permute-start(f32[4,32,128]{2,1,0:T(8,128)S(1)} %get-tuple-element.45.sent), channel_id=1, source_target_pairs={{0,2},{1,3},{2,0},{3,1},{4,6},{5,7},{6,4},{7,5},{8,10},{9,11},{10,... | collective-permute-start | bytes 196616 | tf_op jit(solution)/shard_map/ppermute | solution.py:771
  35.1 2.7 %collective-permute-done.9.came = f32[4,32,128]{2,1,0:T(8,128)S(1)} collective-permute-done((f32[4,32,128]{2,1,0:T(8,128)S(1)}, f32[4,32,128]{2,1,0:T(8,128)S(1)}, u32[]{:S(2)}, u32[]{:S(2)}) %collective-permute-start.9) | collective-permute-done | bytes 65568 | tf_op jit(solution)/shard_map/ppermute | solution.py:771
  37.8 4.2 %shard_map.132 = (f32[2,16,32,128]{3,2,1,0:T(8,128)S(1)}, f32[2,16,32,128]{3,2,1,0:T(8,128)S(1)}) custom-call(f32[18,72,128]{2,1,0:T(8,128)S(1)} %get-tuple-element.43.phi, f32[16,72,128]{2,1,0:T(8,128)S(1)} %get-tuple-element.44.change, f32[16,72,128]{2,1,0:T(8,128)S(1)} %get-tuple-element.38.diag, f32[17,72,128]{2,1,0:T(8,128)S(1)} %get-tuple-element.39.fx, ...), custom_call_target="tpu_custom_call" | custom-call | tf_op jit(solution)/shard_map/pallas_call | solution.py:715
  42.1 1.9 %collective-permute-done.10.came.refs_1_ = f32[2,16,32,128]{3,2,1,0:T(8,128)S(1)} collective-permute-done((f32[2,16,32,128]{3,2,1,0:T(8,128)S(1)}, f32[2,16,32,128]{3,2,1,0:T(8,128)S(1)}, u32[]{:S(2)}, u32[]{:S(2)}) %collective-permute-start.10) | collective-permute-done | bytes 524320 | tf_op jit(solution)/shard_map/ppermute | solution.py:748
  44.3 1.2 %collective-permute-start.11 = (f32[1,2,2,32,128]{4,3,2,1,0:T(8,128)S(1)}, f32[1,2,2,32,128]{4,3,2,1,0:T(8,128)S(1)}, u32[]{:S(2)}, u32[]{:S(2)}) collective-permute-start(f32[1,2,2,32,128]{4,3,2,1,0:T(8,128)S(1)} %shard_map.134.refs_2_), channel_id=1, source_target_pairs={{0,4},{4,0},{1,5},{5,1},{2,6},{6,2},{3,7},{7,3},{8,12},{12,8},{9,1... | collective-permute-start | bytes 196616 | tf_op jit(solution)/shard_map/ppermute | solution.py:745
  46.5 1.2 %collective-permute-start.16 = (f32[1,2,2,32,128]{4,3,2,1,0:T(8,128)S(1)}, f32[1,2,2,32,128]{4,3,2,1,0:T(8,128)S(1)}, u32[]{:S(2)}, u32[]{:S(2)}) collective-permute-start(f32[1,2,2,32,128]{4,3,2,1,0:T(8,128)S(1)} %shard_map.135.refs_2_), channel_id=1, source_target_pairs={{0,4},{4,0},{1,5},{5,1},{2,6},{6,2},{3,7},{7,3},{8,12},{12,8},{9,1... | collective-permute-start | bytes 196616 | tf_op jit(solution)/shard_map/ppermute | solution.py:745
  47.9 1.0 %collective-permute-start.15 = (f32[1,2,2,32,128]{4,3,2,1,0:T(8,128)S(1)}, f32[1,2,2,32,128]{4,3,2,1,0:T(8,128)S(1)}, u32[]{:S(2)}, u32[]{:S(2)}) collective-permute-start(f32[1,2,2,32,128]{4,3,2,1,0:T(8,128)S(1)} %shard_map.136.refs_2_), channel_id=1, source_target_pairs={{0,4},{4,0},{1,5},{5,1},{2,6},{6,2},{3,7},{7,3},{8,12},{12,8},{9,1... | collective-permute-start | bytes 196616 | tf_op jit(solution)/shard_map/ppermute | solution.py:745
  49.3 2.2 %collective-permute-start.12 = (f32[2,2,32,128]{3,2,1,0:T(8,128)S(1)}, f32[2,2,32,128]{3,2,1,0:T(8,128)S(1)}, u32[]{:S(2)}, u32[]{:S(2)}) collective-permute-start(f32[2,2,32,128]{3,2,1,0:T(8,128)S(1)} %shard_map.138), channel_id=1, source_target_pairs={{0,16},{8,24},{16,0},{24,8},{1,17},{9,25},{17,1},{25,9},{2,18},{10... | collective-permute-start | bytes 196616 | tf_op jit(solution)/shard_map/ppermute | solution.py:751
  51.5 2.7 %collective-permute-start.14 = (f32[2,2,32,128]{3,2,1,0:T(8,128)S(1)}, f32[2,2,32,128]{3,2,1,0:T(8,128)S(1)}, u32[]{:S(2)}, u32[]{:S(2)}) collective-permute-start(f32[2,2,32,128]{3,2,1,0:T(8,128)S(1)} %shard_map.139), channel_id=1, source_target_pairs={{0,24},{8,16},{16,8},{24,0},{1,25},{9,17},{17,9},{25,1},{2,26},{10... | collective-permute-start | bytes 196616 | tf_op jit(solution)/shard_map/ppermute | solution.py:751
  54.3 2.3 %collective-permute-done.12.refs_0_ = f32[2,2,32,128]{3,2,1,0:T(8,128)S(1)} collective-permute-done((f32[2,2,32,128]{3,2,1,0:T(8,128)S(1)}, f32[2,2,32,128]{3,2,1,0:T(8,128)S(1)}, u32[]{:S(2)}, u32[]{:S(2)}) %collective-permute-start.12) | collective-permute-done | bytes 65568 | tf_op jit(solution)/shard_map/ppermute | solution.py:751
  56.6 1.2 %collective-permute-done.14.refs_1_ = f32[2,2,32,128]{3,2,1,0:T(8,128)S(1)} collective-permute-done((f32[2,2,32,128]{3,2,1,0:T(8,128)S(1)}, f32[2,2,32,128]{3,2,1,0:T(8,128)S(1)}, u32[]{:S(2)}, u32[]{:S(2)}) %collective-permute-start.14) | collective-permute-done | bytes 65568 | tf_op jit(solution)/shard_map/ppermute | solution.py:751
  59.1 12.4 %all_to_all.5.tiles = f32[32,8,128]{2,1,0:T(8,128)S(1)} all-to-all(f32[32,8,128]{2,1,0:T(8,128)S(1)} %broadcast_in_dim.3), channel_id=1, replica_groups=mesh['src'=4,'gx'=2,'gy'=4] {'src','gx','gy'}, dimensions={0} | all-to-all | bytes 262144 | tf_op jit(solution)/shard_map/all_to_all | solution.py:832
  71.5 1.0 %shard_map.144 = (f32[8,32,32]{2,1,0:T(8,128)}, f32[8,32,32]{2,1,0:T(8,128)}, f32[2]{0:T(128)}) custom-call(f32[32,8,128]{2,1,0:T(8,128)S(1)} %all_to_all.5.tiles, f32[8,32,32]{2,1,0:T(8,128)S(1)} %get-tuple-element.49.w_k, f32[8,32,32]{2,1,0:T(8,128)S(1)} %get-tuple-element.50.w_a, f32[8,32,32]{2,1,0:T(8,128)S(1)} %copy-done, f32[8,32,32]{2,1,0:T(8,128)S(1)} %copy-done.1), custom_call_target="tpu_custom_call" | custom-call | tf_op jit(solution)/shard_map/pallas_call | solution.py:715
  (56 shorter events, 8.2 us)
Async XLA Ops:
  2.6 8.1 %copy-start.8 = (s32[1024]{0:T(1024)S(1)}, s32[1024]{0:T(1024)}, u32[]{:S(2)}) copy-start(s32[1024]{0:T(1024)} %param.14) | copy-start | bytes 12292
  2.7 13.7 %collective-permute-start = (f32[28,32,128]{2,1,0:T(8,128)}, f32[28,32,128]{2,1,0:T(8,128)S(1)}, u32[]{:S(2)}, u32[]{:S(2)}) collective-permute-start(f32[28,32,128]{2,1,0:T(8,128)} %get-tuple-element.28), channel_id=1, source_target_pairs={{0,4},{4,0},{1,5},{5,1},{2,6},{6,2},{3,7},{7,3},{8,12},{12,8},{9,1... | collective-permute-start | bytes 1376264 | tf_op jit(solution)/shard_map/ppermute | solution.py:745
  5.7 7.2 %collective-permute-start.3 = (f32[4,32,128]{2,1,0:T(8,128)}, f32[4,32,128]{2,1,0:T(8,128)S(1)}, u32[]{:S(2)}, u32[]{:S(2)}) collective-permute-start(f32[4,32,128]{2,1,0:T(8,128)} %get-tuple-element.29), channel_id=1, source_target_pairs={{0,24},{8,16},{16,8},{24,0},{1,25},{9,17},{17,9},{25,1},{2,26},{10... | collective-permute-start | bytes 196616 | tf_op jit(solution)/shard_map/ppermute | solution.py:751
  9.3 5.6 %collective-permute-start.2 = (f32[4,32,128]{2,1,0:T(8,128)}, f32[4,32,128]{2,1,0:T(8,128)S(1)}, u32[]{:S(2)}, u32[]{:S(2)}) collective-permute-start(f32[4,32,128]{2,1,0:T(8,128)} %get-tuple-element.29), channel_id=1, source_target_pairs={{0,16},{8,24},{16,0},{24,8},{1,17},{9,25},{17,1},{25,9},{2,18},{10... | collective-permute-start | bytes 196616 | tf_op jit(solution)/shard_map/ppermute | solution.py:751
  9.3 5.6 %collective-permute-start.1 = (f32[4,32,128]{2,1,0:T(8,128)}, f32[4,32,128]{2,1,0:T(8,128)S(1)}, u32[]{:S(2)}, u32[]{:S(2)}) collective-permute-start(f32[4,32,128]{2,1,0:T(8,128)} %get-tuple-element.29), channel_id=1, source_target_pairs={{0,8},{8,0},{16,24},{24,16},{1,9},{9,1},{17,25},{25,17},{2,10},{10... | collective-permute-start | bytes 196616 | tf_op jit(solution)/shard_map/ppermute | solution.py:751
  12.8 3.6 %copy-start.2 = (f32[4,8,32,128]{3,2,1,0:T(8,128)S(1)}, f32[4,8,32,128]{3,2,1,0:T(8,128)}, u32[]{:S(2)}) copy-start(f32[4,8,32,128]{3,2,1,0:T(8,128)} %refs_0_.2) | copy-start | bytes 1572868
  15.0 6.3 %collective-permute-start.5 = (f32[12,32,128]{2,1,0:T(8,128)S(1)}, f32[12,32,128]{2,1,0:T(8,128)S(1)}, u32[]{:S(2)}, u32[]{:S(2)}) collective-permute-start(f32[12,32,128]{2,1,0:T(8,128)S(1)} %shard_map.123.refs_3_.joined), channel_id=1, source_target_pairs={{0,4},{4,0},{1,5},{5,1},{2,6},{6,2},{3,7},{7,3},{8,12},{12,8},{9,1... | collective-permute-start | bytes 589832 | tf_op jit(solution)/shard_map/ppermute | solution.py:745
  17.0 4.7 %collective-permute-start.4 = (f32[2,16,32,128]{3,2,1,0:T(8,128)S(1)}, f32[2,16,32,128]{3,2,1,0:T(8,128)S(1)}, u32[]{:S(2)}, u32[]{:S(2)}) collective-permute-start(f32[2,16,32,128]{3,2,1,0:T(8,128)S(1)} %get-tuple-element.32.refs_1_.refs_3_), channel_id=1, source_target_pairs={{0,1},{1,0},{2,3},{3,2},{4,5},{5,4},{6,7},{7,6},{8,9},{9,8},{10,11... | collective-permute-start | bytes 1572872 | tf_op jit(solution)/shard_map/ppermute | solution.py:748
  21.6 2.0 %collective-permute-start.7 = (f32[2,16,32,128]{3,2,1,0:T(8,128)S(1)}, f32[2,16,32,128]{3,2,1,0:T(8,128)S(1)}, u32[]{:S(2)}, u32[]{:S(2)}) collective-permute-start(f32[2,16,32,128]{3,2,1,0:T(8,128)S(1)} %shard_map.126.refs_3_.refs_0_.vector), channel_id=1, source_target_pairs={{0,1},{1,0},{2,3},{3,2},{4,5},{5,4},{6,7},{7,6},{8,9},{9,8},{10,11... | collective-permute-start | bytes 1572872 | tf_op jit(solution)/shard_map/ppermute | solution.py:748
  21.7 3.5 %copy-start.6 = (f32[16]{0:T(128)S(1)}, f32[16]{0:T(128)}, u32[]{:S(2)}) copy-start(f32[16]{0:T(128)} %kap_table.1) | copy-start | bytes 196
  21.7 3.4 %copy-start.7 = (f32[16]{0:T(128)S(1)}, f32[16]{0:T(128)}, u32[]{:S(2)}) copy-start(f32[16]{0:T(128)} %abs_table.1) | copy-start | bytes 196
  21.7 5.8 %collective-permute-start.6 = (f32[2,4,24,128]{3,2,1,0:T(8,128)S(1)}, f32[2,4,24,128]{3,2,1,0:T(8,128)S(1)}, u32[]{:S(2)}, u32[]{:S(2)}) collective-permute-start(f32[2,4,24,128]{3,2,1,0:T(8,128)S(1)} %shard_map.127.refs_2_), channel_id=1, source_target_pairs={{0,2},{1,3},{2,0},{3,1},{4,6},{5,7},{6,4},{7,5},{8,10},{9,11},{10,... | collective-permute-start | bytes 294920 | tf_op jit(solution)/shard_map/ppermute | solution.py:771
  23.6 5.5 %collective-permute-start.8 = (f32[2,4,24,128]{3,2,1,0:T(8,128)S(1)}, f32[2,4,24,128]{3,2,1,0:T(8,128)S(1)}, u32[]{:S(2)}, u32[]{:S(2)}) collective-permute-start(f32[2,4,24,128]{3,2,1,0:T(8,128)S(1)} %shard_map.128.refs_6_), channel_id=1, source_target_pairs={{0,2},{1,3},{2,0},{3,1},{4,6},{5,7},{6,4},{7,5},{8,10},{9,11},{10,... | collective-permute-start | bytes 294920 | tf_op jit(solution)/shard_map/ppermute | solution.py:771
  33.5 4.3 %collective-permute-start.9 = (f32[4,32,128]{2,1,0:T(8,128)S(1)}, f32[4,32,128]{2,1,0:T(8,128)S(1)}, u32[]{:S(2)}, u32[]{:S(2)}) collective-permute-start(f32[4,32,128]{2,1,0:T(8,128)S(1)} %get-tuple-element.45.sent), channel_id=1, source_target_pairs={{0,2},{1,3},{2,0},{3,1},{4,6},{5,7},{6,4},{7,5},{8,10},{9,11},{10,... | collective-permute-start | bytes 196616 | tf_op jit(solution)/shard_map/ppermute | solution.py:771
  42.0 2.0 %collective-permute-start.10 = (f32[2,16,32,128]{3,2,1,0:T(8,128)S(1)}, f32[2,16,32,128]{3,2,1,0:T(8,128)S(1)}, u32[]{:S(2)}, u32[]{:S(2)}) collective-permute-start(f32[2,16,32,128]{3,2,1,0:T(8,128)S(1)} %get-tuple-element.47), channel_id=1, source_target_pairs={{0,1},{1,0},{2,3},{3,2},{4,5},{5,4},{6,7},{7,6},{8,9},{9,8},{10,11... | collective-permute-start | bytes 1572872 | tf_op jit(solution)/shard_map/ppermute | solution.py:748
  44.3 5.0 %collective-permute-start.11 = (f32[1,2,2,32,128]{4,3,2,1,0:T(8,128)S(1)}, f32[1,2,2,32,128]{4,3,2,1,0:T(8,128)S(1)}, u32[]{:S(2)}, u32[]{:S(2)}) collective-permute-start(f32[1,2,2,32,128]{4,3,2,1,0:T(8,128)S(1)} %shard_map.134.refs_2_), channel_id=1, source_target_pairs={{0,4},{4,0},{1,5},{5,1},{2,6},{6,2},{3,7},{7,3},{8,12},{12,8},{9,1... | collective-permute-start | bytes 196616 | tf_op jit(solution)/shard_map/ppermute | solution.py:745
  45.5 6.0 %collective-permute-start.13 = (f32[1,2,2,32,128]{4,3,2,1,0:T(8,128)S(1)}, f32[1,2,2,32,128]{4,3,2,1,0:T(8,128)S(1)}, u32[]{:S(2)}, u32[]{:S(2)}) collective-permute-start(f32[1,2,2,32,128]{4,3,2,1,0:T(8,128)S(1)} %shard_map.133.refs_2_), channel_id=1, source_target_pairs={{0,4},{4,0},{1,5},{5,1},{2,6},{6,2},{3,7},{7,3},{8,12},{12,8},{9,1... | collective-permute-start | bytes 196616 | tf_op jit(solution)/shard_map/ppermute | solution.py:745
  46.5 7.7 %collective-permute-start.16 = (f32[1,2,2,32,128]{4,3,2,1,0:T(8,128)S(1)}, f32[1,2,2,32,128]{4,3,2,1,0:T(8,128)S(1)}, u32[]{:S(2)}, u32[]{:S(2)}) collective-permute-start(f32[1,2,2,32,128]{4,3,2,1,0:T(8,128)S(1)} %shard_map.135.refs_2_), channel_id=1, source_target_pairs={{0,4},{4,0},{1,5},{5,1},{2,6},{6,2},{3,7},{7,3},{8,12},{12,8},{9,1... | collective-permute-start | bytes 196616 | tf_op jit(solution)/shard_map/ppermute | solution.py:745
  47.9 6.4 %collective-permute-start.15 = (f32[1,2,2,32,128]{4,3,2,1,0:T(8,128)S(1)}, f32[1,2,2,32,128]{4,3,2,1,0:T(8,128)S(1)}, u32[]{:S(2)}, u32[]{:S(2)}) collective-permute-start(f32[1,2,2,32,128]{4,3,2,1,0:T(8,128)S(1)} %shard_map.136.refs_2_), channel_id=1, source_target_pairs={{0,4},{4,0},{1,5},{5,1},{2,6},{6,2},{3,7},{7,3},{8,12},{12,8},{9,1... | collective-permute-start | bytes 196616 | tf_op jit(solution)/shard_map/ppermute | solution.py:745
  49.3 7.3 %collective-permute-start.12 = (f32[2,2,32,128]{3,2,1,0:T(8,128)S(1)}, f32[2,2,32,128]{3,2,1,0:T(8,128)S(1)}, u32[]{:S(2)}, u32[]{:S(2)}) collective-permute-start(f32[2,2,32,128]{3,2,1,0:T(8,128)S(1)} %shard_map.138), channel_id=1, source_target_pairs={{0,16},{8,24},{16,0},{24,8},{1,17},{9,25},{17,1},{25,9},{2,18},{10... | collective-permute-start | bytes 196616 | tf_op jit(solution)/shard_map/ppermute | solution.py:751
  51.5 6.2 %collective-permute-start.14 = (f32[2,2,32,128]{3,2,1,0:T(8,128)S(1)}, f32[2,2,32,128]{3,2,1,0:T(8,128)S(1)}, u32[]{:S(2)}, u32[]{:S(2)}) collective-permute-start(f32[2,2,32,128]{3,2,1,0:T(8,128)S(1)} %shard_map.139), channel_id=1, source_target_pairs={{0,24},{8,16},{16,8},{24,0},{1,25},{9,17},{17,9},{25,1},{2,26},{10... | collective-permute-start | bytes 196616 | tf_op jit(solution)/shard_map/ppermute | solution.py:751
  54.2 4.3 %collective-permute-start.17 = (f32[2,2,32,128]{3,2,1,0:T(8,128)S(1)}, f32[2,2,32,128]{3,2,1,0:T(8,128)S(1)}, u32[]{:S(2)}, u32[]{:S(2)}) collective-permute-start(f32[2,2,32,128]{3,2,1,0:T(8,128)S(1)} %shard_map.142), channel_id=1, source_target_pairs={{0,8},{8,0},{16,24},{24,16},{1,9},{9,1},{17,25},{25,17},{2,10},{10... | collective-permute-start | bytes 196616 | tf_op jit(solution)/shard_map/ppermute | solution.py:751
  54.3 4.2 %copy-start.4 = (f32[8,32,32]{2,1,0:T(8,128)S(1)}, f32[8,32,32]{2,1,0:T(8,128)}, u32[]{:S(2)}) copy-start(f32[8,32,32]{2,1,0:T(8,128)} %refs_6_.1) | copy-start | bytes 98308
  54.3 4.2 %copy-start.5 = (f32[8,32,32]{2,1,0:T(8,128)S(1)}, f32[8,32,32]{2,1,0:T(8,128)}, u32[]{:S(2)}) copy-start(f32[8,32,32]{2,1,0:T(8,128)} %refs_7_.1) | copy-start | bytes 98308
  (3 other events, 5.8 us)

commit v14 on v13

--- a/solution.py
+++ b/solution.py
@@ -359,21 +359,24 @@
         edges_of(fields.at[f], got.at[f], edge.at[f], y, c)
 
 
-def solve(b, bufs, diag, fx, fy, fz, unroll):
-    planes = b.shape[0]
+def solve(b, bufs, diag, fx, fy, fy_back, fz, y, unroll):
+    planes, rows, _ = b.shape
     _, pairs = chebyshev_scalars()
+    one = jnp.where(y >= 0, 1, 0)
+    at = pl.ds(HALO, rows)
     for step, (keep, push) in enumerate(pairs):
         src, dst = bufs[step % 2], bufs[(step + 1) % 2]
 
         def body(i, carry):
-            u = src[i + 1]
-            coef_y, coef_z = fy[i], fz[i]
+            u = src[i + 1, at, :]
+            coef_z = fz[i]
             left = b[i] - diag[i] * u
-            left = left + fx[i] * src[i] + fx[i + 1] * src[i + 2]
-            left = left + coef_y * shifted(u, -1, 0) + shifted(coef_y * u, 1, 0)
+            left = left + fx[i] * src[i, at, :] + fx[i + 1] * src[i + 2, at, :]
+            left = left + fy[i] * src[i + 1, pl.ds(HALO + one, rows), :]
+            left = left + fy_back[i] * src[i + 1, pl.ds(HALO - one, rows), :]
             left = left + coef_z * shifted(u, -1, 1) + shifted(coef_z * u, 1, 1)
-            change = u if step == 0 else u - dst[i + 1]
-            dst[i + 1] = u + keep * change + push * left
+            change = u if step == 0 else u - dst[i + 1, at, :]
+            dst[i + 1, at, :] = u + keep * change + push * left
             return carry
 
         lax.fori_loop(0, planes, body, 0, unroll=unroll)
@@ -406,6 +409,15 @@
         blank = jnp.zeros(ref.shape[1:], jnp.float32)
         ref[0] = blank
         ref[ref.shape[0] - 1] = blank
+
+
+def blank_rim(*refs):
+    blank_ends(*refs)
+    for ref in refs:
+        planes, rows, lanes = ref.shape
+        none = jnp.zeros((planes, HALO, lanes), jnp.float32)
+        ref[:, pl.ds(0, HALO), :] = none
+        ref[:, pl.ds(rows - HALO, HALO), :] = none
 
 
 def owned_rows(shape, base, count):
@@ -467,7 +479,7 @@
     sums[0], sums[1] = lax.fori_loop(0, planes, set_up, (zero, zero), unroll=4)
 
 
-def halo_kernel(kap_table, abs_table, edge, kap, diag_in, fx_in, fy_in, fz_in, diag, fx, fy, fz):
+def halo_kernel(kap_table, abs_table, edge, kap, diag_in, fx_in, fy_in, fz_in, diag, fx, fy, fy_back, fz):
     _, _, y, _ = places(2)
     planes, rows, lanes = diag.shape
     for ref, old in ((diag, diag_in), (fx, fx_in), (fy, fy_in), (fz, fz_in)):
@@ -502,9 +514,15 @@
         fy[i, beside_it, :] = fy_in[i, beside_it, :] + face_up
         diag[i, beside_it, :] = diag_in[i, beside_it, :] + face_up + face_down
 
+    def turn(i, carry):
+        fy_back[i] = shifted(fy[i], 1, 0)
+        return carry
+
+    lax.fori_loop(0, planes, turn, 0, unroll=4)
+
 
 def first_kernel(
-    diag, fx, fy, fz, count, sums, mine, got_photon, vector, got_vector, photon_edge, edge,
+    diag, fx, fy, fy_back, fz, count, sums, mine, got_photon, vector, got_vector, photon_edge, edge,
     phi, change, message,
     vk, va, b, buf_a, buf_b,
 ):
@@ -514,7 +532,9 @@
     framed(phi, 1, mine, got_photon.at[0], photon_edge.at[0], y, c)
     framed(vk, 1, vector.at[0], got_vector.at[0], edge.at[0], y, c)
     framed(va, 0, vector.at[1], got_vector.at[1], edge.at[1], y, c)
-    blank_ends(phi, vk, buf_a, buf_b)
+    blank_ends(phi, vk)
+    blank_rim(buf_a, buf_b)
+    at = pl.ds(HALO, rows)
     theta, _ = chebyshev_scalars()
 
     def set_up(i, carry):
@@ -526,15 +546,15 @@
             total = total + flow + jnp.where(first, 0.5 * v * p, -shifted(flow, 1, axis))
         total = -(va[i] * p + total)
         b[i] = total
-        buf_a[i + 1] = total * (1.0 / theta)
+        buf_a[i + 1, at, :] = total * (1.0 / theta)
         return carry
 
     lax.fori_loop(0, planes, set_up, 0, unroll=4)
-    found = solve(b, (buf_a, buf_b), diag, fx, fy, fz, UNROLL)
+    found = solve(b, (buf_a, buf_b), diag, fx, fy, fy_back, fz, y, UNROLL)
     owned = owned_rows((rows, lanes), HALO * y, 2 * cy)
 
     def add_up(i, carry):
-        u = found[i + 1]
+        u = found[i + 1, at, :]
         change[i] = u
         part = jnp.where(owned, count[i], 0.0) * u
         return carry[0] + folded(part), carry[1] + folded(part * phi[i + 1])
@@ -544,13 +564,13 @@
     first = (2 * cy - HALO) * (1 - y) + HALO * y
     for g, part in enumerate((sums[0], seen, cross, sums[1])):
         message[g, pl.ds(0, GROUP * REACH), :] = packed_edges(
-            [near_rows(found, 1 + GROUP * g + j, first, y) for j in range(GROUP)]
+            [near_rows(found, 1 + GROUP * g + j, HALO + first, y) for j in range(GROUP)]
         )
         message[g, pl.ds(GROUP * REACH, 8), :] = part
 
 
 def second_kernel(
-    phi, change, diag, fx, fy, fz, count, sent, came,
+    phi, change, diag, fx, fy, fy_back, fz, count, sent, came,
     own, message,
     b, buf_a, buf_b, grad_k, grad_a,
     *, dets,
@@ -569,7 +589,8 @@
     part = seen_sum / total
     level = (cross - part * square) / (total * mean)
     inverse = 1.0 / mean
-    blank_ends(buf_a, buf_b)
+    blank_rim(buf_a, buf_b)
+    at = pl.ds(HALO, rows)
     theta, _ = chebyshev_scalars()
 
     def weighted(n, u, p):
@@ -578,7 +599,7 @@
     def set_up(i, carry):
         value = weighted(count[i], change[i], phi[i + 1])
         b[i] = value
-        buf_a[i + 1] = value * (1.0 / theta)
+        buf_a[i + 1, at, :] = value * (1.0 / theta)
         return carry
 
     lax.fori_loop(0, planes, set_up, 0, unroll=4)
@@ -586,12 +607,12 @@
         u = edge_tile(came[i // GROUP], i % GROUP, y)
         value = weighted(count[i, edge, :], u, phi[i + 1, edge, :])
         b[i, edge, :] = value
-        buf_a[i + 1, edge, :] = value * (1.0 / theta)
-    dual = solve(b, (buf_a, buf_b), diag, fx, fy, fz, UNROLL)
+        buf_a[i + 1, pl.ds(HALO + 2 * cy * (1 - y), HALO), :] = value * (1.0 / theta)
+    dual = solve(b, (buf_a, buf_b), diag, fx, fy, fy_back, fz, y, UNROLL)
 
     def product(i, carry):
-        p, u = phi[i + 1], dual[i + 1]
-        grad = (p - phi[i]) * (u - dual[i]) + (p - phi[i + 2]) * (u - dual[i + 2])
+        p, u = phi[i + 1], dual[i + 1, at, :]
+        grad = (p - phi[i]) * (u - dual[i, at, :]) + (p - phi[i + 2]) * (u - dual[i + 2, at, :])
         both = p * u
         for axis in range(2):
             flow = (p - beyond(p, 1, axis)) * (u - beyond(u, 1, axis))
@@ -788,27 +809,28 @@
     (vector_sent,) = run(vector_edge_kernel, edge, vector, vector_got, after=(sent,))
     frame, wide = (planes, rows, cz), (planes + 2, rows, cz)
     float_frame, float_wide = float_block(*frame), float_block(*wide)
+    rimmed = float_block(planes + 2, rows + 2 * HALO, cz)
     coefs = (f32(*frame), f32(planes + 1, rows, cz), f32(*frame), f32(*frame))
     kap, *partial, sums = run(
         stencil_kernel, (f32(*wide), *coefs, f32(2, 8, cz)),
         kappa_table, absorb_table, mine, fields, got, count, after=(vector_sent,), cost=long,
         smem=(0, 1), scratch=(float_frame,),
     )
-    diag, fx, fy, fz = run(
-        halo_kernel, coefs, kappa_table, absorb_table, photon_edge, kap, *partial, smem=(0, 1)
+    diag, fx, fy, fy_back, fz = run(
+        halo_kernel, (*coefs[:3], f32(*frame), coefs[3]), kappa_table, absorb_table, photon_edge, kap, *partial, smem=(0, 1)
     )
     phi, change, sent = run(
         first_kernel, (f32(*wide), f32(*frame), f32(4, GROUP * REACH + 8, cz)),
-        diag, fx, fy, fz, count, sums, mine, got, vector, vector_got,
+        diag, fx, fy, fy_back, fz, count, sums, mine, got, vector, vector_got,
         photon_edge, across_y(vector_sent),
-        scratch=(float_wide, float_frame, float_frame, float_wide, float_wide),
+        scratch=(float_wide, float_frame, float_frame, rimmed, rimmed),
     )
     heard = across_y(sent)
     own, message = run(
         functools.partial(second_kernel, dets=dets),
         (f32(2, planes, cy, cz), f32(2, planes, cy, cz)),
-        phi, change, diag, fx, fy, fz, count, sent, heard,
-        scratch=(float_frame, float_wide, float_wide, float_frame, float_frame),
+        phi, change, diag, fx, fy, fy_back, fz, count, sent, heard,
+        scratch=(float_frame, rimmed, rimmed, float_frame, float_frame),
     )
     piece = f32(2, groups, cy, cz)
     got = swap_core(message)

time: 72.6 us -> 73.4 us (1.011)
  Pallas kernels: 19.8 us -> 20.6 us
    pallas_call x24, Pallas kernels: 19.8 us -> 20.6 us  [run(): pl.pallas_call(body if waits else kernel, out_shape=tuple(outs), in_specs...]
where the time goes in v14:
time: 73.4 us; the launch traced here: 73.2 us
  starting transfers between devices  22 us (30%)
  Pallas kernels  20.6 us (28%)
  waiting for transfers between devices  16.6 us (23%)
  blocking collectives  12.4 us (17%)
  between operations  1.61 us (2%)
    pallas_call x24, Pallas kernels, run(): pl.pallas_call(body if waits else kernel, out_shape=tuple(outs), in_specs...  20.6 us
    all_to_all x1, blocking collectives, per_device_paired(): lax.all_to_all(jnp.broadcast_to(tile, (8 * n, 8, 128)), everyone, 0, 0)  12.4 us
    ppermute x6, starting transfers between devices, along_z(): return lax.ppermute(value, 'src', [(i, i ^ k) for i in range(n)])  9.3 us
    ppermute x6, starting transfers between devices, swap_x(): return lax.ppermute(value, 'gx', [(0, 1), (1, 0)])  7.76 us
    ppermute x6, waiting for transfers between devices, along_z(): return lax.ppermute(value, 'src', [(i, i ^ k) for i in range(n)])  6.25 us
    ppermute x6, waiting for transfers between devices, swap_x(): return lax.ppermute(value, 'gx', [(0, 1), (1, 0)])  4.81 us
    ppermute x3, starting transfers between devices, across_y(): return lax.ppermute(value, 'gy', [(i, (i + 2) % 4) for i in range(4)])  4.75 us
    ppermute x3, waiting for transfers between devices, across_y(): return lax.ppermute(value, 'gy', [(i, (i + 2) % 4) for i in range(4)])  3.42 us
  transfers between devices with their start and end apart: 18, of which 12 were waited for; matrix products, arithmetic and copies ran while one was open for 0% of the time, Pallas kernels for 10%

profile of v14, /device:TPU:0, one launch (start us, length us, event | category | flops | bytes accessed | tf_op | source)
XLA Modules:
  0.0 73.2 jit_solution(3975449818521247912)
XLA Ops:
  0.6 2.0 %shard_map.122 = (f32[4,32,128]{2,1,0:T(8,128)}, f32[28,32,128]{2,1,0:T(8,128)}) custom-call(f32[4,8,32,128]{3,2,1,0:T(8,128)} %refs_0_.2, s32[8,32,128]{2,1,0:T(8,128)} %refs_1_.2, f32[8,32,32]{2,1,0:T(8,128)} %vk.5, f32[8,32,32]{2,1,0:T(8,128)} %va.5), custom_call_target="tpu_custom_call" | custom-call | tf_op jit(solution)/shard_map/pallas_call | solution.py:736
  2.7 3.0 %collective-permute-start = (f32[28,32,128]{2,1,0:T(8,128)}, f32[28,32,128]{2,1,0:T(8,128)S(1)}, u32[]{:S(2)}, u32[]{:S(2)}) collective-permute-start(f32[28,32,128]{2,1,0:T(8,128)} %get-tuple-element.29), channel_id=1, source_target_pairs={{0,4},{4,0},{1,5},{5,1},{2,6},{6,2},{3,7},{7,3},{8,12},{12,8},{9,1... | collective-permute-start | bytes 1376264 | tf_op jit(solution)/shard_map/ppermute | solution.py:766
  5.7 3.6 %collective-permute-start.3 = (f32[4,32,128]{2,1,0:T(8,128)}, f32[4,32,128]{2,1,0:T(8,128)S(1)}, u32[]{:S(2)}, u32[]{:S(2)}) collective-permute-start(f32[4,32,128]{2,1,0:T(8,128)} %get-tuple-element.30), channel_id=1, source_target_pairs={{0,24},{8,16},{16,8},{24,0},{1,25},{9,17},{17,9},{25,1},{2,26},{10... | collective-permute-start | bytes 196616 | tf_op jit(solution)/shard_map/ppermute | solution.py:772
  10.7 2.1 %shard_map.121 = (f32[16,72,128]{2,1,0:T(8,128)S(1)}, f32[1,128]{1,0:T(1,128)S(1)}) custom-call(s32[1,1024]{1,0:T(1,128)S(1)} %bitcast.1, f32[1]{0:T(128)S(6)} %copy.13.beta_prev), custom_call_target="tpu_custom_call" | custom-call | flops 301989888 | bytes 589824 | tf_op jit(solution)/shard_map/pallas_call | solution.py:736
  12.8 2.0 %collective-permute-done.2.refs_1_ = f32[4,32,128]{2,1,0:T(8,128)S(1)} collective-permute-done((f32[4,32,128]{2,1,0:T(8,128)}, f32[4,32,128]{2,1,0:T(8,128)S(1)}, u32[]{:S(2)}, u32[]{:S(2)}) %collective-permute-start.2) | collective-permute-done | bytes 65568 | tf_op jit(solution)/shard_map/ppermute | solution.py:772
  15.5 0.9 %collective-permute-done.refs_2_.refs_1_ = f32[28,32,128]{2,1,0:T(8,128)S(1)} collective-permute-done((f32[28,32,128]{2,1,0:T(8,128)}, f32[28,32,128]{2,1,0:T(8,128)S(1)}, u32[]{:S(2)}, u32[]{:S(2)}) %collective-permute-start) | collective-permute-done | bytes 458784 | tf_op jit(solution)/shard_map/ppermute | solution.py:766
  17.5 3.7 %collective-permute-done.5.refs_2_ = f32[12,32,128]{2,1,0:T(8,128)S(1)} collective-permute-done((f32[12,32,128]{2,1,0:T(8,128)S(1)}, f32[12,32,128]{2,1,0:T(8,128)S(1)}, u32[]{:S(2)}, u32[]{:S(2)}) %collective-permute-start.5) | collective-permute-done | bytes 196640 | tf_op jit(solution)/shard_map/ppermute | solution.py:766
  21.7 1.6 %collective-permute-start.6 = (f32[2,4,24,128]{3,2,1,0:T(8,128)S(1)}, f32[2,4,24,128]{3,2,1,0:T(8,128)S(1)}, u32[]{:S(2)}, u32[]{:S(2)}) collective-permute-start(f32[2,4,24,128]{3,2,1,0:T(8,128)S(1)} %shard_map.127.refs_2_), channel_id=1, source_target_pairs={{0,2},{1,3},{2,0},{3,1},{4,6},{5,7},{6,4},{7,5},{8,10},{9,11},{10,... | collective-permute-start | bytes 294920 | tf_op jit(solution)/shard_map/ppermute | solution.py:792
  23.6 1.6 %collective-permute-start.8 = (f32[2,4,24,128]{3,2,1,0:T(8,128)S(1)}, f32[2,4,24,128]{3,2,1,0:T(8,128)S(1)}, u32[]{:S(2)}, u32[]{:S(2)}) collective-permute-start(f32[2,4,24,128]{3,2,1,0:T(8,128)S(1)} %shard_map.128.refs_6_), channel_id=1, source_target_pairs={{0,2},{1,3},{2,0},{3,1},{4,6},{5,7},{6,4},{7,5},{8,10},{9,11},{10,... | collective-permute-start | bytes 294920 | tf_op jit(solution)/shard_map/ppermute | solution.py:792
  25.2 2.3 %shard_map.129 = (f32[18,72,128]{2,1,0:T(8,128)S(1)}, f32[16,72,128]{2,1,0:T(8,128)S(1)}, f32[17,72,128]{2,1,0:T(8,128)S(1)}, f32[16,72,128]{2,1,0:T(8,128)S(1)}...) custom-call(f32[16]{0:T(128)S(1)} %copy-done.6, f32[16]{0:T(128)S(1)} %copy-done.7, ...), custom_call_target="tpu_custom_call" | custom-call | flops 1000000000 | bytes 67108864 | tf_op jit(solution)/shard_map/pallas_call | solution.py:736
  29.1 4.7 %shard_map.131 = (f32[18,72,128]{2,1,0:T(8,128)S(1)}, f32[16,72,128]{2,1,0:T(8,128)S(1)}, f32[4,32,128]{2,1,0:T(8,128)S(1)}) custom-call(f32[16,72,128]{2,1,0:T(8,128)S(1)} %get-tuple-element.39.diag, f32[17,72,128]{2,1,0:T(8,128)S(1)} %get-tuple-element.40.fx, f32[16,72,128]{2,1,0:T(8,128)S(1)} %get-tuple-element.41.fy, ...), custom_call_target="tpu_custom_call" | custom-call | tf_op jit(solution)/shard_map/pallas_call | solution.py:736
  33.8 1.6 %collective-permute-start.9 = (f32[4,32,128]{2,1,0:T(8,128)S(1)}, f32[4,32,128]{2,1,0:T(8,128)S(1)}, u32[]{:S(2)}, u32[]{:S(2)}) collective-permute-start(f32[4,32,128]{2,1,0:T(8,128)S(1)} %get-tuple-element.47.sent), channel_id=1, source_target_pairs={{0,2},{1,3},{2,0},{3,1},{4,6},{5,7},{6,4},{7,5},{8,10},{9,11},{10,... | collective-permute-start | bytes 196616 | tf_op jit(solution)/shard_map/ppermute | solution.py:792
  35.4 2.7 %collective-permute-done.9.came = f32[4,32,128]{2,1,0:T(8,128)S(1)} collective-permute-done((f32[4,32,128]{2,1,0:T(8,128)S(1)}, f32[4,32,128]{2,1,0:T(8,128)S(1)}, u32[]{:S(2)}, u32[]{:S(2)}) %collective-permute-start.9) | collective-permute-done | bytes 65568 | tf_op jit(solution)/shard_map/ppermute | solution.py:792
  38.1 4.6 %shard_map.132 = (f32[2,16,32,128]{3,2,1,0:T(8,128)S(1)}, f32[2,16,32,128]{3,2,1,0:T(8,128)S(1)}) custom-call(f32[18,72,128]{2,1,0:T(8,128)S(1)} %get-tuple-element.45.phi, f32[16,72,128]{2,1,0:T(8,128)S(1)} %get-tuple-element.46.change, f32[16,72,128]{2,1,0:T(8,128)S(1)} %get-tuple-element.39.diag, f32[17,72,128]{2,1,0:T(8,128)S(1)} %get-tuple-element.40.fx, ...), custom_call_target="tpu_custom_call" | custom-call | tf_op jit(solution)/shard_map/pallas_call | solution.py:736
  42.8 1.9 %collective-permute-done.10.came.refs_1_ = f32[2,16,32,128]{3,2,1,0:T(8,128)S(1)} collective-permute-done((f32[2,16,32,128]{3,2,1,0:T(8,128)S(1)}, f32[2,16,32,128]{3,2,1,0:T(8,128)S(1)}, u32[]{:S(2)}, u32[]{:S(2)}) %collective-permute-start.10) | collective-permute-done | bytes 524320 | tf_op jit(solution)/shard_map/ppermute | solution.py:769
  45.0 1.2 %collective-permute-start.11 = (f32[1,2,2,32,128]{4,3,2,1,0:T(8,128)S(1)}, f32[1,2,2,32,128]{4,3,2,1,0:T(8,128)S(1)}, u32[]{:S(2)}, u32[]{:S(2)}) collective-permute-start(f32[1,2,2,32,128]{4,3,2,1,0:T(8,128)S(1)} %shard_map.134.refs_2_), channel_id=1, source_target_pairs={{0,4},{4,0},{1,5},{5,1},{2,6},{6,2},{3,7},{7,3},{8,12},{12,8},{9,1... | collective-permute-start | bytes 196616 | tf_op jit(solution)/shard_map/ppermute | solution.py:766
  47.3 1.2 %collective-permute-start.16 = (f32[1,2,2,32,128]{4,3,2,1,0:T(8,128)S(1)}, f32[1,2,2,32,128]{4,3,2,1,0:T(8,128)S(1)}, u32[]{:S(2)}, u32[]{:S(2)}) collective-permute-start(f32[1,2,2,32,128]{4,3,2,1,0:T(8,128)S(1)} %shard_map.135.refs_2_), channel_id=1, source_target_pairs={{0,4},{4,0},{1,5},{5,1},{2,6},{6,2},{3,7},{7,3},{8,12},{12,8},{9,1... | collective-permute-start | bytes 196616 | tf_op jit(solution)/shard_map/ppermute | solution.py:766
  48.6 1.0 %collective-permute-start.15 = (f32[1,2,2,32,128]{4,3,2,1,0:T(8,128)S(1)}, f32[1,2,2,32,128]{4,3,2,1,0:T(8,128)S(1)}, u32[]{:S(2)}, u32[]{:S(2)}) collective-permute-start(f32[1,2,2,32,128]{4,3,2,1,0:T(8,128)S(1)} %shard_map.136.refs_2_), channel_id=1, source_target_pairs={{0,4},{4,0},{1,5},{5,1},{2,6},{6,2},{3,7},{7,3},{8,12},{12,8},{9,1... | collective-permute-start | bytes 196616 | tf_op jit(solution)/shard_map/ppermute | solution.py:766
  50.1 2.2 %collective-permute-start.12 = (f32[2,2,32,128]{3,2,1,0:T(8,128)S(1)}, f32[2,2,32,128]{3,2,1,0:T(8,128)S(1)}, u32[]{:S(2)}, u32[]{:S(2)}) collective-permute-start(f32[2,2,32,128]{3,2,1,0:T(8,128)S(1)} %shard_map.138), channel_id=1, source_target_pairs={{0,16},{8,24},{16,0},{24,8},{1,17},{9,25},{17,1},{25,9},{2,18},{10... | collective-permute-start | bytes 196616 | tf_op jit(solution)/shard_map/ppermute | solution.py:772
  52.3 2.7 %collective-permute-start.14 = (f32[2,2,32,128]{3,2,1,0:T(8,128)S(1)}, f32[2,2,32,128]{3,2,1,0:T(8,128)S(1)}, u32[]{:S(2)}, u32[]{:S(2)}) collective-permute-start(f32[2,2,32,128]{3,2,1,0:T(8,128)S(1)} %shard_map.139), channel_id=1, source_target_pairs={{0,24},{8,16},{16,8},{24,0},{1,25},{9,17},{17,9},{25,1},{2,26},{10... | collective-permute-start | bytes 196616 | tf_op jit(solution)/shard_map/ppermute | solution.py:772
  55.1 2.3 %collective-permute-done.12.refs_0_ = f32[2,2,32,128]{3,2,1,0:T(8,128)S(1)} collective-permute-done((f32[2,2,32,128]{3,2,1,0:T(8,128)S(1)}, f32[2,2,32,128]{3,2,1,0:T(8,128)S(1)}, u32[]{:S(2)}, u32[]{:S(2)}) %collective-permute-start.12) | collective-permute-done | bytes 65568 | tf_op jit(solution)/shard_map/ppermute | solution.py:772
  57.3 1.2 %collective-permute-done.14.refs_1_ = f32[2,2,32,128]{3,2,1,0:T(8,128)S(1)} collective-permute-done((f32[2,2,32,128]{3,2,1,0:T(8,128)S(1)}, f32[2,2,32,128]{3,2,1,0:T(8,128)S(1)}, u32[]{:S(2)}, u32[]{:S(2)}) %collective-permute-start.14) | collective-permute-done | bytes 65568 | tf_op jit(solution)/shard_map/ppermute | solution.py:772
  59.9 12.4 %all_to_all.5.tiles = f32[32,8,128]{2,1,0:T(8,128)S(1)} all-to-all(f32[32,8,128]{2,1,0:T(8,128)S(1)} %broadcast_in_dim.3), channel_id=1, replica_groups=mesh['src'=4,'gx'=2,'gy'=4] {'src','gx','gy'}, dimensions={0} | all-to-all | bytes 262144 | tf_op jit(solution)/shard_map/all_to_all | solution.py:854
  72.2 1.0 %shard_map.144 = (f32[8,32,32]{2,1,0:T(8,128)}, f32[8,32,32]{2,1,0:T(8,128)}, f32[2]{0:T(128)}) custom-call(f32[32,8,128]{2,1,0:T(8,128)S(1)} %all_to_all.5.tiles, f32[8,32,32]{2,1,0:T(8,128)S(1)} %get-tuple-element.51.w_k, f32[8,32,32]{2,1,0:T(8,128)S(1)} %get-tuple-element.52.w_a, f32[8,32,32]{2,1,0:T(8,128)S(1)} %copy-done, f32[8,32,32]{2,1,0:T(8,128)S(1)} %copy-done.1), custom_call_target="tpu_custom_call" | custom-call | tf_op jit(solution)/shard_map/pallas_call | solution.py:736
  (56 shorter events, 8.2 us)
Async XLA Ops:
  2.6 8.1 %copy-start.8 = (s32[1024]{0:T(1024)S(1)}, s32[1024]{0:T(1024)}, u32[]{:S(2)}) copy-start(s32[1024]{0:T(1024)} %param.14) | copy-start | bytes 12292
  2.7 13.7 %collective-permute-start = (f32[28,32,128]{2,1,0:T(8,128)}, f32[28,32,128]{2,1,0:T(8,128)S(1)}, u32[]{:S(2)}, u32[]{:S(2)}) collective-permute-start(f32[28,32,128]{2,1,0:T(8,128)} %get-tuple-element.29), channel_id=1, source_target_pairs={{0,4},{4,0},{1,5},{5,1},{2,6},{6,2},{3,7},{7,3},{8,12},{12,8},{9,1... | collective-permute-start | bytes 1376264 | tf_op jit(solution)/shard_map/ppermute | solution.py:766
  5.7 7.2 %collective-permute-start.3 = (f32[4,32,128]{2,1,0:T(8,128)}, f32[4,32,128]{2,1,0:T(8,128)S(1)}, u32[]{:S(2)}, u32[]{:S(2)}) collective-permute-start(f32[4,32,128]{2,1,0:T(8,128)} %get-tuple-element.30), channel_id=1, source_target_pairs={{0,24},{8,16},{16,8},{24,0},{1,25},{9,17},{17,9},{25,1},{2,26},{10... | collective-permute-start | bytes 196616 | tf_op jit(solution)/shard_map/ppermute | solution.py:772
  9.3 5.6 %collective-permute-start.2 = (f32[4,32,128]{2,1,0:T(8,128)}, f32[4,32,128]{2,1,0:T(8,128)S(1)}, u32[]{:S(2)}, u32[]{:S(2)}) collective-permute-start(f32[4,32,128]{2,1,0:T(8,128)} %get-tuple-element.30), channel_id=1, source_target_pairs={{0,16},{8,24},{16,0},{24,8},{1,17},{9,25},{17,1},{25,9},{2,18},{10... | collective-permute-start | bytes 196616 | tf_op jit(solution)/shard_map/ppermute | solution.py:772
  9.3 5.6 %collective-permute-start.1 = (f32[4,32,128]{2,1,0:T(8,128)}, f32[4,32,128]{2,1,0:T(8,128)S(1)}, u32[]{:S(2)}, u32[]{:S(2)}) collective-permute-start(f32[4,32,128]{2,1,0:T(8,128)} %get-tuple-element.30), channel_id=1, source_target_pairs={{0,8},{8,0},{16,24},{24,16},{1,9},{9,1},{17,25},{25,17},{2,10},{10... | collective-permute-start | bytes 196616 | tf_op jit(solution)/shard_map/ppermute | solution.py:772
  12.8 3.6 %copy-start.2 = (f32[4,8,32,128]{3,2,1,0:T(8,128)S(1)}, f32[4,8,32,128]{3,2,1,0:T(8,128)}, u32[]{:S(2)}) copy-start(f32[4,8,32,128]{3,2,1,0:T(8,128)} %refs_0_.2) | copy-start | bytes 1572868
  15.0 6.3 %collective-permute-start.5 = (f32[12,32,128]{2,1,0:T(8,128)S(1)}, f32[12,32,128]{2,1,0:T(8,128)S(1)}, u32[]{:S(2)}, u32[]{:S(2)}) collective-permute-start(f32[12,32,128]{2,1,0:T(8,128)S(1)} %shard_map.123.refs_3_.joined), channel_id=1, source_target_pairs={{0,4},{4,0},{1,5},{5,1},{2,6},{6,2},{3,7},{7,3},{8,12},{12,8},{9,1... | collective-permute-start | bytes 589832 | tf_op jit(solution)/shard_map/ppermute | solution.py:766
  17.0 4.7 %collective-permute-start.4 = (f32[2,16,32,128]{3,2,1,0:T(8,128)S(1)}, f32[2,16,32,128]{3,2,1,0:T(8,128)S(1)}, u32[]{:S(2)}, u32[]{:S(2)}) collective-permute-start(f32[2,16,32,128]{3,2,1,0:T(8,128)S(1)} %get-tuple-element.33.refs_1_.refs_3_), channel_id=1, source_target_pairs={{0,1},{1,0},{2,3},{3,2},{4,5},{5,4},{6,7},{7,6},{8,9},{9,8},{10,11... | collective-permute-start | bytes 1572872 | tf_op jit(solution)/shard_map/ppermute | solution.py:769
  21.6 2.0 %collective-permute-start.7 = (f32[2,16,32,128]{3,2,1,0:T(8,128)S(1)}, f32[2,16,32,128]{3,2,1,0:T(8,128)S(1)}, u32[]{:S(2)}, u32[]{:S(2)}) collective-permute-start(f32[2,16,32,128]{3,2,1,0:T(8,128)S(1)} %shard_map.126.refs_3_.refs_0_.vector), channel_id=1, source_target_pairs={{0,1},{1,0},{2,3},{3,2},{4,5},{5,4},{6,7},{7,6},{8,9},{9,8},{10,11... | collective-permute-start | bytes 1572872 | tf_op jit(solution)/shard_map/ppermute | solution.py:769
  21.7 3.5 %copy-start.6 = (f32[16]{0:T(128)S(1)}, f32[16]{0:T(128)}, u32[]{:S(2)}) copy-start(f32[16]{0:T(128)} %kap_table.1) | copy-start | bytes 196
  21.7 3.4 %copy-start.7 = (f32[16]{0:T(128)S(1)}, f32[16]{0:T(128)}, u32[]{:S(2)}) copy-start(f32[16]{0:T(128)} %abs_table.1) | copy-start | bytes 196
  21.7 5.8 %collective-permute-start.6 = (f32[2,4,24,128]{3,2,1,0:T(8,128)S(1)}, f32[2,4,24,128]{3,2,1,0:T(8,128)S(1)}, u32[]{:S(2)}, u32[]{:S(2)}) collective-permute-start(f32[2,4,24,128]{3,2,1,0:T(8,128)S(1)} %shard_map.127.refs_2_), channel_id=1, source_target_pairs={{0,2},{1,3},{2,0},{3,1},{4,6},{5,7},{6,4},{7,5},{8,10},{9,11},{10,... | collective-permute-start | bytes 294920 | tf_op jit(solution)/shard_map/ppermute | solution.py:792
  23.6 5.5 %collective-permute-start.8 = (f32[2,4,24,128]{3,2,1,0:T(8,128)S(1)}, f32[2,4,24,128]{3,2,1,0:T(8,128)S(1)}, u32[]{:S(2)}, u32[]{:S(2)}) collective-permute-start(f32[2,4,24,128]{3,2,1,0:T(8,128)S(1)} %shard_map.128.refs_6_), channel_id=1, source_target_pairs={{0,2},{1,3},{2,0},{3,1},{4,6},{5,7},{6,4},{7,5},{8,10},{9,11},{10,... | collective-permute-start | bytes 294920 | tf_op jit(solution)/shard_map/ppermute | solution.py:792
  33.8 4.3 %collective-permute-start.9 = (f32[4,32,128]{2,1,0:T(8,128)S(1)}, f32[4,32,128]{2,1,0:T(8,128)S(1)}, u32[]{:S(2)}, u32[]{:S(2)}) collective-permute-start(f32[4,32,128]{2,1,0:T(8,128)S(1)} %get-tuple-element.47.sent), channel_id=1, source_target_pairs={{0,2},{1,3},{2,0},{3,1},{4,6},{5,7},{6,4},{7,5},{8,10},{9,11},{10,... | collective-permute-start | bytes 196616 | tf_op jit(solution)/shard_map/ppermute | solution.py:792
  42.8 2.0 %collective-permute-start.10 = (f32[2,16,32,128]{3,2,1,0:T(8,128)S(1)}, f32[2,16,32,128]{3,2,1,0:T(8,128)S(1)}, u32[]{:S(2)}, u32[]{:S(2)}) collective-permute-start(f32[2,16,32,128]{3,2,1,0:T(8,128)S(1)} %get-tuple-element.49), channel_id=1, source_target_pairs={{0,1},{1,0},{2,3},{3,2},{4,5},{5,4},{6,7},{7,6},{8,9},{9,8},{10,11... | collective-permute-start | bytes 1572872 | tf_op jit(solution)/shard_map/ppermute | solution.py:769
  45.0 5.0 %collective-permute-start.11 = (f32[1,2,2,32,128]{4,3,2,1,0:T(8,128)S(1)}, f32[1,2,2,32,128]{4,3,2,1,0:T(8,128)S(1)}, u32[]{:S(2)}, u32[]{:S(2)}) collective-permute-start(f32[1,2,2,32,128]{4,3,2,1,0:T(8,128)S(1)} %shard_map.134.refs_2_), channel_id=1, source_target_pairs={{0,4},{4,0},{1,5},{5,1},{2,6},{6,2},{3,7},{7,3},{8,12},{12,8},{9,1... | collective-permute-start | bytes 196616 | tf_op jit(solution)/shard_map/ppermute | solution.py:766
  46.2 6.0 %collective-permute-start.13 = (f32[1,2,2,32,128]{4,3,2,1,0:T(8,128)S(1)}, f32[1,2,2,32,128]{4,3,2,1,0:T(8,128)S(1)}, u32[]{:S(2)}, u32[]{:S(2)}) collective-permute-start(f32[1,2,2,32,128]{4,3,2,1,0:T(8,128)S(1)} %shard_map.133.refs_2_), channel_id=1, source_target_pairs={{0,4},{4,0},{1,5},{5,1},{2,6},{6,2},{3,7},{7,3},{8,12},{12,8},{9,1... | collective-permute-start | bytes 196616 | tf_op jit(solution)/shard_map/ppermute | solution.py:766
  47.3 7.7 %collective-permute-start.16 = (f32[1,2,2,32,128]{4,3,2,1,0:T(8,128)S(1)}, f32[1,2,2,32,128]{4,3,2,1,0:T(8,128)S(1)}, u32[]{:S(2)}, u32[]{:S(2)}) collective-permute-start(f32[1,2,2,32,128]{4,3,2,1,0:T(8,128)S(1)} %shard_map.135.refs_2_), channel_id=1, source_target_pairs={{0,4},{4,0},{1,5},{5,1},{2,6},{6,2},{3,7},{7,3},{8,12},{12,8},{9,1... | collective-permute-start | bytes 196616 | tf_op jit(solution)/shard_map/ppermute | solution.py:766
  48.6 6.4 %collective-permute-start.15 = (f32[1,2,2,32,128]{4,3,2,1,0:T(8,128)S(1)}, f32[1,2,2,32,128]{4,3,2,1,0:T(8,128)S(1)}, u32[]{:S(2)}, u32[]{:S(2)}) collective-permute-start(f32[1,2,2,32,128]{4,3,2,1,0:T(8,128)S(1)} %shard_map.136.refs_2_), channel_id=1, source_target_pairs={{0,4},{4,0},{1,5},{5,1},{2,6},{6,2},{3,7},{7,3},{8,12},{12,8},{9,1... | collective-permute-start | bytes 196616 | tf_op jit(solution)/shard_map/ppermute | solution.py:766
  50.1 7.3 %collective-permute-start.12 = (f32[2,2,32,128]{3,2,1,0:T(8,128)S(1)}, f32[2,2,32,128]{3,2,1,0:T(8,128)S(1)}, u32[]{:S(2)}, u32[]{:S(2)}) collective-permute-start(f32[2,2,32,128]{3,2,1,0:T(8,128)S(1)} %shard_map.138), channel_id=1, source_target_pairs={{0,16},{8,24},{16,0},{24,8},{1,17},{9,25},{17,1},{25,9},{2,18},{10... | collective-permute-start | bytes 196616 | tf_op jit(solution)/shard_map/ppermute | solution.py:772
  52.3 6.2 %collective-permute-start.14 = (f32[2,2,32,128]{3,2,1,0:T(8,128)S(1)}, f32[2,2,32,128]{3,2,1,0:T(8,128)S(1)}, u32[]{:S(2)}, u32[]{:S(2)}) collective-permute-start(f32[2,2,32,128]{3,2,1,0:T(8,128)S(1)} %shard_map.139), channel_id=1, source_target_pairs={{0,24},{8,16},{16,8},{24,0},{1,25},{9,17},{17,9},{25,1},{2,26},{10... | collective-permute-start | bytes 196616 | tf_op jit(solution)/shard_map/ppermute | solution.py:772
  54.9 4.3 %collective-permute-start.17 = (f32[2,2,32,128]{3,2,1,0:T(8,128)S(1)}, f32[2,2,32,128]{3,2,1,0:T(8,128)S(1)}, u32[]{:S(2)}, u32[]{:S(2)}) collective-permute-start(f32[2,2,32,128]{3,2,1,0:T(8,128)S(1)} %shard_map.142), channel_id=1, source_target_pairs={{0,8},{8,0},{16,24},{24,16},{1,9},{9,1},{17,25},{25,17},{2,10},{10... | collective-permute-start | bytes 196616 | tf_op jit(solution)/shard_map/ppermute | solution.py:772
  55.0 4.2 %copy-start.4 = (f32[8,32,32]{2,1,0:T(8,128)S(1)}, f32[8,32,32]{2,1,0:T(8,128)}, u32[]{:S(2)}) copy-start(f32[8,32,32]{2,1,0:T(8,128)} %refs_6_.1) | copy-start | bytes 98308
  55.1 4.2 %copy-start.5 = (f32[8,32,32]{2,1,0:T(8,128)S(1)}, f32[8,32,32]{2,1,0:T(8,128)}, u32[]{:S(2)}) copy-start(f32[8,32,32]{2,1,0:T(8,128)} %refs_7_.1) | copy-start | bytes 98308
  (3 other events, 5.8 us)

commit v15 on v13

--- a/solution.py
+++ b/solution.py
@@ -651,7 +651,6 @@
     beta_prev = refs[0]
     parts = refs[1 : 1 + parts_n]
     vk, va, qk, qa, w_k, w_a, tile = refs[1 + parts_n :]
-    s, x, y, c = places(2)
     slab = 128 // n
     for f, (q_ref, w) in enumerate(((qk, w_k), (qa, w_a))):
         for q in range(vk.shape[0] // n):
@@ -660,34 +659,31 @@
                 i = n * q + j
                 w[i] = whole[:, slab * j : slab * (j + 1)] - beta_prev[:, : vk.shape[2]] * q_ref[i]
 
-    def dot(a, b):
-        return jnp.sum(jnp.sum(a * b, axis=0))
+    def total(value):
+        return jnp.sum(jnp.sum(jnp.sum(value, axis=0), axis=0, keepdims=True), axis=1, keepdims=True)
 
     wk, wa, v_k, v_a = w_k[...], w_a[...], vk[...], va[...]
-    one = jnp.ones((1, 1), jnp.float32)
-    wv = (dot(wk, v_k) + dot(wa, v_a)) * one
-    vv = (dot(v_k, v_k) + dot(v_a, v_a)) * one
+    wv = total(wk * v_k + wa * v_a)
+    vv = total(v_k * v_k + v_a * v_a)
     a = jnp.where(vv > 0.0, wv / jnp.where(vv > 0.0, vv, 1.0), 0.0)
     u_k, u_a = wk - a * v_k, wa - a * v_a
-    uv = (dot(u_k, v_k) + dot(u_a, v_a)) * one
-    uu = (dot(u_k, u_k) + dot(u_a, u_a)) * one
-    me = ((s * 2 + x) * 2 + y) * 2 + c
-    lane = index_along((8, 128), 1)
-    row = index_along((8, 128), 0)
-    values = jnp.zeros((8, 128), jnp.float32)
+    uv = total(u_k * v_k + u_a * v_a)
+    uu = total(u_k * u_k + u_a * u_a)
+    lane = index_along((1, 128), 1)
+    values = jnp.zeros((1, 128), jnp.float32)
     for i, value in enumerate((wv, vv, a, uv, uu)):
-        values = jnp.where(row == i, value, values)
-    tile[...] = jnp.where(lane == me, values, 0.0)
+        values = jnp.where(lane == i, value, values)
+    tile[...] = values
 
 
 def final_kernel(tiles, w_k, w_a, vk, va, next_k, next_a, coefs, *, cells):
-    tile = jnp.sum(tiles[...], axis=0)
-    wv, vv, a, uv, uu = (tile[i : i + 1] for i in range(5))
-    wv_sum = jnp.sum(wv, axis=1, keepdims=True)
-    vv_sum = jnp.sum(vv, axis=1, keepdims=True)
+    tile = jnp.concatenate([tiles[i] for i in range(tiles.shape[0])], axis=0)
+    wv, vv, a, uv, uu = (tile[:, i : i + 1] for i in range(5))
+    wv_sum = jnp.sum(wv, axis=0, keepdims=True)
+    vv_sum = jnp.sum(vv, axis=0, keepdims=True)
     alpha = wv_sum / cells / (vv_sum / cells + eps_norm)
     off = alpha - a
-    rr = jnp.sum(uu - 2.0 * off * uv + off * off * vv, axis=1, keepdims=True)
+    rr = jnp.sum(uu - 2.0 * off * uv + off * off * vv, axis=0, keepdims=True)
     beta = jnp.sqrt(rr / cells + eps_norm)
     next_k[...] = (w_k[...] - alpha * vk[...]) / beta
     next_a[...] = (w_a[...] - alpha * va[...]) / beta
@@ -825,11 +821,11 @@
     parts = [distant, totals[0]] + [received[k] for k in range(1, n // 2)]
     w_k, w_a, tile = run(
         functools.partial(project_kernel, parts_n=len(parts), n=n),
-        (f32(*v_kappa.shape), f32(*v_kappa.shape), f32(8, 128)),
+        (f32(*v_kappa.shape), f32(*v_kappa.shape), f32(1, 128)),
         beta_row, *parts, v_kappa, v_absorb, q_kappa, q_absorb,
     )
     everyone = ("src", "gx", "gy")
-    tiles = lax.all_to_all(jnp.broadcast_to(tile, (8 * n, 8, 128)), everyone, 0, 0)
+    tiles = lax.all_to_all(jnp.broadcast_to(tile, (8 * n, 1, 128)), everyone, 0, 0)
     return tuple(run(
         functools.partial(final_kernel, cells=cells),
         (f32(*v_kappa.shape), f32(*v_kappa.shape), f32(2)),

time: 72.6 us -> 71.5 us (0.985)
  blocking collectives: 12.4 us -> 11.3 us
    all_to_all x1, blocking collectives: 12.4 us -> 11.3 us  [per_device_paired(): lax.all_to_all(jnp.broadcast_to(tile, (8 * n, 1, 128)), everyone, 0, 0)]
where the time goes in v15:
time: 71.5 us; the launch traced here: 71.3 us
  starting transfers between devices  22 us (31%)
  Pallas kernels  19.7 us (28%)
  waiting for transfers between devices  16.7 us (23%)
  blocking collectives  11.3 us (16%)
  between operations  1.59 us (2%)
    pallas_call x24, Pallas kernels, run(): pl.pallas_call(body if waits else kernel, out_shape=tuple(outs), in_specs...  19.7 us
    all_to_all x1, blocking collectives, per_device_paired(): lax.all_to_all(jnp.broadcast_to(tile, (8 * n, 1, 128)), everyone, 0, 0)  11.3 us
    ppermute x6, starting transfers between devices, along_z(): return lax.ppermute(value, 'src', [(i, i ^ k) for i in range(n)])  9.3 us
    ppermute x6, starting transfers between devices, swap_x(): return lax.ppermute(value, 'gx', [(0, 1), (1, 0)])  7.76 us
    ppermute x6, waiting for transfers between devices, along_z(): return lax.ppermute(value, 'src', [(i, i ^ k) for i in range(n)])  6.25 us
    ppermute x6, waiting for transfers between devices, swap_x(): return lax.ppermute(value, 'gx', [(0, 1), (1, 0)])  4.81 us
    ppermute x3, starting transfers between devices, across_y(): return lax.ppermute(value, 'gy', [(i, (i + 2) % 4) for i in range(4)])  4.75 us
    ppermute x3, waiting for transfers between devices, across_y(): return lax.ppermute(value, 'gy', [(i, (i + 2) % 4) for i in range(4)])  3.48 us
  transfers between devices with their start and end apart: 18, of which 12 were waited for; matrix products, arithmetic and copies ran while one was open for 0% of the time, Pallas kernels for 10%

profile of v15, /device:TPU:0, one launch (start us, length us, event | category | flops | bytes accessed | tf_op | source)
XLA Modules:
  0.0 71.3 jit_solution(11122438776338293003)
XLA Ops:
  0.6 2.0 %shard_map.122 = (f32[4,32,128]{2,1,0:T(8,128)}, f32[28,32,128]{2,1,0:T(8,128)}) custom-call(f32[4,8,32,128]{3,2,1,0:T(8,128)} %refs_0_.2, s32[8,32,128]{2,1,0:T(8,128)} %refs_1_.2, f32[8,32,32]{2,1,0:T(8,128)} %vk.5, f32[8,32,32]{2,1,0:T(8,128)} %va.5), custom_call_target="tpu_custom_call" | custom-call | tf_op jit(solution)/shard_map/pallas_call | solution.py:711
  2.7 3.0 %collective-permute-start = (f32[28,32,128]{2,1,0:T(8,128)}, f32[28,32,128]{2,1,0:T(8,128)S(1)}, u32[]{:S(2)}, u32[]{:S(2)}) collective-permute-start(f32[28,32,128]{2,1,0:T(8,128)} %get-tuple-element.28), channel_id=1, source_target_pairs={{0,4},{4,0},{1,5},{5,1},{2,6},{6,2},{3,7},{7,3},{8,12},{12,8},{9,1... | collective-permute-start | bytes 1376264 | tf_op jit(solution)/shard_map/ppermute | solution.py:741
  5.7 3.6 %collective-permute-start.3 = (f32[4,32,128]{2,1,0:T(8,128)}, f32[4,32,128]{2,1,0:T(8,128)S(1)}, u32[]{:S(2)}, u32[]{:S(2)}) collective-permute-start(f32[4,32,128]{2,1,0:T(8,128)} %get-tuple-element.29), channel_id=1, source_target_pairs={{0,24},{8,16},{16,8},{24,0},{1,25},{9,17},{17,9},{25,1},{2,26},{10... | collective-permute-start | bytes 196616 | tf_op jit(solution)/shard_map/ppermute | solution.py:747
  10.7 2.1 %shard_map.121 = (f32[16,72,128]{2,1,0:T(8,128)S(1)}, f32[1,128]{1,0:T(1,128)S(1)}) custom-call(s32[1,1024]{1,0:T(1,128)S(1)} %bitcast.3, f32[1]{0:T(128)S(6)} %copy.13.beta_prev), custom_call_target="tpu_custom_call" | custom-call | flops 301989888 | bytes 589824 | tf_op jit(solution)/shard_map/pallas_call | solution.py:711
  12.8 2.0 %collective-permute-done.2.refs_1_ = f32[4,32,128]{2,1,0:T(8,128)S(1)} collective-permute-done((f32[4,32,128]{2,1,0:T(8,128)}, f32[4,32,128]{2,1,0:T(8,128)S(1)}, u32[]{:S(2)}, u32[]{:S(2)}) %collective-permute-start.2) | collective-permute-done | bytes 65568 | tf_op jit(solution)/shard_map/ppermute | solution.py:747
  15.5 0.9 %collective-permute-done.refs_2_.refs_1_ = f32[28,32,128]{2,1,0:T(8,128)S(1)} collective-permute-done((f32[28,32,128]{2,1,0:T(8,128)}, f32[28,32,128]{2,1,0:T(8,128)S(1)}, u32[]{:S(2)}, u32[]{:S(2)}) %collective-permute-start) | collective-permute-done | bytes 458784 | tf_op jit(solution)/shard_map/ppermute | solution.py:741
  17.5 3.7 %collective-permute-done.5.refs_2_ = f32[12,32,128]{2,1,0:T(8,128)S(1)} collective-permute-done((f32[12,32,128]{2,1,0:T(8,128)S(1)}, f32[12,32,128]{2,1,0:T(8,128)S(1)}, u32[]{:S(2)}, u32[]{:S(2)}) %collective-permute-start.5) | collective-permute-done | bytes 196640 | tf_op jit(solution)/shard_map/ppermute | solution.py:741
  21.7 1.6 %collective-permute-start.6 = (f32[2,4,24,128]{3,2,1,0:T(8,128)S(1)}, f32[2,4,24,128]{3,2,1,0:T(8,128)S(1)}, u32[]{:S(2)}, u32[]{:S(2)}) collective-permute-start(f32[2,4,24,128]{3,2,1,0:T(8,128)S(1)} %shard_map.127.refs_2_), channel_id=1, source_target_pairs={{0,2},{1,3},{2,0},{3,1},{4,6},{5,7},{6,4},{7,5},{8,10},{9,11},{10,... | collective-permute-start | bytes 294920 | tf_op jit(solution)/shard_map/ppermute | solution.py:767
  23.6 1.6 %collective-permute-start.8 = (f32[2,4,24,128]{3,2,1,0:T(8,128)S(1)}, f32[2,4,24,128]{3,2,1,0:T(8,128)S(1)}, u32[]{:S(2)}, u32[]{:S(2)}) collective-permute-start(f32[2,4,24,128]{3,2,1,0:T(8,128)S(1)} %shard_map.128.refs_6_), channel_id=1, source_target_pairs={{0,2},{1,3},{2,0},{3,1},{4,6},{5,7},{6,4},{7,5},{8,10},{9,11},{10,... | collective-permute-start | bytes 294920 | tf_op jit(solution)/shard_map/ppermute | solution.py:767
  25.2 2.3 %shard_map.129 = (f32[18,72,128]{2,1,0:T(8,128)S(1)}, f32[16,72,128]{2,1,0:T(8,128)S(1)}, f32[17,72,128]{2,1,0:T(8,128)S(1)}, f32[16,72,128]{2,1,0:T(8,128)S(1)}...) custom-call(f32[16]{0:T(128)S(1)} %copy-done.6, f32[16]{0:T(128)S(1)} %copy-done.7, ...), custom_call_target="tpu_custom_call" | custom-call | flops 1000000000 | bytes 67108864 | tf_op jit(solution)/shard_map/pallas_call | solution.py:711
  29.1 4.4 %shard_map.131 = (f32[18,72,128]{2,1,0:T(8,128)S(1)}, f32[16,72,128]{2,1,0:T(8,128)S(1)}, f32[4,32,128]{2,1,0:T(8,128)S(1)}) custom-call(f32[16,72,128]{2,1,0:T(8,128)S(1)} %get-tuple-element.38.diag, f32[17,72,128]{2,1,0:T(8,128)S(1)} %get-tuple-element.39.fx, f32[16,72,128]{2,1,0:T(8,128)S(1)} %get-tuple-element.40.fy, ...), custom_call_target="tpu_custom_call" | custom-call | tf_op jit(solution)/shard_map/pallas_call | solution.py:711
  33.5 1.6 %collective-permute-start.9 = (f32[4,32,128]{2,1,0:T(8,128)S(1)}, f32[4,32,128]{2,1,0:T(8,128)S(1)}, u32[]{:S(2)}, u32[]{:S(2)}) collective-permute-start(f32[4,32,128]{2,1,0:T(8,128)S(1)} %get-tuple-element.45.sent), channel_id=1, source_target_pairs={{0,2},{1,3},{2,0},{3,1},{4,6},{5,7},{6,4},{7,5},{8,10},{9,11},{10,... | collective-permute-start | bytes 196616 | tf_op jit(solution)/shard_map/ppermute | solution.py:767
  35.1 2.7 %collective-permute-done.9.came = f32[4,32,128]{2,1,0:T(8,128)S(1)} collective-permute-done((f32[4,32,128]{2,1,0:T(8,128)S(1)}, f32[4,32,128]{2,1,0:T(8,128)S(1)}, u32[]{:S(2)}, u32[]{:S(2)}) %collective-permute-start.9) | collective-permute-done | bytes 65568 | tf_op jit(solution)/shard_map/ppermute | solution.py:767
  37.8 4.2 %shard_map.132 = (f32[2,16,32,128]{3,2,1,0:T(8,128)S(1)}, f32[2,16,32,128]{3,2,1,0:T(8,128)S(1)}) custom-call(f32[18,72,128]{2,1,0:T(8,128)S(1)} %get-tuple-element.43.phi, f32[16,72,128]{2,1,0:T(8,128)S(1)} %get-tuple-element.44.change, f32[16,72,128]{2,1,0:T(8,128)S(1)} %get-tuple-element.38.diag, f32[17,72,128]{2,1,0:T(8,128)S(1)} %get-tuple-element.39.fx, ...), custom_call_target="tpu_custom_call" | custom-call | tf_op jit(solution)/shard_map/pallas_call | solution.py:711
  42.1 1.9 %collective-permute-done.10.came.refs_1_ = f32[2,16,32,128]{3,2,1,0:T(8,128)S(1)} collective-permute-done((f32[2,16,32,128]{3,2,1,0:T(8,128)S(1)}, f32[2,16,32,128]{3,2,1,0:T(8,128)S(1)}, u32[]{:S(2)}, u32[]{:S(2)}) %collective-permute-start.10) | collective-permute-done | bytes 524320 | tf_op jit(solution)/shard_map/ppermute | solution.py:744
  44.3 1.2 %collective-permute-start.11 = (f32[1,2,2,32,128]{4,3,2,1,0:T(8,128)S(1)}, f32[1,2,2,32,128]{4,3,2,1,0:T(8,128)S(1)}, u32[]{:S(2)}, u32[]{:S(2)}) collective-permute-start(f32[1,2,2,32,128]{4,3,2,1,0:T(8,128)S(1)} %shard_map.134.refs_2_), channel_id=1, source_target_pairs={{0,4},{4,0},{1,5},{5,1},{2,6},{6,2},{3,7},{7,3},{8,12},{12,8},{9,1... | collective-permute-start | bytes 196616 | tf_op jit(solution)/shard_map/ppermute | solution.py:741
  46.5 1.2 %collective-permute-start.16 = (f32[1,2,2,32,128]{4,3,2,1,0:T(8,128)S(1)}, f32[1,2,2,32,128]{4,3,2,1,0:T(8,128)S(1)}, u32[]{:S(2)}, u32[]{:S(2)}) collective-permute-start(f32[1,2,2,32,128]{4,3,2,1,0:T(8,128)S(1)} %shard_map.135.refs_2_), channel_id=1, source_target_pairs={{0,4},{4,0},{1,5},{5,1},{2,6},{6,2},{3,7},{7,3},{8,12},{12,8},{9,1... | collective-permute-start | bytes 196616 | tf_op jit(solution)/shard_map/ppermute | solution.py:741
  47.9 1.0 %collective-permute-start.15 = (f32[1,2,2,32,128]{4,3,2,1,0:T(8,128)S(1)}, f32[1,2,2,32,128]{4,3,2,1,0:T(8,128)S(1)}, u32[]{:S(2)}, u32[]{:S(2)}) collective-permute-start(f32[1,2,2,32,128]{4,3,2,1,0:T(8,128)S(1)} %shard_map.136.refs_2_), channel_id=1, source_target_pairs={{0,4},{4,0},{1,5},{5,1},{2,6},{6,2},{3,7},{7,3},{8,12},{12,8},{9,1... | collective-permute-start | bytes 196616 | tf_op jit(solution)/shard_map/ppermute | solution.py:741
  49.3 2.2 %collective-permute-start.12 = (f32[2,2,32,128]{3,2,1,0:T(8,128)S(1)}, f32[2,2,32,128]{3,2,1,0:T(8,128)S(1)}, u32[]{:S(2)}, u32[]{:S(2)}) collective-permute-start(f32[2,2,32,128]{3,2,1,0:T(8,128)S(1)} %shard_map.138), channel_id=1, source_target_pairs={{0,16},{8,24},{16,0},{24,8},{1,17},{9,25},{17,1},{25,9},{2,18},{10... | collective-permute-start | bytes 196616 | tf_op jit(solution)/shard_map/ppermute | solution.py:747
  51.5 2.7 %collective-permute-start.14 = (f32[2,2,32,128]{3,2,1,0:T(8,128)S(1)}, f32[2,2,32,128]{3,2,1,0:T(8,128)S(1)}, u32[]{:S(2)}, u32[]{:S(2)}) collective-permute-start(f32[2,2,32,128]{3,2,1,0:T(8,128)S(1)} %shard_map.139), channel_id=1, source_target_pairs={{0,24},{8,16},{16,8},{24,0},{1,25},{9,17},{17,9},{25,1},{2,26},{10... | collective-permute-start | bytes 196616 | tf_op jit(solution)/shard_map/ppermute | solution.py:747
  54.3 2.3 %collective-permute-done.12.refs_0_ = f32[2,2,32,128]{3,2,1,0:T(8,128)S(1)} collective-permute-done((f32[2,2,32,128]{3,2,1,0:T(8,128)S(1)}, f32[2,2,32,128]{3,2,1,0:T(8,128)S(1)}, u32[]{:S(2)}, u32[]{:S(2)}) %collective-permute-start.12) | collective-permute-done | bytes 65568 | tf_op jit(solution)/shard_map/ppermute | solution.py:747
  56.6 1.2 %collective-permute-done.14.refs_1_ = f32[2,2,32,128]{3,2,1,0:T(8,128)S(1)} collective-permute-done((f32[2,2,32,128]{3,2,1,0:T(8,128)S(1)}, f32[2,2,32,128]{3,2,1,0:T(8,128)S(1)}, u32[]{:S(2)}, u32[]{:S(2)}) %collective-permute-start.14) | collective-permute-done | bytes 65568 | tf_op jit(solution)/shard_map/ppermute | solution.py:747
  59.0 11.3 %all_to_all.5.tiles = f32[32,1,128]{2,1,0:T(1,128)S(1)} all-to-all(f32[32,1,128]{2,1,0:T(1,128)S(1)} %broadcast_in_dim.3), channel_id=1, replica_groups=mesh['src'=4,'gx'=2,'gy'=4] {'src','gx','gy'}, dimensions={0} | all-to-all | bytes 32768 | tf_op jit(solution)/shard_map/all_to_all | solution.py:828
  70.3 1.0 %shard_map.144 = (f32[8,32,32]{2,1,0:T(8,128)}, f32[8,32,32]{2,1,0:T(8,128)}, f32[2]{0:T(128)}) custom-call(f32[32,1,128]{2,1,0:T(1,128)S(1)} %all_to_all.5.tiles, f32[8,32,32]{2,1,0:T(8,128)S(1)} %get-tuple-element.49.w_k, f32[8,32,32]{2,1,0:T(8,128)S(1)} %get-tuple-element.50.w_a, f32[8,32,32]{2,1,0:T(8,128)S(1)} %copy-done.1, f32[8,32,32]{2,1,0:T(8,128)S(1)} %copy-done.2), custom_call_target="tpu_custom_call" | custom-call | tf_op jit(solution)/shard_map/pallas_call | solution.py:711
  (56 shorter events, 8.1 us)
Async XLA Ops:
  2.6 8.1 %copy-start.8 = (s32[1024]{0:T(1024)S(1)}, s32[1024]{0:T(1024)}, u32[]{:S(2)}) copy-start(s32[1024]{0:T(1024)} %param.14) | copy-start | bytes 12292
  2.7 13.7 %collective-permute-start = (f32[28,32,128]{2,1,0:T(8,128)}, f32[28,32,128]{2,1,0:T(8,128)S(1)}, u32[]{:S(2)}, u32[]{:S(2)}) collective-permute-start(f32[28,32,128]{2,1,0:T(8,128)} %get-tuple-element.28), channel_id=1, source_target_pairs={{0,4},{4,0},{1,5},{5,1},{2,6},{6,2},{3,7},{7,3},{8,12},{12,8},{9,1... | collective-permute-start | bytes 1376264 | tf_op jit(solution)/shard_map/ppermute | solution.py:741
  5.7 7.2 %collective-permute-start.3 = (f32[4,32,128]{2,1,0:T(8,128)}, f32[4,32,128]{2,1,0:T(8,128)S(1)}, u32[]{:S(2)}, u32[]{:S(2)}) collective-permute-start(f32[4,32,128]{2,1,0:T(8,128)} %get-tuple-element.29), channel_id=1, source_target_pairs={{0,24},{8,16},{16,8},{24,0},{1,25},{9,17},{17,9},{25,1},{2,26},{10... | collective-permute-start | bytes 196616 | tf_op jit(solution)/shard_map/ppermute | solution.py:747
  9.3 5.6 %collective-permute-start.2 = (f32[4,32,128]{2,1,0:T(8,128)}, f32[4,32,128]{2,1,0:T(8,128)S(1)}, u32[]{:S(2)}, u32[]{:S(2)}) collective-permute-start(f32[4,32,128]{2,1,0:T(8,128)} %get-tuple-element.29), channel_id=1, source_target_pairs={{0,16},{8,24},{16,0},{24,8},{1,17},{9,25},{17,1},{25,9},{2,18},{10... | collective-permute-start | bytes 196616 | tf_op jit(solution)/shard_map/ppermute | solution.py:747
  9.3 5.6 %collective-permute-start.1 = (f32[4,32,128]{2,1,0:T(8,128)}, f32[4,32,128]{2,1,0:T(8,128)S(1)}, u32[]{:S(2)}, u32[]{:S(2)}) collective-permute-start(f32[4,32,128]{2,1,0:T(8,128)} %get-tuple-element.29), channel_id=1, source_target_pairs={{0,8},{8,0},{16,24},{24,16},{1,9},{9,1},{17,25},{25,17},{2,10},{10... | collective-permute-start | bytes 196616 | tf_op jit(solution)/shard_map/ppermute | solution.py:747
  12.8 3.6 %copy-start = (f32[4,8,32,128]{3,2,1,0:T(8,128)S(1)}, f32[4,8,32,128]{3,2,1,0:T(8,128)}, u32[]{:S(2)}) copy-start(f32[4,8,32,128]{3,2,1,0:T(8,128)} %refs_0_.2) | copy-start | bytes 1572868
  15.0 6.3 %collective-permute-start.5 = (f32[12,32,128]{2,1,0:T(8,128)S(1)}, f32[12,32,128]{2,1,0:T(8,128)S(1)}, u32[]{:S(2)}, u32[]{:S(2)}) collective-permute-start(f32[12,32,128]{2,1,0:T(8,128)S(1)} %shard_map.123.refs_3_.joined), channel_id=1, source_target_pairs={{0,4},{4,0},{1,5},{5,1},{2,6},{6,2},{3,7},{7,3},{8,12},{12,8},{9,1... | collective-permute-start | bytes 589832 | tf_op jit(solution)/shard_map/ppermute | solution.py:741
  17.0 4.7 %collective-permute-start.4 = (f32[2,16,32,128]{3,2,1,0:T(8,128)S(1)}, f32[2,16,32,128]{3,2,1,0:T(8,128)S(1)}, u32[]{:S(2)}, u32[]{:S(2)}) collective-permute-start(f32[2,16,32,128]{3,2,1,0:T(8,128)S(1)} %get-tuple-element.32.refs_1_.refs_3_), channel_id=1, source_target_pairs={{0,1},{1,0},{2,3},{3,2},{4,5},{5,4},{6,7},{7,6},{8,9},{9,8},{10,11... | collective-permute-start | bytes 1572872 | tf_op jit(solution)/shard_map/ppermute | solution.py:744
  21.6 2.0 %collective-permute-start.7 = (f32[2,16,32,128]{3,2,1,0:T(8,128)S(1)}, f32[2,16,32,128]{3,2,1,0:T(8,128)S(1)}, u32[]{:S(2)}, u32[]{:S(2)}) collective-permute-start(f32[2,16,32,128]{3,2,1,0:T(8,128)S(1)} %shard_map.126.refs_3_.refs_0_.vector), channel_id=1, source_target_pairs={{0,1},{1,0},{2,3},{3,2},{4,5},{5,4},{6,7},{7,6},{8,9},{9,8},{10,11... | collective-permute-start | bytes 1572872 | tf_op jit(solution)/shard_map/ppermute | solution.py:744
  21.7 3.5 %copy-start.6 = (f32[16]{0:T(128)S(1)}, f32[16]{0:T(128)}, u32[]{:S(2)}) copy-start(f32[16]{0:T(128)} %kap_table.1) | copy-start | bytes 196
  21.7 3.4 %copy-start.7 = (f32[16]{0:T(128)S(1)}, f32[16]{0:T(128)}, u32[]{:S(2)}) copy-start(f32[16]{0:T(128)} %abs_table.1) | copy-start | bytes 196
  21.7 5.8 %collective-permute-start.6 = (f32[2,4,24,128]{3,2,1,0:T(8,128)S(1)}, f32[2,4,24,128]{3,2,1,0:T(8,128)S(1)}, u32[]{:S(2)}, u32[]{:S(2)}) collective-permute-start(f32[2,4,24,128]{3,2,1,0:T(8,128)S(1)} %shard_map.127.refs_2_), channel_id=1, source_target_pairs={{0,2},{1,3},{2,0},{3,1},{4,6},{5,7},{6,4},{7,5},{8,10},{9,11},{10,... | collective-permute-start | bytes 294920 | tf_op jit(solution)/shard_map/ppermute | solution.py:767
  23.6 5.5 %collective-permute-start.8 = (f32[2,4,24,128]{3,2,1,0:T(8,128)S(1)}, f32[2,4,24,128]{3,2,1,0:T(8,128)S(1)}, u32[]{:S(2)}, u32[]{:S(2)}) collective-permute-start(f32[2,4,24,128]{3,2,1,0:T(8,128)S(1)} %shard_map.128.refs_6_), channel_id=1, source_target_pairs={{0,2},{1,3},{2,0},{3,1},{4,6},{5,7},{6,4},{7,5},{8,10},{9,11},{10,... | collective-permute-start | bytes 294920 | tf_op jit(solution)/shard_map/ppermute | solution.py:767
  33.5 4.3 %collective-permute-start.9 = (f32[4,32,128]{2,1,0:T(8,128)S(1)}, f32[4,32,128]{2,1,0:T(8,128)S(1)}, u32[]{:S(2)}, u32[]{:S(2)}) collective-permute-start(f32[4,32,128]{2,1,0:T(8,128)S(1)} %get-tuple-element.45.sent), channel_id=1, source_target_pairs={{0,2},{1,3},{2,0},{3,1},{4,6},{5,7},{6,4},{7,5},{8,10},{9,11},{10,... | collective-permute-start | bytes 196616 | tf_op jit(solution)/shard_map/ppermute | solution.py:767
  42.0 2.0 %collective-permute-start.10 = (f32[2,16,32,128]{3,2,1,0:T(8,128)S(1)}, f32[2,16,32,128]{3,2,1,0:T(8,128)S(1)}, u32[]{:S(2)}, u32[]{:S(2)}) collective-permute-start(f32[2,16,32,128]{3,2,1,0:T(8,128)S(1)} %get-tuple-element.47), channel_id=1, source_target_pairs={{0,1},{1,0},{2,3},{3,2},{4,5},{5,4},{6,7},{7,6},{8,9},{9,8},{10,11... | collective-permute-start | bytes 1572872 | tf_op jit(solution)/shard_map/ppermute | solution.py:744
  44.3 5.0 %collective-permute-start.11 = (f32[1,2,2,32,128]{4,3,2,1,0:T(8,128)S(1)}, f32[1,2,2,32,128]{4,3,2,1,0:T(8,128)S(1)}, u32[]{:S(2)}, u32[]{:S(2)}) collective-permute-start(f32[1,2,2,32,128]{4,3,2,1,0:T(8,128)S(1)} %shard_map.134.refs_2_), channel_id=1, source_target_pairs={{0,4},{4,0},{1,5},{5,1},{2,6},{6,2},{3,7},{7,3},{8,12},{12,8},{9,1... | collective-permute-start | bytes 196616 | tf_op jit(solution)/shard_map/ppermute | solution.py:741
  45.5 6.0 %collective-permute-start.13 = (f32[1,2,2,32,128]{4,3,2,1,0:T(8,128)S(1)}, f32[1,2,2,32,128]{4,3,2,1,0:T(8,128)S(1)}, u32[]{:S(2)}, u32[]{:S(2)}) collective-permute-start(f32[1,2,2,32,128]{4,3,2,1,0:T(8,128)S(1)} %shard_map.133.refs_2_), channel_id=1, source_target_pairs={{0,4},{4,0},{1,5},{5,1},{2,6},{6,2},{3,7},{7,3},{8,12},{12,8},{9,1... | collective-permute-start | bytes 196616 | tf_op jit(solution)/shard_map/ppermute | solution.py:741
  46.5 7.7 %collective-permute-start.16 = (f32[1,2,2,32,128]{4,3,2,1,0:T(8,128)S(1)}, f32[1,2,2,32,128]{4,3,2,1,0:T(8,128)S(1)}, u32[]{:S(2)}, u32[]{:S(2)}) collective-permute-start(f32[1,2,2,32,128]{4,3,2,1,0:T(8,128)S(1)} %shard_map.135.refs_2_), channel_id=1, source_target_pairs={{0,4},{4,0},{1,5},{5,1},{2,6},{6,2},{3,7},{7,3},{8,12},{12,8},{9,1... | collective-permute-start | bytes 196616 | tf_op jit(solution)/shard_map/ppermute | solution.py:741
  47.9 6.4 %collective-permute-start.15 = (f32[1,2,2,32,128]{4,3,2,1,0:T(8,128)S(1)}, f32[1,2,2,32,128]{4,3,2,1,0:T(8,128)S(1)}, u32[]{:S(2)}, u32[]{:S(2)}) collective-permute-start(f32[1,2,2,32,128]{4,3,2,1,0:T(8,128)S(1)} %shard_map.136.refs_2_), channel_id=1, source_target_pairs={{0,4},{4,0},{1,5},{5,1},{2,6},{6,2},{3,7},{7,3},{8,12},{12,8},{9,1... | collective-permute-start | bytes 196616 | tf_op jit(solution)/shard_map/ppermute | solution.py:741
  49.3 7.3 %collective-permute-start.12 = (f32[2,2,32,128]{3,2,1,0:T(8,128)S(1)}, f32[2,2,32,128]{3,2,1,0:T(8,128)S(1)}, u32[]{:S(2)}, u32[]{:S(2)}) collective-permute-start(f32[2,2,32,128]{3,2,1,0:T(8,128)S(1)} %shard_map.138), channel_id=1, source_target_pairs={{0,16},{8,24},{16,0},{24,8},{1,17},{9,25},{17,1},{25,9},{2,18},{10... | collective-permute-start | bytes 196616 | tf_op jit(solution)/shard_map/ppermute | solution.py:747
  51.5 6.2 %collective-permute-start.14 = (f32[2,2,32,128]{3,2,1,0:T(8,128)S(1)}, f32[2,2,32,128]{3,2,1,0:T(8,128)S(1)}, u32[]{:S(2)}, u32[]{:S(2)}) collective-permute-start(f32[2,2,32,128]{3,2,1,0:T(8,128)S(1)} %shard_map.139), channel_id=1, source_target_pairs={{0,24},{8,16},{16,8},{24,0},{1,25},{9,17},{17,9},{25,1},{2,26},{10... | collective-permute-start | bytes 196616 | tf_op jit(solution)/shard_map/ppermute | solution.py:747
  54.2 4.3 %collective-permute-start.17 = (f32[2,2,32,128]{3,2,1,0:T(8,128)S(1)}, f32[2,2,32,128]{3,2,1,0:T(8,128)S(1)}, u32[]{:S(2)}, u32[]{:S(2)}) collective-permute-start(f32[2,2,32,128]{3,2,1,0:T(8,128)S(1)} %shard_map.142), channel_id=1, source_target_pairs={{0,8},{8,0},{16,24},{24,16},{1,9},{9,1},{17,25},{25,17},{2,10},{10... | collective-permute-start | bytes 196616 | tf_op jit(solution)/shard_map/ppermute | solution.py:747
  54.3 4.2 %copy-start.4 = (f32[8,32,32]{2,1,0:T(8,128)S(1)}, f32[8,32,32]{2,1,0:T(8,128)}, u32[]{:S(2)}) copy-start(f32[8,32,32]{2,1,0:T(8,128)} %refs_6_.1) | copy-start | bytes 98308
  54.3 4.2 %copy-start.5 = (f32[8,32,32]{2,1,0:T(8,128)S(1)}, f32[8,32,32]{2,1,0:T(8,128)}, u32[]{:S(2)}) copy-start(f32[8,32,32]{2,1,0:T(8,128)} %refs_7_.1) | copy-start | bytes 98308
  (3 other events, 5.8 us)

commit v16 on v15

--- a/solution.py
+++ b/solution.py
@@ -190,16 +190,15 @@
     return jnp.concatenate([ref[per * q + j] for j in range(per)], axis=1)
 
 
-def pack_kernel(bg, labels, vk, va, packed, message, raw, v_in, sems):
+def pack_kernel(bg, vk, va, packed, message, v_in, sems):
     _, x, _, _ = places(2)
     half = bg.shape[0] // 2
-    cx = labels.shape[0]
+    cx = bg.shape[1]
     copies = [
         pltpu.make_async_copy(src, dst, sems.at[i])
         for i, (src, dst) in enumerate((
             (vk, v_in.at[0]),
             (va, v_in.at[1]),
-            (labels, raw),
             *((bg.at[half * (1 - x) + i], message.at[pl.ds(cx * i, cx)]) for i in range(half)),
         ))
     ]
@@ -211,10 +210,8 @@
         for q in range(groups):
             planes = packed_planes(v_in.at[f], q)
             packed[groups * f + q] = planes
-            message[cx * (half + 1) + groups * f + q] = planes
-    copies[2].wait()
-    message[pl.ds(cx * half, cx)] = raw[...].astype(jnp.float32)
-    for copy in copies[3:]:
+            message[cx * half + groups * f + q] = planes
+    for copy in copies[2:]:
         copy.wait()
 
 
@@ -242,7 +239,7 @@
     lax.fori_loop(0, planes // 2, body, 0)
 
 
-def photon_kernel(bg, labels, msg, mine, fields, raw, sems):
+def photon_kernel(bg, labels, msg, labels_came, mine, fields, raw, sems):
     _, x, _, c = places(2)
     half = bg.shape[0] // 2
     cx = labels.shape[0]
@@ -259,7 +256,7 @@
         copy.start()
     mine[pl.ds(there, cx)] = msg[pl.ds(cx * c, cx)]
     fields[0, pl.ds(there, cx)] = msg[pl.ds(cx * (1 - c), cx)]
-    fields[1, pl.ds(there, cx)] = msg[pl.ds(cx * half, cx)]
+    fields[1, pl.ds(there, cx)] = labels_came[...].astype(jnp.float32)
     for copy in copies:
         copy.wait()
     fields[1, pl.ds(here, cx)] = raw[...].astype(jnp.float32)
@@ -750,16 +747,17 @@
     float_block = lambda *shape: (shape, jnp.float32)
     raw_labels = (block, jnp.int32)
     packed, message = run(
-        pack_kernel, (f32(2 * groups, cy, cz), f32((sources // 2 + 1) * cx + 2 * groups, cy, cz)),
-        background, labels, v_kappa, v_absorb, hbm=(0, 1, 2, 3),
-        scratch=(raw_labels, float_block(2, *v_kappa.shape)), copies=3 + sources // 2, mib=60,
+        pack_kernel, (f32(2 * groups, cy, cz), f32(sources // 2 * cx + 2 * groups, cy, cz)),
+        background, v_kappa, v_absorb, hbm=(0, 1, 2),
+        scratch=(float_block(2, *v_kappa.shape),), copies=2 + sources // 2, mib=60,
     )
     long = pl.CostEstimate(flops=10**9, bytes_accessed=2**26, transcendentals=0)
+    labels_came = swap_x(labels)
     came = swap_x(message)
     slabs = [along_z(packed, k) for k in range(1, n)]
     count, beta_row = run(
         functools.partial(count_kernel, ny=ny, nz=cz, half=2 * cy, halo=HALO),
-        (f32(planes, rows, cz), f32(1, cz)), det_cells.reshape(1, dets), beta_prev, smem=(1,),
+        (f32(planes, rows, cz), f32(1, cz)), det_cells.reshape(1, dets), beta_prev, smem=(1,), after=(labels_came,),
         cost=pl.CostEstimate(flops=2 * planes * rows * cz * dets, bytes_accessed=planes * rows * cz * 4, transcendentals=0),
     )
 
@@ -771,7 +769,7 @@
     (half_vector,) = run(own_half_kernel, (f32(2, *block),), v_kappa, v_absorb, joined)
     mine, fields = run(
         photon_kernel, (f32(planes, cy, cz), f32(2, planes, cy, cz)),
-        background, labels, came, after=(joined,), hbm=(0, 1), scratch=(raw_labels,), copies=3,
+        background, labels, came, labels_came, after=(joined,), hbm=(0, 1), scratch=(raw_labels,), copies=3,
     )
     got = swap_core(fields)
     (vector,) = run(

time: 71.5 us -> 70.7 us (0.989)
  waiting for transfers between devices: 16.7 us -> 15.4 us
  starting transfers between devices: 22 us -> 22.8 us
    ppermute x6 -> x7, waiting for transfers between devices: 4.81 us -> 3.11 us  [swap_x(): return lax.ppermute(value, 'gx', [(0, 1), (1, 0)])]
    ppermute x6 -> x7, starting transfers between devices: 7.76 us -> 8.89 us  [swap_x(): return lax.ppermute(value, 'gx', [(0, 1), (1, 0)])]
  transfers between devices with their start and end apart: 18 -> 19, of which waited for: 12 -> 9; matrix products, arithmetic and copies ran while one was open for 0% -> 0% of each run, Pallas kernels for 10% -> 13%
where the time goes in v16:
time: 70.7 us; the launch traced here: 70.6 us
  starting transfers between devices  22.8 us (32%)
  Pallas kernels  19.6 us (28%)
  waiting for transfers between devices  15.4 us (22%)
  blocking collectives  11.2 us (16%)
  between operations  1.6 us (2%)
    pallas_call x24, Pallas kernels, run(): pl.pallas_call(body if waits else kernel, out_shape=tuple(outs), in_specs...  19.6 us
    all_to_all x1, blocking collectives, per_device_paired(): lax.all_to_all(jnp.broadcast_to(tile, (8 * n, 1, 128)), everyone, 0, 0)  11.2 us
    ppermute x6, starting transfers between devices, along_z(): return lax.ppermute(value, 'src', [(i, i ^ k) for i in range(n)])  8.92 us
    ppermute x7, starting transfers between devices, swap_x(): return lax.ppermute(value, 'gx', [(0, 1), (1, 0)])  8.89 us
    ppermute x6, waiting for transfers between devices, along_z(): return lax.ppermute(value, 'src', [(i, i ^ k) for i in range(n)])  6.66 us
    ppermute x3, starting transfers between devices, across_y(): return lax.ppermute(value, 'gy', [(i, (i + 2) % 4) for i in range(4)])  4.75 us
    ppermute x3, waiting for transfers between devices, across_y(): return lax.ppermute(value, 'gy', [(i, (i + 2) % 4) for i in range(4)])  3.48 us
    ppermute x7, waiting for transfers between devices, swap_x(): return lax.ppermute(value, 'gx', [(0, 1), (1, 0)])  3.11 us
  transfers between devices with their start and end apart: 19, of which 9 were waited for; matrix products, arithmetic and copies ran while one was open for 0% of the time, Pallas kernels for 13%

profile of v16, /device:TPU:0, one launch (start us, length us, event | category | flops | bytes accessed | tf_op | source)
XLA Modules:
  0.0 70.6 jit_solution(4686010078263224427)
XLA Ops:
  0.6 3.0 %collective-permute-start = (s32[8,32,128]{2,1,0:T(8,128)}, s32[8,32,128]{2,1,0:T(8,128)S(1)}, u32[]{:S(2)}, u32[]{:S(2)}) collective-permute-start(s32[8,32,128]{2,1,0:T(8,128)} %refs_1_.3), channel_id=1, source_target_pairs={{0,4},{4,0},{1,5},{5,1},{2,6},{6,2},{3,7},{7,3},{8,12},{12,8},{9,1... | collective-permute-start | bytes 393224 | tf_op jit(solution)/shard_map/ppermute | solution.py:738
  3.6 1.9 %shard_map.122 = (f32[4,32,128]{2,1,0:T(8,128)}, f32[20,32,128]{2,1,0:T(8,128)}) custom-call(f32[4,8,32,128]{3,2,1,0:T(8,128)} %refs_0_.2, f32[8,32,32]{2,1,0:T(8,128)} %vk.5, f32[8,32,32]{2,1,0:T(8,128)} %va.5), custom_call_target="tpu_custom_call" | custom-call | tf_op jit(solution)/shard_map/pallas_call | solution.py:708
  5.6 4.1 %collective-permute-start.4 = (f32[4,32,128]{2,1,0:T(8,128)}, f32[4,32,128]{2,1,0:T(8,128)S(1)}, u32[]{:S(2)}, u32[]{:S(2)}) collective-permute-start(f32[4,32,128]{2,1,0:T(8,128)} %get-tuple-element.29), channel_id=1, source_target_pairs={{0,24},{8,16},{16,8},{24,0},{1,25},{9,17},{17,9},{25,1},{2,26},{10... | collective-permute-start | bytes 196616 | tf_op jit(solution)/shard_map/ppermute | solution.py:744
  11.0 2.1 %shard_map.121 = (f32[16,72,128]{2,1,0:T(8,128)S(1)}, f32[1,128]{1,0:T(1,128)S(1)}) custom-call(s32[1,1024]{1,0:T(1,128)S(1)} %bitcast.3, f32[1]{0:T(128)S(6)} %copy.13.refs_1_, s32[8,32,128]{2,1,0:T(8,128)S(1)} %collective-permute-done.refs_2_.refs_3_), custom_call_target="tpu_custom_call" | custom-call | flops 301989888 | bytes 589824 | tf_op jit(solution)/shard_map/pallas_call | solution.py:708
  13.1 2.1 %collective-permute-done.3.refs_1_ = f32[4,32,128]{2,1,0:T(8,128)S(1)} collective-permute-done((f32[4,32,128]{2,1,0:T(8,128)}, f32[4,32,128]{2,1,0:T(8,128)S(1)}, u32[]{:S(2)}, u32[]{:S(2)}) %collective-permute-start.3) | collective-permute-done | bytes 65568 | tf_op jit(solution)/shard_map/ppermute | solution.py:744
  15.2 1.6 %collective-permute-start.6 = (f32[12,32,128]{2,1,0:T(8,128)S(1)}, f32[12,32,128]{2,1,0:T(8,128)S(1)}, u32[]{:S(2)}, u32[]{:S(2)}) collective-permute-start(f32[12,32,128]{2,1,0:T(8,128)S(1)} %shard_map.123.refs_4_.joined), channel_id=1, source_target_pairs={{0,4},{4,0},{1,5},{5,1},{2,6},{6,2},{3,7},{7,3},{8,12},{12,8},{9,1... | collective-permute-start | bytes 589832 | tf_op jit(solution)/shard_map/ppermute | solution.py:738
  17.9 3.1 %collective-permute-done.6.refs_2_ = f32[12,32,128]{2,1,0:T(8,128)S(1)} collective-permute-done((f32[12,32,128]{2,1,0:T(8,128)S(1)}, f32[12,32,128]{2,1,0:T(8,128)S(1)}, u32[]{:S(2)}, u32[]{:S(2)}) %collective-permute-start.6) | collective-permute-done | bytes 196640 | tf_op jit(solution)/shard_map/ppermute | solution.py:738
  21.5 1.6 %collective-permute-start.7 = (f32[2,4,24,128]{3,2,1,0:T(8,128)S(1)}, f32[2,4,24,128]{3,2,1,0:T(8,128)S(1)}, u32[]{:S(2)}, u32[]{:S(2)}) collective-permute-start(f32[2,4,24,128]{3,2,1,0:T(8,128)S(1)} %shard_map.127.refs_2_), channel_id=1, source_target_pairs={{0,2},{1,3},{2,0},{3,1},{4,6},{5,7},{6,4},{7,5},{8,10},{9,11},{10,... | collective-permute-start | bytes 294920 | tf_op jit(solution)/shard_map/ppermute | solution.py:765
  23.4 1.6 %collective-permute-start.9 = (f32[2,4,24,128]{3,2,1,0:T(8,128)S(1)}, f32[2,4,24,128]{3,2,1,0:T(8,128)S(1)}, u32[]{:S(2)}, u32[]{:S(2)}) collective-permute-start(f32[2,4,24,128]{3,2,1,0:T(8,128)S(1)} %shard_map.128.refs_6_), channel_id=1, source_target_pairs={{0,2},{1,3},{2,0},{3,1},{4,6},{5,7},{6,4},{7,5},{8,10},{9,11},{10,... | collective-permute-start | bytes 294920 | tf_op jit(solution)/shard_map/ppermute | solution.py:765
  25.0 2.3 %shard_map.129 = (f32[18,72,128]{2,1,0:T(8,128)S(1)}, f32[16,72,128]{2,1,0:T(8,128)S(1)}, f32[17,72,128]{2,1,0:T(8,128)S(1)}, f32[16,72,128]{2,1,0:T(8,128)S(1)}...) custom-call(f32[16]{0:T(128)S(1)} %copy-done.6, f32[16]{0:T(128)S(1)} %copy-done.7, ...), custom_call_target="tpu_custom_call" | custom-call | flops 1000000000 | bytes 67108864 | tf_op jit(solution)/shard_map/pallas_call | solution.py:708
  27.3 0.8 %shard_map.130 = (f32[16,72,128]{2,1,0:T(8,128)S(1)}, f32[17,72,128]{2,1,0:T(8,128)S(1)}, f32[16,72,128]{2,1,0:T(8,128)S(1)}, f32[16,72,128]{2,1,0:T(8,128)S(1)}) custom-call(f32[16]{0:T(128)S(1)} %copy-done.6, f32[16]{0:T(128)S(1)} %copy-done.7, f32[2,4,24,128]{3,2,1,0:T(8,128)S(1)} %collective-permute-done.7.edge.photon_edge, ...), custom_call_target="tpu_custom_call" | custom-call | tf_op jit(solution)/shard_map/pallas_call | solution.py:708
  28.9 4.4 %shard_map.131 = (f32[18,72,128]{2,1,0:T(8,128)S(1)}, f32[16,72,128]{2,1,0:T(8,128)S(1)}, f32[4,32,128]{2,1,0:T(8,128)S(1)}) custom-call(f32[16,72,128]{2,1,0:T(8,128)S(1)} %get-tuple-element.38.diag, f32[17,72,128]{2,1,0:T(8,128)S(1)} %get-tuple-element.39.fx, f32[16,72,128]{2,1,0:T(8,128)S(1)} %get-tuple-element.40.fy, ...), custom_call_target="tpu_custom_call" | custom-call | tf_op jit(solution)/shard_map/pallas_call | solution.py:708
  33.3 1.6 %collective-permute-start.10 = (f32[4,32,128]{2,1,0:T(8,128)S(1)}, f32[4,32,128]{2,1,0:T(8,128)S(1)}, u32[]{:S(2)}, u32[]{:S(2)}) collective-permute-start(f32[4,32,128]{2,1,0:T(8,128)S(1)} %get-tuple-element.45.sent), channel_id=1, source_target_pairs={{0,2},{1,3},{2,0},{3,1},{4,6},{5,7},{6,4},{7,5},{8,10},{9,11},{10,... | collective-permute-start | bytes 196616 | tf_op jit(solution)/shard_map/ppermute | solution.py:765
  34.9 2.7 %collective-permute-done.10.came = f32[4,32,128]{2,1,0:T(8,128)S(1)} collective-permute-done((f32[4,32,128]{2,1,0:T(8,128)S(1)}, f32[4,32,128]{2,1,0:T(8,128)S(1)}, u32[]{:S(2)}, u32[]{:S(2)}) %collective-permute-start.10) | collective-permute-done | bytes 65568 | tf_op jit(solution)/shard_map/ppermute | solution.py:765
  37.6 4.2 %shard_map.132 = (f32[2,16,32,128]{3,2,1,0:T(8,128)S(1)}, f32[2,16,32,128]{3,2,1,0:T(8,128)S(1)}) custom-call(f32[18,72,128]{2,1,0:T(8,128)S(1)} %get-tuple-element.43.phi, f32[16,72,128]{2,1,0:T(8,128)S(1)} %get-tuple-element.44.change, f32[16,72,128]{2,1,0:T(8,128)S(1)} %get-tuple-element.38.diag, f32[17,72,128]{2,1,0:T(8,128)S(1)} %get-tuple-element.39.fx, ...), custom_call_target="tpu_custom_call" | custom-call | tf_op jit(solution)/shard_map/pallas_call | solution.py:708
  41.9 1.9 %collective-permute-done.11.came.refs_1_ = f32[2,16,32,128]{3,2,1,0:T(8,128)S(1)} collective-permute-done((f32[2,16,32,128]{3,2,1,0:T(8,128)S(1)}, f32[2,16,32,128]{3,2,1,0:T(8,128)S(1)}, u32[]{:S(2)}, u32[]{:S(2)}) %collective-permute-start.11) | collective-permute-done | bytes 524320 | tf_op jit(solution)/shard_map/ppermute | solution.py:741
  44.1 1.6 %collective-permute-start.12 = (f32[1,2,2,32,128]{4,3,2,1,0:T(8,128)S(1)}, f32[1,2,2,32,128]{4,3,2,1,0:T(8,128)S(1)}, u32[]{:S(2)}, u32[]{:S(2)}) collective-permute-start(f32[1,2,2,32,128]{4,3,2,1,0:T(8,128)S(1)} %shard_map.134.refs_2_), channel_id=1, source_target_pairs={{0,4},{4,0},{1,5},{5,1},{2,6},{6,2},{3,7},{7,3},{8,12},{12,8},{9,1... | collective-permute-start | bytes 196616 | tf_op jit(solution)/shard_map/ppermute | solution.py:738
  46.3 1.6 %collective-permute-start.17 = (f32[1,2,2,32,128]{4,3,2,1,0:T(8,128)S(1)}, f32[1,2,2,32,128]{4,3,2,1,0:T(8,128)S(1)}, u32[]{:S(2)}, u32[]{:S(2)}) collective-permute-start(f32[1,2,2,32,128]{4,3,2,1,0:T(8,128)S(1)} %shard_map.135.refs_2_), channel_id=1, source_target_pairs={{0,4},{4,0},{1,5},{5,1},{2,6},{6,2},{3,7},{7,3},{8,12},{12,8},{9,1... | collective-permute-start | bytes 196616 | tf_op jit(solution)/shard_map/ppermute | solution.py:738
  49.0 2.0 %collective-permute-start.13 = (f32[2,2,32,128]{3,2,1,0:T(8,128)S(1)}, f32[2,2,32,128]{3,2,1,0:T(8,128)S(1)}, u32[]{:S(2)}, u32[]{:S(2)}) collective-permute-start(f32[2,2,32,128]{3,2,1,0:T(8,128)S(1)} %shard_map.138), channel_id=1, source_target_pairs={{0,16},{8,24},{16,0},{24,8},{1,17},{9,25},{17,1},{25,9},{2,18},{10... | collective-permute-start | bytes 196616 | tf_op jit(solution)/shard_map/ppermute | solution.py:744
  51.0 2.2 %collective-permute-start.15 = (f32[2,2,32,128]{3,2,1,0:T(8,128)S(1)}, f32[2,2,32,128]{3,2,1,0:T(8,128)S(1)}, u32[]{:S(2)}, u32[]{:S(2)}) collective-permute-start(f32[2,2,32,128]{3,2,1,0:T(8,128)S(1)} %shard_map.139), channel_id=1, source_target_pairs={{0,24},{8,16},{16,8},{24,0},{1,25},{9,17},{17,9},{25,1},{2,26},{10... | collective-permute-start | bytes 196616 | tf_op jit(solution)/shard_map/ppermute | solution.py:744
  53.3 2.5 %collective-permute-done.13.refs_0_ = f32[2,2,32,128]{3,2,1,0:T(8,128)S(1)} collective-permute-done((f32[2,2,32,128]{3,2,1,0:T(8,128)S(1)}, f32[2,2,32,128]{3,2,1,0:T(8,128)S(1)}, u32[]{:S(2)}, u32[]{:S(2)}) %collective-permute-start.13) | collective-permute-done | bytes 65568 | tf_op jit(solution)/shard_map/ppermute | solution.py:744
  55.8 1.4 %collective-permute-done.15.refs_1_ = f32[2,2,32,128]{3,2,1,0:T(8,128)S(1)} collective-permute-done((f32[2,2,32,128]{3,2,1,0:T(8,128)S(1)}, f32[2,2,32,128]{3,2,1,0:T(8,128)S(1)}, u32[]{:S(2)}, u32[]{:S(2)}) %collective-permute-start.15) | collective-permute-done | bytes 65568 | tf_op jit(solution)/shard_map/ppermute | solution.py:744
  58.4 11.2 %all_to_all.5.tiles = f32[32,1,128]{2,1,0:T(1,128)S(1)} all-to-all(f32[32,1,128]{2,1,0:T(1,128)S(1)} %broadcast_in_dim.3), channel_id=1, replica_groups=mesh['src'=4,'gx'=2,'gy'=4] {'src','gx','gy'}, dimensions={0} | all-to-all | bytes 32768 | tf_op jit(solution)/shard_map/all_to_all | solution.py:826
  69.6 1.0 %shard_map.144 = (f32[8,32,32]{2,1,0:T(8,128)}, f32[8,32,32]{2,1,0:T(8,128)}, f32[2]{0:T(128)}) custom-call(f32[32,1,128]{2,1,0:T(1,128)S(1)} %all_to_all.5.tiles, f32[8,32,32]{2,1,0:T(8,128)S(1)} %get-tuple-element.49.w_k, f32[8,32,32]{2,1,0:T(8,128)S(1)} %get-tuple-element.50.w_a, f32[8,32,32]{2,1,0:T(8,128)S(1)} %copy-done.1, f32[8,32,32]{2,1,0:T(8,128)S(1)} %copy-done.2), custom_call_target="tpu_custom_call" | custom-call | tf_op jit(solution)/shard_map/pallas_call | solution.py:708
  (58 shorter events, 6.6 us)
Async XLA Ops:
  0.6 10.3 %collective-permute-start = (s32[8,32,128]{2,1,0:T(8,128)}, s32[8,32,128]{2,1,0:T(8,128)S(1)}, u32[]{:S(2)}, u32[]{:S(2)}) collective-permute-start(s32[8,32,128]{2,1,0:T(8,128)} %refs_1_.3), channel_id=1, source_target_pairs={{0,4},{4,0},{1,5},{5,1},{2,6},{6,2},{3,7},{7,3},{8,12},{12,8},{9,1... | collective-permute-start | bytes 393224 | tf_op jit(solution)/shard_map/ppermute | solution.py:738
  5.5 5.4 %copy-start.8 = (s32[1024]{0:T(1024)S(1)}, s32[1024]{0:T(1024)}, u32[]{:S(2)}) copy-start(s32[1024]{0:T(1024)} %param.14) | copy-start | bytes 12292
  5.5 11.3 %collective-permute-start.1 = (f32[20,32,128]{2,1,0:T(8,128)}, f32[20,32,128]{2,1,0:T(8,128)S(1)}, u32[]{:S(2)}, u32[]{:S(2)}) collective-permute-start(f32[20,32,128]{2,1,0:T(8,128)} %get-tuple-element.28), channel_id=1, source_target_pairs={{0,4},{4,0},{1,5},{5,1},{2,6},{6,2},{3,7},{7,3},{8,12},{12,8},{9,1... | collective-permute-start | bytes 983048 | tf_op jit(solution)/shard_map/ppermute | solution.py:738
  5.6 7.5 %collective-permute-start.4 = (f32[4,32,128]{2,1,0:T(8,128)}, f32[4,32,128]{2,1,0:T(8,128)S(1)}, u32[]{:S(2)}, u32[]{:S(2)}) collective-permute-start(f32[4,32,128]{2,1,0:T(8,128)} %get-tuple-element.29), channel_id=1, source_target_pairs={{0,24},{8,16},{16,8},{24,0},{1,25},{9,17},{17,9},{25,1},{2,26},{10... | collective-permute-start | bytes 196616 | tf_op jit(solution)/shard_map/ppermute | solution.py:744
  9.7 5.5 %collective-permute-start.3 = (f32[4,32,128]{2,1,0:T(8,128)}, f32[4,32,128]{2,1,0:T(8,128)S(1)}, u32[]{:S(2)}, u32[]{:S(2)}) collective-permute-start(f32[4,32,128]{2,1,0:T(8,128)} %get-tuple-element.29), channel_id=1, source_target_pairs={{0,16},{8,24},{16,0},{24,8},{1,17},{9,25},{17,1},{25,9},{2,18},{10... | collective-permute-start | bytes 196616 | tf_op jit(solution)/shard_map/ppermute | solution.py:744
  9.7 5.5 %collective-permute-start.2 = (f32[4,32,128]{2,1,0:T(8,128)}, f32[4,32,128]{2,1,0:T(8,128)S(1)}, u32[]{:S(2)}, u32[]{:S(2)}) collective-permute-start(f32[4,32,128]{2,1,0:T(8,128)} %get-tuple-element.29), channel_id=1, source_target_pairs={{0,8},{8,0},{16,24},{24,16},{1,9},{9,1},{17,25},{25,17},{2,10},{10... | collective-permute-start | bytes 196616 | tf_op jit(solution)/shard_map/ppermute | solution.py:744
  13.1 3.7 %copy-start = (f32[4,8,32,128]{3,2,1,0:T(8,128)S(1)}, f32[4,8,32,128]{3,2,1,0:T(8,128)}, u32[]{:S(2)}) copy-start(f32[4,8,32,128]{3,2,1,0:T(8,128)} %refs_0_.2) | copy-start | bytes 1572868
  15.2 5.8 %collective-permute-start.6 = (f32[12,32,128]{2,1,0:T(8,128)S(1)}, f32[12,32,128]{2,1,0:T(8,128)S(1)}, u32[]{:S(2)}, u32[]{:S(2)}) collective-permute-start(f32[12,32,128]{2,1,0:T(8,128)S(1)} %shard_map.123.refs_4_.joined), channel_id=1, source_target_pairs={{0,4},{4,0},{1,5},{5,1},{2,6},{6,2},{3,7},{7,3},{8,12},{12,8},{9,1... | collective-permute-start | bytes 589832 | tf_op jit(solution)/shard_map/ppermute | solution.py:738
  17.4 4.0 %collective-permute-start.5 = (f32[2,16,32,128]{3,2,1,0:T(8,128)S(1)}, f32[2,16,32,128]{3,2,1,0:T(8,128)S(1)}, u32[]{:S(2)}, u32[]{:S(2)}) collective-permute-start(f32[2,16,32,128]{3,2,1,0:T(8,128)S(1)} %get-tuple-element.32.refs_1_.refs_3_), channel_id=1, source_target_pairs={{0,1},{1,0},{2,3},{3,2},{4,5},{5,4},{6,7},{7,6},{8,9},{9,8},{10,11... | collective-permute-start | bytes 1572872 | tf_op jit(solution)/shard_map/ppermute | solution.py:741
  21.4 2.0 %collective-permute-start.8 = (f32[2,16,32,128]{3,2,1,0:T(8,128)S(1)}, f32[2,16,32,128]{3,2,1,0:T(8,128)S(1)}, u32[]{:S(2)}, u32[]{:S(2)}) collective-permute-start(f32[2,16,32,128]{3,2,1,0:T(8,128)S(1)} %shard_map.126.refs_3_.refs_0_.vector), channel_id=1, source_target_pairs={{0,1},{1,0},{2,3},{3,2},{4,5},{5,4},{6,7},{7,6},{8,9},{9,8},{10,11... | collective-permute-start | bytes 1572872 | tf_op jit(solution)/shard_map/ppermute | solution.py:741
  21.5 3.5 %copy-start.6 = (f32[16]{0:T(128)S(1)}, f32[16]{0:T(128)}, u32[]{:S(2)}) copy-start(f32[16]{0:T(128)} %kap_table.1) | copy-start | bytes 196
  21.5 5.8 %collective-permute-start.7 = (f32[2,4,24,128]{3,2,1,0:T(8,128)S(1)}, f32[2,4,24,128]{3,2,1,0:T(8,128)S(1)}, u32[]{:S(2)}, u32[]{:S(2)}) collective-permute-start(f32[2,4,24,128]{3,2,1,0:T(8,128)S(1)} %shard_map.127.refs_2_), channel_id=1, source_target_pairs={{0,2},{1,3},{2,0},{3,1},{4,6},{5,7},{6,4},{7,5},{8,10},{9,11},{10,... | collective-permute-start | bytes 294920 | tf_op jit(solution)/shard_map/ppermute | solution.py:765
  23.4 5.5 %collective-permute-start.9 = (f32[2,4,24,128]{3,2,1,0:T(8,128)S(1)}, f32[2,4,24,128]{3,2,1,0:T(8,128)S(1)}, u32[]{:S(2)}, u32[]{:S(2)}) collective-permute-start(f32[2,4,24,128]{3,2,1,0:T(8,128)S(1)} %shard_map.128.refs_6_), channel_id=1, source_target_pairs={{0,2},{1,3},{2,0},{3,1},{4,6},{5,7},{6,4},{7,5},{8,10},{9,11},{10,... | collective-permute-start | bytes 294920 | tf_op jit(solution)/shard_map/ppermute | solution.py:765
  33.3 4.3 %collective-permute-start.10 = (f32[4,32,128]{2,1,0:T(8,128)S(1)}, f32[4,32,128]{2,1,0:T(8,128)S(1)}, u32[]{:S(2)}, u32[]{:S(2)}) collective-permute-start(f32[4,32,128]{2,1,0:T(8,128)S(1)} %get-tuple-element.45.sent), channel_id=1, source_target_pairs={{0,2},{1,3},{2,0},{3,1},{4,6},{5,7},{6,4},{7,5},{8,10},{9,11},{10,... | collective-permute-start | bytes 196616 | tf_op jit(solution)/shard_map/ppermute | solution.py:765
  41.8 2.0 %collective-permute-start.11 = (f32[2,16,32,128]{3,2,1,0:T(8,128)S(1)}, f32[2,16,32,128]{3,2,1,0:T(8,128)S(1)}, u32[]{:S(2)}, u32[]{:S(2)}) collective-permute-start(f32[2,16,32,128]{3,2,1,0:T(8,128)S(1)} %get-tuple-element.47), channel_id=1, source_target_pairs={{0,1},{1,0},{2,3},{3,2},{4,5},{5,4},{6,7},{7,6},{8,9},{9,8},{10,11... | collective-permute-start | bytes 1572872 | tf_op jit(solution)/shard_map/ppermute | solution.py:741
  44.1 4.9 %collective-permute-start.12 = (f32[1,2,2,32,128]{4,3,2,1,0:T(8,128)S(1)}, f32[1,2,2,32,128]{4,3,2,1,0:T(8,128)S(1)}, u32[]{:S(2)}, u32[]{:S(2)}) collective-permute-start(f32[1,2,2,32,128]{4,3,2,1,0:T(8,128)S(1)} %shard_map.134.refs_2_), channel_id=1, source_target_pairs={{0,4},{4,0},{1,5},{5,1},{2,6},{6,2},{3,7},{7,3},{8,12},{12,8},{9,1... | collective-permute-start | bytes 196616 | tf_op jit(solution)/shard_map/ppermute | solution.py:738
  45.7 5.3 %collective-permute-start.14 = (f32[1,2,2,32,128]{4,3,2,1,0:T(8,128)S(1)}, f32[1,2,2,32,128]{4,3,2,1,0:T(8,128)S(1)}, u32[]{:S(2)}, u32[]{:S(2)}) collective-permute-start(f32[1,2,2,32,128]{4,3,2,1,0:T(8,128)S(1)} %shard_map.133.refs_2_), channel_id=1, source_target_pairs={{0,4},{4,0},{1,5},{5,1},{2,6},{6,2},{3,7},{7,3},{8,12},{12,8},{9,1... | collective-permute-start | bytes 196616 | tf_op jit(solution)/shard_map/ppermute | solution.py:738
  46.3 6.8 %collective-permute-start.17 = (f32[1,2,2,32,128]{4,3,2,1,0:T(8,128)S(1)}, f32[1,2,2,32,128]{4,3,2,1,0:T(8,128)S(1)}, u32[]{:S(2)}, u32[]{:S(2)}) collective-permute-start(f32[1,2,2,32,128]{4,3,2,1,0:T(8,128)S(1)} %shard_map.135.refs_2_), channel_id=1, source_target_pairs={{0,4},{4,0},{1,5},{5,1},{2,6},{6,2},{3,7},{7,3},{8,12},{12,8},{9,1... | collective-permute-start | bytes 196616 | tf_op jit(solution)/shard_map/ppermute | solution.py:738
  48.0 5.2 %collective-permute-start.16 = (f32[1,2,2,32,128]{4,3,2,1,0:T(8,128)S(1)}, f32[1,2,2,32,128]{4,3,2,1,0:T(8,128)S(1)}, u32[]{:S(2)}, u32[]{:S(2)}) collective-permute-start(f32[1,2,2,32,128]{4,3,2,1,0:T(8,128)S(1)} %shard_map.136.refs_2_), channel_id=1, source_target_pairs={{0,4},{4,0},{1,5},{5,1},{2,6},{6,2},{3,7},{7,3},{8,12},{12,8},{9,1... | collective-permute-start | bytes 196616 | tf_op jit(solution)/shard_map/ppermute | solution.py:738
  49.0 6.8 %collective-permute-start.13 = (f32[2,2,32,128]{3,2,1,0:T(8,128)S(1)}, f32[2,2,32,128]{3,2,1,0:T(8,128)S(1)}, u32[]{:S(2)}, u32[]{:S(2)}) collective-permute-start(f32[2,2,32,128]{3,2,1,0:T(8,128)S(1)} %shard_map.138), channel_id=1, source_target_pairs={{0,16},{8,24},{16,0},{24,8},{1,17},{9,25},{17,1},{25,9},{2,18},{10... | collective-permute-start | bytes 196616 | tf_op jit(solution)/shard_map/ppermute | solution.py:744
  51.0 6.3 %collective-permute-start.15 = (f32[2,2,32,128]{3,2,1,0:T(8,128)S(1)}, f32[2,2,32,128]{3,2,1,0:T(8,128)S(1)}, u32[]{:S(2)}, u32[]{:S(2)}) collective-permute-start(f32[2,2,32,128]{3,2,1,0:T(8,128)S(1)} %shard_map.139), channel_id=1, source_target_pairs={{0,24},{8,16},{16,8},{24,0},{1,25},{9,17},{17,9},{25,1},{2,26},{10... | collective-permute-start | bytes 196616 | tf_op jit(solution)/shard_map/ppermute | solution.py:744
  53.1 4.7 %collective-permute-start.18 = (f32[2,2,32,128]{3,2,1,0:T(8,128)S(1)}, f32[2,2,32,128]{3,2,1,0:T(8,128)S(1)}, u32[]{:S(2)}, u32[]{:S(2)}) collective-permute-start(f32[2,2,32,128]{3,2,1,0:T(8,128)S(1)} %shard_map.142), channel_id=1, source_target_pairs={{0,8},{8,0},{16,24},{24,16},{1,9},{9,1},{17,25},{25,17},{2,10},{10... | collective-permute-start | bytes 196616 | tf_op jit(solution)/shard_map/ppermute | solution.py:744
  53.3 4.6 %copy-start.4 = (f32[8,32,32]{2,1,0:T(8,128)S(1)}, f32[8,32,32]{2,1,0:T(8,128)}, u32[]{:S(2)}) copy-start(f32[8,32,32]{2,1,0:T(8,128)} %refs_6_.1) | copy-start | bytes 98308
  53.3 4.6 %copy-start.5 = (f32[8,32,32]{2,1,0:T(8,128)S(1)}, f32[8,32,32]{2,1,0:T(8,128)}, u32[]{:S(2)}) copy-start(f32[8,32,32]{2,1,0:T(8,128)} %refs_7_.1) | copy-start | bytes 98308
  (4 other events, 9.6 us)

commit v17 on v16

--- a/solution.py
+++ b/solution.py
@@ -500,25 +500,37 @@
         diag[i, beside_it, :] = diag_in[i, beside_it, :] + face_up + face_down
 
 
+def density_kernel(mine, got, edge, phi, phi_y, phi_z):
+    _, _, y, c = places(2)
+    framed(phi, 1, mine, got.at[0], edge.at[0], y, c)
+    blank_ends(phi)
+
+    def differ(i, carry):
+        p = phi[i + 1]
+        phi_y[i], phi_z[i] = p - beyond(p, 1, 0), p - beyond(p, 1, 1)
+        return carry
+
+    lax.fori_loop(0, phi_y.shape[0], differ, 0, unroll=4)
+
+
 def first_kernel(
-    diag, fx, fy, fz, count, sums, mine, got_photon, vector, got_vector, photon_edge, edge,
-    phi, change, message,
+    phi, phi_y, phi_z, diag, fx, fy, fz, count, sums, vector, got_vector, edge,
+    change, message,
     vk, va, b, buf_a, buf_b,
 ):
     _, _, y, c = places(2)
     planes, rows, lanes = change.shape
-    cy = mine.shape[1]
-    framed(phi, 1, mine, got_photon.at[0], photon_edge.at[0], y, c)
+    cy = vector.shape[2]
     framed(vk, 1, vector.at[0], got_vector.at[0], edge.at[0], y, c)
     framed(va, 0, vector.at[1], got_vector.at[1], edge.at[1], y, c)
-    blank_ends(phi, vk, buf_a, buf_b)
+    blank_ends(vk, buf_a, buf_b)
     theta, _ = chebyshev_scalars()
 
     def set_up(i, carry):
         v, p = vk[i + 1], phi[i + 1]
         total = 0.5 * (v + vk[i]) * (p - phi[i]) + 0.5 * (v + vk[i + 2]) * (p - phi[i + 2])
-        for axis in range(2):
-            flow = 0.5 * (v + beyond(v, 1, axis)) * (p - beyond(p, 1, axis))
+        for axis, step in enumerate((phi_y, phi_z)):
+            flow = 0.5 * (v + beyond(v, 1, axis)) * step[i]
             first = index_along(v.shape, axis) == 0
             total = total + flow + jnp.where(first, 0.5 * v * p, -shifted(flow, 1, axis))
         total = -(va[i] * p + total)
@@ -539,15 +551,17 @@
     zero = jnp.zeros((8, lanes), jnp.float32)
     seen, cross = lax.fori_loop(0, planes, add_up, (zero, zero), unroll=4)
     first = (2 * cy - HALO) * (1 - y) + HALO * y
-    for g, part in enumerate((sums[0], seen, cross, sums[1])):
-        message[g, pl.ds(0, GROUP * REACH), :] = packed_edges(
+    size = GROUP * REACH
+    for g in range(planes // GROUP):
+        message[pl.ds(size * g, size), :] = packed_edges(
             [near_rows(found, 1 + GROUP * g + j, first, y) for j in range(GROUP)]
         )
-        message[g, pl.ds(GROUP * REACH, 8), :] = part
+    rows_of_sums = [jnp.sum(part, axis=0, keepdims=True) for part in (sums[0], seen, cross, sums[1])]
+    message[pl.ds(REACH * planes, 8), :] = jnp.concatenate([*rows_of_sums, zero[:4]], axis=0)
 
 
 def second_kernel(
-    phi, change, diag, fx, fy, fz, count, sent, came,
+    phi, phi_y, phi_z, change, diag, fx, fy, fz, count, sent, came,
     own, message,
     b, buf_a, buf_b, grad_k, grad_a,
     *, dets,
@@ -557,11 +571,9 @@
     cy = (rows - HALO) // 2
     base = HALO * y
     edge = pl.ds(2 * cy * (1 - y), HALO)
-    tail = pl.ds(GROUP * REACH, 8)
-    total, seen_sum, cross, square = (
-        jnp.sum(jnp.sum(sent[g, tail, :] + came[g, tail, :], axis=0, keepdims=True), axis=1, keepdims=True)
-        for g in range(4)
-    )
+    tail = pl.ds(REACH * planes, 8)
+    sums = jnp.sum(sent[tail, :] + came[tail, :], axis=1, keepdims=True)
+    total, seen_sum, cross, square = (sums[g : g + 1] for g in range(4))
     mean = total / dets
     part = seen_sum / total
     level = (cross - part * square) / (total * mean)
@@ -579,8 +591,9 @@
         return carry
 
     lax.fori_loop(0, planes, set_up, 0, unroll=4)
+    size = GROUP * REACH
     for i in range(planes):
-        u = edge_tile(came[i // GROUP], i % GROUP, y)
+        u = edge_tile(came[pl.ds(size * (i // GROUP), size), :], i % GROUP, y)
         value = weighted(count[i, edge, :], u, phi[i + 1, edge, :])
         b[i, edge, :] = value
         buf_a[i + 1, edge, :] = value * (1.0 / theta)
@@ -590,8 +603,8 @@
         p, u = phi[i + 1], dual[i + 1]
         grad = (p - phi[i]) * (u - dual[i]) + (p - phi[i + 2]) * (u - dual[i + 2])
         both = p * u
-        for axis in range(2):
-            flow = (p - beyond(p, 1, axis)) * (u - beyond(u, 1, axis))
+        for axis, step in enumerate((phi_y, phi_z)):
+            flow = step[i] * (u - beyond(u, 1, axis))
             first = index_along(p.shape, axis) == 0
             grad = grad + flow + jnp.where(first, both, shifted(flow, 1, axis))
         grad_k[i] = -0.5 * grad
@@ -791,17 +804,19 @@
     diag, fx, fy, fz = run(
         halo_kernel, coefs, kappa_table, absorb_table, photon_edge, kap, *partial, smem=(0, 1)
     )
-    phi, change, sent = run(
-        first_kernel, (f32(*wide), f32(*frame), f32(4, GROUP * REACH + 8, cz)),
-        diag, fx, fy, fz, count, sums, mine, got, vector, vector_got,
-        photon_edge, across_y(vector_sent),
+    densities = run(
+        density_kernel, (f32(*wide), f32(*frame), f32(*frame)), mine, got, photon_edge, after=(fz,)
+    )
+    change, sent = run(
+        first_kernel, (f32(*frame), f32(REACH * planes + 8, cz)),
+        *densities, diag, fx, fy, fz, count, sums, vector, vector_got, across_y(vector_sent),
         scratch=(float_wide, float_frame, float_frame, float_wide, float_wide),
     )
     heard = across_y(sent)
     own, message = run(
         functools.partial(second_kernel, dets=dets),
         (f32(2, planes, cy, cz), f32(2, planes, cy, cz)),
-        phi, change, diag, fx, fy, fz, count, sent, heard,
+        *densities, change, diag, fx, fy, fz, count, sent, heard,
         scratch=(float_frame, float_wide, float_wide, float_frame, float_frame),
     )
     piece = f32(2, groups, cy, cz)

time: 70.7 us -> 70 us (0.990)
    pallas_call x24 -> x25, Pallas kernels: 19.6 us -> 19.5 us  [run(): pl.pallas_call(body if waits else kernel, out_shape=tuple(outs), in_specs...]
  transfers between devices with their start and end apart: 19 -> 19, of which waited for: 9 -> 9; matrix products, arithmetic and copies ran while one was open for 0% -> 0% of each run, Pallas kernels for 13% -> 14%
where the time goes in v17:
time: 70 us; the launch traced here: 69.8 us
  starting transfers between devices  22.8 us (33%)
  Pallas kernels  19.5 us (28%)
  waiting for transfers between devices  14.7 us (21%)
  blocking collectives  11.2 us (16%)
  between operations  1.61 us (2%)
    pallas_call x25, Pallas kernels, run(): pl.pallas_call(body if waits else kernel, out_shape=tuple(outs), in_specs...  19.5 us
    all_to_all x1, blocking collectives, per_device_paired(): lax.all_to_all(jnp.broadcast_to(tile, (8 * n, 1, 128)), everyone, 0, 0)  11.2 us
    ppermute x6, starting transfers between devices, along_z(): return lax.ppermute(value, 'src', [(i, i ^ k) for i in range(n)])  8.91 us
    ppermute x7, starting transfers between devices, swap_x(): return lax.ppermute(value, 'gx', [(0, 1), (1, 0)])  8.89 us
    ppermute x6, waiting for transfers between devices, along_z(): return lax.ppermute(value, 'src', [(i, i ^ k) for i in range(n)])  6.67 us
    ppermute x3, starting transfers between devices, across_y(): return lax.ppermute(value, 'gy', [(i, (i + 2) % 4) for i in range(4)])  4.75 us
    ppermute x7, waiting for transfers between devices, swap_x(): return lax.ppermute(value, 'gx', [(0, 1), (1, 0)])  3.11 us
    ppermute x3, waiting for transfers between devices, across_y(): return lax.ppermute(value, 'gy', [(i, (i + 2) % 4) for i in range(4)])  2.85 us
  transfers between devices with their start and end apart: 19, of which 9 were waited for; matrix products, arithmetic and copies ran while one was open for 0% of the time, Pallas kernels for 14%

profile of v17, /device:TPU:0, one launch (start us, length us, event | category | flops | bytes accessed | tf_op | source)
XLA Modules:
  0.0 69.8 jit_solution(10064863623067454623)
XLA Ops:
  0.6 3.0 %collective-permute-start = (s32[8,32,128]{2,1,0:T(8,128)}, s32[8,32,128]{2,1,0:T(8,128)S(1)}, u32[]{:S(2)}, u32[]{:S(2)}) collective-permute-start(s32[8,32,128]{2,1,0:T(8,128)} %refs_1_.3), channel_id=1, source_target_pairs={{0,4},{4,0},{1,5},{5,1},{2,6},{6,2},{3,7},{7,3},{8,12},{12,8},{9,1... | collective-permute-start | bytes 393224 | tf_op jit(solution)/shard_map/ppermute | solution.py:751
  3.6 1.9 %shard_map.122 = (f32[4,32,128]{2,1,0:T(8,128)}, f32[20,32,128]{2,1,0:T(8,128)}) custom-call(f32[4,8,32,128]{3,2,1,0:T(8,128)} %refs_0_.2, f32[8,32,32]{2,1,0:T(8,128)} %vk.5, f32[8,32,32]{2,1,0:T(8,128)} %va.5), custom_call_target="tpu_custom_call" | custom-call | tf_op jit(solution)/shard_map/pallas_call | solution.py:721
  5.6 4.1 %collective-permute-start.4 = (f32[4,32,128]{2,1,0:T(8,128)}, f32[4,32,128]{2,1,0:T(8,128)S(1)}, u32[]{:S(2)}, u32[]{:S(2)}) collective-permute-start(f32[4,32,128]{2,1,0:T(8,128)} %get-tuple-element.31), channel_id=1, source_target_pairs={{0,24},{8,16},{16,8},{24,0},{1,25},{9,17},{17,9},{25,1},{2,26},{10... | collective-permute-start | bytes 196616 | tf_op jit(solution)/shard_map/ppermute | solution.py:757
  11.0 2.1 %shard_map.121 = (f32[16,72,128]{2,1,0:T(8,128)S(1)}, f32[1,128]{1,0:T(1,128)S(1)}) custom-call(s32[1,1024]{1,0:T(1,128)S(1)} %bitcast.3, f32[1]{0:T(128)S(6)} %copy.13.refs_1_, s32[8,32,128]{2,1,0:T(8,128)S(1)} %collective-permute-done.refs_2_.refs_3_), custom_call_target="tpu_custom_call" | custom-call | flops 301989888 | bytes 589824 | tf_op jit(solution)/shard_map/pallas_call | solution.py:721
  13.1 2.1 %collective-permute-done.3.refs_1_ = f32[4,32,128]{2,1,0:T(8,128)S(1)} collective-permute-done((f32[4,32,128]{2,1,0:T(8,128)}, f32[4,32,128]{2,1,0:T(8,128)S(1)}, u32[]{:S(2)}, u32[]{:S(2)}) %collective-permute-start.3) | collective-permute-done | bytes 65568 | tf_op jit(solution)/shard_map/ppermute | solution.py:757
  15.2 1.6 %collective-permute-start.6 = (f32[12,32,128]{2,1,0:T(8,128)S(1)}, f32[12,32,128]{2,1,0:T(8,128)S(1)}, u32[]{:S(2)}, u32[]{:S(2)}) collective-permute-start(f32[12,32,128]{2,1,0:T(8,128)S(1)} %shard_map.123.refs_4_.joined), channel_id=1, source_target_pairs={{0,4},{4,0},{1,5},{5,1},{2,6},{6,2},{3,7},{7,3},{8,12},{12,8},{9,1... | collective-permute-start | bytes 589832 | tf_op jit(solution)/shard_map/ppermute | solution.py:751
  17.9 3.1 %collective-permute-done.6.refs_2_ = f32[12,32,128]{2,1,0:T(8,128)S(1)} collective-permute-done((f32[12,32,128]{2,1,0:T(8,128)S(1)}, f32[12,32,128]{2,1,0:T(8,128)S(1)}, u32[]{:S(2)}, u32[]{:S(2)}) %collective-permute-start.6) | collective-permute-done | bytes 196640 | tf_op jit(solution)/shard_map/ppermute | solution.py:751
  21.5 1.6 %collective-permute-start.7 = (f32[2,4,24,128]{3,2,1,0:T(8,128)S(1)}, f32[2,4,24,128]{3,2,1,0:T(8,128)S(1)}, u32[]{:S(2)}, u32[]{:S(2)}) collective-permute-start(f32[2,4,24,128]{3,2,1,0:T(8,128)S(1)} %shard_map.127.refs_2_), channel_id=1, source_target_pairs={{0,2},{1,3},{2,0},{3,1},{4,6},{5,7},{6,4},{7,5},{8,10},{9,11},{10,... | collective-permute-start | bytes 294920 | tf_op jit(solution)/shard_map/ppermute | solution.py:778
  23.4 1.6 %collective-permute-start.9 = (f32[2,4,24,128]{3,2,1,0:T(8,128)S(1)}, f32[2,4,24,128]{3,2,1,0:T(8,128)S(1)}, u32[]{:S(2)}, u32[]{:S(2)}) collective-permute-start(f32[2,4,24,128]{3,2,1,0:T(8,128)S(1)} %shard_map.128.refs_6_), channel_id=1, source_target_pairs={{0,2},{1,3},{2,0},{3,1},{4,6},{5,7},{6,4},{7,5},{8,10},{9,11},{10,... | collective-permute-start | bytes 294920 | tf_op jit(solution)/shard_map/ppermute | solution.py:778
  25.0 2.3 %shard_map.129 = (f32[18,72,128]{2,1,0:T(8,128)S(1)}, f32[16,72,128]{2,1,0:T(8,128)S(1)}, f32[17,72,128]{2,1,0:T(8,128)S(1)}, f32[16,72,128]{2,1,0:T(8,128)S(1)}...) custom-call(f32[16]{0:T(128)S(1)} %copy-done.6, f32[16]{0:T(128)S(1)} %copy-done.7, ...), custom_call_target="tpu_custom_call" | custom-call | flops 1000000000 | bytes 67108864 | tf_op jit(solution)/shard_map/pallas_call | solution.py:721
  27.3 0.8 %shard_map.130 = (f32[16,72,128]{2,1,0:T(8,128)S(1)}, f32[17,72,128]{2,1,0:T(8,128)S(1)}, f32[16,72,128]{2,1,0:T(8,128)S(1)}, f32[16,72,128]{2,1,0:T(8,128)S(1)}) custom-call(f32[16]{0:T(128)S(1)} %copy-done.6, f32[16]{0:T(128)S(1)} %copy-done.7, f32[2,4,24,128]{3,2,1,0:T(8,128)S(1)} %collective-permute-done.7.edge.refs_2_, ...), custom_call_target="tpu_custom_call" | custom-call | tf_op jit(solution)/shard_map/pallas_call | solution.py:721
  28.9 3.9 %shard_map.132 = (f32[16,72,128]{2,1,0:T(8,128)S(1)}, f32[104,128]{1,0:T(8,128)S(1)}) custom-call(f32[18,72,128]{2,1,0:T(8,128)S(1)} %get-tuple-element.41.phi, f32[16,72,128]{2,1,0:T(8,128)S(1)} %get-tuple-element.42.phi_y, f32[16,72,128]{2,1,0:T(8,128)S(1)} %get-tuple-element.43.phi_z, f32[16,72,128]{2,1,0:T(8,128)S(1)} %get-tuple-element.44.diag, ...), custom_call_target="tpu_custom_call" | custom-call | tf_op jit(solution)/shard_map/pallas_call | solution.py:721
  32.8 1.6 %collective-permute-start.10 = (f32[104,128]{1,0:T(8,128)S(1)}, f32[104,128]{1,0:T(8,128)S(1)}, u32[]{:S(2)}, u32[]{:S(2)}) collective-permute-start(f32[104,128]{1,0:T(8,128)S(1)} %get-tuple-element.49.sent), channel_id=1, source_target_pairs={{0,2},{1,3},{2,0},{3,1},{4,6},{5,7},{6,4},{7,5},{8,10},{9,11},{10,... | collective-permute-start | bytes 159752 | tf_op jit(solution)/shard_map/ppermute | solution.py:778
  34.4 2.6 %collective-permute-done.10.came = f32[104,128]{1,0:T(8,128)S(1)} collective-permute-done((f32[104,128]{1,0:T(8,128)S(1)}, f32[104,128]{1,0:T(8,128)S(1)}, u32[]{:S(2)}, u32[]{:S(2)}) %collective-permute-start.10) | collective-permute-done | bytes 53280 | tf_op jit(solution)/shard_map/ppermute | solution.py:778
  37.0 4.1 %shard_map.133 = (f32[2,16,32,128]{3,2,1,0:T(8,128)S(1)}, f32[2,16,32,128]{3,2,1,0:T(8,128)S(1)}) custom-call(f32[18,72,128]{2,1,0:T(8,128)S(1)} %get-tuple-element.41.phi, f32[16,72,128]{2,1,0:T(8,128)S(1)} %get-tuple-element.42.phi_y, f32[16,72,128]{2,1,0:T(8,128)S(1)} %get-tuple-element.43.phi_z, f32[16,72,128]{2,1,0:T(8,128)S(1)} %get-tuple-element.48.change, ...), custom_call_target="tpu_custom_call" | custom-call | tf_op jit(solution)/shard_map/pallas_call | solution.py:721
  41.1 1.9 %collective-permute-done.11.came.refs_1_ = f32[2,16,32,128]{3,2,1,0:T(8,128)S(1)} collective-permute-done((f32[2,16,32,128]{3,2,1,0:T(8,128)S(1)}, f32[2,16,32,128]{3,2,1,0:T(8,128)S(1)}, u32[]{:S(2)}, u32[]{:S(2)}) %collective-permute-start.11) | collective-permute-done | bytes 524320 | tf_op jit(solution)/shard_map/ppermute | solution.py:754
  43.3 1.6 %collective-permute-start.12 = (f32[1,2,2,32,128]{4,3,2,1,0:T(8,128)S(1)}, f32[1,2,2,32,128]{4,3,2,1,0:T(8,128)S(1)}, u32[]{:S(2)}, u32[]{:S(2)}) collective-permute-start(f32[1,2,2,32,128]{4,3,2,1,0:T(8,128)S(1)} %shard_map.135.refs_2_), channel_id=1, source_target_pairs={{0,4},{4,0},{1,5},{5,1},{2,6},{6,2},{3,7},{7,3},{8,12},{12,8},{9,1... | collective-permute-start | bytes 196616 | tf_op jit(solution)/shard_map/ppermute | solution.py:751
  45.6 1.6 %collective-permute-start.17 = (f32[1,2,2,32,128]{4,3,2,1,0:T(8,128)S(1)}, f32[1,2,2,32,128]{4,3,2,1,0:T(8,128)S(1)}, u32[]{:S(2)}, u32[]{:S(2)}) collective-permute-start(f32[1,2,2,32,128]{4,3,2,1,0:T(8,128)S(1)} %shard_map.136.refs_2_), channel_id=1, source_target_pairs={{0,4},{4,0},{1,5},{5,1},{2,6},{6,2},{3,7},{7,3},{8,12},{12,8},{9,1... | collective-permute-start | bytes 196616 | tf_op jit(solution)/shard_map/ppermute | solution.py:751
  48.3 2.0 %collective-permute-start.13 = (f32[2,2,32,128]{3,2,1,0:T(8,128)S(1)}, f32[2,2,32,128]{3,2,1,0:T(8,128)S(1)}, u32[]{:S(2)}, u32[]{:S(2)}) collective-permute-start(f32[2,2,32,128]{3,2,1,0:T(8,128)S(1)} %shard_map.139), channel_id=1, source_target_pairs={{0,16},{8,24},{16,0},{24,8},{1,17},{9,25},{17,1},{25,9},{2,18},{10... | collective-permute-start | bytes 196616 | tf_op jit(solution)/shard_map/ppermute | solution.py:757
  50.2 2.1 %collective-permute-start.15 = (f32[2,2,32,128]{3,2,1,0:T(8,128)S(1)}, f32[2,2,32,128]{3,2,1,0:T(8,128)S(1)}, u32[]{:S(2)}, u32[]{:S(2)}) collective-permute-start(f32[2,2,32,128]{3,2,1,0:T(8,128)S(1)} %shard_map.140), channel_id=1, source_target_pairs={{0,24},{8,16},{16,8},{24,0},{1,25},{9,17},{17,9},{25,1},{2,26},{10... | collective-permute-start | bytes 196616 | tf_op jit(solution)/shard_map/ppermute | solution.py:757
  52.6 2.5 %collective-permute-done.13.refs_0_ = f32[2,2,32,128]{3,2,1,0:T(8,128)S(1)} collective-permute-done((f32[2,2,32,128]{3,2,1,0:T(8,128)S(1)}, f32[2,2,32,128]{3,2,1,0:T(8,128)S(1)}, u32[]{:S(2)}, u32[]{:S(2)}) %collective-permute-start.13) | collective-permute-done | bytes 65568 | tf_op jit(solution)/shard_map/ppermute | solution.py:757
  55.1 1.4 %collective-permute-done.15.refs_1_ = f32[2,2,32,128]{3,2,1,0:T(8,128)S(1)} collective-permute-done((f32[2,2,32,128]{3,2,1,0:T(8,128)S(1)}, f32[2,2,32,128]{3,2,1,0:T(8,128)S(1)}, u32[]{:S(2)}, u32[]{:S(2)}) %collective-permute-start.15) | collective-permute-done | bytes 65568 | tf_op jit(solution)/shard_map/ppermute | solution.py:757
  57.7 11.2 %all_to_all.5.tiles = f32[32,1,128]{2,1,0:T(1,128)S(1)} all-to-all(f32[32,1,128]{2,1,0:T(1,128)S(1)} %broadcast_in_dim.3), channel_id=1, replica_groups=mesh['src'=4,'gx'=2,'gy'=4] {'src','gx','gy'}, dimensions={0} | all-to-all | bytes 32768 | tf_op jit(solution)/shard_map/all_to_all | solution.py:841
  68.8 1.0 %shard_map.145 = (f32[8,32,32]{2,1,0:T(8,128)}, f32[8,32,32]{2,1,0:T(8,128)}, f32[2]{0:T(128)}) custom-call(f32[32,1,128]{2,1,0:T(1,128)S(1)} %all_to_all.5.tiles, f32[8,32,32]{2,1,0:T(8,128)S(1)} %get-tuple-element.53.w_k, f32[8,32,32]{2,1,0:T(8,128)S(1)} %get-tuple-element.54.w_a, f32[8,32,32]{2,1,0:T(8,128)S(1)} %copy-done.1, f32[8,32,32]{2,1,0:T(8,128)S(1)} %copy-done.2), custom_call_target="tpu_custom_call" | custom-call | tf_op jit(solution)/shard_map/pallas_call | solution.py:721
  (59 shorter events, 6.6 us)
Async XLA Ops:
  0.6 10.3 %collective-permute-start = (s32[8,32,128]{2,1,0:T(8,128)}, s32[8,32,128]{2,1,0:T(8,128)S(1)}, u32[]{:S(2)}, u32[]{:S(2)}) collective-permute-start(s32[8,32,128]{2,1,0:T(8,128)} %refs_1_.3), channel_id=1, source_target_pairs={{0,4},{4,0},{1,5},{5,1},{2,6},{6,2},{3,7},{7,3},{8,12},{12,8},{9,1... | collective-permute-start | bytes 393224 | tf_op jit(solution)/shard_map/ppermute | solution.py:751
  5.5 5.4 %copy-start.8 = (s32[1024]{0:T(1024)S(1)}, s32[1024]{0:T(1024)}, u32[]{:S(2)}) copy-start(s32[1024]{0:T(1024)} %param.14) | copy-start | bytes 12292
  5.5 11.3 %collective-permute-start.1 = (f32[20,32,128]{2,1,0:T(8,128)}, f32[20,32,128]{2,1,0:T(8,128)S(1)}, u32[]{:S(2)}, u32[]{:S(2)}) collective-permute-start(f32[20,32,128]{2,1,0:T(8,128)} %get-tuple-element.30), channel_id=1, source_target_pairs={{0,4},{4,0},{1,5},{5,1},{2,6},{6,2},{3,7},{7,3},{8,12},{12,8},{9,1... | collective-permute-start | bytes 983048 | tf_op jit(solution)/shard_map/ppermute | solution.py:751
  5.6 7.5 %collective-permute-start.4 = (f32[4,32,128]{2,1,0:T(8,128)}, f32[4,32,128]{2,1,0:T(8,128)S(1)}, u32[]{:S(2)}, u32[]{:S(2)}) collective-permute-start(f32[4,32,128]{2,1,0:T(8,128)} %get-tuple-element.31), channel_id=1, source_target_pairs={{0,24},{8,16},{16,8},{24,0},{1,25},{9,17},{17,9},{25,1},{2,26},{10... | collective-permute-start | bytes 196616 | tf_op jit(solution)/shard_map/ppermute | solution.py:757
  9.7 5.5 %collective-permute-start.3 = (f32[4,32,128]{2,1,0:T(8,128)}, f32[4,32,128]{2,1,0:T(8,128)S(1)}, u32[]{:S(2)}, u32[]{:S(2)}) collective-permute-start(f32[4,32,128]{2,1,0:T(8,128)} %get-tuple-element.31), channel_id=1, source_target_pairs={{0,16},{8,24},{16,0},{24,8},{1,17},{9,25},{17,1},{25,9},{2,18},{10... | collective-permute-start | bytes 196616 | tf_op jit(solution)/shard_map/ppermute | solution.py:757
  9.7 5.5 %collective-permute-start.2 = (f32[4,32,128]{2,1,0:T(8,128)}, f32[4,32,128]{2,1,0:T(8,128)S(1)}, u32[]{:S(2)}, u32[]{:S(2)}) collective-permute-start(f32[4,32,128]{2,1,0:T(8,128)} %get-tuple-element.31), channel_id=1, source_target_pairs={{0,8},{8,0},{16,24},{24,16},{1,9},{9,1},{17,25},{25,17},{2,10},{10... | collective-permute-start | bytes 196616 | tf_op jit(solution)/shard_map/ppermute | solution.py:757
  13.1 3.7 %copy-start = (f32[4,8,32,128]{3,2,1,0:T(8,128)S(1)}, f32[4,8,32,128]{3,2,1,0:T(8,128)}, u32[]{:S(2)}) copy-start(f32[4,8,32,128]{3,2,1,0:T(8,128)} %refs_0_.2) | copy-start | bytes 1572868
  15.2 5.8 %collective-permute-start.6 = (f32[12,32,128]{2,1,0:T(8,128)S(1)}, f32[12,32,128]{2,1,0:T(8,128)S(1)}, u32[]{:S(2)}, u32[]{:S(2)}) collective-permute-start(f32[12,32,128]{2,1,0:T(8,128)S(1)} %shard_map.123.refs_4_.joined), channel_id=1, source_target_pairs={{0,4},{4,0},{1,5},{5,1},{2,6},{6,2},{3,7},{7,3},{8,12},{12,8},{9,1... | collective-permute-start | bytes 589832 | tf_op jit(solution)/shard_map/ppermute | solution.py:751
  17.4 4.0 %collective-permute-start.5 = (f32[2,16,32,128]{3,2,1,0:T(8,128)S(1)}, f32[2,16,32,128]{3,2,1,0:T(8,128)S(1)}, u32[]{:S(2)}, u32[]{:S(2)}) collective-permute-start(f32[2,16,32,128]{3,2,1,0:T(8,128)S(1)} %get-tuple-element.34.refs_1_.refs_3_), channel_id=1, source_target_pairs={{0,1},{1,0},{2,3},{3,2},{4,5},{5,4},{6,7},{7,6},{8,9},{9,8},{10,11... | collective-permute-start | bytes 1572872 | tf_op jit(solution)/shard_map/ppermute | solution.py:754
  21.4 2.0 %collective-permute-start.8 = (f32[2,16,32,128]{3,2,1,0:T(8,128)S(1)}, f32[2,16,32,128]{3,2,1,0:T(8,128)S(1)}, u32[]{:S(2)}, u32[]{:S(2)}) collective-permute-start(f32[2,16,32,128]{3,2,1,0:T(8,128)S(1)} %shard_map.126.refs_3_.refs_0_.vector), channel_id=1, source_target_pairs={{0,1},{1,0},{2,3},{3,2},{4,5},{5,4},{6,7},{7,6},{8,9},{9,8},{10,11... | collective-permute-start | bytes 1572872 | tf_op jit(solution)/shard_map/ppermute | solution.py:754
  21.5 3.5 %copy-start.6 = (f32[16]{0:T(128)S(1)}, f32[16]{0:T(128)}, u32[]{:S(2)}) copy-start(f32[16]{0:T(128)} %kap_table.1) | copy-start | bytes 196
  21.5 5.8 %collective-permute-start.7 = (f32[2,4,24,128]{3,2,1,0:T(8,128)S(1)}, f32[2,4,24,128]{3,2,1,0:T(8,128)S(1)}, u32[]{:S(2)}, u32[]{:S(2)}) collective-permute-start(f32[2,4,24,128]{3,2,1,0:T(8,128)S(1)} %shard_map.127.refs_2_), channel_id=1, source_target_pairs={{0,2},{1,3},{2,0},{3,1},{4,6},{5,7},{6,4},{7,5},{8,10},{9,11},{10,... | collective-permute-start | bytes 294920 | tf_op jit(solution)/shard_map/ppermute | solution.py:778
  23.4 5.5 %collective-permute-start.9 = (f32[2,4,24,128]{3,2,1,0:T(8,128)S(1)}, f32[2,4,24,128]{3,2,1,0:T(8,128)S(1)}, u32[]{:S(2)}, u32[]{:S(2)}) collective-permute-start(f32[2,4,24,128]{3,2,1,0:T(8,128)S(1)} %shard_map.128.refs_6_), channel_id=1, source_target_pairs={{0,2},{1,3},{2,0},{3,1},{4,6},{5,7},{6,4},{7,5},{8,10},{9,11},{10,... | collective-permute-start | bytes 294920 | tf_op jit(solution)/shard_map/ppermute | solution.py:778
  32.8 4.2 %collective-permute-start.10 = (f32[104,128]{1,0:T(8,128)S(1)}, f32[104,128]{1,0:T(8,128)S(1)}, u32[]{:S(2)}, u32[]{:S(2)}) collective-permute-start(f32[104,128]{1,0:T(8,128)S(1)} %get-tuple-element.49.sent), channel_id=1, source_target_pairs={{0,2},{1,3},{2,0},{3,1},{4,6},{5,7},{6,4},{7,5},{8,10},{9,11},{10,... | collective-permute-start | bytes 159752 | tf_op jit(solution)/shard_map/ppermute | solution.py:778
  41.1 2.0 %collective-permute-start.11 = (f32[2,16,32,128]{3,2,1,0:T(8,128)S(1)}, f32[2,16,32,128]{3,2,1,0:T(8,128)S(1)}, u32[]{:S(2)}, u32[]{:S(2)}) collective-permute-start(f32[2,16,32,128]{3,2,1,0:T(8,128)S(1)} %get-tuple-element.51), channel_id=1, source_target_pairs={{0,1},{1,0},{2,3},{3,2},{4,5},{5,4},{6,7},{7,6},{8,9},{9,8},{10,11... | collective-permute-start | bytes 1572872 | tf_op jit(solution)/shard_map/ppermute | solution.py:754
  43.3 4.9 %collective-permute-start.12 = (f32[1,2,2,32,128]{4,3,2,1,0:T(8,128)S(1)}, f32[1,2,2,32,128]{4,3,2,1,0:T(8,128)S(1)}, u32[]{:S(2)}, u32[]{:S(2)}) collective-permute-start(f32[1,2,2,32,128]{4,3,2,1,0:T(8,128)S(1)} %shard_map.135.refs_2_), channel_id=1, source_target_pairs={{0,4},{4,0},{1,5},{5,1},{2,6},{6,2},{3,7},{7,3},{8,12},{12,8},{9,1... | collective-permute-start | bytes 196616 | tf_op jit(solution)/shard_map/ppermute | solution.py:751
  44.9 5.3 %collective-permute-start.14 = (f32[1,2,2,32,128]{4,3,2,1,0:T(8,128)S(1)}, f32[1,2,2,32,128]{4,3,2,1,0:T(8,128)S(1)}, u32[]{:S(2)}, u32[]{:S(2)}) collective-permute-start(f32[1,2,2,32,128]{4,3,2,1,0:T(8,128)S(1)} %shard_map.134.refs_2_), channel_id=1, source_target_pairs={{0,4},{4,0},{1,5},{5,1},{2,6},{6,2},{3,7},{7,3},{8,12},{12,8},{9,1... | collective-permute-start | bytes 196616 | tf_op jit(solution)/shard_map/ppermute | solution.py:751
  45.6 6.8 %collective-permute-start.17 = (f32[1,2,2,32,128]{4,3,2,1,0:T(8,128)S(1)}, f32[1,2,2,32,128]{4,3,2,1,0:T(8,128)S(1)}, u32[]{:S(2)}, u32[]{:S(2)}) collective-permute-start(f32[1,2,2,32,128]{4,3,2,1,0:T(8,128)S(1)} %shard_map.136.refs_2_), channel_id=1, source_target_pairs={{0,4},{4,0},{1,5},{5,1},{2,6},{6,2},{3,7},{7,3},{8,12},{12,8},{9,1... | collective-permute-start | bytes 196616 | tf_op jit(solution)/shard_map/ppermute | solution.py:751
  47.3 5.2 %collective-permute-start.16 = (f32[1,2,2,32,128]{4,3,2,1,0:T(8,128)S(1)}, f32[1,2,2,32,128]{4,3,2,1,0:T(8,128)S(1)}, u32[]{:S(2)}, u32[]{:S(2)}) collective-permute-start(f32[1,2,2,32,128]{4,3,2,1,0:T(8,128)S(1)} %shard_map.137.refs_2_), channel_id=1, source_target_pairs={{0,4},{4,0},{1,5},{5,1},{2,6},{6,2},{3,7},{7,3},{8,12},{12,8},{9,1... | collective-permute-start | bytes 196616 | tf_op jit(solution)/shard_map/ppermute | solution.py:751
  48.3 6.8 %collective-permute-start.13 = (f32[2,2,32,128]{3,2,1,0:T(8,128)S(1)}, f32[2,2,32,128]{3,2,1,0:T(8,128)S(1)}, u32[]{:S(2)}, u32[]{:S(2)}) collective-permute-start(f32[2,2,32,128]{3,2,1,0:T(8,128)S(1)} %shard_map.139), channel_id=1, source_target_pairs={{0,16},{8,24},{16,0},{24,8},{1,17},{9,25},{17,1},{25,9},{2,18},{10... | collective-permute-start | bytes 196616 | tf_op jit(solution)/shard_map/ppermute | solution.py:757
  50.2 6.3 %collective-permute-start.15 = (f32[2,2,32,128]{3,2,1,0:T(8,128)S(1)}, f32[2,2,32,128]{3,2,1,0:T(8,128)S(1)}, u32[]{:S(2)}, u32[]{:S(2)}) collective-permute-start(f32[2,2,32,128]{3,2,1,0:T(8,128)S(1)} %shard_map.140), channel_id=1, source_target_pairs={{0,24},{8,16},{16,8},{24,0},{1,25},{9,17},{17,9},{25,1},{2,26},{10... | collective-permute-start | bytes 196616 | tf_op jit(solution)/shard_map/ppermute | solution.py:757
  52.4 4.8 %collective-permute-start.18 = (f32[2,2,32,128]{3,2,1,0:T(8,128)S(1)}, f32[2,2,32,128]{3,2,1,0:T(8,128)S(1)}, u32[]{:S(2)}, u32[]{:S(2)}) collective-permute-start(f32[2,2,32,128]{3,2,1,0:T(8,128)S(1)} %shard_map.143), channel_id=1, source_target_pairs={{0,8},{8,0},{16,24},{24,16},{1,9},{9,1},{17,25},{25,17},{2,10},{10... | collective-permute-start | bytes 196616 | tf_op jit(solution)/shard_map/ppermute | solution.py:757
  52.5 4.6 %copy-start.4 = (f32[8,32,32]{2,1,0:T(8,128)S(1)}, f32[8,32,32]{2,1,0:T(8,128)}, u32[]{:S(2)}) copy-start(f32[8,32,32]{2,1,0:T(8,128)} %refs_6_.1) | copy-start | bytes 98308
  52.6 4.6 %copy-start.5 = (f32[8,32,32]{2,1,0:T(8,128)S(1)}, f32[8,32,32]{2,1,0:T(8,128)}, u32[]{:S(2)}) copy-start(f32[8,32,32]{2,1,0:T(8,128)} %refs_7_.1) | copy-start | bytes 98308
  (4 other events, 9.6 us)

commit v18 on v17

--- a/solution.py
+++ b/solution.py
@@ -356,11 +356,12 @@
         edges_of(fields.at[f], got.at[f], edge.at[f], y, c)
 
 
-def solve(b, bufs, diag, fx, fy, fz, unroll):
+def solve(b, bufs, diag, fx, fy, fz, unroll, finish=None, begin=0):
     planes = b.shape[0]
     _, pairs = chebyshev_scalars()
     for step, (keep, push) in enumerate(pairs):
         src, dst = bufs[step % 2], bufs[(step + 1) % 2]
+        ends = finish is not None and step + 1 == len(pairs)
 
         def body(i, carry):
             u = src[i + 1]
@@ -370,11 +371,14 @@
             left = left + coef_y * shifted(u, -1, 0) + shifted(coef_y * u, 1, 0)
             left = left + coef_z * shifted(u, -1, 1) + shifted(coef_z * u, 1, 1)
             change = u if step == 0 else u - dst[i + 1]
-            dst[i + 1] = u + keep * change + push * left
+            value = u + keep * change + push * left
+            if ends:
+                return finish(i, value, carry)
+            dst[i + 1] = value
             return carry
 
-        lax.fori_loop(0, planes, body, 0, unroll=unroll)
-    return bufs[len(pairs) % 2]
+        added = lax.fori_loop(0, planes, body, begin if ends else 0, unroll=unroll)
+    return bufs[len(pairs) % 2] if finish is None else added
 
 
 def folded(value):
@@ -539,22 +543,20 @@
         return carry
 
     lax.fori_loop(0, planes, set_up, 0, unroll=4)
-    found = solve(b, (buf_a, buf_b), diag, fx, fy, fz, UNROLL)
     owned = owned_rows((rows, lanes), HALO * y, 2 * cy)
 
-    def add_up(i, carry):
-        u = found[i + 1]
+    def add_up(i, u, carry):
         change[i] = u
         part = jnp.where(owned, count[i], 0.0) * u
         return carry[0] + folded(part), carry[1] + folded(part * phi[i + 1])
 
     zero = jnp.zeros((8, lanes), jnp.float32)
-    seen, cross = lax.fori_loop(0, planes, add_up, (zero, zero), unroll=4)
+    seen, cross = solve(b, (buf_a, buf_b), diag, fx, fy, fz, UNROLL, add_up, (zero, zero))
     first = (2 * cy - HALO) * (1 - y) + HALO * y
     size = GROUP * REACH
     for g in range(planes // GROUP):
         message[pl.ds(size * g, size), :] = packed_edges(
-            [near_rows(found, 1 + GROUP * g + j, first, y) for j in range(GROUP)]
+            [near_rows(change, GROUP * g + j, first, y) for j in range(GROUP)]
         )
     rows_of_sums = [jnp.sum(part, axis=0, keepdims=True) for part in (sums[0], seen, cross, sums[1])]
     message[pl.ds(REACH * planes, 8), :] = jnp.concatenate([*rows_of_sums, zero[:4]], axis=0)
@@ -730,7 +732,7 @@
 
 
 HALO = 8
-UNROLL = 16
+UNROLL = 8
 REACH = 6
 GROUP = 4
 

time: 70 us -> 70.5 us (level)
  no operation moved by 1% of the time
where the time goes in v18:
time: 70.5 us; the launch traced here: 70.3 us
  starting transfers between devices  22.8 us (32%)
  Pallas kernels  19.9 us (28%)
  waiting for transfers between devices  14.7 us (21%)
  blocking collectives  11.2 us (16%)
  between operations  1.61 us (2%)
    pallas_call x25, Pallas kernels, run(): pl.pallas_call(body if waits else kernel, out_shape=tuple(outs), in_specs...  19.9 us
    all_to_all x1, blocking collectives, per_device_paired(): lax.all_to_all(jnp.broadcast_to(tile, (8 * n, 1, 128)), everyone, 0, 0)  11.2 us
    ppermute x6, starting transfers between devices, along_z(): return lax.ppermute(value, 'src', [(i, i ^ k) for i in range(n)])  8.91 us
    ppermute x7, starting transfers between devices, swap_x(): return lax.ppermute(value, 'gx', [(0, 1), (1, 0)])  8.89 us
    ppermute x6, waiting for transfers between devices, along_z(): return lax.ppermute(value, 'src', [(i, i ^ k) for i in range(n)])  6.67 us
    ppermute x3, starting transfers between devices, across_y(): return lax.ppermute(value, 'gy', [(i, (i + 2) % 4) for i in range(4)])  4.75 us
    ppermute x7, waiting for transfers between devices, swap_x(): return lax.ppermute(value, 'gx', [(0, 1), (1, 0)])  3.11 us
    ppermute x3, waiting for transfers between devices, across_y(): return lax.ppermute(value, 'gy', [(i, (i + 2) % 4) for i in range(4)])  2.85 us
  transfers between devices with their start and end apart: 19, of which 9 were waited for; matrix products, arithmetic and copies ran while one was open for 0% of the time, Pallas kernels for 14%

profile of v18, /device:TPU:0, one launch (start us, length us, event | category | flops | bytes accessed | tf_op | source)
XLA Modules:
  0.0 70.3 jit_solution(16017926693996774272)
XLA Ops:
  0.6 3.0 %collective-permute-start = (s32[8,32,128]{2,1,0:T(8,128)}, s32[8,32,128]{2,1,0:T(8,128)S(1)}, u32[]{:S(2)}, u32[]{:S(2)}) collective-permute-start(s32[8,32,128]{2,1,0:T(8,128)} %refs_1_.3), channel_id=1, source_target_pairs={{0,4},{4,0},{1,5},{5,1},{2,6},{6,2},{3,7},{7,3},{8,12},{12,8},{9,1... | collective-permute-start | bytes 393224 | tf_op jit(solution)/shard_map/ppermute | solution.py:753
  3.6 1.9 %shard_map.122 = (f32[4,32,128]{2,1,0:T(8,128)}, f32[20,32,128]{2,1,0:T(8,128)}) custom-call(f32[4,8,32,128]{3,2,1,0:T(8,128)} %refs_0_.2, f32[8,32,32]{2,1,0:T(8,128)} %vk.5, f32[8,32,32]{2,1,0:T(8,128)} %va.5), custom_call_target="tpu_custom_call" | custom-call | tf_op jit(solution)/shard_map/pallas_call | solution.py:723
  5.6 4.1 %collective-permute-start.4 = (f32[4,32,128]{2,1,0:T(8,128)}, f32[4,32,128]{2,1,0:T(8,128)S(1)}, u32[]{:S(2)}, u32[]{:S(2)}) collective-permute-start(f32[4,32,128]{2,1,0:T(8,128)} %get-tuple-element.31), channel_id=1, source_target_pairs={{0,24},{8,16},{16,8},{24,0},{1,25},{9,17},{17,9},{25,1},{2,26},{10... | collective-permute-start | bytes 196616 | tf_op jit(solution)/shard_map/ppermute | solution.py:759
  11.0 2.1 %shard_map.121 = (f32[16,72,128]{2,1,0:T(8,128)S(1)}, f32[1,128]{1,0:T(1,128)S(1)}) custom-call(s32[1,1024]{1,0:T(1,128)S(1)} %bitcast.3, f32[1]{0:T(128)S(6)} %copy.13.refs_1_, s32[8,32,128]{2,1,0:T(8,128)S(1)} %collective-permute-done.refs_2_.refs_3_), custom_call_target="tpu_custom_call" | custom-call | flops 301989888 | bytes 589824 | tf_op jit(solution)/shard_map/pallas_call | solution.py:723
  13.1 2.1 %collective-permute-done.3.refs_1_ = f32[4,32,128]{2,1,0:T(8,128)S(1)} collective-permute-done((f32[4,32,128]{2,1,0:T(8,128)}, f32[4,32,128]{2,1,0:T(8,128)S(1)}, u32[]{:S(2)}, u32[]{:S(2)}) %collective-permute-start.3) | collective-permute-done | bytes 65568 | tf_op jit(solution)/shard_map/ppermute | solution.py:759
  15.2 1.6 %collective-permute-start.6 = (f32[12,32,128]{2,1,0:T(8,128)S(1)}, f32[12,32,128]{2,1,0:T(8,128)S(1)}, u32[]{:S(2)}, u32[]{:S(2)}) collective-permute-start(f32[12,32,128]{2,1,0:T(8,128)S(1)} %shard_map.123.refs_4_.joined), channel_id=1, source_target_pairs={{0,4},{4,0},{1,5},{5,1},{2,6},{6,2},{3,7},{7,3},{8,12},{12,8},{9,1... | collective-permute-start | bytes 589832 | tf_op jit(solution)/shard_map/ppermute | solution.py:753
  17.9 3.1 %collective-permute-done.6.refs_2_ = f32[12,32,128]{2,1,0:T(8,128)S(1)} collective-permute-done((f32[12,32,128]{2,1,0:T(8,128)S(1)}, f32[12,32,128]{2,1,0:T(8,128)S(1)}, u32[]{:S(2)}, u32[]{:S(2)}) %collective-permute-start.6) | collective-permute-done | bytes 196640 | tf_op jit(solution)/shard_map/ppermute | solution.py:753
  21.5 1.6 %collective-permute-start.7 = (f32[2,4,24,128]{3,2,1,0:T(8,128)S(1)}, f32[2,4,24,128]{3,2,1,0:T(8,128)S(1)}, u32[]{:S(2)}, u32[]{:S(2)}) collective-permute-start(f32[2,4,24,128]{3,2,1,0:T(8,128)S(1)} %shard_map.127.refs_2_), channel_id=1, source_target_pairs={{0,2},{1,3},{2,0},{3,1},{4,6},{5,7},{6,4},{7,5},{8,10},{9,11},{10,... | collective-permute-start | bytes 294920 | tf_op jit(solution)/shard_map/ppermute | solution.py:780
  23.4 1.6 %collective-permute-start.9 = (f32[2,4,24,128]{3,2,1,0:T(8,128)S(1)}, f32[2,4,24,128]{3,2,1,0:T(8,128)S(1)}, u32[]{:S(2)}, u32[]{:S(2)}) collective-permute-start(f32[2,4,24,128]{3,2,1,0:T(8,128)S(1)} %shard_map.128.refs_6_), channel_id=1, source_target_pairs={{0,2},{1,3},{2,0},{3,1},{4,6},{5,7},{6,4},{7,5},{8,10},{9,11},{10,... | collective-permute-start | bytes 294920 | tf_op jit(solution)/shard_map/ppermute | solution.py:780
  25.0 2.3 %shard_map.129 = (f32[18,72,128]{2,1,0:T(8,128)S(1)}, f32[16,72,128]{2,1,0:T(8,128)S(1)}, f32[17,72,128]{2,1,0:T(8,128)S(1)}, f32[16,72,128]{2,1,0:T(8,128)S(1)}...) custom-call(f32[16]{0:T(128)S(1)} %copy-done.6, f32[16]{0:T(128)S(1)} %copy-done.7, ...), custom_call_target="tpu_custom_call" | custom-call | flops 1000000000 | bytes 67108864 | tf_op jit(solution)/shard_map/pallas_call | solution.py:723
  27.3 0.8 %shard_map.130 = (f32[16,72,128]{2,1,0:T(8,128)S(1)}, f32[17,72,128]{2,1,0:T(8,128)S(1)}, f32[16,72,128]{2,1,0:T(8,128)S(1)}, f32[16,72,128]{2,1,0:T(8,128)S(1)}) custom-call(f32[16]{0:T(128)S(1)} %copy-done.6, f32[16]{0:T(128)S(1)} %copy-done.7, f32[2,4,24,128]{3,2,1,0:T(8,128)S(1)} %collective-permute-done.7.edge.refs_2_, ...), custom_call_target="tpu_custom_call" | custom-call | tf_op jit(solution)/shard_map/pallas_call | solution.py:723
  28.9 4.1 %shard_map.132 = (f32[16,72,128]{2,1,0:T(8,128)S(1)}, f32[104,128]{1,0:T(8,128)S(1)}) custom-call(f32[18,72,128]{2,1,0:T(8,128)S(1)} %get-tuple-element.41.phi, f32[16,72,128]{2,1,0:T(8,128)S(1)} %get-tuple-element.42.phi_y, f32[16,72,128]{2,1,0:T(8,128)S(1)} %get-tuple-element.43.phi_z, f32[16,72,128]{2,1,0:T(8,128)S(1)} %get-tuple-element.44.diag, ...), custom_call_target="tpu_custom_call" | custom-call | tf_op jit(solution)/shard_map/pallas_call | solution.py:723
  33.0 1.6 %collective-permute-start.10 = (f32[104,128]{1,0:T(8,128)S(1)}, f32[104,128]{1,0:T(8,128)S(1)}, u32[]{:S(2)}, u32[]{:S(2)}) collective-permute-start(f32[104,128]{1,0:T(8,128)S(1)} %get-tuple-element.49.sent), channel_id=1, source_target_pairs={{0,2},{1,3},{2,0},{3,1},{4,6},{5,7},{6,4},{7,5},{8,10},{9,11},{10,... | collective-permute-start | bytes 159752 | tf_op jit(solution)/shard_map/ppermute | solution.py:780
  34.6 2.6 %collective-permute-done.10.came = f32[104,128]{1,0:T(8,128)S(1)} collective-permute-done((f32[104,128]{1,0:T(8,128)S(1)}, f32[104,128]{1,0:T(8,128)S(1)}, u32[]{:S(2)}, u32[]{:S(2)}) %collective-permute-start.10) | collective-permute-done | bytes 53280 | tf_op jit(solution)/shard_map/ppermute | solution.py:780
  37.2 4.3 %shard_map.133 = (f32[2,16,32,128]{3,2,1,0:T(8,128)S(1)}, f32[2,16,32,128]{3,2,1,0:T(8,128)S(1)}) custom-call(f32[18,72,128]{2,1,0:T(8,128)S(1)} %get-tuple-element.41.phi, f32[16,72,128]{2,1,0:T(8,128)S(1)} %get-tuple-element.42.phi_y, f32[16,72,128]{2,1,0:T(8,128)S(1)} %get-tuple-element.43.phi_z, f32[16,72,128]{2,1,0:T(8,128)S(1)} %get-tuple-element.48.change, ...), custom_call_target="tpu_custom_call" | custom-call | tf_op jit(solution)/shard_map/pallas_call | solution.py:723
  41.6 1.9 %collective-permute-done.11.came.refs_1_ = f32[2,16,32,128]{3,2,1,0:T(8,128)S(1)} collective-permute-done((f32[2,16,32,128]{3,2,1,0:T(8,128)S(1)}, f32[2,16,32,128]{3,2,1,0:T(8,128)S(1)}, u32[]{:S(2)}, u32[]{:S(2)}) %collective-permute-start.11) | collective-permute-done | bytes 524320 | tf_op jit(solution)/shard_map/ppermute | solution.py:756
  43.8 1.6 %collective-permute-start.12 = (f32[1,2,2,32,128]{4,3,2,1,0:T(8,128)S(1)}, f32[1,2,2,32,128]{4,3,2,1,0:T(8,128)S(1)}, u32[]{:S(2)}, u32[]{:S(2)}) collective-permute-start(f32[1,2,2,32,128]{4,3,2,1,0:T(8,128)S(1)} %shard_map.135.refs_2_), channel_id=1, source_target_pairs={{0,4},{4,0},{1,5},{5,1},{2,6},{6,2},{3,7},{7,3},{8,12},{12,8},{9,1... | collective-permute-start | bytes 196616 | tf_op jit(solution)/shard_map/ppermute | solution.py:753
  46.0 1.6 %collective-permute-start.17 = (f32[1,2,2,32,128]{4,3,2,1,0:T(8,128)S(1)}, f32[1,2,2,32,128]{4,3,2,1,0:T(8,128)S(1)}, u32[]{:S(2)}, u32[]{:S(2)}) collective-permute-start(f32[1,2,2,32,128]{4,3,2,1,0:T(8,128)S(1)} %shard_map.136.refs_2_), channel_id=1, source_target_pairs={{0,4},{4,0},{1,5},{5,1},{2,6},{6,2},{3,7},{7,3},{8,12},{12,8},{9,1... | collective-permute-start | bytes 196616 | tf_op jit(solution)/shard_map/ppermute | solution.py:753
  48.7 2.0 %collective-permute-start.13 = (f32[2,2,32,128]{3,2,1,0:T(8,128)S(1)}, f32[2,2,32,128]{3,2,1,0:T(8,128)S(1)}, u32[]{:S(2)}, u32[]{:S(2)}) collective-permute-start(f32[2,2,32,128]{3,2,1,0:T(8,128)S(1)} %shard_map.139), channel_id=1, source_target_pairs={{0,16},{8,24},{16,0},{24,8},{1,17},{9,25},{17,1},{25,9},{2,18},{10... | collective-permute-start | bytes 196616 | tf_op jit(solution)/shard_map/ppermute | solution.py:759
  50.7 2.1 %collective-permute-start.15 = (f32[2,2,32,128]{3,2,1,0:T(8,128)S(1)}, f32[2,2,32,128]{3,2,1,0:T(8,128)S(1)}, u32[]{:S(2)}, u32[]{:S(2)}) collective-permute-start(f32[2,2,32,128]{3,2,1,0:T(8,128)S(1)} %shard_map.140), channel_id=1, source_target_pairs={{0,24},{8,16},{16,8},{24,0},{1,25},{9,17},{17,9},{25,1},{2,26},{10... | collective-permute-start | bytes 196616 | tf_op jit(solution)/shard_map/ppermute | solution.py:759
  53.0 2.5 %collective-permute-done.13.refs_0_ = f32[2,2,32,128]{3,2,1,0:T(8,128)S(1)} collective-permute-done((f32[2,2,32,128]{3,2,1,0:T(8,128)S(1)}, f32[2,2,32,128]{3,2,1,0:T(8,128)S(1)}, u32[]{:S(2)}, u32[]{:S(2)}) %collective-permute-start.13) | collective-permute-done | bytes 65568 | tf_op jit(solution)/shard_map/ppermute | solution.py:759
  55.5 1.4 %collective-permute-done.15.refs_1_ = f32[2,2,32,128]{3,2,1,0:T(8,128)S(1)} collective-permute-done((f32[2,2,32,128]{3,2,1,0:T(8,128)S(1)}, f32[2,2,32,128]{3,2,1,0:T(8,128)S(1)}, u32[]{:S(2)}, u32[]{:S(2)}) %collective-permute-start.15) | collective-permute-done | bytes 65568 | tf_op jit(solution)/shard_map/ppermute | solution.py:759
  58.1 11.2 %all_to_all.5.tiles = f32[32,1,128]{2,1,0:T(1,128)S(1)} all-to-all(f32[32,1,128]{2,1,0:T(1,128)S(1)} %broadcast_in_dim.3), channel_id=1, replica_groups=mesh['src'=4,'gx'=2,'gy'=4] {'src','gx','gy'}, dimensions={0} | all-to-all | bytes 32768 | tf_op jit(solution)/shard_map/all_to_all | solution.py:843
  69.3 1.0 %shard_map.145 = (f32[8,32,32]{2,1,0:T(8,128)}, f32[8,32,32]{2,1,0:T(8,128)}, f32[2]{0:T(128)}) custom-call(f32[32,1,128]{2,1,0:T(1,128)S(1)} %all_to_all.5.tiles, f32[8,32,32]{2,1,0:T(8,128)S(1)} %get-tuple-element.53.w_k, f32[8,32,32]{2,1,0:T(8,128)S(1)} %get-tuple-element.54.w_a, f32[8,32,32]{2,1,0:T(8,128)S(1)} %copy-done.1, f32[8,32,32]{2,1,0:T(8,128)S(1)} %copy-done.2), custom_call_target="tpu_custom_call" | custom-call | tf_op jit(solution)/shard_map/pallas_call | solution.py:723
  (59 shorter events, 6.6 us)
Async XLA Ops:
  0.6 10.3 %collective-permute-start = (s32[8,32,128]{2,1,0:T(8,128)}, s32[8,32,128]{2,1,0:T(8,128)S(1)}, u32[]{:S(2)}, u32[]{:S(2)}) collective-permute-start(s32[8,32,128]{2,1,0:T(8,128)} %refs_1_.3), channel_id=1, source_target_pairs={{0,4},{4,0},{1,5},{5,1},{2,6},{6,2},{3,7},{7,3},{8,12},{12,8},{9,1... | collective-permute-start | bytes 393224 | tf_op jit(solution)/shard_map/ppermute | solution.py:753
  5.5 5.4 %copy-start.8 = (s32[1024]{0:T(1024)S(1)}, s32[1024]{0:T(1024)}, u32[]{:S(2)}) copy-start(s32[1024]{0:T(1024)} %param.14) | copy-start | bytes 12292
  5.5 11.3 %collective-permute-start.1 = (f32[20,32,128]{2,1,0:T(8,128)}, f32[20,32,128]{2,1,0:T(8,128)S(1)}, u32[]{:S(2)}, u32[]{:S(2)}) collective-permute-start(f32[20,32,128]{2,1,0:T(8,128)} %get-tuple-element.30), channel_id=1, source_target_pairs={{0,4},{4,0},{1,5},{5,1},{2,6},{6,2},{3,7},{7,3},{8,12},{12,8},{9,1... | collective-permute-start | bytes 983048 | tf_op jit(solution)/shard_map/ppermute | solution.py:753
  5.6 7.5 %collective-permute-start.4 = (f32[4,32,128]{2,1,0:T(8,128)}, f32[4,32,128]{2,1,0:T(8,128)S(1)}, u32[]{:S(2)}, u32[]{:S(2)}) collective-permute-start(f32[4,32,128]{2,1,0:T(8,128)} %get-tuple-element.31), channel_id=1, source_target_pairs={{0,24},{8,16},{16,8},{24,0},{1,25},{9,17},{17,9},{25,1},{2,26},{10... | collective-permute-start | bytes 196616 | tf_op jit(solution)/shard_map/ppermute | solution.py:759
  9.7 5.5 %collective-permute-start.3 = (f32[4,32,128]{2,1,0:T(8,128)}, f32[4,32,128]{2,1,0:T(8,128)S(1)}, u32[]{:S(2)}, u32[]{:S(2)}) collective-permute-start(f32[4,32,128]{2,1,0:T(8,128)} %get-tuple-element.31), channel_id=1, source_target_pairs={{0,16},{8,24},{16,0},{24,8},{1,17},{9,25},{17,1},{25,9},{2,18},{10... | collective-permute-start | bytes 196616 | tf_op jit(solution)/shard_map/ppermute | solution.py:759
  9.7 5.5 %collective-permute-start.2 = (f32[4,32,128]{2,1,0:T(8,128)}, f32[4,32,128]{2,1,0:T(8,128)S(1)}, u32[]{:S(2)}, u32[]{:S(2)}) collective-permute-start(f32[4,32,128]{2,1,0:T(8,128)} %get-tuple-element.31), channel_id=1, source_target_pairs={{0,8},{8,0},{16,24},{24,16},{1,9},{9,1},{17,25},{25,17},{2,10},{10... | collective-permute-start | bytes 196616 | tf_op jit(solution)/shard_map/ppermute | solution.py:759
  13.1 3.7 %copy-start = (f32[4,8,32,128]{3,2,1,0:T(8,128)S(1)}, f32[4,8,32,128]{3,2,1,0:T(8,128)}, u32[]{:S(2)}) copy-start(f32[4,8,32,128]{3,2,1,0:T(8,128)} %refs_0_.2) | copy-start | bytes 1572868
  15.2 5.8 %collective-permute-start.6 = (f32[12,32,128]{2,1,0:T(8,128)S(1)}, f32[12,32,128]{2,1,0:T(8,128)S(1)}, u32[]{:S(2)}, u32[]{:S(2)}) collective-permute-start(f32[12,32,128]{2,1,0:T(8,128)S(1)} %shard_map.123.refs_4_.joined), channel_id=1, source_target_pairs={{0,4},{4,0},{1,5},{5,1},{2,6},{6,2},{3,7},{7,3},{8,12},{12,8},{9,1... | collective-permute-start | bytes 589832 | tf_op jit(solution)/shard_map/ppermute | solution.py:753
  17.4 4.0 %collective-permute-start.5 = (f32[2,16,32,128]{3,2,1,0:T(8,128)S(1)}, f32[2,16,32,128]{3,2,1,0:T(8,128)S(1)}, u32[]{:S(2)}, u32[]{:S(2)}) collective-permute-start(f32[2,16,32,128]{3,2,1,0:T(8,128)S(1)} %get-tuple-element.34.refs_1_.refs_3_), channel_id=1, source_target_pairs={{0,1},{1,0},{2,3},{3,2},{4,5},{5,4},{6,7},{7,6},{8,9},{9,8},{10,11... | collective-permute-start | bytes 1572872 | tf_op jit(solution)/shard_map/ppermute | solution.py:756
  21.4 2.0 %collective-permute-start.8 = (f32[2,16,32,128]{3,2,1,0:T(8,128)S(1)}, f32[2,16,32,128]{3,2,1,0:T(8,128)S(1)}, u32[]{:S(2)}, u32[]{:S(2)}) collective-permute-start(f32[2,16,32,128]{3,2,1,0:T(8,128)S(1)} %shard_map.126.refs_3_.refs_0_.vector), channel_id=1, source_target_pairs={{0,1},{1,0},{2,3},{3,2},{4,5},{5,4},{6,7},{7,6},{8,9},{9,8},{10,11... | collective-permute-start | bytes 1572872 | tf_op jit(solution)/shard_map/ppermute | solution.py:756
  21.5 3.5 %copy-start.6 = (f32[16]{0:T(128)S(1)}, f32[16]{0:T(128)}, u32[]{:S(2)}) copy-start(f32[16]{0:T(128)} %kap_table.1) | copy-start | bytes 196
  21.5 5.8 %collective-permute-start.7 = (f32[2,4,24,128]{3,2,1,0:T(8,128)S(1)}, f32[2,4,24,128]{3,2,1,0:T(8,128)S(1)}, u32[]{:S(2)}, u32[]{:S(2)}) collective-permute-start(f32[2,4,24,128]{3,2,1,0:T(8,128)S(1)} %shard_map.127.refs_2_), channel_id=1, source_target_pairs={{0,2},{1,3},{2,0},{3,1},{4,6},{5,7},{6,4},{7,5},{8,10},{9,11},{10,... | collective-permute-start | bytes 294920 | tf_op jit(solution)/shard_map/ppermute | solution.py:780
  23.4 5.5 %collective-permute-start.9 = (f32[2,4,24,128]{3,2,1,0:T(8,128)S(1)}, f32[2,4,24,128]{3,2,1,0:T(8,128)S(1)}, u32[]{:S(2)}, u32[]{:S(2)}) collective-permute-start(f32[2,4,24,128]{3,2,1,0:T(8,128)S(1)} %shard_map.128.refs_6_), channel_id=1, source_target_pairs={{0,2},{1,3},{2,0},{3,1},{4,6},{5,7},{6,4},{7,5},{8,10},{9,11},{10,... | collective-permute-start | bytes 294920 | tf_op jit(solution)/shard_map/ppermute | solution.py:780
  33.0 4.2 %collective-permute-start.10 = (f32[104,128]{1,0:T(8,128)S(1)}, f32[104,128]{1,0:T(8,128)S(1)}, u32[]{:S(2)}, u32[]{:S(2)}) collective-permute-start(f32[104,128]{1,0:T(8,128)S(1)} %get-tuple-element.49.sent), channel_id=1, source_target_pairs={{0,2},{1,3},{2,0},{3,1},{4,6},{5,7},{6,4},{7,5},{8,10},{9,11},{10,... | collective-permute-start | bytes 159752 | tf_op jit(solution)/shard_map/ppermute | solution.py:780
  41.5 2.0 %collective-permute-start.11 = (f32[2,16,32,128]{3,2,1,0:T(8,128)S(1)}, f32[2,16,32,128]{3,2,1,0:T(8,128)S(1)}, u32[]{:S(2)}, u32[]{:S(2)}) collective-permute-start(f32[2,16,32,128]{3,2,1,0:T(8,128)S(1)} %get-tuple-element.51), channel_id=1, source_target_pairs={{0,1},{1,0},{2,3},{3,2},{4,5},{5,4},{6,7},{7,6},{8,9},{9,8},{10,11... | collective-permute-start | bytes 1572872 | tf_op jit(solution)/shard_map/ppermute | solution.py:756
  43.8 4.9 %collective-permute-start.12 = (f32[1,2,2,32,128]{4,3,2,1,0:T(8,128)S(1)}, f32[1,2,2,32,128]{4,3,2,1,0:T(8,128)S(1)}, u32[]{:S(2)}, u32[]{:S(2)}) collective-permute-start(f32[1,2,2,32,128]{4,3,2,1,0:T(8,128)S(1)} %shard_map.135.refs_2_), channel_id=1, source_target_pairs={{0,4},{4,0},{1,5},{5,1},{2,6},{6,2},{3,7},{7,3},{8,12},{12,8},{9,1... | collective-permute-start | bytes 196616 | tf_op jit(solution)/shard_map/ppermute | solution.py:753
  45.4 5.3 %collective-permute-start.14 = (f32[1,2,2,32,128]{4,3,2,1,0:T(8,128)S(1)}, f32[1,2,2,32,128]{4,3,2,1,0:T(8,128)S(1)}, u32[]{:S(2)}, u32[]{:S(2)}) collective-permute-start(f32[1,2,2,32,128]{4,3,2,1,0:T(8,128)S(1)} %shard_map.134.refs_2_), channel_id=1, source_target_pairs={{0,4},{4,0},{1,5},{5,1},{2,6},{6,2},{3,7},{7,3},{8,12},{12,8},{9,1... | collective-permute-start | bytes 196616 | tf_op jit(solution)/shard_map/ppermute | solution.py:753
  46.0 6.8 %collective-permute-start.17 = (f32[1,2,2,32,128]{4,3,2,1,0:T(8,128)S(1)}, f32[1,2,2,32,128]{4,3,2,1,0:T(8,128)S(1)}, u32[]{:S(2)}, u32[]{:S(2)}) collective-permute-start(f32[1,2,2,32,128]{4,3,2,1,0:T(8,128)S(1)} %shard_map.136.refs_2_), channel_id=1, source_target_pairs={{0,4},{4,0},{1,5},{5,1},{2,6},{6,2},{3,7},{7,3},{8,12},{12,8},{9,1... | collective-permute-start | bytes 196616 | tf_op jit(solution)/shard_map/ppermute | solution.py:753
  47.8 5.2 %collective-permute-start.16 = (f32[1,2,2,32,128]{4,3,2,1,0:T(8,128)S(1)}, f32[1,2,2,32,128]{4,3,2,1,0:T(8,128)S(1)}, u32[]{:S(2)}, u32[]{:S(2)}) collective-permute-start(f32[1,2,2,32,128]{4,3,2,1,0:T(8,128)S(1)} %shard_map.137.refs_2_), channel_id=1, source_target_pairs={{0,4},{4,0},{1,5},{5,1},{2,6},{6,2},{3,7},{7,3},{8,12},{12,8},{9,1... | collective-permute-start | bytes 196616 | tf_op jit(solution)/shard_map/ppermute | solution.py:753
  48.7 6.8 %collective-permute-start.13 = (f32[2,2,32,128]{3,2,1,0:T(8,128)S(1)}, f32[2,2,32,128]{3,2,1,0:T(8,128)S(1)}, u32[]{:S(2)}, u32[]{:S(2)}) collective-permute-start(f32[2,2,32,128]{3,2,1,0:T(8,128)S(1)} %shard_map.139), channel_id=1, source_target_pairs={{0,16},{8,24},{16,0},{24,8},{1,17},{9,25},{17,1},{25,9},{2,18},{10... | collective-permute-start | bytes 196616 | tf_op jit(solution)/shard_map/ppermute | solution.py:759
  50.7 6.3 %collective-permute-start.15 = (f32[2,2,32,128]{3,2,1,0:T(8,128)S(1)}, f32[2,2,32,128]{3,2,1,0:T(8,128)S(1)}, u32[]{:S(2)}, u32[]{:S(2)}) collective-permute-start(f32[2,2,32,128]{3,2,1,0:T(8,128)S(1)} %shard_map.140), channel_id=1, source_target_pairs={{0,24},{8,16},{16,8},{24,0},{1,25},{9,17},{17,9},{25,1},{2,26},{10... | collective-permute-start | bytes 196616 | tf_op jit(solution)/shard_map/ppermute | solution.py:759
  52.9 4.8 %collective-permute-start.18 = (f32[2,2,32,128]{3,2,1,0:T(8,128)S(1)}, f32[2,2,32,128]{3,2,1,0:T(8,128)S(1)}, u32[]{:S(2)}, u32[]{:S(2)}) collective-permute-start(f32[2,2,32,128]{3,2,1,0:T(8,128)S(1)} %shard_map.143), channel_id=1, source_target_pairs={{0,8},{8,0},{16,24},{24,16},{1,9},{9,1},{17,25},{25,17},{2,10},{10... | collective-permute-start | bytes 196616 | tf_op jit(solution)/shard_map/ppermute | solution.py:759
  53.0 4.6 %copy-start.4 = (f32[8,32,32]{2,1,0:T(8,128)S(1)}, f32[8,32,32]{2,1,0:T(8,128)}, u32[]{:S(2)}) copy-start(f32[8,32,32]{2,1,0:T(8,128)} %refs_6_.1) | copy-start | bytes 98308
  53.0 4.6 %copy-start.5 = (f32[8,32,32]{2,1,0:T(8,128)S(1)}, f32[8,32,32]{2,1,0:T(8,128)}, u32[]{:S(2)}) copy-start(f32[8,32,32]{2,1,0:T(8,128)} %refs_7_.1) | copy-start | bytes 98308
  (4 other events, 9.6 us)

commit v19 on v17

--- a/solution.py
+++ b/solution.py
@@ -838,7 +838,7 @@
         beta_row, *parts, v_kappa, v_absorb, q_kappa, q_absorb,
     )
     everyone = ("src", "gx", "gy")
-    tiles = lax.all_to_all(jnp.broadcast_to(tile, (8 * n, 1, 128)), everyone, 0, 0)
+    tiles = lax.all_gather(tile, everyone)
     return tuple(run(
         functools.partial(final_kernel, cells=cells),
         (f32(*v_kappa.shape), f32(*v_kappa.shape), f32(2)),

time: 70 us -> 98.7 us (1.41)
  blocking collectives: 11.2 us -> 39.9 us
    all_gather x0 -> x1, blocking collectives: none -> 39.9 us  [per_device_paired(): tiles = lax.all_gather(tile, everyone)]
    all_to_all x1 -> x0, blocking collectives: 11.2 us -> none  [per_device_paired(): lax.all_to_all(jnp.broadcast_to(tile, (8 * n, 1, 128)), everyone, 0, 0)]
  transfers between devices with their start and end apart: 19 -> 19, of which waited for: 9 -> 9; matrix products, arithmetic and copies ran while one was open for 0% -> 0% of each run, Pallas kernels for 14% -> 10%
where the time goes in v19:
time: 98.7 us; the launch traced here: 98.6 us
  blocking collectives  39.9 us (40%)
  starting transfers between devices  22.8 us (23%)
  Pallas kernels  19.5 us (20%)
  waiting for transfers between devices  14.7 us (15%)
  between operations  1.6 us (2%)
    all_gather x1, blocking collectives, per_device_paired(): tiles = lax.all_gather(tile, everyone)  39.9 us
    pallas_call x25, Pallas kernels, run(): pl.pallas_call(body if waits else kernel, out_shape=tuple(outs), in_specs...  19.5 us
    ppermute x6, starting transfers between devices, along_z(): return lax.ppermute(value, 'src', [(i, i ^ k) for i in range(n)])  8.91 us
    ppermute x7, starting transfers between devices, swap_x(): return lax.ppermute(value, 'gx', [(0, 1), (1, 0)])  8.89 us
    ppermute x6, waiting for transfers between devices, along_z(): return lax.ppermute(value, 'src', [(i, i ^ k) for i in range(n)])  6.67 us
    ppermute x3, starting transfers between devices, across_y(): return lax.ppermute(value, 'gy', [(i, (i + 2) % 4) for i in range(4)])  4.75 us
    ppermute x7, waiting for transfers between devices, swap_x(): return lax.ppermute(value, 'gx', [(0, 1), (1, 0)])  3.11 us
    ppermute x3, waiting for transfers between devices, across_y(): return lax.ppermute(value, 'gy', [(i, (i + 2) % 4) for i in range(4)])  2.85 us
  transfers between devices with their start and end apart: 19, of which 9 were waited for; matrix products, arithmetic and copies ran while one was open for 0% of the time, Pallas kernels for 10%

profile of v19, /device:TPU:0, one launch (start us, length us, event | category | flops | bytes accessed | tf_op | source)
XLA Modules:
  0.0 98.6 jit_solution(8454683850776438180)
XLA Ops:
  0.6 3.0 %collective-permute-start = (s32[8,32,128]{2,1,0:T(8,128)}, s32[8,32,128]{2,1,0:T(8,128)S(1)}, u32[]{:S(2)}, u32[]{:S(2)}) collective-permute-start(s32[8,32,128]{2,1,0:T(8,128)} %refs_1_.3), channel_id=1, source_target_pairs={{0,4},{4,0},{1,5},{5,1},{2,6},{6,2},{3,7},{7,3},{8,12},{12,8},{9,1... | collective-permute-start | bytes 393224 | tf_op jit(solution)/shard_map/ppermute | solution.py:751
  3.6 1.9 %shard_map.122 = (f32[4,32,128]{2,1,0:T(8,128)}, f32[20,32,128]{2,1,0:T(8,128)}) custom-call(f32[4,8,32,128]{3,2,1,0:T(8,128)} %refs_0_.2, f32[8,32,32]{2,1,0:T(8,128)} %vk.5, f32[8,32,32]{2,1,0:T(8,128)} %va.5), custom_call_target="tpu_custom_call" | custom-call | tf_op jit(solution)/shard_map/pallas_call | solution.py:721
  5.6 4.1 %collective-permute-start.4 = (f32[4,32,128]{2,1,0:T(8,128)}, f32[4,32,128]{2,1,0:T(8,128)S(1)}, u32[]{:S(2)}, u32[]{:S(2)}) collective-permute-start(f32[4,32,128]{2,1,0:T(8,128)} %get-tuple-element.31), channel_id=1, source_target_pairs={{0,24},{8,16},{16,8},{24,0},{1,25},{9,17},{17,9},{25,1},{2,26},{10... | collective-permute-start | bytes 196616 | tf_op jit(solution)/shard_map/ppermute | solution.py:757
  11.0 2.1 %shard_map.121 = (f32[16,72,128]{2,1,0:T(8,128)S(1)}, f32[1,128]{1,0:T(1,128)S(1)}) custom-call(s32[1,1024]{1,0:T(1,128)S(1)} %bitcast.3, f32[1]{0:T(128)S(6)} %copy.13.refs_1_, s32[8,32,128]{2,1,0:T(8,128)S(1)} %collective-permute-done.refs_2_.refs_3_), custom_call_target="tpu_custom_call" | custom-call | flops 301989888 | bytes 589824 | tf_op jit(solution)/shard_map/pallas_call | solution.py:721
  13.1 2.1 %collective-permute-done.3.refs_1_ = f32[4,32,128]{2,1,0:T(8,128)S(1)} collective-permute-done((f32[4,32,128]{2,1,0:T(8,128)}, f32[4,32,128]{2,1,0:T(8,128)S(1)}, u32[]{:S(2)}, u32[]{:S(2)}) %collective-permute-start.3) | collective-permute-done | bytes 65568 | tf_op jit(solution)/shard_map/ppermute | solution.py:757
  15.2 1.6 %collective-permute-start.6 = (f32[12,32,128]{2,1,0:T(8,128)S(1)}, f32[12,32,128]{2,1,0:T(8,128)S(1)}, u32[]{:S(2)}, u32[]{:S(2)}) collective-permute-start(f32[12,32,128]{2,1,0:T(8,128)S(1)} %shard_map.123.refs_4_.joined), channel_id=1, source_target_pairs={{0,4},{4,0},{1,5},{5,1},{2,6},{6,2},{3,7},{7,3},{8,12},{12,8},{9,1... | collective-permute-start | bytes 589832 | tf_op jit(solution)/shard_map/ppermute | solution.py:751
  17.9 3.1 %collective-permute-done.6.refs_2_ = f32[12,32,128]{2,1,0:T(8,128)S(1)} collective-permute-done((f32[12,32,128]{2,1,0:T(8,128)S(1)}, f32[12,32,128]{2,1,0:T(8,128)S(1)}, u32[]{:S(2)}, u32[]{:S(2)}) %collective-permute-start.6) | collective-permute-done | bytes 196640 | tf_op jit(solution)/shard_map/ppermute | solution.py:751
  21.5 1.6 %collective-permute-start.7 = (f32[2,4,24,128]{3,2,1,0:T(8,128)S(1)}, f32[2,4,24,128]{3,2,1,0:T(8,128)S(1)}, u32[]{:S(2)}, u32[]{:S(2)}) collective-permute-start(f32[2,4,24,128]{3,2,1,0:T(8,128)S(1)} %shard_map.127.refs_2_), channel_id=1, source_target_pairs={{0,2},{1,3},{2,0},{3,1},{4,6},{5,7},{6,4},{7,5},{8,10},{9,11},{10,... | collective-permute-start | bytes 294920 | tf_op jit(solution)/shard_map/ppermute | solution.py:778
  23.4 1.6 %collective-permute-start.9 = (f32[2,4,24,128]{3,2,1,0:T(8,128)S(1)}, f32[2,4,24,128]{3,2,1,0:T(8,128)S(1)}, u32[]{:S(2)}, u32[]{:S(2)}) collective-permute-start(f32[2,4,24,128]{3,2,1,0:T(8,128)S(1)} %shard_map.128.refs_6_), channel_id=1, source_target_pairs={{0,2},{1,3},{2,0},{3,1},{4,6},{5,7},{6,4},{7,5},{8,10},{9,11},{10,... | collective-permute-start | bytes 294920 | tf_op jit(solution)/shard_map/ppermute | solution.py:778
  25.0 2.3 %shard_map.129 = (f32[18,72,128]{2,1,0:T(8,128)S(1)}, f32[16,72,128]{2,1,0:T(8,128)S(1)}, f32[17,72,128]{2,1,0:T(8,128)S(1)}, f32[16,72,128]{2,1,0:T(8,128)S(1)}...) custom-call(f32[16]{0:T(128)S(1)} %copy-done.6, f32[16]{0:T(128)S(1)} %copy-done.7, ...), custom_call_target="tpu_custom_call" | custom-call | flops 1000000000 | bytes 67108864 | tf_op jit(solution)/shard_map/pallas_call | solution.py:721
  27.3 0.8 shard_map.130
  28.9 3.9 %shard_map.132 = (f32[16,72,128]{2,1,0:T(8,128)S(1)}, f32[104,128]{1,0:T(8,128)S(1)}) custom-call(f32[18,72,128]{2,1,0:T(8,128)S(1)} %get-tuple-element.41.phi, f32[16,72,128]{2,1,0:T(8,128)S(1)} %get-tuple-element.42.phi_y, f32[16,72,128]{2,1,0:T(8,128)S(1)} %get-tuple-element.43.phi_z, f32[16,72,128]{2,1,0:T(8,128)S(1)} %get-tuple-element.44.diag, ...), custom_call_target="tpu_custom_call" | custom-call | tf_op jit(solution)/shard_map/pallas_call | solution.py:721
  32.8 1.6 %collective-permute-start.10 = (f32[104,128]{1,0:T(8,128)S(1)}, f32[104,128]{1,0:T(8,128)S(1)}, u32[]{:S(2)}, u32[]{:S(2)}) collective-permute-start(f32[104,128]{1,0:T(8,128)S(1)} %get-tuple-element.49.sent), channel_id=1, source_target_pairs={{0,2},{1,3},{2,0},{3,1},{4,6},{5,7},{6,4},{7,5},{8,10},{9,11},{10,... | collective-permute-start | bytes 159752 | tf_op jit(solution)/shard_map/ppermute | solution.py:778
  34.4 2.6 %collective-permute-done.10.came = f32[104,128]{1,0:T(8,128)S(1)} collective-permute-done((f32[104,128]{1,0:T(8,128)S(1)}, f32[104,128]{1,0:T(8,128)S(1)}, u32[]{:S(2)}, u32[]{:S(2)}) %collective-permute-start.10) | collective-permute-done | bytes 53280 | tf_op jit(solution)/shard_map/ppermute | solution.py:778
  37.0 4.1 %shard_map.133 = (f32[2,16,32,128]{3,2,1,0:T(8,128)S(1)}, f32[2,16,32,128]{3,2,1,0:T(8,128)S(1)}) custom-call(f32[18,72,128]{2,1,0:T(8,128)S(1)} %get-tuple-element.41.phi, f32[16,72,128]{2,1,0:T(8,128)S(1)} %get-tuple-element.42.phi_y, f32[16,72,128]{2,1,0:T(8,128)S(1)} %get-tuple-element.43.phi_z, f32[16,72,128]{2,1,0:T(8,128)S(1)} %get-tuple-element.48.change, ...), custom_call_target="tpu_custom_call" | custom-call | tf_op jit(solution)/shard_map/pallas_call | solution.py:721
  41.1 1.9 %collective-permute-done.11.came.refs_1_ = f32[2,16,32,128]{3,2,1,0:T(8,128)S(1)} collective-permute-done((f32[2,16,32,128]{3,2,1,0:T(8,128)S(1)}, f32[2,16,32,128]{3,2,1,0:T(8,128)S(1)}, u32[]{:S(2)}, u32[]{:S(2)}) %collective-permute-start.11) | collective-permute-done | bytes 524320 | tf_op jit(solution)/shard_map/ppermute | solution.py:754
  43.3 1.6 %collective-permute-start.12 = (f32[1,2,2,32,128]{4,3,2,1,0:T(8,128)S(1)}, f32[1,2,2,32,128]{4,3,2,1,0:T(8,128)S(1)}, u32[]{:S(2)}, u32[]{:S(2)}) collective-permute-start(f32[1,2,2,32,128]{4,3,2,1,0:T(8,128)S(1)} %shard_map.135.refs_2_), channel_id=1, source_target_pairs={{0,4},{4,0},{1,5},{5,1},{2,6},{6,2},{3,7},{7,3},{8,12},{12,8},{9,1... | collective-permute-start | bytes 196616 | tf_op jit(solution)/shard_map/ppermute | solution.py:751
  45.6 1.6 %collective-permute-start.17 = (f32[1,2,2,32,128]{4,3,2,1,0:T(8,128)S(1)}, f32[1,2,2,32,128]{4,3,2,1,0:T(8,128)S(1)}, u32[]{:S(2)}, u32[]{:S(2)}) collective-permute-start(f32[1,2,2,32,128]{4,3,2,1,0:T(8,128)S(1)} %shard_map.136.refs_2_), channel_id=1, source_target_pairs={{0,4},{4,0},{1,5},{5,1},{2,6},{6,2},{3,7},{7,3},{8,12},{12,8},{9,1... | collective-permute-start | bytes 196616 | tf_op jit(solution)/shard_map/ppermute | solution.py:751
  48.3 2.0 %collective-permute-start.13 = (f32[2,2,32,128]{3,2,1,0:T(8,128)S(1)}, f32[2,2,32,128]{3,2,1,0:T(8,128)S(1)}, u32[]{:S(2)}, u32[]{:S(2)}) collective-permute-start(f32[2,2,32,128]{3,2,1,0:T(8,128)S(1)} %shard_map.139), channel_id=1, source_target_pairs={{0,16},{8,24},{16,0},{24,8},{1,17},{9,25},{17,1},{25,9},{2,18},{10... | collective-permute-start | bytes 196616 | tf_op jit(solution)/shard_map/ppermute | solution.py:757
  50.2 2.1 %collective-permute-start.15 = (f32[2,2,32,128]{3,2,1,0:T(8,128)S(1)}, f32[2,2,32,128]{3,2,1,0:T(8,128)S(1)}, u32[]{:S(2)}, u32[]{:S(2)}) collective-permute-start(f32[2,2,32,128]{3,2,1,0:T(8,128)S(1)} %shard_map.140), channel_id=1, source_target_pairs={{0,24},{8,16},{16,8},{24,0},{1,25},{9,17},{17,9},{25,1},{2,26},{10... | collective-permute-start | bytes 196616 | tf_op jit(solution)/shard_map/ppermute | solution.py:757
  52.6 2.5 %collective-permute-done.13.refs_0_ = f32[2,2,32,128]{3,2,1,0:T(8,128)S(1)} collective-permute-done((f32[2,2,32,128]{3,2,1,0:T(8,128)S(1)}, f32[2,2,32,128]{3,2,1,0:T(8,128)S(1)}, u32[]{:S(2)}, u32[]{:S(2)}) %collective-permute-start.13) | collective-permute-done | bytes 65568 | tf_op jit(solution)/shard_map/ppermute | solution.py:757
  55.1 1.4 %collective-permute-done.15.refs_1_ = f32[2,2,32,128]{3,2,1,0:T(8,128)S(1)} collective-permute-done((f32[2,2,32,128]{3,2,1,0:T(8,128)S(1)}, f32[2,2,32,128]{3,2,1,0:T(8,128)S(1)}, u32[]{:S(2)}, u32[]{:S(2)}) %collective-permute-start.15) | collective-permute-done | bytes 65568 | tf_op jit(solution)/shard_map/ppermute | solution.py:757
  57.6 39.9 %all-gather.1.tiles = f32[32,1,128]{2,1,0:T(1,128)S(1)} all-gather(f32[1,1,128]{2,1,0:T(1,128)S(1)} %bitcast.2), channel_id=2, replica_groups=mesh['src'=4,'gx'=2,'gy'=4] {'src','gx','gy'}, dimensions={0}, use_global_device_ids=true | all-gather | bytes 16896 | tf_op jit(solution)/shard_map/all_gather | solution.py:841
  97.6 1.0 shard_map.145
  (58 shorter events, 6.6 us)
Async XLA Ops:
  0.6 10.3 %collective-permute-start = (s32[8,32,128]{2,1,0:T(8,128)}, s32[8,32,128]{2,1,0:T(8,128)S(1)}, u32[]{:S(2)}, u32[]{:S(2)}) collective-permute-start(s32[8,32,128]{2,1,0:T(8,128)} %refs_1_.3), channel_id=1, source_target_pairs={{0,4},{4,0},{1,5},{5,1},{2,6},{6,2},{3,7},{7,3},{8,12},{12,8},{9,1... | collective-permute-start | bytes 393224 | tf_op jit(solution)/shard_map/ppermute | solution.py:751
  5.5 5.4 %copy-start.8 = (s32[1024]{0:T(1024)S(1)}, s32[1024]{0:T(1024)}, u32[]{:S(2)}) copy-start(s32[1024]{0:T(1024)} %param.14) | copy-start | bytes 12292
  5.5 11.3 %collective-permute-start.1 = (f32[20,32,128]{2,1,0:T(8,128)}, f32[20,32,128]{2,1,0:T(8,128)S(1)}, u32[]{:S(2)}, u32[]{:S(2)}) collective-permute-start(f32[20,32,128]{2,1,0:T(8,128)} %get-tuple-element.30), channel_id=1, source_target_pairs={{0,4},{4,0},{1,5},{5,1},{2,6},{6,2},{3,7},{7,3},{8,12},{12,8},{9,1... | collective-permute-start | bytes 983048 | tf_op jit(solution)/shard_map/ppermute | solution.py:751
  5.6 7.5 %collective-permute-start.4 = (f32[4,32,128]{2,1,0:T(8,128)}, f32[4,32,128]{2,1,0:T(8,128)S(1)}, u32[]{:S(2)}, u32[]{:S(2)}) collective-permute-start(f32[4,32,128]{2,1,0:T(8,128)} %get-tuple-element.31), channel_id=1, source_target_pairs={{0,24},{8,16},{16,8},{24,0},{1,25},{9,17},{17,9},{25,1},{2,26},{10... | collective-permute-start | bytes 196616 | tf_op jit(solution)/shard_map/ppermute | solution.py:757
  9.7 5.5 %collective-permute-start.3 = (f32[4,32,128]{2,1,0:T(8,128)}, f32[4,32,128]{2,1,0:T(8,128)S(1)}, u32[]{:S(2)}, u32[]{:S(2)}) collective-permute-start(f32[4,32,128]{2,1,0:T(8,128)} %get-tuple-element.31), channel_id=1, source_target_pairs={{0,16},{8,24},{16,0},{24,8},{1,17},{9,25},{17,1},{25,9},{2,18},{10... | collective-permute-start | bytes 196616 | tf_op jit(solution)/shard_map/ppermute | solution.py:757
  9.7 5.5 %collective-permute-start.2 = (f32[4,32,128]{2,1,0:T(8,128)}, f32[4,32,128]{2,1,0:T(8,128)S(1)}, u32[]{:S(2)}, u32[]{:S(2)}) collective-permute-start(f32[4,32,128]{2,1,0:T(8,128)} %get-tuple-element.31), channel_id=1, source_target_pairs={{0,8},{8,0},{16,24},{24,16},{1,9},{9,1},{17,25},{25,17},{2,10},{10... | collective-permute-start | bytes 196616 | tf_op jit(solution)/shard_map/ppermute | solution.py:757
  13.1 3.7 %copy-start = (f32[4,8,32,128]{3,2,1,0:T(8,128)S(1)}, f32[4,8,32,128]{3,2,1,0:T(8,128)}, u32[]{:S(2)}) copy-start(f32[4,8,32,128]{3,2,1,0:T(8,128)} %refs_0_.2) | copy-start | bytes 1572868
  15.2 5.8 %collective-permute-start.6 = (f32[12,32,128]{2,1,0:T(8,128)S(1)}, f32[12,32,128]{2,1,0:T(8,128)S(1)}, u32[]{:S(2)}, u32[]{:S(2)}) collective-permute-start(f32[12,32,128]{2,1,0:T(8,128)S(1)} %shard_map.123.refs_4_.joined), channel_id=1, source_target_pairs={{0,4},{4,0},{1,5},{5,1},{2,6},{6,2},{3,7},{7,3},{8,12},{12,8},{9,1... | collective-permute-start | bytes 589832 | tf_op jit(solution)/shard_map/ppermute | solution.py:751
  17.4 4.0 %collective-permute-start.5 = (f32[2,16,32,128]{3,2,1,0:T(8,128)S(1)}, f32[2,16,32,128]{3,2,1,0:T(8,128)S(1)}, u32[]{:S(2)}, u32[]{:S(2)}) collective-permute-start(f32[2,16,32,128]{3,2,1,0:T(8,128)S(1)} %get-tuple-element.34.refs_1_.refs_3_), channel_id=1, source_target_pairs={{0,1},{1,0},{2,3},{3,2},{4,5},{5,4},{6,7},{7,6},{8,9},{9,8},{10,11... | collective-permute-start | bytes 1572872 | tf_op jit(solution)/shard_map/ppermute | solution.py:754
  21.4 2.0 %collective-permute-start.8 = (f32[2,16,32,128]{3,2,1,0:T(8,128)S(1)}, f32[2,16,32,128]{3,2,1,0:T(8,128)S(1)}, u32[]{:S(2)}, u32[]{:S(2)}) collective-permute-start(f32[2,16,32,128]{3,2,1,0:T(8,128)S(1)} %shard_map.126.refs_3_.refs_0_.vector), channel_id=1, source_target_pairs={{0,1},{1,0},{2,3},{3,2},{4,5},{5,4},{6,7},{7,6},{8,9},{9,8},{10,11... | collective-permute-start | bytes 1572872 | tf_op jit(solution)/shard_map/ppermute | solution.py:754
  21.5 3.5 %copy-start.6 = (f32[16]{0:T(128)S(1)}, f32[16]{0:T(128)}, u32[]{:S(2)}) copy-start(f32[16]{0:T(128)} %kap_table.1) | copy-start | bytes 196
  21.5 5.8 %collective-permute-start.7 = (f32[2,4,24,128]{3,2,1,0:T(8,128)S(1)}, f32[2,4,24,128]{3,2,1,0:T(8,128)S(1)}, u32[]{:S(2)}, u32[]{:S(2)}) collective-permute-start(f32[2,4,24,128]{3,2,1,0:T(8,128)S(1)} %shard_map.127.refs_2_), channel_id=1, source_target_pairs={{0,2},{1,3},{2,0},{3,1},{4,6},{5,7},{6,4},{7,5},{8,10},{9,11},{10,... | collective-permute-start | bytes 294920 | tf_op jit(solution)/shard_map/ppermute | solution.py:778
  23.4 5.5 %collective-permute-start.9 = (f32[2,4,24,128]{3,2,1,0:T(8,128)S(1)}, f32[2,4,24,128]{3,2,1,0:T(8,128)S(1)}, u32[]{:S(2)}, u32[]{:S(2)}) collective-permute-start(f32[2,4,24,128]{3,2,1,0:T(8,128)S(1)} %shard_map.128.refs_6_), channel_id=1, source_target_pairs={{0,2},{1,3},{2,0},{3,1},{4,6},{5,7},{6,4},{7,5},{8,10},{9,11},{10,... | collective-permute-start | bytes 294920 | tf_op jit(solution)/shard_map/ppermute | solution.py:778
  32.8 4.2 %collective-permute-start.10 = (f32[104,128]{1,0:T(8,128)S(1)}, f32[104,128]{1,0:T(8,128)S(1)}, u32[]{:S(2)}, u32[]{:S(2)}) collective-permute-start(f32[104,128]{1,0:T(8,128)S(1)} %get-tuple-element.49.sent), channel_id=1, source_target_pairs={{0,2},{1,3},{2,0},{3,1},{4,6},{5,7},{6,4},{7,5},{8,10},{9,11},{10,... | collective-permute-start | bytes 159752 | tf_op jit(solution)/shard_map/ppermute | solution.py:778
  41.1 2.0 %collective-permute-start.11 = (f32[2,16,32,128]{3,2,1,0:T(8,128)S(1)}, f32[2,16,32,128]{3,2,1,0:T(8,128)S(1)}, u32[]{:S(2)}, u32[]{:S(2)}) collective-permute-start(f32[2,16,32,128]{3,2,1,0:T(8,128)S(1)} %get-tuple-element.51), channel_id=1, source_target_pairs={{0,1},{1,0},{2,3},{3,2},{4,5},{5,4},{6,7},{7,6},{8,9},{9,8},{10,11... | collective-permute-start | bytes 1572872 | tf_op jit(solution)/shard_map/ppermute | solution.py:754
  43.3 4.9 %collective-permute-start.12 = (f32[1,2,2,32,128]{4,3,2,1,0:T(8,128)S(1)}, f32[1,2,2,32,128]{4,3,2,1,0:T(8,128)S(1)}, u32[]{:S(2)}, u32[]{:S(2)}) collective-permute-start(f32[1,2,2,32,128]{4,3,2,1,0:T(8,128)S(1)} %shard_map.135.refs_2_), channel_id=1, source_target_pairs={{0,4},{4,0},{1,5},{5,1},{2,6},{6,2},{3,7},{7,3},{8,12},{12,8},{9,1... | collective-permute-start | bytes 196616 | tf_op jit(solution)/shard_map/ppermute | solution.py:751
  44.9 5.3 %collective-permute-start.14 = (f32[1,2,2,32,128]{4,3,2,1,0:T(8,128)S(1)}, f32[1,2,2,32,128]{4,3,2,1,0:T(8,128)S(1)}, u32[]{:S(2)}, u32[]{:S(2)}) collective-permute-start(f32[1,2,2,32,128]{4,3,2,1,0:T(8,128)S(1)} %shard_map.134.refs_2_), channel_id=1, source_target_pairs={{0,4},{4,0},{1,5},{5,1},{2,6},{6,2},{3,7},{7,3},{8,12},{12,8},{9,1... | collective-permute-start | bytes 196616 | tf_op jit(solution)/shard_map/ppermute | solution.py:751
  45.6 6.8 %collective-permute-start.17 = (f32[1,2,2,32,128]{4,3,2,1,0:T(8,128)S(1)}, f32[1,2,2,32,128]{4,3,2,1,0:T(8,128)S(1)}, u32[]{:S(2)}, u32[]{:S(2)}) collective-permute-start(f32[1,2,2,32,128]{4,3,2,1,0:T(8,128)S(1)} %shard_map.136.refs_2_), channel_id=1, source_target_pairs={{0,4},{4,0},{1,5},{5,1},{2,6},{6,2},{3,7},{7,3},{8,12},{12,8},{9,1... | collective-permute-start | bytes 196616 | tf_op jit(solution)/shard_map/ppermute | solution.py:751
  47.3 5.2 %collective-permute-start.16 = (f32[1,2,2,32,128]{4,3,2,1,0:T(8,128)S(1)}, f32[1,2,2,32,128]{4,3,2,1,0:T(8,128)S(1)}, u32[]{:S(2)}, u32[]{:S(2)}) collective-permute-start(f32[1,2,2,32,128]{4,3,2,1,0:T(8,128)S(1)} %shard_map.137.refs_2_), channel_id=1, source_target_pairs={{0,4},{4,0},{1,5},{5,1},{2,6},{6,2},{3,7},{7,3},{8,12},{12,8},{9,1... | collective-permute-start | bytes 196616 | tf_op jit(solution)/shard_map/ppermute | solution.py:751
  48.3 6.8 %collective-permute-start.13 = (f32[2,2,32,128]{3,2,1,0:T(8,128)S(1)}, f32[2,2,32,128]{3,2,1,0:T(8,128)S(1)}, u32[]{:S(2)}, u32[]{:S(2)}) collective-permute-start(f32[2,2,32,128]{3,2,1,0:T(8,128)S(1)} %shard_map.139), channel_id=1, source_target_pairs={{0,16},{8,24},{16,0},{24,8},{1,17},{9,25},{17,1},{25,9},{2,18},{10... | collective-permute-start | bytes 196616 | tf_op jit(solution)/shard_map/ppermute | solution.py:757
  50.2 6.3 %collective-permute-start.15 = (f32[2,2,32,128]{3,2,1,0:T(8,128)S(1)}, f32[2,2,32,128]{3,2,1,0:T(8,128)S(1)}, u32[]{:S(2)}, u32[]{:S(2)}) collective-permute-start(f32[2,2,32,128]{3,2,1,0:T(8,128)S(1)} %shard_map.140), channel_id=1, source_target_pairs={{0,24},{8,16},{16,8},{24,0},{1,25},{9,17},{17,9},{25,1},{2,26},{10... | collective-permute-start | bytes 196616 | tf_op jit(solution)/shard_map/ppermute | solution.py:757
  52.4 4.8 %collective-permute-start.18 = (f32[2,2,32,128]{3,2,1,0:T(8,128)S(1)}, f32[2,2,32,128]{3,2,1,0:T(8,128)S(1)}, u32[]{:S(2)}, u32[]{:S(2)}) collective-permute-start(f32[2,2,32,128]{3,2,1,0:T(8,128)S(1)} %shard_map.143), channel_id=1, source_target_pairs={{0,8},{8,0},{16,24},{24,16},{1,9},{9,1},{17,25},{25,17},{2,10},{10... | collective-permute-start | bytes 196616 | tf_op jit(solution)/shard_map/ppermute | solution.py:757
  52.5 4.6 %copy-start.4 = (f32[8,32,32]{2,1,0:T(8,128)S(1)}, f32[8,32,32]{2,1,0:T(8,128)}, u32[]{:S(2)}) copy-start(f32[8,32,32]{2,1,0:T(8,128)} %refs_6_.1) | copy-start | bytes 98308
  52.6 4.6 %copy-start.5 = (f32[8,32,32]{2,1,0:T(8,128)S(1)}, f32[8,32,32]{2,1,0:T(8,128)}, u32[]{:S(2)}) copy-start(f32[8,32,32]{2,1,0:T(8,128)} %refs_7_.1) | copy-start | bytes 98308
  (4 other events, 9.6 us)

commit v20 on v17

--- a/solution.py
+++ b/solution.py
@@ -356,7 +356,7 @@
         edges_of(fields.at[f], got.at[f], edge.at[f], y, c)
 
 
-def solve(b, bufs, diag, fx, fy, fz, unroll):
+def solve(b, bufs, diag, fx, fy, fz, unroll, after_step=None):
     planes = b.shape[0]
     _, pairs = chebyshev_scalars()
     for step, (keep, push) in enumerate(pairs):
@@ -374,6 +374,8 @@
             return carry
 
         lax.fori_loop(0, planes, body, 0, unroll=unroll)
+        if after_step is not None:
+            after_step(step + 1, dst)
     return bufs[len(pairs) % 2]
 
 
@@ -513,55 +515,117 @@
     lax.fori_loop(0, phi_y.shape[0], differ, 0, unroll=4)
 
 
-def first_kernel(
-    phi, phi_y, phi_z, diag, fx, fy, fz, count, sums, vector, got_vector, edge,
-    change, message,
-    vk, va, b, buf_a, buf_b,
-):
-    _, _, y, c = places(2)
-    planes, rows, lanes = change.shape
-    cy = vector.shape[2]
-    framed(vk, 1, vector.at[0], got_vector.at[0], edge.at[0], y, c)
-    framed(va, 0, vector.at[1], got_vector.at[1], edge.at[1], y, c)
-    blank_ends(vk, buf_a, buf_b)
+def rhs_into(b, buf, phi, vk, va, phi_y, phi_z):
     theta, _ = chebyshev_scalars()
 
     def set_up(i, carry):
         v, p = vk[i + 1], phi[i + 1]
         total = 0.5 * (v + vk[i]) * (p - phi[i]) + 0.5 * (v + vk[i + 2]) * (p - phi[i + 2])
         for axis, step in enumerate((phi_y, phi_z)):
-            flow = 0.5 * (v + beyond(v, 1, axis)) * step[i]
+            difference = p - beyond(p, 1, axis) if step is None else step[i]
+            flow = 0.5 * (v + beyond(v, 1, axis)) * difference
             first = index_along(v.shape, axis) == 0
             total = total + flow + jnp.where(first, 0.5 * v * p, -shifted(flow, 1, axis))
         total = -(va[i] * p + total)
         b[i] = total
-        buf_a[i + 1] = total * (1.0 / theta)
+        buf[i + 1] = total * (1.0 / theta)
         return carry
 
-    lax.fori_loop(0, planes, set_up, 0, unroll=4)
-    found = solve(b, (buf_a, buf_b), diag, fx, fy, fz, UNROLL)
-    owned = owned_rows((rows, lanes), HALO * y, 2 * cy)
+    lax.fori_loop(0, b.shape[0], set_up, 0, unroll=4)
+
+
+def tile_places(rows, y):
+    size = HALO * 3
+    return (rows - size) * (1 - y), (rows - 2 * HALO) * (1 - y) + HALO * y, (rows - size) * (1 - y) + 2 * HALO * y
+
+
+def ahead_kernel(
+    diag, fx, fy, fz, count, mine, got_photon, vector, got_vector,
+    change, far, sums,
+    phi, vk, va, b, buf_a, buf_b,
+):
+    _, _, y, c = places(2)
+    planes, rows, lanes = change.shape
+    cy = mine.shape[1]
+    none = jnp.zeros((planes, HALO, lanes), jnp.float32)
+    halo_rows = pl.ds(2 * cy * (1 - y), HALO)
+    for ref, shift, own, got in (
+        (phi, 1, mine, got_photon.at[0]), (vk, 1, vector.at[0], got_vector.at[0]), (va, 0, vector.at[1], got_vector.at[1])
+    ):
+        framed_own(ref, shift, own, got, y, c)
+        ref[pl.ds(shift, planes), halo_rows, :] = none
+    blank_ends(phi, vk, buf_a, buf_b)
+    rhs_into(b, buf_a, phi, vk, va, None, None)
+    _, near_row, far_row = tile_places(rows, y)
+
+    def save(step, buf):
+        if step < far.shape[0]:
+            far[step] = buf[pl.ds(1, planes), pl.ds(far_row, HALO), :]
+
+    save(0, buf_a)
+    found = solve(b, (buf_a, buf_b), diag, fx, fy, fz, UNROLL, save)
+    at_row = index_along((rows, lanes), 0)
+    summed = owned_rows((rows, lanes), HALO * y, 2 * cy) & ((at_row < near_row) | (at_row >= near_row + HALO))
 
     def add_up(i, carry):
         u = found[i + 1]
         change[i] = u
-        part = jnp.where(owned, count[i], 0.0) * u
+        part = jnp.where(summed, count[i], 0.0) * u
         return carry[0] + folded(part), carry[1] + folded(part * phi[i + 1])
 
     zero = jnp.zeros((8, lanes), jnp.float32)
-    seen, cross = lax.fori_loop(0, planes, add_up, (zero, zero), unroll=4)
-    first = (2 * cy - HALO) * (1 - y) + HALO * y
+    sums[0], sums[1] = lax.fori_loop(0, planes, add_up, (zero, zero), unroll=4)
+
+
+def beside_kernel(
+    phi, diag, fx, fy, fz, count, sums, found_sums, far, vector, got_vector, edge,
+    near, message,
+    phi_in, vk, va, b, buf_a, buf_b,
+):
+    _, _, y, c = places(2)
+    planes, rows, lanes = diag.shape
+    cy = (rows - HALO) // 2
+    all_row, near_row, far_row = tile_places(rows, y)
+    window = pl.ds(pl.multiple_of(all_row, 8), 3 * HALO)
+    inner = c != y
+    source = pl.ds((cy - 2 * HALO) * (1 - y), 2 * HALO)
+    for ref, shift, f in ((vk, 1, 0), (va, 0, 1)):
+        for i in range(planes):
+            own = jnp.where(inner, vector[f, i, source, :], got_vector[f, i, source, :])
+            ref[shift + i, pl.ds(HALO * y, 2 * HALO), :] = own
+            tile = edge_tile(edge[f, i // GROUP], i % GROUP, y)
+            ref[shift + i, pl.ds(2 * HALO * (1 - y), HALO), :] = tile
+    phi_in[...] = phi[:, window, :]
+    blank_ends(vk, buf_a, buf_b)
+    rhs_into(b, buf_a, phi_in, vk, va, None, None)
+    given = pl.ds(2 * HALO * y, HALO)
+
+    def give(step, buf):
+        if step < far.shape[0]:
+            buf[pl.ds(1, planes), given, :] = far[step]
+
+    give(0, buf_a)
+    views = (ref.at[:, window, :] for ref in (diag, fx, fy, fz))
+    found = solve(b, (buf_a, buf_b), *views, UNROLL, give)
+    seen, cross = found_sums[0], found_sums[1]
+    near_rows_at = pl.ds(pl.multiple_of(near_row, 8), HALO)
+    for i in range(planes):
+        u = found[i + 1, pl.ds(HALO, HALO), :]
+        near[i] = u
+        part = count[i, near_rows_at, :] * u
+        seen, cross = seen + part, cross + part * phi[i + 1, near_rows_at, :]
     size = GROUP * REACH
     for g in range(planes // GROUP):
         message[pl.ds(size * g, size), :] = packed_edges(
-            [near_rows(found, 1 + GROUP * g + j, first, y) for j in range(GROUP)]
+            [near_rows(near, GROUP * g + j, 0, y) for j in range(GROUP)]
         )
     rows_of_sums = [jnp.sum(part, axis=0, keepdims=True) for part in (sums[0], seen, cross, sums[1])]
-    message[pl.ds(REACH * planes, 8), :] = jnp.concatenate([*rows_of_sums, zero[:4]], axis=0)
+    none = jnp.zeros((4, lanes), jnp.float32)
+    message[pl.ds(REACH * planes, 8), :] = jnp.concatenate([*rows_of_sums, none], axis=0)
 
 
 def second_kernel(
-    phi, phi_y, phi_z, change, diag, fx, fy, fz, count, sent, came,
+    phi, phi_y, phi_z, change, near, diag, fx, fy, fz, count, sent, came,
     own, message,
     b, buf_a, buf_b, grad_k, grad_a,
     *, dets,
@@ -571,6 +635,7 @@
     cy = (rows - HALO) // 2
     base = HALO * y
     edge = pl.ds(2 * cy * (1 - y), HALO)
+    beside_edge = pl.ds(pl.multiple_of(tile_places(rows, y)[1], 8), HALO)
     tail = pl.ds(REACH * planes, 8)
     sums = jnp.sum(sent[tail, :] + came[tail, :], axis=1, keepdims=True)
     total, seen_sum, cross, square = (sums[g : g + 1] for g in range(4))
@@ -593,10 +658,11 @@
     lax.fori_loop(0, planes, set_up, 0, unroll=4)
     size = GROUP * REACH
     for i in range(planes):
-        u = edge_tile(came[pl.ds(size * (i // GROUP), size), :], i % GROUP, y)
-        value = weighted(count[i, edge, :], u, phi[i + 1, edge, :])
-        b[i, edge, :] = value
-        buf_a[i + 1, edge, :] = value * (1.0 / theta)
+        outer = edge_tile(came[pl.ds(size * (i // GROUP), size), :], i % GROUP, y)
+        for rows_at, u in ((edge, outer), (beside_edge, near[i])):
+            value = weighted(count[i, rows_at, :], u, phi[i + 1, rows_at, :])
+            b[i, rows_at, :] = value
+            buf_a[i + 1, rows_at, :] = value * (1.0 / theta)
     dual = solve(b, (buf_a, buf_b), diag, fx, fy, fz, UNROLL)
 
     def product(i, carry):
@@ -693,7 +759,7 @@
     vv_sum = jnp.sum(vv, axis=0, keepdims=True)
     alpha = wv_sum / cells / (vv_sum / cells + eps_norm)
     off = alpha - a
-    rr = jnp.sum(uu - 2.0 * off * uv + off * off * vv, axis=0, keepdims=True)
+    rr = jnp.sum(uu - 2.0 * off * uv + off * (off * vv), axis=0, keepdims=True)
     beta = jnp.sqrt(rr / cells + eps_norm)
     next_k[...] = (w_k[...] - alpha * vk[...]) / beta
     next_a[...] = (w_a[...] - alpha * va[...]) / beta
@@ -785,38 +851,45 @@
         background, labels, came, labels_came, after=(joined,), hbm=(0, 1), scratch=(raw_labels,), copies=3,
     )
     got = swap_core(fields)
+    frame, wide = (planes, rows, cz), (planes + 2, rows, cz)
+    float_frame, float_wide = float_block(*frame), float_block(*wide)
+    coefs = (f32(*frame), f32(planes + 1, rows, cz), f32(*frame), f32(*frame))
+    kap, *partial, sums = run(
+        stencil_kernel, (f32(*wide), *coefs, f32(2, 8, cz)),
+        kappa_table, absorb_table, mine, fields, got, count,
+        smem=(0, 1), scratch=(float_frame,),
+    )
     (vector,) = run(
-        vector_kernel, (f32(2, planes, cy, cz),), half_vector, came, joined_came, after=(mine,)
+        vector_kernel, (f32(2, planes, cy, cz),), half_vector, came, joined_came, after=(kap,)
     )
     edge = (f32(2, *edge_shape(planes, cz)),)
     (sent,) = run(photon_edge_kernel, edge, mine, fields, got, after=(vector,))
     photon_edge = across_y(sent)
     vector_got = swap_core(vector)
     (vector_sent,) = run(vector_edge_kernel, edge, vector, vector_got, after=(sent,))
-    frame, wide = (planes, rows, cz), (planes + 2, rows, cz)
-    float_frame, float_wide = float_block(*frame), float_block(*wide)
-    coefs = (f32(*frame), f32(planes + 1, rows, cz), f32(*frame), f32(*frame))
-    kap, *partial, sums = run(
-        stencil_kernel, (f32(*wide), *coefs, f32(2, 8, cz)),
-        kappa_table, absorb_table, mine, fields, got, count, after=(vector_sent,), cost=long,
-        smem=(0, 1), scratch=(float_frame,),
+    window = lambda count: float_block(count, 3 * HALO, cz)
+    change, far, found_sums = run(
+        ahead_kernel, (f32(*frame), f32(ITERS - 1, planes, HALO, cz), f32(2, 8, cz)),
+        *partial, count, mine, got, vector, vector_got, after=(vector_sent,),
+        scratch=(float_wide, float_wide, float_frame, float_frame, float_wide, float_wide),
     )
     diag, fx, fy, fz = run(
-        halo_kernel, coefs, kappa_table, absorb_table, photon_edge, kap, *partial, smem=(0, 1)
+        halo_kernel, coefs, kappa_table, absorb_table, photon_edge, kap, *partial, after=(change,), smem=(0, 1)
     )
     densities = run(
         density_kernel, (f32(*wide), f32(*frame), f32(*frame)), mine, got, photon_edge, after=(fz,)
     )
-    change, sent = run(
-        first_kernel, (f32(*frame), f32(REACH * planes + 8, cz)),
-        *densities, diag, fx, fy, fz, count, sums, vector, vector_got, across_y(vector_sent),
-        scratch=(float_wide, float_frame, float_frame, float_wide, float_wide),
+    near, sent = run(
+        beside_kernel, (f32(planes, HALO, cz), f32(REACH * planes + 8, cz)),
+        densities[0], diag, fx, fy, fz, count, sums, found_sums, far, vector, vector_got, across_y(vector_sent),
+        scratch=(window(planes + 2), window(planes + 2), window(planes), window(planes), window(planes + 2),
+                 window(planes + 2)),
     )
     heard = across_y(sent)
     own, message = run(
         functools.partial(second_kernel, dets=dets),
         (f32(2, planes, cy, cz), f32(2, planes, cy, cz)),
-        *densities, change, diag, fx, fy, fz, count, sent, heard,
+        *densities, change, near, diag, fx, fy, fz, count, sent, heard,
         scratch=(float_frame, float_wide, float_wide, float_frame, float_frame),
     )
     piece = f32(2, groups, cy, cz)

time: 70 us -> 76.2 us (1.089)
  waiting for transfers between devices: 14.7 us -> 17.5 us
  Pallas kernels: 19.5 us -> 21.6 us
  local copies, waits for them, and re-layouts: 0.07 us -> 1.64 us
  blocking collectives: 11.2 us -> 10.3 us
    ppermute x7, waiting for transfers between devices: 3.11 us -> 7.49 us  [swap_x(): return lax.ppermute(value, 'gx', [(0, 1), (1, 0)])]
    ppermute x6, waiting for transfers between devices: 6.67 us -> 4.19 us  [along_z(): return lax.ppermute(value, 'src', [(i, i ^ k) for i in range(n)])]
    pallas_call x25 -> x26, Pallas kernels: 19.5 us -> 21.6 us  [run(): pl.pallas_call(body if waits else kernel, out_shape=tuple(outs), in_specs...]
    unnamed x18, local copies, waits for them, and re-layouts: 0.05 us -> 1.63 us
    ppermute x6, starting transfers between devices: 8.91 us -> 10 us  [along_z(): return lax.ppermute(value, 'src', [(i, i ^ k) for i in range(n)])]
    ppermute x3, waiting for transfers between devices: 2.85 us -> 3.89 us  [across_y(): return lax.ppermute(value, 'gy', [(i, (i + 2) % 4) for i in range(4)])]
    all_to_all x1, blocking collectives: 11.2 us -> 10.3 us  [per_device_paired(): lax.all_to_all(jnp.broadcast_to(tile, (8 * n, 1, 128)), everyone, 0, 0)]
    ppermute x3, starting transfers between devices: 4.75 us -> 3.99 us  [across_y(): return lax.ppermute(value, 'gy', [(i, (i + 2) % 4) for i in range(4)])]
  transfers between devices with their start and end apart: 19 -> 19, of which waited for: 9 -> 6; matrix products, arithmetic and copies ran while one was open for 0% -> 0% of each run, Pallas kernels for 14% -> 15%
where the time goes in v20:
time: 76.2 us; the launch traced here: 76 us
  starting transfers between devices  23.3 us (31%)
  Pallas kernels  21.6 us (28%)
  waiting for transfers between devices  17.5 us (23%)
  blocking collectives  10.3 us (14%)
  between operations  1.65 us (2%)
  local copies, waits for them, and re-layouts  1.64 us (2%)
    pallas_call x26, Pallas kernels, run(): pl.pallas_call(body if waits else kernel, out_shape=tuple(outs), in_specs...  21.6 us
    all_to_all x1, blocking collectives, per_device_paired(): lax.all_to_all(jnp.broadcast_to(tile, (8 * n, 1, 128)), everyone, 0, 0)  10.3 us
    ppermute x6, starting transfers between devices, along_z(): return lax.ppermute(value, 'src', [(i, i ^ k) for i in range(n)])  10 us
    ppermute x7, starting transfers between devices, swap_x(): return lax.ppermute(value, 'gx', [(0, 1), (1, 0)])  9.14 us
    ppermute x7, waiting for transfers between devices, swap_x(): return lax.ppermute(value, 'gx', [(0, 1), (1, 0)])  7.49 us
    ppermute x6, waiting for transfers between devices, along_z(): return lax.ppermute(value, 'src', [(i, i ^ k) for i in range(n)])  4.19 us
    ppermute x3, starting transfers between devices, across_y(): return lax.ppermute(value, 'gy', [(i, (i + 2) % 4) for i in range(4)])  3.99 us
    ppermute x3, waiting for transfers between devices, across_y(): return lax.ppermute(value, 'gy', [(i, (i + 2) % 4) for i in range(4)])  3.89 us
  transfers between devices with their start and end apart: 19, of which 6 were waited for; matrix products, arithmetic and copies ran while one was open for 0% of the time, Pallas kernels for 15%

profile of v20, /device:TPU:0, one launch (start us, length us, event | category | flops | bytes accessed | tf_op | source)
XLA Modules:
  0.0 76.0 jit_solution(1492004760805033039)
XLA Ops:
  0.6 1.9 %shard_map.122 = (f32[4,32,128]{2,1,0:T(8,128)}, f32[20,32,128]{2,1,0:T(8,128)}) custom-call(f32[4,8,32,128]{3,2,1,0:T(8,128)} %refs_0_.2, f32[8,32,32]{2,1,0:T(8,128)} %vk.5, f32[8,32,32]{2,1,0:T(8,128)} %va.5), custom_call_target="tpu_custom_call" | custom-call | tf_op jit(solution)/shard_map/pallas_call | solution.py:787
  2.6 3.0 %collective-permute-start.1 = (f32[20,32,128]{2,1,0:T(8,128)}, f32[20,32,128]{2,1,0:T(8,128)S(1)}, u32[]{:S(2)}, u32[]{:S(2)}) collective-permute-start(f32[20,32,128]{2,1,0:T(8,128)} %get-tuple-element.33), channel_id=1, source_target_pairs={{0,4},{4,0},{1,5},{5,1},{2,6},{6,2},{3,7},{7,3},{8,12},{12,8},{9,1... | collective-permute-start | bytes 983048 | tf_op jit(solution)/shard_map/ppermute | solution.py:817
  5.7 4.1 %collective-permute-start.4 = (f32[4,32,128]{2,1,0:T(8,128)}, f32[4,32,128]{2,1,0:T(8,128)S(1)}, u32[]{:S(2)}, u32[]{:S(2)}) collective-permute-start(f32[4,32,128]{2,1,0:T(8,128)} %get-tuple-element.34), channel_id=1, source_target_pairs={{0,24},{8,16},{16,8},{24,0},{1,25},{9,17},{17,9},{25,1},{2,26},{10... | collective-permute-start | bytes 196616 | tf_op jit(solution)/shard_map/ppermute | solution.py:823
  10.9 5.4 %collective-permute-done.refs_2_.refs_3_ = s32[8,32,128]{2,1,0:T(8,128)S(1)} collective-permute-done((s32[8,32,128]{2,1,0:T(8,128)S(1)}, s32[8,32,128]{2,1,0:T(8,128)S(1)}, u32[]{:S(2)}, u32[]{:S(2)}) %collective-permute-start) | collective-permute-done | bytes 131104 | tf_op jit(solution)/shard_map/ppermute | solution.py:817
  16.3 2.1 %shard_map.121 = (f32[16,72,128]{2,1,0:T(8,128)S(1)}, f32[1,128]{1,0:T(1,128)S(1)}) custom-call(s32[1,1024]{1,0:T(1,128)S(1)} %bitcast.3, f32[1]{0:T(128)S(6)} %copy.13.refs_1_, s32[8,32,128]{2,1,0:T(8,128)S(1)} %collective-permute-done.refs_2_.refs_3_), custom_call_target="tpu_custom_call" | custom-call | flops 301989888 | bytes 589824 | tf_op jit(solution)/shard_map/pallas_call | solution.py:787
  18.5 0.9 %copy-done = f32[4,8,32,128]{3,2,1,0:T(8,128)S(1)} copy-done((f32[4,8,32,128]{3,2,1,0:T(8,128)S(1)}, f32[4,8,32,128]{3,2,1,0:T(8,128)}, u32[]{:S(2)}) %copy-start) | copy-done | bytes 524312
  20.1 1.8 %collective-permute-start.6 = (f32[12,32,128]{2,1,0:T(8,128)S(1)}, f32[12,32,128]{2,1,0:T(8,128)S(1)}, u32[]{:S(2)}, u32[]{:S(2)}) collective-permute-start(f32[12,32,128]{2,1,0:T(8,128)S(1)} %shard_map.123.refs_4_.joined), channel_id=1, source_target_pairs={{0,4},{4,0},{1,5},{5,1},{2,6},{6,2},{3,7},{7,3},{8,12},{12,8},{9,1... | collective-permute-start | bytes 589832 | tf_op jit(solution)/shard_map/ppermute | solution.py:817
  23.0 2.3 %shard_map.126 = (f32[18,72,128]{2,1,0:T(8,128)S(1)}, f32[16,72,128]{2,1,0:T(8,128)S(1)}, f32[17,72,128]{2,1,0:T(8,128)S(1)}, f32[16,72,128]{2,1,0:T(8,128)S(1)}...) custom-call(f32[16]{0:T(128)S(1)} %copy-done.6, f32[16]{0:T(128)S(1)} %copy-done.7, ...), custom_call_target="tpu_custom_call" | custom-call | tf_op jit(solution)/shard_map/pallas_call | solution.py:787
  25.3 2.1 %collective-permute-done.6.refs_2_ = f32[12,32,128]{2,1,0:T(8,128)S(1)} collective-permute-done((f32[12,32,128]{2,1,0:T(8,128)S(1)}, f32[12,32,128]{2,1,0:T(8,128)S(1)}, u32[]{:S(2)}, u32[]{:S(2)}) %collective-permute-start.6) | collective-permute-done | bytes 196640 | tf_op jit(solution)/shard_map/ppermute | solution.py:817
  27.9 1.8 %collective-permute-start.7 = (f32[2,4,24,128]{3,2,1,0:T(8,128)S(1)}, f32[2,4,24,128]{3,2,1,0:T(8,128)S(1)}, u32[]{:S(2)}, u32[]{:S(2)}) collective-permute-start(f32[2,4,24,128]{3,2,1,0:T(8,128)S(1)} %shard_map.128.refs_2_), channel_id=1, source_target_pairs={{0,2},{1,3},{2,0},{3,1},{4,6},{5,7},{6,4},{7,5},{8,10},{9,11},{10,... | collective-permute-start | bytes 294920 | tf_op jit(solution)/shard_map/ppermute | solution.py:844
  29.8 1.8 %collective-permute-start.9 = (f32[2,4,24,128]{3,2,1,0:T(8,128)S(1)}, f32[2,4,24,128]{3,2,1,0:T(8,128)S(1)}, u32[]{:S(2)}, u32[]{:S(2)}) collective-permute-start(f32[2,4,24,128]{3,2,1,0:T(8,128)S(1)} %shard_map.129.refs_9_), channel_id=1, source_target_pairs={{0,2},{1,3},{2,0},{3,1},{4,6},{5,7},{6,4},{7,5},{8,10},{9,11},{10,... | collective-permute-start | bytes 294920 | tf_op jit(solution)/shard_map/ppermute | solution.py:844
  31.6 4.2 %shard_map.130 = (f32[16,72,128]{2,1,0:T(8,128)S(1)}, f32[5,16,8,128]{3,2,1,0:T(8,128)S(1)}, f32[2,8,128]{2,1,0:T(8,128)S(1)}) custom-call(f32[16,72,128]{2,1,0:T(8,128)S(1)} %get-tuple-element.39.refs_0_.refs_4_, f32[17,72,128]{2,1,0:T(8,128)S(1)} %get-tuple-element.40.refs_1_.refs_5_, f32[16,72,128]{2,1,0:T(8,128)S(1)} %get-tuple-element.41.refs_2_.refs_6_, ...), custom_call_target="tpu_custom_call" | custom-call | tf_op jit(solution)/shard_map/pallas_call | solution.py:787
  37.2 1.8 %shard_map.133 = (f32[16,8,128]{2,1,0:T(8,128)S(1)}, f32[104,128]{1,0:T(8,128)S(1)}) custom-call(f32[18,72,128]{2,1,0:T(8,128)S(1)} %get-tuple-element.45.phi, f32[16,72,128]{2,1,0:T(8,128)S(1)} %get-tuple-element.48.diag, f32[17,72,128]{2,1,0:T(8,128)S(1)} %get-tuple-element.49.fx, f32[16,72,128]{2,1,0:T(8,128)S(1)} %get-tuple-element.50.fy, ...), custom_call_target="tpu_custom_call" | custom-call | tf_op jit(solution)/shard_map/pallas_call | solution.py:787
  39.4 3.9 %collective-permute-done.10.came = f32[104,128]{1,0:T(8,128)S(1)} collective-permute-done((f32[104,128]{1,0:T(8,128)S(1)}, f32[104,128]{1,0:T(8,128)S(1)}, u32[]{:S(2)}, u32[]{:S(2)}) %collective-permute-start.10) | collective-permute-done | bytes 53280 | tf_op jit(solution)/shard_map/ppermute | solution.py:844
  43.2 4.1 %shard_map.134 = (f32[2,16,32,128]{3,2,1,0:T(8,128)S(1)}, f32[2,16,32,128]{3,2,1,0:T(8,128)S(1)}) custom-call(f32[18,72,128]{2,1,0:T(8,128)S(1)} %get-tuple-element.45.phi, f32[16,72,128]{2,1,0:T(8,128)S(1)} %get-tuple-element.46.phi_y, f32[16,72,128]{2,1,0:T(8,128)S(1)} %get-tuple-element.47.phi_z, f32[16,72,128]{2,1,0:T(8,128)S(1)} %get-tuple-element.43.refs_8_.change, ...), custom_call_target="tpu_custom_call" | custom-call | tf_op jit(solution)/shard_map/pallas_call | solution.py:787
  47.4 1.9 %collective-permute-done.11.came.refs_1_ = f32[2,16,32,128]{3,2,1,0:T(8,128)S(1)} collective-permute-done((f32[2,16,32,128]{3,2,1,0:T(8,128)S(1)}, f32[2,16,32,128]{3,2,1,0:T(8,128)S(1)}, u32[]{:S(2)}, u32[]{:S(2)}) %collective-permute-start.11) | collective-permute-done | bytes 524320 | tf_op jit(solution)/shard_map/ppermute | solution.py:820
  49.6 1.6 %collective-permute-start.12 = (f32[1,2,2,32,128]{4,3,2,1,0:T(8,128)S(1)}, f32[1,2,2,32,128]{4,3,2,1,0:T(8,128)S(1)}, u32[]{:S(2)}, u32[]{:S(2)}) collective-permute-start(f32[1,2,2,32,128]{4,3,2,1,0:T(8,128)S(1)} %shard_map.136.refs_2_), channel_id=1, source_target_pairs={{0,4},{4,0},{1,5},{5,1},{2,6},{6,2},{3,7},{7,3},{8,12},{12,8},{9,1... | collective-permute-start | bytes 196616 | tf_op jit(solution)/shard_map/ppermute | solution.py:817
  51.8 1.6 %collective-permute-start.17 = (f32[1,2,2,32,128]{4,3,2,1,0:T(8,128)S(1)}, f32[1,2,2,32,128]{4,3,2,1,0:T(8,128)S(1)}, u32[]{:S(2)}, u32[]{:S(2)}) collective-permute-start(f32[1,2,2,32,128]{4,3,2,1,0:T(8,128)S(1)} %shard_map.137.refs_2_), channel_id=1, source_target_pairs={{0,4},{4,0},{1,5},{5,1},{2,6},{6,2},{3,7},{7,3},{8,12},{12,8},{9,1... | collective-permute-start | bytes 196616 | tf_op jit(solution)/shard_map/ppermute | solution.py:817
  54.5 2.7 %collective-permute-start.13 = (f32[2,2,32,128]{3,2,1,0:T(8,128)S(1)}, f32[2,2,32,128]{3,2,1,0:T(8,128)S(1)}, u32[]{:S(2)}, u32[]{:S(2)}) collective-permute-start(f32[2,2,32,128]{3,2,1,0:T(8,128)S(1)} %shard_map.140), channel_id=1, source_target_pairs={{0,16},{8,24},{16,0},{24,8},{1,17},{9,25},{17,1},{25,9},{2,18},{10... | collective-permute-start | bytes 196616 | tf_op jit(solution)/shard_map/ppermute | solution.py:823
  57.2 2.7 %collective-permute-start.15 = (f32[2,2,32,128]{3,2,1,0:T(8,128)S(1)}, f32[2,2,32,128]{3,2,1,0:T(8,128)S(1)}, u32[]{:S(2)}, u32[]{:S(2)}) collective-permute-start(f32[2,2,32,128]{3,2,1,0:T(8,128)S(1)} %shard_map.141), channel_id=1, source_target_pairs={{0,24},{8,16},{16,8},{24,0},{1,25},{9,17},{17,9},{25,1},{2,26},{10... | collective-permute-start | bytes 196616 | tf_op jit(solution)/shard_map/ppermute | solution.py:823
  60.0 3.3 %collective-permute-done.15.refs_1_ = f32[2,2,32,128]{3,2,1,0:T(8,128)S(1)} collective-permute-done((f32[2,2,32,128]{3,2,1,0:T(8,128)S(1)}, f32[2,2,32,128]{3,2,1,0:T(8,128)S(1)}, u32[]{:S(2)}, u32[]{:S(2)}) %collective-permute-start.15) | collective-permute-done | bytes 65568 | tf_op jit(solution)/shard_map/ppermute | solution.py:823
  63.3 0.9 %collective-permute-done.18.refs_3_ = f32[2,2,32,128]{3,2,1,0:T(8,128)S(1)} collective-permute-done((f32[2,2,32,128]{3,2,1,0:T(8,128)S(1)}, f32[2,2,32,128]{3,2,1,0:T(8,128)S(1)}, u32[]{:S(2)}, u32[]{:S(2)}) %collective-permute-start.18) | collective-permute-done | bytes 65568 | tf_op jit(solution)/shard_map/ppermute | solution.py:823
  64.7 10.3 %all_to_all.5.tiles = f32[32,1,128]{2,1,0:T(1,128)S(1)} all-to-all(f32[32,1,128]{2,1,0:T(1,128)S(1)} %broadcast_in_dim.3), channel_id=1, replica_groups=mesh['src'=4,'gx'=2,'gy'=4] {'src','gx','gy'}, dimensions={0} | all-to-all | bytes 32768 | tf_op jit(solution)/shard_map/all_to_all | solution.py:914
  75.0 1.0 %shard_map.146 = (f32[8,32,32]{2,1,0:T(8,128)}, f32[8,32,32]{2,1,0:T(8,128)}, f32[2]{0:T(128)}) custom-call(f32[32,1,128]{2,1,0:T(1,128)S(1)} %all_to_all.5.tiles, f32[8,32,32]{2,1,0:T(8,128)S(1)} %get-tuple-element.59.w_k, f32[8,32,32]{2,1,0:T(8,128)S(1)} %get-tuple-element.60.w_a, f32[8,32,32]{2,1,0:T(8,128)S(1)} %copy-done.1, f32[8,32,32]{2,1,0:T(8,128)S(1)} %copy-done.2), custom_call_target="tpu_custom_call" | custom-call | tf_op jit(solution)/shard_map/pallas_call | solution.py:787
  (60 shorter events, 7.2 us)
Async XLA Ops:
  0.6 4.9 %copy-start.3 = (s32[8,32,128]{2,1,0:T(8,128)S(1)}, s32[8,32,128]{2,1,0:T(8,128)}, u32[]{:S(2)}) copy-start(s32[8,32,128]{2,1,0:T(8,128)} %refs_1_.3) | copy-start | bytes 393220
  2.6 13.7 %copy-start.8 = (s32[1024]{0:T(1024)S(1)}, s32[1024]{0:T(1024)}, u32[]{:S(2)}) copy-start(s32[1024]{0:T(1024)} %param.14) | copy-start | bytes 12292
  2.6 15.9 %collective-permute-start.1 = (f32[20,32,128]{2,1,0:T(8,128)}, f32[20,32,128]{2,1,0:T(8,128)S(1)}, u32[]{:S(2)}, u32[]{:S(2)}) collective-permute-start(f32[20,32,128]{2,1,0:T(8,128)} %get-tuple-element.33), channel_id=1, source_target_pairs={{0,4},{4,0},{1,5},{5,1},{2,6},{6,2},{3,7},{7,3},{8,12},{12,8},{9,1... | collective-permute-start | bytes 983048 | tf_op jit(solution)/shard_map/ppermute | solution.py:817
  5.6 10.7 %collective-permute-start = (s32[8,32,128]{2,1,0:T(8,128)S(1)}, s32[8,32,128]{2,1,0:T(8,128)S(1)}, u32[]{:S(2)}, u32[]{:S(2)}) collective-permute-start(s32[8,32,128]{2,1,0:T(8,128)S(1)} %copy-done.3), channel_id=1, source_target_pairs={{0,4},{4,0},{1,5},{5,1},{2,6},{6,2},{3,7},{7,3},{8,12},{12,8},{9,1... | collective-permute-start | bytes 393224 | tf_op jit(solution)/shard_map/ppermute | solution.py:817
  5.7 12.8 %collective-permute-start.4 = (f32[4,32,128]{2,1,0:T(8,128)}, f32[4,32,128]{2,1,0:T(8,128)S(1)}, u32[]{:S(2)}, u32[]{:S(2)}) collective-permute-start(f32[4,32,128]{2,1,0:T(8,128)} %get-tuple-element.34), channel_id=1, source_target_pairs={{0,24},{8,16},{16,8},{24,0},{1,25},{9,17},{17,9},{25,1},{2,26},{10... | collective-permute-start | bytes 196616 | tf_op jit(solution)/shard_map/ppermute | solution.py:823
  9.7 8.7 %collective-permute-start.3 = (f32[4,32,128]{2,1,0:T(8,128)}, f32[4,32,128]{2,1,0:T(8,128)S(1)}, u32[]{:S(2)}, u32[]{:S(2)}) collective-permute-start(f32[4,32,128]{2,1,0:T(8,128)} %get-tuple-element.34), channel_id=1, source_target_pairs={{0,16},{8,24},{16,0},{24,8},{1,17},{9,25},{17,1},{25,9},{2,18},{10... | collective-permute-start | bytes 196616 | tf_op jit(solution)/shard_map/ppermute | solution.py:823
  9.7 8.7 %collective-permute-start.2 = (f32[4,32,128]{2,1,0:T(8,128)}, f32[4,32,128]{2,1,0:T(8,128)S(1)}, u32[]{:S(2)}, u32[]{:S(2)}) collective-permute-start(f32[4,32,128]{2,1,0:T(8,128)} %get-tuple-element.34), channel_id=1, source_target_pairs={{0,8},{8,0},{16,24},{24,16},{1,9},{9,1},{17,25},{25,17},{2,10},{10... | collective-permute-start | bytes 196616 | tf_op jit(solution)/shard_map/ppermute | solution.py:823
  18.5 3.4 %copy-start.1 = (f32[8,32,32]{2,1,0:T(8,128)S(1)}, f32[8,32,32]{2,1,0:T(8,128)}, u32[]{:S(2)}) copy-start(f32[8,32,32]{2,1,0:T(8,128)} %vk.5) | copy-start | bytes 98308
  20.0 2.3 %collective-permute-start.5 = (f32[2,16,32,128]{3,2,1,0:T(8,128)S(1)}, f32[2,16,32,128]{3,2,1,0:T(8,128)S(1)}, u32[]{:S(2)}, u32[]{:S(2)}) collective-permute-start(f32[2,16,32,128]{3,2,1,0:T(8,128)S(1)} %get-tuple-element.37.fields.refs_1_), channel_id=1, source_target_pairs={{0,1},{1,0},{2,3},{3,2},{4,5},{5,4},{6,7},{7,6},{8,9},{9,8},{10,11... | collective-permute-start | bytes 1572872 | tf_op jit(solution)/shard_map/ppermute | solution.py:820
  20.1 7.3 %collective-permute-start.6 = (f32[12,32,128]{2,1,0:T(8,128)S(1)}, f32[12,32,128]{2,1,0:T(8,128)S(1)}, u32[]{:S(2)}, u32[]{:S(2)}) collective-permute-start(f32[12,32,128]{2,1,0:T(8,128)S(1)} %shard_map.123.refs_4_.joined), channel_id=1, source_target_pairs={{0,4},{4,0},{1,5},{5,1},{2,6},{6,2},{3,7},{7,3},{8,12},{12,8},{9,1... | collective-permute-start | bytes 589832 | tf_op jit(solution)/shard_map/ppermute | solution.py:817
  27.8 2.0 %collective-permute-start.8 = (f32[2,16,32,128]{3,2,1,0:T(8,128)S(1)}, f32[2,16,32,128]{3,2,1,0:T(8,128)S(1)}, u32[]{:S(2)}, u32[]{:S(2)}) collective-permute-start(f32[2,16,32,128]{3,2,1,0:T(8,128)S(1)} %shard_map.127.refs_3_.refs_0_.refs_7_.vector), channel_id=1, source_target_pairs={{0,1},{1,0},{2,3},{3,2},{4,5},{5,4},{6,7},{7,6},{8,9},{9,8},{10,11... | collective-permute-start | bytes 1572872 | tf_op jit(solution)/shard_map/ppermute | solution.py:820
  27.9 8.0 %collective-permute-start.7 = (f32[2,4,24,128]{3,2,1,0:T(8,128)S(1)}, f32[2,4,24,128]{3,2,1,0:T(8,128)S(1)}, u32[]{:S(2)}, u32[]{:S(2)}) collective-permute-start(f32[2,4,24,128]{3,2,1,0:T(8,128)S(1)} %shard_map.128.refs_2_), channel_id=1, source_target_pairs={{0,2},{1,3},{2,0},{3,1},{4,6},{5,7},{6,4},{7,5},{8,10},{9,11},{10,... | collective-permute-start | bytes 294920 | tf_op jit(solution)/shard_map/ppermute | solution.py:844
  29.8 7.4 %collective-permute-start.9 = (f32[2,4,24,128]{3,2,1,0:T(8,128)S(1)}, f32[2,4,24,128]{3,2,1,0:T(8,128)S(1)}, u32[]{:S(2)}, u32[]{:S(2)}) collective-permute-start(f32[2,4,24,128]{3,2,1,0:T(8,128)S(1)} %shard_map.129.refs_9_), channel_id=1, source_target_pairs={{0,2},{1,3},{2,0},{3,1},{4,6},{5,7},{6,4},{7,5},{8,10},{9,11},{10,... | collective-permute-start | bytes 294920 | tf_op jit(solution)/shard_map/ppermute | solution.py:844
  39.0 4.2 %collective-permute-start.10 = (f32[104,128]{1,0:T(8,128)S(1)}, f32[104,128]{1,0:T(8,128)S(1)}, u32[]{:S(2)}, u32[]{:S(2)}) collective-permute-start(f32[104,128]{1,0:T(8,128)S(1)} %get-tuple-element.55.sent), channel_id=1, source_target_pairs={{0,2},{1,3},{2,0},{3,1},{4,6},{5,7},{6,4},{7,5},{8,10},{9,11},{10,... | collective-permute-start | bytes 159752 | tf_op jit(solution)/shard_map/ppermute | solution.py:844
  47.3 2.0 %collective-permute-start.11 = (f32[2,16,32,128]{3,2,1,0:T(8,128)S(1)}, f32[2,16,32,128]{3,2,1,0:T(8,128)S(1)}, u32[]{:S(2)}, u32[]{:S(2)}) collective-permute-start(f32[2,16,32,128]{3,2,1,0:T(8,128)S(1)} %get-tuple-element.57), channel_id=1, source_target_pairs={{0,1},{1,0},{2,3},{3,2},{4,5},{5,4},{6,7},{7,6},{8,9},{9,8},{10,11... | collective-permute-start | bytes 1572872 | tf_op jit(solution)/shard_map/ppermute | solution.py:820
  49.6 4.9 %collective-permute-start.12 = (f32[1,2,2,32,128]{4,3,2,1,0:T(8,128)S(1)}, f32[1,2,2,32,128]{4,3,2,1,0:T(8,128)S(1)}, u32[]{:S(2)}, u32[]{:S(2)}) collective-permute-start(f32[1,2,2,32,128]{4,3,2,1,0:T(8,128)S(1)} %shard_map.136.refs_2_), channel_id=1, source_target_pairs={{0,4},{4,0},{1,5},{5,1},{2,6},{6,2},{3,7},{7,3},{8,12},{12,8},{9,1... | collective-permute-start | bytes 196616 | tf_op jit(solution)/shard_map/ppermute | solution.py:817
  51.2 6.0 %collective-permute-start.14 = (f32[1,2,2,32,128]{4,3,2,1,0:T(8,128)S(1)}, f32[1,2,2,32,128]{4,3,2,1,0:T(8,128)S(1)}, u32[]{:S(2)}, u32[]{:S(2)}) collective-permute-start(f32[1,2,2,32,128]{4,3,2,1,0:T(8,128)S(1)} %shard_map.135.refs_2_), channel_id=1, source_target_pairs={{0,4},{4,0},{1,5},{5,1},{2,6},{6,2},{3,7},{7,3},{8,12},{12,8},{9,1... | collective-permute-start | bytes 196616 | tf_op jit(solution)/shard_map/ppermute | solution.py:817
  51.8 8.0 %collective-permute-start.17 = (f32[1,2,2,32,128]{4,3,2,1,0:T(8,128)S(1)}, f32[1,2,2,32,128]{4,3,2,1,0:T(8,128)S(1)}, u32[]{:S(2)}, u32[]{:S(2)}) collective-permute-start(f32[1,2,2,32,128]{4,3,2,1,0:T(8,128)S(1)} %shard_map.137.refs_2_), channel_id=1, source_target_pairs={{0,4},{4,0},{1,5},{5,1},{2,6},{6,2},{3,7},{7,3},{8,12},{12,8},{9,1... | collective-permute-start | bytes 196616 | tf_op jit(solution)/shard_map/ppermute | solution.py:817
  53.6 6.4 %collective-permute-start.16 = (f32[1,2,2,32,128]{4,3,2,1,0:T(8,128)S(1)}, f32[1,2,2,32,128]{4,3,2,1,0:T(8,128)S(1)}, u32[]{:S(2)}, u32[]{:S(2)}) collective-permute-start(f32[1,2,2,32,128]{4,3,2,1,0:T(8,128)S(1)} %shard_map.138.refs_2_), channel_id=1, source_target_pairs={{0,4},{4,0},{1,5},{5,1},{2,6},{6,2},{3,7},{7,3},{8,12},{12,8},{9,1... | collective-permute-start | bytes 196616 | tf_op jit(solution)/shard_map/ppermute | solution.py:817
  54.5 5.5 %collective-permute-start.13 = (f32[2,2,32,128]{3,2,1,0:T(8,128)S(1)}, f32[2,2,32,128]{3,2,1,0:T(8,128)S(1)}, u32[]{:S(2)}, u32[]{:S(2)}) collective-permute-start(f32[2,2,32,128]{3,2,1,0:T(8,128)S(1)} %shard_map.140), channel_id=1, source_target_pairs={{0,16},{8,24},{16,0},{24,8},{1,17},{9,25},{17,1},{25,9},{2,18},{10... | collective-permute-start | bytes 196616 | tf_op jit(solution)/shard_map/ppermute | solution.py:823
  57.2 6.1 %collective-permute-start.15 = (f32[2,2,32,128]{3,2,1,0:T(8,128)S(1)}, f32[2,2,32,128]{3,2,1,0:T(8,128)S(1)}, u32[]{:S(2)}, u32[]{:S(2)}) collective-permute-start(f32[2,2,32,128]{3,2,1,0:T(8,128)S(1)} %shard_map.141), channel_id=1, source_target_pairs={{0,24},{8,16},{16,8},{24,0},{1,25},{9,17},{17,9},{25,1},{2,26},{10... | collective-permute-start | bytes 196616 | tf_op jit(solution)/shard_map/ppermute | solution.py:823
  59.9 4.3 %collective-permute-start.18 = (f32[2,2,32,128]{3,2,1,0:T(8,128)S(1)}, f32[2,2,32,128]{3,2,1,0:T(8,128)S(1)}, u32[]{:S(2)}, u32[]{:S(2)}) collective-permute-start(f32[2,2,32,128]{3,2,1,0:T(8,128)S(1)} %shard_map.144), channel_id=1, source_target_pairs={{0,8},{8,0},{16,24},{24,16},{1,9},{9,1},{17,25},{25,17},{2,10},{10... | collective-permute-start | bytes 196616 | tf_op jit(solution)/shard_map/ppermute | solution.py:823
  60.0 4.2 %copy-start.4 = (f32[8,32,32]{2,1,0:T(8,128)S(1)}, f32[8,32,32]{2,1,0:T(8,128)}, u32[]{:S(2)}) copy-start(f32[8,32,32]{2,1,0:T(8,128)} %refs_6_.1) | copy-start | bytes 98308
  60.0 4.2 %copy-start.5 = (f32[8,32,32]{2,1,0:T(8,128)S(1)}, f32[8,32,32]{2,1,0:T(8,128)}, u32[]{:S(2)}) copy-start(f32[8,32,32]{2,1,0:T(8,128)} %refs_7_.1) | copy-start | bytes 98308
  (4 other events, 5.8 us)

commit v21 on v17

--- a/solution.py
+++ b/solution.py
@@ -538,7 +538,7 @@
         buf_a[i + 1] = total * (1.0 / theta)
         return carry
 
-    lax.fori_loop(0, planes, set_up, 0, unroll=4)
+    lax.fori_loop(0, planes, set_up, 0, unroll=8)
     found = solve(b, (buf_a, buf_b), diag, fx, fy, fz, UNROLL)
     owned = owned_rows((rows, lanes), HALO * y, 2 * cy)
 
@@ -549,7 +549,7 @@
         return carry[0] + folded(part), carry[1] + folded(part * phi[i + 1])
 
     zero = jnp.zeros((8, lanes), jnp.float32)
-    seen, cross = lax.fori_loop(0, planes, add_up, (zero, zero), unroll=4)
+    seen, cross = lax.fori_loop(0, planes, add_up, (zero, zero), unroll=8)
     first = (2 * cy - HALO) * (1 - y) + HALO * y
     size = GROUP * REACH
     for g in range(planes // GROUP):
@@ -590,7 +590,7 @@
         buf_a[i + 1] = value * (1.0 / theta)
         return carry
 
-    lax.fori_loop(0, planes, set_up, 0, unroll=4)
+    lax.fori_loop(0, planes, set_up, 0, unroll=8)
     size = GROUP * REACH
     for i in range(planes):
         u = edge_tile(came[pl.ds(size * (i // GROUP), size), :], i % GROUP, y)
@@ -614,7 +614,7 @@
             message[f, i] = ref[i, pl.ds(base + cy * (1 - c), cy), :]
         return carry
 
-    lax.fori_loop(0, planes, product, 0, unroll=4)
+    lax.fori_loop(0, planes, product, 0, unroll=8)
 
 
 def packed_slabs(own, came, half, choices, outs):
@@ -693,7 +693,7 @@
     vv_sum = jnp.sum(vv, axis=0, keepdims=True)
     alpha = wv_sum / cells / (vv_sum / cells + eps_norm)
     off = alpha - a
-    rr = jnp.sum(uu - 2.0 * off * uv + off * off * vv, axis=0, keepdims=True)
+    rr = jnp.sum(uu - 2.0 * off * uv + off * (off * vv), axis=0, keepdims=True)
     beta = jnp.sqrt(rr / cells + eps_norm)
     next_k[...] = (w_k[...] - alpha * vk[...]) / beta
     next_a[...] = (w_a[...] - alpha * va[...]) / beta

time: 70 us -> 69.7 us (level)
  no operation moved by 1% of the time
where the time goes in v21:
time: 69.7 us; the launch traced here: 69.5 us
  starting transfers between devices  22.8 us (33%)
  Pallas kernels  19.1 us (27%)
  waiting for transfers between devices  14.7 us (21%)
  blocking collectives  11.2 us (16%)
  between operations  1.61 us (2%)
    pallas_call x25, Pallas kernels, run(): pl.pallas_call(body if waits else kernel, out_shape=tuple(outs), in_specs...  19.1 us
    all_to_all x1, blocking collectives, per_device_paired(): lax.all_to_all(jnp.broadcast_to(tile, (8 * n, 1, 128)), everyone, 0, 0)  11.2 us
    ppermute x6, starting transfers between devices, along_z(): return lax.ppermute(value, 'src', [(i, i ^ k) for i in range(n)])  8.91 us
    ppermute x7, starting transfers between devices, swap_x(): return lax.ppermute(value, 'gx', [(0, 1), (1, 0)])  8.89 us
    ppermute x6, waiting for transfers between devices, along_z(): return lax.ppermute(value, 'src', [(i, i ^ k) for i in range(n)])  6.67 us
    ppermute x3, starting transfers between devices, across_y(): return lax.ppermute(value, 'gy', [(i, (i + 2) % 4) for i in range(4)])  4.75 us
    ppermute x7, waiting for transfers between devices, swap_x(): return lax.ppermute(value, 'gx', [(0, 1), (1, 0)])  3.11 us
    ppermute x3, waiting for transfers between devices, across_y(): return lax.ppermute(value, 'gy', [(i, (i + 2) % 4) for i in range(4)])  2.85 us
  transfers between devices with their start and end apart: 19, of which 9 were waited for; matrix products, arithmetic and copies ran while one was open for 0% of the time, Pallas kernels for 14%

profile of v21, /device:TPU:0, one launch (start us, length us, event | category | flops | bytes accessed | tf_op | source)
XLA Modules:
  0.0 69.5 jit_solution(761021590456523521)
XLA Ops:
  0.6 3.0 %collective-permute-start = (s32[8,32,128]{2,1,0:T(8,128)}, s32[8,32,128]{2,1,0:T(8,128)S(1)}, u32[]{:S(2)}, u32[]{:S(2)}) collective-permute-start(s32[8,32,128]{2,1,0:T(8,128)} %refs_1_.3), channel_id=1, source_target_pairs={{0,4},{4,0},{1,5},{5,1},{2,6},{6,2},{3,7},{7,3},{8,12},{12,8},{9,1... | collective-permute-start | bytes 393224 | tf_op jit(solution)/shard_map/ppermute | solution.py:751
  3.6 1.9 %shard_map.122 = (f32[4,32,128]{2,1,0:T(8,128)}, f32[20,32,128]{2,1,0:T(8,128)}) custom-call(f32[4,8,32,128]{3,2,1,0:T(8,128)} %refs_0_.2, f32[8,32,32]{2,1,0:T(8,128)} %vk.5, f32[8,32,32]{2,1,0:T(8,128)} %va.5), custom_call_target="tpu_custom_call" | custom-call | tf_op jit(solution)/shard_map/pallas_call | solution.py:721
  5.6 4.1 %collective-permute-start.4 = (f32[4,32,128]{2,1,0:T(8,128)}, f32[4,32,128]{2,1,0:T(8,128)S(1)}, u32[]{:S(2)}, u32[]{:S(2)}) collective-permute-start(f32[4,32,128]{2,1,0:T(8,128)} %get-tuple-element.31), channel_id=1, source_target_pairs={{0,24},{8,16},{16,8},{24,0},{1,25},{9,17},{17,9},{25,1},{2,26},{10... | collective-permute-start | bytes 196616 | tf_op jit(solution)/shard_map/ppermute | solution.py:757
  11.0 2.1 %shard_map.121 = (f32[16,72,128]{2,1,0:T(8,128)S(1)}, f32[1,128]{1,0:T(1,128)S(1)}) custom-call(s32[1,1024]{1,0:T(1,128)S(1)} %bitcast.3, f32[1]{0:T(128)S(6)} %copy.13.refs_1_, s32[8,32,128]{2,1,0:T(8,128)S(1)} %collective-permute-done.refs_2_.refs_3_), custom_call_target="tpu_custom_call" | custom-call | flops 301989888 | bytes 589824 | tf_op jit(solution)/shard_map/pallas_call | solution.py:721
  13.1 2.1 %collective-permute-done.3.refs_1_ = f32[4,32,128]{2,1,0:T(8,128)S(1)} collective-permute-done((f32[4,32,128]{2,1,0:T(8,128)}, f32[4,32,128]{2,1,0:T(8,128)S(1)}, u32[]{:S(2)}, u32[]{:S(2)}) %collective-permute-start.3) | collective-permute-done | bytes 65568 | tf_op jit(solution)/shard_map/ppermute | solution.py:757
  15.2 1.6 %collective-permute-start.6 = (f32[12,32,128]{2,1,0:T(8,128)S(1)}, f32[12,32,128]{2,1,0:T(8,128)S(1)}, u32[]{:S(2)}, u32[]{:S(2)}) collective-permute-start(f32[12,32,128]{2,1,0:T(8,128)S(1)} %shard_map.123.refs_4_.joined), channel_id=1, source_target_pairs={{0,4},{4,0},{1,5},{5,1},{2,6},{6,2},{3,7},{7,3},{8,12},{12,8},{9,1... | collective-permute-start | bytes 589832 | tf_op jit(solution)/shard_map/ppermute | solution.py:751
  17.9 3.1 %collective-permute-done.6.refs_2_ = f32[12,32,128]{2,1,0:T(8,128)S(1)} collective-permute-done((f32[12,32,128]{2,1,0:T(8,128)S(1)}, f32[12,32,128]{2,1,0:T(8,128)S(1)}, u32[]{:S(2)}, u32[]{:S(2)}) %collective-permute-start.6) | collective-permute-done | bytes 196640 | tf_op jit(solution)/shard_map/ppermute | solution.py:751
  21.5 1.6 %collective-permute-start.7 = (f32[2,4,24,128]{3,2,1,0:T(8,128)S(1)}, f32[2,4,24,128]{3,2,1,0:T(8,128)S(1)}, u32[]{:S(2)}, u32[]{:S(2)}) collective-permute-start(f32[2,4,24,128]{3,2,1,0:T(8,128)S(1)} %shard_map.127.refs_2_), channel_id=1, source_target_pairs={{0,2},{1,3},{2,0},{3,1},{4,6},{5,7},{6,4},{7,5},{8,10},{9,11},{10,... | collective-permute-start | bytes 294920 | tf_op jit(solution)/shard_map/ppermute | solution.py:778
  23.4 1.6 %collective-permute-start.9 = (f32[2,4,24,128]{3,2,1,0:T(8,128)S(1)}, f32[2,4,24,128]{3,2,1,0:T(8,128)S(1)}, u32[]{:S(2)}, u32[]{:S(2)}) collective-permute-start(f32[2,4,24,128]{3,2,1,0:T(8,128)S(1)} %shard_map.128.refs_6_), channel_id=1, source_target_pairs={{0,2},{1,3},{2,0},{3,1},{4,6},{5,7},{6,4},{7,5},{8,10},{9,11},{10,... | collective-permute-start | bytes 294920 | tf_op jit(solution)/shard_map/ppermute | solution.py:778
  25.0 2.3 %shard_map.129 = (f32[18,72,128]{2,1,0:T(8,128)S(1)}, f32[16,72,128]{2,1,0:T(8,128)S(1)}, f32[17,72,128]{2,1,0:T(8,128)S(1)}, f32[16,72,128]{2,1,0:T(8,128)S(1)}...) custom-call(f32[16]{0:T(128)S(1)} %copy-done.6, f32[16]{0:T(128)S(1)} %copy-done.7, ...), custom_call_target="tpu_custom_call" | custom-call | flops 1000000000 | bytes 67108864 | tf_op jit(solution)/shard_map/pallas_call | solution.py:721
  27.3 0.8 %shard_map.130 = (f32[16,72,128]{2,1,0:T(8,128)S(1)}, f32[17,72,128]{2,1,0:T(8,128)S(1)}, f32[16,72,128]{2,1,0:T(8,128)S(1)}, f32[16,72,128]{2,1,0:T(8,128)S(1)}) custom-call(f32[16]{0:T(128)S(1)} %copy-done.6, f32[16]{0:T(128)S(1)} %copy-done.7, f32[2,4,24,128]{3,2,1,0:T(8,128)S(1)} %collective-permute-done.7.edge.refs_2_, ...), custom_call_target="tpu_custom_call" | custom-call | tf_op jit(solution)/shard_map/pallas_call | solution.py:721
  28.9 3.8 %shard_map.132 = (f32[16,72,128]{2,1,0:T(8,128)S(1)}, f32[104,128]{1,0:T(8,128)S(1)}) custom-call(f32[18,72,128]{2,1,0:T(8,128)S(1)} %get-tuple-element.41.phi, f32[16,72,128]{2,1,0:T(8,128)S(1)} %get-tuple-element.42.phi_y, f32[16,72,128]{2,1,0:T(8,128)S(1)} %get-tuple-element.43.phi_z, f32[16,72,128]{2,1,0:T(8,128)S(1)} %get-tuple-element.44.diag, ...), custom_call_target="tpu_custom_call" | custom-call | tf_op jit(solution)/shard_map/pallas_call | solution.py:721
  32.7 1.6 %collective-permute-start.10 = (f32[104,128]{1,0:T(8,128)S(1)}, f32[104,128]{1,0:T(8,128)S(1)}, u32[]{:S(2)}, u32[]{:S(2)}) collective-permute-start(f32[104,128]{1,0:T(8,128)S(1)} %get-tuple-element.49.sent), channel_id=1, source_target_pairs={{0,2},{1,3},{2,0},{3,1},{4,6},{5,7},{6,4},{7,5},{8,10},{9,11},{10,... | collective-permute-start | bytes 159752 | tf_op jit(solution)/shard_map/ppermute | solution.py:778
  34.3 2.6 %collective-permute-done.10.came = f32[104,128]{1,0:T(8,128)S(1)} collective-permute-done((f32[104,128]{1,0:T(8,128)S(1)}, f32[104,128]{1,0:T(8,128)S(1)}, u32[]{:S(2)}, u32[]{:S(2)}) %collective-permute-start.10) | collective-permute-done | bytes 53280 | tf_op jit(solution)/shard_map/ppermute | solution.py:778
  36.9 3.8 %shard_map.133 = (f32[2,16,32,128]{3,2,1,0:T(8,128)S(1)}, f32[2,16,32,128]{3,2,1,0:T(8,128)S(1)}) custom-call(f32[18,72,128]{2,1,0:T(8,128)S(1)} %get-tuple-element.41.phi, f32[16,72,128]{2,1,0:T(8,128)S(1)} %get-tuple-element.42.phi_y, f32[16,72,128]{2,1,0:T(8,128)S(1)} %get-tuple-element.43.phi_z, f32[16,72,128]{2,1,0:T(8,128)S(1)} %get-tuple-element.48.change, ...), custom_call_target="tpu_custom_call" | custom-call | tf_op jit(solution)/shard_map/pallas_call | solution.py:721
  40.8 1.9 %collective-permute-done.11.came.refs_1_ = f32[2,16,32,128]{3,2,1,0:T(8,128)S(1)} collective-permute-done((f32[2,16,32,128]{3,2,1,0:T(8,128)S(1)}, f32[2,16,32,128]{3,2,1,0:T(8,128)S(1)}, u32[]{:S(2)}, u32[]{:S(2)}) %collective-permute-start.11) | collective-permute-done | bytes 524320 | tf_op jit(solution)/shard_map/ppermute | solution.py:754
  43.0 1.6 %collective-permute-start.12 = (f32[1,2,2,32,128]{4,3,2,1,0:T(8,128)S(1)}, f32[1,2,2,32,128]{4,3,2,1,0:T(8,128)S(1)}, u32[]{:S(2)}, u32[]{:S(2)}) collective-permute-start(f32[1,2,2,32,128]{4,3,2,1,0:T(8,128)S(1)} %shard_map.135.refs_2_), channel_id=1, source_target_pairs={{0,4},{4,0},{1,5},{5,1},{2,6},{6,2},{3,7},{7,3},{8,12},{12,8},{9,1... | collective-permute-start | bytes 196616 | tf_op jit(solution)/shard_map/ppermute | solution.py:751
  45.3 1.6 %collective-permute-start.17 = (f32[1,2,2,32,128]{4,3,2,1,0:T(8,128)S(1)}, f32[1,2,2,32,128]{4,3,2,1,0:T(8,128)S(1)}, u32[]{:S(2)}, u32[]{:S(2)}) collective-permute-start(f32[1,2,2,32,128]{4,3,2,1,0:T(8,128)S(1)} %shard_map.136.refs_2_), channel_id=1, source_target_pairs={{0,4},{4,0},{1,5},{5,1},{2,6},{6,2},{3,7},{7,3},{8,12},{12,8},{9,1... | collective-permute-start | bytes 196616 | tf_op jit(solution)/shard_map/ppermute | solution.py:751
  47.9 2.0 %collective-permute-start.13 = (f32[2,2,32,128]{3,2,1,0:T(8,128)S(1)}, f32[2,2,32,128]{3,2,1,0:T(8,128)S(1)}, u32[]{:S(2)}, u32[]{:S(2)}) collective-permute-start(f32[2,2,32,128]{3,2,1,0:T(8,128)S(1)} %shard_map.139), channel_id=1, source_target_pairs={{0,16},{8,24},{16,0},{24,8},{1,17},{9,25},{17,1},{25,9},{2,18},{10... | collective-permute-start | bytes 196616 | tf_op jit(solution)/shard_map/ppermute | solution.py:757
  49.9 2.1 %collective-permute-start.15 = (f32[2,2,32,128]{3,2,1,0:T(8,128)S(1)}, f32[2,2,32,128]{3,2,1,0:T(8,128)S(1)}, u32[]{:S(2)}, u32[]{:S(2)}) collective-permute-start(f32[2,2,32,128]{3,2,1,0:T(8,128)S(1)} %shard_map.140), channel_id=1, source_target_pairs={{0,24},{8,16},{16,8},{24,0},{1,25},{9,17},{17,9},{25,1},{2,26},{10... | collective-permute-start | bytes 196616 | tf_op jit(solution)/shard_map/ppermute | solution.py:757
  52.2 2.5 %collective-permute-done.13.refs_0_ = f32[2,2,32,128]{3,2,1,0:T(8,128)S(1)} collective-permute-done((f32[2,2,32,128]{3,2,1,0:T(8,128)S(1)}, f32[2,2,32,128]{3,2,1,0:T(8,128)S(1)}, u32[]{:S(2)}, u32[]{:S(2)}) %collective-permute-start.13) | collective-permute-done | bytes 65568 | tf_op jit(solution)/shard_map/ppermute | solution.py:757
  54.7 1.4 %collective-permute-done.15.refs_1_ = f32[2,2,32,128]{3,2,1,0:T(8,128)S(1)} collective-permute-done((f32[2,2,32,128]{3,2,1,0:T(8,128)S(1)}, f32[2,2,32,128]{3,2,1,0:T(8,128)S(1)}, u32[]{:S(2)}, u32[]{:S(2)}) %collective-permute-start.15) | collective-permute-done | bytes 65568 | tf_op jit(solution)/shard_map/ppermute | solution.py:757
  57.3 11.2 %all_to_all.5.tiles = f32[32,1,128]{2,1,0:T(1,128)S(1)} all-to-all(f32[32,1,128]{2,1,0:T(1,128)S(1)} %broadcast_in_dim.3), channel_id=1, replica_groups=mesh['src'=4,'gx'=2,'gy'=4] {'src','gx','gy'}, dimensions={0} | all-to-all | bytes 32768 | tf_op jit(solution)/shard_map/all_to_all | solution.py:841
  68.5 1.0 %shard_map.145 = (f32[8,32,32]{2,1,0:T(8,128)}, f32[8,32,32]{2,1,0:T(8,128)}, f32[2]{0:T(128)}) custom-call(f32[32,1,128]{2,1,0:T(1,128)S(1)} %all_to_all.5.tiles, f32[8,32,32]{2,1,0:T(8,128)S(1)} %get-tuple-element.53.w_k, f32[8,32,32]{2,1,0:T(8,128)S(1)} %get-tuple-element.54.w_a, f32[8,32,32]{2,1,0:T(8,128)S(1)} %copy-done.1, f32[8,32,32]{2,1,0:T(8,128)S(1)} %copy-done.2), custom_call_target="tpu_custom_call" | custom-call | tf_op jit(solution)/shard_map/pallas_call | solution.py:721
  (59 shorter events, 6.6 us)
Async XLA Ops:
  0.6 10.3 %collective-permute-start = (s32[8,32,128]{2,1,0:T(8,128)}, s32[8,32,128]{2,1,0:T(8,128)S(1)}, u32[]{:S(2)}, u32[]{:S(2)}) collective-permute-start(s32[8,32,128]{2,1,0:T(8,128)} %refs_1_.3), channel_id=1, source_target_pairs={{0,4},{4,0},{1,5},{5,1},{2,6},{6,2},{3,7},{7,3},{8,12},{12,8},{9,1... | collective-permute-start | bytes 393224 | tf_op jit(solution)/shard_map/ppermute | solution.py:751
  5.5 5.4 %copy-start.8 = (s32[1024]{0:T(1024)S(1)}, s32[1024]{0:T(1024)}, u32[]{:S(2)}) copy-start(s32[1024]{0:T(1024)} %param.14) | copy-start | bytes 12292
  5.5 11.3 %collective-permute-start.1 = (f32[20,32,128]{2,1,0:T(8,128)}, f32[20,32,128]{2,1,0:T(8,128)S(1)}, u32[]{:S(2)}, u32[]{:S(2)}) collective-permute-start(f32[20,32,128]{2,1,0:T(8,128)} %get-tuple-element.30), channel_id=1, source_target_pairs={{0,4},{4,0},{1,5},{5,1},{2,6},{6,2},{3,7},{7,3},{8,12},{12,8},{9,1... | collective-permute-start | bytes 983048 | tf_op jit(solution)/shard_map/ppermute | solution.py:751
  5.6 7.5 %collective-permute-start.4 = (f32[4,32,128]{2,1,0:T(8,128)}, f32[4,32,128]{2,1,0:T(8,128)S(1)}, u32[]{:S(2)}, u32[]{:S(2)}) collective-permute-start(f32[4,32,128]{2,1,0:T(8,128)} %get-tuple-element.31), channel_id=1, source_target_pairs={{0,24},{8,16},{16,8},{24,0},{1,25},{9,17},{17,9},{25,1},{2,26},{10... | collective-permute-start | bytes 196616 | tf_op jit(solution)/shard_map/ppermute | solution.py:757
  9.7 5.5 %collective-permute-start.3 = (f32[4,32,128]{2,1,0:T(8,128)}, f32[4,32,128]{2,1,0:T(8,128)S(1)}, u32[]{:S(2)}, u32[]{:S(2)}) collective-permute-start(f32[4,32,128]{2,1,0:T(8,128)} %get-tuple-element.31), channel_id=1, source_target_pairs={{0,16},{8,24},{16,0},{24,8},{1,17},{9,25},{17,1},{25,9},{2,18},{10... | collective-permute-start | bytes 196616 | tf_op jit(solution)/shard_map/ppermute | solution.py:757
  9.7 5.5 %collective-permute-start.2 = (f32[4,32,128]{2,1,0:T(8,128)}, f32[4,32,128]{2,1,0:T(8,128)S(1)}, u32[]{:S(2)}, u32[]{:S(2)}) collective-permute-start(f32[4,32,128]{2,1,0:T(8,128)} %get-tuple-element.31), channel_id=1, source_target_pairs={{0,8},{8,0},{16,24},{24,16},{1,9},{9,1},{17,25},{25,17},{2,10},{10... | collective-permute-start | bytes 196616 | tf_op jit(solution)/shard_map/ppermute | solution.py:757
  13.1 3.7 %copy-start = (f32[4,8,32,128]{3,2,1,0:T(8,128)S(1)}, f32[4,8,32,128]{3,2,1,0:T(8,128)}, u32[]{:S(2)}) copy-start(f32[4,8,32,128]{3,2,1,0:T(8,128)} %refs_0_.2) | copy-start | bytes 1572868
  15.2 5.8 %collective-permute-start.6 = (f32[12,32,128]{2,1,0:T(8,128)S(1)}, f32[12,32,128]{2,1,0:T(8,128)S(1)}, u32[]{:S(2)}, u32[]{:S(2)}) collective-permute-start(f32[12,32,128]{2,1,0:T(8,128)S(1)} %shard_map.123.refs_4_.joined), channel_id=1, source_target_pairs={{0,4},{4,0},{1,5},{5,1},{2,6},{6,2},{3,7},{7,3},{8,12},{12,8},{9,1... | collective-permute-start | bytes 589832 | tf_op jit(solution)/shard_map/ppermute | solution.py:751
  17.4 4.0 %collective-permute-start.5 = (f32[2,16,32,128]{3,2,1,0:T(8,128)S(1)}, f32[2,16,32,128]{3,2,1,0:T(8,128)S(1)}, u32[]{:S(2)}, u32[]{:S(2)}) collective-permute-start(f32[2,16,32,128]{3,2,1,0:T(8,128)S(1)} %get-tuple-element.34.refs_1_.refs_3_), channel_id=1, source_target_pairs={{0,1},{1,0},{2,3},{3,2},{4,5},{5,4},{6,7},{7,6},{8,9},{9,8},{10,11... | collective-permute-start | bytes 1572872 | tf_op jit(solution)/shard_map/ppermute | solution.py:754
  21.4 2.0 %collective-permute-start.8 = (f32[2,16,32,128]{3,2,1,0:T(8,128)S(1)}, f32[2,16,32,128]{3,2,1,0:T(8,128)S(1)}, u32[]{:S(2)}, u32[]{:S(2)}) collective-permute-start(f32[2,16,32,128]{3,2,1,0:T(8,128)S(1)} %shard_map.126.refs_3_.refs_0_.vector), channel_id=1, source_target_pairs={{0,1},{1,0},{2,3},{3,2},{4,5},{5,4},{6,7},{7,6},{8,9},{9,8},{10,11... | collective-permute-start | bytes 1572872 | tf_op jit(solution)/shard_map/ppermute | solution.py:754
  21.5 3.5 %copy-start.6 = (f32[16]{0:T(128)S(1)}, f32[16]{0:T(128)}, u32[]{:S(2)}) copy-start(f32[16]{0:T(128)} %kap_table.1) | copy-start | bytes 196
  21.5 5.8 %collective-permute-start.7 = (f32[2,4,24,128]{3,2,1,0:T(8,128)S(1)}, f32[2,4,24,128]{3,2,1,0:T(8,128)S(1)}, u32[]{:S(2)}, u32[]{:S(2)}) collective-permute-start(f32[2,4,24,128]{3,2,1,0:T(8,128)S(1)} %shard_map.127.refs_2_), channel_id=1, source_target_pairs={{0,2},{1,3},{2,0},{3,1},{4,6},{5,7},{6,4},{7,5},{8,10},{9,11},{10,... | collective-permute-start | bytes 294920 | tf_op jit(solution)/shard_map/ppermute | solution.py:778
  23.4 5.5 %collective-permute-start.9 = (f32[2,4,24,128]{3,2,1,0:T(8,128)S(1)}, f32[2,4,24,128]{3,2,1,0:T(8,128)S(1)}, u32[]{:S(2)}, u32[]{:S(2)}) collective-permute-start(f32[2,4,24,128]{3,2,1,0:T(8,128)S(1)} %shard_map.128.refs_6_), channel_id=1, source_target_pairs={{0,2},{1,3},{2,0},{3,1},{4,6},{5,7},{6,4},{7,5},{8,10},{9,11},{10,... | collective-permute-start | bytes 294920 | tf_op jit(solution)/shard_map/ppermute | solution.py:778
  32.7 4.2 %collective-permute-start.10 = (f32[104,128]{1,0:T(8,128)S(1)}, f32[104,128]{1,0:T(8,128)S(1)}, u32[]{:S(2)}, u32[]{:S(2)}) collective-permute-start(f32[104,128]{1,0:T(8,128)S(1)} %get-tuple-element.49.sent), channel_id=1, source_target_pairs={{0,2},{1,3},{2,0},{3,1},{4,6},{5,7},{6,4},{7,5},{8,10},{9,11},{10,... | collective-permute-start | bytes 159752 | tf_op jit(solution)/shard_map/ppermute | solution.py:778
  40.7 2.0 %collective-permute-start.11 = (f32[2,16,32,128]{3,2,1,0:T(8,128)S(1)}, f32[2,16,32,128]{3,2,1,0:T(8,128)S(1)}, u32[]{:S(2)}, u32[]{:S(2)}) collective-permute-start(f32[2,16,32,128]{3,2,1,0:T(8,128)S(1)} %get-tuple-element.51), channel_id=1, source_target_pairs={{0,1},{1,0},{2,3},{3,2},{4,5},{5,4},{6,7},{7,6},{8,9},{9,8},{10,11... | collective-permute-start | bytes 1572872 | tf_op jit(solution)/shard_map/ppermute | solution.py:754
  43.0 4.9 %collective-permute-start.12 = (f32[1,2,2,32,128]{4,3,2,1,0:T(8,128)S(1)}, f32[1,2,2,32,128]{4,3,2,1,0:T(8,128)S(1)}, u32[]{:S(2)}, u32[]{:S(2)}) collective-permute-start(f32[1,2,2,32,128]{4,3,2,1,0:T(8,128)S(1)} %shard_map.135.refs_2_), channel_id=1, source_target_pairs={{0,4},{4,0},{1,5},{5,1},{2,6},{6,2},{3,7},{7,3},{8,12},{12,8},{9,1... | collective-permute-start | bytes 196616 | tf_op jit(solution)/shard_map/ppermute | solution.py:751
  44.6 5.3 %collective-permute-start.14 = (f32[1,2,2,32,128]{4,3,2,1,0:T(8,128)S(1)}, f32[1,2,2,32,128]{4,3,2,1,0:T(8,128)S(1)}, u32[]{:S(2)}, u32[]{:S(2)}) collective-permute-start(f32[1,2,2,32,128]{4,3,2,1,0:T(8,128)S(1)} %shard_map.134.refs_2_), channel_id=1, source_target_pairs={{0,4},{4,0},{1,5},{5,1},{2,6},{6,2},{3,7},{7,3},{8,12},{12,8},{9,1... | collective-permute-start | bytes 196616 | tf_op jit(solution)/shard_map/ppermute | solution.py:751
  45.3 6.8 %collective-permute-start.17 = (f32[1,2,2,32,128]{4,3,2,1,0:T(8,128)S(1)}, f32[1,2,2,32,128]{4,3,2,1,0:T(8,128)S(1)}, u32[]{:S(2)}, u32[]{:S(2)}) collective-permute-start(f32[1,2,2,32,128]{4,3,2,1,0:T(8,128)S(1)} %shard_map.136.refs_2_), channel_id=1, source_target_pairs={{0,4},{4,0},{1,5},{5,1},{2,6},{6,2},{3,7},{7,3},{8,12},{12,8},{9,1... | collective-permute-start | bytes 196616 | tf_op jit(solution)/shard_map/ppermute | solution.py:751
  47.0 5.2 %collective-permute-start.16 = (f32[1,2,2,32,128]{4,3,2,1,0:T(8,128)S(1)}, f32[1,2,2,32,128]{4,3,2,1,0:T(8,128)S(1)}, u32[]{:S(2)}, u32[]{:S(2)}) collective-permute-start(f32[1,2,2,32,128]{4,3,2,1,0:T(8,128)S(1)} %shard_map.137.refs_2_), channel_id=1, source_target_pairs={{0,4},{4,0},{1,5},{5,1},{2,6},{6,2},{3,7},{7,3},{8,12},{12,8},{9,1... | collective-permute-start | bytes 196616 | tf_op jit(solution)/shard_map/ppermute | solution.py:751
  47.9 6.8 %collective-permute-start.13 = (f32[2,2,32,128]{3,2,1,0:T(8,128)S(1)}, f32[2,2,32,128]{3,2,1,0:T(8,128)S(1)}, u32[]{:S(2)}, u32[]{:S(2)}) collective-permute-start(f32[2,2,32,128]{3,2,1,0:T(8,128)S(1)} %shard_map.139), channel_id=1, source_target_pairs={{0,16},{8,24},{16,0},{24,8},{1,17},{9,25},{17,1},{25,9},{2,18},{10... | collective-permute-start | bytes 196616 | tf_op jit(solution)/shard_map/ppermute | solution.py:757
  49.9 6.3 %collective-permute-start.15 = (f32[2,2,32,128]{3,2,1,0:T(8,128)S(1)}, f32[2,2,32,128]{3,2,1,0:T(8,128)S(1)}, u32[]{:S(2)}, u32[]{:S(2)}) collective-permute-start(f32[2,2,32,128]{3,2,1,0:T(8,128)S(1)} %shard_map.140), channel_id=1, source_target_pairs={{0,24},{8,16},{16,8},{24,0},{1,25},{9,17},{17,9},{25,1},{2,26},{10... | collective-permute-start | bytes 196616 | tf_op jit(solution)/shard_map/ppermute | solution.py:757
  52.1 4.8 %collective-permute-start.18 = (f32[2,2,32,128]{3,2,1,0:T(8,128)S(1)}, f32[2,2,32,128]{3,2,1,0:T(8,128)S(1)}, u32[]{:S(2)}, u32[]{:S(2)}) collective-permute-start(f32[2,2,32,128]{3,2,1,0:T(8,128)S(1)} %shard_map.143), channel_id=1, source_target_pairs={{0,8},{8,0},{16,24},{24,16},{1,9},{9,1},{17,25},{25,17},{2,10},{10... | collective-permute-start | bytes 196616 | tf_op jit(solution)/shard_map/ppermute | solution.py:757
  52.2 4.6 %copy-start.4 = (f32[8,32,32]{2,1,0:T(8,128)S(1)}, f32[8,32,32]{2,1,0:T(8,128)}, u32[]{:S(2)}) copy-start(f32[8,32,32]{2,1,0:T(8,128)} %refs_6_.1) | copy-start | bytes 98308
  52.2 4.6 %copy-start.5 = (f32[8,32,32]{2,1,0:T(8,128)S(1)}, f32[8,32,32]{2,1,0:T(8,128)}, u32[]{:S(2)}) copy-start(f32[8,32,32]{2,1,0:T(8,128)} %refs_7_.1) | copy-start | bytes 98308
  (4 other events, 9.6 us)

commit v22 on v21

--- a/solution.py
+++ b/solution.py
@@ -837,7 +837,7 @@
         (f32(*v_kappa.shape), f32(*v_kappa.shape), f32(1, 128)),
         beta_row, *parts, v_kappa, v_absorb, q_kappa, q_absorb,
     )
-    everyone = ("src", "gx", "gy")
+    everyone = ("gy", "gx", "src")
     tiles = lax.all_to_all(jnp.broadcast_to(tile, (8 * n, 1, 128)), everyone, 0, 0)
     return tuple(run(
         functools.partial(final_kernel, cells=cells),

time: 69.7 us -> 69.6 us (level)
  no operation moved by 1% of the time
where the time goes in v22:
time: 69.6 us; the launch traced here: 69.5 us
  starting transfers between devices  22.8 us (33%)
  Pallas kernels  19.1 us (27%)
  waiting for transfers between devices  14.7 us (21%)
  blocking collectives  11.1 us (16%)
  between operations  1.61 us (2%)
    pallas_call x25, Pallas kernels, run(): pl.pallas_call(body if waits else kernel, out_shape=tuple(outs), in_specs...  19.1 us
    all_to_all x1, blocking collectives, per_device_paired(): lax.all_to_all(jnp.broadcast_to(tile, (8 * n, 1, 128)), everyone, 0, 0)  11.1 us
    ppermute x6, starting transfers between devices, along_z(): return lax.ppermute(value, 'src', [(i, i ^ k) for i in range(n)])  8.91 us
    ppermute x7, starting transfers between devices, swap_x(): return lax.ppermute(value, 'gx', [(0, 1), (1, 0)])  8.89 us
    ppermute x6, waiting for transfers between devices, along_z(): return lax.ppermute(value, 'src', [(i, i ^ k) for i in range(n)])  6.67 us
    ppermute x3, starting transfers between devices, across_y(): return lax.ppermute(value, 'gy', [(i, (i + 2) % 4) for i in range(4)])  4.75 us
    ppermute x7, waiting for transfers between devices, swap_x(): return lax.ppermute(value, 'gx', [(0, 1), (1, 0)])  3.11 us
    ppermute x3, waiting for transfers between devices, across_y(): return lax.ppermute(value, 'gy', [(i, (i + 2) % 4) for i in range(4)])  2.85 us
  transfers between devices with their start and end apart: 19, of which 9 were waited for; matrix products, arithmetic and copies ran while one was open for 0% of the time, Pallas kernels for 14%

profile of v22, /device:TPU:0, one launch (start us, length us, event | category | flops | bytes accessed | tf_op | source)
XLA Modules:
  0.0 69.5 jit_solution(10214605329342180972)
XLA Ops:
  0.6 3.0 %collective-permute-start = (s32[8,32,128]{2,1,0:T(8,128)}, s32[8,32,128]{2,1,0:T(8,128)S(1)}, u32[]{:S(2)}, u32[]{:S(2)}) collective-permute-start(s32[8,32,128]{2,1,0:T(8,128)} %refs_1_.3), channel_id=1, source_target_pairs={{0,4},{4,0},{1,5},{5,1},{2,6},{6,2},{3,7},{7,3},{8,12},{12,8},{9,1... | collective-permute-start | bytes 393224 | tf_op jit(solution)/shard_map/ppermute | solution.py:751
  3.6 1.9 %shard_map.122 = (f32[4,32,128]{2,1,0:T(8,128)}, f32[20,32,128]{2,1,0:T(8,128)}) custom-call(f32[4,8,32,128]{3,2,1,0:T(8,128)} %refs_0_.2, f32[8,32,32]{2,1,0:T(8,128)} %vk.5, f32[8,32,32]{2,1,0:T(8,128)} %va.5), custom_call_target="tpu_custom_call" | custom-call | tf_op jit(solution)/shard_map/pallas_call | solution.py:721
  5.6 4.1 %collective-permute-start.4 = (f32[4,32,128]{2,1,0:T(8,128)}, f32[4,32,128]{2,1,0:T(8,128)S(1)}, u32[]{:S(2)}, u32[]{:S(2)}) collective-permute-start(f32[4,32,128]{2,1,0:T(8,128)} %get-tuple-element.31), channel_id=1, source_target_pairs={{0,24},{8,16},{16,8},{24,0},{1,25},{9,17},{17,9},{25,1},{2,26},{10... | collective-permute-start | bytes 196616 | tf_op jit(solution)/shard_map/ppermute | solution.py:757
  11.0 2.1 %shard_map.121 = (f32[16,72,128]{2,1,0:T(8,128)S(1)}, f32[1,128]{1,0:T(1,128)S(1)}) custom-call(s32[1,1024]{1,0:T(1,128)S(1)} %bitcast.3, f32[1]{0:T(128)S(6)} %copy.13.refs_1_, s32[8,32,128]{2,1,0:T(8,128)S(1)} %collective-permute-done.refs_2_.refs_3_), custom_call_target="tpu_custom_call" | custom-call | flops 301989888 | bytes 589824 | tf_op jit(solution)/shard_map/pallas_call | solution.py:721
  13.1 2.1 %collective-permute-done.3.refs_1_ = f32[4,32,128]{2,1,0:T(8,128)S(1)} collective-permute-done((f32[4,32,128]{2,1,0:T(8,128)}, f32[4,32,128]{2,1,0:T(8,128)S(1)}, u32[]{:S(2)}, u32[]{:S(2)}) %collective-permute-start.3) | collective-permute-done | bytes 65568 | tf_op jit(solution)/shard_map/ppermute | solution.py:757
  15.2 1.6 %collective-permute-start.6 = (f32[12,32,128]{2,1,0:T(8,128)S(1)}, f32[12,32,128]{2,1,0:T(8,128)S(1)}, u32[]{:S(2)}, u32[]{:S(2)}) collective-permute-start(f32[12,32,128]{2,1,0:T(8,128)S(1)} %shard_map.123.refs_4_.joined), channel_id=1, source_target_pairs={{0,4},{4,0},{1,5},{5,1},{2,6},{6,2},{3,7},{7,3},{8,12},{12,8},{9,1... | collective-permute-start | bytes 589832 | tf_op jit(solution)/shard_map/ppermute | solution.py:751
  17.9 3.1 %collective-permute-done.6.refs_2_ = f32[12,32,128]{2,1,0:T(8,128)S(1)} collective-permute-done((f32[12,32,128]{2,1,0:T(8,128)S(1)}, f32[12,32,128]{2,1,0:T(8,128)S(1)}, u32[]{:S(2)}, u32[]{:S(2)}) %collective-permute-start.6) | collective-permute-done | bytes 196640 | tf_op jit(solution)/shard_map/ppermute | solution.py:751
  21.5 1.6 %collective-permute-start.7 = (f32[2,4,24,128]{3,2,1,0:T(8,128)S(1)}, f32[2,4,24,128]{3,2,1,0:T(8,128)S(1)}, u32[]{:S(2)}, u32[]{:S(2)}) collective-permute-start(f32[2,4,24,128]{3,2,1,0:T(8,128)S(1)} %shard_map.127.refs_2_), channel_id=1, source_target_pairs={{0,2},{1,3},{2,0},{3,1},{4,6},{5,7},{6,4},{7,5},{8,10},{9,11},{10,... | collective-permute-start | bytes 294920 | tf_op jit(solution)/shard_map/ppermute | solution.py:778
  23.4 1.6 %collective-permute-start.9 = (f32[2,4,24,128]{3,2,1,0:T(8,128)S(1)}, f32[2,4,24,128]{3,2,1,0:T(8,128)S(1)}, u32[]{:S(2)}, u32[]{:S(2)}) collective-permute-start(f32[2,4,24,128]{3,2,1,0:T(8,128)S(1)} %shard_map.128.refs_6_), channel_id=1, source_target_pairs={{0,2},{1,3},{2,0},{3,1},{4,6},{5,7},{6,4},{7,5},{8,10},{9,11},{10,... | collective-permute-start | bytes 294920 | tf_op jit(solution)/shard_map/ppermute | solution.py:778
  25.0 2.3 %shard_map.129 = (f32[18,72,128]{2,1,0:T(8,128)S(1)}, f32[16,72,128]{2,1,0:T(8,128)S(1)}, f32[17,72,128]{2,1,0:T(8,128)S(1)}, f32[16,72,128]{2,1,0:T(8,128)S(1)}...) custom-call(f32[16]{0:T(128)S(1)} %copy-done.6, f32[16]{0:T(128)S(1)} %copy-done.7, ...), custom_call_target="tpu_custom_call" | custom-call | flops 1000000000 | bytes 67108864 | tf_op jit(solution)/shard_map/pallas_call | solution.py:721
  27.3 0.8 %shard_map.130 = (f32[16,72,128]{2,1,0:T(8,128)S(1)}, f32[17,72,128]{2,1,0:T(8,128)S(1)}, f32[16,72,128]{2,1,0:T(8,128)S(1)}, f32[16,72,128]{2,1,0:T(8,128)S(1)}) custom-call(f32[16]{0:T(128)S(1)} %copy-done.6, f32[16]{0:T(128)S(1)} %copy-done.7, f32[2,4,24,128]{3,2,1,0:T(8,128)S(1)} %collective-permute-done.7.edge.refs_2_, ...), custom_call_target="tpu_custom_call" | custom-call | tf_op jit(solution)/shard_map/pallas_call | solution.py:721
  28.9 3.8 %shard_map.132 = (f32[16,72,128]{2,1,0:T(8,128)S(1)}, f32[104,128]{1,0:T(8,128)S(1)}) custom-call(f32[18,72,128]{2,1,0:T(8,128)S(1)} %get-tuple-element.41.phi, f32[16,72,128]{2,1,0:T(8,128)S(1)} %get-tuple-element.42.phi_y, f32[16,72,128]{2,1,0:T(8,128)S(1)} %get-tuple-element.43.phi_z, f32[16,72,128]{2,1,0:T(8,128)S(1)} %get-tuple-element.44.diag, ...), custom_call_target="tpu_custom_call" | custom-call | tf_op jit(solution)/shard_map/pallas_call | solution.py:721
  32.7 1.6 %collective-permute-start.10 = (f32[104,128]{1,0:T(8,128)S(1)}, f32[104,128]{1,0:T(8,128)S(1)}, u32[]{:S(2)}, u32[]{:S(2)}) collective-permute-start(f32[104,128]{1,0:T(8,128)S(1)} %get-tuple-element.49.sent), channel_id=1, source_target_pairs={{0,2},{1,3},{2,0},{3,1},{4,6},{5,7},{6,4},{7,5},{8,10},{9,11},{10,... | collective-permute-start | bytes 159752 | tf_op jit(solution)/shard_map/ppermute | solution.py:778
  34.3 2.6 %collective-permute-done.10.came = f32[104,128]{1,0:T(8,128)S(1)} collective-permute-done((f32[104,128]{1,0:T(8,128)S(1)}, f32[104,128]{1,0:T(8,128)S(1)}, u32[]{:S(2)}, u32[]{:S(2)}) %collective-permute-start.10) | collective-permute-done | bytes 53280 | tf_op jit(solution)/shard_map/ppermute | solution.py:778
  36.9 3.8 %shard_map.133 = (f32[2,16,32,128]{3,2,1,0:T(8,128)S(1)}, f32[2,16,32,128]{3,2,1,0:T(8,128)S(1)}) custom-call(f32[18,72,128]{2,1,0:T(8,128)S(1)} %get-tuple-element.41.phi, f32[16,72,128]{2,1,0:T(8,128)S(1)} %get-tuple-element.42.phi_y, f32[16,72,128]{2,1,0:T(8,128)S(1)} %get-tuple-element.43.phi_z, f32[16,72,128]{2,1,0:T(8,128)S(1)} %get-tuple-element.48.change, ...), custom_call_target="tpu_custom_call" | custom-call | tf_op jit(solution)/shard_map/pallas_call | solution.py:721
  40.8 1.9 %collective-permute-done.11.came.refs_1_ = f32[2,16,32,128]{3,2,1,0:T(8,128)S(1)} collective-permute-done((f32[2,16,32,128]{3,2,1,0:T(8,128)S(1)}, f32[2,16,32,128]{3,2,1,0:T(8,128)S(1)}, u32[]{:S(2)}, u32[]{:S(2)}) %collective-permute-start.11) | collective-permute-done | bytes 524320 | tf_op jit(solution)/shard_map/ppermute | solution.py:754
  43.0 1.6 %collective-permute-start.12 = (f32[1,2,2,32,128]{4,3,2,1,0:T(8,128)S(1)}, f32[1,2,2,32,128]{4,3,2,1,0:T(8,128)S(1)}, u32[]{:S(2)}, u32[]{:S(2)}) collective-permute-start(f32[1,2,2,32,128]{4,3,2,1,0:T(8,128)S(1)} %shard_map.135.refs_2_), channel_id=1, source_target_pairs={{0,4},{4,0},{1,5},{5,1},{2,6},{6,2},{3,7},{7,3},{8,12},{12,8},{9,1... | collective-permute-start | bytes 196616 | tf_op jit(solution)/shard_map/ppermute | solution.py:751
  45.3 1.6 %collective-permute-start.17 = (f32[1,2,2,32,128]{4,3,2,1,0:T(8,128)S(1)}, f32[1,2,2,32,128]{4,3,2,1,0:T(8,128)S(1)}, u32[]{:S(2)}, u32[]{:S(2)}) collective-permute-start(f32[1,2,2,32,128]{4,3,2,1,0:T(8,128)S(1)} %shard_map.136.refs_2_), channel_id=1, source_target_pairs={{0,4},{4,0},{1,5},{5,1},{2,6},{6,2},{3,7},{7,3},{8,12},{12,8},{9,1... | collective-permute-start | bytes 196616 | tf_op jit(solution)/shard_map/ppermute | solution.py:751
  47.9 2.0 %collective-permute-start.13 = (f32[2,2,32,128]{3,2,1,0:T(8,128)S(1)}, f32[2,2,32,128]{3,2,1,0:T(8,128)S(1)}, u32[]{:S(2)}, u32[]{:S(2)}) collective-permute-start(f32[2,2,32,128]{3,2,1,0:T(8,128)S(1)} %shard_map.139), channel_id=1, source_target_pairs={{0,16},{8,24},{16,0},{24,8},{1,17},{9,25},{17,1},{25,9},{2,18},{10... | collective-permute-start | bytes 196616 | tf_op jit(solution)/shard_map/ppermute | solution.py:757
  49.9 2.1 %collective-permute-start.15 = (f32[2,2,32,128]{3,2,1,0:T(8,128)S(1)}, f32[2,2,32,128]{3,2,1,0:T(8,128)S(1)}, u32[]{:S(2)}, u32[]{:S(2)}) collective-permute-start(f32[2,2,32,128]{3,2,1,0:T(8,128)S(1)} %shard_map.140), channel_id=1, source_target_pairs={{0,24},{8,16},{16,8},{24,0},{1,25},{9,17},{17,9},{25,1},{2,26},{10... | collective-permute-start | bytes 196616 | tf_op jit(solution)/shard_map/ppermute | solution.py:757
  52.2 2.5 %collective-permute-done.13.refs_0_ = f32[2,2,32,128]{3,2,1,0:T(8,128)S(1)} collective-permute-done((f32[2,2,32,128]{3,2,1,0:T(8,128)S(1)}, f32[2,2,32,128]{3,2,1,0:T(8,128)S(1)}, u32[]{:S(2)}, u32[]{:S(2)}) %collective-permute-start.13) | collective-permute-done | bytes 65568 | tf_op jit(solution)/shard_map/ppermute | solution.py:757
  54.7 1.4 %collective-permute-done.15.refs_1_ = f32[2,2,32,128]{3,2,1,0:T(8,128)S(1)} collective-permute-done((f32[2,2,32,128]{3,2,1,0:T(8,128)S(1)}, f32[2,2,32,128]{3,2,1,0:T(8,128)S(1)}, u32[]{:S(2)}, u32[]{:S(2)}) %collective-permute-start.15) | collective-permute-done | bytes 65568 | tf_op jit(solution)/shard_map/ppermute | solution.py:757
  57.3 11.1 %all_to_all.5.tiles = f32[32,1,128]{2,1,0:T(1,128)S(1)} all-to-all(f32[32,1,128]{2,1,0:T(1,128)S(1)} %broadcast_in_dim.3), channel_id=1, replica_groups=mesh['src'=4,'gx'=2,'gy'=4] {'gy','gx','src'}, dimensions={0} | all-to-all | bytes 32768 | tf_op jit(solution)/shard_map/all_to_all | solution.py:841
  68.5 1.0 %shard_map.145 = (f32[8,32,32]{2,1,0:T(8,128)}, f32[8,32,32]{2,1,0:T(8,128)}, f32[2]{0:T(128)}) custom-call(f32[32,1,128]{2,1,0:T(1,128)S(1)} %all_to_all.5.tiles, f32[8,32,32]{2,1,0:T(8,128)S(1)} %get-tuple-element.53.w_k, f32[8,32,32]{2,1,0:T(8,128)S(1)} %get-tuple-element.54.w_a, f32[8,32,32]{2,1,0:T(8,128)S(1)} %copy-done.1, f32[8,32,32]{2,1,0:T(8,128)S(1)} %copy-done.2), custom_call_target="tpu_custom_call" | custom-call | tf_op jit(solution)/shard_map/pallas_call | solution.py:721
  (59 shorter events, 6.6 us)
Async XLA Ops:
  0.6 10.3 %collective-permute-start = (s32[8,32,128]{2,1,0:T(8,128)}, s32[8,32,128]{2,1,0:T(8,128)S(1)}, u32[]{:S(2)}, u32[]{:S(2)}) collective-permute-start(s32[8,32,128]{2,1,0:T(8,128)} %refs_1_.3), channel_id=1, source_target_pairs={{0,4},{4,0},{1,5},{5,1},{2,6},{6,2},{3,7},{7,3},{8,12},{12,8},{9,1... | collective-permute-start | bytes 393224 | tf_op jit(solution)/shard_map/ppermute | solution.py:751
  5.5 5.4 %copy-start.8 = (s32[1024]{0:T(1024)S(1)}, s32[1024]{0:T(1024)}, u32[]{:S(2)}) copy-start(s32[1024]{0:T(1024)} %param.14) | copy-start | bytes 12292
  5.5 11.3 %collective-permute-start.1 = (f32[20,32,128]{2,1,0:T(8,128)}, f32[20,32,128]{2,1,0:T(8,128)S(1)}, u32[]{:S(2)}, u32[]{:S(2)}) collective-permute-start(f32[20,32,128]{2,1,0:T(8,128)} %get-tuple-element.30), channel_id=1, source_target_pairs={{0,4},{4,0},{1,5},{5,1},{2,6},{6,2},{3,7},{7,3},{8,12},{12,8},{9,1... | collective-permute-start | bytes 983048 | tf_op jit(solution)/shard_map/ppermute | solution.py:751
  5.6 7.5 %collective-permute-start.4 = (f32[4,32,128]{2,1,0:T(8,128)}, f32[4,32,128]{2,1,0:T(8,128)S(1)}, u32[]{:S(2)}, u32[]{:S(2)}) collective-permute-start(f32[4,32,128]{2,1,0:T(8,128)} %get-tuple-element.31), channel_id=1, source_target_pairs={{0,24},{8,16},{16,8},{24,0},{1,25},{9,17},{17,9},{25,1},{2,26},{10... | collective-permute-start | bytes 196616 | tf_op jit(solution)/shard_map/ppermute | solution.py:757
  9.7 5.5 %collective-permute-start.3 = (f32[4,32,128]{2,1,0:T(8,128)}, f32[4,32,128]{2,1,0:T(8,128)S(1)}, u32[]{:S(2)}, u32[]{:S(2)}) collective-permute-start(f32[4,32,128]{2,1,0:T(8,128)} %get-tuple-element.31), channel_id=1, source_target_pairs={{0,16},{8,24},{16,0},{24,8},{1,17},{9,25},{17,1},{25,9},{2,18},{10... | collective-permute-start | bytes 196616 | tf_op jit(solution)/shard_map/ppermute | solution.py:757
  9.7 5.5 %collective-permute-start.2 = (f32[4,32,128]{2,1,0:T(8,128)}, f32[4,32,128]{2,1,0:T(8,128)S(1)}, u32[]{:S(2)}, u32[]{:S(2)}) collective-permute-start(f32[4,32,128]{2,1,0:T(8,128)} %get-tuple-element.31), channel_id=1, source_target_pairs={{0,8},{8,0},{16,24},{24,16},{1,9},{9,1},{17,25},{25,17},{2,10},{10... | collective-permute-start | bytes 196616 | tf_op jit(solution)/shard_map/ppermute | solution.py:757
  13.1 3.7 %copy-start = (f32[4,8,32,128]{3,2,1,0:T(8,128)S(1)}, f32[4,8,32,128]{3,2,1,0:T(8,128)}, u32[]{:S(2)}) copy-start(f32[4,8,32,128]{3,2,1,0:T(8,128)} %refs_0_.2) | copy-start | bytes 1572868
  15.2 5.8 %collective-permute-start.6 = (f32[12,32,128]{2,1,0:T(8,128)S(1)}, f32[12,32,128]{2,1,0:T(8,128)S(1)}, u32[]{:S(2)}, u32[]{:S(2)}) collective-permute-start(f32[12,32,128]{2,1,0:T(8,128)S(1)} %shard_map.123.refs_4_.joined), channel_id=1, source_target_pairs={{0,4},{4,0},{1,5},{5,1},{2,6},{6,2},{3,7},{7,3},{8,12},{12,8},{9,1... | collective-permute-start | bytes 589832 | tf_op jit(solution)/shard_map/ppermute | solution.py:751
  17.4 4.0 %collective-permute-start.5 = (f32[2,16,32,128]{3,2,1,0:T(8,128)S(1)}, f32[2,16,32,128]{3,2,1,0:T(8,128)S(1)}, u32[]{:S(2)}, u32[]{:S(2)}) collective-permute-start(f32[2,16,32,128]{3,2,1,0:T(8,128)S(1)} %get-tuple-element.34.refs_1_.refs_3_), channel_id=1, source_target_pairs={{0,1},{1,0},{2,3},{3,2},{4,5},{5,4},{6,7},{7,6},{8,9},{9,8},{10,11... | collective-permute-start | bytes 1572872 | tf_op jit(solution)/shard_map/ppermute | solution.py:754
  21.4 2.0 %collective-permute-start.8 = (f32[2,16,32,128]{3,2,1,0:T(8,128)S(1)}, f32[2,16,32,128]{3,2,1,0:T(8,128)S(1)}, u32[]{:S(2)}, u32[]{:S(2)}) collective-permute-start(f32[2,16,32,128]{3,2,1,0:T(8,128)S(1)} %shard_map.126.refs_3_.refs_0_.vector), channel_id=1, source_target_pairs={{0,1},{1,0},{2,3},{3,2},{4,5},{5,4},{6,7},{7,6},{8,9},{9,8},{10,11... | collective-permute-start | bytes 1572872 | tf_op jit(solution)/shard_map/ppermute | solution.py:754
  21.5 3.5 %copy-start.6 = (f32[16]{0:T(128)S(1)}, f32[16]{0:T(128)}, u32[]{:S(2)}) copy-start(f32[16]{0:T(128)} %kap_table.1) | copy-start | bytes 196
  21.5 5.8 %collective-permute-start.7 = (f32[2,4,24,128]{3,2,1,0:T(8,128)S(1)}, f32[2,4,24,128]{3,2,1,0:T(8,128)S(1)}, u32[]{:S(2)}, u32[]{:S(2)}) collective-permute-start(f32[2,4,24,128]{3,2,1,0:T(8,128)S(1)} %shard_map.127.refs_2_), channel_id=1, source_target_pairs={{0,2},{1,3},{2,0},{3,1},{4,6},{5,7},{6,4},{7,5},{8,10},{9,11},{10,... | collective-permute-start | bytes 294920 | tf_op jit(solution)/shard_map/ppermute | solution.py:778
  23.4 5.5 %collective-permute-start.9 = (f32[2,4,24,128]{3,2,1,0:T(8,128)S(1)}, f32[2,4,24,128]{3,2,1,0:T(8,128)S(1)}, u32[]{:S(2)}, u32[]{:S(2)}) collective-permute-start(f32[2,4,24,128]{3,2,1,0:T(8,128)S(1)} %shard_map.128.refs_6_), channel_id=1, source_target_pairs={{0,2},{1,3},{2,0},{3,1},{4,6},{5,7},{6,4},{7,5},{8,10},{9,11},{10,... | collective-permute-start | bytes 294920 | tf_op jit(solution)/shard_map/ppermute | solution.py:778
  32.7 4.2 %collective-permute-start.10 = (f32[104,128]{1,0:T(8,128)S(1)}, f32[104,128]{1,0:T(8,128)S(1)}, u32[]{:S(2)}, u32[]{:S(2)}) collective-permute-start(f32[104,128]{1,0:T(8,128)S(1)} %get-tuple-element.49.sent), channel_id=1, source_target_pairs={{0,2},{1,3},{2,0},{3,1},{4,6},{5,7},{6,4},{7,5},{8,10},{9,11},{10,... | collective-permute-start | bytes 159752 | tf_op jit(solution)/shard_map/ppermute | solution.py:778
  40.7 2.0 %collective-permute-start.11 = (f32[2,16,32,128]{3,2,1,0:T(8,128)S(1)}, f32[2,16,32,128]{3,2,1,0:T(8,128)S(1)}, u32[]{:S(2)}, u32[]{:S(2)}) collective-permute-start(f32[2,16,32,128]{3,2,1,0:T(8,128)S(1)} %get-tuple-element.51), channel_id=1, source_target_pairs={{0,1},{1,0},{2,3},{3,2},{4,5},{5,4},{6,7},{7,6},{8,9},{9,8},{10,11... | collective-permute-start | bytes 1572872 | tf_op jit(solution)/shard_map/ppermute | solution.py:754
  43.0 4.9 %collective-permute-start.12 = (f32[1,2,2,32,128]{4,3,2,1,0:T(8,128)S(1)}, f32[1,2,2,32,128]{4,3,2,1,0:T(8,128)S(1)}, u32[]{:S(2)}, u32[]{:S(2)}) collective-permute-start(f32[1,2,2,32,128]{4,3,2,1,0:T(8,128)S(1)} %shard_map.135.refs_2_), channel_id=1, source_target_pairs={{0,4},{4,0},{1,5},{5,1},{2,6},{6,2},{3,7},{7,3},{8,12},{12,8},{9,1... | collective-permute-start | bytes 196616 | tf_op jit(solution)/shard_map/ppermute | solution.py:751
  44.6 5.3 %collective-permute-start.14 = (f32[1,2,2,32,128]{4,3,2,1,0:T(8,128)S(1)}, f32[1,2,2,32,128]{4,3,2,1,0:T(8,128)S(1)}, u32[]{:S(2)}, u32[]{:S(2)}) collective-permute-start(f32[1,2,2,32,128]{4,3,2,1,0:T(8,128)S(1)} %shard_map.134.refs_2_), channel_id=1, source_target_pairs={{0,4},{4,0},{1,5},{5,1},{2,6},{6,2},{3,7},{7,3},{8,12},{12,8},{9,1... | collective-permute-start | bytes 196616 | tf_op jit(solution)/shard_map/ppermute | solution.py:751
  45.3 6.8 %collective-permute-start.17 = (f32[1,2,2,32,128]{4,3,2,1,0:T(8,128)S(1)}, f32[1,2,2,32,128]{4,3,2,1,0:T(8,128)S(1)}, u32[]{:S(2)}, u32[]{:S(2)}) collective-permute-start(f32[1,2,2,32,128]{4,3,2,1,0:T(8,128)S(1)} %shard_map.136.refs_2_), channel_id=1, source_target_pairs={{0,4},{4,0},{1,5},{5,1},{2,6},{6,2},{3,7},{7,3},{8,12},{12,8},{9,1... | collective-permute-start | bytes 196616 | tf_op jit(solution)/shard_map/ppermute | solution.py:751
  47.0 5.2 %collective-permute-start.16 = (f32[1,2,2,32,128]{4,3,2,1,0:T(8,128)S(1)}, f32[1,2,2,32,128]{4,3,2,1,0:T(8,128)S(1)}, u32[]{:S(2)}, u32[]{:S(2)}) collective-permute-start(f32[1,2,2,32,128]{4,3,2,1,0:T(8,128)S(1)} %shard_map.137.refs_2_), channel_id=1, source_target_pairs={{0,4},{4,0},{1,5},{5,1},{2,6},{6,2},{3,7},{7,3},{8,12},{12,8},{9,1... | collective-permute-start | bytes 196616 | tf_op jit(solution)/shard_map/ppermute | solution.py:751
  47.9 6.8 %collective-permute-start.13 = (f32[2,2,32,128]{3,2,1,0:T(8,128)S(1)}, f32[2,2,32,128]{3,2,1,0:T(8,128)S(1)}, u32[]{:S(2)}, u32[]{:S(2)}) collective-permute-start(f32[2,2,32,128]{3,2,1,0:T(8,128)S(1)} %shard_map.139), channel_id=1, source_target_pairs={{0,16},{8,24},{16,0},{24,8},{1,17},{9,25},{17,1},{25,9},{2,18},{10... | collective-permute-start | bytes 196616 | tf_op jit(solution)/shard_map/ppermute | solution.py:757
  49.9 6.3 %collective-permute-start.15 = (f32[2,2,32,128]{3,2,1,0:T(8,128)S(1)}, f32[2,2,32,128]{3,2,1,0:T(8,128)S(1)}, u32[]{:S(2)}, u32[]{:S(2)}) collective-permute-start(f32[2,2,32,128]{3,2,1,0:T(8,128)S(1)} %shard_map.140), channel_id=1, source_target_pairs={{0,24},{8,16},{16,8},{24,0},{1,25},{9,17},{17,9},{25,1},{2,26},{10... | collective-permute-start | bytes 196616 | tf_op jit(solution)/shard_map/ppermute | solution.py:757
  52.1 4.8 %collective-permute-start.18 = (f32[2,2,32,128]{3,2,1,0:T(8,128)S(1)}, f32[2,2,32,128]{3,2,1,0:T(8,128)S(1)}, u32[]{:S(2)}, u32[]{:S(2)}) collective-permute-start(f32[2,2,32,128]{3,2,1,0:T(8,128)S(1)} %shard_map.143), channel_id=1, source_target_pairs={{0,8},{8,0},{16,24},{24,16},{1,9},{9,1},{17,25},{25,17},{2,10},{10... | collective-permute-start | bytes 196616 | tf_op jit(solution)/shard_map/ppermute | solution.py:757
  52.2 4.6 %copy-start.4 = (f32[8,32,32]{2,1,0:T(8,128)S(1)}, f32[8,32,32]{2,1,0:T(8,128)}, u32[]{:S(2)}) copy-start(f32[8,32,32]{2,1,0:T(8,128)} %refs_6_.1) | copy-start | bytes 98308
  52.2 4.6 %copy-start.5 = (f32[8,32,32]{2,1,0:T(8,128)S(1)}, f32[8,32,32]{2,1,0:T(8,128)}, u32[]{:S(2)}) copy-start(f32[8,32,32]{2,1,0:T(8,128)} %refs_7_.1) | copy-start | bytes 98308
  (4 other events, 9.6 us)

commit v23 on v21

--- a/solution.py
+++ b/solution.py
@@ -636,9 +636,9 @@
                 outs[i, f, q] = piece
 
 
-def send_kernel(own, came, out, *, k):
+def send_kernel(own, came, out, *, choices):
     _, x, _, _ = places(2)
-    packed_slabs(own, came, 1 - x, (k,), out)
+    packed_slabs(own, came, 1 - x, choices, out)
 
 
 def keep_kernel(own, came, kept):
@@ -646,8 +646,8 @@
     packed_slabs(own, came, x, range(kept.shape[0]), kept)
 
 
-def add_kernel(kept, came, out, *, k):
-    out[...] = kept[k] + came[0]
+def add_kernel(kept, came, out, *, k, at):
+    out[...] = kept[k] + came[at]
 
 
 def sum_kernel(*refs):
@@ -822,12 +822,17 @@
     piece = f32(2, groups, cy, cz)
     got = swap_core(message)
     crossed, last = {}, ()
-    for k in reversed(range(n)):
-        last = run(functools.partial(send_kernel, k=k), (f32(1, *piece.shape),), own, got, after=last)
-        crossed[k] = swap_x(last[0])
+    half = n // 2
+    for choices in (*((k,) for k in reversed(range(half, n))), tuple(range(half))):
+        last = run(
+            functools.partial(send_kernel, choices=choices), (f32(len(choices), *piece.shape),), own, got, after=last
+        )
+        value = swap_x(last[0])
+        crossed.update({k: (value, at) for at, k in enumerate(choices)})
     (kept,) = run(keep_kernel, (f32(n, *piece.shape),), own, got, after=last)
     totals = {
-        k: run(functools.partial(add_kernel, k=k), (piece,), kept, value)[0] for k, value in crossed.items()
+        k: run(functools.partial(add_kernel, k=k, at=at), (piece,), kept, value)[0]
+        for k, (value, at) in crossed.items()
     }
     received = {k: along_z(totals[k], k) for k in reversed(range(1, n))}
     (distant,) = run(sum_kernel, (piece,), *(received[k] for k in range(n // 2, n)), cost=long)

time: 69.7 us -> 71.3 us (1.023)
  waiting for transfers between devices: 14.7 us -> 16.7 us
    ppermute x7 -> x6, waiting for transfers between devices: 3.11 us -> 5.47 us  [swap_x(): return lax.ppermute(value, 'gx', [(0, 1), (1, 0)])]
    ppermute x7 -> x6, starting transfers between devices: 8.89 us -> 8.29 us  [swap_x(): return lax.ppermute(value, 'gx', [(0, 1), (1, 0)])]
    pallas_call x25 -> x24, Pallas kernels: 19.1 us -> 19 us  [run(): pl.pallas_call(body if waits else kernel, out_shape=tuple(outs), in_specs...]
  transfers between devices with their start and end apart: 19 -> 18, of which waited for: 9 -> 10; matrix products, arithmetic and copies ran while one was open for 0% -> 0% of each run, Pallas kernels for 14% -> 14%
where the time goes in v23:
time: 71.3 us; the launch traced here: 71.1 us
  starting transfers between devices  22.5 us (32%)
  Pallas kernels  19 us (27%)
  waiting for transfers between devices  16.7 us (23%)
  blocking collectives  11.2 us (16%)
  between operations  1.59 us (2%)
    pallas_call x24, Pallas kernels, run(): pl.pallas_call(body if waits else kernel, out_shape=tuple(outs), in_specs...  19 us
    all_to_all x1, blocking collectives, per_device_paired(): lax.all_to_all(jnp.broadcast_to(tile, (8 * n, 1, 128)), everyone, 0, 0)  11.2 us
    ppermute x6, starting transfers between devices, along_z(): return lax.ppermute(value, 'src', [(i, i ^ k) for i in range(n)])  9.23 us
    ppermute x6, starting transfers between devices, swap_x(): return lax.ppermute(value, 'gx', [(0, 1), (1, 0)])  8.29 us
    ppermute x6, waiting for transfers between devices, along_z(): return lax.ppermute(value, 'src', [(i, i ^ k) for i in range(n)])  6.26 us
    ppermute x6, waiting for transfers between devices, swap_x(): return lax.ppermute(value, 'gx', [(0, 1), (1, 0)])  5.47 us
    ppermute x3, starting transfers between devices, across_y(): return lax.ppermute(value, 'gy', [(i, (i + 2) % 4) for i in range(4)])  4.75 us
    ppermute x3, waiting for transfers between devices, across_y(): return lax.ppermute(value, 'gy', [(i, (i + 2) % 4) for i in range(4)])  2.85 us
  transfers between devices with their start and end apart: 18, of which 10 were waited for; matrix products, arithmetic and copies ran while one was open for 0% of the time, Pallas kernels for 14%

profile of v23, /device:TPU:0, one launch (start us, length us, event | category | flops | bytes accessed | tf_op | source)
XLA Modules:
  0.0 71.1 jit_solution(8610293780782089813)
XLA Ops:
  0.6 3.0 %collective-permute-start = (s32[8,32,128]{2,1,0:T(8,128)}, s32[8,32,128]{2,1,0:T(8,128)S(1)}, u32[]{:S(2)}, u32[]{:S(2)}) collective-permute-start(s32[8,32,128]{2,1,0:T(8,128)} %refs_1_.3), channel_id=1, source_target_pairs={{0,4},{4,0},{1,5},{5,1},{2,6},{6,2},{3,7},{7,3},{8,12},{12,8},{9,1... | collective-permute-start | bytes 393224 | tf_op jit(solution)/shard_map/ppermute | solution.py:751
  3.6 1.9 %shard_map.122 = (f32[4,32,128]{2,1,0:T(8,128)}, f32[20,32,128]{2,1,0:T(8,128)}) custom-call(f32[4,8,32,128]{3,2,1,0:T(8,128)} %refs_0_.2, f32[8,32,32]{2,1,0:T(8,128)} %vk.5, f32[8,32,32]{2,1,0:T(8,128)} %va.5), custom_call_target="tpu_custom_call" | custom-call | tf_op jit(solution)/shard_map/pallas_call | solution.py:721
  5.6 4.1 %collective-permute-start.4 = (f32[4,32,128]{2,1,0:T(8,128)}, f32[4,32,128]{2,1,0:T(8,128)S(1)}, u32[]{:S(2)}, u32[]{:S(2)}) collective-permute-start(f32[4,32,128]{2,1,0:T(8,128)} %get-tuple-element.31), channel_id=1, source_target_pairs={{0,24},{8,16},{16,8},{24,0},{1,25},{9,17},{17,9},{25,1},{2,26},{10... | collective-permute-start | bytes 196616 | tf_op jit(solution)/shard_map/ppermute | solution.py:757
  11.0 2.1 %shard_map.121 = (f32[16,72,128]{2,1,0:T(8,128)S(1)}, f32[1,128]{1,0:T(1,128)S(1)}) custom-call(s32[1,1024]{1,0:T(1,128)S(1)} %bitcast.3, f32[1]{0:T(128)S(6)} %copy.13.refs_1_, s32[8,32,128]{2,1,0:T(8,128)S(1)} %collective-permute-done.refs_2_.refs_3_), custom_call_target="tpu_custom_call" | custom-call | flops 301989888 | bytes 589824 | tf_op jit(solution)/shard_map/pallas_call | solution.py:721
  13.1 2.1 %collective-permute-done.3.refs_1_ = f32[4,32,128]{2,1,0:T(8,128)S(1)} collective-permute-done((f32[4,32,128]{2,1,0:T(8,128)}, f32[4,32,128]{2,1,0:T(8,128)S(1)}, u32[]{:S(2)}, u32[]{:S(2)}) %collective-permute-start.3) | collective-permute-done | bytes 65568 | tf_op jit(solution)/shard_map/ppermute | solution.py:757
  15.2 1.6 %collective-permute-start.6 = (f32[12,32,128]{2,1,0:T(8,128)S(1)}, f32[12,32,128]{2,1,0:T(8,128)S(1)}, u32[]{:S(2)}, u32[]{:S(2)}) collective-permute-start(f32[12,32,128]{2,1,0:T(8,128)S(1)} %shard_map.123.refs_4_.joined), channel_id=1, source_target_pairs={{0,4},{4,0},{1,5},{5,1},{2,6},{6,2},{3,7},{7,3},{8,12},{12,8},{9,1... | collective-permute-start | bytes 589832 | tf_op jit(solution)/shard_map/ppermute | solution.py:751
  17.9 3.1 %collective-permute-done.6.refs_2_ = f32[12,32,128]{2,1,0:T(8,128)S(1)} collective-permute-done((f32[12,32,128]{2,1,0:T(8,128)S(1)}, f32[12,32,128]{2,1,0:T(8,128)S(1)}, u32[]{:S(2)}, u32[]{:S(2)}) %collective-permute-start.6) | collective-permute-done | bytes 196640 | tf_op jit(solution)/shard_map/ppermute | solution.py:751
  21.5 1.6 %collective-permute-start.7 = (f32[2,4,24,128]{3,2,1,0:T(8,128)S(1)}, f32[2,4,24,128]{3,2,1,0:T(8,128)S(1)}, u32[]{:S(2)}, u32[]{:S(2)}) collective-permute-start(f32[2,4,24,128]{3,2,1,0:T(8,128)S(1)} %shard_map.127.refs_2_), channel_id=1, source_target_pairs={{0,2},{1,3},{2,0},{3,1},{4,6},{5,7},{6,4},{7,5},{8,10},{9,11},{10,... | collective-permute-start | bytes 294920 | tf_op jit(solution)/shard_map/ppermute | solution.py:778
  23.4 1.6 %collective-permute-start.9 = (f32[2,4,24,128]{3,2,1,0:T(8,128)S(1)}, f32[2,4,24,128]{3,2,1,0:T(8,128)S(1)}, u32[]{:S(2)}, u32[]{:S(2)}) collective-permute-start(f32[2,4,24,128]{3,2,1,0:T(8,128)S(1)} %shard_map.128.refs_6_), channel_id=1, source_target_pairs={{0,2},{1,3},{2,0},{3,1},{4,6},{5,7},{6,4},{7,5},{8,10},{9,11},{10,... | collective-permute-start | bytes 294920 | tf_op jit(solution)/shard_map/ppermute | solution.py:778
  25.0 2.3 %shard_map.129 = (f32[18,72,128]{2,1,0:T(8,128)S(1)}, f32[16,72,128]{2,1,0:T(8,128)S(1)}, f32[17,72,128]{2,1,0:T(8,128)S(1)}, f32[16,72,128]{2,1,0:T(8,128)S(1)}...) custom-call(f32[16]{0:T(128)S(1)} %copy-done.6, f32[16]{0:T(128)S(1)} %copy-done.7, ...), custom_call_target="tpu_custom_call" | custom-call | flops 1000000000 | bytes 67108864 | tf_op jit(solution)/shard_map/pallas_call | solution.py:721
  27.3 0.8 %shard_map.130 = (f32[16,72,128]{2,1,0:T(8,128)S(1)}, f32[17,72,128]{2,1,0:T(8,128)S(1)}, f32[16,72,128]{2,1,0:T(8,128)S(1)}, f32[16,72,128]{2,1,0:T(8,128)S(1)}) custom-call(f32[16]{0:T(128)S(1)} %copy-done.6, f32[16]{0:T(128)S(1)} %copy-done.7, f32[2,4,24,128]{3,2,1,0:T(8,128)S(1)} %collective-permute-done.7.edge.refs_2_, ...), custom_call_target="tpu_custom_call" | custom-call | tf_op jit(solution)/shard_map/pallas_call | solution.py:721
  28.9 3.8 %shard_map.132 = (f32[16,72,128]{2,1,0:T(8,128)S(1)}, f32[104,128]{1,0:T(8,128)S(1)}) custom-call(f32[18,72,128]{2,1,0:T(8,128)S(1)} %get-tuple-element.41.phi, f32[16,72,128]{2,1,0:T(8,128)S(1)} %get-tuple-element.42.phi_y, f32[16,72,128]{2,1,0:T(8,128)S(1)} %get-tuple-element.43.phi_z, f32[16,72,128]{2,1,0:T(8,128)S(1)} %get-tuple-element.44.diag, ...), custom_call_target="tpu_custom_call" | custom-call | tf_op jit(solution)/shard_map/pallas_call | solution.py:721
  32.7 1.6 %collective-permute-start.10 = (f32[104,128]{1,0:T(8,128)S(1)}, f32[104,128]{1,0:T(8,128)S(1)}, u32[]{:S(2)}, u32[]{:S(2)}) collective-permute-start(f32[104,128]{1,0:T(8,128)S(1)} %get-tuple-element.49.sent), channel_id=1, source_target_pairs={{0,2},{1,3},{2,0},{3,1},{4,6},{5,7},{6,4},{7,5},{8,10},{9,11},{10,... | collective-permute-start | bytes 159752 | tf_op jit(solution)/shard_map/ppermute | solution.py:778
  34.3 2.6 %collective-permute-done.10.came = f32[104,128]{1,0:T(8,128)S(1)} collective-permute-done((f32[104,128]{1,0:T(8,128)S(1)}, f32[104,128]{1,0:T(8,128)S(1)}, u32[]{:S(2)}, u32[]{:S(2)}) %collective-permute-start.10) | collective-permute-done | bytes 53280 | tf_op jit(solution)/shard_map/ppermute | solution.py:778
  36.9 3.8 %shard_map.133 = (f32[2,16,32,128]{3,2,1,0:T(8,128)S(1)}, f32[2,16,32,128]{3,2,1,0:T(8,128)S(1)}) custom-call(f32[18,72,128]{2,1,0:T(8,128)S(1)} %get-tuple-element.41.phi, f32[16,72,128]{2,1,0:T(8,128)S(1)} %get-tuple-element.42.phi_y, f32[16,72,128]{2,1,0:T(8,128)S(1)} %get-tuple-element.43.phi_z, f32[16,72,128]{2,1,0:T(8,128)S(1)} %get-tuple-element.48.change, ...), custom_call_target="tpu_custom_call" | custom-call | tf_op jit(solution)/shard_map/pallas_call | solution.py:721
  40.8 1.9 %collective-permute-done.11.came.refs_1_ = f32[2,16,32,128]{3,2,1,0:T(8,128)S(1)} collective-permute-done((f32[2,16,32,128]{3,2,1,0:T(8,128)S(1)}, f32[2,16,32,128]{3,2,1,0:T(8,128)S(1)}, u32[]{:S(2)}, u32[]{:S(2)}) %collective-permute-start.11) | collective-permute-done | bytes 524320 | tf_op jit(solution)/shard_map/ppermute | solution.py:754
  43.0 1.6 %collective-permute-start.12 = (f32[1,2,2,32,128]{4,3,2,1,0:T(8,128)S(1)}, f32[1,2,2,32,128]{4,3,2,1,0:T(8,128)S(1)}, u32[]{:S(2)}, u32[]{:S(2)}) collective-permute-start(f32[1,2,2,32,128]{4,3,2,1,0:T(8,128)S(1)} %shard_map.135.refs_2_), channel_id=1, source_target_pairs={{0,4},{4,0},{1,5},{5,1},{2,6},{6,2},{3,7},{7,3},{8,12},{12,8},{9,1... | collective-permute-start | bytes 196616 | tf_op jit(solution)/shard_map/ppermute | solution.py:751
  45.4 1.5 %collective-permute-start.14 = (f32[1,2,2,32,128]{4,3,2,1,0:T(8,128)S(1)}, f32[1,2,2,32,128]{4,3,2,1,0:T(8,128)S(1)}, u32[]{:S(2)}, u32[]{:S(2)}) collective-permute-start(f32[1,2,2,32,128]{4,3,2,1,0:T(8,128)S(1)} %shard_map.134.refs_2_), channel_id=1, source_target_pairs={{0,4},{4,0},{1,5},{5,1},{2,6},{6,2},{3,7},{7,3},{8,12},{12,8},{9,1... | collective-permute-start | bytes 196616 | tf_op jit(solution)/shard_map/ppermute | solution.py:751
  47.5 2.0 %collective-permute-start.13 = (f32[2,2,32,128]{3,2,1,0:T(8,128)S(1)}, f32[2,2,32,128]{3,2,1,0:T(8,128)S(1)}, u32[]{:S(2)}, u32[]{:S(2)}) collective-permute-start(f32[2,2,32,128]{3,2,1,0:T(8,128)S(1)} %shard_map.138), channel_id=1, source_target_pairs={{0,16},{8,24},{16,0},{24,8},{1,17},{9,25},{17,1},{25,9},{2,18},{10... | collective-permute-start | bytes 196616 | tf_op jit(solution)/shard_map/ppermute | solution.py:757
  49.4 2.1 %collective-permute-done.14.came = f32[1,2,2,32,128]{4,3,2,1,0:T(8,128)S(1)} collective-permute-done((f32[1,2,2,32,128]{4,3,2,1,0:T(8,128)S(1)}, f32[1,2,2,32,128]{4,3,2,1,0:T(8,128)S(1)}, u32[]{:S(2)}, u32[]{:S(2)}) %collective-permute-start.14) | collective-permute-done | bytes 65568 | tf_op jit(solution)/shard_map/ppermute | solution.py:751
  51.6 2.5 %collective-permute-start.15 = (f32[2,2,32,128]{3,2,1,0:T(8,128)S(1)}, f32[2,2,32,128]{3,2,1,0:T(8,128)S(1)}, u32[]{:S(2)}, u32[]{:S(2)}) collective-permute-start(f32[2,2,32,128]{3,2,1,0:T(8,128)S(1)} %shard_map.139), channel_id=1, source_target_pairs={{0,24},{8,16},{16,8},{24,0},{1,25},{9,17},{17,9},{25,1},{2,26},{10... | collective-permute-start | bytes 196616 | tf_op jit(solution)/shard_map/ppermute | solution.py:757
  54.2 3.5 %collective-permute-done.15.refs_1_ = f32[2,2,32,128]{3,2,1,0:T(8,128)S(1)} collective-permute-done((f32[2,2,32,128]{3,2,1,0:T(8,128)S(1)}, f32[2,2,32,128]{3,2,1,0:T(8,128)S(1)}, u32[]{:S(2)}, u32[]{:S(2)}) %collective-permute-start.15) | collective-permute-done | bytes 65568 | tf_op jit(solution)/shard_map/ppermute | solution.py:757
  58.9 11.2 %all_to_all.5.tiles = f32[32,1,128]{2,1,0:T(1,128)S(1)} all-to-all(f32[32,1,128]{2,1,0:T(1,128)S(1)} %broadcast_in_dim.3), channel_id=1, replica_groups=mesh['src'=4,'gx'=2,'gy'=4] {'src','gx','gy'}, dimensions={0} | all-to-all | bytes 32768 | tf_op jit(solution)/shard_map/all_to_all | solution.py:846
  70.1 1.0 %shard_map.144 = (f32[8,32,32]{2,1,0:T(8,128)}, f32[8,32,32]{2,1,0:T(8,128)}, f32[2]{0:T(128)}) custom-call(f32[32,1,128]{2,1,0:T(1,128)S(1)} %all_to_all.5.tiles, f32[8,32,32]{2,1,0:T(8,128)S(1)} %get-tuple-element.53.w_k, f32[8,32,32]{2,1,0:T(8,128)S(1)} %get-tuple-element.54.w_a, f32[8,32,32]{2,1,0:T(8,128)S(1)} %copy-done.1, f32[8,32,32]{2,1,0:T(8,128)S(1)} %copy-done.2), custom_call_target="tpu_custom_call" | custom-call | tf_op jit(solution)/shard_map/pallas_call | solution.py:721
  (56 shorter events, 6.3 us)
Async XLA Ops:
  0.6 10.3 %collective-permute-start = (s32[8,32,128]{2,1,0:T(8,128)}, s32[8,32,128]{2,1,0:T(8,128)S(1)}, u32[]{:S(2)}, u32[]{:S(2)}) collective-permute-start(s32[8,32,128]{2,1,0:T(8,128)} %refs_1_.3), channel_id=1, source_target_pairs={{0,4},{4,0},{1,5},{5,1},{2,6},{6,2},{3,7},{7,3},{8,12},{12,8},{9,1... | collective-permute-start | bytes 393224 | tf_op jit(solution)/shard_map/ppermute | solution.py:751
  5.5 5.4 %copy-start.8 = (s32[1024]{0:T(1024)S(1)}, s32[1024]{0:T(1024)}, u32[]{:S(2)}) copy-start(s32[1024]{0:T(1024)} %param.14) | copy-start | bytes 12292
  5.5 11.3 %collective-permute-start.1 = (f32[20,32,128]{2,1,0:T(8,128)}, f32[20,32,128]{2,1,0:T(8,128)S(1)}, u32[]{:S(2)}, u32[]{:S(2)}) collective-permute-start(f32[20,32,128]{2,1,0:T(8,128)} %get-tuple-element.30), channel_id=1, source_target_pairs={{0,4},{4,0},{1,5},{5,1},{2,6},{6,2},{3,7},{7,3},{8,12},{12,8},{9,1... | collective-permute-start | bytes 983048 | tf_op jit(solution)/shard_map/ppermute | solution.py:751
  5.6 7.5 %collective-permute-start.4 = (f32[4,32,128]{2,1,0:T(8,128)}, f32[4,32,128]{2,1,0:T(8,128)S(1)}, u32[]{:S(2)}, u32[]{:S(2)}) collective-permute-start(f32[4,32,128]{2,1,0:T(8,128)} %get-tuple-element.31), channel_id=1, source_target_pairs={{0,24},{8,16},{16,8},{24,0},{1,25},{9,17},{17,9},{25,1},{2,26},{10... | collective-permute-start | bytes 196616 | tf_op jit(solution)/shard_map/ppermute | solution.py:757
  9.7 5.5 %collective-permute-start.3 = (f32[4,32,128]{2,1,0:T(8,128)}, f32[4,32,128]{2,1,0:T(8,128)S(1)}, u32[]{:S(2)}, u32[]{:S(2)}) collective-permute-start(f32[4,32,128]{2,1,0:T(8,128)} %get-tuple-element.31), channel_id=1, source_target_pairs={{0,16},{8,24},{16,0},{24,8},{1,17},{9,25},{17,1},{25,9},{2,18},{10... | collective-permute-start | bytes 196616 | tf_op jit(solution)/shard_map/ppermute | solution.py:757
  9.7 5.5 %collective-permute-start.2 = (f32[4,32,128]{2,1,0:T(8,128)}, f32[4,32,128]{2,1,0:T(8,128)S(1)}, u32[]{:S(2)}, u32[]{:S(2)}) collective-permute-start(f32[4,32,128]{2,1,0:T(8,128)} %get-tuple-element.31), channel_id=1, source_target_pairs={{0,8},{8,0},{16,24},{24,16},{1,9},{9,1},{17,25},{25,17},{2,10},{10... | collective-permute-start | bytes 196616 | tf_op jit(solution)/shard_map/ppermute | solution.py:757
  13.1 3.7 %copy-start = (f32[4,8,32,128]{3,2,1,0:T(8,128)S(1)}, f32[4,8,32,128]{3,2,1,0:T(8,128)}, u32[]{:S(2)}) copy-start(f32[4,8,32,128]{3,2,1,0:T(8,128)} %refs_0_.2) | copy-start | bytes 1572868
  15.2 5.8 %collective-permute-start.6 = (f32[12,32,128]{2,1,0:T(8,128)S(1)}, f32[12,32,128]{2,1,0:T(8,128)S(1)}, u32[]{:S(2)}, u32[]{:S(2)}) collective-permute-start(f32[12,32,128]{2,1,0:T(8,128)S(1)} %shard_map.123.refs_4_.joined), channel_id=1, source_target_pairs={{0,4},{4,0},{1,5},{5,1},{2,6},{6,2},{3,7},{7,3},{8,12},{12,8},{9,1... | collective-permute-start | bytes 589832 | tf_op jit(solution)/shard_map/ppermute | solution.py:751
  17.4 4.0 %collective-permute-start.5 = (f32[2,16,32,128]{3,2,1,0:T(8,128)S(1)}, f32[2,16,32,128]{3,2,1,0:T(8,128)S(1)}, u32[]{:S(2)}, u32[]{:S(2)}) collective-permute-start(f32[2,16,32,128]{3,2,1,0:T(8,128)S(1)} %get-tuple-element.34.refs_1_.refs_3_), channel_id=1, source_target_pairs={{0,1},{1,0},{2,3},{3,2},{4,5},{5,4},{6,7},{7,6},{8,9},{9,8},{10,11... | collective-permute-start | bytes 1572872 | tf_op jit(solution)/shard_map/ppermute | solution.py:754
  21.4 2.0 %collective-permute-start.8 = (f32[2,16,32,128]{3,2,1,0:T(8,128)S(1)}, f32[2,16,32,128]{3,2,1,0:T(8,128)S(1)}, u32[]{:S(2)}, u32[]{:S(2)}) collective-permute-start(f32[2,16,32,128]{3,2,1,0:T(8,128)S(1)} %shard_map.126.refs_3_.refs_0_.vector), channel_id=1, source_target_pairs={{0,1},{1,0},{2,3},{3,2},{4,5},{5,4},{6,7},{7,6},{8,9},{9,8},{10,11... | collective-permute-start | bytes 1572872 | tf_op jit(solution)/shard_map/ppermute | solution.py:754
  21.5 3.5 %copy-start.6 = (f32[16]{0:T(128)S(1)}, f32[16]{0:T(128)}, u32[]{:S(2)}) copy-start(f32[16]{0:T(128)} %kap_table.1) | copy-start | bytes 196
  21.5 3.4 %copy-start.7 = (f32[16]{0:T(128)S(1)}, f32[16]{0:T(128)}, u32[]{:S(2)}) copy-start(f32[16]{0:T(128)} %abs_table.1) | copy-start | bytes 196
  21.5 5.8 %collective-permute-start.7 = (f32[2,4,24,128]{3,2,1,0:T(8,128)S(1)}, f32[2,4,24,128]{3,2,1,0:T(8,128)S(1)}, u32[]{:S(2)}, u32[]{:S(2)}) collective-permute-start(f32[2,4,24,128]{3,2,1,0:T(8,128)S(1)} %shard_map.127.refs_2_), channel_id=1, source_target_pairs={{0,2},{1,3},{2,0},{3,1},{4,6},{5,7},{6,4},{7,5},{8,10},{9,11},{10,... | collective-permute-start | bytes 294920 | tf_op jit(solution)/shard_map/ppermute | solution.py:778
  23.4 5.5 %collective-permute-start.9 = (f32[2,4,24,128]{3,2,1,0:T(8,128)S(1)}, f32[2,4,24,128]{3,2,1,0:T(8,128)S(1)}, u32[]{:S(2)}, u32[]{:S(2)}) collective-permute-start(f32[2,4,24,128]{3,2,1,0:T(8,128)S(1)} %shard_map.128.refs_6_), channel_id=1, source_target_pairs={{0,2},{1,3},{2,0},{3,1},{4,6},{5,7},{6,4},{7,5},{8,10},{9,11},{10,... | collective-permute-start | bytes 294920 | tf_op jit(solution)/shard_map/ppermute | solution.py:778
  32.7 4.2 %collective-permute-start.10 = (f32[104,128]{1,0:T(8,128)S(1)}, f32[104,128]{1,0:T(8,128)S(1)}, u32[]{:S(2)}, u32[]{:S(2)}) collective-permute-start(f32[104,128]{1,0:T(8,128)S(1)} %get-tuple-element.49.sent), channel_id=1, source_target_pairs={{0,2},{1,3},{2,0},{3,1},{4,6},{5,7},{6,4},{7,5},{8,10},{9,11},{10,... | collective-permute-start | bytes 159752 | tf_op jit(solution)/shard_map/ppermute | solution.py:778
  40.7 2.0 %collective-permute-start.11 = (f32[2,16,32,128]{3,2,1,0:T(8,128)S(1)}, f32[2,16,32,128]{3,2,1,0:T(8,128)S(1)}, u32[]{:S(2)}, u32[]{:S(2)}) collective-permute-start(f32[2,16,32,128]{3,2,1,0:T(8,128)S(1)} %get-tuple-element.51), channel_id=1, source_target_pairs={{0,1},{1,0},{2,3},{3,2},{4,5},{5,4},{6,7},{7,6},{8,9},{9,8},{10,11... | collective-permute-start | bytes 1572872 | tf_op jit(solution)/shard_map/ppermute | solution.py:754
  43.0 4.4 %collective-permute-start.12 = (f32[1,2,2,32,128]{4,3,2,1,0:T(8,128)S(1)}, f32[1,2,2,32,128]{4,3,2,1,0:T(8,128)S(1)}, u32[]{:S(2)}, u32[]{:S(2)}) collective-permute-start(f32[1,2,2,32,128]{4,3,2,1,0:T(8,128)S(1)} %shard_map.135.refs_2_), channel_id=1, source_target_pairs={{0,4},{4,0},{1,5},{5,1},{2,6},{6,2},{3,7},{7,3},{8,12},{12,8},{9,1... | collective-permute-start | bytes 196616 | tf_op jit(solution)/shard_map/ppermute | solution.py:751
  44.8 9.3 %collective-permute-start.16 = (f32[2,2,2,32,128]{4,3,2,1,0:T(8,128)S(1)}, f32[2,2,2,32,128]{4,3,2,1,0:T(8,128)S(1)}, u32[]{:S(2)}, u32[]{:S(2)}) collective-permute-start(f32[2,2,2,32,128]{4,3,2,1,0:T(8,128)S(1)} %shard_map.136.refs_2_), channel_id=1, source_target_pairs={{0,4},{4,0},{1,5},{5,1},{2,6},{6,2},{3,7},{7,3},{8,12},{12,8},{9,1... | collective-permute-start | bytes 393224 | tf_op jit(solution)/shard_map/ppermute | solution.py:751
  45.4 6.2 %collective-permute-start.14 = (f32[1,2,2,32,128]{4,3,2,1,0:T(8,128)S(1)}, f32[1,2,2,32,128]{4,3,2,1,0:T(8,128)S(1)}, u32[]{:S(2)}, u32[]{:S(2)}) collective-permute-start(f32[1,2,2,32,128]{4,3,2,1,0:T(8,128)S(1)} %shard_map.134.refs_2_), channel_id=1, source_target_pairs={{0,4},{4,0},{1,5},{5,1},{2,6},{6,2},{3,7},{7,3},{8,12},{12,8},{9,1... | collective-permute-start | bytes 196616 | tf_op jit(solution)/shard_map/ppermute | solution.py:751
  47.5 6.8 %collective-permute-start.13 = (f32[2,2,32,128]{3,2,1,0:T(8,128)S(1)}, f32[2,2,32,128]{3,2,1,0:T(8,128)S(1)}, u32[]{:S(2)}, u32[]{:S(2)}) collective-permute-start(f32[2,2,32,128]{3,2,1,0:T(8,128)S(1)} %shard_map.138), channel_id=1, source_target_pairs={{0,16},{8,24},{16,0},{24,8},{1,17},{9,25},{17,1},{25,9},{2,18},{10... | collective-permute-start | bytes 196616 | tf_op jit(solution)/shard_map/ppermute | solution.py:757
  51.6 6.1 %collective-permute-start.15 = (f32[2,2,32,128]{3,2,1,0:T(8,128)S(1)}, f32[2,2,32,128]{3,2,1,0:T(8,128)S(1)}, u32[]{:S(2)}, u32[]{:S(2)}) collective-permute-start(f32[2,2,32,128]{3,2,1,0:T(8,128)S(1)} %shard_map.139), channel_id=1, source_target_pairs={{0,24},{8,16},{16,8},{24,0},{1,25},{9,17},{17,9},{25,1},{2,26},{10... | collective-permute-start | bytes 196616 | tf_op jit(solution)/shard_map/ppermute | solution.py:757
  54.0 4.4 %collective-permute-start.17 = (f32[2,2,32,128]{3,2,1,0:T(8,128)S(1)}, f32[2,2,32,128]{3,2,1,0:T(8,128)S(1)}, u32[]{:S(2)}, u32[]{:S(2)}) collective-permute-start(f32[2,2,32,128]{3,2,1,0:T(8,128)S(1)} %shard_map.142), channel_id=1, source_target_pairs={{0,8},{8,0},{16,24},{24,16},{1,9},{9,1},{17,25},{25,17},{2,10},{10... | collective-permute-start | bytes 196616 | tf_op jit(solution)/shard_map/ppermute | solution.py:757
  54.2 4.2 %copy-start.4 = (f32[8,32,32]{2,1,0:T(8,128)S(1)}, f32[8,32,32]{2,1,0:T(8,128)}, u32[]{:S(2)}) copy-start(f32[8,32,32]{2,1,0:T(8,128)} %refs_6_.1) | copy-start | bytes 98308
  54.2 4.2 %copy-start.5 = (f32[8,32,32]{2,1,0:T(8,128)S(1)}, f32[8,32,32]{2,1,0:T(8,128)}, u32[]{:S(2)}) copy-start(f32[8,32,32]{2,1,0:T(8,128)} %refs_7_.1) | copy-start | bytes 98308
  (3 other events, 6.2 us)

commit v24 on v21

--- a/solution.py
+++ b/solution.py
@@ -617,33 +617,40 @@
     lax.fori_loop(0, planes, product, 0, unroll=8)
 
 
-def packed_slabs(own, came, half, choices, outs):
+def packed_slabs(own, came, half, out):
     s, _, _, _ = places(2)
     _, planes, cy, lanes = own.shape
-    n = planes // 2 // outs.shape[2]
+    n, _, groups = out.shape[:3]
     slab = lanes // n
-    lane = index_along((cy, lanes), 1) // slab
+    block = index_along((cy, lanes), 1) // slab
     for f in range(2):
-        for q in range(outs.shape[2]):
+        for q in range(groups):
             at = planes // 2 * half + n * q
             parts = [own[f, at + j] + came[f, at + j] for j in range(n)]
-            for i, k in enumerate(choices):
-                to = s ^ k
-                piece = jnp.zeros((cy, lanes), jnp.float32)
+            size = n // 2
+            while size:
+                low = block & size == 0
                 for j in range(n):
-                    moved = pltpu.roll(parts[j], ((j - to + n) % n) * slab, 1)
-                    piece = jnp.where(lane == j, moved, piece)
-                outs[i, f, q] = piece
-
-
-def send_kernel(own, came, out, *, k):
+                    if not j & size:
+                        a, b = parts[j], parts[j | size]
+                        parts[j] = jnp.where(low, a, shifted(b, size * slab, 1))
+                        parts[j | size] = jnp.where(low, shifted(a, -size * slab, 1), b)
+                size //= 2
+            for t in range(n):
+                out[s ^ t, f, q] = parts[t]
+
+
+def send_kernel(own, came, *refs):
     _, x, _, _ = places(2)
-    packed_slabs(own, came, 1 - x, (k,), out)
+    outs, packed = refs[:-1], refs[-1]
+    packed_slabs(own, came, 1 - x, packed)
+    for k, out in enumerate(outs):
+        out[0] = packed[k]
 
 
 def keep_kernel(own, came, kept):
     _, x, _, _ = places(2)
-    packed_slabs(own, came, x, range(kept.shape[0]), kept)
+    packed_slabs(own, came, x, kept)
 
 
 def add_kernel(kept, came, out, *, k):
@@ -821,11 +828,11 @@
     )
     piece = f32(2, groups, cy, cz)
     got = swap_core(message)
-    crossed, last = {}, ()
-    for k in reversed(range(n)):
-        last = run(functools.partial(send_kernel, k=k), (f32(1, *piece.shape),), own, got, after=last)
-        crossed[k] = swap_x(last[0])
-    (kept,) = run(keep_kernel, (f32(n, *piece.shape),), own, got, after=last)
+    last = run(
+        send_kernel, [f32(1, *piece.shape)] * n, own, got, scratch=(float_block(n, *piece.shape),)
+    )
+    crossed = {k: swap_x(last[k]) for k in reversed(range(n))}
+    (kept,) = run(keep_kernel, (f32(n, *piece.shape),), own, got, after=(last[0],))
     totals = {
         k: run(functools.partial(add_kernel, k=k), (piece,), kept, value)[0] for k, value in crossed.items()
     }

time: 69.7 us -> 69.6 us (level)
    pallas_call x25 -> x22, Pallas kernels: 19.1 us -> 18.7 us  [run(): pl.pallas_call(body if waits else kernel, out_shape=tuple(outs), in_specs...]
  transfers between devices with their start and end apart: 19 -> 19, of which waited for: 9 -> 10; matrix products, arithmetic and copies ran while one was open for 0% -> 0% of each run, Pallas kernels for 14% -> 13%
where the time goes in v24:
time: 69.6 us; the launch traced here: 69.5 us
  starting transfers between devices  22.8 us (33%)
  Pallas kernels  18.7 us (27%)
  waiting for transfers between devices  14.9 us (21%)
  blocking collectives  11.4 us (16%)
  between operations  1.57 us (2%)
    pallas_call x22, Pallas kernels, run(): pl.pallas_call(body if waits else kernel, out_shape=tuple(outs), in_specs...  18.7 us
    all_to_all x1, blocking collectives, per_device_paired(): lax.all_to_all(jnp.broadcast_to(tile, (8 * n, 1, 128)), everyone, 0, 0)  11.4 us
    ppermute x6, starting transfers between devices, along_z(): return lax.ppermute(value, 'src', [(i, i ^ k) for i in range(n)])  9.08 us
    ppermute x7, starting transfers between devices, swap_x(): return lax.ppermute(value, 'gx', [(0, 1), (1, 0)])  8.76 us
    ppermute x6, waiting for transfers between devices, along_z(): return lax.ppermute(value, 'src', [(i, i ^ k) for i in range(n)])  6.42 us
    ppermute x3, starting transfers between devices, across_y(): return lax.ppermute(value, 'gy', [(i, (i + 2) % 4) for i in range(4)])  4.75 us
    ppermute x7, waiting for transfers between devices, swap_x(): return lax.ppermute(value, 'gx', [(0, 1), (1, 0)])  3.47 us
    ppermute x3, waiting for transfers between devices, across_y(): return lax.ppermute(value, 'gy', [(i, (i + 2) % 4) for i in range(4)])  2.85 us
  transfers between devices with their start and end apart: 19, of which 10 were waited for; matrix products, arithmetic and copies ran while one was open for 0% of the time, Pallas kernels for 13%

profile of v24, /device:TPU:0, one launch (start us, length us, event | category | flops | bytes accessed | tf_op | source)
XLA Modules:
  0.0 69.5 jit_solution(9912263599520603796)
XLA Ops:
  0.6 3.0 %collective-permute-start = (s32[8,32,128]{2,1,0:T(8,128)}, s32[8,32,128]{2,1,0:T(8,128)S(1)}, u32[]{:S(2)}, u32[]{:S(2)}) collective-permute-start(s32[8,32,128]{2,1,0:T(8,128)} %refs_1_.3), channel_id=1, source_target_pairs={{0,4},{4,0},{1,5},{5,1},{2,6},{6,2},{3,7},{7,3},{8,12},{12,8},{9,1... | collective-permute-start | bytes 393224 | tf_op jit(solution)/shard_map/ppermute | solution.py:758
  3.6 1.9 %shard_map.122 = (f32[4,32,128]{2,1,0:T(8,128)}, f32[20,32,128]{2,1,0:T(8,128)}) custom-call(f32[4,8,32,128]{3,2,1,0:T(8,128)} %refs_0_.2, f32[8,32,32]{2,1,0:T(8,128)} %vk.5, f32[8,32,32]{2,1,0:T(8,128)} %va.5), custom_call_target="tpu_custom_call" | custom-call | tf_op jit(solution)/shard_map/pallas_call | solution.py:728
  5.6 4.1 %collective-permute-start.4 = (f32[4,32,128]{2,1,0:T(8,128)}, f32[4,32,128]{2,1,0:T(8,128)S(1)}, u32[]{:S(2)}, u32[]{:S(2)}) collective-permute-start(f32[4,32,128]{2,1,0:T(8,128)} %get-tuple-element.35), channel_id=1, source_target_pairs={{0,24},{8,16},{16,8},{24,0},{1,25},{9,17},{17,9},{25,1},{2,26},{10... | collective-permute-start | bytes 196616 | tf_op jit(solution)/shard_map/ppermute | solution.py:764
  11.0 2.1 %shard_map.121 = (f32[16,72,128]{2,1,0:T(8,128)S(1)}, f32[1,128]{1,0:T(1,128)S(1)}) custom-call(s32[1,1024]{1,0:T(1,128)S(1)} %bitcast.3, f32[1]{0:T(128)S(6)} %copy.13.refs_1_, s32[8,32,128]{2,1,0:T(8,128)S(1)} %collective-permute-done.refs_2_.refs_3_), custom_call_target="tpu_custom_call" | custom-call | flops 301989888 | bytes 589824 | tf_op jit(solution)/shard_map/pallas_call | solution.py:728
  13.1 2.1 %collective-permute-done.3.refs_1_ = f32[4,32,128]{2,1,0:T(8,128)S(1)} collective-permute-done((f32[4,32,128]{2,1,0:T(8,128)}, f32[4,32,128]{2,1,0:T(8,128)S(1)}, u32[]{:S(2)}, u32[]{:S(2)}) %collective-permute-start.3) | collective-permute-done | bytes 65568 | tf_op jit(solution)/shard_map/ppermute | solution.py:764
  15.2 1.6 %collective-permute-start.6 = (f32[12,32,128]{2,1,0:T(8,128)S(1)}, f32[12,32,128]{2,1,0:T(8,128)S(1)}, u32[]{:S(2)}, u32[]{:S(2)}) collective-permute-start(f32[12,32,128]{2,1,0:T(8,128)S(1)} %shard_map.123.refs_4_.joined), channel_id=1, source_target_pairs={{0,4},{4,0},{1,5},{5,1},{2,6},{6,2},{3,7},{7,3},{8,12},{12,8},{9,1... | collective-permute-start | bytes 589832 | tf_op jit(solution)/shard_map/ppermute | solution.py:758
  17.9 3.1 %collective-permute-done.6.refs_2_ = f32[12,32,128]{2,1,0:T(8,128)S(1)} collective-permute-done((f32[12,32,128]{2,1,0:T(8,128)S(1)}, f32[12,32,128]{2,1,0:T(8,128)S(1)}, u32[]{:S(2)}, u32[]{:S(2)}) %collective-permute-start.6) | collective-permute-done | bytes 196640 | tf_op jit(solution)/shard_map/ppermute | solution.py:758
  21.5 1.6 %collective-permute-start.7 = (f32[2,4,24,128]{3,2,1,0:T(8,128)S(1)}, f32[2,4,24,128]{3,2,1,0:T(8,128)S(1)}, u32[]{:S(2)}, u32[]{:S(2)}) collective-permute-start(f32[2,4,24,128]{3,2,1,0:T(8,128)S(1)} %shard_map.127.refs_2_), channel_id=1, source_target_pairs={{0,2},{1,3},{2,0},{3,1},{4,6},{5,7},{6,4},{7,5},{8,10},{9,11},{10,... | collective-permute-start | bytes 294920 | tf_op jit(solution)/shard_map/ppermute | solution.py:785
  23.4 1.6 %collective-permute-start.9 = (f32[2,4,24,128]{3,2,1,0:T(8,128)S(1)}, f32[2,4,24,128]{3,2,1,0:T(8,128)S(1)}, u32[]{:S(2)}, u32[]{:S(2)}) collective-permute-start(f32[2,4,24,128]{3,2,1,0:T(8,128)S(1)} %shard_map.128.refs_6_), channel_id=1, source_target_pairs={{0,2},{1,3},{2,0},{3,1},{4,6},{5,7},{6,4},{7,5},{8,10},{9,11},{10,... | collective-permute-start | bytes 294920 | tf_op jit(solution)/shard_map/ppermute | solution.py:785
  25.0 2.3 %shard_map.129 = (f32[18,72,128]{2,1,0:T(8,128)S(1)}, f32[16,72,128]{2,1,0:T(8,128)S(1)}, f32[17,72,128]{2,1,0:T(8,128)S(1)}, f32[16,72,128]{2,1,0:T(8,128)S(1)}...) custom-call(f32[16]{0:T(128)S(1)} %copy-done.6, f32[16]{0:T(128)S(1)} %copy-done.7, ...), custom_call_target="tpu_custom_call" | custom-call | flops 1000000000 | bytes 67108864 | tf_op jit(solution)/shard_map/pallas_call | solution.py:728
  27.3 0.8 %shard_map.130 = (f32[16,72,128]{2,1,0:T(8,128)S(1)}, f32[17,72,128]{2,1,0:T(8,128)S(1)}, f32[16,72,128]{2,1,0:T(8,128)S(1)}, f32[16,72,128]{2,1,0:T(8,128)S(1)}) custom-call(f32[16]{0:T(128)S(1)} %copy-done.6, f32[16]{0:T(128)S(1)} %copy-done.7, f32[2,4,24,128]{3,2,1,0:T(8,128)S(1)} %collective-permute-done.7.edge.refs_2_, ...), custom_call_target="tpu_custom_call" | custom-call | tf_op jit(solution)/shard_map/pallas_call | solution.py:728
  28.9 3.8 %shard_map.132 = (f32[16,72,128]{2,1,0:T(8,128)S(1)}, f32[104,128]{1,0:T(8,128)S(1)}) custom-call(f32[18,72,128]{2,1,0:T(8,128)S(1)} %get-tuple-element.45.phi, f32[16,72,128]{2,1,0:T(8,128)S(1)} %get-tuple-element.46.phi_y, f32[16,72,128]{2,1,0:T(8,128)S(1)} %get-tuple-element.47.phi_z, f32[16,72,128]{2,1,0:T(8,128)S(1)} %get-tuple-element.48.diag, ...), custom_call_target="tpu_custom_call" | custom-call | tf_op jit(solution)/shard_map/pallas_call | solution.py:728
  32.7 1.6 %collective-permute-start.10 = (f32[104,128]{1,0:T(8,128)S(1)}, f32[104,128]{1,0:T(8,128)S(1)}, u32[]{:S(2)}, u32[]{:S(2)}) collective-permute-start(f32[104,128]{1,0:T(8,128)S(1)} %get-tuple-element.53.sent), channel_id=1, source_target_pairs={{0,2},{1,3},{2,0},{3,1},{4,6},{5,7},{6,4},{7,5},{8,10},{9,11},{10,... | collective-permute-start | bytes 159752 | tf_op jit(solution)/shard_map/ppermute | solution.py:785
  34.3 2.6 %collective-permute-done.10.came = f32[104,128]{1,0:T(8,128)S(1)} collective-permute-done((f32[104,128]{1,0:T(8,128)S(1)}, f32[104,128]{1,0:T(8,128)S(1)}, u32[]{:S(2)}, u32[]{:S(2)}) %collective-permute-start.10) | collective-permute-done | bytes 53280 | tf_op jit(solution)/shard_map/ppermute | solution.py:785
  36.9 3.8 %shard_map.133 = (f32[2,16,32,128]{3,2,1,0:T(8,128)S(1)}, f32[2,16,32,128]{3,2,1,0:T(8,128)S(1)}) custom-call(f32[18,72,128]{2,1,0:T(8,128)S(1)} %get-tuple-element.45.phi, f32[16,72,128]{2,1,0:T(8,128)S(1)} %get-tuple-element.46.phi_y, f32[16,72,128]{2,1,0:T(8,128)S(1)} %get-tuple-element.47.phi_z, f32[16,72,128]{2,1,0:T(8,128)S(1)} %get-tuple-element.52.change, ...), custom_call_target="tpu_custom_call" | custom-call | tf_op jit(solution)/shard_map/pallas_call | solution.py:728
  40.8 1.9 %collective-permute-done.11.came.refs_1_ = f32[2,16,32,128]{3,2,1,0:T(8,128)S(1)} collective-permute-done((f32[2,16,32,128]{3,2,1,0:T(8,128)S(1)}, f32[2,16,32,128]{3,2,1,0:T(8,128)S(1)}, u32[]{:S(2)}, u32[]{:S(2)}) %collective-permute-start.11) | collective-permute-done | bytes 524320 | tf_op jit(solution)/shard_map/ppermute | solution.py:761
  43.0 1.6 %collective-permute-start.12 = (f32[1,2,2,32,128]{4,3,2,1,0:T(8,128)S(1)}, f32[1,2,2,32,128]{4,3,2,1,0:T(8,128)S(1)}, u32[]{:S(2)}, u32[]{:S(2)}) collective-permute-start(f32[1,2,2,32,128]{4,3,2,1,0:T(8,128)S(1)} %get-tuple-element.57), channel_id=1, source_target_pairs={{0,4},{4,0},{1,5},{5,1},{2,6},{6,2},{3,7},{7,3},{8,12},{12,8},{9,1... | collective-permute-start | bytes 196616 | tf_op jit(solution)/shard_map/ppermute | solution.py:758
  45.1 1.5 %collective-permute-start.17 = (f32[1,2,2,32,128]{4,3,2,1,0:T(8,128)S(1)}, f32[1,2,2,32,128]{4,3,2,1,0:T(8,128)S(1)}, u32[]{:S(2)}, u32[]{:S(2)}) collective-permute-start(f32[1,2,2,32,128]{4,3,2,1,0:T(8,128)S(1)} %get-tuple-element.59), channel_id=1, source_target_pairs={{0,4},{4,0},{1,5},{5,1},{2,6},{6,2},{3,7},{7,3},{8,12},{12,8},{9,1... | collective-permute-start | bytes 196616 | tf_op jit(solution)/shard_map/ppermute | solution.py:758
  47.7 2.0 %collective-permute-start.13 = (f32[2,2,32,128]{3,2,1,0:T(8,128)S(1)}, f32[2,2,32,128]{3,2,1,0:T(8,128)S(1)}, u32[]{:S(2)}, u32[]{:S(2)}) collective-permute-start(f32[2,2,32,128]{3,2,1,0:T(8,128)S(1)} %shard_map.136), channel_id=1, source_target_pairs={{0,16},{8,24},{16,0},{24,8},{1,17},{9,25},{17,1},{25,9},{2,18},{10... | collective-permute-start | bytes 196616 | tf_op jit(solution)/shard_map/ppermute | solution.py:764
  49.7 2.3 %collective-permute-start.15 = (f32[2,2,32,128]{3,2,1,0:T(8,128)S(1)}, f32[2,2,32,128]{3,2,1,0:T(8,128)S(1)}, u32[]{:S(2)}, u32[]{:S(2)}) collective-permute-start(f32[2,2,32,128]{3,2,1,0:T(8,128)S(1)} %shard_map.137), channel_id=1, source_target_pairs={{0,24},{8,16},{16,8},{24,0},{1,25},{9,17},{17,9},{25,1},{2,26},{10... | collective-permute-start | bytes 196616 | tf_op jit(solution)/shard_map/ppermute | solution.py:764
  52.2 2.2 %collective-permute-done.13.refs_0_ = f32[2,2,32,128]{3,2,1,0:T(8,128)S(1)} collective-permute-done((f32[2,2,32,128]{3,2,1,0:T(8,128)S(1)}, f32[2,2,32,128]{3,2,1,0:T(8,128)S(1)}, u32[]{:S(2)}, u32[]{:S(2)}) %collective-permute-start.13) | collective-permute-done | bytes 65568 | tf_op jit(solution)/shard_map/ppermute | solution.py:764
  54.4 1.4 %collective-permute-done.15.refs_1_ = f32[2,2,32,128]{3,2,1,0:T(8,128)S(1)} collective-permute-done((f32[2,2,32,128]{3,2,1,0:T(8,128)S(1)}, f32[2,2,32,128]{3,2,1,0:T(8,128)S(1)}, u32[]{:S(2)}, u32[]{:S(2)}) %collective-permute-start.15) | collective-permute-done | bytes 65568 | tf_op jit(solution)/shard_map/ppermute | solution.py:764
  57.0 11.4 %all_to_all.5.tiles = f32[32,1,128]{2,1,0:T(1,128)S(1)} all-to-all(f32[32,1,128]{2,1,0:T(1,128)S(1)} %broadcast_in_dim.3), channel_id=1, replica_groups=mesh['src'=4,'gx'=2,'gy'=4] {'src','gx','gy'}, dimensions={0} | all-to-all | bytes 32768 | tf_op jit(solution)/shard_map/all_to_all | solution.py:848
  68.5 1.0 %shard_map.142 = (f32[8,32,32]{2,1,0:T(8,128)}, f32[8,32,32]{2,1,0:T(8,128)}, f32[2]{0:T(128)}) custom-call(f32[32,1,128]{2,1,0:T(1,128)S(1)} %all_to_all.5.tiles, f32[8,32,32]{2,1,0:T(8,128)S(1)} %get-tuple-element.61.w_k, f32[8,32,32]{2,1,0:T(8,128)S(1)} %get-tuple-element.62.w_a, f32[8,32,32]{2,1,0:T(8,128)S(1)} %copy-done.1, f32[8,32,32]{2,1,0:T(8,128)S(1)} %copy-done.2), custom_call_target="tpu_custom_call" | custom-call | tf_op jit(solution)/shard_map/pallas_call | solution.py:728
  (56 shorter events, 6.6 us)
Async XLA Ops:
  0.6 10.3 %collective-permute-start = (s32[8,32,128]{2,1,0:T(8,128)}, s32[8,32,128]{2,1,0:T(8,128)S(1)}, u32[]{:S(2)}, u32[]{:S(2)}) collective-permute-start(s32[8,32,128]{2,1,0:T(8,128)} %refs_1_.3), channel_id=1, source_target_pairs={{0,4},{4,0},{1,5},{5,1},{2,6},{6,2},{3,7},{7,3},{8,12},{12,8},{9,1... | collective-permute-start | bytes 393224 | tf_op jit(solution)/shard_map/ppermute | solution.py:758
  5.5 5.4 %copy-start.8 = (s32[1024]{0:T(1024)S(1)}, s32[1024]{0:T(1024)}, u32[]{:S(2)}) copy-start(s32[1024]{0:T(1024)} %param.14) | copy-start | bytes 12292
  5.5 11.3 %collective-permute-start.1 = (f32[20,32,128]{2,1,0:T(8,128)}, f32[20,32,128]{2,1,0:T(8,128)S(1)}, u32[]{:S(2)}, u32[]{:S(2)}) collective-permute-start(f32[20,32,128]{2,1,0:T(8,128)} %get-tuple-element.34), channel_id=1, source_target_pairs={{0,4},{4,0},{1,5},{5,1},{2,6},{6,2},{3,7},{7,3},{8,12},{12,8},{9,1... | collective-permute-start | bytes 983048 | tf_op jit(solution)/shard_map/ppermute | solution.py:758
  5.6 7.5 %collective-permute-start.4 = (f32[4,32,128]{2,1,0:T(8,128)}, f32[4,32,128]{2,1,0:T(8,128)S(1)}, u32[]{:S(2)}, u32[]{:S(2)}) collective-permute-start(f32[4,32,128]{2,1,0:T(8,128)} %get-tuple-element.35), channel_id=1, source_target_pairs={{0,24},{8,16},{16,8},{24,0},{1,25},{9,17},{17,9},{25,1},{2,26},{10... | collective-permute-start | bytes 196616 | tf_op jit(solution)/shard_map/ppermute | solution.py:764
  9.7 5.5 %collective-permute-start.3 = (f32[4,32,128]{2,1,0:T(8,128)}, f32[4,32,128]{2,1,0:T(8,128)S(1)}, u32[]{:S(2)}, u32[]{:S(2)}) collective-permute-start(f32[4,32,128]{2,1,0:T(8,128)} %get-tuple-element.35), channel_id=1, source_target_pairs={{0,16},{8,24},{16,0},{24,8},{1,17},{9,25},{17,1},{25,9},{2,18},{10... | collective-permute-start | bytes 196616 | tf_op jit(solution)/shard_map/ppermute | solution.py:764
  9.7 5.5 %collective-permute-start.2 = (f32[4,32,128]{2,1,0:T(8,128)}, f32[4,32,128]{2,1,0:T(8,128)S(1)}, u32[]{:S(2)}, u32[]{:S(2)}) collective-permute-start(f32[4,32,128]{2,1,0:T(8,128)} %get-tuple-element.35), channel_id=1, source_target_pairs={{0,8},{8,0},{16,24},{24,16},{1,9},{9,1},{17,25},{25,17},{2,10},{10... | collective-permute-start | bytes 196616 | tf_op jit(solution)/shard_map/ppermute | solution.py:764
  13.1 3.7 %copy-start = (f32[4,8,32,128]{3,2,1,0:T(8,128)S(1)}, f32[4,8,32,128]{3,2,1,0:T(8,128)}, u32[]{:S(2)}) copy-start(f32[4,8,32,128]{3,2,1,0:T(8,128)} %refs_0_.2) | copy-start | bytes 1572868
  15.2 5.8 %collective-permute-start.6 = (f32[12,32,128]{2,1,0:T(8,128)S(1)}, f32[12,32,128]{2,1,0:T(8,128)S(1)}, u32[]{:S(2)}, u32[]{:S(2)}) collective-permute-start(f32[12,32,128]{2,1,0:T(8,128)S(1)} %shard_map.123.refs_4_.joined), channel_id=1, source_target_pairs={{0,4},{4,0},{1,5},{5,1},{2,6},{6,2},{3,7},{7,3},{8,12},{12,8},{9,1... | collective-permute-start | bytes 589832 | tf_op jit(solution)/shard_map/ppermute | solution.py:758
  17.4 4.0 %collective-permute-start.5 = (f32[2,16,32,128]{3,2,1,0:T(8,128)S(1)}, f32[2,16,32,128]{3,2,1,0:T(8,128)S(1)}, u32[]{:S(2)}, u32[]{:S(2)}) collective-permute-start(f32[2,16,32,128]{3,2,1,0:T(8,128)S(1)} %get-tuple-element.38.refs_1_.refs_3_), channel_id=1, source_target_pairs={{0,1},{1,0},{2,3},{3,2},{4,5},{5,4},{6,7},{7,6},{8,9},{9,8},{10,11... | collective-permute-start | bytes 1572872 | tf_op jit(solution)/shard_map/ppermute | solution.py:761
  21.4 2.0 %collective-permute-start.8 = (f32[2,16,32,128]{3,2,1,0:T(8,128)S(1)}, f32[2,16,32,128]{3,2,1,0:T(8,128)S(1)}, u32[]{:S(2)}, u32[]{:S(2)}) collective-permute-start(f32[2,16,32,128]{3,2,1,0:T(8,128)S(1)} %shard_map.126.refs_3_.refs_0_.vector), channel_id=1, source_target_pairs={{0,1},{1,0},{2,3},{3,2},{4,5},{5,4},{6,7},{7,6},{8,9},{9,8},{10,11... | collective-permute-start | bytes 1572872 | tf_op jit(solution)/shard_map/ppermute | solution.py:761
  21.5 3.5 %copy-start.6 = (f32[16]{0:T(128)S(1)}, f32[16]{0:T(128)}, u32[]{:S(2)}) copy-start(f32[16]{0:T(128)} %kap_table.1) | copy-start | bytes 196
  21.5 5.8 %collective-permute-start.7 = (f32[2,4,24,128]{3,2,1,0:T(8,128)S(1)}, f32[2,4,24,128]{3,2,1,0:T(8,128)S(1)}, u32[]{:S(2)}, u32[]{:S(2)}) collective-permute-start(f32[2,4,24,128]{3,2,1,0:T(8,128)S(1)} %shard_map.127.refs_2_), channel_id=1, source_target_pairs={{0,2},{1,3},{2,0},{3,1},{4,6},{5,7},{6,4},{7,5},{8,10},{9,11},{10,... | collective-permute-start | bytes 294920 | tf_op jit(solution)/shard_map/ppermute | solution.py:785
  23.4 5.5 %collective-permute-start.9 = (f32[2,4,24,128]{3,2,1,0:T(8,128)S(1)}, f32[2,4,24,128]{3,2,1,0:T(8,128)S(1)}, u32[]{:S(2)}, u32[]{:S(2)}) collective-permute-start(f32[2,4,24,128]{3,2,1,0:T(8,128)S(1)} %shard_map.128.refs_6_), channel_id=1, source_target_pairs={{0,2},{1,3},{2,0},{3,1},{4,6},{5,7},{6,4},{7,5},{8,10},{9,11},{10,... | collective-permute-start | bytes 294920 | tf_op jit(solution)/shard_map/ppermute | solution.py:785
  32.7 4.2 %collective-permute-start.10 = (f32[104,128]{1,0:T(8,128)S(1)}, f32[104,128]{1,0:T(8,128)S(1)}, u32[]{:S(2)}, u32[]{:S(2)}) collective-permute-start(f32[104,128]{1,0:T(8,128)S(1)} %get-tuple-element.53.sent), channel_id=1, source_target_pairs={{0,2},{1,3},{2,0},{3,1},{4,6},{5,7},{6,4},{7,5},{8,10},{9,11},{10,... | collective-permute-start | bytes 159752 | tf_op jit(solution)/shard_map/ppermute | solution.py:785
  40.7 2.0 %collective-permute-start.11 = (f32[2,16,32,128]{3,2,1,0:T(8,128)S(1)}, f32[2,16,32,128]{3,2,1,0:T(8,128)S(1)}, u32[]{:S(2)}, u32[]{:S(2)}) collective-permute-start(f32[2,16,32,128]{3,2,1,0:T(8,128)S(1)} %get-tuple-element.55), channel_id=1, source_target_pairs={{0,1},{1,0},{2,3},{3,2},{4,5},{5,4},{6,7},{7,6},{8,9},{9,8},{10,11... | collective-permute-start | bytes 1572872 | tf_op jit(solution)/shard_map/ppermute | solution.py:761
  43.0 4.7 %collective-permute-start.12 = (f32[1,2,2,32,128]{4,3,2,1,0:T(8,128)S(1)}, f32[1,2,2,32,128]{4,3,2,1,0:T(8,128)S(1)}, u32[]{:S(2)}, u32[]{:S(2)}) collective-permute-start(f32[1,2,2,32,128]{4,3,2,1,0:T(8,128)S(1)} %get-tuple-element.57), channel_id=1, source_target_pairs={{0,4},{4,0},{1,5},{5,1},{2,6},{6,2},{3,7},{7,3},{8,12},{12,8},{9,1... | collective-permute-start | bytes 196616 | tf_op jit(solution)/shard_map/ppermute | solution.py:758
  44.6 5.1 %collective-permute-start.14 = (f32[1,2,2,32,128]{4,3,2,1,0:T(8,128)S(1)}, f32[1,2,2,32,128]{4,3,2,1,0:T(8,128)S(1)}, u32[]{:S(2)}, u32[]{:S(2)}) collective-permute-start(f32[1,2,2,32,128]{4,3,2,1,0:T(8,128)S(1)} %get-tuple-element.58), channel_id=1, source_target_pairs={{0,4},{4,0},{1,5},{5,1},{2,6},{6,2},{3,7},{7,3},{8,12},{12,8},{9,1... | collective-permute-start | bytes 196616 | tf_op jit(solution)/shard_map/ppermute | solution.py:758
  45.1 7.0 %collective-permute-start.17 = (f32[1,2,2,32,128]{4,3,2,1,0:T(8,128)S(1)}, f32[1,2,2,32,128]{4,3,2,1,0:T(8,128)S(1)}, u32[]{:S(2)}, u32[]{:S(2)}) collective-permute-start(f32[1,2,2,32,128]{4,3,2,1,0:T(8,128)S(1)} %get-tuple-element.59), channel_id=1, source_target_pairs={{0,4},{4,0},{1,5},{5,1},{2,6},{6,2},{3,7},{7,3},{8,12},{12,8},{9,1... | collective-permute-start | bytes 196616 | tf_op jit(solution)/shard_map/ppermute | solution.py:758
  46.6 5.6 %collective-permute-start.16 = (f32[1,2,2,32,128]{4,3,2,1,0:T(8,128)S(1)}, f32[1,2,2,32,128]{4,3,2,1,0:T(8,128)S(1)}, u32[]{:S(2)}, u32[]{:S(2)}) collective-permute-start(f32[1,2,2,32,128]{4,3,2,1,0:T(8,128)S(1)} %get-tuple-element.56.refs_2_), channel_id=1, source_target_pairs={{0,4},{4,0},{1,5},{5,1},{2,6},{6,2},{3,7},{7,3},{8,12},{12,8},{9,1... | collective-permute-start | bytes 196616 | tf_op jit(solution)/shard_map/ppermute | solution.py:758
  47.7 6.7 %collective-permute-start.13 = (f32[2,2,32,128]{3,2,1,0:T(8,128)S(1)}, f32[2,2,32,128]{3,2,1,0:T(8,128)S(1)}, u32[]{:S(2)}, u32[]{:S(2)}) collective-permute-start(f32[2,2,32,128]{3,2,1,0:T(8,128)S(1)} %shard_map.136), channel_id=1, source_target_pairs={{0,16},{8,24},{16,0},{24,8},{1,17},{9,25},{17,1},{25,9},{2,18},{10... | collective-permute-start | bytes 196616 | tf_op jit(solution)/shard_map/ppermute | solution.py:764
  49.7 6.1 %collective-permute-start.15 = (f32[2,2,32,128]{3,2,1,0:T(8,128)S(1)}, f32[2,2,32,128]{3,2,1,0:T(8,128)S(1)}, u32[]{:S(2)}, u32[]{:S(2)}) collective-permute-start(f32[2,2,32,128]{3,2,1,0:T(8,128)S(1)} %shard_map.137), channel_id=1, source_target_pairs={{0,24},{8,16},{16,8},{24,0},{1,25},{9,17},{17,9},{25,1},{2,26},{10... | collective-permute-start | bytes 196616 | tf_op jit(solution)/shard_map/ppermute | solution.py:764
  52.0 4.5 %collective-permute-start.18 = (f32[2,2,32,128]{3,2,1,0:T(8,128)S(1)}, f32[2,2,32,128]{3,2,1,0:T(8,128)S(1)}, u32[]{:S(2)}, u32[]{:S(2)}) collective-permute-start(f32[2,2,32,128]{3,2,1,0:T(8,128)S(1)} %shard_map.140), channel_id=1, source_target_pairs={{0,8},{8,0},{16,24},{24,16},{1,9},{9,1},{17,25},{25,17},{2,10},{10... | collective-permute-start | bytes 196616 | tf_op jit(solution)/shard_map/ppermute | solution.py:764
  52.2 4.4 %copy-start.4 = (f32[8,32,32]{2,1,0:T(8,128)S(1)}, f32[8,32,32]{2,1,0:T(8,128)}, u32[]{:S(2)}) copy-start(f32[8,32,32]{2,1,0:T(8,128)} %refs_6_.1) | copy-start | bytes 98308
  52.2 4.4 %copy-start.5 = (f32[8,32,32]{2,1,0:T(8,128)S(1)}, f32[8,32,32]{2,1,0:T(8,128)}, u32[]{:S(2)}) copy-start(f32[8,32,32]{2,1,0:T(8,128)} %refs_7_.1) | copy-start | bytes 98308
  (4 other events, 9.6 us)

commit v25 on v21

--- a/solution.py
+++ b/solution.py
@@ -549,7 +549,7 @@
         return carry[0] + folded(part), carry[1] + folded(part * phi[i + 1])
 
     zero = jnp.zeros((8, lanes), jnp.float32)
-    seen, cross = lax.fori_loop(0, planes, add_up, (zero, zero), unroll=8)
+    seen, cross = lax.fori_loop(0, planes, add_up, (zero, zero), unroll=UNROLL)
     first = (2 * cy - HALO) * (1 - y) + HALO * y
     size = GROUP * REACH
     for g in range(planes // GROUP):
@@ -614,7 +614,7 @@
             message[f, i] = ref[i, pl.ds(base + cy * (1 - c), cy), :]
         return carry
 
-    lax.fori_loop(0, planes, product, 0, unroll=8)
+    lax.fori_loop(0, planes, product, 0, unroll=UNROLL)
 
 
 def packed_slabs(own, came, half, choices, outs):

time: 69.7 us -> 70.1 us (level)
  no operation moved by 1% of the time
where the time goes in v25:
time: 70.1 us; the launch traced here: 69.9 us
  starting transfers between devices  22.8 us (33%)
  Pallas kernels  19.5 us (28%)
  waiting for transfers between devices  14.7 us (21%)
  blocking collectives  11.2 us (16%)
  between operations  1.61 us (2%)
    pallas_call x25, Pallas kernels, run(): pl.pallas_call(body if waits else kernel, out_shape=tuple(outs), in_specs...  19.5 us
    all_to_all x1, blocking collectives, per_device_paired(): lax.all_to_all(jnp.broadcast_to(tile, (8 * n, 1, 128)), everyone, 0, 0)  11.2 us
    ppermute x6, starting transfers between devices, along_z(): return lax.ppermute(value, 'src', [(i, i ^ k) for i in range(n)])  8.91 us
    ppermute x7, starting transfers between devices, swap_x(): return lax.ppermute(value, 'gx', [(0, 1), (1, 0)])  8.89 us
    ppermute x6, waiting for transfers between devices, along_z(): return lax.ppermute(value, 'src', [(i, i ^ k) for i in range(n)])  6.67 us
    ppermute x3, starting transfers between devices, across_y(): return lax.ppermute(value, 'gy', [(i, (i + 2) % 4) for i in range(4)])  4.75 us
    ppermute x7, waiting for transfers between devices, swap_x(): return lax.ppermute(value, 'gx', [(0, 1), (1, 0)])  3.11 us
    ppermute x3, waiting for transfers between devices, across_y(): return lax.ppermute(value, 'gy', [(i, (i + 2) % 4) for i in range(4)])  2.85 us
  transfers between devices with their start and end apart: 19, of which 9 were waited for; matrix products, arithmetic and copies ran while one was open for 0% of the time, Pallas kernels for 14%

profile of v25, /device:TPU:0, one launch (start us, length us, event | category | flops | bytes accessed | tf_op | source)
XLA Modules:
  0.0 69.9 jit_solution(5274121708373613480)
XLA Ops:
  0.6 3.0 %collective-permute-start = (s32[8,32,128]{2,1,0:T(8,128)}, s32[8,32,128]{2,1,0:T(8,128)S(1)}, u32[]{:S(2)}, u32[]{:S(2)}) collective-permute-start(s32[8,32,128]{2,1,0:T(8,128)} %refs_1_.3), channel_id=1, source_target_pairs={{0,4},{4,0},{1,5},{5,1},{2,6},{6,2},{3,7},{7,3},{8,12},{12,8},{9,1... | collective-permute-start | bytes 393224 | tf_op jit(solution)/shard_map/ppermute | solution.py:751
  3.6 1.9 %shard_map.122 = (f32[4,32,128]{2,1,0:T(8,128)}, f32[20,32,128]{2,1,0:T(8,128)}) custom-call(f32[4,8,32,128]{3,2,1,0:T(8,128)} %refs_0_.2, f32[8,32,32]{2,1,0:T(8,128)} %vk.5, f32[8,32,32]{2,1,0:T(8,128)} %va.5), custom_call_target="tpu_custom_call" | custom-call | tf_op jit(solution)/shard_map/pallas_call | solution.py:721
  5.6 4.1 %collective-permute-start.4 = (f32[4,32,128]{2,1,0:T(8,128)}, f32[4,32,128]{2,1,0:T(8,128)S(1)}, u32[]{:S(2)}, u32[]{:S(2)}) collective-permute-start(f32[4,32,128]{2,1,0:T(8,128)} %get-tuple-element.31), channel_id=1, source_target_pairs={{0,24},{8,16},{16,8},{24,0},{1,25},{9,17},{17,9},{25,1},{2,26},{10... | collective-permute-start | bytes 196616 | tf_op jit(solution)/shard_map/ppermute | solution.py:757
  11.0 2.1 %shard_map.121 = (f32[16,72,128]{2,1,0:T(8,128)S(1)}, f32[1,128]{1,0:T(1,128)S(1)}) custom-call(s32[1,1024]{1,0:T(1,128)S(1)} %bitcast.3, f32[1]{0:T(128)S(6)} %copy.13.refs_1_, s32[8,32,128]{2,1,0:T(8,128)S(1)} %collective-permute-done.refs_2_.refs_3_), custom_call_target="tpu_custom_call" | custom-call | flops 301989888 | bytes 589824 | tf_op jit(solution)/shard_map/pallas_call | solution.py:721
  13.1 2.1 %collective-permute-done.3.refs_1_ = f32[4,32,128]{2,1,0:T(8,128)S(1)} collective-permute-done((f32[4,32,128]{2,1,0:T(8,128)}, f32[4,32,128]{2,1,0:T(8,128)S(1)}, u32[]{:S(2)}, u32[]{:S(2)}) %collective-permute-start.3) | collective-permute-done | bytes 65568 | tf_op jit(solution)/shard_map/ppermute | solution.py:757
  15.2 1.6 %collective-permute-start.6 = (f32[12,32,128]{2,1,0:T(8,128)S(1)}, f32[12,32,128]{2,1,0:T(8,128)S(1)}, u32[]{:S(2)}, u32[]{:S(2)}) collective-permute-start(f32[12,32,128]{2,1,0:T(8,128)S(1)} %shard_map.123.refs_4_.joined), channel_id=1, source_target_pairs={{0,4},{4,0},{1,5},{5,1},{2,6},{6,2},{3,7},{7,3},{8,12},{12,8},{9,1... | collective-permute-start | bytes 589832 | tf_op jit(solution)/shard_map/ppermute | solution.py:751
  17.9 3.1 %collective-permute-done.6.refs_2_ = f32[12,32,128]{2,1,0:T(8,128)S(1)} collective-permute-done((f32[12,32,128]{2,1,0:T(8,128)S(1)}, f32[12,32,128]{2,1,0:T(8,128)S(1)}, u32[]{:S(2)}, u32[]{:S(2)}) %collective-permute-start.6) | collective-permute-done | bytes 196640 | tf_op jit(solution)/shard_map/ppermute | solution.py:751
  21.5 1.6 %collective-permute-start.7 = (f32[2,4,24,128]{3,2,1,0:T(8,128)S(1)}, f32[2,4,24,128]{3,2,1,0:T(8,128)S(1)}, u32[]{:S(2)}, u32[]{:S(2)}) collective-permute-start(f32[2,4,24,128]{3,2,1,0:T(8,128)S(1)} %shard_map.127.refs_2_), channel_id=1, source_target_pairs={{0,2},{1,3},{2,0},{3,1},{4,6},{5,7},{6,4},{7,5},{8,10},{9,11},{10,... | collective-permute-start | bytes 294920 | tf_op jit(solution)/shard_map/ppermute | solution.py:778
  23.4 1.6 %collective-permute-start.9 = (f32[2,4,24,128]{3,2,1,0:T(8,128)S(1)}, f32[2,4,24,128]{3,2,1,0:T(8,128)S(1)}, u32[]{:S(2)}, u32[]{:S(2)}) collective-permute-start(f32[2,4,24,128]{3,2,1,0:T(8,128)S(1)} %shard_map.128.refs_6_), channel_id=1, source_target_pairs={{0,2},{1,3},{2,0},{3,1},{4,6},{5,7},{6,4},{7,5},{8,10},{9,11},{10,... | collective-permute-start | bytes 294920 | tf_op jit(solution)/shard_map/ppermute | solution.py:778
  25.0 2.3 %shard_map.129 = (f32[18,72,128]{2,1,0:T(8,128)S(1)}, f32[16,72,128]{2,1,0:T(8,128)S(1)}, f32[17,72,128]{2,1,0:T(8,128)S(1)}, f32[16,72,128]{2,1,0:T(8,128)S(1)}...) custom-call(f32[16]{0:T(128)S(1)} %copy-done.6, f32[16]{0:T(128)S(1)} %copy-done.7, ...), custom_call_target="tpu_custom_call" | custom-call | flops 1000000000 | bytes 67108864 | tf_op jit(solution)/shard_map/pallas_call | solution.py:721
  27.3 0.8 %shard_map.130 = (f32[16,72,128]{2,1,0:T(8,128)S(1)}, f32[17,72,128]{2,1,0:T(8,128)S(1)}, f32[16,72,128]{2,1,0:T(8,128)S(1)}, f32[16,72,128]{2,1,0:T(8,128)S(1)}) custom-call(f32[16]{0:T(128)S(1)} %copy-done.6, f32[16]{0:T(128)S(1)} %copy-done.7, f32[2,4,24,128]{3,2,1,0:T(8,128)S(1)} %collective-permute-done.7.edge.refs_2_, ...), custom_call_target="tpu_custom_call" | custom-call | tf_op jit(solution)/shard_map/pallas_call | solution.py:721
  28.9 3.8 %shard_map.132 = (f32[16,72,128]{2,1,0:T(8,128)S(1)}, f32[104,128]{1,0:T(8,128)S(1)}) custom-call(f32[18,72,128]{2,1,0:T(8,128)S(1)} %get-tuple-element.41.phi, f32[16,72,128]{2,1,0:T(8,128)S(1)} %get-tuple-element.42.phi_y, f32[16,72,128]{2,1,0:T(8,128)S(1)} %get-tuple-element.43.phi_z, f32[16,72,128]{2,1,0:T(8,128)S(1)} %get-tuple-element.44.diag, ...), custom_call_target="tpu_custom_call" | custom-call | tf_op jit(solution)/shard_map/pallas_call | solution.py:721
  32.7 1.6 %collective-permute-start.10 = (f32[104,128]{1,0:T(8,128)S(1)}, f32[104,128]{1,0:T(8,128)S(1)}, u32[]{:S(2)}, u32[]{:S(2)}) collective-permute-start(f32[104,128]{1,0:T(8,128)S(1)} %get-tuple-element.49.sent), channel_id=1, source_target_pairs={{0,2},{1,3},{2,0},{3,1},{4,6},{5,7},{6,4},{7,5},{8,10},{9,11},{10,... | collective-permute-start | bytes 159752 | tf_op jit(solution)/shard_map/ppermute | solution.py:778
  34.2 2.6 %collective-permute-done.10.came = f32[104,128]{1,0:T(8,128)S(1)} collective-permute-done((f32[104,128]{1,0:T(8,128)S(1)}, f32[104,128]{1,0:T(8,128)S(1)}, u32[]{:S(2)}, u32[]{:S(2)}) %collective-permute-start.10) | collective-permute-done | bytes 53280 | tf_op jit(solution)/shard_map/ppermute | solution.py:778
  36.9 4.3 %shard_map.133 = (f32[2,16,32,128]{3,2,1,0:T(8,128)S(1)}, f32[2,16,32,128]{3,2,1,0:T(8,128)S(1)}) custom-call(f32[18,72,128]{2,1,0:T(8,128)S(1)} %get-tuple-element.41.phi, f32[16,72,128]{2,1,0:T(8,128)S(1)} %get-tuple-element.42.phi_y, f32[16,72,128]{2,1,0:T(8,128)S(1)} %get-tuple-element.43.phi_z, f32[16,72,128]{2,1,0:T(8,128)S(1)} %get-tuple-element.48.change, ...), custom_call_target="tpu_custom_call" | custom-call | tf_op jit(solution)/shard_map/pallas_call | solution.py:721
  41.2 1.9 %collective-permute-done.11.came.refs_1_ = f32[2,16,32,128]{3,2,1,0:T(8,128)S(1)} collective-permute-done((f32[2,16,32,128]{3,2,1,0:T(8,128)S(1)}, f32[2,16,32,128]{3,2,1,0:T(8,128)S(1)}, u32[]{:S(2)}, u32[]{:S(2)}) %collective-permute-start.11) | collective-permute-done | bytes 524320 | tf_op jit(solution)/shard_map/ppermute | solution.py:754
  43.4 1.6 %collective-permute-start.12 = (f32[1,2,2,32,128]{4,3,2,1,0:T(8,128)S(1)}, f32[1,2,2,32,128]{4,3,2,1,0:T(8,128)S(1)}, u32[]{:S(2)}, u32[]{:S(2)}) collective-permute-start(f32[1,2,2,32,128]{4,3,2,1,0:T(8,128)S(1)} %shard_map.135.refs_2_), channel_id=1, source_target_pairs={{0,4},{4,0},{1,5},{5,1},{2,6},{6,2},{3,7},{7,3},{8,12},{12,8},{9,1... | collective-permute-start | bytes 196616 | tf_op jit(solution)/shard_map/ppermute | solution.py:751
  45.7 1.6 %collective-permute-start.17 = (f32[1,2,2,32,128]{4,3,2,1,0:T(8,128)S(1)}, f32[1,2,2,32,128]{4,3,2,1,0:T(8,128)S(1)}, u32[]{:S(2)}, u32[]{:S(2)}) collective-permute-start(f32[1,2,2,32,128]{4,3,2,1,0:T(8,128)S(1)} %shard_map.136.refs_2_), channel_id=1, source_target_pairs={{0,4},{4,0},{1,5},{5,1},{2,6},{6,2},{3,7},{7,3},{8,12},{12,8},{9,1... | collective-permute-start | bytes 196616 | tf_op jit(solution)/shard_map/ppermute | solution.py:751
  48.3 2.0 %collective-permute-start.13 = (f32[2,2,32,128]{3,2,1,0:T(8,128)S(1)}, f32[2,2,32,128]{3,2,1,0:T(8,128)S(1)}, u32[]{:S(2)}, u32[]{:S(2)}) collective-permute-start(f32[2,2,32,128]{3,2,1,0:T(8,128)S(1)} %shard_map.139), channel_id=1, source_target_pairs={{0,16},{8,24},{16,0},{24,8},{1,17},{9,25},{17,1},{25,9},{2,18},{10... | collective-permute-start | bytes 196616 | tf_op jit(solution)/shard_map/ppermute | solution.py:757
  50.3 2.1 %collective-permute-start.15 = (f32[2,2,32,128]{3,2,1,0:T(8,128)S(1)}, f32[2,2,32,128]{3,2,1,0:T(8,128)S(1)}, u32[]{:S(2)}, u32[]{:S(2)}) collective-permute-start(f32[2,2,32,128]{3,2,1,0:T(8,128)S(1)} %shard_map.140), channel_id=1, source_target_pairs={{0,24},{8,16},{16,8},{24,0},{1,25},{9,17},{17,9},{25,1},{2,26},{10... | collective-permute-start | bytes 196616 | tf_op jit(solution)/shard_map/ppermute | solution.py:757
  52.7 2.5 %collective-permute-done.13.refs_0_ = f32[2,2,32,128]{3,2,1,0:T(8,128)S(1)} collective-permute-done((f32[2,2,32,128]{3,2,1,0:T(8,128)S(1)}, f32[2,2,32,128]{3,2,1,0:T(8,128)S(1)}, u32[]{:S(2)}, u32[]{:S(2)}) %collective-permute-start.13) | collective-permute-done | bytes 65568 | tf_op jit(solution)/shard_map/ppermute | solution.py:757
  55.1 1.4 %collective-permute-done.15.refs_1_ = f32[2,2,32,128]{3,2,1,0:T(8,128)S(1)} collective-permute-done((f32[2,2,32,128]{3,2,1,0:T(8,128)S(1)}, f32[2,2,32,128]{3,2,1,0:T(8,128)S(1)}, u32[]{:S(2)}, u32[]{:S(2)}) %collective-permute-start.15) | collective-permute-done | bytes 65568 | tf_op jit(solution)/shard_map/ppermute | solution.py:757
  57.7 11.2 %all_to_all.5.tiles = f32[32,1,128]{2,1,0:T(1,128)S(1)} all-to-all(f32[32,1,128]{2,1,0:T(1,128)S(1)} %broadcast_in_dim.3), channel_id=1, replica_groups=mesh['src'=4,'gx'=2,'gy'=4] {'src','gx','gy'}, dimensions={0} | all-to-all | bytes 32768 | tf_op jit(solution)/shard_map/all_to_all | solution.py:841
  68.9 1.0 %shard_map.145 = (f32[8,32,32]{2,1,0:T(8,128)}, f32[8,32,32]{2,1,0:T(8,128)}, f32[2]{0:T(128)}) custom-call(f32[32,1,128]{2,1,0:T(1,128)S(1)} %all_to_all.5.tiles, f32[8,32,32]{2,1,0:T(8,128)S(1)} %get-tuple-element.53.w_k, f32[8,32,32]{2,1,0:T(8,128)S(1)} %get-tuple-element.54.w_a, f32[8,32,32]{2,1,0:T(8,128)S(1)} %copy-done.1, f32[8,32,32]{2,1,0:T(8,128)S(1)} %copy-done.2), custom_call_target="tpu_custom_call" | custom-call | tf_op jit(solution)/shard_map/pallas_call | solution.py:721
  (59 shorter events, 6.6 us)
Async XLA Ops:
  0.6 10.3 %collective-permute-start = (s32[8,32,128]{2,1,0:T(8,128)}, s32[8,32,128]{2,1,0:T(8,128)S(1)}, u32[]{:S(2)}, u32[]{:S(2)}) collective-permute-start(s32[8,32,128]{2,1,0:T(8,128)} %refs_1_.3), channel_id=1, source_target_pairs={{0,4},{4,0},{1,5},{5,1},{2,6},{6,2},{3,7},{7,3},{8,12},{12,8},{9,1... | collective-permute-start | bytes 393224 | tf_op jit(solution)/shard_map/ppermute | solution.py:751
  5.5 5.4 %copy-start.8 = (s32[1024]{0:T(1024)S(1)}, s32[1024]{0:T(1024)}, u32[]{:S(2)}) copy-start(s32[1024]{0:T(1024)} %param.14) | copy-start | bytes 12292
  5.5 11.3 %collective-permute-start.1 = (f32[20,32,128]{2,1,0:T(8,128)}, f32[20,32,128]{2,1,0:T(8,128)S(1)}, u32[]{:S(2)}, u32[]{:S(2)}) collective-permute-start(f32[20,32,128]{2,1,0:T(8,128)} %get-tuple-element.30), channel_id=1, source_target_pairs={{0,4},{4,0},{1,5},{5,1},{2,6},{6,2},{3,7},{7,3},{8,12},{12,8},{9,1... | collective-permute-start | bytes 983048 | tf_op jit(solution)/shard_map/ppermute | solution.py:751
  5.6 7.5 %collective-permute-start.4 = (f32[4,32,128]{2,1,0:T(8,128)}, f32[4,32,128]{2,1,0:T(8,128)S(1)}, u32[]{:S(2)}, u32[]{:S(2)}) collective-permute-start(f32[4,32,128]{2,1,0:T(8,128)} %get-tuple-element.31), channel_id=1, source_target_pairs={{0,24},{8,16},{16,8},{24,0},{1,25},{9,17},{17,9},{25,1},{2,26},{10... | collective-permute-start | bytes 196616 | tf_op jit(solution)/shard_map/ppermute | solution.py:757
  9.7 5.5 %collective-permute-start.3 = (f32[4,32,128]{2,1,0:T(8,128)}, f32[4,32,128]{2,1,0:T(8,128)S(1)}, u32[]{:S(2)}, u32[]{:S(2)}) collective-permute-start(f32[4,32,128]{2,1,0:T(8,128)} %get-tuple-element.31), channel_id=1, source_target_pairs={{0,16},{8,24},{16,0},{24,8},{1,17},{9,25},{17,1},{25,9},{2,18},{10... | collective-permute-start | bytes 196616 | tf_op jit(solution)/shard_map/ppermute | solution.py:757
  9.7 5.5 %collective-permute-start.2 = (f32[4,32,128]{2,1,0:T(8,128)}, f32[4,32,128]{2,1,0:T(8,128)S(1)}, u32[]{:S(2)}, u32[]{:S(2)}) collective-permute-start(f32[4,32,128]{2,1,0:T(8,128)} %get-tuple-element.31), channel_id=1, source_target_pairs={{0,8},{8,0},{16,24},{24,16},{1,9},{9,1},{17,25},{25,17},{2,10},{10... | collective-permute-start | bytes 196616 | tf_op jit(solution)/shard_map/ppermute | solution.py:757
  13.1 3.7 %copy-start = (f32[4,8,32,128]{3,2,1,0:T(8,128)S(1)}, f32[4,8,32,128]{3,2,1,0:T(8,128)}, u32[]{:S(2)}) copy-start(f32[4,8,32,128]{3,2,1,0:T(8,128)} %refs_0_.2) | copy-start | bytes 1572868
  15.2 5.8 %collective-permute-start.6 = (f32[12,32,128]{2,1,0:T(8,128)S(1)}, f32[12,32,128]{2,1,0:T(8,128)S(1)}, u32[]{:S(2)}, u32[]{:S(2)}) collective-permute-start(f32[12,32,128]{2,1,0:T(8,128)S(1)} %shard_map.123.refs_4_.joined), channel_id=1, source_target_pairs={{0,4},{4,0},{1,5},{5,1},{2,6},{6,2},{3,7},{7,3},{8,12},{12,8},{9,1... | collective-permute-start | bytes 589832 | tf_op jit(solution)/shard_map/ppermute | solution.py:751
  17.4 4.0 %collective-permute-start.5 = (f32[2,16,32,128]{3,2,1,0:T(8,128)S(1)}, f32[2,16,32,128]{3,2,1,0:T(8,128)S(1)}, u32[]{:S(2)}, u32[]{:S(2)}) collective-permute-start(f32[2,16,32,128]{3,2,1,0:T(8,128)S(1)} %get-tuple-element.34.refs_1_.refs_3_), channel_id=1, source_target_pairs={{0,1},{1,0},{2,3},{3,2},{4,5},{5,4},{6,7},{7,6},{8,9},{9,8},{10,11... | collective-permute-start | bytes 1572872 | tf_op jit(solution)/shard_map/ppermute | solution.py:754
  21.4 2.0 %collective-permute-start.8 = (f32[2,16,32,128]{3,2,1,0:T(8,128)S(1)}, f32[2,16,32,128]{3,2,1,0:T(8,128)S(1)}, u32[]{:S(2)}, u32[]{:S(2)}) collective-permute-start(f32[2,16,32,128]{3,2,1,0:T(8,128)S(1)} %shard_map.126.refs_3_.refs_0_.vector), channel_id=1, source_target_pairs={{0,1},{1,0},{2,3},{3,2},{4,5},{5,4},{6,7},{7,6},{8,9},{9,8},{10,11... | collective-permute-start | bytes 1572872 | tf_op jit(solution)/shard_map/ppermute | solution.py:754
  21.5 3.5 %copy-start.6 = (f32[16]{0:T(128)S(1)}, f32[16]{0:T(128)}, u32[]{:S(2)}) copy-start(f32[16]{0:T(128)} %kap_table.1) | copy-start | bytes 196
  21.5 5.8 %collective-permute-start.7 = (f32[2,4,24,128]{3,2,1,0:T(8,128)S(1)}, f32[2,4,24,128]{3,2,1,0:T(8,128)S(1)}, u32[]{:S(2)}, u32[]{:S(2)}) collective-permute-start(f32[2,4,24,128]{3,2,1,0:T(8,128)S(1)} %shard_map.127.refs_2_), channel_id=1, source_target_pairs={{0,2},{1,3},{2,0},{3,1},{4,6},{5,7},{6,4},{7,5},{8,10},{9,11},{10,... | collective-permute-start | bytes 294920 | tf_op jit(solution)/shard_map/ppermute | solution.py:778
  23.4 5.5 %collective-permute-start.9 = (f32[2,4,24,128]{3,2,1,0:T(8,128)S(1)}, f32[2,4,24,128]{3,2,1,0:T(8,128)S(1)}, u32[]{:S(2)}, u32[]{:S(2)}) collective-permute-start(f32[2,4,24,128]{3,2,1,0:T(8,128)S(1)} %shard_map.128.refs_6_), channel_id=1, source_target_pairs={{0,2},{1,3},{2,0},{3,1},{4,6},{5,7},{6,4},{7,5},{8,10},{9,11},{10,... | collective-permute-start | bytes 294920 | tf_op jit(solution)/shard_map/ppermute | solution.py:778
  32.7 4.2 %collective-permute-start.10 = (f32[104,128]{1,0:T(8,128)S(1)}, f32[104,128]{1,0:T(8,128)S(1)}, u32[]{:S(2)}, u32[]{:S(2)}) collective-permute-start(f32[104,128]{1,0:T(8,128)S(1)} %get-tuple-element.49.sent), channel_id=1, source_target_pairs={{0,2},{1,3},{2,0},{3,1},{4,6},{5,7},{6,4},{7,5},{8,10},{9,11},{10,... | collective-permute-start | bytes 159752 | tf_op jit(solution)/shard_map/ppermute | solution.py:778
  41.1 2.0 %collective-permute-start.11 = (f32[2,16,32,128]{3,2,1,0:T(8,128)S(1)}, f32[2,16,32,128]{3,2,1,0:T(8,128)S(1)}, u32[]{:S(2)}, u32[]{:S(2)}) collective-permute-start(f32[2,16,32,128]{3,2,1,0:T(8,128)S(1)} %get-tuple-element.51), channel_id=1, source_target_pairs={{0,1},{1,0},{2,3},{3,2},{4,5},{5,4},{6,7},{7,6},{8,9},{9,8},{10,11... | collective-permute-start | bytes 1572872 | tf_op jit(solution)/shard_map/ppermute | solution.py:754
  43.4 4.9 %collective-permute-start.12 = (f32[1,2,2,32,128]{4,3,2,1,0:T(8,128)S(1)}, f32[1,2,2,32,128]{4,3,2,1,0:T(8,128)S(1)}, u32[]{:S(2)}, u32[]{:S(2)}) collective-permute-start(f32[1,2,2,32,128]{4,3,2,1,0:T(8,128)S(1)} %shard_map.135.refs_2_), channel_id=1, source_target_pairs={{0,4},{4,0},{1,5},{5,1},{2,6},{6,2},{3,7},{7,3},{8,12},{12,8},{9,1... | collective-permute-start | bytes 196616 | tf_op jit(solution)/shard_map/ppermute | solution.py:751
  45.0 5.3 %collective-permute-start.14 = (f32[1,2,2,32,128]{4,3,2,1,0:T(8,128)S(1)}, f32[1,2,2,32,128]{4,3,2,1,0:T(8,128)S(1)}, u32[]{:S(2)}, u32[]{:S(2)}) collective-permute-start(f32[1,2,2,32,128]{4,3,2,1,0:T(8,128)S(1)} %shard_map.134.refs_2_), channel_id=1, source_target_pairs={{0,4},{4,0},{1,5},{5,1},{2,6},{6,2},{3,7},{7,3},{8,12},{12,8},{9,1... | collective-permute-start | bytes 196616 | tf_op jit(solution)/shard_map/ppermute | solution.py:751
  45.7 6.8 %collective-permute-start.17 = (f32[1,2,2,32,128]{4,3,2,1,0:T(8,128)S(1)}, f32[1,2,2,32,128]{4,3,2,1,0:T(8,128)S(1)}, u32[]{:S(2)}, u32[]{:S(2)}) collective-permute-start(f32[1,2,2,32,128]{4,3,2,1,0:T(8,128)S(1)} %shard_map.136.refs_2_), channel_id=1, source_target_pairs={{0,4},{4,0},{1,5},{5,1},{2,6},{6,2},{3,7},{7,3},{8,12},{12,8},{9,1... | collective-permute-start | bytes 196616 | tf_op jit(solution)/shard_map/ppermute | solution.py:751
  47.4 5.2 %collective-permute-start.16 = (f32[1,2,2,32,128]{4,3,2,1,0:T(8,128)S(1)}, f32[1,2,2,32,128]{4,3,2,1,0:T(8,128)S(1)}, u32[]{:S(2)}, u32[]{:S(2)}) collective-permute-start(f32[1,2,2,32,128]{4,3,2,1,0:T(8,128)S(1)} %shard_map.137.refs_2_), channel_id=1, source_target_pairs={{0,4},{4,0},{1,5},{5,1},{2,6},{6,2},{3,7},{7,3},{8,12},{12,8},{9,1... | collective-permute-start | bytes 196616 | tf_op jit(solution)/shard_map/ppermute | solution.py:751
  48.3 6.8 %collective-permute-start.13 = (f32[2,2,32,128]{3,2,1,0:T(8,128)S(1)}, f32[2,2,32,128]{3,2,1,0:T(8,128)S(1)}, u32[]{:S(2)}, u32[]{:S(2)}) collective-permute-start(f32[2,2,32,128]{3,2,1,0:T(8,128)S(1)} %shard_map.139), channel_id=1, source_target_pairs={{0,16},{8,24},{16,0},{24,8},{1,17},{9,25},{17,1},{25,9},{2,18},{10... | collective-permute-start | bytes 196616 | tf_op jit(solution)/shard_map/ppermute | solution.py:757
  50.3 6.3 %collective-permute-start.15 = (f32[2,2,32,128]{3,2,1,0:T(8,128)S(1)}, f32[2,2,32,128]{3,2,1,0:T(8,128)S(1)}, u32[]{:S(2)}, u32[]{:S(2)}) collective-permute-start(f32[2,2,32,128]{3,2,1,0:T(8,128)S(1)} %shard_map.140), channel_id=1, source_target_pairs={{0,24},{8,16},{16,8},{24,0},{1,25},{9,17},{17,9},{25,1},{2,26},{10... | collective-permute-start | bytes 196616 | tf_op jit(solution)/shard_map/ppermute | solution.py:757
  52.5 4.8 %collective-permute-start.18 = (f32[2,2,32,128]{3,2,1,0:T(8,128)S(1)}, f32[2,2,32,128]{3,2,1,0:T(8,128)S(1)}, u32[]{:S(2)}, u32[]{:S(2)}) collective-permute-start(f32[2,2,32,128]{3,2,1,0:T(8,128)S(1)} %shard_map.143), channel_id=1, source_target_pairs={{0,8},{8,0},{16,24},{24,16},{1,9},{9,1},{17,25},{25,17},{2,10},{10... | collective-permute-start | bytes 196616 | tf_op jit(solution)/shard_map/ppermute | solution.py:757
  52.6 4.6 %copy-start.4 = (f32[8,32,32]{2,1,0:T(8,128)S(1)}, f32[8,32,32]{2,1,0:T(8,128)}, u32[]{:S(2)}) copy-start(f32[8,32,32]{2,1,0:T(8,128)} %refs_6_.1) | copy-start | bytes 98308
  52.6 4.6 %copy-start.5 = (f32[8,32,32]{2,1,0:T(8,128)S(1)}, f32[8,32,32]{2,1,0:T(8,128)}, u32[]{:S(2)}) copy-start(f32[8,32,32]{2,1,0:T(8,128)} %refs_7_.1) | copy-start | bytes 98308
  (4 other events, 9.6 us)

commit v26 on v24

--- a/solution.py
+++ b/solution.py
@@ -549,7 +549,7 @@
         return carry[0] + folded(part), carry[1] + folded(part * phi[i + 1])
 
     zero = jnp.zeros((8, lanes), jnp.float32)
-    seen, cross = lax.fori_loop(0, planes, add_up, (zero, zero), unroll=8)
+    seen, cross = lax.fori_loop(0, planes, add_up, (zero, zero), unroll=UNROLL)
     first = (2 * cy - HALO) * (1 - y) + HALO * y
     size = GROUP * REACH
     for g in range(planes // GROUP):

time: 69.6 us -> 69.6 us (level)
  no operation moved by 1% of the time
where the time goes in v26:
time: 69.6 us; the launch traced here: 69.4 us
  starting transfers between devices  22.8 us (33%)
  Pallas kernels  18.7 us (27%)
  waiting for transfers between devices  14.9 us (21%)
  blocking collectives  11.4 us (16%)
  between operations  1.57 us (2%)
    pallas_call x22, Pallas kernels, run(): pl.pallas_call(body if waits else kernel, out_shape=tuple(outs), in_specs...  18.7 us
    all_to_all x1, blocking collectives, per_device_paired(): lax.all_to_all(jnp.broadcast_to(tile, (8 * n, 1, 128)), everyone, 0, 0)  11.4 us
    ppermute x6, starting transfers between devices, along_z(): return lax.ppermute(value, 'src', [(i, i ^ k) for i in range(n)])  9.08 us
    ppermute x7, starting transfers between devices, swap_x(): return lax.ppermute(value, 'gx', [(0, 1), (1, 0)])  8.76 us
    ppermute x6, waiting for transfers between devices, along_z(): return lax.ppermute(value, 'src', [(i, i ^ k) for i in range(n)])  6.42 us
    ppermute x3, starting transfers between devices, across_y(): return lax.ppermute(value, 'gy', [(i, (i + 2) % 4) for i in range(4)])  4.75 us
    ppermute x7, waiting for transfers between devices, swap_x(): return lax.ppermute(value, 'gx', [(0, 1), (1, 0)])  3.47 us
    ppermute x3, waiting for transfers between devices, across_y(): return lax.ppermute(value, 'gy', [(i, (i + 2) % 4) for i in range(4)])  2.85 us
  transfers between devices with their start and end apart: 19, of which 10 were waited for; matrix products, arithmetic and copies ran while one was open for 0% of the time, Pallas kernels for 13%

profile of v26, /device:TPU:0, one launch (start us, length us, event | category | flops | bytes accessed | tf_op | source)
XLA Modules:
  0.0 69.4 jit_solution(2423322365590898925)
XLA Ops:
  0.6 3.0 %collective-permute-start = (s32[8,32,128]{2,1,0:T(8,128)}, s32[8,32,128]{2,1,0:T(8,128)S(1)}, u32[]{:S(2)}, u32[]{:S(2)}) collective-permute-start(s32[8,32,128]{2,1,0:T(8,128)} %refs_1_.3), channel_id=1, source_target_pairs={{0,4},{4,0},{1,5},{5,1},{2,6},{6,2},{3,7},{7,3},{8,12},{12,8},{9,1... | collective-permute-start | bytes 393224 | tf_op jit(solution)/shard_map/ppermute | solution.py:758
  3.6 1.9 %shard_map.122 = (f32[4,32,128]{2,1,0:T(8,128)}, f32[20,32,128]{2,1,0:T(8,128)}) custom-call(f32[4,8,32,128]{3,2,1,0:T(8,128)} %refs_0_.2, f32[8,32,32]{2,1,0:T(8,128)} %vk.5, f32[8,32,32]{2,1,0:T(8,128)} %va.5), custom_call_target="tpu_custom_call" | custom-call | tf_op jit(solution)/shard_map/pallas_call | solution.py:728
  5.6 4.1 %collective-permute-start.4 = (f32[4,32,128]{2,1,0:T(8,128)}, f32[4,32,128]{2,1,0:T(8,128)S(1)}, u32[]{:S(2)}, u32[]{:S(2)}) collective-permute-start(f32[4,32,128]{2,1,0:T(8,128)} %get-tuple-element.35), channel_id=1, source_target_pairs={{0,24},{8,16},{16,8},{24,0},{1,25},{9,17},{17,9},{25,1},{2,26},{10... | collective-permute-start | bytes 196616 | tf_op jit(solution)/shard_map/ppermute | solution.py:764
  11.0 2.1 %shard_map.121 = (f32[16,72,128]{2,1,0:T(8,128)S(1)}, f32[1,128]{1,0:T(1,128)S(1)}) custom-call(s32[1,1024]{1,0:T(1,128)S(1)} %bitcast.3, f32[1]{0:T(128)S(6)} %copy.13.refs_1_, s32[8,32,128]{2,1,0:T(8,128)S(1)} %collective-permute-done.refs_2_.refs_3_), custom_call_target="tpu_custom_call" | custom-call | flops 301989888 | bytes 589824 | tf_op jit(solution)/shard_map/pallas_call | solution.py:728
  13.1 2.1 %collective-permute-done.3.refs_1_ = f32[4,32,128]{2,1,0:T(8,128)S(1)} collective-permute-done((f32[4,32,128]{2,1,0:T(8,128)}, f32[4,32,128]{2,1,0:T(8,128)S(1)}, u32[]{:S(2)}, u32[]{:S(2)}) %collective-permute-start.3) | collective-permute-done | bytes 65568 | tf_op jit(solution)/shard_map/ppermute | solution.py:764
  15.2 1.6 %collective-permute-start.6 = (f32[12,32,128]{2,1,0:T(8,128)S(1)}, f32[12,32,128]{2,1,0:T(8,128)S(1)}, u32[]{:S(2)}, u32[]{:S(2)}) collective-permute-start(f32[12,32,128]{2,1,0:T(8,128)S(1)} %shard_map.123.refs_4_.joined), channel_id=1, source_target_pairs={{0,4},{4,0},{1,5},{5,1},{2,6},{6,2},{3,7},{7,3},{8,12},{12,8},{9,1... | collective-permute-start | bytes 589832 | tf_op jit(solution)/shard_map/ppermute | solution.py:758
  17.9 3.1 %collective-permute-done.6.refs_2_ = f32[12,32,128]{2,1,0:T(8,128)S(1)} collective-permute-done((f32[12,32,128]{2,1,0:T(8,128)S(1)}, f32[12,32,128]{2,1,0:T(8,128)S(1)}, u32[]{:S(2)}, u32[]{:S(2)}) %collective-permute-start.6) | collective-permute-done | bytes 196640 | tf_op jit(solution)/shard_map/ppermute | solution.py:758
  21.5 1.6 %collective-permute-start.7 = (f32[2,4,24,128]{3,2,1,0:T(8,128)S(1)}, f32[2,4,24,128]{3,2,1,0:T(8,128)S(1)}, u32[]{:S(2)}, u32[]{:S(2)}) collective-permute-start(f32[2,4,24,128]{3,2,1,0:T(8,128)S(1)} %shard_map.127.refs_2_), channel_id=1, source_target_pairs={{0,2},{1,3},{2,0},{3,1},{4,6},{5,7},{6,4},{7,5},{8,10},{9,11},{10,... | collective-permute-start | bytes 294920 | tf_op jit(solution)/shard_map/ppermute | solution.py:785
  23.4 1.6 %collective-permute-start.9 = (f32[2,4,24,128]{3,2,1,0:T(8,128)S(1)}, f32[2,4,24,128]{3,2,1,0:T(8,128)S(1)}, u32[]{:S(2)}, u32[]{:S(2)}) collective-permute-start(f32[2,4,24,128]{3,2,1,0:T(8,128)S(1)} %shard_map.128.refs_6_), channel_id=1, source_target_pairs={{0,2},{1,3},{2,0},{3,1},{4,6},{5,7},{6,4},{7,5},{8,10},{9,11},{10,... | collective-permute-start | bytes 294920 | tf_op jit(solution)/shard_map/ppermute | solution.py:785
  25.0 2.3 %shard_map.129 = (f32[18,72,128]{2,1,0:T(8,128)S(1)}, f32[16,72,128]{2,1,0:T(8,128)S(1)}, f32[17,72,128]{2,1,0:T(8,128)S(1)}, f32[16,72,128]{2,1,0:T(8,128)S(1)}...) custom-call(f32[16]{0:T(128)S(1)} %copy-done.6, f32[16]{0:T(128)S(1)} %copy-done.7, ...), custom_call_target="tpu_custom_call" | custom-call | flops 1000000000 | bytes 67108864 | tf_op jit(solution)/shard_map/pallas_call | solution.py:728
  27.3 0.8 %shard_map.130 = (f32[16,72,128]{2,1,0:T(8,128)S(1)}, f32[17,72,128]{2,1,0:T(8,128)S(1)}, f32[16,72,128]{2,1,0:T(8,128)S(1)}, f32[16,72,128]{2,1,0:T(8,128)S(1)}) custom-call(f32[16]{0:T(128)S(1)} %copy-done.6, f32[16]{0:T(128)S(1)} %copy-done.7, f32[2,4,24,128]{3,2,1,0:T(8,128)S(1)} %collective-permute-done.7.edge.refs_2_, ...), custom_call_target="tpu_custom_call" | custom-call | tf_op jit(solution)/shard_map/pallas_call | solution.py:728
  28.9 3.8 %shard_map.132 = (f32[16,72,128]{2,1,0:T(8,128)S(1)}, f32[104,128]{1,0:T(8,128)S(1)}) custom-call(f32[18,72,128]{2,1,0:T(8,128)S(1)} %get-tuple-element.45.phi, f32[16,72,128]{2,1,0:T(8,128)S(1)} %get-tuple-element.46.phi_y, f32[16,72,128]{2,1,0:T(8,128)S(1)} %get-tuple-element.47.phi_z, f32[16,72,128]{2,1,0:T(8,128)S(1)} %get-tuple-element.48.diag, ...), custom_call_target="tpu_custom_call" | custom-call | tf_op jit(solution)/shard_map/pallas_call | solution.py:728
  32.7 1.6 %collective-permute-start.10 = (f32[104,128]{1,0:T(8,128)S(1)}, f32[104,128]{1,0:T(8,128)S(1)}, u32[]{:S(2)}, u32[]{:S(2)}) collective-permute-start(f32[104,128]{1,0:T(8,128)S(1)} %get-tuple-element.53.sent), channel_id=1, source_target_pairs={{0,2},{1,3},{2,0},{3,1},{4,6},{5,7},{6,4},{7,5},{8,10},{9,11},{10,... | collective-permute-start | bytes 159752 | tf_op jit(solution)/shard_map/ppermute | solution.py:785
  34.2 2.6 %collective-permute-done.10.came = f32[104,128]{1,0:T(8,128)S(1)} collective-permute-done((f32[104,128]{1,0:T(8,128)S(1)}, f32[104,128]{1,0:T(8,128)S(1)}, u32[]{:S(2)}, u32[]{:S(2)}) %collective-permute-start.10) | collective-permute-done | bytes 53280 | tf_op jit(solution)/shard_map/ppermute | solution.py:785
  36.9 3.8 %shard_map.133 = (f32[2,16,32,128]{3,2,1,0:T(8,128)S(1)}, f32[2,16,32,128]{3,2,1,0:T(8,128)S(1)}) custom-call(f32[18,72,128]{2,1,0:T(8,128)S(1)} %get-tuple-element.45.phi, f32[16,72,128]{2,1,0:T(8,128)S(1)} %get-tuple-element.46.phi_y, f32[16,72,128]{2,1,0:T(8,128)S(1)} %get-tuple-element.47.phi_z, f32[16,72,128]{2,1,0:T(8,128)S(1)} %get-tuple-element.52.change, ...), custom_call_target="tpu_custom_call" | custom-call | tf_op jit(solution)/shard_map/pallas_call | solution.py:728
  40.8 1.9 %collective-permute-done.11.came.refs_1_ = f32[2,16,32,128]{3,2,1,0:T(8,128)S(1)} collective-permute-done((f32[2,16,32,128]{3,2,1,0:T(8,128)S(1)}, f32[2,16,32,128]{3,2,1,0:T(8,128)S(1)}, u32[]{:S(2)}, u32[]{:S(2)}) %collective-permute-start.11) | collective-permute-done | bytes 524320 | tf_op jit(solution)/shard_map/ppermute | solution.py:761
  42.9 1.6 %collective-permute-start.12 = (f32[1,2,2,32,128]{4,3,2,1,0:T(8,128)S(1)}, f32[1,2,2,32,128]{4,3,2,1,0:T(8,128)S(1)}, u32[]{:S(2)}, u32[]{:S(2)}) collective-permute-start(f32[1,2,2,32,128]{4,3,2,1,0:T(8,128)S(1)} %get-tuple-element.57), channel_id=1, source_target_pairs={{0,4},{4,0},{1,5},{5,1},{2,6},{6,2},{3,7},{7,3},{8,12},{12,8},{9,1... | collective-permute-start | bytes 196616 | tf_op jit(solution)/shard_map/ppermute | solution.py:758
  45.0 1.5 %collective-permute-start.17 = (f32[1,2,2,32,128]{4,3,2,1,0:T(8,128)S(1)}, f32[1,2,2,32,128]{4,3,2,1,0:T(8,128)S(1)}, u32[]{:S(2)}, u32[]{:S(2)}) collective-permute-start(f32[1,2,2,32,128]{4,3,2,1,0:T(8,128)S(1)} %get-tuple-element.59), channel_id=1, source_target_pairs={{0,4},{4,0},{1,5},{5,1},{2,6},{6,2},{3,7},{7,3},{8,12},{12,8},{9,1... | collective-permute-start | bytes 196616 | tf_op jit(solution)/shard_map/ppermute | solution.py:758
  47.7 2.0 %collective-permute-start.13 = (f32[2,2,32,128]{3,2,1,0:T(8,128)S(1)}, f32[2,2,32,128]{3,2,1,0:T(8,128)S(1)}, u32[]{:S(2)}, u32[]{:S(2)}) collective-permute-start(f32[2,2,32,128]{3,2,1,0:T(8,128)S(1)} %shard_map.136), channel_id=1, source_target_pairs={{0,16},{8,24},{16,0},{24,8},{1,17},{9,25},{17,1},{25,9},{2,18},{10... | collective-permute-start | bytes 196616 | tf_op jit(solution)/shard_map/ppermute | solution.py:764
  49.7 2.3 %collective-permute-start.15 = (f32[2,2,32,128]{3,2,1,0:T(8,128)S(1)}, f32[2,2,32,128]{3,2,1,0:T(8,128)S(1)}, u32[]{:S(2)}, u32[]{:S(2)}) collective-permute-start(f32[2,2,32,128]{3,2,1,0:T(8,128)S(1)} %shard_map.137), channel_id=1, source_target_pairs={{0,24},{8,16},{16,8},{24,0},{1,25},{9,17},{17,9},{25,1},{2,26},{10... | collective-permute-start | bytes 196616 | tf_op jit(solution)/shard_map/ppermute | solution.py:764
  52.2 2.2 %collective-permute-done.13.refs_0_ = f32[2,2,32,128]{3,2,1,0:T(8,128)S(1)} collective-permute-done((f32[2,2,32,128]{3,2,1,0:T(8,128)S(1)}, f32[2,2,32,128]{3,2,1,0:T(8,128)S(1)}, u32[]{:S(2)}, u32[]{:S(2)}) %collective-permute-start.13) | collective-permute-done | bytes 65568 | tf_op jit(solution)/shard_map/ppermute | solution.py:764
  54.4 1.4 %collective-permute-done.15.refs_1_ = f32[2,2,32,128]{3,2,1,0:T(8,128)S(1)} collective-permute-done((f32[2,2,32,128]{3,2,1,0:T(8,128)S(1)}, f32[2,2,32,128]{3,2,1,0:T(8,128)S(1)}, u32[]{:S(2)}, u32[]{:S(2)}) %collective-permute-start.15) | collective-permute-done | bytes 65568 | tf_op jit(solution)/shard_map/ppermute | solution.py:764
  57.0 11.4 %all_to_all.5.tiles = f32[32,1,128]{2,1,0:T(1,128)S(1)} all-to-all(f32[32,1,128]{2,1,0:T(1,128)S(1)} %broadcast_in_dim.3), channel_id=1, replica_groups=mesh['src'=4,'gx'=2,'gy'=4] {'src','gx','gy'}, dimensions={0} | all-to-all | bytes 32768 | tf_op jit(solution)/shard_map/all_to_all | solution.py:848
  68.4 1.0 %shard_map.142 = (f32[8,32,32]{2,1,0:T(8,128)}, f32[8,32,32]{2,1,0:T(8,128)}, f32[2]{0:T(128)}) custom-call(f32[32,1,128]{2,1,0:T(1,128)S(1)} %all_to_all.5.tiles, f32[8,32,32]{2,1,0:T(8,128)S(1)} %get-tuple-element.61.w_k, f32[8,32,32]{2,1,0:T(8,128)S(1)} %get-tuple-element.62.w_a, f32[8,32,32]{2,1,0:T(8,128)S(1)} %copy-done.1, f32[8,32,32]{2,1,0:T(8,128)S(1)} %copy-done.2), custom_call_target="tpu_custom_call" | custom-call | tf_op jit(solution)/shard_map/pallas_call | solution.py:728
  (56 shorter events, 6.6 us)
Async XLA Ops:
  0.6 10.3 %collective-permute-start = (s32[8,32,128]{2,1,0:T(8,128)}, s32[8,32,128]{2,1,0:T(8,128)S(1)}, u32[]{:S(2)}, u32[]{:S(2)}) collective-permute-start(s32[8,32,128]{2,1,0:T(8,128)} %refs_1_.3), channel_id=1, source_target_pairs={{0,4},{4,0},{1,5},{5,1},{2,6},{6,2},{3,7},{7,3},{8,12},{12,8},{9,1... | collective-permute-start | bytes 393224 | tf_op jit(solution)/shard_map/ppermute | solution.py:758
  5.5 5.4 %copy-start.8 = (s32[1024]{0:T(1024)S(1)}, s32[1024]{0:T(1024)}, u32[]{:S(2)}) copy-start(s32[1024]{0:T(1024)} %param.14) | copy-start | bytes 12292
  5.5 11.3 %collective-permute-start.1 = (f32[20,32,128]{2,1,0:T(8,128)}, f32[20,32,128]{2,1,0:T(8,128)S(1)}, u32[]{:S(2)}, u32[]{:S(2)}) collective-permute-start(f32[20,32,128]{2,1,0:T(8,128)} %get-tuple-element.34), channel_id=1, source_target_pairs={{0,4},{4,0},{1,5},{5,1},{2,6},{6,2},{3,7},{7,3},{8,12},{12,8},{9,1... | collective-permute-start | bytes 983048 | tf_op jit(solution)/shard_map/ppermute | solution.py:758
  5.6 7.5 %collective-permute-start.4 = (f32[4,32,128]{2,1,0:T(8,128)}, f32[4,32,128]{2,1,0:T(8,128)S(1)}, u32[]{:S(2)}, u32[]{:S(2)}) collective-permute-start(f32[4,32,128]{2,1,0:T(8,128)} %get-tuple-element.35), channel_id=1, source_target_pairs={{0,24},{8,16},{16,8},{24,0},{1,25},{9,17},{17,9},{25,1},{2,26},{10... | collective-permute-start | bytes 196616 | tf_op jit(solution)/shard_map/ppermute | solution.py:764
  9.7 5.5 %collective-permute-start.3 = (f32[4,32,128]{2,1,0:T(8,128)}, f32[4,32,128]{2,1,0:T(8,128)S(1)}, u32[]{:S(2)}, u32[]{:S(2)}) collective-permute-start(f32[4,32,128]{2,1,0:T(8,128)} %get-tuple-element.35), channel_id=1, source_target_pairs={{0,16},{8,24},{16,0},{24,8},{1,17},{9,25},{17,1},{25,9},{2,18},{10... | collective-permute-start | bytes 196616 | tf_op jit(solution)/shard_map/ppermute | solution.py:764
  9.7 5.5 %collective-permute-start.2 = (f32[4,32,128]{2,1,0:T(8,128)}, f32[4,32,128]{2,1,0:T(8,128)S(1)}, u32[]{:S(2)}, u32[]{:S(2)}) collective-permute-start(f32[4,32,128]{2,1,0:T(8,128)} %get-tuple-element.35), channel_id=1, source_target_pairs={{0,8},{8,0},{16,24},{24,16},{1,9},{9,1},{17,25},{25,17},{2,10},{10... | collective-permute-start | bytes 196616 | tf_op jit(solution)/shard_map/ppermute | solution.py:764
  13.1 3.7 %copy-start = (f32[4,8,32,128]{3,2,1,0:T(8,128)S(1)}, f32[4,8,32,128]{3,2,1,0:T(8,128)}, u32[]{:S(2)}) copy-start(f32[4,8,32,128]{3,2,1,0:T(8,128)} %refs_0_.2) | copy-start | bytes 1572868
  15.2 5.8 %collective-permute-start.6 = (f32[12,32,128]{2,1,0:T(8,128)S(1)}, f32[12,32,128]{2,1,0:T(8,128)S(1)}, u32[]{:S(2)}, u32[]{:S(2)}) collective-permute-start(f32[12,32,128]{2,1,0:T(8,128)S(1)} %shard_map.123.refs_4_.joined), channel_id=1, source_target_pairs={{0,4},{4,0},{1,5},{5,1},{2,6},{6,2},{3,7},{7,3},{8,12},{12,8},{9,1... | collective-permute-start | bytes 589832 | tf_op jit(solution)/shard_map/ppermute | solution.py:758
  17.4 4.0 %collective-permute-start.5 = (f32[2,16,32,128]{3,2,1,0:T(8,128)S(1)}, f32[2,16,32,128]{3,2,1,0:T(8,128)S(1)}, u32[]{:S(2)}, u32[]{:S(2)}) collective-permute-start(f32[2,16,32,128]{3,2,1,0:T(8,128)S(1)} %get-tuple-element.38.refs_1_.refs_3_), channel_id=1, source_target_pairs={{0,1},{1,0},{2,3},{3,2},{4,5},{5,4},{6,7},{7,6},{8,9},{9,8},{10,11... | collective-permute-start | bytes 1572872 | tf_op jit(solution)/shard_map/ppermute | solution.py:761
  21.4 2.0 %collective-permute-start.8 = (f32[2,16,32,128]{3,2,1,0:T(8,128)S(1)}, f32[2,16,32,128]{3,2,1,0:T(8,128)S(1)}, u32[]{:S(2)}, u32[]{:S(2)}) collective-permute-start(f32[2,16,32,128]{3,2,1,0:T(8,128)S(1)} %shard_map.126.refs_3_.refs_0_.vector), channel_id=1, source_target_pairs={{0,1},{1,0},{2,3},{3,2},{4,5},{5,4},{6,7},{7,6},{8,9},{9,8},{10,11... | collective-permute-start | bytes 1572872 | tf_op jit(solution)/shard_map/ppermute | solution.py:761
  21.5 3.5 %copy-start.6 = (f32[16]{0:T(128)S(1)}, f32[16]{0:T(128)}, u32[]{:S(2)}) copy-start(f32[16]{0:T(128)} %kap_table.1) | copy-start | bytes 196
  21.5 5.8 %collective-permute-start.7 = (f32[2,4,24,128]{3,2,1,0:T(8,128)S(1)}, f32[2,4,24,128]{3,2,1,0:T(8,128)S(1)}, u32[]{:S(2)}, u32[]{:S(2)}) collective-permute-start(f32[2,4,24,128]{3,2,1,0:T(8,128)S(1)} %shard_map.127.refs_2_), channel_id=1, source_target_pairs={{0,2},{1,3},{2,0},{3,1},{4,6},{5,7},{6,4},{7,5},{8,10},{9,11},{10,... | collective-permute-start | bytes 294920 | tf_op jit(solution)/shard_map/ppermute | solution.py:785
  23.4 5.5 %collective-permute-start.9 = (f32[2,4,24,128]{3,2,1,0:T(8,128)S(1)}, f32[2,4,24,128]{3,2,1,0:T(8,128)S(1)}, u32[]{:S(2)}, u32[]{:S(2)}) collective-permute-start(f32[2,4,24,128]{3,2,1,0:T(8,128)S(1)} %shard_map.128.refs_6_), channel_id=1, source_target_pairs={{0,2},{1,3},{2,0},{3,1},{4,6},{5,7},{6,4},{7,5},{8,10},{9,11},{10,... | collective-permute-start | bytes 294920 | tf_op jit(solution)/shard_map/ppermute | solution.py:785
  32.7 4.2 %collective-permute-start.10 = (f32[104,128]{1,0:T(8,128)S(1)}, f32[104,128]{1,0:T(8,128)S(1)}, u32[]{:S(2)}, u32[]{:S(2)}) collective-permute-start(f32[104,128]{1,0:T(8,128)S(1)} %get-tuple-element.53.sent), channel_id=1, source_target_pairs={{0,2},{1,3},{2,0},{3,1},{4,6},{5,7},{6,4},{7,5},{8,10},{9,11},{10,... | collective-permute-start | bytes 159752 | tf_op jit(solution)/shard_map/ppermute | solution.py:785
  40.7 2.0 %collective-permute-start.11 = (f32[2,16,32,128]{3,2,1,0:T(8,128)S(1)}, f32[2,16,32,128]{3,2,1,0:T(8,128)S(1)}, u32[]{:S(2)}, u32[]{:S(2)}) collective-permute-start(f32[2,16,32,128]{3,2,1,0:T(8,128)S(1)} %get-tuple-element.55), channel_id=1, source_target_pairs={{0,1},{1,0},{2,3},{3,2},{4,5},{5,4},{6,7},{7,6},{8,9},{9,8},{10,11... | collective-permute-start | bytes 1572872 | tf_op jit(solution)/shard_map/ppermute | solution.py:761
  42.9 4.7 %collective-permute-start.12 = (f32[1,2,2,32,128]{4,3,2,1,0:T(8,128)S(1)}, f32[1,2,2,32,128]{4,3,2,1,0:T(8,128)S(1)}, u32[]{:S(2)}, u32[]{:S(2)}) collective-permute-start(f32[1,2,2,32,128]{4,3,2,1,0:T(8,128)S(1)} %get-tuple-element.57), channel_id=1, source_target_pairs={{0,4},{4,0},{1,5},{5,1},{2,6},{6,2},{3,7},{7,3},{8,12},{12,8},{9,1... | collective-permute-start | bytes 196616 | tf_op jit(solution)/shard_map/ppermute | solution.py:758
  44.5 5.1 %collective-permute-start.14 = (f32[1,2,2,32,128]{4,3,2,1,0:T(8,128)S(1)}, f32[1,2,2,32,128]{4,3,2,1,0:T(8,128)S(1)}, u32[]{:S(2)}, u32[]{:S(2)}) collective-permute-start(f32[1,2,2,32,128]{4,3,2,1,0:T(8,128)S(1)} %get-tuple-element.58), channel_id=1, source_target_pairs={{0,4},{4,0},{1,5},{5,1},{2,6},{6,2},{3,7},{7,3},{8,12},{12,8},{9,1... | collective-permute-start | bytes 196616 | tf_op jit(solution)/shard_map/ppermute | solution.py:758
  45.0 7.0 %collective-permute-start.17 = (f32[1,2,2,32,128]{4,3,2,1,0:T(8,128)S(1)}, f32[1,2,2,32,128]{4,3,2,1,0:T(8,128)S(1)}, u32[]{:S(2)}, u32[]{:S(2)}) collective-permute-start(f32[1,2,2,32,128]{4,3,2,1,0:T(8,128)S(1)} %get-tuple-element.59), channel_id=1, source_target_pairs={{0,4},{4,0},{1,5},{5,1},{2,6},{6,2},{3,7},{7,3},{8,12},{12,8},{9,1... | collective-permute-start | bytes 196616 | tf_op jit(solution)/shard_map/ppermute | solution.py:758
  46.5 5.6 %collective-permute-start.16 = (f32[1,2,2,32,128]{4,3,2,1,0:T(8,128)S(1)}, f32[1,2,2,32,128]{4,3,2,1,0:T(8,128)S(1)}, u32[]{:S(2)}, u32[]{:S(2)}) collective-permute-start(f32[1,2,2,32,128]{4,3,2,1,0:T(8,128)S(1)} %get-tuple-element.56.refs_2_), channel_id=1, source_target_pairs={{0,4},{4,0},{1,5},{5,1},{2,6},{6,2},{3,7},{7,3},{8,12},{12,8},{9,1... | collective-permute-start | bytes 196616 | tf_op jit(solution)/shard_map/ppermute | solution.py:758
  47.7 6.7 %collective-permute-start.13 = (f32[2,2,32,128]{3,2,1,0:T(8,128)S(1)}, f32[2,2,32,128]{3,2,1,0:T(8,128)S(1)}, u32[]{:S(2)}, u32[]{:S(2)}) collective-permute-start(f32[2,2,32,128]{3,2,1,0:T(8,128)S(1)} %shard_map.136), channel_id=1, source_target_pairs={{0,16},{8,24},{16,0},{24,8},{1,17},{9,25},{17,1},{25,9},{2,18},{10... | collective-permute-start | bytes 196616 | tf_op jit(solution)/shard_map/ppermute | solution.py:764
  49.7 6.1 %collective-permute-start.15 = (f32[2,2,32,128]{3,2,1,0:T(8,128)S(1)}, f32[2,2,32,128]{3,2,1,0:T(8,128)S(1)}, u32[]{:S(2)}, u32[]{:S(2)}) collective-permute-start(f32[2,2,32,128]{3,2,1,0:T(8,128)S(1)} %shard_map.137), channel_id=1, source_target_pairs={{0,24},{8,16},{16,8},{24,0},{1,25},{9,17},{17,9},{25,1},{2,26},{10... | collective-permute-start | bytes 196616 | tf_op jit(solution)/shard_map/ppermute | solution.py:764
  52.0 4.5 %collective-permute-start.18 = (f32[2,2,32,128]{3,2,1,0:T(8,128)S(1)}, f32[2,2,32,128]{3,2,1,0:T(8,128)S(1)}, u32[]{:S(2)}, u32[]{:S(2)}) collective-permute-start(f32[2,2,32,128]{3,2,1,0:T(8,128)S(1)} %shard_map.140), channel_id=1, source_target_pairs={{0,8},{8,0},{16,24},{24,16},{1,9},{9,1},{17,25},{25,17},{2,10},{10... | collective-permute-start | bytes 196616 | tf_op jit(solution)/shard_map/ppermute | solution.py:764
  52.1 4.4 %copy-start.4 = (f32[8,32,32]{2,1,0:T(8,128)S(1)}, f32[8,32,32]{2,1,0:T(8,128)}, u32[]{:S(2)}) copy-start(f32[8,32,32]{2,1,0:T(8,128)} %refs_6_.1) | copy-start | bytes 98308
  52.1 4.4 %copy-start.5 = (f32[8,32,32]{2,1,0:T(8,128)S(1)}, f32[8,32,32]{2,1,0:T(8,128)}, u32[]{:S(2)}) copy-start(f32[8,32,32]{2,1,0:T(8,128)} %refs_7_.1) | copy-start | bytes 98308
  (4 other events, 9.6 us)
